TPU v7x, 32 devices: a whole 2x2x4 slice. The times are simulated.
32 devices in a mesh: grp: 4 (over x, core), blk: 8 (over z, y).
Axes of the slice: x: 2, y: 2, z: 4, core: 2. Of those that a mesh axis runs over, the one named last changes fastest.
Arguments:
- tokens: bfloat16 [8, 1024, 1536], P('grp', 'blk'), may hold values from -6 to 6
- cotangent: bfloat16 [8, 1024, 1536], P('grp', 'blk'), may hold values from -6 to 6
- segment_ids: int32 [8, 1024], P('grp', 'blk'), may hold values from 0 to 7, as said below
- position_ids: int32 [8, 1024], P('grp', 'blk'), may hold values from 0 to 1023, as said below
- w_attend: float32 [1536, 2048], P('blk'), may hold values from -0.15625 to 0.15625
- w_out: float32 [1536, 1536], P('blk'), may hold values from -1.25 to 1.25
- w_gate: float32 [1536, 8960], P('blk'), may hold values from -0.15625 to 0.15625
- w_up: float32 [1536, 8960], P('blk'), may hold values from -0.15625 to 0.15625
- w_down: float32 [8960, 1536], P('blk'), may hold values from -0.0625 to 0.0625
- small_params: float32 [5120], P('blk'), may hold values from -2 to 4, as said below
- first_attend: float32 [1536, 2048], P('blk'), may hold values from -9.1552734e-05 to 9.1552734e-05
- first_out: float32 [1536, 1536], P('blk'), may hold values from -9.1552734e-05 to 9.1552734e-05
- first_gate: float32 [1536, 8960], P('blk'), may hold values from -9.1552734e-05 to 9.1552734e-05
- first_up: float32 [1536, 8960], P('blk'), may hold values from -9.1552734e-05 to 9.1552734e-05
- first_down: float32 [8960, 1536], P('blk'), may hold values from -9.1552734e-05 to 9.1552734e-05
- first_small: float32 [5120], P('blk'), may hold values from -0.00036621094 to 0.00036621094
- second_attend: float32 [1536, 2048], P('blk'), may hold values from 1.1325313e-09 to 4.4873882e-09
- second_out: float32 [1536, 1536], P('blk'), may hold values from 1.1325313e-09 to 4.4873882e-09
- second_gate: float32 [1536, 8960], P('blk'), may hold values from 1.1325313e-09 to 4.4873882e-09
- second_up: float32 [1536, 8960], P('blk'), may hold values from 1.1325313e-09 to 4.4873882e-09
- second_down: float32 [8960, 1536], P('blk'), may hold values from 1.1325313e-09 to 4.4873882e-09
- second_small: float32 [5120], P('blk'), may hold values from 1.7949553e-08 to 7.265295e-08
Outputs:
- out_tokens: bfloat16 [8, 1024, 1536], P('grp', 'blk')
- grad_tokens: bfloat16 [8, 1024, 1536], P('grp', 'blk')
- grad_norm: float32 [], replicated
- new_first_attend: float32 [1536, 2048], P('blk')
- new_second_attend: float32 [1536, 2048], P('blk')
- new_attend: float32 [1536, 2048], P('blk')
- new_first_out: float32 [1536, 1536], P('blk')
- new_second_out: float32 [1536, 1536], P('blk')
- new_out: float32 [1536, 1536], P('blk')
- new_first_gate: float32 [1536, 8960], P('blk')
- new_second_gate: float32 [1536, 8960], P('blk')
- new_gate: float32 [1536, 8960], P('blk')
- new_first_up: float32 [1536, 8960], P('blk')
- new_second_up: float32 [1536, 8960], P('blk')
- new_up: float32 [1536, 8960], P('blk')
- new_first_down: float32 [8960, 1536], P('blk')
- new_second_down: float32 [8960, 1536], P('blk')
- new_down: float32 [8960, 1536], P('blk')
- new_first_small: float32 [5120], P('blk')
- new_second_small: float32 [5120], P('blk')
- new_small: float32 [5120], P('blk')
Inputs may be any that keep to these rules, and one draw needn't show every extreme that they name: `segment_ids`: within each row the ids start at 0 and never fall. Of each aligned group of 2 rows exactly one holds a single document; every other row holds exactly 8 documents. `position_ids`: each token's distance from the first token of its document (its run of equal segment ids) in its row. `small_params`: the gains (the first 3072 entries) are positive.
All inputs are finite; a program needn't handle non-finite values.
Results may differ from a plain program's by a relative error of at most 0.028.
Values may be sent and summed in bfloat16 or wider, within the bound.
No kernel may reach another device: no remote copies, remote signals or barrier semaphores. Data moves between devices by JAX's collectives and lax.ppermute only.
A program may use at most 512 MiB of HBM per device.

v0:
```python
import jax
import jax.numpy as jnp
from jax import lax
from jax.sharding import PartitionSpec as P

D = 1536
FF = 8960
H = 12
KVH = 2
HD = 128
STEP = 10
HQD = 1536
KVD = 256


NORM_EPS = 1e-06
ROPE_BASE = 10000.0
CLIP_NORM = 1.0
BETA_FIRST = 0.9
BETA_SECOND = 0.95
ADAM_EPS = 1e-08
WEIGHT_DECAY = 0.1
RATE_ATTEND = 0.06
RATE_OUT = 0.5
RATE_GATE = 0.06
RATE_DOWN = 0.03
RATE_VECTOR = 0.5
NEG_LARGE = -1e30


def norm_apply(values, gain):
    return values * lax.rsqrt(jnp.mean(values * values, axis=-1, keepdims=True) + NORM_EPS) * gain


def rotate(values, position):
    half = values.shape[-1] // 2
    freqs = ROPE_BASE ** (-2.0 * jnp.arange(half, dtype=jnp.float32) / values.shape[-1])
    angles = position.astype(jnp.float32)[:, None] * freqs[None, :]
    cosine = jnp.cos(angles)[:, None, :]
    sine = jnp.sin(angles)[:, None, :]
    first_half = values[..., :half]
    second_half = values[..., half:]
    return jnp.concatenate(
        [first_half * cosine - second_half * sine, second_half * cosine + first_half * sine],
        axis=-1,
    )


def swish_product(gate, up_proj):
    return jax.nn.silu(gate) * up_proj


def left_product(left_side, right_side):
    return lax.dot_general(
        left_side, right_side, (((0,), (0,)), ((), ())), preferred_element_type=jnp.float32
    )


def right_transposed(left_side, right_side):
    return lax.dot_general(
        left_side, right_side, (((1,), (1,)), ((), ())), preferred_element_type=jnp.float32
    )


def square_total(arrays):
    return sum((jnp.sum(member * member) for member in arrays))


def unchanged(state_in):
    return state_in


def adam_step(weight, grad, first, second, rate, decay):
    first_new = BETA_FIRST * first + (1.0 - BETA_FIRST) * grad
    second_new = BETA_SECOND * second + (1.0 - BETA_SECOND) * grad * grad
    first_hat = first_new / (1.0 - BETA_FIRST**STEP)
    second_hat = second_new / (1.0 - BETA_SECOND**STEP)
    weight_new = weight - rate * (first_hat / (jnp.sqrt(second_hat) + ADAM_EPS) + decay * weight)
    return (first_new, second_new, weight_new)


def on_device(
    tokens,
    cotangent,
    segment_ids,
    position_ids,
    w_attend,
    w_out,
    w_gate,
    w_up,
    w_down,
    small_params,
    first_attend,
    first_out,
    first_gate,
    first_up,
    first_down,
    first_small,
    second_attend,
    second_out,
    second_gate,
    second_up,
    second_down,
    second_small,
):
    rows_here = tokens.shape[0]
    block_len = tokens.shape[1]
    blk_count = lax.axis_size("blk")
    seq_len = block_len * blk_count
    token_count = rows_here * block_len
    head_group = H // KVH
    score_scale = HD ** (-0.5)
    attend_full, out_full, gate_full, up_full, down_full, vector_full = (
        lax.all_gather(w_attend.astype(jnp.bfloat16), "blk", axis=0, tiled=True),
        lax.all_gather(w_out.astype(jnp.bfloat16), "blk", axis=0, tiled=True),
        lax.all_gather(w_gate.astype(jnp.bfloat16), "blk", axis=0, tiled=True),
        lax.all_gather(w_up.astype(jnp.bfloat16), "blk", axis=0, tiled=True),
        lax.all_gather(w_down.astype(jnp.bfloat16), "blk", axis=0, tiled=True),
        lax.all_gather(small_params.astype(jnp.bfloat16), "blk", axis=0, tiled=True),
    )
    vector = vector_full.astype(jnp.float32)
    gain_one = vector[:D]
    gain_two = vector[D : 2 * D]
    bias = vector[2 * D :]
    flat = tokens.reshape(token_count, D).astype(jnp.float32)
    positions = position_ids.reshape(token_count)
    h_one = norm_apply(flat, gain_one).astype(jnp.bfloat16)
    mixed = jnp.dot(h_one, attend_full, preferred_element_type=jnp.float32) + bias
    query = rotate(mixed[:, :HQD].reshape(token_count, H, HD), positions).astype(jnp.bfloat16)
    key_rot = rotate(mixed[:, HQD : HQD + KVD].reshape(token_count, KVH, HD), positions).astype(
        jnp.bfloat16
    )
    value_low = mixed[:, HQD + KVD :].astype(jnp.bfloat16)
    query_heads = query.reshape(rows_here, block_len, KVH, head_group, HD).transpose(0, 2, 3, 1, 4)
    key_send = key_rot.reshape(rows_here, block_len, KVD)
    value_send = value_low.reshape(rows_here, block_len, KVD)
    seg_send = segment_ids.astype(jnp.bfloat16)
    query_index = lax.axis_index("blk") * block_len + jnp.arange(block_len, dtype=jnp.int32)
    query_last = lax.axis_index("blk") * block_len + block_len - 1

    def visible(first_index, row_count, seg_keys):
        key_index = first_index + jnp.arange(row_count, dtype=jnp.int32)
        causal = key_index[None, :] <= query_index[:, None]
        same_doc = seg_keys[:, None, :] == seg_send[:, :, None]
        return jnp.logical_and(causal[None, :, :], same_doc)[:, None, None, :, :]

    stat_shape = (rows_here, KVH, head_group, block_len)
    start_state = (
        jnp.full(stat_shape, NEG_LARGE, jnp.float32),
        jnp.zeros(stat_shape, jnp.float32),
        jnp.zeros(stat_shape + (HD,), jnp.float32),
    )
    first_index = jnp.int32(0)
    key_piece = lax.all_gather(key_send, "blk", axis=1, tiled=True)
    value_piece = lax.all_gather(value_send, "blk", axis=1, tiled=True)
    seg_piece = lax.all_gather(seg_send, "blk", axis=1, tiled=True)
    row_count = key_piece.shape[1]

    def attend_piece(state_in):
        running_max, running_sum, running_out = state_in
        keys_here = key_piece.reshape(rows_here, row_count, KVH, HD)
        values_here = value_piece.reshape(rows_here, row_count, KVH, HD)
        scores = (
            jnp.einsum(
                "rkgqd,rnkd->rkgqn", query_heads, keys_here, preferred_element_type=jnp.float32
            )
            * score_scale
        )
        allowed = visible(first_index, row_count, seg_piece)
        scores = jnp.where(allowed, scores, NEG_LARGE)
        new_max = jnp.maximum(running_max, jnp.max(scores, axis=-1))
        weights = jnp.where(allowed, jnp.exp(scores - new_max[..., None]), 0.0)
        running_sum = jnp.sum(weights, axis=-1)
        running_out = jnp.einsum(
            "rkgqn,rnkd->rkgqd",
            weights.astype(jnp.bfloat16),
            values_here,
            preferred_element_type=jnp.float32,
        )
        return (new_max, running_sum, running_out)

    running_max, running_sum, running_out = lax.cond(
        first_index > query_last, unchanged, attend_piece, start_state
    )
    attended_heads = running_out / running_sum[..., None]
    log_total = running_max + jnp.log(running_sum)
    att_in = attended_heads.transpose(0, 3, 1, 2, 4).reshape(token_count, HQD).astype(jnp.bfloat16)
    resid = flat + jnp.dot(att_in, out_full, preferred_element_type=jnp.float32)
    h_two = norm_apply(resid, gain_two).astype(jnp.bfloat16)
    gate = jnp.dot(h_two, gate_full, preferred_element_type=jnp.float32)
    up_proj = jnp.dot(h_two, up_full, preferred_element_type=jnp.float32)
    hidden = swish_product(gate, up_proj).astype(jnp.bfloat16)
    out_tokens = (resid + jnp.dot(hidden, down_full, preferred_element_type=jnp.float32)).astype(
        jnp.bfloat16
    )
    dy_low = cotangent.reshape(token_count, D)
    d_hidden = right_transposed(dy_low, down_full)
    swish_value, swish_back = jax.vjp(swish_product, gate, up_proj)
    d_gate, d_up = swish_back(d_hidden)
    d_gate = d_gate.astype(jnp.bfloat16)
    d_up = d_up.astype(jnp.bfloat16)
    d_htwo = right_transposed(d_gate, gate_full) + right_transposed(d_up, up_full)
    norm_value_two, norm_back_two = jax.vjp(norm_apply, resid, gain_two)
    d_resid_norm, grad_gain_two = norm_back_two(d_htwo)
    d_resid = dy_low.astype(jnp.float32) + d_resid_norm
    d_att = d_resid.astype(jnp.bfloat16)
    d_attended = right_transposed(d_att, out_full).astype(jnp.bfloat16)
    grad_heads = d_attended.reshape(rows_here, block_len, KVH, head_group, HD).transpose(
        0, 2, 3, 1, 4
    )
    row_delta = jnp.sum(grad_heads.astype(jnp.float32) * attended_heads, axis=-1)
    key_all, value_all, seg_all = (
        lax.all_gather(key_send, "blk", axis=1, tiled=True),
        lax.all_gather(value_send, "blk", axis=1, tiled=True),
        lax.all_gather(seg_send, "blk", axis=1, tiled=True),
    )
    key_block = min(512, seq_len)
    block_count = seq_len // key_block

    def back_block(block_step, state_now):
        first_index = block_step * key_block

        def grads_piece(state_in):
            dq_sum, dk_all, dv_all = state_in
            keys_here = lax.dynamic_slice_in_dim(key_all, first_index, key_block, 1).reshape(
                rows_here, key_block, KVH, HD
            )
            values_here = lax.dynamic_slice_in_dim(value_all, first_index, key_block, 1).reshape(
                rows_here, key_block, KVH, HD
            )
            seg_here = lax.dynamic_slice_in_dim(seg_all, first_index, key_block, 1)
            scores = (
                jnp.einsum(
                    "rkgqd,rnkd->rkgqn", query_heads, keys_here, preferred_element_type=jnp.float32
                )
                * score_scale
            )
            allowed = visible(first_index, key_block, seg_here)
            probs = jnp.where(allowed, jnp.exp(scores - log_total[..., None]), 0.0)
            probs_low = probs.astype(jnp.bfloat16)
            dprob = jnp.einsum(
                "rkgqd,rnkd->rkgqn", grad_heads, values_here, preferred_element_type=jnp.float32
            )
            dscore = (probs * (dprob - row_delta[..., None])).astype(jnp.bfloat16)
            dq_sum = dq_sum + jnp.einsum(
                "rkgqn,rnkd->rkgqd", dscore, keys_here, preferred_element_type=jnp.float32
            )
            dk_piece = jnp.einsum(
                "rkgqn,rkgqd->rnkd", dscore, query_heads, preferred_element_type=jnp.float32
            )
            dv_piece = jnp.einsum(
                "rkgqn,rkgqd->rnkd", probs_low, grad_heads, preferred_element_type=jnp.float32
            )
            dk_all = lax.dynamic_update_slice_in_dim(dk_all, dk_piece, first_index, 1)
            dv_all = lax.dynamic_update_slice_in_dim(dv_all, dv_piece, first_index, 1)
            return (dq_sum, dk_all, dv_all)

        return lax.cond(first_index > query_last, unchanged, grads_piece, state_now)

    back_start = (
        jnp.zeros(stat_shape + (HD,), jnp.float32),
        jnp.zeros((rows_here, seq_len, KVH, HD), jnp.float32),
        jnp.zeros((rows_here, seq_len, KVH, HD), jnp.float32),
    )
    dq_sum, dk_all, dv_all = lax.fori_loop(0, block_count, back_block, back_start)
    dk_here, dv_here = (
        lax.psum_scatter(
            dk_all.reshape(rows_here, seq_len, KVD).astype(jnp.bfloat16),
            "blk",
            scatter_dimension=1,
            tiled=True,
        ).astype(jnp.float32),
        lax.psum_scatter(
            dv_all.reshape(rows_here, seq_len, KVD).astype(jnp.bfloat16),
            "blk",
            scatter_dimension=1,
            tiled=True,
        ).astype(jnp.float32),
    )
    dq_tokens = (dq_sum * score_scale).transpose(0, 3, 1, 2, 4).reshape(token_count, H, HD)
    d_query = rotate(dq_tokens, -positions).reshape(token_count, HQD)
    d_key = rotate((dk_here * score_scale).reshape(token_count, KVH, HD), -positions).reshape(
        token_count, KVD
    )
    d_value = dv_here.reshape(token_count, KVD)
    d_mixed = jnp.concatenate([d_query, d_key, d_value], axis=1).astype(jnp.bfloat16)
    grad_bias = jnp.sum(d_mixed.astype(jnp.float32), axis=0)
    d_hone = right_transposed(d_mixed, attend_full)
    norm_value_one, norm_back_one = jax.vjp(norm_apply, flat, gain_one)
    d_flat_norm, grad_gain_one = norm_back_one(d_hone)
    grad_tokens = (d_resid + d_flat_norm).astype(jnp.bfloat16)
    vector_term = jnp.concatenate([grad_gain_one, grad_gain_two, grad_bias])
    d_gate_up = jnp.concatenate([d_gate, d_up], axis=1)
    share_gate_up = lax.psum_scatter(
        left_product(h_two, d_gate_up).astype(jnp.bfloat16), "blk", scatter_dimension=0, tiled=True
    ).astype(jnp.float32)
    share_down = lax.psum_scatter(
        left_product(hidden, dy_low).astype(jnp.bfloat16), "blk", scatter_dimension=0, tiled=True
    ).astype(jnp.float32)
    share_attend, share_out, share_vector = (
        lax.psum_scatter(
            left_product(h_one, d_mixed).astype(jnp.bfloat16),
            "blk",
            scatter_dimension=0,
            tiled=True,
        ).astype(jnp.float32),
        lax.psum_scatter(
            left_product(att_in, d_att).astype(jnp.bfloat16), "blk", scatter_dimension=0, tiled=True
        ).astype(jnp.float32),
        lax.psum_scatter(
            vector_term.astype(jnp.bfloat16), "blk", scatter_dimension=0, tiled=True
        ).astype(jnp.float32),
    )
    share_attend, share_out, share_gate_up, share_down, share_vector = (
        lax.psum(share_attend.astype(jnp.bfloat16), "grp").astype(jnp.float32),
        lax.psum(share_out.astype(jnp.bfloat16), "grp").astype(jnp.float32),
        lax.psum(share_gate_up.astype(jnp.bfloat16), "grp").astype(jnp.float32),
        lax.psum(share_down.astype(jnp.bfloat16), "grp").astype(jnp.float32),
        lax.psum(share_vector.astype(jnp.bfloat16), "grp").astype(jnp.float32),
    )
    square_sum = lax.psum(
        square_total((share_attend, share_out, share_gate_up, share_down, share_vector)), "blk"
    )
    grad_norm = jnp.sqrt(square_sum)
    factor = jnp.minimum(1.0, CLIP_NORM / (grad_norm + 1e-06))
    new_first_attend, new_second_attend, new_attend = adam_step(
        w_attend, factor * share_attend, first_attend, second_attend, RATE_ATTEND, WEIGHT_DECAY
    )
    new_first_out, new_second_out, new_out = adam_step(
        w_out, factor * share_out, first_out, second_out, RATE_OUT, WEIGHT_DECAY
    )
    new_first_gate, new_second_gate, new_gate = adam_step(
        w_gate, factor * share_gate_up[:, :FF], first_gate, second_gate, RATE_GATE, WEIGHT_DECAY
    )
    new_first_up, new_second_up, new_up = adam_step(
        w_up, factor * share_gate_up[:, FF:], first_up, second_up, RATE_GATE, WEIGHT_DECAY
    )
    new_first_down, new_second_down, new_down = adam_step(
        w_down, factor * share_down, first_down, second_down, RATE_DOWN, WEIGHT_DECAY
    )
    new_first_small, new_second_small, new_small = adam_step(
        small_params, factor * share_vector, first_small, second_small, RATE_VECTOR, 0.0
    )
    return (
        out_tokens.reshape(rows_here, block_len, D),
        grad_tokens.reshape(rows_here, block_len, D),
        grad_norm,
        new_first_attend,
        new_second_attend,
        new_attend,
        new_first_out,
        new_second_out,
        new_out,
        new_first_gate,
        new_second_gate,
        new_gate,
        new_first_up,
        new_second_up,
        new_up,
        new_first_down,
        new_second_down,
        new_down,
        new_first_small,
        new_second_small,
        new_small,
    )


def solution(mesh):
    placed = (
        P("grp", "blk", None),
        P("grp", "blk", None),
        P("grp", "blk"),
        P("grp", "blk"),
        P("blk", None),
        P("blk", None),
        P("blk", None),
        P("blk", None),
        P("blk", None),
        P("blk"),
        P("blk", None),
        P("blk", None),
        P("blk", None),
        P("blk", None),
        P("blk", None),
        P("blk"),
        P("blk", None),
        P("blk", None),
        P("blk", None),
        P("blk", None),
        P("blk", None),
        P("blk"),
    )
    return jax.shard_map(
        on_device,
        mesh=mesh,
        in_specs=placed,
        out_specs=(
            P("grp", "blk", None),
            P("grp", "blk", None),
            P(),
            P("blk", None),
            P("blk", None),
            P("blk", None),
            P("blk", None),
            P("blk", None),
            P("blk", None),
            P("blk", None),
            P("blk", None),
            P("blk", None),
            P("blk", None),
            P("blk", None),
            P("blk", None),
            P("blk", None),
            P("blk", None),
            P("blk", None),
            P("blk"),
            P("blk"),
            P("blk"),
        ),
        check_vma=False,
    )
```

profile of v0, /device:TPU:0, one launch (start us, length us, event | category | flops | bytes accessed | tf_op | source)
XLA Modules:
  0.0 3928.1 jit_solution(13765729786965574789)
XLA Ops:
  10.5 32.5 all-gather
  48.7 64.0 %all-gather.9.cloned.1.call-done = bf16[1536,2048]{1,0:T(8,128)(2,1)} async-done(((bf16[192,2048]{1,0:T(8,128)(2,1)}), bf16[1536,2048]{1,0:T(8,128)(2,1)}) %all-gather.9.cloned.1.call-update) | async-done | bytes 6291472 | tf_op jit(solution)/shard_map/all_gather | solution.py:114
  139.8 17.7 all_gather.30
  164.4 36.5 all-gather.13.cloned.1.call-done
  200.9 19.7 conditional.2
  225.6 56.7 %all-gather.15.cloned.1.call-done = bf16[1536,1536]{1,0:T(8,128)(2,1)} async-done(((bf16[192,1536]{1,0:T(8,128)(2,1)}), bf16[1536,1536]{1,0:T(8,128)(2,1)}) %all-gather.15.cloned.1.call-update) | async-done | bytes 4718608 | tf_op jit(solution)/shard_map/all_gather | solution.py:115
  287.5 519.6 %all-gather.17.cloned.1.call-done = bf16[1536,8960]{1,0:T(8,128)(2,1)} async-done(((bf16[192,8960]{1,0:T(8,128)(2,1)}), bf16[1536,8960]{1,0:T(8,128)(2,1)}) %all-gather.17.cloned.1.call-update) | async-done | bytes 27525136 | tf_op jit(solution)/shard_map/all_gather | solution.py:116
  822.1 511.7 %all-gather.19.cloned.1.call-done = bf16[1536,8960]{1,0:T(8,128)(2,1)} async-done(((bf16[192,8960]{1,0:T(8,128)(2,1)}), bf16[1536,8960]{1,0:T(8,128)(2,1)}) %all-gather.19.cloned.1.call-update) | async-done | bytes 27525136 | tf_op jit(solution)/shard_map/all_gather | solution.py:117
  1333.8 15.5 fusion.87
  1349.3 511.3 %all-gather.21.cloned.1.call-done = bf16[8960,1536]{1,0:T(8,128)(2,1)} async-done(((bf16[1120,1536]{1,0:T(8,128)(2,1)}), bf16[8960,1536]{1,0:T(8,128)(2,1)}) %all-gather.21.cloned.1.call-update) | async-done | bytes 27525136 | tf_op jit(solution)/shard_map/all_gather | solution.py:118
  1860.6 21.4 multiply_convert_fusion
  1896.9 15.6 multiply_reduce_fusion.1
  1955.0 61.4 %reduce-scatter.19.cloned.1.call-done = bf16[128,512]{1,0:T(8,128)(2,1)} async-done(((bf16[1024,512]{1,0:T(8,128)(2,1)}), bf16[128,512]{1,0:T(8,128)(2,1)}) %reduce-scatter.19.cloned.1.call-update) | async-done | bytes 131088
  2018.8 64.5 %reduce-scatter.21.cloned.1.call-done = bf16[128,512]{1,0:T(8,128)(2,1)} async-done(((bf16[1024,512]{1,0:T(8,128)(2,1)}), bf16[128,512]{1,0:T(8,128)(2,1)}) %reduce-scatter.21.cloned.1.call-update) | async-done | bytes 131088
  2106.7 25.1 convolution_convert_fusion
  2131.9 49.8 %reduce-scatter.13.cloned.1.call-done = bf16[192,1536]{1,0:T(8,128)(2,1)} async-done(((bf16[1536,1536]{1,0:T(8,128)(2,1)}), bf16[192,1536]{1,0:T(8,128)(2,1)}) %reduce-scatter.13.cloned.1.call-update) | async-done | bytes 589840 | tf_op jit(solution)/shard_map/reduce_scatter | solution.py:307
  2181.6 121.9 %reduce-scatter.11.cloned.1.call-done = bf16[192,2048]{1,0:T(8,128)(2,1)} async-done(((bf16[1536,2048]{1,0:T(8,128)(2,1)}), bf16[192,2048]{1,0:T(8,128)(2,1)}) %reduce-scatter.11.cloned.1.call-update) | async-done | bytes 786448 | tf_op jit(solution)/shard_map/reduce_scatter | solution.py:301
  2303.5 440.1 %reduce-scatter.17.cloned.1.call-done = bf16[1120,1536]{1,0:T(8,128)(2,1)} async-done(((bf16[8960,1536]{1,0:T(8,128)(2,1)}), bf16[1120,1536]{1,0:T(8,128)(2,1)}) %reduce-scatter.17.cloned.1.call-update) | async-done | bytes 3440656 | tf_op jit(solution)/shard_map/reduce_scatter | solution.py:297
  2743.6 862.0 %reduce-scatter.15.cloned.1.call-done = bf16[192,17920]{1,0:T(8,128)(2,1)} async-done(((bf16[1536,17920]{1,0:T(8,128)(2,1)}), bf16[192,17920]{1,0:T(8,128)(2,1)}) %reduce-scatter.15.cloned.1.call-update) | async-done | bytes 6881296 | tf_op jit(solution)/shard_map/reduce_scatter | solution.py:294
  3607.6 15.8 fusion.41
  3629.9 35.3 all-reduce
  3674.8 140.6 %all-reduce.4.cloned.1.call-done = (bf16[192,2048]{1,0:T(8,128)(2,1)}, bf16[192,1536]{1,0:T(8,128)(2,1)}, bf16[192,17920]{1,0:T(8,128)(2,1)}, bf16[1120,1536]{1,0:T(8,128)(2,1)}) async-done(((bf16[192,2048]{1,0:T(8,128)(2,1)}, bf16[192,1536]{1,0:T(8,128)(2,1)}, bf16[192,17920]{1,0:T(8,128)(2,1)}, bf16[1120,1536]{1,0:T(8,128)(2,1)}), (bf16[192,2048]{1,0:T(8,128)(2,1)}, bf16[192,1536]{1,0:T(8,128)(2,1)}, ...) | async-done | bytes 11698192 | tf_op jit(solution)/shard_map/psum | solution.py:315
  3841.9 22.1 psum.47
  3889.3 30.9 multiply_subtract_fusion.1
  (256 shorter events, 257.4 us)
Async XLA Ops:
  7.2 105.5 %all-gather.9.cloned.1.call-start = ((), (), s32[]{:S(2)}) async-start(), calls=%async_computation.6 | async-start | bytes 7077888 | tf_op jit(solution)/shard_map/all_gather | solution.py:114
  9.7 154.7 %all-gather.11.cloned.1.call-start = ((), (), s32[]{:S(2)}) async-start(), calls=%async_computation.7 | async-start | bytes 1179648 | tf_op jit(solution)/shard_map/all_gather | solution.py:154
  47.9 69.4 %copy-start.39 = (f32[256]{0:T(256)}, f32[256]{0:T(256)S(1)}, u32[]{:S(2)}) copy-start(f32[256]{0:T(256)S(1)} %bitcast_rsqrt_fusion) | copy-start | bytes 3076
  48.4 64.3 %copy-start.34 = (f32[1536]{0:T(1024)}, f32[1536]{0:T(1024)S(1)}, u32[]{:S(2)}) copy-start(f32[1536]{0:T(1024)S(1)} %get-tuple-element.512) | copy-start | bytes 18436
  48.7 68.6 %copy-start.14 = (bf16[256,1536]{1,0:T(8,128)(2,1)}, bf16[256,1536]{1,0:T(8,128)(2,1)S(1)}, u32[]{:S(2)}) copy-start(bf16[256,1536]{1,0:T(8,128)(2,1)S(1)} %fusion.52) | copy-start | bytes 2359300
  48.7 74.6 %copy-start.12 = (f32[192,1536]{1,0:T(8,128)S(1)}, f32[192,1536]{1,0:T(8,128)}, u32[]{:S(2)}) copy-start(f32[192,1536]{1,0:T(8,128)} %param.33) | copy-start | bytes 3538948
  121.4 79.5 %all-gather.13.cloned.1.call-start = ((), (), s32[]{:S(2)}) async-start(), calls=%async_computation.8 | async-start | bytes 1179648 | tf_op jit(solution)/shard_map/all_gather | solution.py:155
  123.2 159.1 %all-gather.15.cloned.1.call-start = ((), (), s32[]{:S(2)}) async-start(), calls=%async_computation.9 | async-start | bytes 5308416 | tf_op jit(solution)/shard_map/all_gather | solution.py:115
  124.2 683.0 %all-gather.17.cloned.1.call-start = ((), (), s32[]{:S(2)}) async-start(), calls=%async_computation.10 | async-start | bytes 30965760 | tf_op jit(solution)/shard_map/all_gather | solution.py:116
  129.3 1204.5 %all-gather.19.cloned.1.call-start = ((), (), s32[]{:S(2)}) async-start(), calls=%async_computation.11 | async-start | bytes 30965760 | tf_op jit(solution)/shard_map/all_gather | solution.py:117
  134.5 1726.1 %all-gather.21.cloned.1.call-start = ((), (), s32[]{:S(2)}) async-start(), calls=%async_computation.12 | async-start | bytes 30965760 | tf_op jit(solution)/shard_map/all_gather | solution.py:118
  139.7 1876.7 %reduce-scatter.19.cloned.1.call-start = ((), (), s32[]{:S(2)}) async-start(), calls=%async_computation.17 | async-start | bytes 1179648
  225.6 61.9 %copy-start.10 = (bf16[2,2,6,128,128]{3,0,4,2,1:T(2,128)(2,1)}, bf16[2,2,6,128,128]{3,0,4,2,1:T(2,128)(2,1)S(1)}, u32[]{:S(2)}) copy-start(bf16[2,2,6,128,128]{3,0,4,2,1:T(2,128)(2,1)S(1)} %get-tuple-element.491) | copy-start | bytes 2359300
  287.5 1046.3 %copy-start.23 = (bf16[256,1536]{1,0:T(8,128)(2,1)}, bf16[256,1536]{1,0:T(8,128)(2,1)S(1)}, u32[]{:S(2)}) copy-start(bf16[256,1536]{1,0:T(8,128)(2,1)S(1)} %multiply_convert_fusion.2) | copy-start | bytes 2359300
  822.1 1038.4 %copy-start.26 = (bf16[2,128,1536]{2,1,0:T(8,128)(2,1)S(1)}, bf16[2,128,1536]{2,1,0:T(8,128)(2,1)}, u32[]{:S(2)}) copy-start(bf16[2,128,1536]{2,1,0:T(8,128)(2,1)} %param.29) | copy-start | bytes 2359300
  1941.9 141.4 %reduce-scatter.21.cloned.1.call-start = ((), (), s32[]{:S(2)}) async-start(), calls=%async_computation.18 | async-start | bytes 1179648
  1947.0 234.7 %reduce-scatter.13.cloned.1.call-start = ((), (), s32[]{:S(2)}) async-start(), calls=%async_computation.14 | async-start | bytes 5308416 | tf_op jit(solution)/shard_map/reduce_scatter | solution.py:307
  1952.5 351.1 %reduce-scatter.11.cloned.1.call-start = ((), (), s32[]{:S(2)}) async-start(), calls=%async_computation.13 | async-start | bytes 7077888 | tf_op jit(solution)/shard_map/reduce_scatter | solution.py:301
  1954.3 130.1 %copy-start.15 = (bf16[256,1536]{1,0:T(8,128)(2,1)S(1)}, bf16[256,1536]{1,0:T(8,128)(2,1)}, u32[]{:S(2)}) copy-start(bf16[256,1536]{1,0:T(8,128)(2,1)} %copy-done.14) | copy-start | bytes 2359300
  2089.0 654.7 %reduce-scatter.17.cloned.1.call-start = ((), (), s32[]{:S(2)}) async-start(), calls=%async_computation.16 | async-start | bytes 30965760 | tf_op jit(solution)/shard_map/reduce_scatter | solution.py:297
  2105.6 1500.0 %reduce-scatter.15.cloned.1.call-start = ((), (), s32[]{:S(2)}) async-start(), calls=%async_computation.15 | async-start | bytes 61931520 | tf_op jit(solution)/shard_map/reduce_scatter | solution.py:294
  2131.8 1683.6 %all-reduce.4.cloned.1.call-start = ((), (), s32[]{:S(2)}) async-start(), calls=%async_computation.19 | async-start | bytes 23396352 | tf_op jit(solution)/shard_map/psum | solution.py:315
  3623.7 48.3 %copy-start.38 = (f32[2,128]{1,0:T(2,128)S(1)}, f32[2,128]{1,0:T(2,128)}, u32[]{:S(2)}) copy-start(f32[2,128]{1,0:T(2,128)} %copy-done.37) | copy-start | bytes 3076
  3623.7 48.3 %copy-start.1 = (f32[256,1536]{1,0:T(8,128)S(1)}, f32[256,1536]{1,0:T(8,128)}, u32[]{:S(2)}) copy-start(f32[256,1536]{1,0:T(8,128)} %copy-done) | copy-start | bytes 4718596
  (40 other events, 378.4 us)
Sparse Core Ops, SparseCore 0:
  10.8 101.8 all-gather.8
  121.5 38.3 all-gather.10
  162.6 38.2 all-gather.12
  203.5 78.7 all-gather.14
  284.3 522.8 all-gather.16
  809.1 524.6 all-gather.18
  1335.9 524.6 all-gather.20
  1942.0 74.3 reduce-scatter.18
  2020.8 62.4 reduce-scatter.20
  2087.3 94.2 reduce-scatter.12
  2185.8 117.6 reduce-scatter.10
  2307.3 436.3 reduce-scatter.16
  2748.0 857.5 reduce-scatter.14
  3608.3 207.0 all-reduce.3
where the time goes:
time: 3940 us; the launch traced here: 3930 us
  waiting for transfers between devices  3440 us (87%)
  matrix products  180 us (5%)
  other arithmetic  123 us (3%)
  blocking collectives  114 us (3%)
  local copies, waits for them, and re-layouts  49.7 us (1%)
    reduce_scatter x1, waiting for transfers between devices, on_device(): lax.psum_scatter(left_product(h_two, d_gate_up).astype(jnp.bfloat16), 'bl...  862 us
    all_gather x1, waiting for transfers between devices, on_device(): lax.all_gather(w_gate.astype(jnp.bfloat16), 'blk', axis=0, tiled=True)  520 us
    all_gather x1, waiting for transfers between devices, on_device(): lax.all_gather(w_up.astype(jnp.bfloat16), 'blk', axis=0, tiled=True)  512 us
    all_gather x1, waiting for transfers between devices, on_device(): lax.all_gather(w_down.astype(jnp.bfloat16), 'blk', axis=0, tiled=True)  511 us
    reduce_scatter x1, waiting for transfers between devices, on_device(): lax.psum_scatter(left_product(hidden, dy_low).astype(jnp.bfloat16), 'blk'...  440 us
    psum x1, waiting for transfers between devices, on_device(): lax.psum(share_attend.astype(jnp.bfloat16), 'grp').astype(jnp.float32)  141 us
    unnamed x16, waiting for transfers between devices  126 us
    reduce_scatter x1, waiting for transfers between devices, on_device(): lax.psum_scatter(left_product(h_one, d_mixed).astype(jnp.bfloat16), 'blk'...  122 us
  transfers between devices with their start and end apart: 14, of which 13 were waited for; matrix products, arithmetic and copies ran while one was open for 4% of the time, Pallas kernels for 0%

commit v1 on v0

v1 whole, which is shorter than its diff:
```python
import jax
import jax.numpy as jnp
from jax import lax
from jax.sharding import PartitionSpec as P

D = 1536
FF = 8960
H = 12
KVH = 2
HD = 128
STEP = 10
HQD = 1536
KVD = 256


NORM_EPS = 1e-06
ROPE_BASE = 10000.0
CLIP_NORM = 1.0
BETA_FIRST = 0.9
BETA_SECOND = 0.95
ADAM_EPS = 1e-08
WEIGHT_DECAY = 0.1
RATE_ATTEND = 0.06
RATE_OUT = 0.5
RATE_GATE = 0.06
RATE_DOWN = 0.03
RATE_VECTOR = 0.5
NEG_LARGE = -1e30


def norm_apply(values, gain):
    return values * lax.rsqrt(jnp.mean(values * values, axis=-1, keepdims=True) + NORM_EPS) * gain


def rotate(values, position):
    half = values.shape[-1] // 2
    freqs = ROPE_BASE ** (-2.0 * jnp.arange(half, dtype=jnp.float32) / values.shape[-1])
    angles = position.astype(jnp.float32)[:, None] * freqs[None, :]
    cosine = jnp.cos(angles)[:, None, :]
    sine = jnp.sin(angles)[:, None, :]
    first_half = values[..., :half]
    second_half = values[..., half:]
    return jnp.concatenate(
        [first_half * cosine - second_half * sine, second_half * cosine + first_half * sine],
        axis=-1,
    )


def swish_product(gate, up_proj):
    return jax.nn.silu(gate) * up_proj


def left_product(left_side, right_side):
    return lax.dot_general(
        left_side, right_side, (((0,), (0,)), ((), ())), preferred_element_type=jnp.float32
    )


def right_transposed(left_side, right_side):
    return lax.dot_general(
        left_side, right_side, (((1,), (1,)), ((), ())), preferred_element_type=jnp.float32
    )


def square_total(arrays):
    return sum((jnp.sum(member * member) for member in arrays))


def unchanged(state_in):
    return state_in


def adam_step(weight, grad, first, second, rate, decay):
    first_new = BETA_FIRST * first + (1.0 - BETA_FIRST) * grad
    second_new = BETA_SECOND * second + (1.0 - BETA_SECOND) * grad * grad
    first_hat = first_new / (1.0 - BETA_FIRST**STEP)
    second_hat = second_new / (1.0 - BETA_SECOND**STEP)
    weight_new = weight - rate * (first_hat / (jnp.sqrt(second_hat) + ADAM_EPS) + decay * weight)
    return (first_new, second_new, weight_new)


CORE = [(0, 1), (1, 0), (2, 3), (3, 2)]
CROSS = [(0, 2), (2, 0), (1, 3), (3, 1)]
DIAG = [(0, 3), (3, 0), (1, 2), (2, 1)]


def low(values):
    return values.astype(jnp.bfloat16)


def wide(values):
    return values.astype(jnp.float32)


def swap_core(values):
    return lax.ppermute(values, "grp", CORE)


def swap_cross(values):
    return lax.ppermute(values, "grp", CROSS)


def swap_diag(values):
    return lax.ppermute(values, "grp", DIAG)


def swap_blk(values, bit):
    count = lax.axis_size("blk")
    return lax.ppermute(values, "blk", [(i, i ^ bit) for i in range(count)])


def blk_bit(bit):
    return (lax.axis_index("blk") & bit) != 0


def bits_of(count):
    out = []
    bit = count // 2
    while bit >= 1:
        out.append(bit)
        bit //= 2
    return out


def gather_bits(values, order):
    done = []
    for bit in order:
        other = swap_blk(values, bit)
        mine = blk_bit(bit)
        axis = sum(1 for d in done if d > bit)
        values = jnp.stack(
            [jnp.where(mine, other, values), jnp.where(mine, values, other)], axis=axis
        )
        done.append(bit)
    return values


def scatter_bits(values, axes, order):
    axes = list(axes)
    for bit in order:
        axis = axes.index(bit)
        mine = blk_bit(bit).astype(jnp.int32)
        keep = lax.dynamic_index_in_dim(values, mine, axis, keepdims=False)
        send = lax.dynamic_index_in_dim(values, 1 - mine, axis, keepdims=False)
        values = low(wide(keep) + wide(swap_blk(send, bit)))
        axes.remove(bit)
    return values


def by_place(parts):
    grp = lax.axis_index("grp")
    core = (grp & 1) != 0
    cross = (grp & 2) != 0
    a, b, c, d = parts
    a, b = jnp.where(core, b, a), jnp.where(core, a, b)
    c, d = jnp.where(core, d, c), jnp.where(core, c, d)
    a, c = jnp.where(cross, c, a), jnp.where(cross, a, c)
    b, d = jnp.where(cross, d, b), jnp.where(cross, b, d)
    return [a, b, c, d]


def gather_near(values):
    cross = swap_cross(values)
    both = swap_core(jnp.stack([values, cross]))
    return [values, both[0], cross, both[1]]


def gather_grp(values):
    return by_place(gather_near(values))


def gather_tokens(values, bit):
    half = values.shape[0] // 2
    cross = swap_cross(values)
    over = swap_blk(values, bit)
    first = swap_blk(cross[:half], bit)
    second = swap_cross(over[half:])
    chip = jnp.concatenate([values, cross, over, first, second])
    return jnp.concatenate([chip, swap_core(chip)])


def scatter_tokens(values, bit):
    half_all = values.shape[0] // 2
    rows = half_all // 4
    half = rows // 2
    chip = wide(values[:half_all]) + wide(swap_core(low(values[half_all:])))
    own, cross, over, far = (chip[rows * i : rows * (i + 1)] for i in range(4))
    far = low(far)
    first = wide(swap_blk(far[:half], bit))
    second = wide(swap_cross(far[half:]))
    cross = low(jnp.concatenate([cross[:half] + first, cross[half:]]))
    over = low(jnp.concatenate([over[:half], over[half:] + second]))
    return own + wide(swap_cross(cross)) + wide(swap_blk(over, bit))


def angles_of(position):
    half = HD // 2
    freqs = ROPE_BASE ** (-2.0 * jnp.arange(half, dtype=jnp.float32) / HD)
    return position.astype(jnp.float32)[:, None] * freqs[None, :]


def rotate_by(values, cosine, sine):
    half = HD // 2
    first_half = values[..., :half]
    second_half = values[..., half:]
    return jnp.concatenate(
        [first_half * cosine - second_half * sine, second_half * cosine + first_half * sine],
        axis=-1,
    )


def on_device(
    tokens,
    cotangent,
    segment_ids,
    position_ids,
    w_attend,
    w_out,
    w_gate,
    w_up,
    w_down,
    small_params,
    first_attend,
    first_out,
    first_gate,
    first_up,
    first_down,
    first_small,
    second_attend,
    second_out,
    second_gate,
    second_up,
    second_down,
    second_small,
):
    rows_here, block_len = tokens.shape[:2]
    blk_count = lax.axis_size("blk")
    seq_len = block_len * blk_count
    token_count = rows_here * block_len
    head_group = H // KVH
    score_scale = HD ** (-0.5)
    grp = lax.axis_index("grp")
    blk = lax.axis_index("blk")
    cross_id, core_id = grp // 2, grp % 2
    strip_heads = H // 4
    strip_q = strip_heads * HD
    bits = bits_of(blk_count)
    team = blk_count // 4
    lows = [bit for bit in bits if bit < team]
    spread = [bits[0]] + lows
    low_shape = (2,) * len(lows)
    in_team = blk_bit(team).astype(jnp.int32)
    weight_rows = w_gate.shape[0]
    ff_block = w_down.shape[0]
    quarter = ff_block // 4
    ff_here = quarter * blk_count // 2

    flat_low = tokens.reshape(token_count, D)
    dy_low = cotangent.reshape(token_count, D)
    positions = position_ids.reshape(token_count)
    vector = wide(gather_bits(low(small_params), bits).reshape(-1))
    gain_one = vector[:D]
    gain_two = vector[D : 2 * D]
    bias = vector[2 * D :]
    kv_at = HQD + HD * cross_id + KVD * core_id
    strip_local = low(
        jnp.concatenate(
            [
                lax.dynamic_slice_in_dim(w_attend, strip_q * grp, strip_q, 1),
                lax.dynamic_slice_in_dim(w_attend, kv_at, HD, 1),
            ],
            axis=1,
        )
    )
    strip_bias = jnp.concatenate(
        [
            lax.dynamic_slice_in_dim(bias, strip_q * grp, strip_q, 0),
            lax.dynamic_slice_in_dim(bias, kv_at, HD, 0),
        ]
    )
    strip = gather_bits(strip_local, bits).reshape(D, strip_q + HD)
    near_tokens = jnp.concatenate(gather_near(flat_low))
    near_positions = jnp.concatenate(gather_near(positions))
    seg_all = gather_bits(segment_ids, bits).reshape((blk_count,) + segment_ids.shape)
    seg_all = seg_all.transpose(1, 0, 2).reshape(rows_here, seq_len)

    near_wide = wide(near_tokens)
    near_one = low(norm_apply(near_wide, gain_one))
    mixed = jnp.dot(near_one, strip, preferred_element_type=jnp.float32) + strip_bias
    angles = angles_of(near_positions)[:, None, :]
    turned = jnp.arange(strip_heads + 1)[None, :, None] < strip_heads + 1 - core_id
    angles = jnp.where(turned, angles, 0.0)
    strip_out = low(
        rotate_by(
            mixed.reshape(4 * token_count, strip_heads + 1, HD), jnp.cos(angles), jnp.sin(angles)
        )
    ).reshape(4, token_count, strip_q + HD)
    strips = by_place(
        [
            strip_out[0],
            swap_core(strip_out[1]),
            swap_cross(strip_out[2]),
            swap_diag(strip_out[3]),
        ]
    )
    query = jnp.concatenate([part[:, :strip_q] for part in strips], axis=1)
    key_value = jnp.concatenate([strips[k][:, strip_q:] for k in (0, 2, 1, 3)], axis=1)
    key_value = key_value.reshape(rows_here, block_len, 2 * KVD)
    query_heads = query.reshape(rows_here, block_len, KVH, head_group, HD).transpose(0, 2, 3, 1, 4)
    kv_all = gather_bits(key_value, bits).reshape((blk_count,) + key_value.shape)
    kv_all = kv_all.transpose(1, 0, 2, 3).reshape(rows_here, seq_len, 2, KVH, HD)
    keys_here = kv_all[:, :, 0]
    values_here = kv_all[:, :, 1]

    query_index = blk * block_len + jnp.arange(block_len, dtype=jnp.int32)
    key_index = jnp.arange(seq_len, dtype=jnp.int32)
    causal = key_index[None, :] <= query_index[:, None]
    same_doc = seg_all[:, None, :] == segment_ids[:, :, None]
    allowed = jnp.logical_and(causal[None, :, :], same_doc)[:, None, None, :, :]

    scores = (
        jnp.einsum("rkgqd,rnkd->rkgqn", query_heads, keys_here, preferred_element_type=jnp.float32)
        * score_scale
    )
    scores = jnp.where(allowed, scores, NEG_LARGE)
    row_max = jnp.max(scores, axis=-1)
    weights = jnp.exp(scores - row_max[..., None])
    row_sum = jnp.sum(weights, axis=-1)
    row_out = jnp.einsum(
        "rkgqn,rnkd->rkgqd", low(weights), values_here, preferred_element_type=jnp.float32
    )
    attended_heads = row_out / row_sum[..., None]
    log_total = row_max + jnp.log(row_sum)
    att_in = low(attended_heads.transpose(0, 3, 1, 2, 4).reshape(token_count, HQD))

    out_local = low(lax.dynamic_slice_in_dim(w_out, strip_q * grp, strip_q, 1))
    out_strip = gather_bits(out_local, bits).reshape(HQD, strip_q)
    out_full = jnp.concatenate(gather_grp(out_strip), axis=1)

    def columns(weight):
        parts = low(weight).reshape(weight_rows, 2, 2, blk_count // 4, 4, quarter)
        parts = lax.dynamic_index_in_dim(parts, grp, 4, keepdims=False)
        keep = lax.dynamic_index_in_dim(parts, in_team, 2, keepdims=False)
        send = lax.dynamic_index_in_dim(parts, 1 - in_team, 2, keepdims=False)
        keep = keep.reshape(weight_rows, ff_here)
        got = swap_blk(send.reshape(weight_rows, ff_here), team)
        mine = blk_bit(team)
        pair = jnp.stack([jnp.where(mine, got, keep), jnp.where(mine, keep, got)])
        done = [team]
        for bit in spread:
            other = swap_blk(pair, bit)
            mine = blk_bit(bit)
            axis = sum(1 for d in done if d > bit)
            pair = jnp.stack(
                [jnp.where(mine, other, pair), jnp.where(mine, pair, other)], axis=axis
            )
            done.append(bit)
        return pair.reshape(D, ff_here)

    gate_here = columns(w_gate)
    up_here = columns(w_up)
    down_local = low(lax.dynamic_slice_in_dim(w_down, quarter * grp, quarter, 0))
    down_here = gather_bits(down_local, spread).reshape(ff_here, D)
    dy_team = gather_tokens(dy_low, team)

    flat = wide(flat_low)
    resid = flat + jnp.dot(att_in, out_full, preferred_element_type=jnp.float32)
    h_two = low(norm_apply(resid, gain_two))
    h_team = gather_tokens(h_two, team)
    gate = jnp.dot(h_team, gate_here, preferred_element_type=jnp.float32)
    up_proj = jnp.dot(h_team, up_here, preferred_element_type=jnp.float32)
    hidden = low(swish_product(gate, up_proj))
    share_down = scatter_bits(
        low(left_product(hidden, dy_team)).reshape((2,) + low_shape + (quarter, D)),
        spread,
        lows[::-1] + [bits[0]],
    )
    d_hidden = right_transposed(dy_team, down_here)
    swish_value, swish_back = jax.vjp(swish_product, gate, up_proj)
    d_gate, d_up = swish_back(d_hidden)
    d_gate = low(d_gate)
    d_up = low(d_up)
    d_htwo = scatter_tokens(
        right_transposed(d_gate, gate_here) + right_transposed(d_up, up_here), team
    )
    out_tokens = low(
        resid
        + scatter_tokens(jnp.dot(hidden, down_here, preferred_element_type=jnp.float32), team)
    )

    def share_columns(grad):
        grad = grad.reshape((2, 2) + low_shape + (weight_rows, ff_here))
        grad = scatter_bits(grad, bits, lows[::-1] + [bits[0]])
        keep = lax.dynamic_index_in_dim(grad, in_team, 0, keepdims=False)
        send = lax.dynamic_index_in_dim(grad, 1 - in_team, 0, keepdims=False)
        got = swap_blk(send, team)
        mine = blk_bit(team)
        return jnp.stack([jnp.where(mine, got, keep), jnp.where(mine, keep, got)])

    share_gate = share_columns(low(left_product(h_team, d_gate)))
    share_up = share_columns(low(left_product(h_team, d_up)))

    norm_value_two, norm_back_two = jax.vjp(norm_apply, resid, gain_two)
    d_resid_norm, grad_gain_two = norm_back_two(d_htwo)
    d_resid = wide(dy_low) + d_resid_norm
    d_att = low(d_resid)

    d_attended = low(right_transposed(d_att, out_full))
    grad_heads = d_attended.reshape(rows_here, block_len, KVH, head_group, HD).transpose(
        0, 2, 3, 1, 4
    )
    row_delta = jnp.sum(wide(grad_heads) * attended_heads, axis=-1)
    scores = (
        jnp.einsum("rkgqd,rnkd->rkgqn", query_heads, keys_here, preferred_element_type=jnp.float32)
        * score_scale
    )
    probs = jnp.where(allowed, jnp.exp(scores - log_total[..., None]), 0.0)
    dprob = jnp.einsum(
        "rkgqd,rnkd->rkgqn", grad_heads, values_here, preferred_element_type=jnp.float32
    )
    dscore = low(probs * (dprob - row_delta[..., None]))
    dq_sum = jnp.einsum(
        "rkgqn,rnkd->rkgqd", dscore, keys_here, preferred_element_type=jnp.float32
    )
    dk_all = jnp.einsum(
        "rkgqn,rkgqd->rnkd", dscore, query_heads, preferred_element_type=jnp.float32
    )
    dv_all = jnp.einsum(
        "rkgqn,rkgqd->rnkd", low(probs), grad_heads, preferred_element_type=jnp.float32
    )
    dkv = low(jnp.stack([dk_all * score_scale, dv_all], axis=2))
    dkv = dkv.reshape(rows_here, blk_count, block_len, 2 * KVD).transpose(1, 0, 2, 3)
    dkv = dkv.reshape((2,) * len(bits) + (rows_here, block_len, 2 * KVD))
    dkv = wide(scatter_bits(dkv, bits, bits[::-1])).reshape(token_count, 2, KVH, HD)
    own_angles = angles_of(positions)[:, None, :]
    cosine, sine = jnp.cos(own_angles), -jnp.sin(own_angles)
    dq_tokens = (dq_sum * score_scale).transpose(0, 3, 1, 2, 4).reshape(token_count, H, HD)
    d_query = low(rotate_by(dq_tokens, cosine, sine)).reshape(token_count, HQD)
    d_key = low(rotate_by(dkv[:, 0], cosine, sine))
    d_value = low(dkv[:, 1])
    d_mixed = jnp.concatenate(
        [d_query, d_key.reshape(token_count, KVD), d_value.reshape(token_count, KVD)], axis=1
    )
    grad_bias = jnp.sum(wide(d_mixed), axis=0)
    parts = by_place(
        [
            jnp.concatenate(
                [
                    d_query[:, strip_q * k : strip_q * (k + 1)],
                    (d_value if k % 2 else d_key)[:, k // 2],
                ],
                axis=1,
            )
            for k in range(4)
        ]
    )
    near_d = jnp.concatenate(
        [parts[0], swap_core(parts[1]), swap_cross(parts[2]), swap_diag(parts[3])]
    )
    share_attend = scatter_bits(
        low(left_product(near_one, near_d)).reshape((2,) * len(bits) + (weight_rows, -1)),
        bits,
        bits[::-1],
    )
    near_hone = right_transposed(near_d, strip)
    near_rms = lax.rsqrt(jnp.mean(near_wide * near_wide, axis=-1, keepdims=True) + NORM_EPS)
    gain_one_part = jnp.sum(near_hone * near_wide * near_rms, axis=0)
    half = low(near_hone[token_count : 2 * token_count]), low(near_hone[3 * token_count :])
    other = wide(swap_core(jnp.concatenate(half)))
    d_hone = near_hone[:token_count] + other[:token_count]
    d_hone = d_hone + wide(
        swap_cross(low(near_hone[2 * token_count : 3 * token_count] + other[token_count:]))
    )
    norm_value_one, norm_back_one = jax.vjp(norm_apply, flat, gain_one)
    d_flat_norm, unused_gain = norm_back_one(d_hone)
    grad_tokens = low(d_resid + d_flat_norm)

    near_att = jnp.concatenate(gather_near(att_in))
    d_parts = by_place([d_att[:, strip_q * k : strip_q * (k + 1)] for k in range(4)])
    near_datt = jnp.concatenate(
        [d_parts[0], swap_core(d_parts[1]), swap_cross(d_parts[2]), swap_diag(d_parts[3])]
    )
    share_out = scatter_bits(
        low(left_product(near_att, near_datt)).reshape((2,) * len(bits) + (weight_rows, -1)),
        bits,
        bits[::-1],
    )

    vector_term = jnp.concatenate([gain_one_part, grad_gain_two, grad_bias])
    vector_term = vector_term + swap_cross(vector_term)
    vector_term = vector_term + swap_core(vector_term)
    vector_term = vector_term.reshape((2,) * len(bits) + (-1,))
    axes = list(bits)
    for bit in bits[::-1]:
        axis = axes.index(bit)
        mine = blk_bit(bit).astype(jnp.int32)
        keep = lax.dynamic_index_in_dim(vector_term, mine, axis, keepdims=False)
        send = lax.dynamic_index_in_dim(vector_term, 1 - mine, axis, keepdims=False)
        vector_term = keep + swap_blk(send, bit)
        axes.remove(bit)
    share_vector = vector_term

    square_sum = square_total(
        [wide(s) for s in (share_attend, share_out, share_gate, share_up, share_down)]
    ) + 0.25 * jnp.sum(share_vector * share_vector)
    square_sum = jnp.full((8, 128), square_sum)
    for bit in bits:
        square_sum = square_sum + swap_blk(square_sum, bit)
    square_sum = square_sum + swap_cross(square_sum)
    square_sum = square_sum + swap_core(square_sum)
    grad_norm = jnp.sqrt(square_sum[0, 0])
    factor = jnp.minimum(1.0, CLIP_NORM / (grad_norm + 1e-06))

    attend_parts = gather_grp(share_attend)
    grad_attend = jnp.concatenate(
        [part[:, :strip_q] for part in attend_parts]
        + [attend_parts[k][:, strip_q:] for k in (0, 2, 1, 3)],
        axis=1,
    )
    grad_out = jnp.concatenate(gather_grp(share_out), axis=1)
    grad_down = jnp.concatenate(gather_grp(share_down), axis=0)

    def whole_columns(share):
        parts = jnp.stack(gather_grp(share))
        parts = parts.reshape(4, 2, weight_rows, 2, blk_count // 4, quarter)
        return parts.transpose(2, 3, 1, 4, 0, 5).reshape(weight_rows, FF)

    grad_gate = whole_columns(share_gate)
    grad_up = whole_columns(share_up)

    new_first_attend, new_second_attend, new_attend = adam_step(
        w_attend, factor * wide(grad_attend), first_attend, second_attend, RATE_ATTEND, WEIGHT_DECAY
    )
    new_first_out, new_second_out, new_out = adam_step(
        w_out, factor * wide(grad_out), first_out, second_out, RATE_OUT, WEIGHT_DECAY
    )
    new_first_gate, new_second_gate, new_gate = adam_step(
        w_gate, factor * wide(grad_gate), first_gate, second_gate, RATE_GATE, WEIGHT_DECAY
    )
    new_first_up, new_second_up, new_up = adam_step(
        w_up, factor * wide(grad_up), first_up, second_up, RATE_GATE, WEIGHT_DECAY
    )
    new_first_down, new_second_down, new_down = adam_step(
        w_down, factor * wide(grad_down), first_down, second_down, RATE_DOWN, WEIGHT_DECAY
    )
    new_first_small, new_second_small, new_small = adam_step(
        small_params, factor * share_vector, first_small, second_small, RATE_VECTOR, 0.0
    )
    return (
        out_tokens.reshape(rows_here, block_len, D),
        grad_tokens.reshape(rows_here, block_len, D),
        grad_norm,
        new_first_attend,
        new_second_attend,
        new_attend,
        new_first_out,
        new_second_out,
        new_out,
        new_first_gate,
        new_second_gate,
        new_gate,
        new_first_up,
        new_second_up,
        new_up,
        new_first_down,
        new_second_down,
        new_down,
        new_first_small,
        new_second_small,
        new_small,
    )


def solution(mesh):
    placed = (
        P("grp", "blk", None),
        P("grp", "blk", None),
        P("grp", "blk"),
        P("grp", "blk"),
        P("blk", None),
        P("blk", None),
        P("blk", None),
        P("blk", None),
        P("blk", None),
        P("blk"),
        P("blk", None),
        P("blk", None),
        P("blk", None),
        P("blk", None),
        P("blk", None),
        P("blk"),
        P("blk", None),
        P("blk", None),
        P("blk", None),
        P("blk", None),
        P("blk", None),
        P("blk"),
    )
    return jax.shard_map(
        on_device,
        mesh=mesh,
        in_specs=placed,
        out_specs=(
            P("grp", "blk", None),
            P("grp", "blk", None),
            P(),
            P("blk", None),
            P("blk", None),
            P("blk", None),
            P("blk", None),
            P("blk", None),
            P("blk", None),
            P("blk", None),
            P("blk", None),
            P("blk", None),
            P("blk", None),
            P("blk", None),
            P("blk", None),
            P("blk", None),
            P("blk", None),
            P("blk", None),
            P("blk"),
            P("blk"),
            P("blk"),
        ),
        check_vma=False,
    )
```

time: 3940 us -> 1150 us (0.29)
  waiting for transfers between devices: 3440 us -> 441 us
  local copies, waits for them, and re-layouts: 49.7 us -> 242 us
  blocking collectives: 114 us -> 0 us
  other arithmetic: 123 us -> 221 us
  starting transfers between devices: 1.16 us -> 75.3 us
    all_gather x7 -> x0, waiting for transfers between devices: 1700 us -> none  [the longest x1 520 us: on_device(): lax.all_gather(w_gate.astype(jnp.bfloat16), 'blk', axis=0, tiled=True)]
    reduce_scatter x4 -> x0, waiting for transfers between devices: 1470 us -> none  [the longest x1 862 us: on_device(): lax.psum_scatter(left_product(h_two, d_gate_up).astype(jnp.bfloat16), 'bl...]
    ppermute x0 -> x99, waiting for transfers between devices: none -> 441 us  [the longest x54 362 us: swap_blk(): return lax.ppermute(values, 'blk', [(i, i ^ bit) for i in range(count)])]
    psum x1 -> x0, waiting for transfers between devices: 141 us -> none  [on_device(): lax.psum(share_attend.astype(jnp.bfloat16), 'grp').astype(jnp.float32)]
    unnamed x16 -> x0, waiting for transfers between devices: 126 us -> none
    ppermute x0 -> x99, starting transfers between devices: none -> 75.3 us  [the longest x54 46.7 us: swap_blk(): return lax.ppermute(values, 'blk', [(i, i ^ bit) for i in range(count)])]
    another operation x5 -> x63, other arithmetic: 2.76 us -> 58.3 us  [the longest x11 16.3 us: gather_near(): both = swap_core(jnp.stack([values, cross]))]
    all_gather x2 -> x0, blocking collectives: 50.2 us -> none  [the longest x1 32.5 us: on_device(): lax.all_gather(small_params.astype(jnp.bfloat16), 'blk', axis=0, tiled=True)]
  transfers between devices with their start and end apart: 14 -> 99, of which waited for: 13 -> 48; matrix products, arithmetic and copies ran while one was open for 4% -> 46% of each run, Pallas kernels for 0% -> 0%
where the time goes in v1:
time: 1150 us
  waiting for transfers between devices  441 us (38%)
  local copies, waits for them, and re-layouts  242 us (21%)
  other arithmetic  221 us (19%)
  matrix products  158 us (14%)
  starting transfers between devices  75.3 us (7%)
    ppermute x54, waiting for transfers between devices, swap_blk(): return lax.ppermute(values, 'blk', [(i, i ^ bit) for i in range(count)])  362 us
    ppermute x23, waiting for transfers between devices, swap_cross(): return lax.ppermute(values, 'grp', CROSS)  63 us
    sub x6, other arithmetic, adam_step(): weight - rate * (first_hat / (jnp.sqrt(second_hat) + ADAM_EPS) + decay *...  59 us
    dot_general x5, matrix products, right_transposed(): lax.dot_general(left_side, right_side, (((1,), (1,)), ((), ())), preferre...  54.4 us
    ppermute x54, starting transfers between devices, swap_blk(): return lax.ppermute(values, 'blk', [(i, i ^ bit) for i in range(count)])  46.7 us
    dot_general x5, matrix products, left_product(): lax.dot_general(left_side, right_side, (((0,), (0,)), ((), ())), preferre...  36.8 us
    unnamed x312, local copies, waits for them, and re-layouts  33.9 us
    another operation x8, local copies, waits for them, and re-layouts, whole_columns(): parts = jnp.stack(gather_grp(share))  29.9 us
  transfers between devices with their start and end apart: 99, of which 48 were waited for; matrix products, arithmetic and copies ran while one was open for 46% of the time, Pallas kernels for 0%

profile of v1, /device:TPU:0, one launch (start us, length us, event | category | flops | bytes accessed | tf_op | source)
XLA Modules:
  0.0 1146.2 jit_solution(5174378038956872631)
XLA Ops:
  115.9 15.9 %collective-permute-done.32 = bf16[192,1120]{1,0:T(8,128)(2,1)S(1)} collective-permute-done((bf16[192,1120]{1,0:T(8,128)(2,1)}, bf16[192,1120]{1,0:T(8,128)(2,1)S(1)}, u32[]{:S(2)}, u32[]{:S(2)}) %collective-permute-start.32) | collective-permute-done | bytes 430112 | tf_op jit(solution)/shard_map/ppermute | solution.py:109
  156.6 52.2 %collective-permute-done.35 = bf16[280,1536]{1,0:T(8,128)(2,1)S(1)} collective-permute-done((bf16[280,1536]{1,0:T(8,128)(2,1)S(1)}, bf16[280,1536]{1,0:T(8,128)(2,1)S(1)}, u32[]{:S(2)}, u32[]{:S(2)}) %collective-permute-start.35) | collective-permute-done | bytes 860192 | tf_op jit(solution)/shard_map/ppermute | solution.py:109
  273.2 11.9 %collective-permute-done.17 = bf16[2,2,128,512]{3,2,1,0:T(8,128)(2,1)S(1)} collective-permute-done((bf16[2,2,128,512]{3,2,1,0:T(8,128)(2,1)S(1)}, bf16[2,2,128,512]{3,2,1,0:T(8,128)(2,1)S(1)}, u32[]{:S(2)}, u32[]{:S(2)}) %collective-permute-start.17) | collective-permute-done | bytes 524320 | tf_op jit(solution)/shard_map/ppermute | solution.py:109
  301.4 12.1 %collective-permute-done.18 = bf16[2,2,2,128,512]{4,3,2,1,0:T(8,128)(2,1)} collective-permute-done((bf16[2,2,2,128,512]{4,3,2,1,0:T(8,128)(2,1)}, bf16[2,2,2,128,512]{4,3,2,1,0:T(8,128)(2,1)}, u32[]{:S(2)}, u32[]{:S(2)}) %collective-permute-start.18) | collective-permute-done | bytes 1048608 | tf_op jit(solution)/shard_map/ppermute | solution.py:109
  354.2 13.3 %collective-permute-done.25 = bf16[256,1536]{1,0:T(8,128)(2,1)S(1)} collective-permute-done((bf16[256,1536]{1,0:T(8,128)(2,1)S(1)}, bf16[256,1536]{1,0:T(8,128)(2,1)S(1)}, u32[]{:S(2)}, u32[]{:S(2)}) %collective-permute-start.25) | collective-permute-done | bytes 786464 | tf_op jit(solution)/shard_map/ppermute | solution.py:109
  432.0 18.3 %multiply_convert_fusion.1 = (bf16[2048,1120]{0,1:T(8,128)(2,1)}, bf16[2048,1120]{0,1:T(8,128)(2,1)}, bf16[2048,1120]{0,1:T(8,128)(2,1)}) fusion(f32[2048,1120]{0,1:T(8,128)} %fusion.142, f32[2048,1120]{0,1:T(8,128)} %fusion.143, bf16[2048,1536]{1,0:T(8,128)(2,1)} %copy-done.112, bf16[1120,1536]{1,0:T(8,128)(2,1)S(1)} %bitcast.650), kind=kOutput, calls=%fused_computation.19 | convolution fusion | flops 7083130880 | bytes 41844736 | tf_op jit(solution)/shard_map/dot_general | solution.py:60
  450.3 12.0 %convolution_convert_fusion.1 = bf16[1536,1120]{0,1:T(8,128)(2,1)S(1)} fusion(bf16[2048,1120]{0,1:T(8,128)(2,1)} %get-tuple-element.64, bf16[2048,1536]{1,0:T(8,128)(2,1)} %copy-done.111), kind=kOutput, calls=%fused_computation.25 | convolution fusion | flops 7048151040 | bytes 14319616 | tf_op jit(solution)/shard_map/dot_general | solution.py:54
  462.3 11.3 fusion.145
  509.0 15.4 %convolution_add_fusion = f32[2048,1536]{1,0:T(8,128)} fusion(f32[2048,1536]{1,0:T(8,128)} %fusion.145, bf16[2048,1120]{0,1:T(8,128)(2,1)} %get-tuple-element.63, bf16[1536,1120]{1,0:T(8,128)(2,1)S(1)} %bitcast.646), kind=kOutput, calls=%fused_computation.23 | convolution fusion | flops 7049576448 | bytes 33193984 | tf_op jit(solution)/shard_map/dot_general | solution.py:60
  549.5 15.3 %collective-permute-done.71 = bf16[2,2,192,1120]{3,2,1,0:T(8,128)(2,1)} collective-permute-done((bf16[2,2,192,1120]{3,2,1,0:T(8,128)(2,1)S(1)}, bf16[2,2,192,1120]{3,2,1,0:T(8,128)(2,1)}, u32[]{:S(2)}, u32[]{:S(2)}) %collective-permute-start.71) | collective-permute-done | bytes 1720352 | tf_op jit(solution)/shard_map/ppermute | solution.py:109
  566.9 35.4 %collective-permute-done.74 = bf16[2,2,192,1120]{3,2,1,0:T(8,128)(2,1)} collective-permute-done((bf16[2,2,192,1120]{3,2,1,0:T(8,128)(2,1)}, bf16[2,2,192,1120]{3,2,1,0:T(8,128)(2,1)}, u32[]{:S(2)}, u32[]{:S(2)}) %collective-permute-start.74) | collective-permute-done | bytes 1720352 | tf_op jit(solution)/shard_map/ppermute | solution.py:109
  604.4 22.7 %collective-permute-done.78 = bf16[280,1536]{1,0:T(8,128)(2,1)S(1)} collective-permute-done((bf16[280,1536]{1,0:T(8,128)(2,1)S(1)}, bf16[280,1536]{1,0:T(8,128)(2,1)S(1)}, u32[]{:S(2)}, u32[]{:S(2)}) %collective-permute-start.78) | collective-permute-done | bytes 860192 | tf_op jit(solution)/shard_map/ppermute | solution.py:109
  629.5 16.5 %collective-permute-done.72 = bf16[2,192,1120]{2,1,0:T(8,128)(2,1)S(1)} collective-permute-done((bf16[2,192,1120]{2,1,0:T(8,128)(2,1)S(1)}, bf16[2,192,1120]{2,1,0:T(8,128)(2,1)S(1)}, u32[]{:S(2)}, u32[]{:S(2)}) %collective-permute-start.72) | collective-permute-done | bytes 860192 | tf_op jit(solution)/shard_map/ppermute | solution.py:109
  646.4 18.6 %collective-permute-done.75 = bf16[2,192,1120]{2,1,0:T(8,128)(2,1)S(1)} collective-permute-done((bf16[2,192,1120]{2,1,0:T(8,128)(2,1)S(1)}, bf16[2,192,1120]{2,1,0:T(8,128)(2,1)S(1)}, u32[]{:S(2)}, u32[]{:S(2)}) %collective-permute-start.75) | collective-permute-done | bytes 860192 | tf_op jit(solution)/shard_map/ppermute | solution.py:109
  707.8 18.2 %collective-permute-done.50 = bf16[128,1536]{1,0:T(8,128)(2,1)} collective-permute-done((bf16[128,1536]{1,0:T(8,128)(2,1)}, bf16[128,1536]{1,0:T(8,128)(2,1)}, u32[]{:S(2)}, u32[]{:S(2)}) %collective-permute-start.50) | collective-permute-done | bytes 393248 | tf_op jit(solution)/shard_map/ppermute | solution.py:100
  989.7 12.1 %multiply_bitcast_fusion = f32[192,2,2,2,4,280]{5,3,1,0,2,4:T(2,128)} fusion(bf16[1,2,192,2,2,280]{5,4,3,2,1,0:T(2,128)(2,1)} %stack.443, bf16[1,2,192,2,2,280]{5,4,3,2,1,0:T(2,128)(2,1)} %stack.442, bf16[1,2,192,2,2,280]{5,4,3,2,1,0:T(2,128)(2,1)} %stack.441, bf16[1,2,192,2,2,280]{5,4,3,2,1,0:T(2,128)(2,1)} %stack.440, f32[]{:T(128)S(6)} %min.3), kind=kLoop, calls=%fused_computation.14 | loop fusion | flops 8601600 | bytes 10321924 | tf_op jit(solution)/shard_map/mul | solution.py:541
  1001.8 13.3 %copy.168 = f32[192,2,2,2,4,280]{5,4,3,2,1,0:T(4,128)} copy(f32[192,2,2,2,4,280]{5,3,1,0,2,4:T(2,128)} %multiply_bitcast_fusion) | data formatting | bytes 13762560 | tf_op jit(solution)/shard_map/mul | solution.py:541
  1026.4 12.1 %multiply_bitcast_fusion.1 = f32[192,2,2,2,4,280]{5,3,1,0,2,4:T(2,128)} fusion(bf16[1,2,192,2,2,280]{5,4,3,2,1,0:T(2,128)(2,1)} %stack.435, bf16[1,2,192,2,2,280]{5,4,3,2,1,0:T(2,128)(2,1)} %stack.434, bf16[1,2,192,2,2,280]{5,4,3,2,1,0:T(2,128)(2,1)S(1)} %stack.433, bf16[1,2,192,2,2,280]{5,4,3,2,1,0:T(2,128)(2,1)S(1)} %stack.432, f32[]{:T(128)S(6)} %min.3), kind=kLoop, calls=%fused_computation.15 | loop fusion | flops 8601600 | bytes 10321924 | tf_op jit(solution)/shard_map/mul | solution.py:538
  1038.5 13.3 %copy.167 = f32[192,2,2,2,4,280]{5,4,3,2,1,0:T(4,128)} copy(f32[192,2,2,2,4,280]{5,3,1,0,2,4:T(2,128)} %multiply_bitcast_fusion.1) | data formatting | bytes 13762560 | tf_op jit(solution)/shard_map/mul | solution.py:538
  1051.8 11.4 mul.655
  1063.2 18.4 %multiply_subtract_fusion.2 = (f32[192,8960]{1,0:T(8,128)}, f32[192,8960]{1,0:T(8,128)}, f32[192,8960]{1,0:T(8,128)}) fusion(f32[192,8960]{1,0:T(8,128)} %param.28, f32[192,8960]{1,0:T(8,128)} %mul.655, f32[192,8960]{1,0:T(8,128)} %param.40, f32[192,8960]{1,0:T(8,128)} %param.34), kind=kLoop, calls=%fused_computation.35 | loop fusion | flops 25804800 | bytes 48168960 | tf_op jit(solution)/shard_map/sub | solution.py:78
  1081.6 17.4 %multiply_subtract_fusion = (f32[1120,1536]{1,0:T(8,128)}, f32[1120,1536]{1,0:T(8,128)}, f32[1120,1536]{1,0:T(8,128)}) fusion(f32[1120,1536]{1,0:T(8,128)} %param.30, bf16[280,1536]{1,0:T(8,128)(2,1)} %get-tuple-element.91, bf16[280,1536]{1,0:T(8,128)(2,1)} %get-tuple-element.90, bf16[280,1536]{1,0:T(8,128)(2,1)} %get-tuple-element.89, ...), kind=kLoop, calls=%fused_computation.30 | loop fusion | flops 41287680 | bytes 44728324 | tf_op jit(solution)/shard_map/sub | solution.py:78
  1099.1 14.9 %multiply_subtract_fusion.1 = (f32[192,8960]{1,0:T(8,128)}, f32[192,8960]{1,0:T(8,128)}, f32[192,8960]{1,0:T(8,128)}) fusion(f32[192,8960]{1,0:T(8,128)S(1)} %bitcast.616, f32[192,8960]{1,0:T(8,128)} %mul.665, f32[192,8960]{1,0:T(8,128)} %param.41, f32[192,8960]{1,0:T(8,128)} %param.35), kind=kLoop, calls=%fused_computation.33 | loop fusion | flops 25804800 | bytes 48168960 | tf_op jit(solution)/shard_map/sub | solution.py:78
  1128.2 14.4 %collective-permute-done.59 = bf16[256,1536]{1,0:T(8,128)(2,1)S(1)} collective-permute-done((bf16[256,1536]{1,0:T(8,128)(2,1)S(1)}, bf16[256,1536]{1,0:T(8,128)(2,1)S(1)}, u32[]{:S(2)}, u32[]{:S(2)}) %collective-permute-start.59) | collective-permute-done | bytes 786464 | tf_op jit(solution)/shard_map/ppermute | solution.py:100
  (774 shorter events, 720.0 us)
Async XLA Ops:
  0.7 149.4 %collective-permute-start.43 = (bf16[256,1536]{1,0:T(8,128)(2,1)}, bf16[256,1536]{1,0:T(8,128)(2,1)}, u32[]{:S(2)}, u32[]{:S(2)}) collective-permute-start(bf16[256,1536]{1,0:T(8,128)(2,1)} %bitcast.654), channel_id=1, source_target_pairs={{0,2},{1,3},{2,0},{3,1},{4,6},{5,7},{6,4},{7,5},{8,10},{9,11},{10,... | collective-permute-start | bytes 2359304 | tf_op jit(solution)/shard_map/ppermute | solution.py:109
  3.7 142.1 %collective-permute-start.42 = (bf16[256,1536]{1,0:T(8,128)(2,1)}, bf16[256,1536]{1,0:T(8,128)(2,1)}, u32[]{:S(2)}, u32[]{:S(2)}) collective-permute-start(bf16[256,1536]{1,0:T(8,128)(2,1)} %bitcast.655), channel_id=1, source_target_pairs={{0,16},{16,0},{8,24},{24,8},{1,17},{17,1},{9,25},{25,9},{2,18},{18... | collective-permute-start | bytes 2359304 | tf_op jit(solution)/shard_map/ppermute | solution.py:100
  5.2 72.8 %collective-permute-start.11 = (s32[256]{0:T(256)}, s32[256]{0:T(256)S(1)}, u32[]{:S(2)}, u32[]{:S(2)}) collective-permute-start(s32[256]{0:T(256)} %bitcast.684), channel_id=1, source_target_pairs={{0,16},{16,0},{8,24},{24,8},{1,17},{17,1},{9,25},{25,9},{2,18},{18... | collective-permute-start | bytes 3080 | tf_op jit(solution)/shard_map/ppermute | solution.py:100
  5.8 74.9 %collective-permute-start = (s32[2,128]{1,0:T(2,128)}, s32[2,128]{1,0:T(2,128)S(1)}, u32[]{:S(2)}, u32[]{:S(2)}) collective-permute-start(s32[2,128]{1,0:T(2,128)} %param.24), channel_id=1, source_target_pairs={{0,4},{1,5},{2,6},{3,7},{4,0},{5,1},{6,2},{7,3},{8,12},{9,13},{10,... | collective-permute-start | bytes 3080 | tf_op jit(solution)/shard_map/ppermute | solution.py:109
  9.1 72.1 %collective-permute-start.5 = (bf16[640]{0:T(1024)(128)(2,1)S(1)}, bf16[640]{0:T(1024)(128)(2,1)S(1)}, u32[]{:S(2)}, u32[]{:S(2)}) collective-permute-start(bf16[640]{0:T(1024)(128)(2,1)S(1)} %convert_element_type.440), channel_id=1, source_target_pairs={{0,4},{1,5},{2,6},{3,7},{4,0},{5,1},{6,2},{7,3},{8,12},{9,13},{10,... | collective-permute-start | bytes 3848 | tf_op jit(solution)/shard_map/ppermute | solution.py:109
  141.4 129.4 %collective-permute-start.30 = (bf16[2,192,1120]{2,1,0:T(8,128)(2,1)}, bf16[2,192,1120]{2,1,0:T(8,128)(2,1)}, u32[]{:S(2)}, u32[]{:S(2)}) collective-permute-start(bf16[2,192,1120]{2,1,0:T(8,128)(2,1)} %pad_maximum_fusion.22), channel_id=1, source_target_pairs={{0,4},{1,5},{2,6},{3,7},{4,0},{5,1},{6,2},{7,3},{8,12},{9,13},{10,... | collective-permute-start | bytes 2580488 | tf_op jit(solution)/shard_map/ppermute | solution.py:109
  142.4 128.5 %collective-permute-start.33 = (bf16[2,192,1120]{2,1,0:T(8,128)(2,1)}, bf16[2,192,1120]{2,1,0:T(8,128)(2,1)}, u32[]{:S(2)}, u32[]{:S(2)}) collective-permute-start(bf16[2,192,1120]{2,1,0:T(8,128)(2,1)} %pad_maximum_fusion.23), channel_id=1, source_target_pairs={{0,4},{1,5},{2,6},{3,7},{4,0},{5,1},{6,2},{7,3},{8,12},{9,13},{10,... | collective-permute-start | bytes 2580488 | tf_op jit(solution)/shard_map/ppermute | solution.py:109
  145.9 75.2 %collective-permute-start.4 = (bf16[2,256,1536]{2,1,0:T(8,128)(2,1)S(1)}, bf16[2,256,1536]{2,1,0:T(8,128)(2,1)S(1)}, u32[]{:S(2)}, u32[]{:S(2)}) collective-permute-start(bf16[2,256,1536]{2,1,0:T(8,128)(2,1)S(1)} %pad_maximum_fusion.15), channel_id=1, source_target_pairs={{0,8},{8,0},{16,24},{24,16},{1,9},{9,1},{17,25},{25,17},{2,10},{10... | collective-permute-start | bytes 4718600 | tf_op jit(solution)/shard_map/ppermute | solution.py:96
  150.1 82.6 %collective-permute-start.21 = (bf16[2,2,192,384]{3,2,1,0:T(8,128)(2,1)S(1)}, bf16[2,2,192,384]{3,2,1,0:T(8,128)(2,1)S(1)}, u32[]{:S(2)}, u32[]{:S(2)}) collective-permute-start(bf16[2,2,192,384]{3,2,1,0:T(8,128)(2,1)S(1)} %pad_maximum_fusion.35), channel_id=1, source_target_pairs={{0,1},{1,0},{2,3},{3,2},{4,5},{5,4},{6,7},{7,6},{8,9},{9,8},{10,11... | collective-permute-start | bytes 1769480 | tf_op jit(solution)/shard_map/ppermute | solution.py:109
  244.5 103.3 %collective-permute-start.36 = (bf16[2,280,1536]{2,1,0:T(8,128)(2,1)}, bf16[2,280,1536]{2,1,0:T(8,128)(2,1)}, u32[]{:S(2)}, u32[]{:S(2)}) collective-permute-start(bf16[2,280,1536]{2,1,0:T(8,128)(2,1)} %pad_maximum_fusion.13), channel_id=1, source_target_pairs={{0,1},{1,0},{2,3},{3,2},{4,5},{5,4},{6,7},{7,6},{8,9},{9,8},{10,11... | collective-permute-start | bytes 5160968 | tf_op jit(solution)/shard_map/ppermute | solution.py:109
  270.6 132.2 %collective-permute-start.46 = (bf16[1024,1536]{1,0:T(8,128)(2,1)}, bf16[1024,1536]{1,0:T(8,128)(2,1)}, u32[]{:S(2)}, u32[]{:S(2)}) collective-permute-start(bf16[1024,1536]{1,0:T(8,128)(2,1)} %get-tuple-element.189), channel_id=1, source_target_pairs={{0,8},{8,0},{16,24},{24,16},{1,9},{9,1},{17,25},{25,17},{2,10},{10... | collective-permute-start | bytes 9437192 | tf_op jit(solution)/shard_map/ppermute | solution.py:96
  289.3 95.2 %collective-permute-start.31 = (bf16[2,2,192,1120]{3,2,1,0:T(8,128)(2,1)}, bf16[2,2,192,1120]{3,2,1,0:T(8,128)(2,1)}, u32[]{:S(2)}, u32[]{:S(2)}) collective-permute-start(bf16[2,2,192,1120]{3,2,1,0:T(8,128)(2,1)} %pad_maximum_fusion.9), channel_id=1, source_target_pairs={{0,1},{1,0},{2,3},{3,2},{4,5},{5,4},{6,7},{7,6},{8,9},{9,8},{10,11... | collective-permute-start | bytes 5160968 | tf_op jit(solution)/shard_map/ppermute | solution.py:109
  291.9 108.0 %collective-permute-start.34 = (bf16[2,2,192,1120]{3,2,1,0:T(8,128)(2,1)}, bf16[2,2,192,1120]{3,2,1,0:T(8,128)(2,1)}, u32[]{:S(2)}, u32[]{:S(2)}) collective-permute-start(bf16[2,2,192,1120]{3,2,1,0:T(8,128)(2,1)} %pad_maximum_fusion.10), channel_id=1, source_target_pairs={{0,1},{1,0},{2,3},{3,2},{4,5},{5,4},{6,7},{7,6},{8,9},{9,8},{10,11... | collective-permute-start | bytes 5160968 | tf_op jit(solution)/shard_map/ppermute | solution.py:109
  508.0 94.3 %collective-permute-start.74 = (bf16[2,2,192,1120]{3,2,1,0:T(8,128)(2,1)}, bf16[2,2,192,1120]{3,2,1,0:T(8,128)(2,1)}, u32[]{:S(2)}, u32[]{:S(2)}) collective-permute-start(bf16[2,2,192,1120]{3,2,1,0:T(8,128)(2,1)} %dynamic-slice_bitcast_fusion), channel_id=1, source_target_pairs={{0,1},{1,0},{2,3},{3,2},{4,5},{5,4},{6,7},{7,6},{8,9},{9,8},{10,11... | collective-permute-start | bytes 5160968 | tf_op jit(solution)/shard_map/ppermute | solution.py:109
  544.4 143.7 %collective-permute-start.47 = (bf16[1024,1536]{1,0:T(8,128)(2,1)}, bf16[1024,1536]{1,0:T(8,128)(2,1)}, u32[]{:S(2)}, u32[]{:S(2)}) collective-permute-start(bf16[1024,1536]{1,0:T(8,128)(2,1)} %slice.791), channel_id=1, source_target_pairs={{0,8},{8,0},{16,24},{24,16},{1,9},{9,1},{17,25},{25,17},{2,10},{10... | collective-permute-start | bytes 9437192 | tf_op jit(solution)/shard_map/ppermute | solution.py:96
  546.4 147.7 %collective-permute-start.37 = (bf16[1024,1536]{1,0:T(8,128)(2,1)}, bf16[1024,1536]{1,0:T(8,128)(2,1)S(1)}, u32[]{:S(2)}, u32[]{:S(2)}) collective-permute-start(bf16[1024,1536]{1,0:T(8,128)(2,1)} %slice.792), channel_id=1, source_target_pairs={{0,8},{8,0},{16,24},{24,16},{1,9},{9,1},{17,25},{25,17},{2,10},{10... | collective-permute-start | bytes 9437192 | tf_op jit(solution)/shard_map/ppermute | solution.py:96
  549.4 77.6 %collective-permute-start.78 = (bf16[280,1536]{1,0:T(8,128)(2,1)S(1)}, bf16[280,1536]{1,0:T(8,128)(2,1)S(1)}, u32[]{:S(2)}, u32[]{:S(2)}) collective-permute-start(bf16[280,1536]{1,0:T(8,128)(2,1)S(1)} %dynamic-slice_bitcast_fusion.6), channel_id=1, source_target_pairs={{0,4},{1,5},{2,6},{3,7},{4,0},{5,1},{6,2},{7,3},{8,12},{9,13},{10,... | collective-permute-start | bytes 2580488 | tf_op jit(solution)/shard_map/ppermute | solution.py:109
  566.8 79.2 %collective-permute-start.72 = (bf16[2,192,1120]{2,1,0:T(8,128)(2,1)S(1)}, bf16[2,192,1120]{2,1,0:T(8,128)(2,1)S(1)}, u32[]{:S(2)}, u32[]{:S(2)}) collective-permute-start(bf16[2,192,1120]{2,1,0:T(8,128)(2,1)S(1)} %dynamic-slice_bitcast_fusion.5), channel_id=1, source_target_pairs={{0,4},{1,5},{2,6},{3,7},{4,0},{5,1},{6,2},{7,3},{8,12},{9,13},{10,... | collective-permute-start | bytes 2580488 | tf_op jit(solution)/shard_map/ppermute | solution.py:109
  628.2 73.9 %collective-permute-start.97 = (bf16[280,1536]{1,0:T(8,128)(2,1)S(1)}, bf16[280,1536]{1,0:T(8,128)(2,1)}, u32[]{:S(2)}, u32[]{:S(2)}) collective-permute-start(bf16[280,1536]{1,0:T(8,128)(2,1)S(1)} %get-tuple-element.50), channel_id=1, source_target_pairs={{0,16},{16,0},{8,24},{24,8},{1,17},{17,1},{9,25},{25,9},{2,18},{18... | collective-permute-start | bytes 2580488 | tf_op jit(solution)/shard_map/ppermute | solution.py:100
  726.0 162.7 %collective-permute-start.98 = (bf16[2,280,1536]{2,1,0:T(8,128)(2,1)}, bf16[2,280,1536]{2,1,0:T(8,128)(2,1)}, u32[]{:S(2)}, u32[]{:S(2)}) collective-permute-start(bf16[2,280,1536]{2,1,0:T(8,128)(2,1)} %pad_maximum_fusion.14), channel_id=1, source_target_pairs={{0,8},{8,0},{16,24},{24,16},{1,9},{9,1},{17,25},{25,17},{2,10},{10... | collective-permute-start | bytes 5160968 | tf_op jit(solution)/shard_map/ppermute | solution.py:96
  747.9 163.7 %collective-permute-start.94 = (bf16[2,2,192,1120]{3,2,1,0:T(8,128)(2,1)}, bf16[2,2,192,1120]{3,2,1,0:T(8,128)(2,1)}, u32[]{:S(2)}, u32[]{:S(2)}) collective-permute-start(bf16[2,2,192,1120]{3,2,1,0:T(8,128)(2,1)} %pad_maximum_fusion.11), channel_id=1, source_target_pairs={{0,8},{8,0},{16,24},{24,16},{1,9},{9,1},{17,25},{25,17},{2,10},{10... | collective-permute-start | bytes 5160968 | tf_op jit(solution)/shard_map/ppermute | solution.py:96
  871.5 72.7 %collective-permute-start.96 = (bf16[2,2,192,1120]{3,2,1,0:T(8,128)(2,1)}, bf16[2,2,192,1120]{3,2,1,0:T(8,128)(2,1)}, u32[]{:S(2)}, u32[]{:S(2)}) collective-permute-start(bf16[2,2,192,1120]{3,2,1,0:T(8,128)(2,1)} %pad_maximum_fusion.12), channel_id=1, source_target_pairs={{0,8},{8,0},{16,24},{24,16},{1,9},{9,1},{17,25},{25,17},{2,10},{10... | collective-permute-start | bytes 5160968 | tf_op jit(solution)/shard_map/ppermute | solution.py:96
  986.6 133.9 %collective-permute-start.58 = (bf16[512,1536]{1,0:T(8,128)(2,1)}, bf16[512,1536]{1,0:T(8,128)(2,1)}, u32[]{:S(2)}, u32[]{:S(2)}) collective-permute-start(bf16[512,1536]{1,0:T(8,128)(2,1)} %pad_maximum_fusion.17), channel_id=1, source_target_pairs={{0,8},{8,0},{16,24},{24,16},{1,9},{9,1},{17,25},{25,17},{2,10},{10... | collective-permute-start | bytes 4718600 | tf_op jit(solution)/shard_map/ppermute | solution.py:96
  987.1 132.2 %collective-permute-start.89 = (bf16[192,512]{1,0:T(8,128)(2,1)}, bf16[192,512]{1,0:T(8,128)(2,1)}, u32[]{:S(2)}, u32[]{:S(2)}) collective-permute-start(bf16[192,512]{1,0:T(8,128)(2,1)} %get-tuple-element.54), channel_id=1, source_target_pairs={{0,16},{16,0},{8,24},{24,8},{1,17},{17,1},{9,25},{25,9},{2,18},{18... | collective-permute-start | bytes 589832 | tf_op jit(solution)/shard_map/ppermute | solution.py:100
  (220 other events, 3445.9 us)

commit v2 on v1

v2 whole, which is shorter than its diff:
```python
import functools

import jax
import jax.numpy as jnp
from jax import lax
from jax.experimental import pallas as pl
from jax.experimental.pallas import tpu as pltpu
from jax.sharding import PartitionSpec as P

D = 1536
FF = 8960
H = 12
KVH = 2
HD = 128
STEP = 10
HQD = 1536
KVD = 256


NORM_EPS = 1e-06
ROPE_BASE = 10000.0
CLIP_NORM = 1.0
BETA_FIRST = 0.9
BETA_SECOND = 0.95
ADAM_EPS = 1e-08
WEIGHT_DECAY = 0.1
RATE_ATTEND = 0.06
RATE_OUT = 0.5
RATE_GATE = 0.06
RATE_DOWN = 0.03
RATE_VECTOR = 0.5
NEG_LARGE = -1e30
LOG2E = 1.4426950408889634
VMEM = 48 * 1024 * 1024


def norm_apply(values, gain):
    return values * lax.rsqrt(jnp.mean(values * values, axis=-1, keepdims=True) + NORM_EPS) * gain


def swish_product(gate, up_proj):
    return jax.nn.silu(gate) * up_proj


def left_product(left_side, right_side):
    return lax.dot_general(
        left_side, right_side, (((0,), (0,)), ((), ())), preferred_element_type=jnp.float32
    )


def right_transposed(left_side, right_side):
    return lax.dot_general(
        left_side, right_side, (((1,), (1,)), ((), ())), preferred_element_type=jnp.float32
    )


def square_total(arrays):
    return sum((jnp.sum(member * member) for member in arrays))


def adam_step(weight, grad, first, second, rate, decay):
    first_new = BETA_FIRST * first + (1.0 - BETA_FIRST) * grad
    second_new = BETA_SECOND * second + (1.0 - BETA_SECOND) * grad * grad
    first_hat = first_new / (1.0 - BETA_FIRST**STEP)
    second_hat = second_new / (1.0 - BETA_SECOND**STEP)
    weight_new = weight - rate * (first_hat / (jnp.sqrt(second_hat) + ADAM_EPS) + decay * weight)
    return (first_new, second_new, weight_new)


def strip_starts(blk_count, team_bit, grp, quarter):
    per = blk_count // 4
    return [
        (((high * 2 + team_bit) * per + small) * 4 + grp) * quarter
        for high in range(2)
        for small in range(per)
    ]

def pick_body(blk_count, ids, gate_ref, up_ref, gate_out, up_out):
    quarter = FF // blk_count // 4
    for k in range(4):
        @pl.when(ids[0] == k)
        def _(k=k):
            for src, dst in ((gate_ref, gate_out), (up_ref, up_out)):
                for bit in range(2):
                    parts = [src[:, s:s + quarter] for s in strip_starts(blk_count, bit, k, quarter)]
                    dst[ids[1] ^ bit] = jnp.concatenate(parts, axis=1).astype(jnp.bfloat16)

def pick_columns(ids, gate, up, blk_count):
    rows = gate.shape[0]
    step = 48 if rows % 48 == 0 else rows
    wide_here = FF // 8
    spec = pl.BlockSpec((step, FF), lambda i, ids: (i, 0))
    out = pl.BlockSpec((2, step, wide_here), lambda i, ids: (0, i, 0))
    shape = jax.ShapeDtypeStruct((2, rows, wide_here), jnp.bfloat16)
    return pl.pallas_call(
        functools.partial(pick_body, blk_count),
        grid_spec=pltpu.PrefetchScalarGridSpec(
            num_scalar_prefetch=1, grid=(rows // step,), in_specs=[spec, spec], out_specs=[out, out]),
        out_shape=[shape, shape],
        compiler_params=pltpu.CompilerParams(vmem_limit_bytes=VMEM),
        cost_estimate=pl.CostEstimate(flops=0, bytes_accessed=rows * FF * 10, transcendentals=0),
        name="pick_columns",
    )(ids, gate, up)

def near_at(away):
    return (away & 1) * 2 + (away >> 1)


def adam_body(blk_count, rate, decay, ids, factor_ref, grad_ref, w_ref, m_ref, v_ref, m_out, v_out, w_out):
    quarter = FF // blk_count // 4
    per = blk_count // 4
    parts = []
    grads = [[grad_ref[near_at(ids[0] ^ k), bit] for bit in range(2)] for k in range(4)]
    for high in range(2):
        for bit in range(2):
            for small in range(per):
                at = (high * per + small) * quarter
                for k in range(4):
                    parts.append(grads[k][bit][:, at:at + quarter])
    grad = jnp.concatenate(parts, axis=1).astype(jnp.float32) * factor_ref[0]
    m, v, w = adam_step(w_ref[...], grad, m_ref[...], v_ref[...], rate, decay)
    m_out[...] = m
    v_out[...] = v
    w_out[...] = w

def adam_columns(ids, factor, grad, w, m, v, blk_count, rate, decay):
    rows = w.shape[0]
    step = 32 if rows % 32 == 0 else rows
    spec = pl.BlockSpec((step, FF), lambda i, ids: (i, 0))
    shape = jax.ShapeDtypeStruct((rows, FF), jnp.float32)
    return pl.pallas_call(
        functools.partial(adam_body, blk_count, rate, decay),
        grid_spec=pltpu.PrefetchScalarGridSpec(
            num_scalar_prefetch=1, grid=(rows // step,),
            in_specs=[pl.BlockSpec(memory_space=pltpu.SMEM),
                      pl.BlockSpec((4, 2, step, FF // 8), lambda i, ids: (0, 0, i, 0)), spec, spec, spec],
            out_specs=[spec, spec, spec]),
        out_shape=[shape] * 3,
        compiler_params=pltpu.CompilerParams(vmem_limit_bytes=VMEM),
        cost_estimate=pl.CostEstimate(flops=rows * FF * 20, bytes_accessed=rows * FF * 26, transcendentals=rows * FF),
        name="adam_columns",
    )(ids, factor, grad, w, m, v)

def nt(a, b, **kw):
    return lax.dot_general(a, b, (((1,), (1,)), ((), ())), preferred_element_type=jnp.float32, **kw)

def tn(a, b, **kw):
    return lax.dot_general(a, b, (((0,), (0,)), ((), ())), preferred_element_type=jnp.float32, **kw)

def stack_heads(ref, kvh, group):
    return jnp.concatenate([ref[:, HD * (kvh * group + i): HD * (kvh * group + i + 1)] for i in range(group)], axis=0)

def hidden_from(seg_key_ref, seg_query_ref, first, chunk, block_len, blk):
    key = first + lax.broadcasted_iota(jnp.int32, (chunk, block_len), 0)
    query = blk * block_len + lax.broadcasted_iota(jnp.int32, (chunk, block_len), 1)
    seg_key = seg_key_ref[pl.ds(first, chunk), :]
    counts = jnp.logical_and(key <= query, seg_key == seg_query_ref[0:1, :])
    return jnp.where(counts, 0.0, NEG_LARGE)

def attend_body(chunk, ids, q_ref, k_ref, v_ref, seg_key_ref, seg_query_ref, o_ref, lse_ref, m_s, l_s, acc_s):
    block_len = q_ref.shape[0]
    group = H // KVH
    row = pl.program_id(0)
    per = chunk // block_len
    scale = HD ** (-0.5) * LOG2E
    start = ids[1 + row] // per
    stop = ids[0] // per + 1
    for kvh in range(KVH):
        q = stack_heads(q_ref, kvh, group)
        m_s[...] = jnp.full_like(m_s, NEG_LARGE)
        l_s[...] = jnp.zeros_like(l_s)
        acc_s[...] = jnp.zeros_like(acc_s)

        def step(c, carry):
            keys = k_ref[pl.ds(c * per, per), :, HD * kvh: HD * (kvh + 1)].reshape(chunk, HD)
            vals = v_ref[pl.ds(c * per, per), :, HD * kvh: HD * (kvh + 1)].reshape(chunk, HD)
            bias = hidden_from(seg_key_ref, seg_query_ref, c * chunk, chunk, block_len, ids[0])
            s = nt(keys, q) * scale + jnp.concatenate([bias] * group, axis=1)
            old = m_s[0:1, :]
            new = jnp.maximum(old, jnp.max(s, axis=0, keepdims=True))
            p = jnp.exp2(s - new)
            fade = jnp.exp2(old - new)
            l_s[0:1, :] = l_s[0:1, :] * fade + jnp.sum(p, axis=0, keepdims=True)
            acc_s[...] = acc_s[...] * fade + tn(vals, p.astype(jnp.bfloat16))
            m_s[0:1, :] = new
            return carry

        lax.fori_loop(start, stop, step, 0)
        total = l_s[0:1, :]
        out = (acc_s[...] * (1.0 / total)).T
        for i in range(group):
            o_ref[:, HD * (kvh * group + i): HD * (kvh * group + i + 1)] = out[block_len * i: block_len * (i + 1), :].astype(jnp.bfloat16)
        lse_ref[kvh] = jnp.broadcast_to(m_s[0:1, :] + jnp.log2(total), (8, group * block_len))

def attend(ids, q, kv, seg_key, seg_query, block_len):
    blk_count, rows = kv.shape[:2]
    group = H // KVH
    chunk = 2 * block_len
    many = group * block_len
    return pl.pallas_call(
        functools.partial(attend_body, chunk),
        grid_spec=pltpu.PrefetchScalarGridSpec(
            num_scalar_prefetch=1, grid=(rows,),
            in_specs=[
                pl.BlockSpec((block_len, HQD), lambda r, ids: (r, 0)),
                pl.BlockSpec((blk_count, None, block_len, KVD), lambda r, ids: (0, r, 0, 0)),
                pl.BlockSpec((blk_count, None, block_len, KVD), lambda r, ids: (0, r, 0, 1)),
                pl.BlockSpec((None, blk_count * block_len, HD), lambda r, ids: (r, 0, 0)),
                pl.BlockSpec((None, 8, block_len), lambda r, ids: (r, 0, 0)),
            ],
            out_specs=[
                pl.BlockSpec((block_len, HQD), lambda r, ids: (r, 0)),
                pl.BlockSpec((None, KVH, 8, many), lambda r, ids: (r, 0, 0, 0)),
            ],
            scratch_shapes=[pltpu.VMEM((8, many), jnp.float32), pltpu.VMEM((8, many), jnp.float32), pltpu.VMEM((HD, many), jnp.float32)]),
        out_shape=[
            jax.ShapeDtypeStruct((rows * block_len, HQD), jnp.bfloat16),
            jax.ShapeDtypeStruct((rows, KVH, 8, many), jnp.float32),
        ],
        compiler_params=pltpu.CompilerParams(vmem_limit_bytes=VMEM),
        cost_estimate=pl.CostEstimate(flops=4 * rows * H * block_len * blk_count * block_len * HD, bytes_accessed=8 * 2**20, transcendentals=rows * H * block_len * blk_count * block_len),
        name="attend",
    )(ids, q, kv, kv, seg_key, seg_query)

def turn_back(u, cosine, sine):
    lane = lax.broadcasted_iota(jnp.int32, u.shape, 1)
    other = pltpu.roll(u, HD // 2, 1)
    return u * cosine + jnp.where(lane < HD // 2, other, -other) * sine

def attend_back_body(chunk, ids, q_ref, k_ref, v_ref, seg_key_ref, seg_query_ref, o_ref, do_ref, lse_ref, cos_ref, sin_ref, dq_ref, dkv_ref, dq_s):
    block_len = q_ref.shape[0]
    group = H // KVH
    row = pl.program_id(0)
    per = chunk // block_len
    plain = HD ** (-0.5)
    scale = plain * LOG2E
    start = ids[1 + row] // per
    stop = ids[0] // per + 1
    dkv_ref[...] = jnp.zeros_like(dkv_ref)
    for kvh in range(KVH):
        q = stack_heads(q_ref, kvh, group)
        do = stack_heads(do_ref, kvh, group)
        o = stack_heads(o_ref, kvh, group)
        both = do.astype(jnp.float32) * o.astype(jnp.float32)
        delta = nt(jnp.ones((8, HD), jnp.float32), both, precision=lax.Precision.HIGHEST)[0:1, :]
        lse = lse_ref[kvh][0:1, :]
        dq_s[...] = jnp.zeros_like(dq_s)

        def step(c, carry):
            keys = k_ref[pl.ds(c * per, per), :, HD * kvh: HD * (kvh + 1)].reshape(chunk, HD)
            vals = v_ref[pl.ds(c * per, per), :, HD * kvh: HD * (kvh + 1)].reshape(chunk, HD)
            bias = hidden_from(seg_key_ref, seg_query_ref, c * chunk, chunk, block_len, ids[0])
            s = nt(keys, q) * scale + jnp.concatenate([bias] * group, axis=1)
            p = jnp.exp2(s - lse)
            dp = nt(vals, do)
            ds = (p * (dp - delta)).astype(jnp.bfloat16)
            dk = jnp.dot(ds, q, preferred_element_type=jnp.float32) * plain
            dv = jnp.dot(p.astype(jnp.bfloat16), do, preferred_element_type=jnp.float32)
            dkv_ref[pl.ds(c * per, per), :, HD * kvh: HD * (kvh + 1)] = dk.astype(jnp.bfloat16).reshape(per, block_len, HD)
            dkv_ref[pl.ds(c * per, per), :, KVD + HD * kvh: KVD + HD * (kvh + 1)] = dv.astype(jnp.bfloat16).reshape(per, block_len, HD)
            dq_s[...] += tn(ds, keys)
            return carry

        lax.fori_loop(start, stop, step, 0)
        cosine, sine = cos_ref[...], sin_ref[...]
        for i in range(group):
            u = dq_s[block_len * i: block_len * (i + 1), :] * plain
            at = HD * (kvh * group + i)
            dq_ref[:, at: at + HD] = turn_back(u, cosine, sine).astype(jnp.bfloat16)

def attend_back(ids, q, kv, seg_key, seg_query, o, do, lse, cosine, sine, block_len):
    blk_count, rows = kv.shape[:2]
    group = H // KVH
    chunk = 2 * block_len
    many = group * block_len
    per_row = pl.BlockSpec((block_len, HQD), lambda r, ids: (r, 0))
    turn = pl.BlockSpec((block_len, HD), lambda r, ids: (r, 0))
    return pl.pallas_call(
        functools.partial(attend_back_body, chunk),
        grid_spec=pltpu.PrefetchScalarGridSpec(
            num_scalar_prefetch=1, grid=(rows,),
            in_specs=[
                per_row,
                pl.BlockSpec((blk_count, None, block_len, KVD), lambda r, ids: (0, r, 0, 0)),
                pl.BlockSpec((blk_count, None, block_len, KVD), lambda r, ids: (0, r, 0, 1)),
                pl.BlockSpec((None, blk_count * block_len, HD), lambda r, ids: (r, 0, 0)),
                pl.BlockSpec((None, 8, block_len), lambda r, ids: (r, 0, 0)),
                per_row, per_row,
                pl.BlockSpec((None, KVH, 8, many), lambda r, ids: (r, 0, 0, 0)),
                turn, turn,
            ],
            out_specs=[per_row, pl.BlockSpec((blk_count, None, block_len, 2 * KVD), lambda r, ids: (0, r, 0, 0))],
            scratch_shapes=[pltpu.VMEM((many, HD), jnp.float32)]),
        out_shape=[
            jax.ShapeDtypeStruct((rows * block_len, HQD), jnp.bfloat16),
            jax.ShapeDtypeStruct((blk_count, rows, block_len, 2 * KVD), jnp.bfloat16),
        ],
        compiler_params=pltpu.CompilerParams(vmem_limit_bytes=VMEM),
        cost_estimate=pl.CostEstimate(flops=10 * rows * H * block_len * blk_count * block_len * HD, bytes_accessed=12 * 2**20, transcendentals=rows * H * block_len * blk_count * block_len),
        name="attend_back",
    )(ids, q, kv, kv, seg_key, seg_query, o, do, lse, cosine, sine)


CORE = [(0, 1), (1, 0), (2, 3), (3, 2)]
CROSS = [(0, 2), (2, 0), (1, 3), (3, 1)]
DIAG = [(0, 3), (3, 0), (1, 2), (2, 1)]


def low(values):
    return values.astype(jnp.bfloat16)


def wide(values):
    return values.astype(jnp.float32)


def swap_core(values):
    return lax.ppermute(values, "grp", CORE)


def swap_cross(values):
    return lax.ppermute(values, "grp", CROSS)


def swap_diag(values):
    return lax.ppermute(values, "grp", DIAG)


def swap_blk(values, bit):
    count = lax.axis_size("blk")
    return lax.ppermute(values, "blk", [(i, i ^ bit) for i in range(count)])


def blk_bit(bit):
    return (lax.axis_index("blk") & bit) != 0


def bits_of(count):
    out = []
    bit = count // 2
    while bit >= 1:
        out.append(bit)
        bit //= 2
    return out


def gather_bits(values, order):
    done = []
    for bit in order:
        other = swap_blk(values, bit)
        mine = blk_bit(bit)
        axis = sum(1 for d in done if d > bit)
        values = jnp.stack(
            [jnp.where(mine, other, values), jnp.where(mine, values, other)], axis=axis
        )
        done.append(bit)
    return values


def scatter_bits(values, axes, order):
    axes = list(axes)
    for bit in order:
        axis = axes.index(bit)
        mine = blk_bit(bit).astype(jnp.int32)
        keep = lax.dynamic_index_in_dim(values, mine, axis, keepdims=False)
        send = lax.dynamic_index_in_dim(values, 1 - mine, axis, keepdims=False)
        values = low(wide(keep) + wide(swap_blk(send, bit)))
        axes.remove(bit)
    return values


def by_place(parts):
    grp = lax.axis_index("grp")
    core = (grp & 1) != 0
    cross = (grp & 2) != 0
    a, b, c, d = parts
    a, b = jnp.where(core, b, a), jnp.where(core, a, b)
    c, d = jnp.where(core, d, c), jnp.where(core, c, d)
    a, c = jnp.where(cross, c, a), jnp.where(cross, a, c)
    b, d = jnp.where(cross, d, b), jnp.where(cross, b, d)
    return [a, b, c, d]


def gather_near(values):
    cross = swap_cross(values)
    both = swap_core(jnp.stack([values, cross]))
    return [values, both[0], cross, both[1]]


def gather_grp(values):
    return by_place(gather_near(values))


def gather_tokens(values, bit):
    half = values.shape[0] // 2
    cross = swap_cross(values)
    over = swap_blk(values, bit)
    first = swap_blk(cross[:half], bit)
    second = swap_cross(over[half:])
    chip = jnp.concatenate([values, cross, over, first, second])
    return jnp.concatenate([chip, swap_core(chip)])


def scatter_tokens(values, bit):
    half_all = values.shape[0] // 2
    rows = half_all // 4
    half = rows // 2
    chip = wide(values[:half_all]) + wide(swap_core(low(values[half_all:])))
    own, cross, over, far = (chip[rows * i : rows * (i + 1)] for i in range(4))
    far = low(far)
    first = wide(swap_blk(far[:half], bit))
    second = wide(swap_cross(far[half:]))
    cross = low(jnp.concatenate([cross[:half] + first, cross[half:]]))
    over = low(jnp.concatenate([over[:half], over[half:] + second]))
    return own + wide(swap_cross(cross)) + wide(swap_blk(over, bit))


def angles_of(position):
    half = HD // 2
    freqs = ROPE_BASE ** (-2.0 * jnp.arange(half, dtype=jnp.float32) / HD)
    return position.astype(jnp.float32)[:, None] * freqs[None, :]


def rotate_by(values, cosine, sine):
    half = HD // 2
    first_half = values[..., :half]
    second_half = values[..., half:]
    return jnp.concatenate(
        [first_half * cosine - second_half * sine, second_half * cosine + first_half * sine],
        axis=-1,
    )


def after(values, anchor):
    return lax.optimization_barrier((values, anchor))[0]


def gather_step(values, done, bit):
    other = swap_blk(values, bit)
    mine = blk_bit(bit)
    axis = sum(1 for d in done if d > bit)
    return jnp.stack(
        [jnp.where(mine, other, values), jnp.where(mine, values, other)], axis=axis
    )


def gather_two_ways(values, bits, team):
    lows = [bit for bit in bits if bit < team]
    values = gather_step(values, [], bits[0])
    half = values.shape[-1] // 2
    parts = []
    for part, order in (
        (values[..., :half], [team] + lows),
        (values[..., half:], lows + [team]),
    ):
        done = [bits[0]]
        for bit in order:
            part = gather_step(part, done, bit)
            done.append(bit)
        parts.append(part)
    return jnp.concatenate(parts, axis=-1)


def scatter_two_ways(values, bits, team):
    lows = [bit for bit in bits if bit < team][::-1]
    half = values.shape[-1] // 2
    parts = [
        scatter_bits(values[..., :half], bits, lows + [team]),
        scatter_bits(values[..., half:], bits, [team] + lows),
    ]
    return scatter_bits(jnp.concatenate(parts, axis=-1), bits[:1], bits[:1])


def gather_near_stacked(values):
    both = jnp.stack([values, swap_cross(values)])
    return jnp.concatenate([both, swap_core(both)])


def on_device(
    tokens,
    cotangent,
    segment_ids,
    position_ids,
    w_attend,
    w_out,
    w_gate,
    w_up,
    w_down,
    small_params,
    first_attend,
    first_out,
    first_gate,
    first_up,
    first_down,
    first_small,
    second_attend,
    second_out,
    second_gate,
    second_up,
    second_down,
    second_small,
):
    rows_here, block_len = tokens.shape[:2]
    blk_count = lax.axis_size("blk")
    seq_len = block_len * blk_count
    token_count = rows_here * block_len
    grp = lax.axis_index("grp")
    blk = lax.axis_index("blk")
    cross_id, core_id = grp // 2, grp % 2
    strip_heads = H // 4
    strip_q = strip_heads * HD
    bits = bits_of(blk_count)
    team = blk_count // 4
    lows = [bit for bit in bits if bit < team]
    spread = [bits[0]] + lows
    low_shape = (2,) * len(lows)
    in_team = blk_bit(team).astype(jnp.int32)
    weight_rows = w_gate.shape[0]
    ff_block = w_down.shape[0]
    quarter = ff_block // 4
    ff_here = quarter * blk_count // 2

    ids = jnp.stack([grp, in_team])
    flat_low = tokens.reshape(token_count, D)
    dy_low = cotangent.reshape(token_count, D)
    positions = position_ids.reshape(token_count)
    kv_at = HQD + HD * cross_id + KVD * core_id
    strip_local = low(
        jnp.concatenate(
            [
                lax.dynamic_slice_in_dim(w_attend, strip_q * grp, strip_q, 1),
                lax.dynamic_slice_in_dim(w_attend, kv_at, HD, 1),
            ],
            axis=1,
        )
    )
    small_send = jnp.concatenate([low(small_params), low(segment_ids.reshape(token_count))])
    strip_first = gather_step(strip_local, [], bits[0])
    strip_parts = []
    cut = (strip_q + HD) // 2
    for part, order in (
        (strip_first[..., :cut], [team] + lows),
        (strip_first[..., cut:], lows + [team]),
    ):
        done = [bits[0]]
        for bit in order:
            part = gather_step(part, done, bit)
            done.append(bit)
        strip_parts.append(part)
    strip = jnp.concatenate(strip_parts, axis=-1).reshape(D, strip_q + HD)
    near_tokens = jnp.concatenate(gather_near(flat_low))
    near_positions = jnp.concatenate(gather_near(positions))
    small_all = gather_bits(small_send, bits).reshape(blk_count, -1)
    vector = wide(small_all[:, : small_params.shape[0]].reshape(-1))
    gain_one = vector[:D]
    gain_two = vector[D : 2 * D]
    bias = vector[2 * D :]
    strip_bias = jnp.concatenate(
        [
            lax.dynamic_slice_in_dim(bias, strip_q * grp, strip_q, 0),
            lax.dynamic_slice_in_dim(bias, kv_at, HD, 0),
        ]
    )
    seg_all = small_all[:, small_params.shape[0] :].astype(jnp.int32)
    seg_all = seg_all.reshape(blk_count, rows_here, block_len)
    seg_key = jnp.broadcast_to(
        seg_all.transpose(1, 0, 2).reshape(rows_here, seq_len)[:, :, None], (rows_here, seq_len, HD)
    )
    seg_query = jnp.broadcast_to(segment_ids[:, None, :], (rows_here, 8, block_len))
    first_blk = jnp.sum((seg_all[:, :, -1] < segment_ids[None, :, 0]).astype(jnp.int32), axis=0)
    attend_ids = jnp.concatenate([blk[None], first_blk])

    near_wide = wide(near_tokens)
    near_one = low(norm_apply(near_wide, gain_one))
    mixed = jnp.dot(near_one, strip, preferred_element_type=jnp.float32) + strip_bias
    angles = angles_of(near_positions)[:, None, :]
    turned = jnp.arange(strip_heads + 1)[None, :, None] < strip_heads + 1 - core_id
    angles = jnp.where(turned, angles, 0.0)
    strip_out = low(
        rotate_by(
            mixed.reshape(4 * token_count, strip_heads + 1, HD), jnp.cos(angles), jnp.sin(angles)
        )
    ).reshape(4, token_count, strip_q + HD)
    strips = by_place(
        [
            strip_out[0],
            swap_core(strip_out[1]),
            swap_cross(strip_out[2]),
            swap_diag(strip_out[3]),
        ]
    )
    query = jnp.concatenate([part[:, :strip_q] for part in strips], axis=1)
    key_value = jnp.concatenate([strips[k][:, strip_q:] for k in (0, 2, 1, 3)], axis=1)
    key_value = key_value.reshape(rows_here, block_len, 2 * KVD)
    kv_all = gather_two_ways(key_value, bits, team).reshape((blk_count,) + key_value.shape)

    down_local = low(lax.dynamic_slice_in_dim(w_down, quarter * grp, quarter, 0))
    down_first = swap_blk(after(down_local, strip_first), bits[0])
    gate_two, up_two = pick_columns(ids, w_gate, w_up, blk_count)
    mine_team = blk_bit(team)

    def pair_of(two):
        got = swap_blk(two[1], team)
        return jnp.stack([jnp.where(mine_team, got, two[0]), jnp.where(mine_team, two[0], got)])

    gate_pair = pair_of(after(gate_two, strip_parts))
    up_pair = pair_of(after(up_two, strip_parts))

    def place(values, other, done, bit):
        mine = blk_bit(bit)
        axis = sum(1 for d in done if d > bit)
        return jnp.stack(
            [jnp.where(mine, other, values), jnp.where(mine, values, other)], axis=axis
        )

    def finish(values, done):
        for bit in lows:
            values = place(values, swap_blk(values, bit), done, bit)
            done = done + [bit]
        return values

    gate_first = swap_blk(after(gate_pair, strip_out), bits[0])
    down_here = finish(place(down_local, after(down_first, strip_out), [], bits[0]), [bits[0]])
    down_here = down_here.reshape(ff_here, D)
    up_first = swap_blk(after(up_pair, kv_all), bits[0])
    gate_here = finish(place(gate_pair, after(gate_first, kv_all), [team], bits[0]), [team, bits[0]])
    gate_here = gate_here.reshape(D, ff_here)

    out_local = low(lax.dynamic_slice_in_dim(w_out, strip_q * grp, strip_q, 1))
    out_strip = gather_bits(after(out_local, strip_first), bits).reshape(HQD, strip_q)
    out_full = jnp.concatenate(gather_grp(out_strip), axis=1)
    dy_team = gather_tokens(dy_low, team)

    att_in, lse = attend(attend_ids, query, kv_all, seg_key, seg_query, block_len)

    flat = wide(flat_low)
    resid = flat + jnp.dot(att_in, out_full, preferred_element_type=jnp.float32)
    h_two = low(norm_apply(resid, gain_two))
    h_team = gather_tokens(h_two, team)
    up_here = finish(place(up_pair, after(up_first, h_two), [team], bits[0]), [team, bits[0]])
    up_here = up_here.reshape(D, ff_here)
    d_hidden = right_transposed(dy_team, down_here)
    gate = jnp.dot(h_team, gate_here, preferred_element_type=jnp.float32)
    up_proj = jnp.dot(h_team, up_here, preferred_element_type=jnp.float32)
    hidden = low(swish_product(gate, up_proj))
    down_grad = low(left_product(hidden, dy_team)).reshape((2,) + low_shape + (quarter, D))
    swish_value, swish_back = jax.vjp(swish_product, gate, up_proj)
    d_gate, d_up = swish_back(d_hidden)
    d_gate = low(d_gate)
    d_up = low(d_up)
    d_htwo_part = right_transposed(d_gate, gate_here) + right_transposed(d_up, up_here)
    d_htwo = scatter_tokens(d_htwo_part, team)

    def share_start(grad, axes):
        bit = lows[-1]
        axis = axes.index(bit)
        mine = blk_bit(bit).astype(jnp.int32)
        keep = lax.dynamic_index_in_dim(grad, mine, axis, keepdims=False)
        send = lax.dynamic_index_in_dim(grad, 1 - mine, axis, keepdims=False)
        return keep, swap_blk(send, bit)

    def share_mid(keep, got, axes):
        values = low(wide(keep) + wide(got))
        axes = [bit for bit in axes if bit != lows[-1]]
        for bit in lows[-2::-1]:
            values = scatter_bits(values, axes, [bit])
            axes = [b for b in axes if b != bit]
        mine = blk_bit(bits[0]).astype(jnp.int32)
        keep = lax.dynamic_index_in_dim(values, mine, 0, keepdims=False)
        send = lax.dynamic_index_in_dim(values, 1 - mine, 0, keepdims=False)
        return keep, swap_blk(send, bits[0])

    def share_columns(values):
        keep = lax.dynamic_index_in_dim(values, in_team, 0, keepdims=False)
        send = lax.dynamic_index_in_dim(values, 1 - in_team, 0, keepdims=False)
        got = swap_blk(send, team)
        return jnp.stack(
            [jnp.where(mine_team, got, keep), jnp.where(mine_team, keep, got)]
        )

    down_axes = [bits[0]] + lows
    down_keep, down_got = share_start(down_grad, down_axes)
    late_gate, late_up = after((d_gate, d_up), d_htwo_part)
    column_shape = (2, 2) + low_shape + (weight_rows, ff_here)
    gate_grad = low(left_product(h_team, late_gate)).reshape(column_shape)
    gate_keep, gate_got = share_start(gate_grad, bits)
    up_grad = low(left_product(h_team, late_up)).reshape(column_shape)
    up_keep, up_got = share_start(up_grad, bits)
    down_keep, down_got = share_mid(*after((down_keep, down_got), d_gate), down_axes)
    out_part = jnp.dot(after(hidden, up_grad), down_here, preferred_element_type=jnp.float32)

    norm_value_two, norm_back_two = jax.vjp(norm_apply, resid, gain_two)
    d_resid_norm, grad_gain_two = norm_back_two(d_htwo)
    d_resid = wide(dy_low) + d_resid_norm
    d_att = low(d_resid)

    d_attended = low(right_transposed(d_att, out_full))
    own_angles = angles_of(positions)
    cosine, sine = jnp.cos(own_angles), jnp.sin(own_angles)
    d_query, dkv = attend_back(
        attend_ids,
        query,
        kv_all,
        seg_key,
        seg_query,
        att_in,
        d_attended,
        lse,
        jnp.concatenate([cosine, cosine], axis=1),
        jnp.concatenate([sine, sine], axis=1),
        block_len,
    )
    gate_keep, gate_got = share_mid(*after((gate_keep, gate_got), d_attended), bits)
    share_down = low(wide(down_keep) + wide(after(down_got, d_query)))
    dkv = dkv.reshape((2,) * len(bits) + (rows_here, block_len, 2 * KVD))
    dkv = wide(scatter_two_ways(dkv, bits, team)).reshape(token_count, 2, KVH, HD)
    d_key = low(rotate_by(dkv[:, 0], cosine[:, None], -sine[:, None]))
    d_value = low(dkv[:, 1])
    up_keep, up_got = share_mid(*after((up_keep, up_got), d_query), bits)
    out_tokens = low(resid + scatter_tokens(after(out_part, d_query), team))

    def to_strips(parts):
        parts = by_place(parts)
        return jnp.concatenate(
            [parts[0], swap_core(parts[1]), swap_cross(parts[2]), swap_diag(parts[3])]
        )

    near_dq = to_strips([d_query[:, strip_q * k : strip_q * (k + 1)] for k in range(4)])
    block_shape = (2,) * len(bits) + (weight_rows, -1)
    share_query = scatter_bits(
        low(left_product(near_one, near_dq)).reshape(block_shape), bits, bits[::-1]
    )
    near_dkv = to_strips([(d_value if k % 2 else d_key)[:, k // 2] for k in range(4)])
    share_kv = scatter_bits(
        low(left_product(near_one, near_dkv)).reshape(block_shape), bits, bits[::-1]
    )
    grad_bias = jnp.concatenate(
        [
            jnp.sum(wide(part), axis=0)
            for part in (d_query, d_key.reshape(token_count, KVD), d_value.reshape(token_count, KVD))
        ]
    )
    near_hone = right_transposed(near_dq, strip[:, :strip_q]) + right_transposed(
        near_dkv, strip[:, strip_q:]
    )
    near_rms = lax.rsqrt(jnp.mean(near_wide * near_wide, axis=-1, keepdims=True) + NORM_EPS)
    gain_one_part = jnp.sum(near_hone * near_wide * near_rms, axis=0)

    near_att = jnp.concatenate(gather_near(att_in))
    near_datt = to_strips([d_att[:, strip_q * k : strip_q * (k + 1)] for k in range(4)])
    share_out = scatter_bits(
        low(left_product(near_att, after(near_datt, d_query))).reshape(block_shape),
        bits,
        bits[::-1],
    )

    vector_term = jnp.concatenate([gain_one_part, grad_gain_two, grad_bias])
    vector_term = vector_term + swap_cross(vector_term)
    vector_term = vector_term + swap_core(vector_term)
    vector_term = vector_term.reshape((2,) * len(bits) + (-1,))
    axes = list(bits)
    for bit in bits[::-1]:
        axis = axes.index(bit)
        mine = blk_bit(bit).astype(jnp.int32)
        keep = lax.dynamic_index_in_dim(vector_term, mine, axis, keepdims=False)
        send = lax.dynamic_index_in_dim(vector_term, 1 - mine, axis, keepdims=False)
        vector_term = keep + swap_blk(send, bit)
        axes.remove(bit)
    share_vector = vector_term

    share_gate = share_columns(low(wide(gate_keep) + wide(after(gate_got, d_key))))
    near_gate = gather_near_stacked(share_gate)
    share_up = share_columns(low(wide(up_keep) + wide(after(up_got, near_dkv))))
    near_up = gather_near_stacked(share_up)
    grad_down = jnp.concatenate(gather_grp(share_down), axis=0)
    grad_out = jnp.concatenate(gather_grp(share_out), axis=1)
    query_parts = gather_grp(share_query)
    kv_parts = gather_grp(share_kv)
    grad_attend = jnp.concatenate(query_parts + [kv_parts[k] for k in (0, 2, 1, 3)], axis=1)

    square_sum = square_total(
        [
            wide(s)
            for s in (share_query, share_kv, share_out, share_gate, share_up, share_down)
        ]
    ) + 0.25 * jnp.sum(share_vector * share_vector)
    square_sum = jnp.full((8, 128), square_sum)
    for bit in bits:
        square_sum = square_sum + swap_blk(square_sum, bit)
    square_sum = square_sum + swap_cross(square_sum)
    square_sum = square_sum + swap_core(square_sum)
    grad_norm = jnp.sqrt(square_sum[0, 0])
    factor = jnp.minimum(1.0, CLIP_NORM / (grad_norm + 1e-06))

    half = low(near_hone[token_count : 2 * token_count]), low(near_hone[3 * token_count :])
    other = wide(swap_core(jnp.concatenate(half)))
    d_hone = near_hone[:token_count] + other[:token_count]
    d_hone = d_hone + wide(
        swap_cross(low(near_hone[2 * token_count : 3 * token_count] + other[token_count:]))
    )
    norm_value_one, norm_back_one = jax.vjp(norm_apply, flat, gain_one)
    d_flat_norm, unused_gain = norm_back_one(d_hone)
    grad_tokens = low(d_resid + d_flat_norm)

    new_first_gate, new_second_gate, new_gate = adam_columns(
        ids, factor[None], near_gate, w_gate, first_gate, second_gate, blk_count, RATE_GATE, WEIGHT_DECAY
    )
    new_first_up, new_second_up, new_up = adam_columns(
        ids, factor[None], near_up, w_up, first_up, second_up, blk_count, RATE_GATE, WEIGHT_DECAY
    )
    new_first_attend, new_second_attend, new_attend = adam_step(
        w_attend, factor * wide(grad_attend), first_attend, second_attend, RATE_ATTEND, WEIGHT_DECAY
    )
    new_first_out, new_second_out, new_out = adam_step(
        w_out, factor * wide(grad_out), first_out, second_out, RATE_OUT, WEIGHT_DECAY
    )
    new_first_down, new_second_down, new_down = adam_step(
        w_down, factor * wide(grad_down), first_down, second_down, RATE_DOWN, WEIGHT_DECAY
    )
    new_first_small, new_second_small, new_small = adam_step(
        small_params, factor * share_vector, first_small, second_small, RATE_VECTOR, 0.0
    )
    return (
        out_tokens.reshape(rows_here, block_len, D),
        grad_tokens.reshape(rows_here, block_len, D),
        grad_norm,
        new_first_attend,
        new_second_attend,
        new_attend,
        new_first_out,
        new_second_out,
        new_out,
        new_first_gate,
        new_second_gate,
        new_gate,
        new_first_up,
        new_second_up,
        new_up,
        new_first_down,
        new_second_down,
        new_down,
        new_first_small,
        new_second_small,
        new_small,
    )


def solution(mesh):
    placed = (
        P("grp", "blk", None),
        P("grp", "blk", None),
        P("grp", "blk"),
        P("grp", "blk"),
        P("blk", None),
        P("blk", None),
        P("blk", None),
        P("blk", None),
        P("blk", None),
        P("blk"),
        P("blk", None),
        P("blk", None),
        P("blk", None),
        P("blk", None),
        P("blk", None),
        P("blk"),
        P("blk", None),
        P("blk", None),
        P("blk", None),
        P("blk", None),
        P("blk", None),
        P("blk"),
    )
    return jax.shard_map(
        on_device,
        mesh=mesh,
        in_specs=placed,
        out_specs=(
            P("grp", "blk", None),
            P("grp", "blk", None),
            P(),
            P("blk", None),
            P("blk", None),
            P("blk", None),
            P("blk", None),
            P("blk", None),
            P("blk", None),
            P("blk", None),
            P("blk", None),
            P("blk", None),
            P("blk", None),
            P("blk", None),
            P("blk", None),
            P("blk", None),
            P("blk", None),
            P("blk", None),
            P("blk"),
            P("blk"),
            P("blk"),
        ),
        check_vma=False,
    )
```

time: 1150 us -> 976 us (0.85)
  local copies, waits for them, and re-layouts: 242 us -> 78.5 us
  other arithmetic: 221 us -> 129 us
  Pallas kernels: 0 us -> 52.7 us
  starting transfers between devices: 75.3 us -> 111 us
  matrix products: 158 us -> 144 us
    pallas_call x0 -> x5, Pallas kernels: none -> 52.7 us  [the longest x2 34.4 us: adam_columns(): pl.pallas_call(functools.partial(adam_body, blk_count, rate, decay), grid...]
    mul x5 -> x0, local copies, waits for them, and re-layouts: 49.5 us -> none  [the longest x2 24.8 us: on_device(): factor * wide(grad_gate)]
    sub x6 -> x4, other arithmetic: 59 us -> 19.5 us  [adam_step(): weight - rate * (first_hat / (jnp.sqrt(second_hat) + ADAM_EPS) + decay *...]
    ppermute x54 -> x60, starting transfers between devices: 46.7 us -> 83.5 us  [swap_blk(): return lax.ppermute(values, 'blk', [(i, i ^ bit) for i in range(count)])]
    reshape x12 -> x2, local copies, waits for them, and re-layouts: 36.6 us -> 2.17 us  [the longest x1 2.16 us: on_device(): wide(scatter_two_ways(dkv, bits, team)).reshape(token_count, 2, KVH, HD)]
    another operation x13 -> x4, local copies, waits for them, and re-layouts: 35.1 us -> 2.48 us  [the longest x8 29.9 us: whole_columns(): parts = jnp.stack(gather_grp(share))]
    dot_general x7 -> x1, matrix products: 41.7 us -> 13.9 us  [on_device(): jnp.dot(after(hidden, up_grad), down_here, preferred_element_type=jnp.flo...]
    mul x2 -> x0, other arithmetic: 24.2 us -> none  [the longest x1 12.1 us: on_device(): factor * wide(grad_gate)]
  transfers between devices with their start and end apart: 99 -> 110, of which waited for: 48 -> 49; matrix products, arithmetic and copies ran while one was open for 46% -> 26% of each run, Pallas kernels for 0% -> 5%
where the time goes in v2:
time: 976 us; the launch traced here: 966 us
  waiting for transfers between devices  442 us (45%)
  matrix products  144 us (15%)
  other arithmetic  129 us (13%)
  starting transfers between devices  111 us (11%)
  local copies, waits for them, and re-layouts  78.5 us (8%)
  Pallas kernels  52.7 us (5%)
  between operations  10 us (1%)
    ppermute x60, waiting for transfers between devices, swap_blk(): return lax.ppermute(values, 'blk', [(i, i ^ bit) for i in range(count)])  376 us
    ppermute x60, starting transfers between devices, swap_blk(): return lax.ppermute(values, 'blk', [(i, i ^ bit) for i in range(count)])  83.5 us
    ppermute x25, waiting for transfers between devices, swap_cross(): return lax.ppermute(values, 'grp', CROSS)  59.1 us
    dot_general x6, matrix products, right_transposed(): lax.dot_general(left_side, right_side, (((1,), (1,)), ((), ())), preferre...  57.8 us
    dot_general x6, matrix products, left_product(): lax.dot_general(left_side, right_side, (((0,), (0,)), ((), ())), preferre...  44.9 us
    pallas_call x2, Pallas kernels, adam_columns(): pl.pallas_call(functools.partial(adam_body, blk_count, rate, decay), grid...  34.4 us
    convert_element_type x22, other arithmetic, low(): return values.astype(jnp.bfloat16)  21.9 us
    ppermute x25, starting transfers between devices, swap_cross(): return lax.ppermute(values, 'grp', CROSS)  20.8 us
  transfers between devices with their start and end apart: 110, of which 49 were waited for; matrix products, arithmetic and copies ran while one was open for 26% of the time, Pallas kernels for 5%

profile of v2, /device:TPU:0, one launch (start us, length us, event | category | flops | bytes accessed | tf_op | source)
XLA Modules:
  0.0 966.1 jit_solution(2577734204062620627)
XLA Ops:
  58.2 10.6 %collective-permute-done.21 = bf16[2,192,384]{2,1,0:T(8,128)(2,1)S(1)} collective-permute-done((bf16[2,192,384]{2,1,0:T(8,128)(2,1)S(1)}, bf16[2,192,384]{2,1,0:T(8,128)(2,1)S(1)}, u32[]{:S(2)}, u32[]{:S(2)}) %collective-permute-start.21) | collective-permute-done | bytes 294944 | tf_op jit(solution)/shard_map/ppermute | solution.py:331
  151.8 12.6 %collective-permute-done.15 = bf16[2,128,512]{2,1,0:T(8,128)(2,1)S(1)} collective-permute-done((bf16[2,128,512]{2,1,0:T(8,128)(2,1)S(1)}, bf16[2,128,512]{2,1,0:T(8,128)(2,1)S(1)}, u32[]{:S(2)}, u32[]{:S(2)}) %collective-permute-start.15) | collective-permute-done | bytes 262176 | tf_op jit(solution)/shard_map/ppermute | solution.py:331
  174.0 36.9 %collective-permute-done.18 = bf16[2,2,128,256]{3,2,1,0:T(8,128)(2,1)S(1)} collective-permute-done((bf16[2,2,128,256]{3,2,1,0:T(8,128)(2,1)S(1)}, bf16[2,2,128,256]{3,2,1,0:T(8,128)(2,1)S(1)}, u32[]{:S(2)}, u32[]{:S(2)}) %collective-permute-start.18) | collective-permute-done | bytes 262176 | tf_op jit(solution)/shard_map/ppermute | solution.py:331
  229.2 32.9 %collective-permute-done.31 = bf16[2,192,1120]{2,1,0:T(8,128)(2,1)} collective-permute-done((bf16[2,192,1120]{2,1,0:T(8,128)(2,1)S(1)}, bf16[2,192,1120]{2,1,0:T(8,128)(2,1)}, u32[]{:S(2)}, u32[]{:S(2)}) %collective-permute-start.31) | collective-permute-done | bytes 860192 | tf_op jit(solution)/shard_map/ppermute | solution.py:331
  273.8 27.6 %collective-permute-done.34 = bf16[2,192,1120]{2,1,0:T(8,128)(2,1)S(1)} collective-permute-done((bf16[2,192,1120]{2,1,0:T(8,128)(2,1)}, bf16[2,192,1120]{2,1,0:T(8,128)(2,1)S(1)}, u32[]{:S(2)}, u32[]{:S(2)}) %collective-permute-start.34) | collective-permute-done | bytes 860192 | tf_op jit(solution)/shard_map/ppermute | solution.py:331
  328.8 16.1 %collective-permute-done.32 = bf16[2,2,192,1120]{3,2,1,0:T(8,128)(2,1)S(1)} collective-permute-done((bf16[2,2,192,1120]{3,2,1,0:T(8,128)(2,1)S(1)}, bf16[2,2,192,1120]{3,2,1,0:T(8,128)(2,1)S(1)}, u32[]{:S(2)}, u32[]{:S(2)}) %collective-permute-start.32) | collective-permute-done | bytes 1720352 | tf_op jit(solution)/shard_map/ppermute | solution.py:331
  346.0 35.8 %collective-permute-done.35 = bf16[2,2,192,1120]{3,2,1,0:T(8,128)(2,1)S(1)} collective-permute-done((bf16[2,2,192,1120]{3,2,1,0:T(8,128)(2,1)S(1)}, bf16[2,2,192,1120]{3,2,1,0:T(8,128)(2,1)S(1)}, u32[]{:S(2)}, u32[]{:S(2)}) %collective-permute-start.35) | collective-permute-done | bytes 1720352 | tf_op jit(solution)/shard_map/ppermute | solution.py:331
  385.8 12.2 %fusion.124 = f32[2048,1120]{0,1:T(8,128)} fusion(bf16[2048,1536]{1,0:T(8,128)(2,1)} %constant_dynamic-update-slice_fusion.5, bf16[1536,1120]{1,0:T(8,128)(2,1)S(1)} %bitcast.593), kind=kOutput, calls=%fused_computation.519 | convolution fusion | flops 7046430720 | bytes 18907136 | tf_op jit(solution)/shard_map/dot_general | solution.py:644
  398.0 10.3 %fusion.123 = f32[2048,1120]{0,1:T(8,128)} fusion(bf16[2048,1536]{1,0:T(8,128)(2,1)S(1)} %copy-done.90, bf16[1536,1120]{1,0:T(8,128)(2,1)S(1)} %bitcast.591), kind=kOutput, calls=%fused_computation.518 | convolution fusion | flops 7046430720 | bytes 18907136 | tf_op jit(solution)/shard_map/dot_general | solution.py:643
  408.3 20.6 %multiply_convert_fusion = (bf16[2048,1120]{0,1:T(8,128)(2,1)}, bf16[2048,1120]{0,1:T(8,128)(2,1)}, bf16[2048,1120]{0,1:T(8,128)(2,1)}) fusion(f32[2048,1120]{0,1:T(8,128)} %fusion.123, f32[2048,1120]{0,1:T(8,128)} %fusion.124, bf16[2048,1536]{1,0:T(8,128)(2,1)} %constant_dynamic-update-slice_fusion.16, bf16[1120,1536]{1,0:T(8,128)(2,1)} %bitcast.595), kind=kOutput, calls=%fused_computation.8 | convolution fusion | flops 7083130880 | bytes 41844736 | tf_op jit(solution)/shard_map/dot_general | solution.py:52
  428.8 13.0 %fusion.125 = f32[2048,1536]{1,0:T(8,128)} fusion(bf16[2048,1120]{0,1:T(8,128)(2,1)} %get-tuple-element.75, bf16[1536,1120]{1,0:T(8,128)(2,1)S(1)} %bitcast.592), kind=kOutput, calls=%fused_computation.520 | convolution fusion | flops 7046430720 | bytes 20611072 | tf_op jit(solution)/shard_map/dot_general | solution.py:52
  441.8 13.8 %convolution_add_fusion = f32[2048,1536]{1,0:T(8,128)S(1)} fusion(f32[2048,1536]{1,0:T(8,128)} %fusion.125, bf16[2048,1120]{0,1:T(8,128)(2,1)} %get-tuple-element.68, bf16[1536,1120]{1,0:T(8,128)(2,1)} %bitcast.594), kind=kOutput, calls=%fused_computation.12 | convolution fusion | flops 7049576448 | bytes 33193984 | tf_op jit(solution)/shard_map/dot_general | solution.py:52
  457.7 15.7 %convolution_convert_fusion.2 = bf16[1120,1536]{1,0:T(8,128)(2,1)S(1)} fusion(bf16[2048,1120]{0,1:T(8,128)(2,1)} %get-tuple-element.69, bf16[2048,1536]{1,0:T(8,128)(2,1)} %constant_dynamic-update-slice_fusion.16), kind=kOutput, calls=%fused_computation.15 | convolution fusion | flops 7048151040 | bytes 14319616 | tf_op jit(solution)/shard_map/dot_general | solution.py:46
  490.6 12.4 %convolution_convert_fusion.1 = bf16[1536,1120]{0,1:T(8,128)(2,1)} fusion(bf16[2048,1120]{0,1:T(8,128)(2,1)} %get-tuple-element.68, bf16[2048,1536]{1,0:T(8,128)(2,1)} %constant_dynamic-update-slice_fusion.5), kind=kOutput, calls=%fused_computation.14 | convolution fusion | flops 7048151040 | bytes 14319616 | tf_op jit(solution)/shard_map/dot_general | solution.py:46
  522.3 13.9 %fusion.126 = f32[2048,1536]{1,0:T(8,128)} fusion(bf16[2048,1120]{0,1:T(8,128)(2,1)} %get-tuple-element.69, bf16[1120,1536]{1,0:T(8,128)(2,1)} %bitcast.596), kind=kOutput, calls=%fused_computation.521 | convolution fusion | flops 7046430720 | bytes 20611072 | tf_op jit(solution)/shard_map/dot_general | solution.py:690
  542.8 27.1 %collective-permute-done.47 = bf16[256,1536]{1,0:T(8,128)(2,1)S(1)} collective-permute-done((bf16[256,1536]{1,0:T(8,128)(2,1)S(1)}, bf16[256,1536]{1,0:T(8,128)(2,1)S(1)}, u32[]{:S(2)}, u32[]{:S(2)}) %collective-permute-start.47) | collective-permute-done | bytes 786464 | tf_op jit(solution)/shard_map/ppermute | solution.py:331
  626.7 13.4 %collective-permute-done.77 = bf16[2,2,192,384]{3,2,0,1:T(8,128)(2,1)S(1)} collective-permute-done((bf16[2,2,192,384]{3,2,0,1:T(8,128)(2,1)S(1)}, bf16[2,2,192,384]{3,2,0,1:T(8,128)(2,1)S(1)}, u32[]{:S(2)}, u32[]{:S(2)}) %collective-permute-start.77) | collective-permute-done | bytes 589856 | tf_op jit(solution)/shard_map/ppermute | solution.py:331
  659.0 39.6 %collective-permute-done.57 = bf16[2,2,128,256]{3,2,1,0:T(8,128)(2,1)S(1)} collective-permute-done((bf16[2,2,128,256]{3,2,1,0:T(8,128)(2,1)S(1)}, bf16[2,2,128,256]{3,2,1,0:T(8,128)(2,1)S(1)}, u32[]{:S(2)}, u32[]{:S(2)}) %collective-permute-start.57) | collective-permute-done | bytes 262176 | tf_op jit(solution)/shard_map/ppermute | solution.py:331
  703.4 14.2 %collective-permute-done.60 = bf16[2,128,512]{2,1,0:T(8,128)(2,1)S(1)} collective-permute-done((bf16[2,128,512]{2,1,0:T(8,128)(2,1)S(1)}, bf16[2,128,512]{2,1,0:T(8,128)(2,1)S(1)}, u32[]{:S(2)}, u32[]{:S(2)}) %collective-permute-start.60) | collective-permute-done | bytes 262176 | tf_op jit(solution)/shard_map/ppermute | solution.py:331
  843.3 11.7 %collective-permute-done.106 = bf16[2,192,1120]{2,1,0:T(8,128)(2,1)S(1)} collective-permute-done((bf16[2,192,1120]{2,1,0:T(8,128)(2,1)}, bf16[2,192,1120]{2,1,0:T(8,128)(2,1)S(1)}, u32[]{:S(2)}, u32[]{:S(2)}) %collective-permute-start.106) | collective-permute-done | bytes 860192 | tf_op jit(solution)/shard_map/ppermute | solution.py:322
  857.3 15.3 %collective-permute-done.104 = bf16[2,192,1120]{2,1,0:T(8,128)(2,1)S(1)} collective-permute-done((bf16[2,192,1120]{2,1,0:T(8,128)(2,1)S(1)}, bf16[2,192,1120]{2,1,0:T(8,128)(2,1)S(1)}, u32[]{:S(2)}, u32[]{:S(2)}) %collective-permute-start.104) | collective-permute-done | bytes 860192 | tf_op jit(solution)/shard_map/ppermute | solution.py:322
  877.2 11.8 %multiply_subtract_fusion = (f32[1120,1536]{1,0:T(8,128)}, f32[1120,1536]{1,0:T(8,128)}, f32[1120,1536]{1,0:T(8,128)}) fusion(f32[1120,1536]{1,0:T(8,128)S(1)} %bitcast.578, bf16[280,1536]{1,0:T(8,128)(2,1)} %get-tuple-element.153, bf16[280,1536]{1,0:T(8,128)(2,1)S(1)} %get-tuple-element.152, bf16[280,1536]{1,0:T(8,128)(2,1)S(1)} %get-tuple-element.151, ...), kind=kLoop, calls=%fused_computation.17 | loop fusion | flops 41287680 | bytes 44728324 | tf_op jit(solution)/shard_map/sub | solution.py:66
  926.0 17.2 %adam_columns.3 = (f32[192,8960]{1,0:T(8,128)}, f32[192,8960]{1,0:T(8,128)}, f32[192,8960]{1,0:T(8,128)}) custom-call(s32[2]{0:T(128)S(1)} %pad_add_fusion.2.ids, f32[1]{0:T(128)} %bitcast.170.factor_ref, bf16[4,2,192,1120]{3,2,1,0:T(8,128)(2,1)S(1)} %pad_maximum_fusion.4.grad_ref, f32[192,8960]{1,0:T(8,128)} %w_ref.3, f32[192,8960]{1,0:T(8,128)} %m_ref.3, ...), custom_call_target="tpu_custom_call" | custom-call | flops 34406400 | bytes 44728320 | tf_op jit(solution)/shard_map/adam_columns/pallas_call | solution.py:131
  944.9 17.2 %adam_columns.2 = (f32[192,8960]{1,0:T(8,128)}, f32[192,8960]{1,0:T(8,128)}, f32[192,8960]{1,0:T(8,128)}) custom-call(s32[2]{0:T(128)S(1)} %pad_add_fusion.2.ids, f32[1]{0:T(128)} %bitcast.170.factor_ref, bf16[4,2,192,1120]{3,2,1,0:T(8,128)(2,1)S(1)} %pad_maximum_fusion.3.grad_ref, f32[192,8960]{1,0:T(8,128)} %w_ref.2, f32[192,8960]{1,0:T(8,128)} %m_ref.2, ...), custom_call_target="tpu_custom_call" | custom-call | flops 34406400 | bytes 44728320 | tf_op jit(solution)/shard_map/adam_columns/pallas_call | solution.py:131
  (734 shorter events, 504.1 us)
Async XLA Ops:
  0.7 75.5 %collective-permute-start.37 = (bf16[256,1536]{1,0:T(8,128)(2,1)}, bf16[256,1536]{1,0:T(8,128)(2,1)}, u32[]{:S(2)}, u32[]{:S(2)}) collective-permute-start(bf16[256,1536]{1,0:T(8,128)(2,1)} %bitcast.599), channel_id=1, source_target_pairs={{0,2},{1,3},{2,0},{3,1},{4,6},{5,7},{6,4},{7,5},{8,10},{9,11},{10,... | collective-permute-start | bytes 2359304 | tf_op jit(solution)/shard_map/ppermute | solution.py:331
  3.8 75.0 %collective-permute-start.36 = (bf16[256,1536]{1,0:T(8,128)(2,1)}, bf16[256,1536]{1,0:T(8,128)(2,1)}, u32[]{:S(2)}, u32[]{:S(2)}) collective-permute-start(bf16[256,1536]{1,0:T(8,128)(2,1)} %bitcast.600), channel_id=1, source_target_pairs={{0,16},{16,0},{8,24},{24,8},{1,17},{17,1},{9,25},{25,9},{2,18},{18... | collective-permute-start | bytes 2359304 | tf_op jit(solution)/shard_map/ppermute | solution.py:322
  29.3 51.7 %collective-permute-start.3 = (bf16[256,1536]{1,0:T(8,128)(2,1)S(1)}, bf16[256,1536]{1,0:T(8,128)(2,1)}, u32[]{:S(2)}, u32[]{:S(2)}) collective-permute-start(bf16[256,1536]{1,0:T(8,128)(2,1)S(1)} %bitcast.567), channel_id=1, source_target_pairs={{0,16},{16,0},{8,24},{24,8},{1,17},{17,1},{9,25},{25,9},{2,18},{18... | collective-permute-start | bytes 2359304 | tf_op jit(solution)/shard_map/ppermute | solution.py:322
  68.8 69.4 %collective-permute-start.41 = (bf16[280,1536]{1,0:T(8,128)(2,1)}, bf16[280,1536]{1,0:T(8,128)(2,1)}, u32[]{:S(2)}, u32[]{:S(2)}) collective-permute-start(bf16[280,1536]{1,0:T(8,128)(2,1)} %dynamic-slice_convert_fusion), channel_id=1, source_target_pairs={{0,4},{1,5},{2,6},{3,7},{4,0},{5,1},{6,2},{7,3},{8,12},{9,13},{10,... | collective-permute-start | bytes 2580488 | tf_op jit(solution)/shard_map/ppermute | solution.py:331
  78.8 57.0 %collective-permute-start.22 = (bf16[2,2,192,384]{3,2,1,0:T(8,128)(2,1)}, bf16[2,2,192,384]{3,2,1,0:T(8,128)(2,1)}, u32[]{:S(2)}, u32[]{:S(2)}) collective-permute-start(bf16[2,2,192,384]{3,2,1,0:T(8,128)(2,1)} %pad_maximum_fusion.35), channel_id=1, source_target_pairs={{0,1},{1,0},{2,3},{3,2},{4,5},{5,4},{6,7},{7,6},{8,9},{9,8},{10,11... | collective-permute-start | bytes 1769480 | tf_op jit(solution)/shard_map/ppermute | solution.py:331
  113.7 209.5 %collective-permute-start.40 = (bf16[1024,1536]{1,0:T(8,128)(2,1)}, bf16[1024,1536]{1,0:T(8,128)(2,1)}, u32[]{:S(2)}, u32[]{:S(2)}) collective-permute-start(bf16[1024,1536]{1,0:T(8,128)(2,1)} %get-tuple-element.259), channel_id=1, source_target_pairs={{0,8},{8,0},{16,24},{24,16},{1,9},{9,1},{17,25},{25,17},{2,10},{10... | collective-permute-start | bytes 9437192 | tf_op jit(solution)/shard_map/ppermute | solution.py:318
  138.3 74.8 %collective-permute-start.23 = (bf16[1536,384]{1,0:T(8,128)(2,1)S(1)}, bf16[1536,384]{1,0:T(8,128)(2,1)S(1)}, u32[]{:S(2)}, u32[]{:S(2)}) collective-permute-start(bf16[1536,384]{1,0:T(8,128)(2,1)S(1)} %bitcast.579), channel_id=1, source_target_pairs={{0,16},{16,0},{8,24},{24,8},{1,17},{17,1},{9,25},{25,9},{2,18},{18... | collective-permute-start | bytes 3538952 | tf_op jit(solution)/shard_map/ppermute | solution.py:322
  164.8 97.3 %collective-permute-start.42 = (bf16[2,280,1536]{2,1,0:T(8,128)(2,1)S(1)}, bf16[2,280,1536]{2,1,0:T(8,128)(2,1)}, u32[]{:S(2)}, u32[]{:S(2)}) collective-permute-start(bf16[2,280,1536]{2,1,0:T(8,128)(2,1)S(1)} %pad_maximum_fusion.13), channel_id=1, source_target_pairs={{0,1},{1,0},{2,3},{3,2},{4,5},{5,4},{6,7},{7,6},{8,9},{9,8},{10,11... | collective-permute-start | bytes 5160968 | tf_op jit(solution)/shard_map/ppermute | solution.py:331
  266.2 61.3 %collective-permute-start.73 = (bf16[2,256,1536]{2,1,0:T(8,128)(2,1)S(1)}, bf16[2,256,1536]{2,1,0:T(8,128)(2,1)S(1)}, u32[]{:S(2)}, u32[]{:S(2)}) collective-permute-start(bf16[2,256,1536]{2,1,0:T(8,128)(2,1)S(1)} %pad_maximum_fusion.17), channel_id=1, source_target_pairs={{0,8},{8,0},{16,24},{24,16},{1,9},{9,1},{17,25},{25,17},{2,10},{10... | collective-permute-start | bytes 4718600 | tf_op jit(solution)/shard_map/ppermute | solution.py:318
  321.6 61.3 %collective-permute-start.29 = (bf16[1024,1536]{1,0:T(8,128)(2,1)S(1)}, bf16[1024,1536]{1,0:T(8,128)(2,1)S(1)}, u32[]{:S(2)}, u32[]{:S(2)}) collective-permute-start(bf16[1024,1536]{1,0:T(8,128)(2,1)S(1)} %get-tuple-element.263), channel_id=1, source_target_pairs={{0,8},{8,0},{16,24},{24,16},{1,9},{9,1},{17,25},{25,17},{2,10},{10... | collective-permute-start | bytes 9437192 | tf_op jit(solution)/shard_map/ppermute | solution.py:318
  321.9 59.8 %collective-permute-start.35 = (bf16[2,2,192,1120]{3,2,1,0:T(8,128)(2,1)S(1)}, bf16[2,2,192,1120]{3,2,1,0:T(8,128)(2,1)S(1)}, u32[]{:S(2)}, u32[]{:S(2)}) collective-permute-start(bf16[2,2,192,1120]{3,2,1,0:T(8,128)(2,1)S(1)} %pad_maximum_fusion.10), channel_id=1, source_target_pairs={{0,1},{1,0},{2,3},{3,2},{4,5},{5,4},{6,7},{7,6},{8,9},{9,8},{10,11... | collective-permute-start | bytes 5160968 | tf_op jit(solution)/shard_map/ppermute | solution.py:331
  475.4 60.8 %collective-permute-start.86 = (bf16[2,280,1536]{2,1,0:T(8,128)(2,1)}, bf16[2,280,1536]{2,1,0:T(8,128)(2,1)}, u32[]{:S(2)}, u32[]{:S(2)}) collective-permute-start(bf16[2,280,1536]{2,1,0:T(8,128)(2,1)} %get-tuple-element.154), channel_id=1, source_target_pairs={{0,1},{1,0},{2,3},{3,2},{4,5},{5,4},{6,7},{7,6},{8,9},{9,8},{10,11... | collective-permute-start | bytes 5160968 | tf_op jit(solution)/shard_map/ppermute | solution.py:331
  512.3 71.4 %collective-permute-start.80 = (bf16[2,2,192,1120]{3,2,1,0:T(8,128)(2,1)}, bf16[2,2,192,1120]{3,2,1,0:T(8,128)(2,1)}, u32[]{:S(2)}, u32[]{:S(2)}) collective-permute-start(bf16[2,2,192,1120]{3,2,1,0:T(8,128)(2,1)} %get-tuple-element.144), channel_id=1, source_target_pairs={{0,1},{1,0},{2,3},{3,2},{4,5},{5,4},{6,7},{7,6},{8,9},{9,8},{10,11... | collective-permute-start | bytes 5160968 | tf_op jit(solution)/shard_map/ppermute | solution.py:331
  515.0 76.9 %collective-permute-start.83 = (bf16[2,2,192,1120]{3,2,1,0:T(8,128)(2,1)}, bf16[2,2,192,1120]{3,2,1,0:T(8,128)(2,1)}, u32[]{:S(2)}, u32[]{:S(2)}) collective-permute-start(bf16[2,2,192,1120]{3,2,1,0:T(8,128)(2,1)} %get-tuple-element.142), channel_id=1, source_target_pairs={{0,1},{1,0},{2,3},{3,2},{4,5},{5,4},{6,7},{7,6},{8,9},{9,8},{10,11... | collective-permute-start | bytes 5160968 | tf_op jit(solution)/shard_map/ppermute | solution.py:331
  608.0 93.1 %collective-permute-start.108 = (bf16[280,1536]{1,0:T(8,128)(2,1)S(1)}, bf16[280,1536]{1,0:T(8,128)(2,1)S(1)}, u32[]{:S(2)}, u32[]{:S(2)}) collective-permute-start(bf16[280,1536]{1,0:T(8,128)(2,1)S(1)} %get-tuple-element.112), channel_id=1, source_target_pairs={{0,16},{16,0},{8,24},{24,8},{1,17},{17,1},{9,25},{25,9},{2,18},{18... | collective-permute-start | bytes 2580488 | tf_op jit(solution)/shard_map/ppermute | solution.py:322
  611.7 116.1 %collective-permute-start.81 = (bf16[2,192,1120]{2,1,0:T(8,128)(2,1)}, bf16[2,192,1120]{2,1,0:T(8,128)(2,1)}, u32[]{:S(2)}, u32[]{:S(2)}) collective-permute-start(bf16[2,192,1120]{2,1,0:T(8,128)(2,1)} %dynamic-slice_bitcast_fusion.7), channel_id=1, source_target_pairs={{0,4},{1,5},{2,6},{3,7},{4,0},{5,1},{6,2},{7,3},{8,12},{9,13},{10,... | collective-permute-start | bytes 2580488 | tf_op jit(solution)/shard_map/ppermute | solution.py:331
  618.1 80.6 %collective-permute-start.84 = (bf16[2,192,1120]{2,1,0:T(8,128)(2,1)S(1)}, bf16[2,192,1120]{2,1,0:T(8,128)(2,1)S(1)}, u32[]{:S(2)}, u32[]{:S(2)}) collective-permute-start(bf16[2,192,1120]{2,1,0:T(8,128)(2,1)S(1)} %dynamic-slice_bitcast_fusion.6), channel_id=1, source_target_pairs={{0,4},{1,5},{2,6},{3,7},{4,0},{5,1},{6,2},{7,3},{8,12},{9,13},{10,... | collective-permute-start | bytes 2580488 | tf_op jit(solution)/shard_map/ppermute | solution.py:331
  658.4 234.5 %collective-permute-start.48 = (bf16[1024,1536]{1,0:T(8,128)(2,1)}, bf16[1024,1536]{1,0:T(8,128)(2,1)}, u32[]{:S(2)}, u32[]{:S(2)}) collective-permute-start(bf16[1024,1536]{1,0:T(8,128)(2,1)} %slice.853), channel_id=1, source_target_pairs={{0,8},{8,0},{16,24},{24,16},{1,9},{9,1},{17,25},{25,17},{2,10},{10... | collective-permute-start | bytes 9437192 | tf_op jit(solution)/shard_map/ppermute | solution.py:318
  717.6 156.5 %collective-permute-start.109 = (bf16[2,280,1536]{2,1,0:T(8,128)(2,1)}, bf16[2,280,1536]{2,1,0:T(8,128)(2,1)}, u32[]{:S(2)}, u32[]{:S(2)}) collective-permute-start(bf16[2,280,1536]{2,1,0:T(8,128)(2,1)} %pad_maximum_fusion.14), channel_id=1, source_target_pairs={{0,8},{8,0},{16,24},{24,16},{1,9},{9,1},{17,25},{25,17},{2,10},{10... | collective-permute-start | bytes 5160968 | tf_op jit(solution)/shard_map/ppermute | solution.py:318
  734.6 52.8 %collective-permute-start.85 = (bf16[192,1120]{1,0:T(8,128)(2,1)}, bf16[192,1120]{1,0:T(8,128)(2,1)}, u32[]{:S(2)}, u32[]{:S(2)}) collective-permute-start(bf16[192,1120]{1,0:T(8,128)(2,1)} %dynamic-slice_bitcast_fusion.9), channel_id=1, source_target_pairs={{0,2},{1,3},{2,0},{3,1},{4,6},{5,7},{6,4},{7,5},{8,10},{9,11},{10,... | collective-permute-start | bytes 1290248 | tf_op jit(solution)/shard_map/ppermute | solution.py:331
  735.0 65.2 %collective-permute-start.82 = (bf16[192,1120]{1,0:T(8,128)(2,1)}, bf16[192,1120]{1,0:T(8,128)(2,1)}, u32[]{:S(2)}, u32[]{:S(2)}) collective-permute-start(bf16[192,1120]{1,0:T(8,128)(2,1)} %dynamic-slice_bitcast_fusion.10), channel_id=1, source_target_pairs={{0,2},{1,3},{2,0},{3,1},{4,6},{5,7},{6,4},{7,5},{8,10},{9,11},{10,... | collective-permute-start | bytes 1290248 | tf_op jit(solution)/shard_map/ppermute | solution.py:331
  808.4 80.7 %collective-permute-start.64 = (bf16[512,1536]{1,0:T(8,128)(2,1)}, bf16[512,1536]{1,0:T(8,128)(2,1)}, u32[]{:S(2)}, u32[]{:S(2)}) collective-permute-start(bf16[512,1536]{1,0:T(8,128)(2,1)} %pad_maximum_fusion.16), channel_id=1, source_target_pairs={{0,8},{8,0},{16,24},{24,16},{1,9},{9,1},{17,25},{25,17},{2,10},{10... | collective-permute-start | bytes 4718600 | tf_op jit(solution)/shard_map/ppermute | solution.py:318
  857.3 66.9 %collective-permute-start.107 = (bf16[2,2,192,1120]{3,2,1,0:T(8,128)(2,1)}, bf16[2,2,192,1120]{3,2,1,0:T(8,128)(2,1)}, u32[]{:S(2)}, u32[]{:S(2)}) collective-permute-start(bf16[2,2,192,1120]{3,2,1,0:T(8,128)(2,1)} %pad_maximum_fusion.12), channel_id=1, source_target_pairs={{0,8},{8,0},{16,24},{24,16},{1,9},{9,1},{17,25},{25,17},{2,10},{10... | collective-permute-start | bytes 5160968 | tf_op jit(solution)/shard_map/ppermute | solution.py:318
  874.1 69.1 %collective-permute-start.105 = (bf16[2,2,192,1120]{3,2,1,0:T(8,128)(2,1)}, bf16[2,2,192,1120]{3,2,1,0:T(8,128)(2,1)}, u32[]{:S(2)}, u32[]{:S(2)}) collective-permute-start(bf16[2,2,192,1120]{3,2,1,0:T(8,128)(2,1)} %pad_maximum_fusion.11), channel_id=1, source_target_pairs={{0,8},{8,0},{16,24},{24,16},{1,9},{9,1},{17,25},{25,17},{2,10},{10... | collective-permute-start | bytes 5160968 | tf_op jit(solution)/shard_map/ppermute | solution.py:318
  (206 other events, 3399.8 us)

commit v3 on v2

--- a/solution.py
+++ b/solution.py
@@ -75,28 +75,28 @@
         for small in range(per)
     ]
 
-def pick_body(blk_count, ids, gate_ref, up_ref, gate_out, up_out):
+def pick_body(blk_count, ids, gate_ref, up_ref, out_ref):
     quarter = FF // blk_count // 4
     for k in range(4):
         @pl.when(ids[0] == k)
         def _(k=k):
-            for src, dst in ((gate_ref, gate_out), (up_ref, up_out)):
+            for which, src in enumerate((gate_ref, up_ref)):
                 for bit in range(2):
                     parts = [src[:, s:s + quarter] for s in strip_starts(blk_count, bit, k, quarter)]
-                    dst[ids[1] ^ bit] = jnp.concatenate(parts, axis=1).astype(jnp.bfloat16)
+                    out_ref[ids[1] ^ bit, which] = jnp.concatenate(parts, axis=1).astype(jnp.bfloat16)
 
 def pick_columns(ids, gate, up, blk_count):
     rows = gate.shape[0]
     step = 48 if rows % 48 == 0 else rows
     wide_here = FF // 8
     spec = pl.BlockSpec((step, FF), lambda i, ids: (i, 0))
-    out = pl.BlockSpec((2, step, wide_here), lambda i, ids: (0, i, 0))
-    shape = jax.ShapeDtypeStruct((2, rows, wide_here), jnp.bfloat16)
+    out = pl.BlockSpec((2, 2, step, wide_here), lambda i, ids: (0, 0, i, 0))
+    shape = jax.ShapeDtypeStruct((2, 2, rows, wide_here), jnp.bfloat16)
     return pl.pallas_call(
         functools.partial(pick_body, blk_count),
         grid_spec=pltpu.PrefetchScalarGridSpec(
-            num_scalar_prefetch=1, grid=(rows // step,), in_specs=[spec, spec], out_specs=[out, out]),
-        out_shape=[shape, shape],
+            num_scalar_prefetch=1, grid=(rows // step,), in_specs=[spec, spec], out_specs=out),
+        out_shape=shape,
         compiler_params=pltpu.CompilerParams(vmem_limit_bytes=VMEM),
         cost_estimate=pl.CostEstimate(flops=0, bytes_accessed=rows * FF * 10, transcendentals=0),
         name="pick_columns",
@@ -300,6 +300,84 @@
         name="attend_back",
     )(ids, q, kv, kv, seg_key, seg_query, o, do, lse, cosine, sine)
 
+def nn(a, b):
+    return jnp.dot(a, b, preferred_element_type=jnp.float32)
+
+
+def middle_body(h_ref, dy_ref, wg_ref, wu_ref, wd_ref, hid_ref, dg_ref, du_ref, dh_ref):
+    h = h_ref[...]
+    gate = nn(h, wg_ref[...])
+    up = nn(h, wu_ref[...])
+    sig = 1.0 / (1.0 + jnp.exp(-gate))
+    silu = gate * sig
+    hid_ref[...] = (silu * up).astype(jnp.bfloat16)
+    dhid = nt(dy_ref[...], wd_ref[...])
+    dg = (dhid * up * sig * (1.0 + gate * (1.0 - sig))).astype(jnp.bfloat16)
+    du = (dhid * silu).astype(jnp.bfloat16)
+    dg_ref[...] = dg
+    du_ref[...] = du
+    dh_ref[...] = (nt(dg, wg_ref[...]) + nt(du, wu_ref[...])).astype(jnp.bfloat16)
+
+def middle(h, dy, wg, wu, wd, step=256):
+    T, D = h.shape
+    F = wg.shape[1]
+    row = pl.BlockSpec((step, D), lambda i: (i, 0))
+    rowf = pl.BlockSpec((step, F), lambda i: (i, 0))
+    whole = lambda a: pl.BlockSpec(a.shape, lambda i: (0, 0), pipeline_mode=pl.Buffered(1))
+    return pl.pallas_call(
+        middle_body, grid=(T // step,),
+        in_specs=[row, row, whole(wg), whole(wu), whole(wd)],
+        out_specs=[rowf, rowf, rowf, row],
+        out_shape=[jax.ShapeDtypeStruct((T, F), jnp.bfloat16)] * 3 + [jax.ShapeDtypeStruct((T, D), jnp.bfloat16)],
+        compiler_params=pltpu.CompilerParams(vmem_limit_bytes=VMEM),
+        cost_estimate=pl.CostEstimate(flops=10 * T * D * F, bytes_accessed=40 * 2**20, transcendentals=T * F),
+        name="middle")(h, dy, wg, wu, wd)
+
+def two_grads_body(h_ref, a_ref, b_ref, ga_ref, gb_ref):
+    h = h_ref[...]
+    ga_ref[...] = tn(h, a_ref[...]).astype(jnp.bfloat16)
+    gb_ref[...] = tn(h, b_ref[...]).astype(jnp.bfloat16)
+
+def two_grads(h, a, b, step=256):
+    T, D = h.shape
+    F = a.shape[1]
+    col = pl.BlockSpec((T, step), lambda i: (0, i))
+    whole = lambda v: pl.BlockSpec(v.shape, lambda i: (0, 0), pipeline_mode=pl.Buffered(1))
+    out = pl.BlockSpec((step, F), lambda i: (i, 0))
+    return pl.pallas_call(two_grads_body, grid=(D // step,), in_specs=[col, whole(a), whole(b)], out_specs=[out, out],
+        out_shape=[jax.ShapeDtypeStruct((D, F), jnp.bfloat16)] * 2,
+        compiler_params=pltpu.CompilerParams(vmem_limit_bytes=VMEM),
+        cost_estimate=pl.CostEstimate(flops=4 * T * D * F, bytes_accessed=24 * 2**20, transcendentals=0),
+        name="two_grads")(h, a, b)
+
+def down_grad_body(hid_ref, dy_ref, g_ref):
+    g_ref[...] = tn(hid_ref[...], dy_ref[...]).astype(jnp.bfloat16)
+
+def down_grad(hid, dy, step=512):
+    T, F = hid.shape
+    D = dy.shape[1]
+    return pl.pallas_call(down_grad_body, grid=(D // step,),
+        in_specs=[pl.BlockSpec((T, F), lambda i: (0, 0), pipeline_mode=pl.Buffered(1)), pl.BlockSpec((T, step), lambda i: (0, i))],
+        out_specs=pl.BlockSpec((F, step), lambda i: (0, i)),
+        out_shape=jax.ShapeDtypeStruct((F, D), jnp.bfloat16),
+        compiler_params=pltpu.CompilerParams(vmem_limit_bytes=VMEM),
+        cost_estimate=pl.CostEstimate(flops=2 * T * D * F, bytes_accessed=16 * 2**20, transcendentals=0),
+        name="down_grad")(hid, dy)
+
+def down_body(hid_ref, wd_ref, o_ref):
+    o_ref[...] = nn(hid_ref[...], wd_ref[...]).astype(jnp.bfloat16)
+
+def down(hid, wd, step=256):
+    T, F = hid.shape
+    D = wd.shape[1]
+    return pl.pallas_call(down_body, grid=(T // step,),
+        in_specs=[pl.BlockSpec((step, F), lambda i: (i, 0)), pl.BlockSpec((F, D), lambda i: (0, 0), pipeline_mode=pl.Buffered(1))],
+        out_specs=pl.BlockSpec((step, D), lambda i: (i, 0)),
+        out_shape=jax.ShapeDtypeStruct((T, D), jnp.bfloat16),
+        compiler_params=pltpu.CompilerParams(vmem_limit_bytes=VMEM),
+        cost_estimate=pl.CostEstimate(flops=2 * T * D * F, bytes_accessed=16 * 2**20, transcendentals=0),
+        name="down")(hid, wd)
+
 
 CORE = [(0, 1), (1, 0), (2, 3), (3, 2)]
 CROSS = [(0, 2), (2, 0), (1, 3), (3, 1)]
@@ -399,20 +477,6 @@
     second = swap_cross(over[half:])
     chip = jnp.concatenate([values, cross, over, first, second])
     return jnp.concatenate([chip, swap_core(chip)])
-
-
-def scatter_tokens(values, bit):
-    half_all = values.shape[0] // 2
-    rows = half_all // 4
-    half = rows // 2
-    chip = wide(values[:half_all]) + wide(swap_core(low(values[half_all:])))
-    own, cross, over, far = (chip[rows * i : rows * (i + 1)] for i in range(4))
-    far = low(far)
-    first = wide(swap_blk(far[:half], bit))
-    second = wide(swap_cross(far[half:]))
-    cross = low(jnp.concatenate([cross[:half] + first, cross[half:]]))
-    over = low(jnp.concatenate([over[:half], over[half:] + second]))
-    return own + wide(swap_cross(cross)) + wide(swap_blk(over, bit))
 
 
 def angles_of(position):
@@ -459,16 +523,6 @@
             done.append(bit)
         parts.append(part)
     return jnp.concatenate(parts, axis=-1)
-
-
-def scatter_two_ways(values, bits, team):
-    lows = [bit for bit in bits if bit < team][::-1]
-    half = values.shape[-1] // 2
-    parts = [
-        scatter_bits(values[..., :half], bits, lows + [team]),
-        scatter_bits(values[..., half:], bits, [team] + lows),
-    ]
-    return scatter_bits(jnp.concatenate(parts, axis=-1), bits[:1], bits[:1])
 
 
 def gather_near_stacked(values):
@@ -594,17 +648,22 @@
     key_value = key_value.reshape(rows_here, block_len, 2 * KVD)
     kv_all = gather_two_ways(key_value, bits, team).reshape((blk_count,) + key_value.shape)
 
+    out_piece = weight_rows // 4
+    out_local = low(lax.dynamic_slice_in_dim(w_out, out_piece * grp, out_piece, 0))
+    out_full = lax.all_gather(out_local, ("blk", "grp"), axis=0, tiled=True)
     down_local = low(lax.dynamic_slice_in_dim(w_down, quarter * grp, quarter, 0))
     down_first = swap_blk(after(down_local, strip_first), bits[0])
-    gate_two, up_two = pick_columns(ids, w_gate, w_up, blk_count)
+    picked = pick_columns(ids, w_gate, w_up, blk_count)
     mine_team = blk_bit(team)
-
-    def pair_of(two):
-        got = swap_blk(two[1], team)
-        return jnp.stack([jnp.where(mine_team, got, two[0]), jnp.where(mine_team, two[0], got)])
-
-    gate_pair = pair_of(after(gate_two, strip_parts))
-    up_pair = pair_of(after(up_two, strip_parts))
+    picked_got = after(swap_blk(picked[1], team), strip_out)
+    pair = jnp.stack(
+        [jnp.where(mine_team, picked_got, picked[0]), jnp.where(mine_team, picked[0], picked_got)]
+    )
+    peers = [[i for i in range(blk_count) if (i & team) == t] for t in (0, team)]
+    pairs = lax.all_gather(pair, "blk", axis=0, axis_index_groups=peers)
+    pairs = pairs.reshape((2, blk_count // 4, 2, 2, weight_rows, ff_here)).transpose(3, 0, 2, 1, 4, 5)
+    gate_here = pairs[0].reshape(D, ff_here)
+    up_here = pairs[1].reshape(D, ff_here)
 
     def place(values, other, done, bit):
         mine = blk_bit(bit)
@@ -613,23 +672,22 @@
             [jnp.where(mine, other, values), jnp.where(mine, values, other)], axis=axis
         )
 
-    def finish(values, done):
-        for bit in lows:
-            values = place(values, swap_blk(values, bit), done, bit)
-            done = done + [bit]
-        return values
-
-    gate_first = swap_blk(after(gate_pair, strip_out), bits[0])
-    down_here = finish(place(down_local, after(down_first, strip_out), [], bits[0]), [bits[0]])
+    down_here = place(down_local, after(down_first, strip_out), [], bits[0])
+    done = [bits[0]]
+    for bit in lows:
+        other = after(swap_blk(down_here, bit), kv_all)
+        down_here = place(down_here, other, done, bit)
+        done.append(bit)
     down_here = down_here.reshape(ff_here, D)
-    up_first = swap_blk(after(up_pair, kv_all), bits[0])
-    gate_here = finish(place(gate_pair, after(gate_first, kv_all), [team], bits[0]), [team, bits[0]])
-    gate_here = gate_here.reshape(D, ff_here)
-
-    out_local = low(lax.dynamic_slice_in_dim(w_out, strip_q * grp, strip_q, 1))
-    out_strip = gather_bits(after(out_local, strip_first), bits).reshape(HQD, strip_q)
-    out_full = jnp.concatenate(gather_grp(out_strip), axis=1)
-    dy_team = gather_tokens(dy_low, team)
+
+    dy_half = token_count // 2
+    dy_send = after(dy_low, strip_parts)
+    dy_cross, dy_over = after((swap_cross(dy_send), swap_blk(dy_send, team)), strip_out)
+    dy_first = swap_blk(dy_cross[:dy_half], team)
+    dy_second = swap_cross(dy_over[dy_half:])
+    dy_first, dy_second = after((dy_first, dy_second), kv_all)
+    dy_chip = jnp.concatenate([dy_low, dy_cross, dy_over, dy_first, dy_second])
+    dy_team = jnp.concatenate([dy_chip, swap_core(dy_chip)])
 
     att_in, lse = attend(attend_ids, query, kv_all, seg_key, seg_query, block_len)
 
@@ -637,19 +695,27 @@
     resid = flat + jnp.dot(att_in, out_full, preferred_element_type=jnp.float32)
     h_two = low(norm_apply(resid, gain_two))
     h_team = gather_tokens(h_two, team)
-    up_here = finish(place(up_pair, after(up_first, h_two), [team], bits[0]), [team, bits[0]])
-    up_here = up_here.reshape(D, ff_here)
-    d_hidden = right_transposed(dy_team, down_here)
-    gate = jnp.dot(h_team, gate_here, preferred_element_type=jnp.float32)
-    up_proj = jnp.dot(h_team, up_here, preferred_element_type=jnp.float32)
-    hidden = low(swish_product(gate, up_proj))
-    down_grad = low(left_product(hidden, dy_team)).reshape((2,) + low_shape + (quarter, D))
-    swish_value, swish_back = jax.vjp(swish_product, gate, up_proj)
-    d_gate, d_up = swish_back(d_hidden)
-    d_gate = low(d_gate)
-    d_up = low(d_up)
-    d_htwo_part = right_transposed(d_gate, gate_here) + right_transposed(d_up, up_here)
-    d_htwo = scatter_tokens(d_htwo_part, team)
+    hidden, d_gate, d_up, d_htwo_part = middle(h_team, dy_team, gate_here, up_here, down_here)
+    chip_rows = 4 * token_count
+    half = token_count // 2
+
+    def chip_sum(values, came):
+        return low(wide(values[:chip_rows]) + wide(came))
+
+    def scatter_far(chip):
+        far = chip[3 * token_count :]
+        return swap_blk(far[:half], team), swap_cross(far[half:])
+
+    def scatter_near(chip, first, second):
+        cross, over = (chip[token_count * i : token_count * (i + 1)] for i in (1, 2))
+        cross = jnp.concatenate([low(wide(cross[:half]) + wide(first)), cross[half:]])
+        over = jnp.concatenate([over[:half], low(wide(over[half:]) + wide(second))])
+        return swap_cross(cross), swap_blk(over, team)
+
+    d_came = swap_core(d_htwo_part[chip_rows:])
+    down_grad_part = down_grad(hidden, dy_team).reshape((2,) + low_shape + (quarter, D))
+    d_chip = chip_sum(d_htwo_part, after(d_came, down_grad_part))
+    d_far = scatter_far(d_chip)
 
     def share_start(grad, axes):
         bit = lows[-1]
@@ -679,15 +745,18 @@
         )
 
     down_axes = [bits[0]] + lows
-    down_keep, down_got = share_start(down_grad, down_axes)
-    late_gate, late_up = after((d_gate, d_up), d_htwo_part)
+    down_keep, down_got = share_start(down_grad_part, down_axes)
+    late_gate, late_up = after((d_gate, d_up), d_chip)
     column_shape = (2, 2) + low_shape + (weight_rows, ff_here)
-    gate_grad = low(left_product(h_team, late_gate)).reshape(column_shape)
-    gate_keep, gate_got = share_start(gate_grad, bits)
-    up_grad = low(left_product(h_team, late_up)).reshape(column_shape)
-    up_keep, up_got = share_start(up_grad, bits)
-    down_keep, down_got = share_mid(*after((down_keep, down_got), d_gate), down_axes)
-    out_part = jnp.dot(after(hidden, up_grad), down_here, preferred_element_type=jnp.float32)
+    gate_grad, up_grad = two_grads(h_team, late_gate, late_up)
+    gate_keep, gate_got = share_start(gate_grad.reshape(column_shape), bits)
+    d_far = after(d_far, gate_grad)
+    d_cross, d_over = scatter_near(d_chip, *d_far)
+    out_part = down(after(hidden, d_far), down_here)
+    out_came = swap_core(out_part[chip_rows:])
+    down_keep, down_got = share_mid(*after((down_keep, down_got), out_part), down_axes)
+    d_cross, d_over = after((d_cross, d_over), out_part)
+    d_htwo = wide(d_chip[:token_count]) + wide(d_cross) + wide(d_over)
 
     norm_value_two, norm_back_two = jax.vjp(norm_apply, resid, gain_two)
     d_resid_norm, grad_gain_two = norm_back_two(d_htwo)
@@ -710,14 +779,22 @@
         jnp.concatenate([sine, sine], axis=1),
         block_len,
     )
-    gate_keep, gate_got = share_mid(*after((gate_keep, gate_got), d_attended), bits)
+    gate_keep, gate_got = share_mid(*after((gate_keep, gate_got), d_query), bits)
     share_down = low(wide(down_keep) + wide(after(down_got, d_query)))
     dkv = dkv.reshape((2,) * len(bits) + (rows_here, block_len, 2 * KVD))
-    dkv = wide(scatter_two_ways(dkv, bits, team)).reshape(token_count, 2, KVH, HD)
+    dkv_first = scatter_bits(dkv[..., :KVD], bits, lows[::-1])
+    dkv_second = scatter_bits(dkv[..., KVD:], bits, [team])
+    up_keep, up_got = share_start(after(up_grad, dkv_first).reshape(column_shape), bits)
+    dkv_first = scatter_bits(dkv_first, bits[:2], [team])
+    dkv_second = scatter_bits(dkv_second, [bits[0]] + lows, lows[::-1])
+    dkv = jnp.concatenate([dkv_first, dkv_second], axis=-1)
+    out_chip = chip_sum(out_part, after(out_came, dkv_first))
+    dkv = wide(scatter_bits(dkv, bits[:1], bits[:1])).reshape(token_count, 2, KVH, HD)
     d_key = low(rotate_by(dkv[:, 0], cosine[:, None], -sine[:, None]))
     d_value = low(dkv[:, 1])
-    up_keep, up_got = share_mid(*after((up_keep, up_got), d_query), bits)
-    out_tokens = low(resid + scatter_tokens(after(out_part, d_query), team))
+    out_far = after(scatter_far(out_chip), d_key)
+    out_cross, out_over = scatter_near(out_chip, *out_far)
+    up_keep, up_got = share_mid(*after((up_keep, up_got), d_key), bits)
 
     def to_strips(parts):
         parts = by_place(parts)
@@ -740,6 +817,8 @@
             for part in (d_query, d_key.reshape(token_count, KVD), d_value.reshape(token_count, KVD))
         ]
     )
+    out_cross, out_over = after((out_cross, out_over), near_dkv)
+    out_tokens = low(resid + wide(out_chip[:token_count]) + wide(out_cross) + wide(out_over))
     near_hone = right_transposed(near_dq, strip[:, :strip_q]) + right_transposed(
         near_dkv, strip[:, strip_q:]
     )
@@ -778,6 +857,12 @@
     kv_parts = gather_grp(share_kv)
     grad_attend = jnp.concatenate(query_parts + [kv_parts[k] for k in (0, 2, 1, 3)], axis=1)
 
+    sides = low(near_hone[token_count : 2 * token_count]), low(near_hone[3 * token_count :])
+    other = wide(swap_core(jnp.concatenate(sides)))
+    d_hone = near_hone[:token_count] + other[:token_count]
+    d_hone_cross = swap_cross(
+        low(near_hone[2 * token_count : 3 * token_count] + other[token_count:])
+    )
     square_sum = square_total(
         [
             wide(s)
@@ -791,23 +876,19 @@
     square_sum = square_sum + swap_core(square_sum)
     grad_norm = jnp.sqrt(square_sum[0, 0])
     factor = jnp.minimum(1.0, CLIP_NORM / (grad_norm + 1e-06))
-
-    half = low(near_hone[token_count : 2 * token_count]), low(near_hone[3 * token_count :])
-    other = wide(swap_core(jnp.concatenate(half)))
-    d_hone = near_hone[:token_count] + other[:token_count]
-    d_hone = d_hone + wide(
-        swap_cross(low(near_hone[2 * token_count : 3 * token_count] + other[token_count:]))
+    factor = after(factor, out_tokens)
+
+    new_first_gate, new_second_gate, new_gate = adam_columns(
+        ids, factor[None], near_gate, w_gate, first_gate, second_gate, blk_count, RATE_GATE, WEIGHT_DECAY
+    )
+    new_first_up, new_second_up, new_up = adam_columns(
+        ids, factor[None], near_up, w_up, first_up, second_up, blk_count, RATE_GATE, WEIGHT_DECAY
     )
     norm_value_one, norm_back_one = jax.vjp(norm_apply, flat, gain_one)
+    d_hone = after(d_hone + wide(after(d_hone_cross, new_gate)), new_gate)
     d_flat_norm, unused_gain = norm_back_one(d_hone)
     grad_tokens = low(d_resid + d_flat_norm)
 
-    new_first_gate, new_second_gate, new_gate = adam_columns(
-        ids, factor[None], near_gate, w_gate, first_gate, second_gate, blk_count, RATE_GATE, WEIGHT_DECAY
-    )
-    new_first_up, new_second_up, new_up = adam_columns(
-        ids, factor[None], near_up, w_up, first_up, second_up, blk_count, RATE_GATE, WEIGHT_DECAY
-    )
     new_first_attend, new_second_attend, new_attend = adam_step(
         w_attend, factor * wide(grad_attend), first_attend, second_attend, RATE_ATTEND, WEIGHT_DECAY
     )

time: 976 us -> 902 us (0.924)
  matrix products: 144 us -> 24.8 us
  Pallas kernels: 52.7 us -> 165 us
  waiting for transfers between devices: 442 us -> 368 us
  between operations: 10 us -> 23.1 us
  starting transfers between devices: 111 us -> 99.7 us
    pallas_call x0 -> x4, Pallas kernels: none -> 112 us  [the longest x1 66.1 us: middle(): pl.pallas_call(middle_body, grid=(T // step,), in_specs=[row, row, whole(...]
    ppermute x60 -> x52, waiting for transfers between devices: 376 us -> 316 us  [swap_blk(): return lax.ppermute(values, 'blk', [(i, i ^ bit) for i in range(count)])]
    dot_general x6 -> x3, matrix products: 57.8 us -> 11.5 us  [right_transposed(): lax.dot_general(left_side, right_side, (((1,), (1,)), ((), ())), preferre...]
    dot_general x6 -> x3, matrix products: 44.9 us -> 6.94 us  [left_product(): lax.dot_general(left_side, right_side, (((0,), (0,)), ((), ())), preferre...]
    dot_general x3 -> x0, matrix products: 36.4 us -> none  [the longest x1 13.9 us: on_device(): jnp.dot(after(hidden, up_grad), down_here, preferred_element_type=jnp.flo...]
    ppermute x25 -> x24, waiting for transfers between devices: 59.1 us -> 45.1 us  [swap_cross(): return lax.ppermute(values, 'grp', CROSS)]
    ppermute x60 -> x52, starting transfers between devices: 83.5 us -> 71.4 us  [swap_blk(): return lax.ppermute(values, 'blk', [(i, i ^ bit) for i in range(count)])]
    another operation x9 -> x3, other arithmetic: 15.7 us -> 4.14 us  [the longest x2 2.75 us: on_device(): jnp.stack([jnp.where(mine_team, picked_got, picked[0]), jnp.where(mine_te...]
  transfers between devices with their start and end apart: 110 -> 102, of which waited for: 49 -> 48; matrix products, arithmetic and copies ran while one was open for 26% -> 25% of each run, Pallas kernels for 5% -> 17%
where the time goes in v3:
time: 902 us; the launch traced here: 891 us
  waiting for transfers between devices  368 us (41%)
  Pallas kernels  165 us (18%)
  other arithmetic  131 us (15%)
  starting transfers between devices  99.7 us (11%)
  local copies, waits for them, and re-layouts  78.8 us (9%)
  matrix products  24.8 us (3%)
  between operations  23.1 us (3%)
    ppermute x52, waiting for transfers between devices, swap_blk(): return lax.ppermute(values, 'blk', [(i, i ^ bit) for i in range(count)])  316 us
    ppermute x52, starting transfers between devices, swap_blk(): return lax.ppermute(values, 'blk', [(i, i ^ bit) for i in range(count)])  71.4 us
    pallas_call x1, Pallas kernels, middle(): pl.pallas_call(middle_body, grid=(T // step,), in_specs=[row, row, whole(...  66.1 us
    ppermute x24, waiting for transfers between devices, swap_cross(): return lax.ppermute(values, 'grp', CROSS)  45.1 us
    pallas_call x2, Pallas kernels, adam_columns(): pl.pallas_call(functools.partial(adam_body, blk_count, rate, decay), grid...  34.7 us
    convert_element_type x26, other arithmetic, low(): return values.astype(jnp.bfloat16)  31.2 us
    sub x4, other arithmetic, adam_step(): weight - rate * (first_hat / (jnp.sqrt(second_hat) + ADAM_EPS) + decay *...  24.2 us
    pallas_call x1, Pallas kernels, two_grads(): pl.pallas_call(two_grads_body, grid=(D // step,), in_specs=[col, whole(a)...  22.4 us
  transfers between devices with their start and end apart: 102, of which 48 were waited for; matrix products, arithmetic and copies ran while one was open for 25% of the time, Pallas kernels for 17%

profile of v3, /device:TPU:0, one launch (start us, length us, event | category | flops | bytes accessed | tf_op | source)
XLA Modules:
  0.0 890.9 jit_solution(14213356061845277525)
XLA Ops:
  43.3 30.3 %collective-permute-done.1 = bf16[2,896]{1,0:T(2,128)(2,1)S(1)} collective-permute-done((bf16[2,896]{1,0:T(2,128)(2,1)S(1)}, bf16[2,896]{1,0:T(2,128)(2,1)S(1)}, u32[]{:S(2)}, u32[]{:S(2)}) %collective-permute-start.1) | collective-permute-done | bytes 3616 | tf_op jit(solution)/shard_map/ppermute | solution.py:409
  97.5 8.2 collective-permute-done.7
  128.8 25.5 %collective-permute-done.26 = bf16[256,1536]{1,0:T(8,128)(2,1)S(1)} collective-permute-done((bf16[256,1536]{1,0:T(8,128)(2,1)}, bf16[256,1536]{1,0:T(8,128)(2,1)S(1)}, u32[]{:S(2)}, u32[]{:S(2)}) %collective-permute-start.26) | collective-permute-done | bytes 786464 | tf_op jit(solution)/shard_map/ppermute | solution.py:409
  165.0 18.3 %collective-permute-done.15 = bf16[2,128,512]{2,1,0:T(8,128)(2,1)S(1)} collective-permute-done((bf16[2,128,512]{2,1,0:T(8,128)(2,1)S(1)}, bf16[2,128,512]{2,1,0:T(8,128)(2,1)S(1)}, u32[]{:S(2)}, u32[]{:S(2)}) %collective-permute-start.15) | collective-permute-done | bytes 262176 | tf_op jit(solution)/shard_map/ppermute | solution.py:409
  186.8 8.2 collective-permute-done.18
  204.3 14.4 %collective-permute-done.19 = bf16[2,2,2,128,256]{4,3,2,1,0:T(8,128)(2,1)S(1)} collective-permute-done((bf16[2,2,2,128,256]{4,3,2,1,0:T(8,128)(2,1)S(1)}, bf16[2,2,2,128,256]{4,3,2,1,0:T(8,128)(2,1)S(1)}, u32[]{:S(2)}, u32[]{:S(2)}) %collective-permute-start.19) | collective-permute-done | bytes 524320 | tf_op jit(solution)/shard_map/ppermute | solution.py:409
  218.8 57.3 %collective-permute-done.17 = bf16[2,2,2,128,256]{4,3,2,0,1:T(8,128)(2,1)S(1)} collective-permute-done((bf16[2,2,2,128,256]{4,3,2,0,1:T(8,128)(2,1)S(1)}, bf16[2,2,2,128,256]{4,3,2,0,1:T(8,128)(2,1)S(1)}, u32[]{:S(2)}, u32[]{:S(2)}) %collective-permute-start.17) | collective-permute-done | bytes 524320 | tf_op jit(solution)/shard_map/ppermute | solution.py:409
  293.9 10.6 %collective-permute-done.20 = bf16[256,1536]{1,0:T(8,128)(2,1)S(1)} collective-permute-done((bf16[256,1536]{1,0:T(8,128)(2,1)S(1)}, bf16[256,1536]{1,0:T(8,128)(2,1)S(1)}, u32[]{:S(2)}, u32[]{:S(2)}) %collective-permute-start.20) | collective-permute-done | bytes 786464 | tf_op jit(solution)/shard_map/ppermute | solution.py:400
  335.0 66.1 %middle.1 = (bf16[2048,1120]{1,0:T(8,128)(2,1)}, bf16[2048,1120]{1,0:T(8,128)(2,1)}, bf16[2048,1120]{1,0:T(8,128)(2,1)}, bf16[2048,1536]{1,0:T(8,128)(2,1)}) custom-call(bf16[2048,1536]{1,0:T(8,128)(2,1)} %constant_dynamic-update-slice_fusion.5.h_ref, bf16[2048,1536]{1,0:T(8,128)(2,1)} %constant_dynamic-update-slice_fusion.16.dy_ref, ...), custom_call_target="tpu_custom_call" | custom-call | flops 35232153600 | bytes 41943040 | tf_op jit(solution)/shard_map/middle/pallas_call | solution.py:327
  415.7 11.1 %down_grad.1 = bf16[1120,1536]{1,0:T(8,128)(2,1)S(1)} custom-call(bf16[2048,1120]{1,0:T(8,128)(2,1)} %get-tuple-element.93.hid_ref, bf16[2048,1536]{1,0:T(8,128)(2,1)} %constant_dynamic-update-slice_fusion.16.dy_ref), custom_call_target="tpu_custom_call" | custom-call | flops 7046430720 | bytes 16777216 | tf_op jit(solution)/shard_map/down_grad/pallas_call | solution.py:359
  435.3 22.4 %two_grads.1 = (bf16[1536,1120]{1,0:T(8,128)(2,1)S(1)}, bf16[1536,1120]{1,0:T(8,128)(2,1)}) custom-call(bf16[2048,1536]{1,0:T(8,128)(2,1)} %constant_dynamic-update-slice_fusion.5.h_ref, bf16[2048,1120]{1,0:T(8,128)(2,1)} %get-tuple-element.88.a_ref, bf16[2048,1120]{1,0:T(8,128)(2,1)} %get-tuple-element.89.b_ref), custom_call_target="tpu_custom_call" | custom-call | flops 14092861440 | bytes 25165824 | tf_op jit(solution)/shard_map/two_grads/pallas_call | solution.py:347
  460.3 12.0 %down.1 = bf16[2048,1536]{1,0:T(8,128)(2,1)} custom-call(bf16[2048,1120]{1,0:T(8,128)(2,1)} %get-tuple-element.93.hid_ref, bf16[1120,1536]{1,0:T(8,128)(2,1)S(1)} %bitcast.467), custom_call_target="tpu_custom_call" | custom-call | flops 7046430720 | bytes 16777216 | tf_op jit(solution)/shard_map/down/pallas_call | solution.py:373
  486.6 9.9 %collective-permute-done.37 = bf16[256,1536]{1,0:T(8,128)(2,1)S(1)} collective-permute-done((bf16[256,1536]{1,0:T(8,128)(2,1)S(1)}, bf16[256,1536]{1,0:T(8,128)(2,1)S(1)}, u32[]{:S(2)}, u32[]{:S(2)}) %collective-permute-start.37) | collective-permute-done | bytes 786464 | tf_op jit(solution)/shard_map/ppermute | solution.py:400
  496.5 16.4 %collective-permute-done.38 = bf16[256,1536]{1,0:T(8,128)(2,1)S(1)} collective-permute-done((bf16[256,1536]{1,0:T(8,128)(2,1)S(1)}, bf16[256,1536]{1,0:T(8,128)(2,1)S(1)}, u32[]{:S(2)}, u32[]{:S(2)}) %collective-permute-start.38) | collective-permute-done | bytes 786464 | tf_op jit(solution)/shard_map/ppermute | solution.py:409
  520.9 8.4 attend_back.1
  578.4 11.5 %collective-permute-done.67 = bf16[2,2,192,384]{3,2,0,1:T(8,128)(2,1)S(1)} collective-permute-done((bf16[2,2,192,384]{3,2,0,1:T(8,128)(2,1)S(1)}, bf16[2,2,192,384]{3,2,0,1:T(8,128)(2,1)S(1)}, u32[]{:S(2)}, u32[]{:S(2)}) %collective-permute-start.67) | collective-permute-done | bytes 589856 | tf_op jit(solution)/shard_map/ppermute | solution.py:409
  656.9 16.9 %collective-permute-done.82 = f32[640]{0:T(1024)S(1)} collective-permute-done((f32[640]{0:T(1024)S(1)}, f32[640]{0:T(1024)S(1)}, u32[]{:S(2)}, u32[]{:S(2)}) %collective-permute-start.82) | collective-permute-done | bytes 2592 | tf_op jit(solution)/shard_map/ppermute | solution.py:409
  712.9 10.6 %collective-permute-done.72 = bf16[192,1120]{1,0:T(8,128)(2,1)S(1)} collective-permute-done((bf16[192,1120]{1,0:T(8,128)(2,1)S(1)}, bf16[192,1120]{1,0:T(8,128)(2,1)S(1)}, u32[]{:S(2)}, u32[]{:S(2)}) %collective-permute-start.72) | collective-permute-done | bytes 430112 | tf_op jit(solution)/shard_map/ppermute | solution.py:409
  748.0 9.1 %collective-permute-done.41 = bf16[128,1536]{1,0:T(8,128)(2,1)S(1)} collective-permute-done((bf16[128,1536]{1,0:T(8,128)(2,1)S(1)}, bf16[128,1536]{1,0:T(8,128)(2,1)S(1)}, u32[]{:S(2)}, u32[]{:S(2)}) %collective-permute-start.41) | collective-permute-done | bytes 393248 | tf_op jit(solution)/shard_map/ppermute | solution.py:409
  757.1 13.1 %collective-permute-done.74 = bf16[2,192,1120]{2,1,0:T(8,128)(2,1)S(1)} collective-permute-done((bf16[2,192,1120]{2,1,0:T(8,128)(2,1)S(1)}, bf16[2,192,1120]{2,1,0:T(8,128)(2,1)S(1)}, u32[]{:S(2)}, u32[]{:S(2)}) %collective-permute-start.74) | collective-permute-done | bytes 860192 | tf_op jit(solution)/shard_map/ppermute | solution.py:409
  771.6 11.0 %collective-permute-done.75 = bf16[192,1120]{1,0:T(8,128)(2,1)S(1)} collective-permute-done((bf16[192,1120]{1,0:T(8,128)(2,1)S(1)}, bf16[192,1120]{1,0:T(8,128)(2,1)S(1)}, u32[]{:S(2)}, u32[]{:S(2)}) %collective-permute-start.75) | collective-permute-done | bytes 430112 | tf_op jit(solution)/shard_map/ppermute | solution.py:409
  813.3 18.0 %multiply_subtract_fusion = (f32[1120,1536]{1,0:T(8,128)}, f32[1120,1536]{1,0:T(8,128)}, f32[1120,1536]{1,0:T(8,128)}) fusion(f32[1120,1536]{1,0:T(8,128)} %param.30, bf16[280,1536]{1,0:T(8,128)(2,1)} %get-tuple-element.170, bf16[280,1536]{1,0:T(8,128)(2,1)} %get-tuple-element.169, bf16[280,1536]{1,0:T(8,128)(2,1)} %get-tuple-element.168, ...), kind=kLoop, calls=%fused_computation.6 | loop fusion | flops 41287680 | bytes 44728324 | tf_op jit(solution)/shard_map/sub | solution.py:66
  841.6 17.5 %adam_columns.2 = (f32[192,8960]{1,0:T(8,128)}, f32[192,8960]{1,0:T(8,128)}, f32[192,8960]{1,0:T(8,128)}) custom-call(s32[2]{0:T(128)S(1)} %copy-done.8, f32[1]{0:T(128)} %bitcast.132.factor_ref, bf16[4,2,192,1120]{3,2,1,0:T(8,128)(2,1)S(1)} %pad_maximum_fusion.grad_ref, f32[192,8960]{1,0:T(8,128)} %w_ref.2, f32[192,8960]{1,0:T(8,128)} %m_ref.2, ...), custom_call_target="tpu_custom_call" | custom-call | flops 34406400 | bytes 44728320 | tf_op jit(solution)/shard_map/adam_columns/pallas_call | solution.py:131
  865.3 17.2 %adam_columns.3 = (f32[192,8960]{1,0:T(8,128)}, f32[192,8960]{1,0:T(8,128)}, f32[192,8960]{1,0:T(8,128)}) custom-call(s32[2]{0:T(128)S(1)} %copy-done.8, f32[1]{0:T(128)} %bitcast.132.factor_ref, bf16[4,2,192,1120]{3,2,1,0:T(8,128)(2,1)S(1)} %pad_maximum_fusion.1.grad_ref, f32[192,8960]{1,0:T(8,128)} %w_ref.3, f32[192,8960]{1,0:T(8,128)} %m_ref.3, ...), custom_call_target="tpu_custom_call" | custom-call | flops 34406400 | bytes 44728320 | tf_op jit(solution)/shard_map/adam_columns/pallas_call | solution.py:131
  (671 shorter events, 423.7 us)
Async XLA Ops:
  7.2 274.8 %all-gather.4.cloned.1.call-start = ((), (), s32[]{:S(2)}) async-start(), calls=%async_computation | async-start | bytes 4866048 | tf_op jit(solution)/shard_map/all_gather | solution.py:653
  8.9 314.7 %all-gather.6.cloned.1.call-start = ((), (), s32[]{:S(2)}) async-start(), calls=%async_computation.1 | async-start | bytes 8847360 | tf_op jit(solution)/shard_map/all_gather | solution.py:663
  17.5 64.9 %collective-permute-start.5 = (bf16[192,512]{1,0:T(8,128)(2,1)}, bf16[192,512]{1,0:T(8,128)(2,1)}, u32[]{:S(2)}, u32[]{:S(2)}) collective-permute-start(bf16[192,512]{1,0:T(8,128)(2,1)} %pad_maximum_fusion.35), channel_id=1, source_target_pairs={{0,4},{1,5},{2,6},{3,7},{4,0},{5,1},{6,2},{7,3},{8,12},{9,13},{10,... | collective-permute-start | bytes 589832 | tf_op jit(solution)/shard_map/ppermute | solution.py:409
  17.5 69.9 %collective-permute-start.3 = (bf16[256,1536]{1,0:T(8,128)(2,1)}, bf16[256,1536]{1,0:T(8,128)(2,1)S(1)}, u32[]{:S(2)}, u32[]{:S(2)}) collective-permute-start(bf16[256,1536]{1,0:T(8,128)(2,1)} %bitcast.471), channel_id=1, source_target_pairs={{0,16},{16,0},{8,24},{24,8},{1,17},{17,1},{9,25},{25,9},{2,18},{18... | collective-permute-start | bytes 2359304 | tf_op jit(solution)/shard_map/ppermute | solution.py:400
  27.1 92.2 %collective-permute-start.30 = (bf16[2,192,1120]{2,1,0:T(8,128)(2,1)}, bf16[2,192,1120]{2,1,0:T(8,128)(2,1)}, u32[]{:S(2)}, u32[]{:S(2)}) collective-permute-start(bf16[2,192,1120]{2,1,0:T(8,128)(2,1)} %slice_bitcast_fusion.1), channel_id=1, source_target_pairs={{0,2},{1,3},{2,0},{3,1},{4,6},{5,7},{6,4},{7,5},{8,10},{9,11},{10,... | collective-permute-start | bytes 2580488 | tf_op jit(solution)/shard_map/ppermute | solution.py:409
  37.9 121.0 %collective-permute-start.31 = (bf16[280,1536]{1,0:T(8,128)(2,1)}, bf16[280,1536]{1,0:T(8,128)(2,1)}, u32[]{:S(2)}, u32[]{:S(2)}) collective-permute-start(bf16[280,1536]{1,0:T(8,128)(2,1)} %dynamic-slice_convert_fusion), channel_id=1, source_target_pairs={{0,4},{1,5},{2,6},{3,7},{4,0},{5,1},{6,2},{7,3},{8,12},{9,13},{10,... | collective-permute-start | bytes 2580488 | tf_op jit(solution)/shard_map/ppermute | solution.py:409
  156.3 133.9 %collective-permute-start.27 = (bf16[128,1536]{1,0:T(8,128)(2,1)}, bf16[128,1536]{1,0:T(8,128)(2,1)}, u32[]{:S(2)}, u32[]{:S(2)}) collective-permute-start(bf16[128,1536]{1,0:T(8,128)(2,1)} %slice.332), channel_id=1, source_target_pairs={{0,2},{1,3},{2,0},{3,1},{4,6},{5,7},{6,4},{7,5},{8,10},{9,11},{10,... | collective-permute-start | bytes 1179656 | tf_op jit(solution)/shard_map/ppermute | solution.py:409
  158.8 131.5 %collective-permute-start.28 = (bf16[128,1536]{1,0:T(8,128)(2,1)}, bf16[128,1536]{1,0:T(8,128)(2,1)}, u32[]{:S(2)}, u32[]{:S(2)}) collective-permute-start(bf16[128,1536]{1,0:T(8,128)(2,1)} %slice.333), channel_id=1, source_target_pairs={{0,16},{16,0},{8,24},{24,8},{1,17},{17,1},{9,25},{25,9},{2,18},{18... | collective-permute-start | bytes 1179656 | tf_op jit(solution)/shard_map/ppermute | solution.py:400
  185.3 131.1 %collective-permute-start.32 = (bf16[2,280,1536]{2,1,0:T(8,128)(2,1)}, bf16[2,280,1536]{2,1,0:T(8,128)(2,1)}, u32[]{:S(2)}, u32[]{:S(2)}) collective-permute-start(bf16[2,280,1536]{2,1,0:T(8,128)(2,1)} %pad_maximum_fusion.8), channel_id=1, source_target_pairs={{0,1},{1,0},{2,3},{3,2},{4,5},{5,4},{6,7},{7,6},{8,9},{9,8},{10,11... | collective-permute-start | bytes 5160968 | tf_op jit(solution)/shard_map/ppermute | solution.py:409
  201.7 74.5 %collective-permute-start.17 = (bf16[2,2,2,128,256]{4,3,2,0,1:T(8,128)(2,1)S(1)}, bf16[2,2,2,128,256]{4,3,2,0,1:T(8,128)(2,1)S(1)}, u32[]{:S(2)}, u32[]{:S(2)}) collective-permute-start(bf16[2,2,2,128,256]{4,3,2,0,1:T(8,128)(2,1)S(1)} %pad_maximum_fusion.25), channel_id=1, source_target_pairs={{0,1},{1,0},{2,3},{3,2},{4,5},{5,4},{6,7},{7,6},{8,9},{9,8},{10,11... | collective-permute-start | bytes 1572872 | tf_op jit(solution)/shard_map/ppermute | solution.py:409
  315.9 89.0 %collective-permute-start.62 = (bf16[256,1536]{1,0:T(8,128)(2,1)S(1)}, bf16[256,1536]{1,0:T(8,128)(2,1)}, u32[]{:S(2)}, u32[]{:S(2)}) collective-permute-start(bf16[256,1536]{1,0:T(8,128)(2,1)S(1)} %copy-done.6), channel_id=1, source_target_pairs={{0,16},{16,0},{8,24},{24,8},{1,17},{17,1},{9,25},{25,9},{2,18},{18... | collective-permute-start | bytes 2359304 | tf_op jit(solution)/shard_map/ppermute | solution.py:400
  429.0 50.2 %collective-permute-start.76 = (bf16[2,280,1536]{2,1,0:T(8,128)(2,1)}, bf16[2,280,1536]{2,1,0:T(8,128)(2,1)}, u32[]{:S(2)}, u32[]{:S(2)}) collective-permute-start(bf16[2,280,1536]{2,1,0:T(8,128)(2,1)} %get-tuple-element.171), channel_id=1, source_target_pairs={{0,1},{1,0},{2,3},{3,2},{4,5},{5,4},{6,7},{7,6},{8,9},{9,8},{10,11... | collective-permute-start | bytes 5160968 | tf_op jit(solution)/shard_map/ppermute | solution.py:409
  459.2 109.3 %collective-permute-start.70 = (bf16[2,2,192,1120]{3,2,1,0:T(8,128)(2,1)}, bf16[2,2,192,1120]{3,2,1,0:T(8,128)(2,1)}, u32[]{:S(2)}, u32[]{:S(2)}) collective-permute-start(bf16[2,2,192,1120]{3,2,1,0:T(8,128)(2,1)} %get-tuple-element.165), channel_id=1, source_target_pairs={{0,1},{1,0},{2,3},{3,2},{4,5},{5,4},{6,7},{7,6},{8,9},{9,8},{10,11... | collective-permute-start | bytes 5160968 | tf_op jit(solution)/shard_map/ppermute | solution.py:409
  476.1 254.3 %collective-permute-start.36 = (bf16[1024,1536]{1,0:T(8,128)(2,1)}, bf16[1024,1536]{1,0:T(8,128)(2,1)}, u32[]{:S(2)}, u32[]{:S(2)}) collective-permute-start(bf16[1024,1536]{1,0:T(8,128)(2,1)} %slice.432), channel_id=1, source_target_pairs={{0,8},{8,0},{16,24},{24,16},{1,9},{9,1},{17,25},{25,17},{2,10},{10... | collective-permute-start | bytes 9437192 | tf_op jit(solution)/shard_map/ppermute | solution.py:396
  481.1 52.7 %collective-permute-start.77 = (bf16[280,1536]{1,0:T(8,128)(2,1)S(1)}, bf16[280,1536]{1,0:T(8,128)(2,1)}, u32[]{:S(2)}, u32[]{:S(2)}) collective-permute-start(bf16[280,1536]{1,0:T(8,128)(2,1)S(1)} %dynamic-slice_bitcast_fusion.8), channel_id=1, source_target_pairs={{0,4},{1,5},{2,6},{3,7},{4,0},{5,1},{6,2},{7,3},{8,12},{9,13},{10,... | collective-permute-start | bytes 2580488 | tf_op jit(solution)/shard_map/ppermute | solution.py:409
  553.8 44.4 %collective-permute-start.98 = (bf16[280,1536]{1,0:T(8,128)(2,1)S(1)}, bf16[280,1536]{1,0:T(8,128)(2,1)S(1)}, u32[]{:S(2)}, u32[]{:S(2)}) collective-permute-start(bf16[280,1536]{1,0:T(8,128)(2,1)S(1)} %get-tuple-element.146), channel_id=1, source_target_pairs={{0,16},{16,0},{8,24},{24,8},{1,17},{17,1},{9,25},{25,9},{2,18},{18... | collective-permute-start | bytes 2580488 | tf_op jit(solution)/shard_map/ppermute | solution.py:400
  589.9 137.6 %collective-permute-start.73 = (bf16[2,2,192,1120]{3,2,1,0:T(8,128)(2,1)}, bf16[2,2,192,1120]{3,2,1,0:T(8,128)(2,1)}, u32[]{:S(2)}, u32[]{:S(2)}) collective-permute-start(bf16[2,2,192,1120]{3,2,1,0:T(8,128)(2,1)} %get-tuple-element.163), channel_id=1, source_target_pairs={{0,1},{1,0},{2,3},{3,2},{4,5},{5,4},{6,7},{7,6},{8,9},{9,8},{10,11... | collective-permute-start | bytes 5160968 | tf_op jit(solution)/shard_map/ppermute | solution.py:409
  624.8 67.6 %collective-permute-start.71 = (bf16[2,192,1120]{2,1,0:T(8,128)(2,1)}, bf16[2,192,1120]{2,1,0:T(8,128)(2,1)}, u32[]{:S(2)}, u32[]{:S(2)}) collective-permute-start(bf16[2,192,1120]{2,1,0:T(8,128)(2,1)} %dynamic-slice_bitcast_fusion.7), channel_id=1, source_target_pairs={{0,4},{1,5},{2,6},{3,7},{4,0},{5,1},{6,2},{7,3},{8,12},{9,13},{10,... | collective-permute-start | bytes 2580488 | tf_op jit(solution)/shard_map/ppermute | solution.py:409
  628.2 46.8 %collective-permute-start.58 = (bf16[192,384]{1,0:T(8,128)(2,1)}, bf16[192,384]{1,0:T(8,128)(2,1)}, u32[]{:S(2)}, u32[]{:S(2)}) collective-permute-start(bf16[192,384]{1,0:T(8,128)(2,1)} %dynamic-slice_bitcast_fusion.16), channel_id=1, source_target_pairs={{0,4},{1,5},{2,6},{3,7},{4,0},{5,1},{6,2},{7,3},{8,12},{9,13},{10,... | collective-permute-start | bytes 442376 | tf_op jit(solution)/shard_map/ppermute | solution.py:409
  689.6 47.3 %collective-permute-start.99 = (bf16[2,280,1536]{2,1,0:T(8,128)(2,1)}, bf16[2,280,1536]{2,1,0:T(8,128)(2,1)}, u32[]{:S(2)}, u32[]{:S(2)}) collective-permute-start(bf16[2,280,1536]{2,1,0:T(8,128)(2,1)} %pad_maximum_fusion.9), channel_id=1, source_target_pairs={{0,8},{8,0},{16,24},{24,16},{1,9},{9,1},{17,25},{25,17},{2,10},{10... | collective-permute-start | bytes 5160968 | tf_op jit(solution)/shard_map/ppermute | solution.py:396
  724.6 70.5 %collective-permute-start.88 = (bf16[2,192,1120]{2,1,0:T(8,128)(2,1)}, bf16[2,192,1120]{2,1,0:T(8,128)(2,1)S(1)}, u32[]{:S(2)}, u32[]{:S(2)}) collective-permute-start(bf16[2,192,1120]{2,1,0:T(8,128)(2,1)} %get-tuple-element.228), channel_id=1, source_target_pairs={{0,16},{16,0},{8,24},{24,8},{1,17},{17,1},{9,25},{25,9},{2,18},{18... | collective-permute-start | bytes 2580488 | tf_op jit(solution)/shard_map/ppermute | solution.py:400
  730.0 40.2 %collective-permute-start.74 = (bf16[2,192,1120]{2,1,0:T(8,128)(2,1)S(1)}, bf16[2,192,1120]{2,1,0:T(8,128)(2,1)S(1)}, u32[]{:S(2)}, u32[]{:S(2)}) collective-permute-start(bf16[2,192,1120]{2,1,0:T(8,128)(2,1)S(1)} %dynamic-slice_bitcast_fusion.6), channel_id=1, source_target_pairs={{0,4},{1,5},{2,6},{3,7},{4,0},{5,1},{6,2},{7,3},{8,12},{9,13},{10,... | collective-permute-start | bytes 2580488 | tf_op jit(solution)/shard_map/ppermute | solution.py:409
  746.7 112.3 %collective-permute-start.55 = (bf16[256,1536]{1,0:T(8,128)(2,1)}, bf16[256,1536]{1,0:T(8,128)(2,1)}, u32[]{:S(2)}, u32[]{:S(2)}) collective-permute-start(bf16[256,1536]{1,0:T(8,128)(2,1)} %fusion.25), channel_id=1, source_target_pairs={{0,16},{16,0},{8,24},{24,8},{1,17},{17,1},{9,25},{25,9},{2,18},{18... | collective-permute-start | bytes 2359304 | tf_op jit(solution)/shard_map/ppermute | solution.py:400
  796.7 43.2 %collective-permute-start.89 = (bf16[2,2,192,1120]{3,2,1,0:T(8,128)(2,1)}, bf16[2,2,192,1120]{3,2,1,0:T(8,128)(2,1)}, u32[]{:S(2)}, u32[]{:S(2)}) collective-permute-start(bf16[2,2,192,1120]{3,2,1,0:T(8,128)(2,1)} %pad_maximum_fusion.6), channel_id=1, source_target_pairs={{0,8},{8,0},{16,24},{24,16},{1,9},{9,1},{17,25},{25,17},{2,10},{10... | collective-permute-start | bytes 5160968 | tf_op jit(solution)/shard_map/ppermute | solution.py:396
  (187 other events, 2180.1 us)
Sparse Core Ops, SparseCore 0:
  11.5 96.0 all-gather.3
  122.2 145.0 all-gather.5

commit v4 on v3

--- a/solution.py
+++ b/solution.py
@@ -67,79 +67,92 @@
     return (first_new, second_new, weight_new)
 
 
-def strip_starts(blk_count, team_bit, grp, quarter):
+def halves_of(quarter):
+    first = quarter * 16 // 35
+    return ((0, first), (first, quarter - first))
+
+
+def pick_body(blk_count, ids, gate_ref, up_ref, *out_refs):
+    quarter = FF // blk_count // 4
     per = blk_count // 4
-    return [
-        (((high * 2 + team_bit) * per + small) * 4 + grp) * quarter
-        for high in range(2)
-        for small in range(per)
-    ]
-
-def pick_body(blk_count, ids, gate_ref, up_ref, out_ref):
-    quarter = FF // blk_count // 4
     for k in range(4):
+
         @pl.when(ids[0] == k)
         def _(k=k):
-            for which, src in enumerate((gate_ref, up_ref)):
-                for bit in range(2):
-                    parts = [src[:, s:s + quarter] for s in strip_starts(blk_count, bit, k, quarter)]
-                    out_ref[ids[1] ^ bit, which] = jnp.concatenate(parts, axis=1).astype(jnp.bfloat16)
+            for (at, size), out_ref in zip(halves_of(quarter), out_refs):
+                for which, src in enumerate((gate_ref, up_ref)):
+                    for bit in range(2):
+                        parts = []
+                        for high in range(2):
+                            for small in range(per):
+                                begin = (((high * 2 + bit) * per + small) * 4 + k) * quarter + at
+                                parts.append(src[:, begin : begin + size])
+                        out_ref[ids[1] ^ bit, which] = jnp.concatenate(parts, axis=1).astype(
+                            jnp.bfloat16
+                        )
+
 
 def pick_columns(ids, gate, up, blk_count):
     rows = gate.shape[0]
     step = 48 if rows % 48 == 0 else rows
-    wide_here = FF // 8
+    widths = [size * blk_count // 2 for at, size in halves_of(FF // blk_count // 4)]
     spec = pl.BlockSpec((step, FF), lambda i, ids: (i, 0))
-    out = pl.BlockSpec((2, 2, step, wide_here), lambda i, ids: (0, 0, i, 0))
-    shape = jax.ShapeDtypeStruct((2, 2, rows, wide_here), jnp.bfloat16)
     return pl.pallas_call(
         functools.partial(pick_body, blk_count),
         grid_spec=pltpu.PrefetchScalarGridSpec(
-            num_scalar_prefetch=1, grid=(rows // step,), in_specs=[spec, spec], out_specs=out),
-        out_shape=shape,
+            num_scalar_prefetch=1,
+            grid=(rows // step,),
+            in_specs=[spec, spec],
+            out_specs=[pl.BlockSpec((2, 2, step, w), lambda i, ids: (0, 0, i, 0)) for w in widths],
+        ),
+        out_shape=[jax.ShapeDtypeStruct((2, 2, rows, w), jnp.bfloat16) for w in widths],
         compiler_params=pltpu.CompilerParams(vmem_limit_bytes=VMEM),
         cost_estimate=pl.CostEstimate(flops=0, bytes_accessed=rows * FF * 10, transcendentals=0),
         name="pick_columns",
     )(ids, gate, up)
 
-def near_at(away):
-    return (away & 1) * 2 + (away >> 1)
-
-
-def adam_body(blk_count, rate, decay, ids, factor_ref, grad_ref, w_ref, m_ref, v_ref, m_out, v_out, w_out):
-    quarter = FF // blk_count // 4
+
+def adam_body(blk_count, rate, decay, factor_ref, first_ref, second_ref, w_ref, m_ref, v_ref, m_out, v_out, w_out):
     per = blk_count // 4
+    sizes = [size for at, size in halves_of(FF // blk_count // 4)]
+    grads = [[[ref[k, bit] for bit in range(2)] for k in range(4)] for ref in (first_ref, second_ref)]
     parts = []
-    grads = [[grad_ref[near_at(ids[0] ^ k), bit] for bit in range(2)] for k in range(4)]
     for high in range(2):
         for bit in range(2):
             for small in range(per):
-                at = (high * per + small) * quarter
+                place = high * per + small
                 for k in range(4):
-                    parts.append(grads[k][bit][:, at:at + quarter])
+                    for part, size in zip(grads, sizes):
+                        parts.append(part[k][bit][:, place * size : (place + 1) * size])
     grad = jnp.concatenate(parts, axis=1).astype(jnp.float32) * factor_ref[0]
     m, v, w = adam_step(w_ref[...], grad, m_ref[...], v_ref[...], rate, decay)
     m_out[...] = m
     v_out[...] = v
     w_out[...] = w
 
-def adam_columns(ids, factor, grad, w, m, v, blk_count, rate, decay):
+
+def adam_columns(which, factor, first, second, w, m, v, blk_count, rate, decay):
     rows = w.shape[0]
     step = 32 if rows % 32 == 0 else rows
-    spec = pl.BlockSpec((step, FF), lambda i, ids: (i, 0))
+    spec = pl.BlockSpec((step, FF), lambda i: (i, 0))
     shape = jax.ShapeDtypeStruct((rows, FF), jnp.float32)
+    grads = [
+        pl.BlockSpec((4, None, 2, step, g.shape[-1]), lambda i: (0, which, 0, i, 0))
+        for g in (first, second)
+    ]
     return pl.pallas_call(
         functools.partial(adam_body, blk_count, rate, decay),
-        grid_spec=pltpu.PrefetchScalarGridSpec(
-            num_scalar_prefetch=1, grid=(rows // step,),
-            in_specs=[pl.BlockSpec(memory_space=pltpu.SMEM),
-                      pl.BlockSpec((4, 2, step, FF // 8), lambda i, ids: (0, 0, i, 0)), spec, spec, spec],
-            out_specs=[spec, spec, spec]),
+        grid=(rows // step,),
+        in_specs=[pl.BlockSpec(memory_space=pltpu.SMEM)] + grads + [spec, spec, spec],
+        out_specs=[spec, spec, spec],
         out_shape=[shape] * 3,
         compiler_params=pltpu.CompilerParams(vmem_limit_bytes=VMEM),
-        cost_estimate=pl.CostEstimate(flops=rows * FF * 20, bytes_accessed=rows * FF * 26, transcendentals=rows * FF),
+        cost_estimate=pl.CostEstimate(
+            flops=rows * FF * 20, bytes_accessed=rows * FF * 26, transcendentals=rows * FF
+        ),
         name="adam_columns",
-    )(ids, factor, grad, w, m, v)
+    )(factor, first, second, w, m, v)
+
 
 def nt(a, b, **kw):
     return lax.dot_general(a, b, (((1,), (1,)), ((), ())), preferred_element_type=jnp.float32, **kw)
@@ -304,7 +317,9 @@
     return jnp.dot(a, b, preferred_element_type=jnp.float32)
 
 
-def middle_body(h_ref, dy_ref, wg_ref, wu_ref, wd_ref, hid_ref, dg_ref, du_ref, dh_ref):
+def middle_body(add, order, h_ref, dy_ref, wg_ref, wu_ref, wd_ref, *refs):
+    prev_ref = refs[0] if add else None
+    hid_ref, dg_ref, du_ref, dh_ref = refs[-4:]
     h = h_ref[...]
     gate = nn(h, wg_ref[...])
     up = nn(h, wu_ref[...])
@@ -316,39 +331,66 @@
     du = (dhid * silu).astype(jnp.bfloat16)
     dg_ref[...] = dg
     du_ref[...] = du
-    dh_ref[...] = (nt(dg, wg_ref[...]) + nt(du, wu_ref[...])).astype(jnp.bfloat16)
-
-def middle(h, dy, wg, wu, wd, step=256):
-    T, D = h.shape
-    F = wg.shape[1]
-    row = pl.BlockSpec((step, D), lambda i: (i, 0))
-    rowf = pl.BlockSpec((step, F), lambda i: (i, 0))
-    whole = lambda a: pl.BlockSpec(a.shape, lambda i: (0, 0), pipeline_mode=pl.Buffered(1))
+    dh = nt(dg, wg_ref[...]) + nt(du, wu_ref[...])
+    if add:
+        dh = dh + prev_ref[...].astype(jnp.float32)
+    dh_ref[...] = dh.astype(jnp.bfloat16)
+
+
+def middle(order, h, dy, wg, wu, wd, prev=None):
+    count = h.shape[0]
+    step = count // order.shape[0]
+    wide_here = wg.shape[1]
+    row = pl.BlockSpec((step, D), lambda i, order: (i, 0))
+    placed = pl.BlockSpec((step, D), lambda i, order: (order[i], 0))
+    part = pl.BlockSpec((step, wide_here), lambda i, order: (i, 0))
+    part_placed = pl.BlockSpec((step, wide_here), lambda i, order: (order[i], 0))
+
+    def whole(array):
+        return pl.BlockSpec(array.shape, lambda i, order: (0, 0), pipeline_mode=pl.Buffered(1))
+
+    extra = [] if prev is None else [prev]
     return pl.pallas_call(
-        middle_body, grid=(T // step,),
-        in_specs=[row, row, whole(wg), whole(wu), whole(wd)],
-        out_specs=[rowf, rowf, rowf, row],
-        out_shape=[jax.ShapeDtypeStruct((T, F), jnp.bfloat16)] * 3 + [jax.ShapeDtypeStruct((T, D), jnp.bfloat16)],
+        functools.partial(middle_body, prev is not None),
+        grid_spec=pltpu.PrefetchScalarGridSpec(
+            num_scalar_prefetch=1,
+            grid=(count // step,),
+            in_specs=[row, placed, whole(wg), whole(wu), whole(wd)] + [row] * len(extra),
+            out_specs=[part_placed, part, part, row],
+        ),
+        out_shape=[jax.ShapeDtypeStruct((count, wide_here), jnp.bfloat16)] * 3
+        + [jax.ShapeDtypeStruct((count, D), jnp.bfloat16)],
         compiler_params=pltpu.CompilerParams(vmem_limit_bytes=VMEM),
-        cost_estimate=pl.CostEstimate(flops=10 * T * D * F, bytes_accessed=40 * 2**20, transcendentals=T * F),
-        name="middle")(h, dy, wg, wu, wd)
-
-def two_grads_body(h_ref, a_ref, b_ref, ga_ref, gb_ref):
+        cost_estimate=pl.CostEstimate(
+            flops=10 * count * D * wide_here, bytes_accessed=30 * 2**20, transcendentals=count * wide_here
+        ),
+        name="middle",
+    )(order, h, dy, wg, wu, wd, *extra)
+
+
+def two_grads_body(h_ref, a_ref, b_ref, out_ref):
     h = h_ref[...]
-    ga_ref[...] = tn(h, a_ref[...]).astype(jnp.bfloat16)
-    gb_ref[...] = tn(h, b_ref[...]).astype(jnp.bfloat16)
+    out_ref[0] = tn(h, a_ref[...]).astype(jnp.bfloat16)
+    out_ref[1] = tn(h, b_ref[...]).astype(jnp.bfloat16)
+
 
 def two_grads(h, a, b, step=256):
-    T, D = h.shape
-    F = a.shape[1]
-    col = pl.BlockSpec((T, step), lambda i: (0, i))
-    whole = lambda v: pl.BlockSpec(v.shape, lambda i: (0, 0), pipeline_mode=pl.Buffered(1))
-    out = pl.BlockSpec((step, F), lambda i: (i, 0))
-    return pl.pallas_call(two_grads_body, grid=(D // step,), in_specs=[col, whole(a), whole(b)], out_specs=[out, out],
-        out_shape=[jax.ShapeDtypeStruct((D, F), jnp.bfloat16)] * 2,
+    count = h.shape[0]
+    wide_here = a.shape[1]
+    whole = pl.BlockSpec(a.shape, lambda i: (0, 0), pipeline_mode=pl.Buffered(1))
+    return pl.pallas_call(
+        two_grads_body,
+        grid=(D // step,),
+        in_specs=[pl.BlockSpec((count, step), lambda i: (0, i)), whole, whole],
+        out_specs=pl.BlockSpec((2, step, wide_here), lambda i: (0, i, 0)),
+        out_shape=jax.ShapeDtypeStruct((2, D, wide_here), jnp.bfloat16),
         compiler_params=pltpu.CompilerParams(vmem_limit_bytes=VMEM),
-        cost_estimate=pl.CostEstimate(flops=4 * T * D * F, bytes_accessed=24 * 2**20, transcendentals=0),
-        name="two_grads")(h, a, b)
+        cost_estimate=pl.CostEstimate(
+            flops=4 * count * D * wide_here, bytes_accessed=20 * 2**20, transcendentals=0
+        ),
+        name="two_grads",
+    )(h, a, b)
+
 
 def down_grad_body(hid_ref, dy_ref, g_ref):
     g_ref[...] = tn(hid_ref[...], dy_ref[...]).astype(jnp.bfloat16)
@@ -364,19 +406,36 @@
         cost_estimate=pl.CostEstimate(flops=2 * T * D * F, bytes_accessed=16 * 2**20, transcendentals=0),
         name="down_grad")(hid, dy)
 
-def down_body(hid_ref, wd_ref, o_ref):
-    o_ref[...] = nn(hid_ref[...], wd_ref[...]).astype(jnp.bfloat16)
-
-def down(hid, wd, step=256):
-    T, F = hid.shape
-    D = wd.shape[1]
-    return pl.pallas_call(down_body, grid=(T // step,),
-        in_specs=[pl.BlockSpec((step, F), lambda i: (i, 0)), pl.BlockSpec((F, D), lambda i: (0, 0), pipeline_mode=pl.Buffered(1))],
-        out_specs=pl.BlockSpec((step, D), lambda i: (i, 0)),
-        out_shape=jax.ShapeDtypeStruct((T, D), jnp.bfloat16),
+def down_body(order, hid_a_ref, hid_b_ref, wd_a_ref, wd_b_ref, o_ref):
+    out = nn(hid_a_ref[...], wd_a_ref[...]) + nn(hid_b_ref[...], wd_b_ref[...])
+    o_ref[...] = out.astype(jnp.bfloat16)
+
+
+def down(order, hid_a, hid_b, wd_a, wd_b):
+    count = hid_a.shape[0]
+    step = count // order.shape[0]
+
+    def placed(array):
+        return pl.BlockSpec((step, array.shape[1]), lambda i, order: (order[i], 0))
+
+    def whole(array):
+        return pl.BlockSpec(array.shape, lambda i, order: (0, 0), pipeline_mode=pl.Buffered(1))
+
+    return pl.pallas_call(
+        down_body,
+        grid_spec=pltpu.PrefetchScalarGridSpec(
+            num_scalar_prefetch=1,
+            grid=(count // step,),
+            in_specs=[placed(hid_a), placed(hid_b), whole(wd_a), whole(wd_b)],
+            out_specs=pl.BlockSpec((step, D), lambda i, order: (i, 0)),
+        ),
+        out_shape=jax.ShapeDtypeStruct((count, D), jnp.bfloat16),
         compiler_params=pltpu.CompilerParams(vmem_limit_bytes=VMEM),
-        cost_estimate=pl.CostEstimate(flops=2 * T * D * F, bytes_accessed=16 * 2**20, transcendentals=0),
-        name="down")(hid, wd)
+        cost_estimate=pl.CostEstimate(
+            flops=2 * count * D * (hid_a.shape[1] + hid_b.shape[1]), bytes_accessed=16 * 2**20, transcendentals=0
+        ),
+        name="down",
+    )(order, hid_a, hid_b, wd_a, wd_b)
 
 
 CORE = [(0, 1), (1, 0), (2, 3), (3, 2)]
@@ -506,28 +565,6 @@
     return jnp.stack(
         [jnp.where(mine, other, values), jnp.where(mine, values, other)], axis=axis
     )
-
-
-def gather_two_ways(values, bits, team):
-    lows = [bit for bit in bits if bit < team]
-    values = gather_step(values, [], bits[0])
-    half = values.shape[-1] // 2
-    parts = []
-    for part, order in (
-        (values[..., :half], [team] + lows),
-        (values[..., half:], lows + [team]),
-    ):
-        done = [bits[0]]
-        for bit in order:
-            part = gather_step(part, done, bit)
-            done.append(bit)
-        parts.append(part)
-    return jnp.concatenate(parts, axis=-1)
-
-
-def gather_near_stacked(values):
-    both = jnp.stack([values, swap_cross(values)])
-    return jnp.concatenate([both, swap_core(both)])
 
 
 def on_device(
@@ -572,7 +609,9 @@
     weight_rows = w_gate.shape[0]
     ff_block = w_down.shape[0]
     quarter = ff_block // 4
-    ff_here = quarter * blk_count // 2
+    widths = [size * blk_count // 2 for at, size in halves_of(quarter)]
+    chip_rows = 4 * token_count
+    half = token_count // 2
 
     ids = jnp.stack([grp, in_team])
     flat_low = tokens.reshape(token_count, D)
@@ -588,10 +627,14 @@
             axis=1,
         )
     )
+    small_count = small_params.shape[0]
     small_send = jnp.concatenate([low(small_params), low(segment_ids.reshape(token_count))])
+    strip_wide = strip_q + HD
+    small_send = jnp.pad(small_send, (0, -small_send.shape[0] % strip_wide))
+    strip_local = jnp.concatenate([strip_local, small_send.reshape(-1, strip_wide)])
     strip_first = gather_step(strip_local, [], bits[0])
     strip_parts = []
-    cut = (strip_q + HD) // 2
+    cut = strip_wide // 2
     for part, order in (
         (strip_first[..., :cut], [team] + lows),
         (strip_first[..., cut:], lows + [team]),
@@ -601,11 +644,15 @@
             part = gather_step(part, done, bit)
             done.append(bit)
         strip_parts.append(part)
-    strip = jnp.concatenate(strip_parts, axis=-1).reshape(D, strip_q + HD)
-    near_tokens = jnp.concatenate(gather_near(flat_low))
-    near_positions = jnp.concatenate(gather_near(positions))
-    small_all = gather_bits(small_send, bits).reshape(blk_count, -1)
-    vector = wide(small_all[:, : small_params.shape[0]].reshape(-1))
+    strip_all = jnp.concatenate(strip_parts, axis=-1).reshape(blk_count, -1, strip_wide)
+    strip = strip_all[:, :weight_rows].reshape(D, strip_wide)
+    small_all = strip_all[:, weight_rows:].reshape(blk_count, -1)
+    digits = low(jnp.stack([positions // 64, positions % 64], axis=1))
+    digits = jnp.pad(digits, ((0, 0), (0, HD - 2)))
+    near_all = jnp.concatenate(gather_near(jnp.concatenate([flat_low, digits], axis=1)))
+    near_tokens = near_all[:, :D]
+    near_positions = 64.0 * wide(near_all[:, D]) + wide(near_all[:, D + 1])
+    vector = wide(small_all[:, :small_count].reshape(-1))
     gain_one = vector[:D]
     gain_two = vector[D : 2 * D]
     bias = vector[2 * D :]
@@ -615,7 +662,7 @@
             lax.dynamic_slice_in_dim(bias, kv_at, HD, 0),
         ]
     )
-    seg_all = small_all[:, small_params.shape[0] :].astype(jnp.int32)
+    seg_all = small_all[:, small_count : small_count + token_count].astype(jnp.int32)
     seg_all = seg_all.reshape(blk_count, rows_here, block_len)
     seg_key = jnp.broadcast_to(
         seg_all.transpose(1, 0, 2).reshape(rows_here, seq_len)[:, :, None], (rows_here, seq_len, HD)
@@ -646,24 +693,35 @@
     query = jnp.concatenate([part[:, :strip_q] for part in strips], axis=1)
     key_value = jnp.concatenate([strips[k][:, strip_q:] for k in (0, 2, 1, 3)], axis=1)
     key_value = key_value.reshape(rows_here, block_len, 2 * KVD)
-    kv_all = gather_two_ways(key_value, bits, team).reshape((blk_count,) + key_value.shape)
-
-    out_piece = weight_rows // 4
-    out_local = low(lax.dynamic_slice_in_dim(w_out, out_piece * grp, out_piece, 0))
-    out_full = lax.all_gather(out_local, ("blk", "grp"), axis=0, tiled=True)
-    down_local = low(lax.dynamic_slice_in_dim(w_down, quarter * grp, quarter, 0))
-    down_first = swap_blk(after(down_local, strip_first), bits[0])
-    picked = pick_columns(ids, w_gate, w_up, blk_count)
+    kv_first = gather_step(key_value, [], bits[0])
+    kv_parts = []
+    for part, order in (
+        (kv_first[..., :KVD], [team] + lows),
+        (kv_first[..., KVD:], lows + [team]),
+    ):
+        done = [bits[0]]
+        for bit in order:
+            part = gather_step(part, done, bit)
+            done.append(bit)
+        kv_parts.append(part)
+    kv_all = jnp.concatenate(kv_parts, axis=-1).reshape((blk_count,) + key_value.shape)
+
+    teams = [
+        [g * blk_count + (i | t) for g in range(4) for t in (0, team)]
+        for i in range(blk_count)
+        if not i & team
+    ]
+    dy_team = lax.all_gather(dy_low, ("grp", "blk"), axis=0, tiled=True, axis_index_groups=teams)
+    order = jnp.stack(
+        [
+            (grp ^ (2 * (i & 1) + (i >> 2))) * 2 + (in_team ^ ((i >> 1) & 1))
+            for i in range(8)
+        ]
+    )
+
     mine_team = blk_bit(team)
-    picked_got = after(swap_blk(picked[1], team), strip_out)
-    pair = jnp.stack(
-        [jnp.where(mine_team, picked_got, picked[0]), jnp.where(mine_team, picked[0], picked_got)]
-    )
     peers = [[i for i in range(blk_count) if (i & team) == t] for t in (0, team)]
-    pairs = lax.all_gather(pair, "blk", axis=0, axis_index_groups=peers)
-    pairs = pairs.reshape((2, blk_count // 4, 2, 2, weight_rows, ff_here)).transpose(3, 0, 2, 1, 4, 5)
-    gate_here = pairs[0].reshape(D, ff_here)
-    up_here = pairs[1].reshape(D, ff_here)
+    (low_first, size_first), (low_second, size_second) = halves_of(quarter)
 
     def place(values, other, done, bit):
         mine = blk_bit(bit)
@@ -672,32 +730,94 @@
             [jnp.where(mine, other, values), jnp.where(mine, values, other)], axis=axis
         )
 
-    down_here = place(down_local, after(down_first, strip_out), [], bits[0])
-    done = [bits[0]]
-    for bit in lows:
-        other = after(swap_blk(down_here, bit), kv_all)
-        down_here = place(down_here, other, done, bit)
-        done.append(bit)
-    down_here = down_here.reshape(ff_here, D)
-
-    dy_half = token_count // 2
-    dy_send = after(dy_low, strip_parts)
-    dy_cross, dy_over = after((swap_cross(dy_send), swap_blk(dy_send, team)), strip_out)
-    dy_first = swap_blk(dy_cross[:dy_half], team)
-    dy_second = swap_cross(dy_over[dy_half:])
-    dy_first, dy_second = after((dy_first, dy_second), kv_all)
-    dy_chip = jnp.concatenate([dy_low, dy_cross, dy_over, dy_first, dy_second])
-    dy_team = jnp.concatenate([dy_chip, swap_core(dy_chip)])
+    def lows_of(values, done, anchor):
+        for bit in lows:
+            values = place(values, after(swap_blk(values, bit), anchor), done, bit)
+            done = done + [bit]
+        return values
+
+    def team_pair(mine, got):
+        return jnp.stack([jnp.where(mine_team, got, mine), jnp.where(mine_team, mine, got)])
+
+    def whole_weights(pair):
+        pairs = lax.all_gather(pair, "blk", axis=0, axis_index_groups=peers)
+        pairs = pairs.reshape((2, blk_count // 4) + pair.shape).transpose(3, 0, 2, 1, 4, 5)
+        return pairs[0].reshape(D, -1), pairs[1].reshape(D, -1)
+
+    picked_a, picked_b = pick_columns(ids, w_gate, w_up, blk_count)
+    got_a = swap_blk(after(picked_a[1], strip_parts), team)
+    gate_a, up_a = whole_weights(team_pair(picked_a[0], after(got_a, strips)))
+    got_b = swap_blk(after(picked_b[1], strip_out), team)
+    gate_b, up_b = whole_weights(team_pair(picked_b[0], after(got_b, kv_all)))
+
+    down_at = quarter * grp
+    down_a = low(lax.dynamic_slice_in_dim(w_down, down_at, size_first, 0))
+    down_got = swap_blk(after(down_a, strip_first), bits[0])
+    down_a = place(down_a, after(down_got, strip_out), [], bits[0])
+    down_a = lows_of(down_a, [bits[0]], kv_all).reshape(widths[0], D)
+
+    out_strip = low(lax.dynamic_slice_in_dim(w_out, strip_q * grp, strip_q, 1))
+    out_got = swap_blk(after(out_strip, strip_first), bits[0])
+    out_strip = place(out_strip, after(out_got, strip_parts), [], bits[0])
+    out_got = swap_blk(out_strip, team)
+    out_strip = place(out_strip, after(out_got, strip_out), [bits[0]], team)
+    out_strip = lows_of(out_strip, [bits[0], team], kv_first).reshape(HQD, strip_q)
+    out_cross = after(swap_cross(out_strip), kv_all)
+    out_both = jnp.stack([out_strip, out_cross])
+    out_core = swap_core(out_both)
+    out_full = jnp.concatenate(by_place([out_strip, out_core[0], out_cross, out_core[1]]), axis=1)
+
+    down_b = low(lax.dynamic_slice_in_dim(w_down, down_at + size_first, size_second, 0))
+    down_got_b = swap_blk(after(down_b, kv_all), bits[0])
 
     att_in, lse = attend(attend_ids, query, kv_all, seg_key, seg_query, block_len)
+    down_b = place(down_b, after(down_got_b, att_in), [], bits[0])
 
     flat = wide(flat_low)
     resid = flat + jnp.dot(att_in, out_full, preferred_element_type=jnp.float32)
     h_two = low(norm_apply(resid, gain_two))
     h_team = gather_tokens(h_two, team)
-    hidden, d_gate, d_up, d_htwo_part = middle(h_team, dy_team, gate_here, up_here, down_here)
-    chip_rows = 4 * token_count
-    half = token_count // 2
+    hidden_a, d_gate_a, d_up_a, part_a = middle(order, h_team, dy_team, gate_a, up_a, down_a)
+    down_b = lows_of(down_b, [bits[0]], hidden_a).reshape(widths[1], D)
+    down_share_a = lax.psum_scatter(
+        down_grad(hidden_a, dy_team), "blk", scatter_dimension=0, axis_index_groups=peers, tiled=True
+    )
+    column_grad_a = two_grads(h_team, d_gate_a, d_up_a)
+
+    def part_sent(values, axis, bit):
+        mine = blk_bit(bit).astype(jnp.int32)
+        keep = lax.dynamic_index_in_dim(values, mine, axis, keepdims=False)
+        send = lax.dynamic_index_in_dim(values, 1 - mine, axis, keepdims=False)
+        return keep, swap_blk(send, bit)
+
+    def part_sum(keep, got):
+        return low(wide(keep) + wide(got))
+
+    def columns_first(grad):
+        grad = grad.reshape((2, 2, 2) + low_shape + (weight_rows, -1))
+        return part_sent(grad, 2 + len(lows), lows[-1])
+
+    def columns_second(keep, got):
+        values = part_sum(keep, got)
+        for i in range(len(lows) - 2, -1, -1):
+            values = part_sum(*part_sent(values, 3 + i, lows[i]))
+        return part_sent(values, 1, bits[0])
+
+    def columns_third(keep, got):
+        values = part_sum(keep, got)
+        mine = lax.dynamic_index_in_dim(values, in_team, 1, keepdims=False)
+        send = lax.dynamic_index_in_dim(values, 1 - in_team, 1, keepdims=False)
+        return mine, swap_blk(send, team)
+
+    def columns_last(mine, got):
+        return jnp.stack(
+            [jnp.where(mine_team, got, mine), jnp.where(mine_team, mine, got)], axis=1
+        )
+
+    first_a = columns_first(column_grad_a)
+    hidden_b, d_gate_b, d_up_b, d_htwo_part = middle(
+        order, after(h_team, column_grad_a), dy_team, gate_b, up_b, down_b, part_a
+    )
 
     def chip_sum(values, came):
         return low(wide(values[:chip_rows]) + wide(came))
@@ -713,48 +833,19 @@
         return swap_cross(cross), swap_blk(over, team)
 
     d_came = swap_core(d_htwo_part[chip_rows:])
-    down_grad_part = down_grad(hidden, dy_team).reshape((2,) + low_shape + (quarter, D))
-    d_chip = chip_sum(d_htwo_part, after(d_came, down_grad_part))
+    down_grad_b = down_grad(hidden_b, dy_team)
+    down_share_b = lax.psum_scatter(
+        down_grad_b, "blk", scatter_dimension=0, axis_index_groups=peers, tiled=True
+    )
+    d_chip = chip_sum(d_htwo_part, after(d_came, down_grad_b))
     d_far = scatter_far(d_chip)
-
-    def share_start(grad, axes):
-        bit = lows[-1]
-        axis = axes.index(bit)
-        mine = blk_bit(bit).astype(jnp.int32)
-        keep = lax.dynamic_index_in_dim(grad, mine, axis, keepdims=False)
-        send = lax.dynamic_index_in_dim(grad, 1 - mine, axis, keepdims=False)
-        return keep, swap_blk(send, bit)
-
-    def share_mid(keep, got, axes):
-        values = low(wide(keep) + wide(got))
-        axes = [bit for bit in axes if bit != lows[-1]]
-        for bit in lows[-2::-1]:
-            values = scatter_bits(values, axes, [bit])
-            axes = [b for b in axes if b != bit]
-        mine = blk_bit(bits[0]).astype(jnp.int32)
-        keep = lax.dynamic_index_in_dim(values, mine, 0, keepdims=False)
-        send = lax.dynamic_index_in_dim(values, 1 - mine, 0, keepdims=False)
-        return keep, swap_blk(send, bits[0])
-
-    def share_columns(values):
-        keep = lax.dynamic_index_in_dim(values, in_team, 0, keepdims=False)
-        send = lax.dynamic_index_in_dim(values, 1 - in_team, 0, keepdims=False)
-        got = swap_blk(send, team)
-        return jnp.stack(
-            [jnp.where(mine_team, got, keep), jnp.where(mine_team, keep, got)]
-        )
-
-    down_axes = [bits[0]] + lows
-    down_keep, down_got = share_start(down_grad_part, down_axes)
-    late_gate, late_up = after((d_gate, d_up), d_chip)
-    column_shape = (2, 2) + low_shape + (weight_rows, ff_here)
-    gate_grad, up_grad = two_grads(h_team, late_gate, late_up)
-    gate_keep, gate_got = share_start(gate_grad.reshape(column_shape), bits)
-    d_far = after(d_far, gate_grad)
+    column_grad_b = two_grads(h_team, *after((d_gate_b, d_up_b), d_chip))
+    first_b = columns_first(column_grad_b)
+    d_far = after(d_far, column_grad_b)
     d_cross, d_over = scatter_near(d_chip, *d_far)
-    out_part = down(after(hidden, d_far), down_here)
+    out_part = down(order, *after((hidden_a, hidden_b), d_far), down_a, down_b)
     out_came = swap_core(out_part[chip_rows:])
-    down_keep, down_got = share_mid(*after((down_keep, down_got), out_part), down_axes)
+    second_a = columns_second(*after(first_a, out_part))
     d_cross, d_over = after((d_cross, d_over), out_part)
     d_htwo = wide(d_chip[:token_count]) + wide(d_cross) + wide(d_over)
 
@@ -779,22 +870,26 @@
         jnp.concatenate([sine, sine], axis=1),
         block_len,
     )
-    gate_keep, gate_got = share_mid(*after((gate_keep, gate_got), d_query), bits)
-    share_down = low(wide(down_keep) + wide(after(down_got, d_query)))
+    second_b = columns_second(*after(first_b, d_query))
+    third_a = columns_third(*after(second_a, d_query))
     dkv = dkv.reshape((2,) * len(bits) + (rows_here, block_len, 2 * KVD))
     dkv_first = scatter_bits(dkv[..., :KVD], bits, lows[::-1])
     dkv_second = scatter_bits(dkv[..., KVD:], bits, [team])
-    up_keep, up_got = share_start(after(up_grad, dkv_first).reshape(column_shape), bits)
     dkv_first = scatter_bits(dkv_first, bits[:2], [team])
     dkv_second = scatter_bits(dkv_second, [bits[0]] + lows, lows[::-1])
     dkv = jnp.concatenate([dkv_first, dkv_second], axis=-1)
-    out_chip = chip_sum(out_part, after(out_came, dkv_first))
+    dkv_mid = dkv
+    out_chip = chip_sum(out_part, after(out_came, dkv_mid))
     dkv = wide(scatter_bits(dkv, bits[:1], bits[:1])).reshape(token_count, 2, KVH, HD)
     d_key = low(rotate_by(dkv[:, 0], cosine[:, None], -sine[:, None]))
     d_value = low(dkv[:, 1])
     out_far = after(scatter_far(out_chip), d_key)
     out_cross, out_over = scatter_near(out_chip, *out_far)
-    up_keep, up_got = share_mid(*after((up_keep, up_got), d_key), bits)
+    third_b = columns_third(*after(second_b, d_key))
+    share_a = columns_last(*after(third_a, dkv_mid))
+    all_a = lax.all_gather(share_a, "grp", axis=0)
+    share_down = jnp.concatenate([down_share_a, down_share_b])
+    grad_down = lax.all_gather(share_down, "grp", axis=0, tiled=True)
 
     def to_strips(parts):
         parts = by_place(parts)
@@ -804,13 +899,18 @@
 
     near_dq = to_strips([d_query[:, strip_q * k : strip_q * (k + 1)] for k in range(4)])
     block_shape = (2,) * len(bits) + (weight_rows, -1)
-    share_query = scatter_bits(
-        low(left_product(near_one, near_dq)).reshape(block_shape), bits, bits[::-1]
-    )
+    query_grad = low(left_product(near_one, near_dq)).reshape(block_shape)
+    steps_query = part_sent(after(query_grad, dkv_mid), len(bits) - 1, bits[-1])
     near_dkv = to_strips([(d_value if k % 2 else d_key)[:, k // 2] for k in range(4)])
-    share_kv = scatter_bits(
-        low(left_product(near_one, near_dkv)).reshape(block_shape), bits, bits[::-1]
-    )
+    kv_grad = low(left_product(near_one, near_dkv)).reshape(block_shape)
+    steps_kv = part_sent(kv_grad, len(bits) - 1, bits[-1])
+    for i in range(len(bits) - 2, -1, -1):
+        steps_query = part_sent(part_sum(*after(steps_query, kv_grad)), i, bits[i])
+        kv_sum = part_sum(*steps_kv)
+        kv_grad = kv_sum
+        steps_kv = part_sent(kv_sum, i, bits[i])
+    share_kv = part_sum(*steps_kv)
+    share_query = part_sum(*after(steps_query, share_kv))
     grad_bias = jnp.concatenate(
         [
             jnp.sum(wide(part), axis=0)
@@ -827,11 +927,13 @@
 
     near_att = jnp.concatenate(gather_near(att_in))
     near_datt = to_strips([d_att[:, strip_q * k : strip_q * (k + 1)] for k in range(4)])
-    share_out = scatter_bits(
-        low(left_product(near_att, after(near_datt, d_query))).reshape(block_shape),
-        bits,
-        bits[::-1],
-    )
+    out_grad = low(left_product(near_att, after(near_datt, d_attended))).reshape(block_shape)
+    steps_out = part_sent(out_grad, len(bits) - 1, bits[-1])
+    anchors = [dkv_mid, near_dkv]
+    for i in range(len(bits) - 2, -1, -1):
+        anchor = anchors[min(len(bits) - 2 - i, 1)]
+        steps_out = part_sent(part_sum(*after(steps_out, anchor)), i, bits[i])
+    share_out = part_sum(*after(steps_out, kv_grad))
 
     vector_term = jnp.concatenate([gain_one_part, grad_gain_two, grad_bias])
     vector_term = vector_term + swap_cross(vector_term)
@@ -847,15 +949,12 @@
         axes.remove(bit)
     share_vector = vector_term
 
-    share_gate = share_columns(low(wide(gate_keep) + wide(after(gate_got, d_key))))
-    near_gate = gather_near_stacked(share_gate)
-    share_up = share_columns(low(wide(up_keep) + wide(after(up_got, near_dkv))))
-    near_up = gather_near_stacked(share_up)
-    grad_down = jnp.concatenate(gather_grp(share_down), axis=0)
+    share_b = columns_last(*after(third_b, near_dkv))
+    all_b = lax.all_gather(share_b, "grp", axis=0)
     grad_out = jnp.concatenate(gather_grp(share_out), axis=1)
     query_parts = gather_grp(share_query)
-    kv_parts = gather_grp(share_kv)
-    grad_attend = jnp.concatenate(query_parts + [kv_parts[k] for k in (0, 2, 1, 3)], axis=1)
+    key_parts = gather_grp(share_kv)
+    grad_attend = jnp.concatenate(query_parts + [key_parts[k] for k in (0, 2, 1, 3)], axis=1)
 
     sides = low(near_hone[token_count : 2 * token_count]), low(near_hone[3 * token_count :])
     other = wide(swap_core(jnp.concatenate(sides)))
@@ -866,7 +965,7 @@
     square_sum = square_total(
         [
             wide(s)
-            for s in (share_query, share_kv, share_out, share_gate, share_up, share_down)
+            for s in (share_query, share_kv, share_out, share_a, share_b, share_down)
         ]
     ) + 0.25 * jnp.sum(share_vector * share_vector)
     square_sum = jnp.full((8, 128), square_sum)
@@ -879,10 +978,10 @@
     factor = after(factor, out_tokens)
 
     new_first_gate, new_second_gate, new_gate = adam_columns(
-        ids, factor[None], near_gate, w_gate, first_gate, second_gate, blk_count, RATE_GATE, WEIGHT_DECAY
+        0, factor[None], all_a, all_b, w_gate, first_gate, second_gate, blk_count, RATE_GATE, WEIGHT_DECAY
     )
     new_first_up, new_second_up, new_up = adam_columns(
-        ids, factor[None], near_up, w_up, first_up, second_up, blk_count, RATE_GATE, WEIGHT_DECAY
+        1, factor[None], all_a, all_b, w_up, first_up, second_up, blk_count, RATE_GATE, WEIGHT_DECAY
     )
     norm_value_one, norm_back_one = jax.vjp(norm_apply, flat, gain_one)
     d_hone = after(d_hone + wide(after(d_hone_cross, new_gate)), new_gate)

time: 902 us -> 998 us (1.11)
  waiting for transfers between devices: 368 us -> 463 us
  local copies, waits for them, and re-layouts: 78.8 us -> 94.1 us
    reduce_scatter x0 -> x2, waiting for transfers between devices: none -> 37.7 us  [the longest x1 37.7 us: on_device(): lax.psum_scatter(down_grad_b, 'blk', scatter_dimension=0, axis_index_grou...]
    ppermute x24 -> x19, waiting for transfers between devices: 45.1 us -> 79.9 us  [swap_cross(): return lax.ppermute(values, 'grp', CROSS)]
    ppermute x4, waiting for transfers between devices: 2.89 us -> 20.5 us  [swap_diag(): return lax.ppermute(values, 'grp', DIAG)]
    unnamed x239 -> x258, local copies, waits for them, and re-layouts: 15.2 us -> 27.1 us
    ppermute x52 -> x51, starting transfers between devices: 71.4 us -> 63.6 us  [swap_blk(): return lax.ppermute(values, 'blk', [(i, i ^ bit) for i in range(count)])]
    pallas_call x3 -> x5, Pallas kernels: 101 us -> 92.9 us  [the longest x2 57.6 us: middle(): pl.pallas_call(functools.partial(middle_body, prev is not None), grid_spe...]
    ppermute x52 -> x51, waiting for transfers between devices: 316 us -> 321 us  [swap_blk(): return lax.ppermute(values, 'blk', [(i, i ^ bit) for i in range(count)])]
    ppermute x24 -> x19, starting transfers between devices: 22.1 us -> 20 us  [swap_cross(): return lax.ppermute(values, 'grp', CROSS)]
  transfers between devices with their start and end apart: 102 -> 98, of which waited for: 48 -> 49; matrix products, arithmetic and copies ran while one was open for 25% -> 21% of each run, Pallas kernels for 17% -> 15%
where the time goes in v4:
time: 998 us; the launch traced here: 987 us
  waiting for transfers between devices  463 us (46%)
  Pallas kernels  160 us (16%)
  other arithmetic  134 us (13%)
  local copies, waits for them, and re-layouts  94.1 us (9%)
  starting transfers between devices  91 us (9%)
  between operations  23.1 us (2%)
  matrix products  21.7 us (2%)
    ppermute x51, waiting for transfers between devices, swap_blk(): return lax.ppermute(values, 'blk', [(i, i ^ bit) for i in range(count)])  321 us
    ppermute x19, waiting for transfers between devices, swap_cross(): return lax.ppermute(values, 'grp', CROSS)  79.9 us
    ppermute x51, starting transfers between devices, swap_blk(): return lax.ppermute(values, 'blk', [(i, i ^ bit) for i in range(count)])  63.6 us
    pallas_call x2, Pallas kernels, middle(): pl.pallas_call(functools.partial(middle_body, prev is not None), grid_spe...  57.6 us
    reduce_scatter x1, waiting for transfers between devices, on_device(): lax.psum_scatter(down_grad_b, 'blk', scatter_dimension=0, axis_index_grou...  37.7 us
    pallas_call x2, Pallas kernels, adam_columns(): pl.pallas_call(functools.partial(adam_body, blk_count, rate, decay), grid...  34.2 us
    convert_element_type x25, other arithmetic, low(): return values.astype(jnp.bfloat16)  31.3 us
    unnamed x258, local copies, waits for them, and re-layouts  27.1 us
  transfers between devices with their start and end apart: 98, of which 49 were waited for; matrix products, arithmetic and copies ran while one was open for 21% of the time, Pallas kernels for 15%

profile of v4, /device:TPU:0, one launch (start us, length us, event | category | flops | bytes accessed | tf_op | source)
XLA Modules:
  0.0 987.2 jit_solution(5283057864420844943)
XLA Ops:
  91.4 28.3 %collective-permute-done.10 = bf16[2,128,512]{2,1,0:T(8,128)(2,1)S(1)} collective-permute-done((bf16[2,128,512]{2,1,0:T(8,128)(2,1)S(1)}, bf16[2,128,512]{2,1,0:T(8,128)(2,1)S(1)}, u32[]{:S(2)}, u32[]{:S(2)}) %collective-permute-start.10) | collective-permute-done | bytes 262176 | tf_op jit(solution)/shard_map/ppermute | solution.py:468
  132.4 22.1 %collective-permute-done.14 = bf16[2,2,2,128,256]{4,3,2,1,0:T(8,128)(2,1)S(1)} collective-permute-done((bf16[2,2,2,128,256]{4,3,2,1,0:T(8,128)(2,1)S(1)}, bf16[2,2,2,128,256]{4,3,2,1,0:T(8,128)(2,1)S(1)}, u32[]{:S(2)}, u32[]{:S(2)}) %collective-permute-start.14) | collective-permute-done | bytes 524320 | tf_op jit(solution)/shard_map/ppermute | solution.py:468
  156.4 10.6 %collective-permute-done.28 = bf16[2,192,608]{2,1,0:T(8,128)(2,1)S(1)} collective-permute-done((bf16[2,192,608]{2,1,0:T(8,128)(2,1)S(1)}, bf16[2,192,608]{2,1,0:T(8,128)(2,1)S(1)}, u32[]{:S(2)}, u32[]{:S(2)}) %collective-permute-start.28) | collective-permute-done | bytes 466976 | tf_op jit(solution)/shard_map/ppermute | solution.py:468
  178.0 14.5 %collective-permute-done.16 = bf16[2,192,384]{2,1,0:T(8,128)(2,1)S(1)} collective-permute-done((bf16[2,192,384]{2,1,0:T(8,128)(2,1)S(1)}, bf16[2,192,384]{2,1,0:T(8,128)(2,1)S(1)}, u32[]{:S(2)}, u32[]{:S(2)}) %collective-permute-start.16) | collective-permute-done | bytes 294944 | tf_op jit(solution)/shard_map/ppermute | solution.py:468
  194.3 12.7 %collective-permute-done.17 = bf16[2,2,192,384]{3,2,1,0:T(8,128)(2,1)S(1)} collective-permute-done((bf16[2,2,192,384]{3,2,1,0:T(8,128)(2,1)S(1)}, bf16[2,2,192,384]{3,2,1,0:T(8,128)(2,1)S(1)}, u32[]{:S(2)}, u32[]{:S(2)}) %collective-permute-start.17) | collective-permute-done | bytes 589856 | tf_op jit(solution)/shard_map/ppermute | solution.py:468
  209.9 24.6 %collective-permute-done.18 = bf16[1536,384]{1,0:T(8,128)(2,1)} collective-permute-done((bf16[1536,384]{1,0:T(8,128)(2,1)}, bf16[1536,384]{1,0:T(8,128)(2,1)}, u32[]{:S(2)}, u32[]{:S(2)}) %collective-permute-start.18) | collective-permute-done | bytes 1179680 | tf_op jit(solution)/shard_map/ppermute | solution.py:459
  257.4 9.9 %collective-permute-done.26 = bf16[128,1536]{1,0:T(8,128)(2,1)S(1)} collective-permute-done((bf16[128,1536]{1,0:T(8,128)(2,1)S(1)}, bf16[128,1536]{1,0:T(8,128)(2,1)S(1)}, u32[]{:S(2)}, u32[]{:S(2)}) %collective-permute-start.26) | collective-permute-done | bytes 393248 | tf_op jit(solution)/shard_map/ppermute | solution.py:468
  276.6 11.2 %collective-permute-done.21 = bf16[256,1536]{1,0:T(8,128)(2,1)S(1)} collective-permute-done((bf16[256,1536]{1,0:T(8,128)(2,1)S(1)}, bf16[256,1536]{1,0:T(8,128)(2,1)S(1)}, u32[]{:S(2)}, u32[]{:S(2)}) %collective-permute-start.21) | collective-permute-done | bytes 786464 | tf_op jit(solution)/shard_map/ppermute | solution.py:468
  307.8 16.3 %collective-permute-done.27 = bf16[2,128,1536]{2,1,0:T(8,128)(2,1)S(1)} collective-permute-done((bf16[2,128,1536]{2,1,0:T(8,128)(2,1)S(1)}, bf16[2,128,1536]{2,1,0:T(8,128)(2,1)S(1)}, u32[]{:S(2)}, u32[]{:S(2)}) %collective-permute-start.27) | collective-permute-done | bytes 786464 | tf_op jit(solution)/shard_map/ppermute | solution.py:468
  325.6 20.6 %collective-permute-done.29 = bf16[152,1536]{1,0:T(8,128)(2,1)S(1)} collective-permute-done((bf16[152,1536]{1,0:T(8,128)(2,1)S(1)}, bf16[152,1536]{1,0:T(8,128)(2,1)S(1)}, u32[]{:S(2)}, u32[]{:S(2)}) %collective-permute-start.29) | collective-permute-done | bytes 466976 | tf_op jit(solution)/shard_map/ppermute | solution.py:468
  367.2 22.0 %middle.2 = (bf16[2048,512]{1,0:T(8,128)(2,1)}, bf16[2048,512]{1,0:T(8,128)(2,1)}, bf16[2048,512]{1,0:T(8,128)(2,1)}, bf16[2048,1536]{1,0:T(8,128)(2,1)}) custom-call(s32[8]{0:T(128)S(1)} %stack.335.order, bf16[2048,1536]{1,0:T(8,128)(2,1)} %constant_dynamic-update-slice_fusion.5.h_ref, bf16[2048,1536]{1,0:T(8,128)(2,1)} %all-gather.11.cloned.1.call-done.dy_ref, ...), custom_call_target="tpu_custom_call" | custom-call | flops 16106127360 | bytes 31457280 | tf_op jit(solution)/shard_map/middle/pallas_call | solution.py:353
  392.4 10.1 %two_grads.2 = bf16[2,1536,512]{2,1,0:T(8,128)(2,1)} custom-call(bf16[2048,1536]{1,0:T(8,128)(2,1)} %constant_dynamic-update-slice_fusion.5.h_ref, bf16[2048,512]{1,0:T(8,128)(2,1)S(1)} %copy-done.13, bf16[2048,512]{1,0:T(8,128)(2,1)S(1)} %copy-done.14), custom_call_target="tpu_custom_call" | custom-call | flops 6442450944 | bytes 20971520 | tf_op jit(solution)/shard_map/two_grads/pallas_call | solution.py:381
  406.2 35.6 %middle.3 = (bf16[2048,608]{1,0:T(8,128)(2,1)}, bf16[2048,608]{1,0:T(8,128)(2,1)}, bf16[2048,608]{1,0:T(8,128)(2,1)}, bf16[2048,1536]{1,0:T(8,128)(2,1)}) custom-call(s32[8]{0:T(128)S(1)} %stack.335.order, bf16[2048,1536]{1,0:T(8,128)(2,1)} %constant_dynamic-update-slice_fusion.5.h_ref, bf16[2048,1536]{1,0:T(8,128)(2,1)} %all-gather.11.cloned.1.call-done.dy_ref, ...), custom_call_target="tpu_custom_call" | custom-call | flops 19126026240 | bytes 31457280 | tf_op jit(solution)/shard_map/middle/pallas_call | solution.py:353
  481.3 13.1 %two_grads.3 = bf16[2,1536,608]{2,1,0:T(8,128)(2,1)} custom-call(bf16[2048,1536]{1,0:T(8,128)(2,1)} %constant_dynamic-update-slice_fusion.5.h_ref, bf16[2048,608]{1,0:T(8,128)(2,1)S(1)} %copy-done.15, bf16[2048,608]{1,0:T(8,128)(2,1)S(1)} %copy-done.16), custom_call_target="tpu_custom_call" | custom-call | flops 7650410496 | bytes 20971520 | tf_op jit(solution)/shard_map/two_grads/pallas_call | solution.py:381
  503.8 12.0 %down.1 = bf16[2048,1536]{1,0:T(8,128)(2,1)} custom-call(s32[8]{0:T(128)S(1)} %stack.335.order, bf16[2048,512]{1,0:T(8,128)(2,1)S(1)} %copy-done.11, bf16[2048,608]{1,0:T(8,128)(2,1)} %get-tuple-element.133.hid_ref.hid_b_ref, bf16[512,1536]{1,0:T(8,128)(2,1)S(1)} %bitcast.483, bf16[608,1536]{1,0:T(8,128)(2,1)S(1)} %bitcast.481), custom_call_target="tpu_custom_call" | custom-call | flops 7046430720 | bytes 16777216 | tf_op jit(solution)/shard_map/down/pallas_call | solution.py:424
  530.7 37.7 %reduce-scatter.5.cloned.1.call-done = bf16[152,1536]{1,0:T(8,128)(2,1)} async-done(((bf16[608,1536]{1,0:T(8,128)(2,1)}), bf16[152,1536]{1,0:T(8,128)(2,1)}) %reduce-scatter.5.cloned.1.call-update) | async-done | bytes 466960 | tf_op jit(solution)/shard_map/reduce_scatter | solution.py:837
  595.7 15.0 %collective-permute-done.64 = bf16[256,384]{1,0:T(8,128)(2,1)S(1)} collective-permute-done((bf16[256,384]{1,0:T(8,128)(2,1)S(1)}, bf16[256,384]{1,0:T(8,128)(2,1)S(1)}, u32[]{:S(2)}, u32[]{:S(2)}) %collective-permute-start.64) | collective-permute-done | bytes 196640 | tf_op jit(solution)/shard_map/ppermute | solution.py:463
  632.0 39.8 %collective-permute-done.37 = bf16[2,2,2,128,256]{4,3,2,0,1:T(8,128)(2,1)S(1)} collective-permute-done((bf16[2,2,2,128,256]{4,3,2,0,1:T(8,128)(2,1)S(1)}, bf16[2,2,2,128,256]{4,3,2,0,1:T(8,128)(2,1)S(1)}, u32[]{:S(2)}, u32[]{:S(2)}) %collective-permute-start.37) | collective-permute-done | bytes 524320 | tf_op jit(solution)/shard_map/ppermute | solution.py:468
  677.8 11.4 %collective-permute-done.40 = bf16[2,2,128,256]{3,2,1,0:T(8,128)(2,1)S(1)} collective-permute-done((bf16[2,2,128,256]{3,2,1,0:T(8,128)(2,1)S(1)}, bf16[2,2,128,256]{3,2,1,0:T(8,128)(2,1)S(1)}, u32[]{:S(2)}, u32[]{:S(2)}) %collective-permute-start.40) | collective-permute-done | bytes 262176 | tf_op jit(solution)/shard_map/ppermute | solution.py:468
  703.0 42.7 %collective-permute-done.43 = bf16[2,128,512]{2,1,0:T(8,128)(2,1)} collective-permute-done((bf16[2,128,512]{2,1,0:T(8,128)(2,1)}, bf16[2,128,512]{2,1,0:T(8,128)(2,1)}, u32[]{:S(2)}, u32[]{:S(2)}) %collective-permute-start.43) | collective-permute-done | bytes 262176 | tf_op jit(solution)/shard_map/ppermute | solution.py:468
  887.2 21.2 %collective-permute-done.44 = bf16[256,1536]{1,0:T(8,128)(2,1)S(1)} collective-permute-done((bf16[256,1536]{1,0:T(8,128)(2,1)S(1)}, bf16[256,1536]{1,0:T(8,128)(2,1)S(1)}, u32[]{:S(2)}, u32[]{:S(2)}) %collective-permute-start.44) | collective-permute-done | bytes 786464 | tf_op jit(solution)/shard_map/ppermute | solution.py:459
  917.1 16.9 %multiply_subtract_fusion = (f32[1120,1536]{1,0:T(8,128)}, f32[1120,1536]{1,0:T(8,128)}, f32[1120,1536]{1,0:T(8,128)}) fusion(f32[1120,1536]{1,0:T(8,128)} %param.30, bf16[1120,1536]{1,0:T(8,128)(2,1)} %all-gather.13.cloned.1.call-done, f32[]{:T(128)} %min.3, f32[1120,1536]{1,0:T(8,128)} %param.42, f32[1120,1536]{1,0:T(8,128)} %param.36), kind=kLoop, calls=%fused_computation.5 | loop fusion | flops 29245440 | bytes 44728324 | tf_op jit(solution)/shard_map/sub | solution.py:66
  940.7 17.1 %adam_columns.2 = (f32[192,8960]{1,0:T(8,128)}, f32[192,8960]{1,0:T(8,128)}, f32[192,8960]{1,0:T(8,128)}) custom-call(f32[1]{0:T(128)} %bitcast.154.factor_ref, bf16[4,2,2,192,512]{4,3,2,1,0:T(8,128)(2,1)S(1)} %bitcast.472, bf16[4,2,2,192,608]{4,3,2,1,0:T(8,128)(2,1)} %bitcast.486, f32[192,8960]{1,0:T(8,128)} %w_ref.2, f32[192,8960]{1,0:T(8,128)} %m_ref.2, ...), custom_call_target="tpu_custom_call" | custom-call | flops 34406400 | bytes 44728320 | tf_op jit(solution)/shard_map/adam_columns/pallas_call | solution.py:143
  960.5 17.1 %adam_columns.3 = (f32[192,8960]{1,0:T(8,128)}, f32[192,8960]{1,0:T(8,128)}, f32[192,8960]{1,0:T(8,128)}) custom-call(f32[1]{0:T(128)} %bitcast.154.factor_ref, bf16[4,2,2,192,512]{4,3,2,1,0:T(8,128)(2,1)S(1)} %bitcast.473, bf16[4,2,2,192,608]{4,3,2,1,0:T(8,128)(2,1)} %bitcast.487, f32[192,8960]{1,0:T(8,128)} %w_ref.3, f32[192,8960]{1,0:T(8,128)} %m_ref.3, ...), custom_call_target="tpu_custom_call" | custom-call | flops 34406400 | bytes 44728320 | tf_op jit(solution)/shard_map/adam_columns/pallas_call | solution.py:143
  (700 shorter events, 481.4 us)
Async XLA Ops:
  7.2 343.8 %all-gather.15.cloned.1.call-start = ((), (), s32[]{:S(2)}) async-start(), calls=%async_computation.6 | async-start | bytes 3932160 | tf_op jit(solution)/shard_map/all_gather | solution.py:743
  90.4 264.6 %all-gather.17.cloned.1.call-start = ((), (), s32[]{:S(2)}) async-start(), calls=%async_computation.7 | async-start | bytes 4915200 | tf_op jit(solution)/shard_map/all_gather | solution.py:743
  168.3 194.7 %all-gather.11.cloned.1.call-start = ((), (), s32[]{:S(2)}) async-start(), calls=%async_computation.2 | async-start | bytes 7077888 | tf_op jit(solution)/shard_map/all_gather | solution.py:714
  209.9 289.2 %reduce-scatter.3.cloned.1.call-start = ((), (), s32[]{:S(2)}) async-start(), calls=%async_computation.3 | async-start | bytes 1966080 | tf_op jit(solution)/shard_map/reduce_scatter | solution.py:782
  304.0 55.3 %collective-permute-start.24 = (bf16[1024,1536]{1,0:T(8,128)(2,1)}, bf16[1024,1536]{1,0:T(8,128)(2,1)}, u32[]{:S(2)}, u32[]{:S(2)}) collective-permute-start(bf16[1024,1536]{1,0:T(8,128)(2,1)} %get-tuple-element.348), channel_id=1, source_target_pairs={{0,8},{8,0},{16,24},{24,16},{1,9},{9,1},{17,25},{25,17},{2,10},{10... | collective-permute-start | bytes 9437192 | tf_op jit(solution)/shard_map/ppermute | solution.py:455
  306.9 145.8 %collective-permute-start.60 = (bf16[256,1536]{1,0:T(8,128)(2,1)}, bf16[256,1536]{1,0:T(8,128)(2,1)}, u32[]{:S(2)}, u32[]{:S(2)}) collective-permute-start(bf16[256,1536]{1,0:T(8,128)(2,1)} %get-tuple-element.100.o_ref), channel_id=1, source_target_pairs={{0,16},{16,0},{8,24},{24,8},{1,17},{17,1},{9,25},{25,9},{2,18},{18... | collective-permute-start | bytes 2359304 | tf_op jit(solution)/shard_map/ppermute | solution.py:459
  349.3 53.2 %collective-permute-start.30 = (bf16[2,152,1536]{2,1,0:T(8,128)(2,1)}, bf16[2,152,1536]{2,1,0:T(8,128)(2,1)}, u32[]{:S(2)}, u32[]{:S(2)}) collective-permute-start(bf16[2,152,1536]{2,1,0:T(8,128)(2,1)} %pad_maximum_fusion.12), channel_id=1, source_target_pairs={{0,1},{1,0},{2,3},{3,2},{4,5},{5,4},{6,7},{7,6},{8,9},{9,8},{10,11... | collective-permute-start | bytes 2801672 | tf_op jit(solution)/shard_map/ppermute | solution.py:468
  452.5 115.8 %reduce-scatter.5.cloned.1.call-start = ((), (), s32[]{:S(2)}) async-start(), calls=%async_computation.4 | async-start | bytes 2334720 | tf_op jit(solution)/shard_map/reduce_scatter | solution.py:837
  465.5 59.5 %collective-permute-start.68 = (bf16[2,2,2,192,512]{4,3,2,1,0:T(8,128)(2,1)}, bf16[2,2,2,192,512]{4,3,2,1,0:T(8,128)(2,1)}, u32[]{:S(2)}, u32[]{:S(2)}) collective-permute-start(bf16[2,2,2,192,512]{4,3,2,1,0:T(8,128)(2,1)} %get-tuple-element.223), channel_id=1, source_target_pairs={{0,1},{1,0},{2,3},{3,2},{4,5},{5,4},{6,7},{7,6},{8,9},{9,8},{10,11... | collective-permute-start | bytes 4718600 | tf_op jit(solution)/shard_map/ppermute | solution.py:468
  473.9 443.2 %all-gather.13.cloned.1.call-start = ((), (), s32[]{:S(2)}) async-start(), calls=%async_computation.5 | async-start | bytes 4300800 | tf_op jit(solution)/shard_map/all_gather | solution.py:892
  522.3 50.3 %collective-permute-start.35 = (bf16[256,1536]{1,0:T(8,128)(2,1)}, bf16[256,1536]{1,0:T(8,128)(2,1)}, u32[]{:S(2)}, u32[]{:S(2)}) collective-permute-start(bf16[256,1536]{1,0:T(8,128)(2,1)} %pad_maximum_fusion.21), channel_id=1, source_target_pairs={{0,16},{16,0},{8,24},{24,8},{1,17},{17,1},{9,25},{25,9},{2,18},{18... | collective-permute-start | bytes 2359304 | tf_op jit(solution)/shard_map/ppermute | solution.py:459
  524.4 48.1 %collective-permute-start.36 = (bf16[256,1536]{1,0:T(8,128)(2,1)}, bf16[256,1536]{1,0:T(8,128)(2,1)}, u32[]{:S(2)}, u32[]{:S(2)}) collective-permute-start(bf16[256,1536]{1,0:T(8,128)(2,1)} %pad_maximum_fusion.22), channel_id=1, source_target_pairs={{0,2},{1,3},{2,0},{3,1},{4,6},{5,7},{6,4},{7,5},{8,10},{9,11},{10,... | collective-permute-start | bytes 2359304 | tf_op jit(solution)/shard_map/ppermute | solution.py:468
  528.9 64.3 %collective-permute-start.69 = (bf16[2,2,192,512]{3,2,0,1:T(8,128)(2,1)}, bf16[2,2,192,512]{3,2,0,1:T(8,128)(2,1)}, u32[]{:S(2)}, u32[]{:S(2)}) collective-permute-start(bf16[2,2,192,512]{3,2,0,1:T(8,128)(2,1)} %bitcast.460), channel_id=1, source_target_pairs={{0,4},{1,5},{2,6},{3,7},{4,0},{5,1},{6,2},{7,3},{8,12},{9,13},{10,... | collective-permute-start | bytes 2359304 | tf_op jit(solution)/shard_map/ppermute | solution.py:468
  570.2 363.8 %all-gather.19.cloned.1.call-start = ((), (), s32[]{:S(2)}) async-start(), calls=%async_computation.8 | async-start | bytes 3932160 | tf_op jit(solution)/shard_map/all_gather | solution.py:890
  614.9 58.6 %collective-permute-start.71 = (bf16[2,2,2,192,608]{4,3,2,1,0:T(8,128)(2,1)S(1)}, bf16[2,2,2,192,608]{4,3,2,1,0:T(8,128)(2,1)S(1)}, u32[]{:S(2)}, u32[]{:S(2)}) collective-permute-start(bf16[2,2,2,192,608]{4,3,2,1,0:T(8,128)(2,1)S(1)} %copy-done.49), channel_id=1, source_target_pairs={{0,1},{1,0},{2,3},{3,2},{4,5},{5,4},{6,7},{7,6},{8,9},{9,8},{10,11... | collective-permute-start | bytes 5603336 | tf_op jit(solution)/shard_map/ppermute | solution.py:468
  616.4 237.2 %collective-permute-start.34 = (bf16[1024,1536]{1,0:T(8,128)(2,1)}, bf16[1024,1536]{1,0:T(8,128)(2,1)}, u32[]{:S(2)}, u32[]{:S(2)}) collective-permute-start(bf16[1024,1536]{1,0:T(8,128)(2,1)} %slice.456), channel_id=1, source_target_pairs={{0,8},{8,0},{16,24},{24,16},{1,9},{9,1},{17,25},{25,17},{2,10},{10... | collective-permute-start | bytes 9437192 | tf_op jit(solution)/shard_map/ppermute | solution.py:455
  618.1 53.8 %collective-permute-start.37 = (bf16[2,2,2,128,256]{4,3,2,0,1:T(8,128)(2,1)S(1)}, bf16[2,2,2,128,256]{4,3,2,0,1:T(8,128)(2,1)S(1)}, u32[]{:S(2)}, u32[]{:S(2)}) collective-permute-start(bf16[2,2,2,128,256]{4,3,2,0,1:T(8,128)(2,1)S(1)} %bitcast.524), channel_id=1, source_target_pairs={{0,1},{1,0},{2,3},{3,2},{4,5},{5,4},{6,7},{7,6},{8,9},{9,8},{10,11... | collective-permute-start | bytes 1572872 | tf_op jit(solution)/shard_map/ppermute | solution.py:468
  618.6 74.5 %collective-permute-start.70 = (bf16[2,192,512]{2,1,0:T(8,128)(2,1)S(1)}, bf16[2,192,512]{2,1,0:T(8,128)(2,1)S(1)}, u32[]{:S(2)}, u32[]{:S(2)}) collective-permute-start(bf16[2,192,512]{2,1,0:T(8,128)(2,1)S(1)} %get-tuple-element.297), channel_id=1, source_target_pairs={{0,2},{1,3},{2,0},{3,1},{4,6},{5,7},{6,4},{7,5},{8,10},{9,11},{10,... | collective-permute-start | bytes 1179656 | tf_op jit(solution)/shard_map/ppermute | solution.py:468
  631.3 61.8 %collective-permute-start.65 = (bf16[2,2,192,384]{3,2,1,0:T(8,128)(2,1)S(1)}, bf16[2,2,192,384]{3,2,1,0:T(8,128)(2,1)S(1)}, u32[]{:S(2)}, u32[]{:S(2)}) collective-permute-start(bf16[2,2,192,384]{3,2,1,0:T(8,128)(2,1)S(1)} %get-tuple-element.259), channel_id=1, source_target_pairs={{0,1},{1,0},{2,3},{3,2},{4,5},{5,4},{6,7},{7,6},{8,9},{9,8},{10,11... | collective-permute-start | bytes 1769480 | tf_op jit(solution)/shard_map/ppermute | solution.py:468
  689.2 114.8 %collective-permute-start.72 = (bf16[2,2,192,608]{3,2,0,1:T(8,128)(2,1)}, bf16[2,2,192,608]{3,2,0,1:T(8,128)(2,1)}, u32[]{:S(2)}, u32[]{:S(2)}) collective-permute-start(bf16[2,2,192,608]{3,2,0,1:T(8,128)(2,1)} %bitcast.458), channel_id=1, source_target_pairs={{0,4},{1,5},{2,6},{3,7},{4,0},{5,1},{6,2},{7,3},{8,12},{9,13},{10,... | collective-permute-start | bytes 2801672 | tf_op jit(solution)/shard_map/ppermute | solution.py:468
  692.1 53.5 %collective-permute-start.43 = (bf16[2,128,512]{2,1,0:T(8,128)(2,1)}, bf16[2,128,512]{2,1,0:T(8,128)(2,1)}, u32[]{:S(2)}, u32[]{:S(2)}) collective-permute-start(bf16[2,128,512]{2,1,0:T(8,128)(2,1)} %fusion.48), channel_id=1, source_target_pairs={{0,4},{1,5},{2,6},{3,7},{4,0},{5,1},{6,2},{7,3},{8,12},{9,13},{10,... | collective-permute-start | bytes 786440 | tf_op jit(solution)/shard_map/ppermute | solution.py:468
  698.1 238.1 %all-gather.21.cloned.1.call-start = ((), (), s32[]{:S(2)}) async-start(), calls=%async_computation.9 | async-start | bytes 4915200 | tf_op jit(solution)/shard_map/all_gather | solution.py:953
  772.0 107.9 %collective-permute-start.52 = (bf16[512,1536]{1,0:T(8,128)(2,1)S(1)}, bf16[512,1536]{1,0:T(8,128)(2,1)}, u32[]{:S(2)}, u32[]{:S(2)}) collective-permute-start(bf16[512,1536]{1,0:T(8,128)(2,1)S(1)} %pad_maximum_fusion.6), channel_id=1, source_target_pairs={{0,8},{8,0},{16,24},{24,16},{1,9},{9,1},{17,25},{25,17},{2,10},{10... | collective-permute-start | bytes 4718600 | tf_op jit(solution)/shard_map/ppermute | solution.py:455
  885.5 72.3 %collective-permute-start.53 = (bf16[256,1536]{1,0:T(8,128)(2,1)}, bf16[256,1536]{1,0:T(8,128)(2,1)}, u32[]{:S(2)}, u32[]{:S(2)}) collective-permute-start(bf16[256,1536]{1,0:T(8,128)(2,1)} %fusion.22), channel_id=1, source_target_pairs={{0,16},{16,0},{8,24},{24,8},{1,17},{17,1},{9,25},{25,9},{2,18},{18... | collective-permute-start | bytes 2359304 | tf_op jit(solution)/shard_map/ppermute | solution.py:459
  (193 other events, 2241.7 us)
Sparse Core Ops, SparseCore 0:
  90.6 72.7 all-gather.14
  168.4 98.2 all-gather.16
  268.2 65.0 all-gather.10
  452.6 42.5 reduce-scatter.2
  498.1 70.1 reduce-scatter.4
  570.4 34.4 all-gather.12
  698.2 28.2 all-gather.18
  852.0 50.1 all-gather.20

commit v5 on v4

--- a/solution.py
+++ b/solution.py
@@ -112,10 +112,17 @@
     )(ids, gate, up)
 
 
-def adam_body(blk_count, rate, decay, factor_ref, first_ref, second_ref, w_ref, m_ref, v_ref, m_out, v_out, w_out):
+def near_at(away):
+    return (away & 1) * 2 + (away >> 1)
+
+
+def adam_body(blk_count, rate, decay, ids, factor_ref, first_ref, second_ref, w_ref, m_ref, v_ref, m_out, v_out, w_out):
     per = blk_count // 4
     sizes = [size for at, size in halves_of(FF // blk_count // 4)]
-    grads = [[[ref[k, bit] for bit in range(2)] for k in range(4)] for ref in (first_ref, second_ref)]
+    grads = [
+        [[ref[near_at(ids[0] ^ k), bit] for bit in range(2)] for k in range(4)]
+        for ref in (first_ref, second_ref)
+    ]
     parts = []
     for high in range(2):
         for bit in range(2):
@@ -131,27 +138,30 @@
     w_out[...] = w
 
 
-def adam_columns(which, factor, first, second, w, m, v, blk_count, rate, decay):
+def adam_columns(which, ids, factor, first, second, w, m, v, blk_count, rate, decay):
     rows = w.shape[0]
     step = 32 if rows % 32 == 0 else rows
-    spec = pl.BlockSpec((step, FF), lambda i: (i, 0))
+    spec = pl.BlockSpec((step, FF), lambda i, ids: (i, 0))
     shape = jax.ShapeDtypeStruct((rows, FF), jnp.float32)
     grads = [
-        pl.BlockSpec((4, None, 2, step, g.shape[-1]), lambda i: (0, which, 0, i, 0))
+        pl.BlockSpec((4, None, 2, step, g.shape[-1]), lambda i, ids: (0, which, 0, i, 0))
         for g in (first, second)
     ]
     return pl.pallas_call(
         functools.partial(adam_body, blk_count, rate, decay),
-        grid=(rows // step,),
-        in_specs=[pl.BlockSpec(memory_space=pltpu.SMEM)] + grads + [spec, spec, spec],
-        out_specs=[spec, spec, spec],
+        grid_spec=pltpu.PrefetchScalarGridSpec(
+            num_scalar_prefetch=1,
+            grid=(rows // step,),
+            in_specs=[pl.BlockSpec(memory_space=pltpu.SMEM)] + grads + [spec, spec, spec],
+            out_specs=[spec, spec, spec],
+        ),
         out_shape=[shape] * 3,
         compiler_params=pltpu.CompilerParams(vmem_limit_bytes=VMEM),
         cost_estimate=pl.CostEstimate(
             flops=rows * FF * 20, bytes_accessed=rows * FF * 26, transcendentals=rows * FF
         ),
         name="adam_columns",
-    )(factor, first, second, w, m, v)
+    )(ids, factor, first, second, w, m, v)
 
 
 def nt(a, b, **kw):
@@ -337,26 +347,30 @@
     dh_ref[...] = dh.astype(jnp.bfloat16)
 
 
-def middle(order, h, dy, wg, wu, wd, prev=None):
+def middle(order, h, dy, gate_up, wd, prev=None):
     count = h.shape[0]
     step = count // order.shape[0]
-    wide_here = wg.shape[1]
+    wide_here = wd.shape[0]
     row = pl.BlockSpec((step, D), lambda i, order: (i, 0))
     placed = pl.BlockSpec((step, D), lambda i, order: (order[i], 0))
     part = pl.BlockSpec((step, wide_here), lambda i, order: (i, 0))
     part_placed = pl.BlockSpec((step, wide_here), lambda i, order: (order[i], 0))
-
-    def whole(array):
-        return pl.BlockSpec(array.shape, lambda i, order: (0, 0), pipeline_mode=pl.Buffered(1))
-
+    once = pl.Buffered(1)
     extra = [] if prev is None else [prev]
     return pl.pallas_call(
         functools.partial(middle_body, prev is not None),
         grid_spec=pltpu.PrefetchScalarGridSpec(
             num_scalar_prefetch=1,
             grid=(count // step,),
-            in_specs=[row, placed, whole(wg), whole(wu), whole(wd)] + [row] * len(extra),
-            out_specs=[part_placed, part, part, row],
+            in_specs=[
+                placed,
+                row,
+                pl.BlockSpec((None, D, wide_here), lambda i, order: (0, 0, 0), pipeline_mode=once),
+                pl.BlockSpec((None, D, wide_here), lambda i, order: (1, 0, 0), pipeline_mode=once),
+                pl.BlockSpec((wide_here, D), lambda i, order: (0, 0), pipeline_mode=once),
+            ]
+            + [row] * len(extra),
+            out_specs=[part, part_placed, part_placed, row],
         ),
         out_shape=[jax.ShapeDtypeStruct((count, wide_here), jnp.bfloat16)] * 3
         + [jax.ShapeDtypeStruct((count, D), jnp.bfloat16)],
@@ -365,7 +379,7 @@
             flops=10 * count * D * wide_here, bytes_accessed=30 * 2**20, transcendentals=count * wide_here
         ),
         name="middle",
-    )(order, h, dy, wg, wu, wd, *extra)
+    )(order, h, dy, gate_up, gate_up, wd, *extra)
 
 
 def two_grads_body(h_ref, a_ref, b_ref, out_ref):
@@ -406,36 +420,32 @@
         cost_estimate=pl.CostEstimate(flops=2 * T * D * F, bytes_accessed=16 * 2**20, transcendentals=0),
         name="down_grad")(hid, dy)
 
-def down_body(order, hid_a_ref, hid_b_ref, wd_a_ref, wd_b_ref, o_ref):
+def down_body(hid_a_ref, hid_b_ref, wd_a_ref, wd_b_ref, o_ref):
     out = nn(hid_a_ref[...], wd_a_ref[...]) + nn(hid_b_ref[...], wd_b_ref[...])
     o_ref[...] = out.astype(jnp.bfloat16)
 
 
-def down(order, hid_a, hid_b, wd_a, wd_b):
+def down(hid_a, hid_b, wd_a, wd_b, step):
     count = hid_a.shape[0]
-    step = count // order.shape[0]
-
-    def placed(array):
-        return pl.BlockSpec((step, array.shape[1]), lambda i, order: (order[i], 0))
+
+    def rows(array):
+        return pl.BlockSpec((step, array.shape[1]), lambda i: (i, 0))
 
     def whole(array):
-        return pl.BlockSpec(array.shape, lambda i, order: (0, 0), pipeline_mode=pl.Buffered(1))
+        return pl.BlockSpec(array.shape, lambda i: (0, 0), pipeline_mode=pl.Buffered(1))
 
     return pl.pallas_call(
         down_body,
-        grid_spec=pltpu.PrefetchScalarGridSpec(
-            num_scalar_prefetch=1,
-            grid=(count // step,),
-            in_specs=[placed(hid_a), placed(hid_b), whole(wd_a), whole(wd_b)],
-            out_specs=pl.BlockSpec((step, D), lambda i, order: (i, 0)),
-        ),
+        grid=(count // step,),
+        in_specs=[rows(hid_a), rows(hid_b), whole(wd_a), whole(wd_b)],
+        out_specs=pl.BlockSpec((step, D), lambda i: (i, 0)),
         out_shape=jax.ShapeDtypeStruct((count, D), jnp.bfloat16),
         compiler_params=pltpu.CompilerParams(vmem_limit_bytes=VMEM),
         cost_estimate=pl.CostEstimate(
             flops=2 * count * D * (hid_a.shape[1] + hid_b.shape[1]), bytes_accessed=16 * 2**20, transcendentals=0
         ),
         name="down",
-    )(order, hid_a, hid_b, wd_a, wd_b)
+    )(hid_a, hid_b, wd_a, wd_b)
 
 
 CORE = [(0, 1), (1, 0), (2, 3), (3, 2)]
@@ -565,6 +575,26 @@
     return jnp.stack(
         [jnp.where(mine, other, values), jnp.where(mine, values, other)], axis=axis
     )
+
+
+def gather_near_stacked(values):
+    both = jnp.stack([values, swap_cross(values)])
+    return jnp.concatenate([both, swap_core(both)])
+
+
+def ring_order(count):
+    return list(range(0, count, 2)) + list(range(count - 1, 0, -2))
+
+
+def ring_groups(count):
+    return [[g * count + b for b in ring_order(count)] for g in range(4)]
+
+
+def gather_ring(values):
+    count = lax.axis_size("blk")
+    parts = lax.all_gather(values, ("grp", "blk"), axis=0, axis_index_groups=ring_groups(count))
+    ring = ring_order(count)
+    return [parts[ring.index(b)] for b in range(count)]
 
 
 def on_device(
@@ -632,24 +662,31 @@
     strip_wide = strip_q + HD
     small_send = jnp.pad(small_send, (0, -small_send.shape[0] % strip_wide))
     strip_local = jnp.concatenate([strip_local, small_send.reshape(-1, strip_wide)])
-    strip_first = gather_step(strip_local, [], bits[0])
-    strip_parts = []
-    cut = strip_wide // 2
-    for part, order in (
-        (strip_first[..., :cut], [team] + lows),
-        (strip_first[..., cut:], lows + [team]),
-    ):
-        done = [bits[0]]
-        for bit in order:
-            part = gather_step(part, done, bit)
-            done.append(bit)
-        strip_parts.append(part)
-    strip_all = jnp.concatenate(strip_parts, axis=-1).reshape(blk_count, -1, strip_wide)
-    strip = strip_all[:, :weight_rows].reshape(D, strip_wide)
-    small_all = strip_all[:, weight_rows:].reshape(blk_count, -1)
+    strip_list = gather_ring(strip_local)
+    strip = jnp.concatenate([part[:weight_rows] for part in strip_list])
+    small_all = jnp.stack([part[weight_rows:] for part in strip_list]).reshape(blk_count, -1)
     digits = low(jnp.stack([positions // 64, positions % 64], axis=1))
     digits = jnp.pad(digits, ((0, 0), (0, HD - 2)))
-    near_all = jnp.concatenate(gather_near(jnp.concatenate([flat_low, digits], axis=1)))
+    token_send = jnp.concatenate([flat_low, digits], axis=1)
+    token_cross = swap_cross(token_send)
+    dy_over = swap_blk(dy_low, team)
+    dy_cross = swap_cross(after(dy_low, token_cross))
+
+    def place(values, other, done, bit, lead=0):
+        mine = blk_bit(bit)
+        axis = lead + sum(1 for d in done if d > bit)
+        return jnp.stack(
+            [jnp.where(mine, other, values), jnp.where(mine, values, other)], axis=axis
+        )
+
+    out_strip = low(lax.dynamic_slice_in_dim(w_out, strip_q * grp, strip_q, 1))
+    out_zero = swap_blk(out_strip, bits[0])
+    out_strip = place(out_strip, out_zero, [], bits[0])
+    out_one = swap_blk(out_strip, team)
+    out_strip = place(out_strip, out_one, [bits[0]], team)
+    token_core = swap_core(jnp.stack([token_send, token_cross]))
+    near_all = jnp.concatenate([token_send, token_core[0], token_cross, token_core[1]])
+    near_all = after(near_all, out_strip)
     near_tokens = near_all[:, :D]
     near_positions = 64.0 * wide(near_all[:, D]) + wide(near_all[:, D + 1])
     vector = wide(small_all[:, :small_count].reshape(-1))
@@ -693,25 +730,13 @@
     query = jnp.concatenate([part[:, :strip_q] for part in strips], axis=1)
     key_value = jnp.concatenate([strips[k][:, strip_q:] for k in (0, 2, 1, 3)], axis=1)
     key_value = key_value.reshape(rows_here, block_len, 2 * KVD)
-    kv_first = gather_step(key_value, [], bits[0])
-    kv_parts = []
-    for part, order in (
-        (kv_first[..., :KVD], [team] + lows),
-        (kv_first[..., KVD:], lows + [team]),
-    ):
-        done = [bits[0]]
-        for bit in order:
-            part = gather_step(part, done, bit)
-            done.append(bit)
-        kv_parts.append(part)
-    kv_all = jnp.concatenate(kv_parts, axis=-1).reshape((blk_count,) + key_value.shape)
+    kv_all = jnp.stack(gather_ring(key_value))
 
     teams = [
         [g * blk_count + (i | t) for g in range(4) for t in (0, team)]
         for i in range(blk_count)
         if not i & team
     ]
-    dy_team = lax.all_gather(dy_low, ("grp", "blk"), axis=0, tiled=True, axis_index_groups=teams)
     order = jnp.stack(
         [
             (grp ^ (2 * (i & 1) + (i >> 2))) * 2 + (in_team ^ ((i >> 1) & 1))
@@ -723,62 +748,62 @@
     peers = [[i for i in range(blk_count) if (i & team) == t] for t in (0, team)]
     (low_first, size_first), (low_second, size_second) = halves_of(quarter)
 
-    def place(values, other, done, bit):
-        mine = blk_bit(bit)
-        axis = sum(1 for d in done if d > bit)
+    def team_pair(mine, got):
         return jnp.stack(
-            [jnp.where(mine, other, values), jnp.where(mine, values, other)], axis=axis
+            [jnp.where(mine_team, got, mine), jnp.where(mine_team, mine, got)], axis=1
         )
 
-    def lows_of(values, done, anchor):
+    def lows_of(values, done, anchor, lead=0):
         for bit in lows:
-            values = place(values, after(swap_blk(values, bit), anchor), done, bit)
+            values = place(values, after(swap_blk(values, bit), anchor), done, bit, lead)
             done = done + [bit]
         return values
 
-    def team_pair(mine, got):
-        return jnp.stack([jnp.where(mine_team, got, mine), jnp.where(mine_team, mine, got)])
-
-    def whole_weights(pair):
-        pairs = lax.all_gather(pair, "blk", axis=0, axis_index_groups=peers)
-        pairs = pairs.reshape((2, blk_count // 4) + pair.shape).transpose(3, 0, 2, 1, 4, 5)
-        return pairs[0].reshape(D, -1), pairs[1].reshape(D, -1)
-
     picked_a, picked_b = pick_columns(ids, w_gate, w_up, blk_count)
-    got_a = swap_blk(after(picked_a[1], strip_parts), team)
-    gate_a, up_a = whole_weights(team_pair(picked_a[0], after(got_a, strips)))
+    got_a = swap_blk(after(picked_a[1], out_one), team)
     got_b = swap_blk(after(picked_b[1], strip_out), team)
-    gate_b, up_b = whole_weights(team_pair(picked_b[0], after(got_b, kv_all)))
+    pair_a = after(team_pair(picked_a[0], after(got_a, strip_out)), key_value)
+    pair_a_got = swap_blk(pair_a, bits[0])
 
     down_at = quarter * grp
     down_a = low(lax.dynamic_slice_in_dim(w_down, down_at, size_first, 0))
-    down_got = swap_blk(after(down_a, strip_first), bits[0])
-    down_a = place(down_a, after(down_got, strip_out), [], bits[0])
+    down_got = swap_blk(after(down_a, out_zero), bits[0])
+    down_a = after(place(down_a, after(down_got, strip_out), [], bits[0]), key_value)
     down_a = lows_of(down_a, [bits[0]], kv_all).reshape(widths[0], D)
 
-    out_strip = low(lax.dynamic_slice_in_dim(w_out, strip_q * grp, strip_q, 1))
-    out_got = swap_blk(after(out_strip, strip_first), bits[0])
-    out_strip = place(out_strip, after(out_got, strip_parts), [], bits[0])
-    out_got = swap_blk(out_strip, team)
-    out_strip = place(out_strip, after(out_got, strip_out), [bits[0]], team)
-    out_strip = lows_of(out_strip, [bits[0], team], kv_first).reshape(HQD, strip_q)
-    out_cross = after(swap_cross(out_strip), kv_all)
-    out_both = jnp.stack([out_strip, out_cross])
-    out_core = swap_core(out_both)
+    out_strip = lows_of(out_strip, [bits[0], team], strip_out).reshape(HQD, strip_q)
+    out_cross = swap_cross(after(out_strip, key_value))
+    out_core = swap_core(jnp.stack([out_strip, out_cross]))
     out_full = jnp.concatenate(by_place([out_strip, out_core[0], out_cross, out_core[1]]), axis=1)
-
+    kv_all = after(kv_all, out_full)
+
+    pair_a = place(pair_a, after(pair_a_got, kv_all), [team], bits[0], 1)
+    gate_up_a = lows_of(pair_a, [bits[0], team], kv_all, 1).reshape(2, D, -1)
     down_b = low(lax.dynamic_slice_in_dim(w_down, down_at + size_first, size_second, 0))
     down_got_b = swap_blk(after(down_b, kv_all), bits[0])
+    pair_b = team_pair(picked_b[0], after(got_b, kv_all))
+    pair_b_got = swap_blk(pair_b, bits[0])
+    dy_cross, dy_over = after((dy_cross, dy_over), kv_all)
+    dy_first = swap_blk(dy_cross[:half], team)
+    dy_second = swap_cross(dy_over[half:])
 
     att_in, lse = attend(attend_ids, query, kv_all, seg_key, seg_query, block_len)
-    down_b = place(down_b, after(down_got_b, att_in), [], bits[0])
 
     flat = wide(flat_low)
     resid = flat + jnp.dot(att_in, out_full, preferred_element_type=jnp.float32)
     h_two = low(norm_apply(resid, gain_two))
-    h_team = gather_tokens(h_two, team)
-    hidden_a, d_gate_a, d_up_a, part_a = middle(order, h_team, dy_team, gate_a, up_a, down_a)
+    h_team = lax.all_gather(h_two, ("grp", "blk"), axis=0, tiled=True, axis_index_groups=teams)
+    dy_first, dy_second, down_got_b, pair_b_got = after(
+        (dy_first, dy_second, down_got_b, pair_b_got), h_two
+    )
+    dy_chip = jnp.concatenate([dy_low, dy_cross, dy_over, dy_first, dy_second])
+    dy_team = jnp.concatenate([dy_chip, swap_core(dy_chip)])
+    down_b = place(down_b, down_got_b, [], bits[0])
+    pair_b = place(pair_b, pair_b_got, [team], bits[0], 1)
+    h_team = after(h_team, (dy_team, down_b, pair_b))
+    hidden_a, d_gate_a, d_up_a, part_a = middle(order, h_team, dy_team, gate_up_a, down_a)
     down_b = lows_of(down_b, [bits[0]], hidden_a).reshape(widths[1], D)
+    gate_up_b = lows_of(pair_b, [bits[0], team], hidden_a, 1).reshape(2, D, -1)
     down_share_a = lax.psum_scatter(
         down_grad(hidden_a, dy_team), "blk", scatter_dimension=0, axis_index_groups=peers, tiled=True
     )
@@ -807,7 +832,13 @@
         values = part_sum(keep, got)
         mine = lax.dynamic_index_in_dim(values, in_team, 1, keepdims=False)
         send = lax.dynamic_index_in_dim(values, 1 - in_team, 1, keepdims=False)
-        return mine, swap_blk(send, team)
+        return values, (mine, swap_blk(send, team))
+
+    def rows_second(keep, got):
+        values = part_sum(keep, got)
+        for i in range(len(lows) - 2, -1, -1):
+            values = part_sum(*part_sent(values, 1 + i, lows[i]))
+        return part_sent(values, 0, bits[0])
 
     def columns_last(mine, got):
         return jnp.stack(
@@ -816,7 +847,7 @@
 
     first_a = columns_first(column_grad_a)
     hidden_b, d_gate_b, d_up_b, d_htwo_part = middle(
-        order, after(h_team, column_grad_a), dy_team, gate_b, up_b, down_b, part_a
+        order, after(h_team, column_grad_a), dy_team, gate_up_b, down_b, part_a
     )
 
     def chip_sum(values, came):
@@ -834,8 +865,8 @@
 
     d_came = swap_core(d_htwo_part[chip_rows:])
     down_grad_b = down_grad(hidden_b, dy_team)
-    down_share_b = lax.psum_scatter(
-        down_grad_b, "blk", scatter_dimension=0, axis_index_groups=peers, tiled=True
+    rows_b = part_sent(
+        down_grad_b.reshape((2,) + low_shape + (size_second, D)), len(lows), lows[-1]
     )
     d_chip = chip_sum(d_htwo_part, after(d_came, down_grad_b))
     d_far = scatter_far(d_chip)
@@ -843,9 +874,8 @@
     first_b = columns_first(column_grad_b)
     d_far = after(d_far, column_grad_b)
     d_cross, d_over = scatter_near(d_chip, *d_far)
-    out_part = down(order, *after((hidden_a, hidden_b), d_far), down_a, down_b)
+    out_part = down(*after((hidden_a, hidden_b), d_far), down_a, down_b, token_count)
     out_came = swap_core(out_part[chip_rows:])
-    second_a = columns_second(*after(first_a, out_part))
     d_cross, d_over = after((d_cross, d_over), out_part)
     d_htwo = wide(d_chip[:token_count]) + wide(d_cross) + wide(d_over)
 
@@ -853,6 +883,10 @@
     d_resid_norm, grad_gain_two = norm_back_two(d_htwo)
     d_resid = wide(dy_low) + d_resid_norm
     d_att = low(d_resid)
+    second_a = columns_second(*after(first_a, d_att))
+    rows_b = rows_second(*after(rows_b, d_att))
+    out_chip = chip_sum(out_part, after(out_came, d_att))
+    out_far = scatter_far(out_chip)
 
     d_attended = low(right_transposed(d_att, out_full))
     own_angles = angles_of(positions)
@@ -871,26 +905,19 @@
         block_len,
     )
     second_b = columns_second(*after(first_b, d_query))
-    third_a = columns_third(*after(second_a, d_query))
-    dkv = dkv.reshape((2,) * len(bits) + (rows_here, block_len, 2 * KVD))
-    dkv_first = scatter_bits(dkv[..., :KVD], bits, lows[::-1])
-    dkv_second = scatter_bits(dkv[..., KVD:], bits, [team])
-    dkv_first = scatter_bits(dkv_first, bits[:2], [team])
-    dkv_second = scatter_bits(dkv_second, [bits[0]] + lows, lows[::-1])
-    dkv = jnp.concatenate([dkv_first, dkv_second], axis=-1)
-    dkv_mid = dkv
-    out_chip = chip_sum(out_part, after(out_came, dkv_mid))
-    dkv = wide(scatter_bits(dkv, bits[:1], bits[:1])).reshape(token_count, 2, KVH, HD)
-    d_key = low(rotate_by(dkv[:, 0], cosine[:, None], -sine[:, None]))
-    d_value = low(dkv[:, 1])
-    out_far = after(scatter_far(out_chip), d_key)
-    out_cross, out_over = scatter_near(out_chip, *out_far)
-    third_b = columns_third(*after(second_b, d_key))
-    share_a = columns_last(*after(third_a, dkv_mid))
-    all_a = lax.all_gather(share_a, "grp", axis=0)
+    dkv = jnp.concatenate([dkv[b] for b in ring_order(blk_count)])
+    dkv = lax.psum_scatter(
+        dkv.reshape(blk_count * token_count, 2 * KVD),
+        ("grp", "blk"),
+        scatter_dimension=0,
+        axis_index_groups=ring_groups(blk_count),
+        tiled=True,
+    )
+    sum_a, third_a = columns_third(*after(second_a, d_query))
+    down_share_b = part_sum(*after(rows_b, d_query))
+    out_cross, out_over = scatter_near(out_chip, *after(out_far, d_query))
     share_down = jnp.concatenate([down_share_a, down_share_b])
     grad_down = lax.all_gather(share_down, "grp", axis=0, tiled=True)
-
     def to_strips(parts):
         parts = by_place(parts)
         return jnp.concatenate(
@@ -900,17 +927,22 @@
     near_dq = to_strips([d_query[:, strip_q * k : strip_q * (k + 1)] for k in range(4)])
     block_shape = (2,) * len(bits) + (weight_rows, -1)
     query_grad = low(left_product(near_one, near_dq)).reshape(block_shape)
-    steps_query = part_sent(after(query_grad, dkv_mid), len(bits) - 1, bits[-1])
+    steps_query = part_sent(query_grad, len(bits) - 1, bits[-1])
+    dkv = wide(after(dkv, (sum_a, share_down, query_grad))).reshape(token_count, 2, KVH, HD)
+    d_key = low(rotate_by(dkv[:, 0], cosine[:, None], -sine[:, None]))
+    d_value = low(dkv[:, 1])
     near_dkv = to_strips([(d_value if k % 2 else d_key)[:, k // 2] for k in range(4)])
     kv_grad = low(left_product(near_one, near_dkv)).reshape(block_shape)
     steps_kv = part_sent(kv_grad, len(bits) - 1, bits[-1])
+    sum_b, third_b = columns_third(*after(second_b, d_key))
+    near_a = gather_near_stacked(columns_last(*after(third_a, d_key)))
     for i in range(len(bits) - 2, -1, -1):
-        steps_query = part_sent(part_sum(*after(steps_query, kv_grad)), i, bits[i])
+        steps_query = part_sent(part_sum(*after(steps_query, d_key)), i, bits[i])
         kv_sum = part_sum(*steps_kv)
         kv_grad = kv_sum
         steps_kv = part_sent(kv_sum, i, bits[i])
     share_kv = part_sum(*steps_kv)
-    share_query = part_sum(*after(steps_query, share_kv))
+    share_query = part_sum(*after(steps_query, kv_grad))
     grad_bias = jnp.concatenate(
         [
             jnp.sum(wide(part), axis=0)
@@ -925,11 +957,11 @@
     near_rms = lax.rsqrt(jnp.mean(near_wide * near_wide, axis=-1, keepdims=True) + NORM_EPS)
     gain_one_part = jnp.sum(near_hone * near_wide * near_rms, axis=0)
 
-    near_att = jnp.concatenate(gather_near(att_in))
+    near_att = jnp.concatenate(gather_near(after(att_in, hidden_a)))
     near_datt = to_strips([d_att[:, strip_q * k : strip_q * (k + 1)] for k in range(4)])
     out_grad = low(left_product(near_att, after(near_datt, d_attended))).reshape(block_shape)
     steps_out = part_sent(out_grad, len(bits) - 1, bits[-1])
-    anchors = [dkv_mid, near_dkv]
+    anchors = [d_query, d_key]
     for i in range(len(bits) - 2, -1, -1):
         anchor = anchors[min(len(bits) - 2 - i, 1)]
         steps_out = part_sent(part_sum(*after(steps_out, anchor)), i, bits[i])
@@ -949,8 +981,7 @@
         axes.remove(bit)
     share_vector = vector_term
 
-    share_b = columns_last(*after(third_b, near_dkv))
-    all_b = lax.all_gather(share_b, "grp", axis=0)
+    near_b = gather_near_stacked(columns_last(*after(third_b, kv_grad)))
     grad_out = jnp.concatenate(gather_grp(share_out), axis=1)
     query_parts = gather_grp(share_query)
     key_parts = gather_grp(share_kv)
@@ -965,7 +996,7 @@
     square_sum = square_total(
         [
             wide(s)
-            for s in (share_query, share_kv, share_out, share_a, share_b, share_down)
+            for s in (share_query, share_kv, share_out, sum_a, sum_b, share_down)
         ]
     ) + 0.25 * jnp.sum(share_vector * share_vector)
     square_sum = jnp.full((8, 128), square_sum)
@@ -978,10 +1009,10 @@
     factor = after(factor, out_tokens)
 
     new_first_gate, new_second_gate, new_gate = adam_columns(
-        0, factor[None], all_a, all_b, w_gate, first_gate, second_gate, blk_count, RATE_GATE, WEIGHT_DECAY
+        0, ids, factor[None], near_a, near_b, w_gate, first_gate, second_gate, blk_count, RATE_GATE, WEIGHT_DECAY
     )
     new_first_up, new_second_up, new_up = adam_columns(
-        1, factor[None], all_a, all_b, w_up, first_up, second_up, blk_count, RATE_GATE, WEIGHT_DECAY
+        1, ids, factor[None], near_a, near_b, w_up, first_up, second_up, blk_count, RATE_GATE, WEIGHT_DECAY
     )
     norm_value_one, norm_back_one = jax.vjp(norm_apply, flat, gain_one)
     d_hone = after(d_hone + wide(after(d_hone_cross, new_gate)), new_gate)

time: 998 us -> 954 us (0.956)
  waiting for transfers between devices: 463 us -> 399 us
  starting transfers between devices: 91 us -> 104 us
    ppermute x51 -> x42, waiting for transfers between devices: 321 us -> 254 us  [swap_blk(): return lax.ppermute(values, 'blk', [(i, i ^ bit) for i in range(count)])]
    all_gather x5 -> x3, waiting for transfers between devices: 0.03 us -> 40 us  [the longest x2 40 us: gather_ring(): lax.all_gather(values, ('grp', 'blk'), axis=0, axis_index_groups=ring_gro...]
    reduce_scatter x1, waiting for transfers between devices: 37.7 us -> 0.01 us  [on_device(): lax.psum_scatter(dkv.reshape(blk_count * token_count, 2 * KVD), ('grp', '...]
    ppermute x19 -> x21, waiting for transfers between devices: 79.9 us -> 96.7 us  [swap_cross(): return lax.ppermute(values, 'grp', CROSS)]
    ppermute x4, waiting for transfers between devices: 20.5 us -> 4.03 us  [swap_diag(): return lax.ppermute(values, 'grp', DIAG)]
    unnamed x258 -> x272, local copies, waits for them, and re-layouts: 27.1 us -> 42.2 us
    ppermute x19 -> x21, starting transfers between devices: 20 us -> 34.4 us  [swap_cross(): return lax.ppermute(values, 'grp', CROSS)]
    convert_element_type x25 -> x22, other arithmetic: 31.3 us -> 25.6 us  [low(): return values.astype(jnp.bfloat16)]
  transfers between devices with their start and end apart: 98 -> 91, of which waited for: 49 -> 38; matrix products, arithmetic and copies ran while one was open for 21% -> 23% of each run, Pallas kernels for 15% -> 15%
where the time goes in v5:
time: 954 us; the launch traced here: 942 us
  waiting for transfers between devices  399 us (42%)
  Pallas kernels  162 us (17%)
  other arithmetic  133 us (14%)
  starting transfers between devices  104 us (11%)
  local copies, waits for them, and re-layouts  99.4 us (10%)
  between operations  23.1 us (2%)
  matrix products  20.2 us (2%)
    ppermute x42, waiting for transfers between devices, swap_blk(): return lax.ppermute(values, 'blk', [(i, i ^ bit) for i in range(count)])  254 us
    ppermute x21, waiting for transfers between devices, swap_cross(): return lax.ppermute(values, 'grp', CROSS)  96.7 us
    ppermute x42, starting transfers between devices, swap_blk(): return lax.ppermute(values, 'blk', [(i, i ^ bit) for i in range(count)])  65 us
    pallas_call x2, Pallas kernels, middle(): pl.pallas_call(functools.partial(middle_body, prev is not None), grid_spe...  60.9 us
    unnamed x272, local copies, waits for them, and re-layouts  42.2 us
    all_gather x2, waiting for transfers between devices, gather_ring(): lax.all_gather(values, ('grp', 'blk'), axis=0, axis_index_groups=ring_gro...  40 us
    pallas_call x2, Pallas kernels, adam_columns(): pl.pallas_call(functools.partial(adam_body, blk_count, rate, decay), grid...  35.1 us
    ppermute x21, starting transfers between devices, swap_cross(): return lax.ppermute(values, 'grp', CROSS)  34.4 us
  transfers between devices with their start and end apart: 91, of which 38 were waited for; matrix products, arithmetic and copies ran while one was open for 23% of the time, Pallas kernels for 15%

profile of v5, /device:TPU:0, one launch (start us, length us, event | category | flops | bytes accessed | tf_op | source)
XLA Modules:
  0.0 941.9 jit_solution(304833983220395558)
XLA Ops:
  16.6 14.7 %collective-permute-done = bf16[256,1664]{1,0:T(8,128)(2,1)S(1)} collective-permute-done((bf16[256,1664]{1,0:T(8,128)(2,1)S(1)}, bf16[256,1664]{1,0:T(8,128)(2,1)S(1)}, u32[]{:S(2)}, u32[]{:S(2)}) %collective-permute-start) | collective-permute-done | bytes 852000 | tf_op jit(solution)/shard_map/ppermute | solution.py:469
  38.6 9.6 %collective-permute-done.3 = bf16[2,192,384]{2,1,0:T(8,128)(2,1)S(1)} collective-permute-done((bf16[2,192,384]{2,1,0:T(8,128)(2,1)S(1)}, bf16[2,192,384]{2,1,0:T(8,128)(2,1)S(1)}, u32[]{:S(2)}, u32[]{:S(2)}) %collective-permute-start.3) | collective-permute-done | bytes 294944 | tf_op jit(solution)/shard_map/ppermute | solution.py:478
  58.3 17.3 %all-gather.13.cloned.1.call-done = bf16[8,194,512]{2,1,0:T(8,128)(2,1)} async-done(((bf16[1,194,512]{2,1,0:T(8,128)(2,1)}), bf16[8,194,512]{2,1,0:T(8,128)(2,1)}) %all-gather.13.cloned.1.call-update) | async-done | bytes 1589264 | tf_op jit(solution)/shard_map/all_gather | solution.py:595
  107.8 27.4 %collective-permute-done.8 = bf16[1536,384]{1,0:T(8,128)(2,1)S(1)} collective-permute-done((bf16[1536,384]{1,0:T(8,128)(2,1)S(1)}, bf16[1536,384]{1,0:T(8,128)(2,1)S(1)}, u32[]{:S(2)}, u32[]{:S(2)}) %collective-permute-start.8) | collective-permute-done | bytes 1179680 | tf_op jit(solution)/shard_map/ppermute | solution.py:469
  146.5 22.8 %all-gather.7.cloned.1.call-done = bf16[8,2,128,512]{3,2,1,0:T(8,128)(2,1)} async-done(((bf16[1,2,128,512]{3,2,1,0:T(8,128)(2,1)}), bf16[8,2,128,512]{3,2,1,0:T(8,128)(2,1)}) %all-gather.7.cloned.1.call-update) | async-done | bytes 2097168 | tf_op jit(solution)/shard_map/all_gather | solution.py:595
  210.1 27.5 %collective-permute-done.18 = bf16[2,192,512]{2,1,0:T(8,128)(2,1)S(1)} collective-permute-done((bf16[2,192,512]{2,1,0:T(8,128)(2,1)S(1)}, bf16[2,192,512]{2,1,0:T(8,128)(2,1)S(1)}, u32[]{:S(2)}, u32[]{:S(2)}) %collective-permute-start.18) | collective-permute-done | bytes 393248 | tf_op jit(solution)/shard_map/ppermute | solution.py:478
  239.0 11.2 %collective-permute-done.15 = bf16[2,192,608]{2,1,0:T(8,128)(2,1)S(1)} collective-permute-done((bf16[2,192,608]{2,1,0:T(8,128)(2,1)S(1)}, bf16[2,192,608]{2,1,0:T(8,128)(2,1)S(1)}, u32[]{:S(2)}, u32[]{:S(2)}) %collective-permute-start.15) | collective-permute-done | bytes 466976 | tf_op jit(solution)/shard_map/ppermute | solution.py:478
  250.4 9.6 %collective-permute-start.16 = (bf16[2,2,192,608]{3,2,0,1:T(8,128)(2,1)S(1)}, bf16[2,2,192,608]{3,2,0,1:T(8,128)(2,1)S(1)}, u32[]{:S(2)}, u32[]{:S(2)}) collective-permute-start(bf16[2,2,192,608]{3,2,0,1:T(8,128)(2,1)S(1)} %pad_maximum_fusion.17), channel_id=1, source_target_pairs={{0,4},{1,5},{2,6},{3,7},{4,0},{5,1},{6,2},{7,3},{8,12},{9,13},{10,... | collective-permute-start | bytes 2801672 | tf_op jit(solution)/shard_map/ppermute | solution.py:478
  279.5 31.5 %collective-permute-done.12 = bf16[128,1536]{1,0:T(8,128)(2,1)S(1)} collective-permute-done((bf16[128,1536]{1,0:T(8,128)(2,1)S(1)}, bf16[128,1536]{1,0:T(8,128)(2,1)S(1)}, u32[]{:S(2)}, u32[]{:S(2)}) %collective-permute-start.12) | collective-permute-done | bytes 393248 | tf_op jit(solution)/shard_map/ppermute | solution.py:478
  311.1 30.0 %collective-permute-done.14 = bf16[152,1536]{1,0:T(8,128)(2,1)S(1)} collective-permute-done((bf16[152,1536]{1,0:T(8,128)(2,1)S(1)}, bf16[152,1536]{1,0:T(8,128)(2,1)S(1)}, u32[]{:S(2)}, u32[]{:S(2)}) %collective-permute-start.14) | collective-permute-done | bytes 466976 | tf_op jit(solution)/shard_map/ppermute | solution.py:478
  357.7 25.8 %collective-permute-done.20 = bf16[2,2,2,192,512]{4,3,0,2,1:T(8,128)(2,1)S(1)} collective-permute-done((bf16[2,2,2,192,512]{4,3,0,2,1:T(8,128)(2,1)S(1)}, bf16[2,2,2,192,512]{4,3,0,2,1:T(8,128)(2,1)S(1)}, u32[]{:S(2)}, u32[]{:S(2)}) %collective-permute-start.20) | collective-permute-done | bytes 1572896 | tf_op jit(solution)/shard_map/ppermute | solution.py:478
  389.7 23.3 %middle.2 = (bf16[2048,512]{1,0:T(8,128)(2,1)S(1)}, bf16[2048,512]{1,0:T(8,128)(2,1)S(1)}, bf16[2048,512]{1,0:T(8,128)(2,1)}, bf16[2048,1536]{1,0:T(8,128)(2,1)}) custom-call(s32[8]{0:T(128)S(1)} %stack.310.order, bf16[2048,1536]{1,0:T(8,128)(2,1)} %all-gather.9.cloned.1.call-done.h_ref, bf16[2048,1536]{1,0:T(8,128)(2,1)} %constant_dynamic-update-slice_fusion.5.dy_ref, ...), custom_call_target="tpu_custom_call" | custom-call | flops 16106127360 | bytes 31457280 | tf_op jit(solution)/shard_map/middle/pallas_call | solution.py:360
  415.9 10.2 %two_grads.2 = bf16[2,1536,512]{2,1,0:T(8,128)(2,1)} custom-call(bf16[2048,1536]{1,0:T(8,128)(2,1)} %all-gather.9.cloned.1.call-done.h_ref, bf16[2048,512]{1,0:T(8,128)(2,1)S(1)} %get-tuple-element.144.a_ref, bf16[2048,512]{1,0:T(8,128)(2,1)S(1)} %copy-done.13), custom_call_target="tpu_custom_call" | custom-call | flops 6442450944 | bytes 20971520 | tf_op jit(solution)/shard_map/two_grads/pallas_call | solution.py:395
  431.1 14.5 %collective-permute-done.24 = bf16[2,152,1536]{2,1,0:T(8,128)(2,1)} collective-permute-done((bf16[2,152,1536]{2,1,0:T(8,128)(2,1)}, bf16[2,152,1536]{2,1,0:T(8,128)(2,1)}, u32[]{:S(2)}, u32[]{:S(2)}) %collective-permute-start.24) | collective-permute-done | bytes 933920 | tf_op jit(solution)/shard_map/ppermute | solution.py:478
  447.3 37.6 %middle.3 = (bf16[2048,608]{1,0:T(8,128)(2,1)S(1)}, bf16[2048,608]{1,0:T(8,128)(2,1)}, bf16[2048,608]{1,0:T(8,128)(2,1)}, bf16[2048,1536]{1,0:T(8,128)(2,1)}) custom-call(s32[8]{0:T(128)S(1)} %stack.310.order, bf16[2048,1536]{1,0:T(8,128)(2,1)} %all-gather.9.cloned.1.call-done.h_ref, bf16[2048,1536]{1,0:T(8,128)(2,1)} %constant_dynamic-update-slice_fusion.5.dy_ref, ...), custom_call_target="tpu_custom_call" | custom-call | flops 19126026240 | bytes 31457280 | tf_op jit(solution)/shard_map/middle/pallas_call | solution.py:360
  527.0 13.5 %two_grads.3 = bf16[2,1536,608]{2,1,0:T(8,128)(2,1)} custom-call(bf16[2048,1536]{1,0:T(8,128)(2,1)} %all-gather.9.cloned.1.call-done.h_ref, bf16[2048,608]{1,0:T(8,128)(2,1)S(1)} %copy-done.14, bf16[2048,608]{1,0:T(8,128)(2,1)S(1)} %copy-done.15), custom_call_target="tpu_custom_call" | custom-call | flops 7650410496 | bytes 20971520 | tf_op jit(solution)/shard_map/two_grads/pallas_call | solution.py:395
  550.6 11.5 %down.1 = bf16[2048,1536]{1,0:T(8,128)(2,1)} custom-call(bf16[2048,512]{1,0:T(8,128)(2,1)S(1)} %copy-done.10, bf16[2048,608]{1,0:T(8,128)(2,1)} %copy-done.11, bf16[512,1536]{1,0:T(8,128)(2,1)S(1)} %bitcast.492, bf16[608,1536]{1,0:T(8,128)(2,1)S(1)} %bitcast.489), custom_call_target="tpu_custom_call" | custom-call | flops 7046430720 | bytes 16777216 | tf_op jit(solution)/shard_map/down/pallas_call | solution.py:437
  626.0 59.8 %collective-permute-done.38 = bf16[152,1536]{1,0:T(8,128)(2,1)S(1)} collective-permute-done((bf16[152,1536]{1,0:T(8,128)(2,1)S(1)}, bf16[152,1536]{1,0:T(8,128)(2,1)S(1)}, u32[]{:S(2)}, u32[]{:S(2)}) %collective-permute-start.38) | collective-permute-done | bytes 466976 | tf_op jit(solution)/shard_map/ppermute | solution.py:478
  720.6 18.6 %collective-permute-done.33 = bf16[256,1536]{1,0:T(8,128)(2,1)S(1)} collective-permute-done((bf16[256,1536]{1,0:T(8,128)(2,1)S(1)}, bf16[256,1536]{1,0:T(8,128)(2,1)S(1)}, u32[]{:S(2)}, u32[]{:S(2)}) %collective-permute-start.33) | collective-permute-done | bytes 786464 | tf_op jit(solution)/shard_map/ppermute | solution.py:469
  740.9 14.0 %collective-permute-done.34 = bf16[256,1536]{1,0:T(8,128)(2,1)S(1)} collective-permute-done((bf16[256,1536]{1,0:T(8,128)(2,1)S(1)}, bf16[256,1536]{1,0:T(8,128)(2,1)S(1)}, u32[]{:S(2)}, u32[]{:S(2)}) %collective-permute-start.34) | collective-permute-done | bytes 786464 | tf_op jit(solution)/shard_map/ppermute | solution.py:478
  853.2 11.7 %collective-permute-done.77 = bf16[2,2,192,608]{3,2,1,0:T(8,128)(2,1)S(1)} collective-permute-done((bf16[2,2,192,608]{3,2,1,0:T(8,128)(2,1)S(1)}, bf16[2,2,192,608]{3,2,1,0:T(8,128)(2,1)S(1)}, u32[]{:S(2)}, u32[]{:S(2)}) %collective-permute-start.77) | collective-permute-done | bytes 933920 | tf_op jit(solution)/shard_map/ppermute | solution.py:469
  871.9 17.1 %multiply_subtract_fusion = (f32[1120,1536]{1,0:T(8,128)}, f32[1120,1536]{1,0:T(8,128)}, f32[1120,1536]{1,0:T(8,128)}) fusion(f32[1120,1536]{1,0:T(8,128)} %param.30, bf16[1120,1536]{1,0:T(8,128)(2,1)} %all-gather.11.cloned.1.call-done, f32[]{:T(128)} %min.3, f32[1120,1536]{1,0:T(8,128)} %param.42, f32[1120,1536]{1,0:T(8,128)} %param.36), kind=kLoop, calls=%fused_computation.5 | loop fusion | flops 29245440 | bytes 44728324 | tf_op jit(solution)/shard_map/sub | solution.py:66
  894.4 17.5 %adam_columns.2 = (f32[192,8960]{1,0:T(8,128)}, f32[192,8960]{1,0:T(8,128)}, f32[192,8960]{1,0:T(8,128)}) custom-call(s32[2]{0:T(128)S(1)} %copy-done.7, f32[1]{0:T(128)} %bitcast.141.factor_ref, bf16[4,2,2,192,512]{4,3,2,1,0:T(8,128)(2,1)S(1)} %pad_maximum_fusion.5.first_ref, bf16[4,2,2,192,608]{4,3,2,1,0:T(8,128)(2,1)} %pad_maximum_fusion.2.second_ref, ...), custom_call_target="tpu_custom_call" | custom-call | flops 34406400 | bytes 44728320 | tf_op jit(solution)/shard_map/adam_columns/pallas_call | solution.py:150
  914.6 17.5 %adam_columns.3 = (f32[192,8960]{1,0:T(8,128)}, f32[192,8960]{1,0:T(8,128)}, f32[192,8960]{1,0:T(8,128)}) custom-call(s32[2]{0:T(128)S(1)} %copy-done.7, f32[1]{0:T(128)} %bitcast.141.factor_ref, bf16[4,2,2,192,512]{4,3,2,1,0:T(8,128)(2,1)S(1)} %pad_maximum_fusion.5.first_ref, bf16[4,2,2,192,608]{4,3,2,1,0:T(8,128)(2,1)} %pad_maximum_fusion.2.second_ref, ...), custom_call_target="tpu_custom_call" | custom-call | flops 34406400 | bytes 44728320 | tf_op jit(solution)/shard_map/adam_columns/pallas_call | solution.py:150
  (682 shorter events, 424.4 us)
Async XLA Ops:
  7.2 68.3 %all-gather.13.cloned.1.call-start = ((), (), s32[]{:S(2)}) async-start(), calls=%async_computation.7 | async-start | bytes 1843200 | tf_op jit(solution)/shard_map/all_gather | solution.py:595
  35.5 133.8 %all-gather.7.cloned.1.call-start = ((), (), s32[]{:S(2)}) async-start(), calls=%async_computation.2 | async-start | bytes 2359296 | tf_op jit(solution)/shard_map/all_gather | solution.py:595
  137.0 252.7 %all-gather.9.cloned.1.call-start = ((), (), s32[]{:S(2)}) async-start(), calls=%async_computation.3 | async-start | bytes 7077888 | tf_op jit(solution)/shard_map/all_gather | solution.py:795
  185.4 500.6 %reduce-scatter.5.cloned.1.call-start = ((), (), s32[]{:S(2)}) async-start(), calls=%async_computation.5 | async-start | bytes 1966080 | tf_op jit(solution)/shard_map/reduce_scatter | solution.py:807
  185.5 75.7 %collective-permute-start.11 = (bf16[256,1536]{1,0:T(8,128)(2,1)}, bf16[256,1536]{1,0:T(8,128)(2,1)}, u32[]{:S(2)}, u32[]{:S(2)}) collective-permute-start(bf16[256,1536]{1,0:T(8,128)(2,1)} %bitcast.48), channel_id=1, source_target_pairs={{0,2},{1,3},{2,0},{3,1},{4,6},{5,7},{6,4},{7,5},{8,10},{9,11},{10,... | collective-permute-start | bytes 2359304 | tf_op jit(solution)/shard_map/ppermute | solution.py:478
  205.1 56.0 %collective-permute-start.10 = (bf16[256,1536]{1,0:T(8,128)(2,1)}, bf16[256,1536]{1,0:T(8,128)(2,1)S(1)}, u32[]{:S(2)}, u32[]{:S(2)}) collective-permute-start(bf16[256,1536]{1,0:T(8,128)(2,1)} %bitcast.48), channel_id=1, source_target_pairs={{0,16},{16,0},{8,24},{24,8},{1,17},{17,1},{9,25},{25,9},{2,18},{18... | collective-permute-start | bytes 2359304 | tf_op jit(solution)/shard_map/ppermute | solution.py:469
  250.4 90.7 %collective-permute-start.16 = (bf16[2,2,192,608]{3,2,0,1:T(8,128)(2,1)S(1)}, bf16[2,2,192,608]{3,2,0,1:T(8,128)(2,1)S(1)}, u32[]{:S(2)}, u32[]{:S(2)}) collective-permute-start(bf16[2,2,192,608]{3,2,0,1:T(8,128)(2,1)S(1)} %pad_maximum_fusion.17), channel_id=1, source_target_pairs={{0,4},{1,5},{2,6},{3,7},{4,0},{5,1},{6,2},{7,3},{8,12},{9,13},{10,... | collective-permute-start | bytes 2801672 | tf_op jit(solution)/shard_map/ppermute | solution.py:478
  261.1 83.0 %collective-permute-start.19 = (bf16[2,2,192,512]{3,2,0,1:T(8,128)(2,1)}, bf16[2,2,192,512]{3,2,0,1:T(8,128)(2,1)}, u32[]{:S(2)}, u32[]{:S(2)}) collective-permute-start(bf16[2,2,192,512]{3,2,0,1:T(8,128)(2,1)} %pad_maximum_fusion.23), channel_id=1, source_target_pairs={{0,4},{1,5},{2,6},{3,7},{4,0},{5,1},{6,2},{7,3},{8,12},{9,13},{10,... | collective-permute-start | bytes 2359304 | tf_op jit(solution)/shard_map/ppermute | solution.py:478
  261.2 49.8 %collective-permute-start.12 = (bf16[128,1536]{1,0:T(8,128)(2,1)S(1)}, bf16[128,1536]{1,0:T(8,128)(2,1)S(1)}, u32[]{:S(2)}, u32[]{:S(2)}) collective-permute-start(bf16[128,1536]{1,0:T(8,128)(2,1)S(1)} %slice.489), channel_id=1, source_target_pairs={{0,2},{1,3},{2,0},{3,1},{4,6},{5,7},{6,4},{7,5},{8,10},{9,11},{10,... | collective-permute-start | bytes 1179656 | tf_op jit(solution)/shard_map/ppermute | solution.py:478
  264.8 46.3 %collective-permute-start.13 = (bf16[128,1536]{1,0:T(8,128)(2,1)S(1)}, bf16[128,1536]{1,0:T(8,128)(2,1)S(1)}, u32[]{:S(2)}, u32[]{:S(2)}) collective-permute-start(bf16[128,1536]{1,0:T(8,128)(2,1)S(1)} %slice.490), channel_id=1, source_target_pairs={{0,16},{16,0},{8,24},{24,8},{1,17},{17,1},{9,25},{25,9},{2,18},{18... | collective-permute-start | bytes 1179656 | tf_op jit(solution)/shard_map/ppermute | solution.py:469
  273.0 68.1 %collective-permute-start.14 = (bf16[152,1536]{1,0:T(8,128)(2,1)S(1)}, bf16[152,1536]{1,0:T(8,128)(2,1)S(1)}, u32[]{:S(2)}, u32[]{:S(2)}) collective-permute-start(bf16[152,1536]{1,0:T(8,128)(2,1)S(1)} %dynamic-slice_convert_fusion), channel_id=1, source_target_pairs={{0,4},{1,5},{2,6},{3,7},{4,0},{5,1},{6,2},{7,3},{8,12},{9,13},{10,... | collective-permute-start | bytes 1400840 | tf_op jit(solution)/shard_map/ppermute | solution.py:478
  353.2 72.9 %collective-permute-start.23 = (bf16[2,2,2,192,608]{4,3,0,2,1:T(8,128)(2,1)}, bf16[2,2,2,192,608]{4,3,0,2,1:T(8,128)(2,1)}, u32[]{:S(2)}, u32[]{:S(2)}) collective-permute-start(bf16[2,2,2,192,608]{4,3,0,2,1:T(8,128)(2,1)} %pad_maximum_fusion.7), channel_id=1, source_target_pairs={{0,1},{1,0},{2,3},{3,2},{4,5},{5,4},{6,7},{7,6},{8,9},{9,8},{10,11... | collective-permute-start | bytes 5603336 | tf_op jit(solution)/shard_map/ppermute | solution.py:478
  355.7 89.9 %collective-permute-start.24 = (bf16[2,152,1536]{2,1,0:T(8,128)(2,1)}, bf16[2,152,1536]{2,1,0:T(8,128)(2,1)}, u32[]{:S(2)}, u32[]{:S(2)}) collective-permute-start(bf16[2,152,1536]{2,1,0:T(8,128)(2,1)} %pad_maximum_fusion.19), channel_id=1, source_target_pairs={{0,1},{1,0},{2,3},{3,2},{4,5},{5,4},{6,7},{7,6},{8,9},{9,8},{10,11... | collective-permute-start | bytes 2801672 | tf_op jit(solution)/shard_map/ppermute | solution.py:478
  500.9 96.6 %collective-permute-start.35 = (bf16[2,2,2,192,512]{4,3,2,1,0:T(8,128)(2,1)}, bf16[2,2,2,192,512]{4,3,2,1,0:T(8,128)(2,1)}, u32[]{:S(2)}, u32[]{:S(2)}) collective-permute-start(bf16[2,2,2,192,512]{4,3,2,1,0:T(8,128)(2,1)} %get-tuple-element.258), channel_id=1, source_target_pairs={{0,1},{1,0},{2,3},{3,2},{4,5},{5,4},{6,7},{7,6},{8,9},{9,8},{10,11... | collective-permute-start | bytes 4718600 | tf_op jit(solution)/shard_map/ppermute | solution.py:478
  510.2 87.3 %collective-permute-start.37 = (bf16[2,152,1536]{2,1,0:T(8,128)(2,1)}, bf16[2,152,1536]{2,1,0:T(8,128)(2,1)}, u32[]{:S(2)}, u32[]{:S(2)}) collective-permute-start(bf16[2,152,1536]{2,1,0:T(8,128)(2,1)} %get-tuple-element.280), channel_id=1, source_target_pairs={{0,1},{1,0},{2,3},{3,2},{4,5},{5,4},{6,7},{7,6},{8,9},{9,8},{10,11... | collective-permute-start | bytes 2801672 | tf_op jit(solution)/shard_map/ppermute | solution.py:478
  518.1 238.1 %reduce-scatter.3.cloned.1.call-start = ((), (), s32[]{:S(2)}) async-start(), calls=%async_computation.4 | async-start | bytes 2359296 | tf_op jit(solution)/shard_map/reduce_scatter | solution.py:909
  549.5 139.6 %collective-permute-start.61 = (bf16[2,2,2,192,608]{4,3,2,1,0:T(8,128)(2,1)}, bf16[2,2,2,192,608]{4,3,2,1,0:T(8,128)(2,1)}, u32[]{:S(2)}, u32[]{:S(2)}) collective-permute-start(bf16[2,2,2,192,608]{4,3,2,1,0:T(8,128)(2,1)} %get-tuple-element.252), channel_id=1, source_target_pairs={{0,1},{1,0},{2,3},{3,2},{4,5},{5,4},{6,7},{7,6},{8,9},{9,8},{10,11... | collective-permute-start | bytes 5603336 | tf_op jit(solution)/shard_map/ppermute | solution.py:478
  566.0 123.1 %collective-permute-start.28 = (bf16[1024,1536]{1,0:T(8,128)(2,1)}, bf16[1024,1536]{1,0:T(8,128)(2,1)}, u32[]{:S(2)}, u32[]{:S(2)}) collective-permute-start(bf16[1024,1536]{1,0:T(8,128)(2,1)} %slice.604), channel_id=1, source_target_pairs={{0,8},{8,0},{16,24},{24,16},{1,9},{9,1},{17,25},{25,17},{2,10},{10... | collective-permute-start | bytes 9437192 | tf_op jit(solution)/shard_map/ppermute | solution.py:465
  597.6 274.3 %all-gather.11.cloned.1.call-start = ((), (), s32[]{:S(2)}) async-start(), calls=%async_computation.6 | async-start | bytes 4300800 | tf_op jit(solution)/shard_map/all_gather | solution.py:920
  613.0 104.2 %collective-permute-start.36 = (bf16[2,2,192,512]{3,2,1,0:T(8,128)(2,1)}, bf16[2,2,192,512]{3,2,1,0:T(8,128)(2,1)}, u32[]{:S(2)}, u32[]{:S(2)}) collective-permute-start(bf16[2,2,192,512]{3,2,1,0:T(8,128)(2,1)} %get-tuple-element.296), channel_id=1, source_target_pairs={{0,4},{1,5},{2,6},{3,7},{4,0},{5,1},{6,2},{7,3},{8,12},{9,13},{10,... | collective-permute-start | bytes 2359304 | tf_op jit(solution)/shard_map/ppermute | solution.py:478
  617.5 68.3 %collective-permute-start.38 = (bf16[152,1536]{1,0:T(8,128)(2,1)S(1)}, bf16[152,1536]{1,0:T(8,128)(2,1)S(1)}, u32[]{:S(2)}, u32[]{:S(2)}) collective-permute-start(bf16[152,1536]{1,0:T(8,128)(2,1)S(1)} %get-tuple-element.326), channel_id=1, source_target_pairs={{0,4},{1,5},{2,6},{3,7},{4,0},{5,1},{6,2},{7,3},{8,12},{9,13},{10,... | collective-permute-start | bytes 1400840 | tf_op jit(solution)/shard_map/ppermute | solution.py:478
  621.7 136.0 %collective-permute-start.47 = (bf16[2,2,192,384]{3,2,1,0:T(8,128)(2,1)}, bf16[2,2,192,384]{3,2,1,0:T(8,128)(2,1)S(1)}, u32[]{:S(2)}, u32[]{:S(2)}) collective-permute-start(bf16[2,2,192,384]{3,2,1,0:T(8,128)(2,1)} %get-tuple-element.306), channel_id=1, source_target_pairs={{0,1},{1,0},{2,3},{3,2},{4,5},{5,4},{6,7},{7,6},{8,9},{9,8},{10,11... | collective-permute-start | bytes 1769480 | tf_op jit(solution)/shard_map/ppermute | solution.py:478
  701.2 72.5 %collective-permute-start.62 = (bf16[2,2,192,608]{3,2,1,0:T(8,128)(2,1)}, bf16[2,2,192,608]{3,2,1,0:T(8,128)(2,1)}, u32[]{:S(2)}, u32[]{:S(2)}) collective-permute-start(bf16[2,2,192,608]{3,2,1,0:T(8,128)(2,1)} %get-tuple-element.276), channel_id=1, source_target_pairs={{0,4},{1,5},{2,6},{3,7},{4,0},{5,1},{6,2},{7,3},{8,12},{9,13},{10,... | collective-permute-start | bytes 2801672 | tf_op jit(solution)/shard_map/ppermute | solution.py:478
  844.5 44.5 %collective-permute-start.75 = (bf16[2,2,2,192,512]{4,3,2,1,0:T(8,128)(2,1)}, bf16[2,2,2,192,512]{4,3,2,1,0:T(8,128)(2,1)}, u32[]{:S(2)}, u32[]{:S(2)}) collective-permute-start(bf16[2,2,2,192,512]{4,3,2,1,0:T(8,128)(2,1)} %pad_maximum_fusion.15), channel_id=1, source_target_pairs={{0,8},{8,0},{16,24},{24,16},{1,9},{9,1},{17,25},{25,17},{2,10},{10... | collective-permute-start | bytes 4718600 | tf_op jit(solution)/shard_map/ppermute | solution.py:465
  (183 other events, 2192.1 us)
Sparse Core Ops, SparseCore 0:
  35.6 39.9 all-gather.12
  137.1 32.1 all-gather.6
  185.5 100.6 all-gather.8
  518.2 43.3 reduce-scatter.4
  597.7 73.7 reduce-scatter.2
  688.2 45.3 all-gather.10

commit v6 on v5

--- a/solution.py
+++ b/solution.py
@@ -32,6 +32,7 @@
 NEG_LARGE = -1e30
 LOG2E = 1.4426950408889634
 VMEM = 48 * 1024 * 1024
+SMALL_COST = pl.CostEstimate(flops=1000, bytes_accessed=1000, transcendentals=0)
 
 
 def norm_apply(values, gain):
@@ -107,7 +108,7 @@
         ),
         out_shape=[jax.ShapeDtypeStruct((2, 2, rows, w), jnp.bfloat16) for w in widths],
         compiler_params=pltpu.CompilerParams(vmem_limit_bytes=VMEM),
-        cost_estimate=pl.CostEstimate(flops=0, bytes_accessed=rows * FF * 10, transcendentals=0),
+        cost_estimate=SMALL_COST,
         name="pick_columns",
     )(ids, gate, up)
 
@@ -157,9 +158,7 @@
         ),
         out_shape=[shape] * 3,
         compiler_params=pltpu.CompilerParams(vmem_limit_bytes=VMEM),
-        cost_estimate=pl.CostEstimate(
-            flops=rows * FF * 20, bytes_accessed=rows * FF * 26, transcendentals=rows * FF
-        ),
+        cost_estimate=SMALL_COST,
         name="adam_columns",
     )(ids, factor, first, second, w, m, v)
 
@@ -179,6 +178,12 @@
     seg_key = seg_key_ref[pl.ds(first, chunk), :]
     counts = jnp.logical_and(key <= query, seg_key == seg_query_ref[0:1, :])
     return jnp.where(counts, 0.0, NEG_LARGE)
+
+def ring_pair(ref, c, at):
+    return jnp.concatenate(
+        [ref[c, :, at : at + HD], ref[ref.shape[0] - 1 - c, :, at : at + HD]], axis=0
+    )
+
 
 def attend_body(chunk, ids, q_ref, k_ref, v_ref, seg_key_ref, seg_query_ref, o_ref, lse_ref, m_s, l_s, acc_s):
     block_len = q_ref.shape[0]
@@ -195,8 +200,8 @@
         acc_s[...] = jnp.zeros_like(acc_s)
 
         def step(c, carry):
-            keys = k_ref[pl.ds(c * per, per), :, HD * kvh: HD * (kvh + 1)].reshape(chunk, HD)
-            vals = v_ref[pl.ds(c * per, per), :, HD * kvh: HD * (kvh + 1)].reshape(chunk, HD)
+            keys = ring_pair(k_ref, c, HD * kvh)
+            vals = ring_pair(v_ref, c, HD * kvh)
             bias = hidden_from(seg_key_ref, seg_query_ref, c * chunk, chunk, block_len, ids[0])
             s = nt(keys, q) * scale + jnp.concatenate([bias] * group, axis=1)
             old = m_s[0:1, :]
@@ -241,7 +246,7 @@
             jax.ShapeDtypeStruct((rows, KVH, 8, many), jnp.float32),
         ],
         compiler_params=pltpu.CompilerParams(vmem_limit_bytes=VMEM),
-        cost_estimate=pl.CostEstimate(flops=4 * rows * H * block_len * blk_count * block_len * HD, bytes_accessed=8 * 2**20, transcendentals=rows * H * block_len * blk_count * block_len),
+        cost_estimate=SMALL_COST,
         name="attend",
     )(ids, q, kv, kv, seg_key, seg_query)
 
@@ -270,8 +275,8 @@
         dq_s[...] = jnp.zeros_like(dq_s)
 
         def step(c, carry):
-            keys = k_ref[pl.ds(c * per, per), :, HD * kvh: HD * (kvh + 1)].reshape(chunk, HD)
-            vals = v_ref[pl.ds(c * per, per), :, HD * kvh: HD * (kvh + 1)].reshape(chunk, HD)
+            keys = ring_pair(k_ref, c, HD * kvh)
+            vals = ring_pair(v_ref, c, HD * kvh)
             bias = hidden_from(seg_key_ref, seg_query_ref, c * chunk, chunk, block_len, ids[0])
             s = nt(keys, q) * scale + jnp.concatenate([bias] * group, axis=1)
             p = jnp.exp2(s - lse)
@@ -279,8 +284,9 @@
             ds = (p * (dp - delta)).astype(jnp.bfloat16)
             dk = jnp.dot(ds, q, preferred_element_type=jnp.float32) * plain
             dv = jnp.dot(p.astype(jnp.bfloat16), do, preferred_element_type=jnp.float32)
-            dkv_ref[pl.ds(c * per, per), :, HD * kvh: HD * (kvh + 1)] = dk.astype(jnp.bfloat16).reshape(per, block_len, HD)
-            dkv_ref[pl.ds(c * per, per), :, KVD + HD * kvh: KVD + HD * (kvh + 1)] = dv.astype(jnp.bfloat16).reshape(per, block_len, HD)
+            for at, part in ((HD * kvh, dk.astype(jnp.bfloat16)), (KVD + HD * kvh, dv.astype(jnp.bfloat16))):
+                dkv_ref[c, :, at : at + HD] = part[:block_len]
+                dkv_ref[dkv_ref.shape[0] - 1 - c, :, at : at + HD] = part[block_len:]
             dq_s[...] += tn(ds, keys)
             return carry
 
@@ -319,7 +325,7 @@
             jax.ShapeDtypeStruct((blk_count, rows, block_len, 2 * KVD), jnp.bfloat16),
         ],
         compiler_params=pltpu.CompilerParams(vmem_limit_bytes=VMEM),
-        cost_estimate=pl.CostEstimate(flops=10 * rows * H * block_len * blk_count * block_len * HD, bytes_accessed=12 * 2**20, transcendentals=rows * H * block_len * blk_count * block_len),
+        cost_estimate=SMALL_COST,
         name="attend_back",
     )(ids, q, kv, kv, seg_key, seg_query, o, do, lse, cosine, sine)
 
@@ -375,9 +381,7 @@
         out_shape=[jax.ShapeDtypeStruct((count, wide_here), jnp.bfloat16)] * 3
         + [jax.ShapeDtypeStruct((count, D), jnp.bfloat16)],
         compiler_params=pltpu.CompilerParams(vmem_limit_bytes=VMEM),
-        cost_estimate=pl.CostEstimate(
-            flops=10 * count * D * wide_here, bytes_accessed=30 * 2**20, transcendentals=count * wide_here
-        ),
+        cost_estimate=SMALL_COST,
         name="middle",
     )(order, h, dy, gate_up, gate_up, wd, *extra)
 
@@ -399,9 +403,7 @@
         out_specs=pl.BlockSpec((2, step, wide_here), lambda i: (0, i, 0)),
         out_shape=jax.ShapeDtypeStruct((2, D, wide_here), jnp.bfloat16),
         compiler_params=pltpu.CompilerParams(vmem_limit_bytes=VMEM),
-        cost_estimate=pl.CostEstimate(
-            flops=4 * count * D * wide_here, bytes_accessed=20 * 2**20, transcendentals=0
-        ),
+        cost_estimate=SMALL_COST,
         name="two_grads",
     )(h, a, b)
 
@@ -417,7 +419,7 @@
         out_specs=pl.BlockSpec((F, step), lambda i: (0, i)),
         out_shape=jax.ShapeDtypeStruct((F, D), jnp.bfloat16),
         compiler_params=pltpu.CompilerParams(vmem_limit_bytes=VMEM),
-        cost_estimate=pl.CostEstimate(flops=2 * T * D * F, bytes_accessed=16 * 2**20, transcendentals=0),
+        cost_estimate=SMALL_COST,
         name="down_grad")(hid, dy)
 
 def down_body(hid_a_ref, hid_b_ref, wd_a_ref, wd_b_ref, o_ref):
@@ -441,9 +443,7 @@
         out_specs=pl.BlockSpec((step, D), lambda i: (i, 0)),
         out_shape=jax.ShapeDtypeStruct((count, D), jnp.bfloat16),
         compiler_params=pltpu.CompilerParams(vmem_limit_bytes=VMEM),
-        cost_estimate=pl.CostEstimate(
-            flops=2 * count * D * (hid_a.shape[1] + hid_b.shape[1]), bytes_accessed=16 * 2**20, transcendentals=0
-        ),
+        cost_estimate=SMALL_COST,
         name="down",
     )(hid_a, hid_b, wd_a, wd_b)
 
@@ -592,9 +592,13 @@
 
 def gather_ring(values):
     count = lax.axis_size("blk")
-    parts = lax.all_gather(values, ("grp", "blk"), axis=0, axis_index_groups=ring_groups(count))
-    ring = ring_order(count)
-    return [parts[ring.index(b)] for b in range(count)]
+    return lax.all_gather(values, ("grp", "blk"), axis=0, axis_index_groups=ring_groups(count))
+
+
+def exchange_near(parts):
+    cross = swap_cross(jnp.stack([parts[2], parts[3]]))
+    core = swap_core(jnp.stack([parts[1], cross[1]]))
+    return [parts[0], core[0], cross[0], core[1]]
 
 
 def on_device(
@@ -660,11 +664,13 @@
     small_count = small_params.shape[0]
     small_send = jnp.concatenate([low(small_params), low(segment_ids.reshape(token_count))])
     strip_wide = strip_q + HD
-    small_send = jnp.pad(small_send, (0, -small_send.shape[0] % strip_wide))
+    small_send = jnp.pad(small_send, (0, -small_send.shape[0] % (16 * strip_wide)))
     strip_local = jnp.concatenate([strip_local, small_send.reshape(-1, strip_wide)])
-    strip_list = gather_ring(strip_local)
-    strip = jnp.concatenate([part[:weight_rows] for part in strip_list])
-    small_all = jnp.stack([part[weight_rows:] for part in strip_list]).reshape(blk_count, -1)
+    ring = ring_order(blk_count)
+    strip_ring = gather_ring(strip_local)
+    strip = jnp.concatenate([strip_ring[ring.index(b), :weight_rows] for b in range(blk_count)])
+    small_all = jnp.stack([strip_ring[ring.index(b), weight_rows:] for b in range(blk_count)])
+    small_all = small_all.reshape(blk_count, -1)
     digits = low(jnp.stack([positions // 64, positions % 64], axis=1))
     digits = jnp.pad(digits, ((0, 0), (0, HD - 2)))
     token_send = jnp.concatenate([flat_low, digits], axis=1)
@@ -679,14 +685,27 @@
             [jnp.where(mine, other, values), jnp.where(mine, values, other)], axis=axis
         )
 
-    out_strip = low(lax.dynamic_slice_in_dim(w_out, strip_q * grp, strip_q, 1))
-    out_zero = swap_blk(out_strip, bits[0])
-    out_strip = place(out_strip, out_zero, [], bits[0])
-    out_one = swap_blk(out_strip, team)
-    out_strip = place(out_strip, out_one, [bits[0]], team)
+    mine_team = blk_bit(team)
+    (low_first, size_first), (low_second, size_second) = halves_of(quarter)
+
+    def team_pair(mine, got):
+        return jnp.stack(
+            [jnp.where(mine_team, got, mine), jnp.where(mine_team, mine, got)], axis=1
+        )
+
+    out_local = low(lax.dynamic_slice_in_dim(w_out, strip_q * grp, strip_q, 1))
+    out_ring = gather_ring(after(out_local, strip_ring))
+    picked_a, picked_b = pick_columns(ids, w_gate, w_up, blk_count)
+    got_a = swap_blk(picked_a[1], team)
+    down_here = low(lax.dynamic_slice_in_dim(w_down, quarter * grp, quarter, 0))
+    down_got = swap_blk(after(down_here, token_cross), bits[0])
+    down_here = place(down_here, down_got, [], bits[0])
+    pair_a = team_pair(picked_a[0], got_a)
     token_core = swap_core(jnp.stack([token_send, token_cross]))
     near_all = jnp.concatenate([token_send, token_core[0], token_cross, token_core[1]])
-    near_all = after(near_all, out_strip)
+    near_all = after(near_all, (pair_a, down_here, dy_cross, dy_over))
+    dy_first = swap_blk(dy_cross[:half], team)
+    dy_second = swap_cross(dy_over[half:])
     near_tokens = near_all[:, :D]
     near_positions = 64.0 * wide(near_all[:, D]) + wide(near_all[:, D + 1])
     vector = wide(small_all[:, :small_count].reshape(-1))
@@ -719,18 +738,14 @@
             mixed.reshape(4 * token_count, strip_heads + 1, HD), jnp.cos(angles), jnp.sin(angles)
         )
     ).reshape(4, token_count, strip_q + HD)
-    strips = by_place(
-        [
-            strip_out[0],
-            swap_core(strip_out[1]),
-            swap_cross(strip_out[2]),
-            swap_diag(strip_out[3]),
-        ]
-    )
+    strips = by_place(exchange_near(strip_out))
     query = jnp.concatenate([part[:, :strip_q] for part in strips], axis=1)
     key_value = jnp.concatenate([strips[k][:, strip_q:] for k in (0, 2, 1, 3)], axis=1)
     key_value = key_value.reshape(rows_here, block_len, 2 * KVD)
-    kv_all = jnp.stack(gather_ring(key_value))
+    key_value = after(key_value, (dy_first, dy_second))
+    kv_all = gather_ring(key_value)
+    dy_chip = jnp.concatenate([dy_low, dy_cross, dy_over, dy_first, dy_second])
+    dy_team = jnp.concatenate([dy_chip, swap_core(dy_chip)])
 
     teams = [
         [g * blk_count + (i | t) for g in range(4) for t in (0, team)]
@@ -744,48 +759,35 @@
         ]
     )
 
-    mine_team = blk_bit(team)
     peers = [[i for i in range(blk_count) if (i & team) == t] for t in (0, team)]
-    (low_first, size_first), (low_second, size_second) = halves_of(quarter)
-
-    def team_pair(mine, got):
-        return jnp.stack(
-            [jnp.where(mine_team, got, mine), jnp.where(mine_team, mine, got)], axis=1
-        )
-
-    def lows_of(values, done, anchor, lead=0):
+
+    def lows_of(values, done, lead=0, anchor=None):
         for bit in lows:
-            values = place(values, after(swap_blk(values, bit), anchor), done, bit, lead)
+            got = swap_blk(values, bit)
+            if anchor is not None:
+                got = after(got, anchor)
+            values = place(values, got, done, bit, lead)
             done = done + [bit]
         return values
 
-    picked_a, picked_b = pick_columns(ids, w_gate, w_up, blk_count)
-    got_a = swap_blk(after(picked_a[1], out_one), team)
+    pair_a_got = swap_blk(pair_a, bits[0])
+    down_here = lows_of(down_here, [bits[0]]).reshape(2 * blk_count // 4, quarter, D)
     got_b = swap_blk(after(picked_b[1], strip_out), team)
-    pair_a = after(team_pair(picked_a[0], after(got_a, strip_out)), key_value)
-    pair_a_got = swap_blk(pair_a, bits[0])
-
-    down_at = quarter * grp
-    down_a = low(lax.dynamic_slice_in_dim(w_down, down_at, size_first, 0))
-    down_got = swap_blk(after(down_a, out_zero), bits[0])
-    down_a = after(place(down_a, after(down_got, strip_out), [], bits[0]), key_value)
-    down_a = lows_of(down_a, [bits[0]], kv_all).reshape(widths[0], D)
-
-    out_strip = lows_of(out_strip, [bits[0], team], strip_out).reshape(HQD, strip_q)
-    out_cross = swap_cross(after(out_strip, key_value))
-    out_core = swap_core(jnp.stack([out_strip, out_cross]))
+    pair_a = place(pair_a, after(pair_a_got, key_value), [team], bits[0], 1)
+    pair_b = team_pair(picked_b[0], after(got_b, key_value))
+    kv_all = after(kv_all, (pair_a, pair_b, down_here, dy_team))
+
+    gate_up_a = lows_of(after(pair_a, kv_all), [bits[0], team], 1).reshape(2, D, -1)
+    pair_b = after(pair_b, kv_all)
+    pair_b_got = swap_blk(pair_b, bits[0])
+    down_a = down_here[:, :size_first].reshape(widths[0], D)
+    down_b = down_here[:, size_first:].reshape(widths[1], D)
+
+    out_ring = after(out_ring, key_value)
+    out_strip = jnp.concatenate([out_ring[ring.index(b)] for b in range(blk_count)])
+    out_cross = swap_cross(out_strip)
+    out_core = swap_core(jnp.stack([out_strip, after(out_cross, kv_all)]))
     out_full = jnp.concatenate(by_place([out_strip, out_core[0], out_cross, out_core[1]]), axis=1)
-    kv_all = after(kv_all, out_full)
-
-    pair_a = place(pair_a, after(pair_a_got, kv_all), [team], bits[0], 1)
-    gate_up_a = lows_of(pair_a, [bits[0], team], kv_all, 1).reshape(2, D, -1)
-    down_b = low(lax.dynamic_slice_in_dim(w_down, down_at + size_first, size_second, 0))
-    down_got_b = swap_blk(after(down_b, kv_all), bits[0])
-    pair_b = team_pair(picked_b[0], after(got_b, kv_all))
-    pair_b_got = swap_blk(pair_b, bits[0])
-    dy_cross, dy_over = after((dy_cross, dy_over), kv_all)
-    dy_first = swap_blk(dy_cross[:half], team)
-    dy_second = swap_cross(dy_over[half:])
 
     att_in, lse = attend(attend_ids, query, kv_all, seg_key, seg_query, block_len)
 
@@ -793,19 +795,14 @@
     resid = flat + jnp.dot(att_in, out_full, preferred_element_type=jnp.float32)
     h_two = low(norm_apply(resid, gain_two))
     h_team = lax.all_gather(h_two, ("grp", "blk"), axis=0, tiled=True, axis_index_groups=teams)
-    dy_first, dy_second, down_got_b, pair_b_got = after(
-        (dy_first, dy_second, down_got_b, pair_b_got), h_two
-    )
-    dy_chip = jnp.concatenate([dy_low, dy_cross, dy_over, dy_first, dy_second])
-    dy_team = jnp.concatenate([dy_chip, swap_core(dy_chip)])
-    down_b = place(down_b, down_got_b, [], bits[0])
+    pair_b_got = after(pair_b_got, (h_two, gate_up_a))
     pair_b = place(pair_b, pair_b_got, [team], bits[0], 1)
-    h_team = after(h_team, (dy_team, down_b, pair_b))
+    h_team = after(h_team, (gate_up_a, pair_b))
     hidden_a, d_gate_a, d_up_a, part_a = middle(order, h_team, dy_team, gate_up_a, down_a)
-    down_b = lows_of(down_b, [bits[0]], hidden_a).reshape(widths[1], D)
-    gate_up_b = lows_of(pair_b, [bits[0], team], hidden_a, 1).reshape(2, D, -1)
+    gate_up_b = lows_of(pair_b, [bits[0], team], 1, hidden_a).reshape(2, D, -1)
+    down_grad_a = down_grad(hidden_a, dy_team)
     down_share_a = lax.psum_scatter(
-        down_grad(hidden_a, dy_team), "blk", scatter_dimension=0, axis_index_groups=peers, tiled=True
+        down_grad_a, "blk", scatter_dimension=0, axis_index_groups=peers, tiled=True
     )
     column_grad_a = two_grads(h_team, d_gate_a, d_up_a)
 
@@ -822,11 +819,11 @@
         grad = grad.reshape((2, 2, 2) + low_shape + (weight_rows, -1))
         return part_sent(grad, 2 + len(lows), lows[-1])
 
-    def columns_second(keep, got):
+    def columns_mid(keep, got):
         values = part_sum(keep, got)
         for i in range(len(lows) - 2, -1, -1):
             values = part_sum(*part_sent(values, 3 + i, lows[i]))
-        return part_sent(values, 1, bits[0])
+        return values
 
     def columns_third(keep, got):
         values = part_sum(keep, got)
@@ -847,7 +844,7 @@
 
     first_a = columns_first(column_grad_a)
     hidden_b, d_gate_b, d_up_b, d_htwo_part = middle(
-        order, after(h_team, column_grad_a), dy_team, gate_up_b, down_b, part_a
+        order, after(h_team, (column_grad_a, down_grad_a)), dy_team, gate_up_b, down_b, part_a
     )
 
     def chip_sum(values, came):
@@ -876,17 +873,16 @@
     d_cross, d_over = scatter_near(d_chip, *d_far)
     out_part = down(*after((hidden_a, hidden_b), d_far), down_a, down_b, token_count)
     out_came = swap_core(out_part[chip_rows:])
+    mid_a = columns_mid(*after(first_a, out_part))
+    second_a = part_sent(mid_a, 1, bits[0])
     d_cross, d_over = after((d_cross, d_over), out_part)
     d_htwo = wide(d_chip[:token_count]) + wide(d_cross) + wide(d_over)
 
     norm_value_two, norm_back_two = jax.vjp(norm_apply, resid, gain_two)
     d_resid_norm, grad_gain_two = norm_back_two(d_htwo)
     d_resid = wide(dy_low) + d_resid_norm
-    d_att = low(d_resid)
-    second_a = columns_second(*after(first_a, d_att))
+    d_att = after(low(d_resid), down_share_a)
     rows_b = rows_second(*after(rows_b, d_att))
-    out_chip = chip_sum(out_part, after(out_came, d_att))
-    out_far = scatter_far(out_chip)
 
     d_attended = low(right_transposed(d_att, out_full))
     own_angles = angles_of(positions)
@@ -904,8 +900,6 @@
         jnp.concatenate([sine, sine], axis=1),
         block_len,
     )
-    second_b = columns_second(*after(first_b, d_query))
-    dkv = jnp.concatenate([dkv[b] for b in ring_order(blk_count)])
     dkv = lax.psum_scatter(
         dkv.reshape(blk_count * token_count, 2 * KVD),
         ("grp", "blk"),
@@ -913,50 +907,56 @@
         axis_index_groups=ring_groups(blk_count),
         tiled=True,
     )
+    down_share_b = part_sum(*after(rows_b, d_query))
     sum_a, third_a = columns_third(*after(second_a, d_query))
-    down_share_b = part_sum(*after(rows_b, d_query))
-    out_cross, out_over = scatter_near(out_chip, *after(out_far, d_query))
-    share_down = jnp.concatenate([down_share_a, down_share_b])
-    grad_down = lax.all_gather(share_down, "grp", axis=0, tiled=True)
+
     def to_strips(parts):
-        parts = by_place(parts)
-        return jnp.concatenate(
-            [parts[0], swap_core(parts[1]), swap_cross(parts[2]), swap_diag(parts[3])]
-        )
+        return jnp.concatenate(exchange_near(by_place(parts)))
 
     near_dq = to_strips([d_query[:, strip_q * k : strip_q * (k + 1)] for k in range(4)])
     block_shape = (2,) * len(bits) + (weight_rows, -1)
     query_grad = low(left_product(near_one, near_dq)).reshape(block_shape)
     steps_query = part_sent(query_grad, len(bits) - 1, bits[-1])
-    dkv = wide(after(dkv, (sum_a, share_down, query_grad))).reshape(token_count, 2, KVH, HD)
+    near_a = gather_near_stacked(columns_last(*after(third_a, d_query)))
+    dkv = wide(after(dkv, (query_grad, down_share_b))).reshape(token_count, 2, KVH, HD)
     d_key = low(rotate_by(dkv[:, 0], cosine[:, None], -sine[:, None]))
     d_value = low(dkv[:, 1])
     near_dkv = to_strips([(d_value if k % 2 else d_key)[:, k // 2] for k in range(4)])
+    near_dkv = after(near_dkv, near_a)
     kv_grad = low(left_product(near_one, near_dkv)).reshape(block_shape)
+    grad_bias = jnp.concatenate(
+        [
+            jnp.sum(wide(part), axis=0)
+            for part in (d_query, d_key.reshape(token_count, KVD), d_value.reshape(token_count, KVD))
+        ]
+    )
+    near_hone = right_transposed(near_dq, strip[:, :strip_q]) + right_transposed(
+        near_dkv, strip[:, strip_q:]
+    )
+    near_rms = lax.rsqrt(jnp.mean(near_wide * near_wide, axis=-1, keepdims=True) + NORM_EPS)
+    gain_one_part = jnp.sum(near_hone * near_wide * near_rms, axis=0)
+    vector_rows = -(-small_count // HD)
+    vector_term = jnp.concatenate([gain_one_part, grad_gain_two, grad_bias])
+    vector_term = vector_term.reshape(blk_count, small_count)
+    vector_term = jnp.pad(vector_term, ((0, 0), (0, vector_rows * HD - small_count)))
+    vector_term = low(vector_term).reshape((2,) * len(bits) + (vector_rows, HD))
+    kv_grad = jnp.concatenate([kv_grad, vector_term], axis=-2)
+    kv_pad = -kv_grad.shape[-2] % 16
+    kv_grad = jnp.pad(kv_grad, ((0, 0),) * (len(bits)) + ((0, kv_pad), (0, 0)))
     steps_kv = part_sent(kv_grad, len(bits) - 1, bits[-1])
-    sum_b, third_b = columns_third(*after(second_b, d_key))
-    near_a = gather_near_stacked(columns_last(*after(third_a, d_key)))
+    second_b = part_sent(columns_mid(*after(first_b, dkv)), 1, bits[0])
+    share_down = after(jnp.concatenate([down_share_a, down_share_b]), dkv)
+    grad_down = lax.all_gather(share_down, "grp", axis=0, tiled=True)
     for i in range(len(bits) - 2, -1, -1):
         steps_query = part_sent(part_sum(*after(steps_query, d_key)), i, bits[i])
         kv_sum = part_sum(*steps_kv)
         kv_grad = kv_sum
         steps_kv = part_sent(kv_sum, i, bits[i])
-    share_kv = part_sum(*steps_kv)
+    share_kv_all = wide(steps_kv[0]) + wide(steps_kv[1])
+    share_kv = low(share_kv_all[:weight_rows])
+    vector_part = share_kv_all[weight_rows : weight_rows + vector_rows]
+    sum_b, third_b = columns_third(*after(second_b, kv_grad))
     share_query = part_sum(*after(steps_query, kv_grad))
-    grad_bias = jnp.concatenate(
-        [
-            jnp.sum(wide(part), axis=0)
-            for part in (d_query, d_key.reshape(token_count, KVD), d_value.reshape(token_count, KVD))
-        ]
-    )
-    out_cross, out_over = after((out_cross, out_over), near_dkv)
-    out_tokens = low(resid + wide(out_chip[:token_count]) + wide(out_cross) + wide(out_over))
-    near_hone = right_transposed(near_dq, strip[:, :strip_q]) + right_transposed(
-        near_dkv, strip[:, strip_q:]
-    )
-    near_rms = lax.rsqrt(jnp.mean(near_wide * near_wide, axis=-1, keepdims=True) + NORM_EPS)
-    gain_one_part = jnp.sum(near_hone * near_wide * near_rms, axis=0)
-
     near_att = jnp.concatenate(gather_near(after(att_in, hidden_a)))
     near_datt = to_strips([d_att[:, strip_q * k : strip_q * (k + 1)] for k in range(4)])
     out_grad = low(left_product(near_att, after(near_datt, d_attended))).reshape(block_shape)
@@ -967,21 +967,7 @@
         steps_out = part_sent(part_sum(*after(steps_out, anchor)), i, bits[i])
     share_out = part_sum(*after(steps_out, kv_grad))
 
-    vector_term = jnp.concatenate([gain_one_part, grad_gain_two, grad_bias])
-    vector_term = vector_term + swap_cross(vector_term)
-    vector_term = vector_term + swap_core(vector_term)
-    vector_term = vector_term.reshape((2,) * len(bits) + (-1,))
-    axes = list(bits)
-    for bit in bits[::-1]:
-        axis = axes.index(bit)
-        mine = blk_bit(bit).astype(jnp.int32)
-        keep = lax.dynamic_index_in_dim(vector_term, mine, axis, keepdims=False)
-        send = lax.dynamic_index_in_dim(vector_term, 1 - mine, axis, keepdims=False)
-        vector_term = keep + swap_blk(send, bit)
-        axes.remove(bit)
-    share_vector = vector_term
-
-    near_b = gather_near_stacked(columns_last(*after(third_b, kv_grad)))
+    near_b = gather_near_stacked(columns_last(*third_b))
     grad_out = jnp.concatenate(gather_grp(share_out), axis=1)
     query_parts = gather_grp(share_query)
     key_parts = gather_grp(share_kv)
@@ -998,15 +984,19 @@
             wide(s)
             for s in (share_query, share_kv, share_out, sum_a, sum_b, share_down)
         ]
-    ) + 0.25 * jnp.sum(share_vector * share_vector)
-    square_sum = jnp.full((8, 128), square_sum)
+    )
+    packed = jnp.concatenate([vector_part, jnp.full((8, HD), square_sum)])
+    packed = packed + swap_cross(packed)
+    packed = packed + swap_core(packed)
+    share_vector = packed[:vector_rows].reshape(-1)[:small_count]
+    square_sum = packed[vector_rows:] + jnp.sum(share_vector * share_vector)
     for bit in bits:
         square_sum = square_sum + swap_blk(square_sum, bit)
-    square_sum = square_sum + swap_cross(square_sum)
-    square_sum = square_sum + swap_core(square_sum)
     grad_norm = jnp.sqrt(square_sum[0, 0])
     factor = jnp.minimum(1.0, CLIP_NORM / (grad_norm + 1e-06))
-    factor = after(factor, out_tokens)
+    out_chip = chip_sum(out_part, after(out_came, kv_grad))
+    out_far = scatter_far(out_chip)
+    factor = after(factor, out_chip)
 
     new_first_gate, new_second_gate, new_gate = adam_columns(
         0, ids, factor[None], near_a, near_b, w_gate, first_gate, second_gate, blk_count, RATE_GATE, WEIGHT_DECAY
@@ -1031,6 +1021,10 @@
     new_first_small, new_second_small, new_small = adam_step(
         small_params, factor * share_vector, first_small, second_small, RATE_VECTOR, 0.0
     )
+
+    out_far = after(out_far, new_down)
+    out_near = after(scatter_near(out_chip, *out_far), (new_gate, new_up))
+    out_tokens = low(resid + wide(out_chip[:token_count]) + wide(out_near[0]) + wide(out_near[1]))
     return (
         out_tokens.reshape(rows_here, block_len, D),
         grad_tokens.reshape(rows_here, block_len, D),

time: 954 us -> 870 us (0.912)
  waiting for transfers between devices: 399 us -> 286 us
  local copies, waits for them, and re-layouts: 99.4 us -> 132 us
  starting transfers between devices: 104 us -> 75.3 us
  other arithmetic: 133 us -> 159 us
    ppermute x21 -> x20, waiting for transfers between devices: 96.7 us -> 45.6 us  [swap_cross(): return lax.ppermute(values, 'grp', CROSS)]
    all_gather x2 -> x3, waiting for transfers between devices: 40 us -> 0.01 us  [gather_ring(): lax.all_gather(values, ('grp', 'blk'), axis=0, axis_index_groups=ring_gro...]
    ppermute x42 -> x34, waiting for transfers between devices: 254 us -> 231 us  [swap_blk(): return lax.ppermute(values, 'blk', [(i, i ^ bit) for i in range(count)])]
    ppermute x21 -> x20, starting transfers between devices: 34.4 us -> 20.9 us  [swap_cross(): return lax.ppermute(values, 'grp', CROSS)]
    ppermute x42 -> x34, starting transfers between devices: 65 us -> 52.5 us  [swap_blk(): return lax.ppermute(values, 'blk', [(i, i ^ bit) for i in range(count)])]
    another operation x4 -> x13, other arithmetic: 2.41 us -> 13.8 us  [the longest x1 1.67 us: on_device(): out_core = swap_core(jnp.stack([out_strip, out_cross]))]
    slice x1 -> x9, local copies, waits for them, and re-layouts: 0.1 us -> 11.2 us  [the longest x2 3.59 us: exchange_near(): cross = swap_cross(jnp.stack([parts[2], parts[3]]))]
    unnamed x272 -> x268, local copies, waits for them, and re-layouts: 42.2 us -> 50.4 us
  transfers between devices with their start and end apart: 91 -> 78, of which waited for: 38 -> 28; matrix products, arithmetic and copies ran while one was open for 23% -> 32% of each run, Pallas kernels for 15% -> 13%
where the time goes in v6:
time: 870 us; the launch traced here: 860 us
  waiting for transfers between devices  286 us (33%)
  Pallas kernels  161 us (19%)
  other arithmetic  159 us (18%)
  local copies, waits for them, and re-layouts  132 us (15%)
  starting transfers between devices  75.3 us (9%)
  matrix products  23.9 us (3%)
  between operations  22.1 us (3%)
    ppermute x34, waiting for transfers between devices, swap_blk(): return lax.ppermute(values, 'blk', [(i, i ^ bit) for i in range(count)])  231 us
    pallas_call x2, Pallas kernels, middle(): pl.pallas_call(functools.partial(middle_body, prev is not None), grid_spe...  60.7 us
    ppermute x34, starting transfers between devices, swap_blk(): return lax.ppermute(values, 'blk', [(i, i ^ bit) for i in range(count)])  52.5 us
    unnamed x268, local copies, waits for them, and re-layouts  50.4 us
    ppermute x20, waiting for transfers between devices, swap_cross(): return lax.ppermute(values, 'grp', CROSS)  45.6 us
    pallas_call x2, Pallas kernels, adam_columns(): pl.pallas_call(functools.partial(adam_body, blk_count, rate, decay), grid...  35.3 us
    convert_element_type x21, other arithmetic, low(): return values.astype(jnp.bfloat16)  30.3 us
    sub x4, other arithmetic, adam_step(): weight - rate * (first_hat / (jnp.sqrt(second_hat) + ADAM_EPS) + decay *...  23.7 us
  transfers between devices with their start and end apart: 78, of which 28 were waited for; matrix products, arithmetic and copies ran while one was open for 32% of the time, Pallas kernels for 13%

profile of v6, /device:TPU:0, one launch (start us, length us, event | category | flops | bytes accessed | tf_op | source)
XLA Modules:
  0.0 860.0 jit_solution(18164063207241776027)
XLA Ops:
  41.7 13.4 %collective-permute-done.2 = bf16[2,192,512]{2,1,0:T(8,128)(2,1)} collective-permute-done((bf16[2,192,512]{2,1,0:T(8,128)(2,1)}, bf16[2,192,512]{2,1,0:T(8,128)(2,1)}, u32[]{:S(2)}, u32[]{:S(2)}) %collective-permute-start.2) | collective-permute-done | bytes 393248 | tf_op jit(solution)/shard_map/ppermute | solution.py:478
  57.3 26.1 %collective-permute-done.3 = bf16[280,1536]{1,0:T(8,128)(2,1)} collective-permute-done((bf16[280,1536]{1,0:T(8,128)(2,1)}, bf16[280,1536]{1,0:T(8,128)(2,1)}, u32[]{:S(2)}, u32[]{:S(2)}) %collective-permute-start.3) | collective-permute-done | bytes 860192 | tf_op jit(solution)/shard_map/ppermute | solution.py:478
  187.8 20.4 %collective-permute-done.10 = bf16[2,2,192,512]{3,2,0,1:T(8,128)(2,1)} collective-permute-done((bf16[2,2,192,512]{3,2,0,1:T(8,128)(2,1)}, bf16[2,2,192,512]{3,2,0,1:T(8,128)(2,1)}, u32[]{:S(2)}, u32[]{:S(2)}) %collective-permute-start.10) | collective-permute-done | bytes 786464 | tf_op jit(solution)/shard_map/ppermute | solution.py:478
  236.9 32.9 %collective-permute-done.16 = bf16[2,2,2,192,512]{4,3,0,2,1:T(8,128)(2,1)S(1)} collective-permute-done((bf16[2,2,2,192,512]{4,3,0,2,1:T(8,128)(2,1)S(1)}, bf16[2,2,2,192,512]{4,3,0,2,1:T(8,128)(2,1)S(1)}, u32[]{:S(2)}, u32[]{:S(2)}) %collective-permute-start.16) | collective-permute-done | bytes 1572896 | tf_op jit(solution)/shard_map/ppermute | solution.py:478
  272.3 8.4 collective-permute-done.17
  289.0 8.6 %all-gather.9.cloned.1.call-done.h_ref = bf16[2048,1536]{1,0:T(8,128)(2,1)} async-done(((bf16[256,1536]{1,0:T(8,128)(2,1)}), bf16[2048,1536]{1,0:T(8,128)(2,1)}) %all-gather.9.cloned.1.call-update) | async-done | bytes 6291472 | tf_op jit(solution)/shard_map/all_gather | solution.py:797
  297.6 23.3 %middle.2 = (bf16[2048,512]{1,0:T(8,128)(2,1)S(1)}, bf16[2048,512]{1,0:T(8,128)(2,1)S(1)}, bf16[2048,512]{1,0:T(8,128)(2,1)}, bf16[2048,1536]{1,0:T(8,128)(2,1)}) custom-call(s32[8]{0:T(128)S(1)} %stack.289.order, bf16[2048,1536]{1,0:T(8,128)(2,1)} %all-gather.9.cloned.1.call-done.h_ref, bf16[2048,1536]{1,0:T(8,128)(2,1)} %constant_dynamic-update-slice_fusion.5.dy_ref, ...), custom_call_target="tpu_custom_call" | custom-call | flops 1000 | bytes 1000 | tf_op jit(solution)/shard_map/middle/pallas_call | solution.py:366
  337.3 10.0 %two_grads.2 = bf16[2,1536,512]{2,1,0:T(8,128)(2,1)} custom-call(bf16[2048,1536]{1,0:T(8,128)(2,1)} %all-gather.9.cloned.1.call-done.h_ref, bf16[2048,512]{1,0:T(8,128)(2,1)S(1)} %copy-done.16, bf16[2048,512]{1,0:T(8,128)(2,1)S(1)} %copy-done.17), custom_call_target="tpu_custom_call" | custom-call | flops 1000 | bytes 1000 | tf_op jit(solution)/shard_map/two_grads/pallas_call | solution.py:399
  347.4 37.4 %middle.3 = (bf16[2048,608]{1,0:T(8,128)(2,1)S(1)}, bf16[2048,608]{1,0:T(8,128)(2,1)}, bf16[2048,608]{1,0:T(8,128)(2,1)}, bf16[2048,1536]{1,0:T(8,128)(2,1)}) custom-call(s32[8]{0:T(128)S(1)} %stack.289.order, bf16[2048,1536]{1,0:T(8,128)(2,1)} %all-gather.9.cloned.1.call-done.h_ref, bf16[2048,1536]{1,0:T(8,128)(2,1)} %constant_dynamic-update-slice_fusion.5.dy_ref, ...), custom_call_target="tpu_custom_call" | custom-call | flops 1000 | bytes 1000 | tf_op jit(solution)/shard_map/middle/pallas_call | solution.py:366
  425.5 13.1 %two_grads.3 = bf16[2,1536,608]{2,1,0:T(8,128)(2,1)} custom-call(bf16[2048,1536]{1,0:T(8,128)(2,1)} %all-gather.9.cloned.1.call-done.h_ref, bf16[2048,608]{1,0:T(8,128)(2,1)S(1)} %copy-done.13, bf16[2048,608]{1,0:T(8,128)(2,1)S(1)} %copy-done.14), custom_call_target="tpu_custom_call" | custom-call | flops 1000 | bytes 1000 | tf_op jit(solution)/shard_map/two_grads/pallas_call | solution.py:399
  449.2 11.5 %down.1 = bf16[2048,1536]{1,0:T(8,128)(2,1)} custom-call(bf16[2048,512]{1,0:T(8,128)(2,1)S(1)} %copy-done.6, bf16[2048,608]{1,0:T(8,128)(2,1)} %copy-done.1, bf16[512,1536]{1,0:T(8,128)(2,1)S(1)} %bitcast.492, bf16[608,1536]{1,0:T(8,128)(2,1)S(1)} %bitcast.490), custom_call_target="tpu_custom_call" | custom-call | flops 1000 | bytes 1000 | tf_op jit(solution)/shard_map/down/pallas_call | solution.py:439
  464.6 21.2 %collective-permute-done.31 = bf16[2,2,2,192,512]{4,3,2,1,0:T(8,128)(2,1)} collective-permute-done((bf16[2,2,2,192,512]{4,3,2,1,0:T(8,128)(2,1)}, bf16[2,2,2,192,512]{4,3,2,1,0:T(8,128)(2,1)}, u32[]{:S(2)}, u32[]{:S(2)}) %collective-permute-start.31) | collective-permute-done | bytes 1572896 | tf_op jit(solution)/shard_map/ppermute | solution.py:478
  502.4 8.4 attend_back.1
  517.4 23.6 %collective-permute-done.32 = bf16[2,2,192,512]{3,2,1,0:T(8,128)(2,1)} collective-permute-done((bf16[2,2,192,512]{3,2,1,0:T(8,128)(2,1)}, bf16[2,2,192,512]{3,2,1,0:T(8,128)(2,1)}, u32[]{:S(2)}, u32[]{:S(2)}) %collective-permute-start.32) | collective-permute-done | bytes 786464 | tf_op jit(solution)/shard_map/ppermute | solution.py:478
  547.8 21.5 %collective-permute-done.33 = bf16[2,192,512]{2,1,0:T(8,128)(2,1)S(1)} collective-permute-done((bf16[2,192,512]{2,1,0:T(8,128)(2,1)S(1)}, bf16[2,192,512]{2,1,0:T(8,128)(2,1)S(1)}, u32[]{:S(2)}, u32[]{:S(2)}) %collective-permute-start.33) | collective-permute-done | bytes 393248 | tf_op jit(solution)/shard_map/ppermute | solution.py:478
  576.7 13.9 %collective-permute-done.34 = bf16[2,2,192,512]{3,2,1,0:T(8,128)(2,1)S(1)} collective-permute-done((bf16[2,2,192,512]{3,2,1,0:T(8,128)(2,1)}, bf16[2,2,192,512]{3,2,1,0:T(8,128)(2,1)S(1)}, u32[]{:S(2)}, u32[]{:S(2)}) %collective-permute-start.34) | collective-permute-done | bytes 786464 | tf_op jit(solution)/shard_map/ppermute | solution.py:469
  600.6 9.8 %collective-permute-done.48 = bf16[2,2,192,384]{3,2,1,0:T(8,128)(2,1)S(1)} collective-permute-done((bf16[2,2,192,384]{3,2,1,0:T(8,128)(2,1)S(1)}, bf16[2,2,192,384]{3,2,1,0:T(8,128)(2,1)S(1)}, u32[]{:S(2)}, u32[]{:S(2)}) %collective-permute-start.48) | collective-permute-done | bytes 589856 | tf_op jit(solution)/shard_map/ppermute | solution.py:478
  656.0 16.9 %collective-permute-done.37 = bf16[2,208,128]{2,1,0:T(8,128)(2,1)S(1)} collective-permute-done((bf16[2,208,128]{2,1,0:T(8,128)(2,1)S(1)}, bf16[2,208,128]{2,1,0:T(8,128)(2,1)S(1)}, u32[]{:S(2)}, u32[]{:S(2)}) %collective-permute-start.37) | collective-permute-done | bytes 106528 | tf_op jit(solution)/shard_map/ppermute | solution.py:478
  728.9 8.4 collective-permute-done.60
  739.8 21.2 %collective-permute-done.61 = bf16[2,2,192,608]{3,2,1,0:T(8,128)(2,1)S(1)} collective-permute-done((bf16[2,2,192,608]{3,2,1,0:T(8,128)(2,1)S(1)}, bf16[2,2,192,608]{3,2,1,0:T(8,128)(2,1)S(1)}, u32[]{:S(2)}, u32[]{:S(2)}) %collective-permute-start.61) | collective-permute-done | bytes 933920 | tf_op jit(solution)/shard_map/ppermute | solution.py:469
  773.3 17.5 %adam_columns.2 = (f32[192,8960]{1,0:T(8,128)}, f32[192,8960]{1,0:T(8,128)}, f32[192,8960]{1,0:T(8,128)}) custom-call(s32[2]{0:T(128)S(1)} %copy-done.21, f32[1]{0:T(128)} %bitcast.156.factor_ref, bf16[4,2,2,192,512]{4,3,2,1,0:T(8,128)(2,1)S(1)} %pad_maximum_fusion.6.first_ref, bf16[4,2,2,192,608]{4,3,2,1,0:T(8,128)(2,1)} %pad_maximum_fusion.2.second_ref, ...), custom_call_target="tpu_custom_call" | custom-call | flops 1000 | bytes 1000 | tf_op jit(solution)/shard_map/adam_columns/pallas_call | solution.py:151
  790.9 17.7 %adam_columns.3 = (f32[192,8960]{1,0:T(8,128)}, f32[192,8960]{1,0:T(8,128)}, f32[192,8960]{1,0:T(8,128)}) custom-call(s32[2]{0:T(128)S(1)} %copy-done.21, f32[1]{0:T(128)} %bitcast.156.factor_ref, bf16[4,2,2,192,512]{4,3,2,1,0:T(8,128)(2,1)S(1)} %pad_maximum_fusion.6.first_ref, bf16[4,2,2,192,608]{4,3,2,1,0:T(8,128)(2,1)} %pad_maximum_fusion.2.second_ref, ...), custom_call_target="tpu_custom_call" | custom-call | flops 1000 | bytes 1000 | tf_op jit(solution)/shard_map/adam_columns/pallas_call | solution.py:151
  810.6 16.9 %multiply_subtract_fusion = (f32[1120,1536]{1,0:T(8,128)}, f32[1120,1536]{1,0:T(8,128)}, f32[1120,1536]{1,0:T(8,128)}) fusion(f32[1120,1536]{1,0:T(8,128)} %param.30, bf16[1120,1536]{1,0:T(8,128)(2,1)} %all-gather.11.cloned.1.call-done, f32[]{:T(128)} %min.3, f32[1120,1536]{1,0:T(8,128)} %param.36, f32[1120,1536]{1,0:T(8,128)} %param.42), kind=kLoop, calls=%fused_computation.5 | loop fusion | flops 29245440 | bytes 44728324 | tf_op jit(solution)/shard_map/sub | solution.py:67
  833.1 15.8 %collective-permute-done.59 = bf16[256,1536]{1,0:T(8,128)(2,1)S(1)} collective-permute-done((bf16[256,1536]{1,0:T(8,128)(2,1)S(1)}, bf16[256,1536]{1,0:T(8,128)(2,1)S(1)}, u32[]{:S(2)}, u32[]{:S(2)}) %collective-permute-start.59) | collective-permute-done | bytes 786464 | tf_op jit(solution)/shard_map/ppermute | solution.py:478
  (652 shorter events, 419.9 us)
Async XLA Ops:
  7.2 91.5 %all-gather.13.cloned.1.call-start = ((), (), s32[]{:S(2)}) async-start(), calls=%async_computation.6 | async-start | bytes 1916928 | tf_op jit(solution)/shard_map/all_gather | solution.py:595
  15.9 154.6 %all-gather.17.cloned.1.call-start = ((), (), s32[]{:S(2)}) async-start(), calls=%async_computation.8 | async-start | bytes 1327104 | tf_op jit(solution)/shard_map/all_gather | solution.py:595
  24.8 70.8 %collective-permute-start.5 = (bf16[256,1536]{1,0:T(8,128)(2,1)}, bf16[256,1536]{1,0:T(8,128)(2,1)}, u32[]{:S(2)}, u32[]{:S(2)}) collective-permute-start(bf16[256,1536]{1,0:T(8,128)(2,1)} %bitcast.19), channel_id=1, source_target_pairs={{0,2},{1,3},{2,0},{3,1},{4,6},{5,7},{6,4},{7,5},{8,10},{9,11},{10,... | collective-permute-start | bytes 2359304 | tf_op jit(solution)/shard_map/ppermute | solution.py:478
  32.4 51.0 %collective-permute-start.3 = (bf16[280,1536]{1,0:T(8,128)(2,1)}, bf16[280,1536]{1,0:T(8,128)(2,1)}, u32[]{:S(2)}, u32[]{:S(2)}) collective-permute-start(bf16[280,1536]{1,0:T(8,128)(2,1)} %dynamic-slice_convert_fusion), channel_id=1, source_target_pairs={{0,4},{1,5},{2,6},{3,7},{4,0},{5,1},{6,2},{7,3},{8,12},{9,13},{10,... | collective-permute-start | bytes 2580488 | tf_op jit(solution)/shard_map/ppermute | solution.py:478
  36.6 51.7 %collective-permute-start.1 = (bf16[2,256,1664]{2,1,0:T(8,128)(2,1)}, bf16[2,256,1664]{2,1,0:T(8,128)(2,1)}, u32[]{:S(2)}, u32[]{:S(2)}) collective-permute-start(bf16[2,256,1664]{2,1,0:T(8,128)(2,1)} %pad_maximum_fusion.11), channel_id=1, source_target_pairs={{0,8},{8,0},{16,24},{24,16},{1,9},{9,1},{17,25},{25,17},{2,10},{10... | collective-permute-start | bytes 5111816 | tf_op jit(solution)/shard_map/ppermute | solution.py:465
  37.4 150.4 %collective-permute-start.11 = (bf16[2,192,608]{2,1,0:T(8,128)(2,1)}, bf16[2,192,608]{2,1,0:T(8,128)(2,1)}, u32[]{:S(2)}, u32[]{:S(2)}) collective-permute-start(bf16[2,192,608]{2,1,0:T(8,128)(2,1)} %slice_bitcast_fusion.6), channel_id=1, source_target_pairs={{0,2},{1,3},{2,0},{3,1},{4,6},{5,7},{6,4},{7,5},{8,10},{9,11},{10,... | collective-permute-start | bytes 1400840 | tf_op jit(solution)/shard_map/ppermute | solution.py:478
  86.7 80.4 %collective-permute-start.12 = (bf16[2,280,1536]{2,1,0:T(8,128)(2,1)}, bf16[2,280,1536]{2,1,0:T(8,128)(2,1)}, u32[]{:S(2)}, u32[]{:S(2)}) collective-permute-start(bf16[2,280,1536]{2,1,0:T(8,128)(2,1)} %pad_maximum_fusion.10), channel_id=1, source_target_pairs={{0,1},{1,0},{2,3},{3,2},{4,5},{5,4},{6,7},{7,6},{8,9},{9,8},{10,11... | collective-permute-start | bytes 5160968 | tf_op jit(solution)/shard_map/ppermute | solution.py:478
  119.2 96.4 %all-gather.15.cloned.1.call-start = ((), (), s32[]{:S(2)}) async-start(), calls=%async_computation.7 | async-start | bytes 2359296 | tf_op jit(solution)/shard_map/all_gather | solution.py:595
  155.1 53.1 %collective-permute-start.10 = (bf16[2,2,192,512]{3,2,0,1:T(8,128)(2,1)}, bf16[2,2,192,512]{3,2,0,1:T(8,128)(2,1)}, u32[]{:S(2)}, u32[]{:S(2)}) collective-permute-start(bf16[2,2,192,512]{3,2,0,1:T(8,128)(2,1)} %pad_maximum_fusion.22), channel_id=1, source_target_pairs={{0,4},{1,5},{2,6},{3,7},{4,0},{5,1},{6,2},{7,3},{8,12},{9,13},{10,... | collective-permute-start | bytes 2359304 | tf_op jit(solution)/shard_map/ppermute | solution.py:478
  167.1 130.6 %all-gather.9.cloned.1.call-start = ((), (), s32[]{:S(2)}) async-start(), calls=%async_computation.2 | async-start | bytes 7077888 | tf_op jit(solution)/shard_map/all_gather | solution.py:797
  232.5 263.6 %reduce-scatter.3.cloned.1.call-start = ((), (), s32[]{:S(2)}) async-start(), calls=%async_computation.3 | async-start | bytes 1966080 | tf_op jit(solution)/shard_map/reduce_scatter | solution.py:804
  402.3 209.3 %reduce-scatter.5.cloned.1.call-start = ((), (), s32[]{:S(2)}) async-start(), calls=%async_computation.4 | async-start | bytes 2359296 | tf_op jit(solution)/shard_map/reduce_scatter | solution.py:903
  420.3 75.8 %collective-permute-start.27 = (bf16[2,152,1536]{2,1,0:T(8,128)(2,1)}, bf16[2,152,1536]{2,1,0:T(8,128)(2,1)}, u32[]{:S(2)}, u32[]{:S(2)}) collective-permute-start(bf16[2,152,1536]{2,1,0:T(8,128)(2,1)} %get-tuple-element.258), channel_id=1, source_target_pairs={{0,1},{1,0},{2,3},{3,2},{4,5},{5,4},{6,7},{7,6},{8,9},{9,8},{10,11... | collective-permute-start | bytes 2801672 | tf_op jit(solution)/shard_map/ppermute | solution.py:478
  423.6 62.1 %collective-permute-start.31 = (bf16[2,2,2,192,512]{4,3,2,1,0:T(8,128)(2,1)}, bf16[2,2,2,192,512]{4,3,2,1,0:T(8,128)(2,1)}, u32[]{:S(2)}, u32[]{:S(2)}) collective-permute-start(bf16[2,2,2,192,512]{4,3,2,1,0:T(8,128)(2,1)} %get-tuple-element.242), channel_id=1, source_target_pairs={{0,1},{1,0},{2,3},{3,2},{4,5},{5,4},{6,7},{7,6},{8,9},{9,8},{10,11... | collective-permute-start | bytes 4718600 | tf_op jit(solution)/shard_map/ppermute | solution.py:478
  439.9 52.3 %collective-permute-start.24 = (bf16[256,1536]{1,0:T(8,128)(2,1)S(1)}, bf16[256,1536]{1,0:T(8,128)(2,1)S(1)}, u32[]{:S(2)}, u32[]{:S(2)}) collective-permute-start(bf16[256,1536]{1,0:T(8,128)(2,1)S(1)} %pad_maximum_fusion.25), channel_id=1, source_target_pairs={{0,2},{1,3},{2,0},{3,1},{4,6},{5,7},{6,4},{7,5},{8,10},{9,11},{10,... | collective-permute-start | bytes 2359304 | tf_op jit(solution)/shard_map/ppermute | solution.py:478
  448.0 164.8 %collective-permute-start.51 = (bf16[2,2,2,192,608]{4,3,2,1,0:T(8,128)(2,1)}, bf16[2,2,2,192,608]{4,3,2,1,0:T(8,128)(2,1)}, u32[]{:S(2)}, u32[]{:S(2)}) collective-permute-start(bf16[2,2,2,192,608]{4,3,2,1,0:T(8,128)(2,1)} %get-tuple-element.228), channel_id=1, source_target_pairs={{0,1},{1,0},{2,3},{3,2},{4,5},{5,4},{6,7},{7,6},{8,9},{9,8},{10,11... | collective-permute-start | bytes 5603336 | tf_op jit(solution)/shard_map/ppermute | solution.py:478
  488.7 52.4 %collective-permute-start.32 = (bf16[2,2,192,512]{3,2,1,0:T(8,128)(2,1)}, bf16[2,2,192,512]{3,2,1,0:T(8,128)(2,1)}, u32[]{:S(2)}, u32[]{:S(2)}) collective-permute-start(bf16[2,2,192,512]{3,2,1,0:T(8,128)(2,1)} %get-tuple-element.272), channel_id=1, source_target_pairs={{0,4},{1,5},{2,6},{3,7},{4,0},{5,1},{6,2},{7,3},{8,12},{9,13},{10,... | collective-permute-start | bytes 2359304 | tf_op jit(solution)/shard_map/ppermute | solution.py:478
  492.2 183.8 %collective-permute-start.22 = (bf16[1024,1536]{1,0:T(8,128)(2,1)}, bf16[1024,1536]{1,0:T(8,128)(2,1)}, u32[]{:S(2)}, u32[]{:S(2)}) collective-permute-start(bf16[1024,1536]{1,0:T(8,128)(2,1)} %slice.608), channel_id=1, source_target_pairs={{0,8},{8,0},{16,24},{24,16},{1,9},{9,1},{17,25},{25,17},{2,10},{10... | collective-permute-start | bytes 9437192 | tf_op jit(solution)/shard_map/ppermute | solution.py:465
  498.8 73.5 %collective-permute-start.28 = (bf16[152,1536]{1,0:T(8,128)(2,1)}, bf16[152,1536]{1,0:T(8,128)(2,1)}, u32[]{:S(2)}, u32[]{:S(2)}) collective-permute-start(bf16[152,1536]{1,0:T(8,128)(2,1)} %get-tuple-element.296), channel_id=1, source_target_pairs={{0,4},{1,5},{2,6},{3,7},{4,0},{5,1},{6,2},{7,3},{8,12},{9,13},{10,... | collective-permute-start | bytes 1400840 | tf_op jit(solution)/shard_map/ppermute | solution.py:478
  517.4 293.2 %all-gather.11.cloned.1.call-start = ((), (), s32[]{:S(2)}) async-start(), calls=%async_computation.5 | async-start | bytes 4300800 | tf_op jit(solution)/shard_map/all_gather | solution.py:949
  616.9 75.1 %collective-permute-start.52 = (bf16[2,2,192,608]{3,2,1,0:T(8,128)(2,1)}, bf16[2,2,192,608]{3,2,1,0:T(8,128)(2,1)}, u32[]{:S(2)}, u32[]{:S(2)}) collective-permute-start(bf16[2,2,192,608]{3,2,1,0:T(8,128)(2,1)} %get-tuple-element.254), channel_id=1, source_target_pairs={{0,4},{1,5},{2,6},{3,7},{4,0},{5,1},{6,2},{7,3},{8,12},{9,13},{10,... | collective-permute-start | bytes 2801672 | tf_op jit(solution)/shard_map/ppermute | solution.py:478
  652.3 112.2 %collective-permute-start.63 = (bf16[512,1536]{1,0:T(8,128)(2,1)}, bf16[512,1536]{1,0:T(8,128)(2,1)}, u32[]{:S(2)}, u32[]{:S(2)}) collective-permute-start(bf16[512,1536]{1,0:T(8,128)(2,1)} %pad_maximum_fusion.15), channel_id=1, source_target_pairs={{0,8},{8,0},{16,24},{24,16},{1,9},{9,1},{17,25},{25,17},{2,10},{10... | collective-permute-start | bytes 4718600 | tf_op jit(solution)/shard_map/ppermute | solution.py:465
  699.9 127.6 %collective-permute-start.38 = (bf16[128,1536]{1,0:T(8,128)(2,1)}, bf16[128,1536]{1,0:T(8,128)(2,1)}, u32[]{:S(2)}, u32[]{:S(2)}) collective-permute-start(bf16[128,1536]{1,0:T(8,128)(2,1)} %get-tuple-element.239), channel_id=1, source_target_pairs={{0,2},{1,3},{2,0},{3,1},{4,6},{5,7},{6,4},{7,5},{8,10},{9,11},{10,... | collective-permute-start | bytes 1179656 | tf_op jit(solution)/shard_map/ppermute | solution.py:478
  719.6 107.8 %collective-permute-start.39 = (bf16[128,1536]{1,0:T(8,128)(2,1)}, bf16[128,1536]{1,0:T(8,128)(2,1)}, u32[]{:S(2)}, u32[]{:S(2)}) collective-permute-start(bf16[128,1536]{1,0:T(8,128)(2,1)} %get-tuple-element.238), channel_id=1, source_target_pairs={{0,16},{16,0},{8,24},{24,8},{1,17},{17,1},{9,25},{25,9},{2,18},{18... | collective-permute-start | bytes 1179656 | tf_op jit(solution)/shard_map/ppermute | solution.py:469
  (173 other events, 2098.8 us)
Sparse Core Ops, SparseCore 0:
  16.1 58.3 all-gather.12
  119.4 32.0 all-gather.16
  167.2 46.6 all-gather.14
  232.6 64.9 all-gather.8
  402.5 48.0 reduce-scatter.2
  517.5 57.2 reduce-scatter.4
  629.2 30.4 all-gather.10

commit v7 on v6

--- a/solution.py
+++ b/solution.py
@@ -66,6 +66,10 @@
     second_hat = second_new / (1.0 - BETA_SECOND**STEP)
     weight_new = weight - rate * (first_hat / (jnp.sqrt(second_hat) + ADAM_EPS) + decay * weight)
     return (first_new, second_new, weight_new)
+
+
+def ring_order(count):
+    return list(range(0, count, 2)) + list(range(count - 1, 0, -2))
 
 
 def halves_of(quarter):
@@ -448,6 +452,219 @@
     )(hid_a, hid_b, wd_a, wd_b)
 
 
+def turn(u, cosine, sine):
+    lane = lax.broadcasted_iota(jnp.int32, u.shape, 1)
+    other = pltpu.roll(u, HD // 2, 1)
+    return u * cosine + jnp.where(lane < HD // 2, -other, other) * sine
+
+
+def mix_body(
+    blk_count, rows, small_count, ids, own_ref, cross_ref, core_ref, ring_ref, freq_ref,
+    self_ref, near_ref, far_ref, one_ref, strip_ref, vector_ref,
+):
+    ring = ring_order(blk_count)
+    wide_here = ring_ref.shape[-1]
+    pieces = []
+    for b in range(blk_count):
+        at = ring.index(b)
+        strip_ref[rows * b : rows * (b + 1)] = ring_ref[at, :rows]
+        left = small_count
+        line = rows
+        while left > 0:
+            size = min(left, wide_here)
+            pieces.append(ring_ref[at, line : line + 1, :size].astype(jnp.float32))
+            left -= size
+            line += 1
+    vector = jnp.concatenate(pieces, axis=1)
+    vector_ref[...] = vector
+    gain = vector[:, :D]
+    grp = ids[0]
+    strip_q = wide_here - HD
+    bias = jnp.zeros((1, wide_here), jnp.float32)
+    for k in range(4):
+        kv_at = 2 * D + HQD + HD * (k // 2) + KVD * (k % 2)
+        part = jnp.concatenate(
+            [
+                vector[:, 2 * D + strip_q * k : 2 * D + strip_q * (k + 1)],
+                vector[:, kv_at : kv_at + HD],
+            ],
+            axis=1,
+        )
+        bias = bias + jnp.where(grp == k, part, 0.0)
+    count = own_ref.shape[0]
+    strip = strip_ref[...]
+    for d in range(4):
+        source = (own_ref[...], core_ref[0], cross_ref[...], core_ref[1])[d]
+        x = source[:, :D].astype(jnp.float32)
+        root = lax.rsqrt(jnp.mean(x * x, axis=1, keepdims=True) + NORM_EPS)
+        one = (x * root * gain).astype(jnp.bfloat16)
+        one_ref[count * d : count * (d + 1)] = one
+        mixed = nn(one, strip) + bias
+        digits = source[:, D : D + HD].astype(jnp.float32)
+        position = 64.0 * digits[:, 0:1] + digits[:, 1:2]
+        angles = position * freq_ref[...]
+        cosine, sine = jnp.cos(angles), jnp.sin(angles)
+        for i in range(wide_here // HD):
+            c, s = cosine, sine
+            if i == wide_here // HD - 1:
+                c = jnp.where(grp % 2 == 1, 1.0, c)
+                s = jnp.where(grp % 2 == 1, 0.0, s)
+            at = HD * i
+            out = turn(mixed[:, at : at + HD], c, s).astype(jnp.bfloat16)
+            if d == 0:
+                self_ref[:, at : at + HD] = out
+            elif d == 1:
+                near_ref[:, at : at + HD] = out
+            else:
+                far_ref[d - 2, :, at : at + HD] = out
+
+
+def mix(ids, own, cross, core, ring, freq, blk_count, rows, small_count):
+    count = own.shape[0]
+    wide_here = ring.shape[-1]
+    low16 = jnp.bfloat16
+    return pl.pallas_call(
+        functools.partial(mix_body, blk_count, rows, small_count),
+        in_specs=[pl.BlockSpec(memory_space=pltpu.SMEM)] + [pl.BlockSpec(memory_space=pltpu.VMEM)] * 5,
+        out_specs=[pl.BlockSpec(memory_space=pltpu.VMEM)] * 6,
+        out_shape=[
+            jax.ShapeDtypeStruct((count, wide_here), low16),
+            jax.ShapeDtypeStruct((count, wide_here), low16),
+            jax.ShapeDtypeStruct((2, count, wide_here), low16),
+            jax.ShapeDtypeStruct((4 * count, D), low16),
+            jax.ShapeDtypeStruct((D, wide_here), low16),
+            jax.ShapeDtypeStruct((1, blk_count * small_count), jnp.float32),
+        ],
+        compiler_params=pltpu.CompilerParams(vmem_limit_bytes=VMEM),
+        cost_estimate=SMALL_COST,
+        name="mix",
+    )(ids, own, cross, core, ring, freq)
+
+
+def pack_body(ids, self_ref, cross_ref, core_ref, q_ref, kv_ref):
+    strip_q = self_ref.shape[1] - HD
+    for g in range(4):
+
+        @pl.when(ids[0] == g)
+        def _(g=g):
+            for k in range(4):
+                part = (self_ref[...], core_ref[0], cross_ref[0], core_ref[1])[g ^ k]
+                q_ref[:, strip_q * k : strip_q * (k + 1)] = part[:, :strip_q]
+                at = (k % 2) * KVD + (k // 2) * HD
+                kv_ref[:, at : at + HD] = part[:, strip_q:]
+
+
+def pack(ids, own, cross, core):
+    count = own.shape[0]
+    return pl.pallas_call(
+        pack_body,
+        in_specs=[pl.BlockSpec(memory_space=pltpu.SMEM)] + [pl.BlockSpec(memory_space=pltpu.VMEM)] * 3,
+        out_specs=[pl.BlockSpec(memory_space=pltpu.VMEM)] * 2,
+        out_shape=[
+            jax.ShapeDtypeStruct((count, HQD), jnp.bfloat16),
+            jax.ShapeDtypeStruct((count, 2 * KVD), jnp.bfloat16),
+        ],
+        compiler_params=pltpu.CompilerParams(vmem_limit_bytes=VMEM),
+        cost_estimate=SMALL_COST,
+        name="pack",
+    )(ids, own, cross, core)
+
+
+def turn_dkv_body(ids, dkv_ref, cos_ref, sin_ref, self_ref, near_ref, far_ref, sum_ref):
+    items = []
+    sums = [None] * 4
+    for k in range(4):
+        at = (k % 2) * KVD + (k // 2) * HD
+        part = dkv_ref[:, at : at + HD]
+        if k % 2 == 0:
+            part = turn_back(part.astype(jnp.float32), cos_ref[...], sin_ref[...]).astype(jnp.bfloat16)
+        items.append(part)
+        sums[(k % 2) * 2 + k // 2] = jnp.sum(part.astype(jnp.float32), axis=0, keepdims=True)
+    sum_ref[...] = jnp.concatenate(sums, axis=1)
+    for g in range(4):
+
+        @pl.when(ids[0] == g)
+        def _(g=g):
+            self_ref[...] = items[g]
+            near_ref[...] = items[g ^ 1]
+            far_ref[0] = items[g ^ 2]
+            far_ref[1] = items[g ^ 3]
+
+
+def turn_dkv(ids, dkv, cosine, sine):
+    count = dkv.shape[0]
+    return pl.pallas_call(
+        turn_dkv_body,
+        in_specs=[pl.BlockSpec(memory_space=pltpu.SMEM)] + [pl.BlockSpec(memory_space=pltpu.VMEM)] * 3,
+        out_specs=[pl.BlockSpec(memory_space=pltpu.VMEM)] * 4,
+        out_shape=[
+            jax.ShapeDtypeStruct((count, HD), jnp.bfloat16),
+            jax.ShapeDtypeStruct((count, HD), jnp.bfloat16),
+            jax.ShapeDtypeStruct((2, count, HD), jnp.bfloat16),
+            jax.ShapeDtypeStruct((1, 2 * KVD), jnp.float32),
+        ],
+        compiler_params=pltpu.CompilerParams(vmem_limit_bytes=VMEM),
+        cost_estimate=SMALL_COST,
+        name="turn_dkv",
+    )(ids, dkv, cosine, sine)
+
+
+def kv_grad_body(
+    blk_count, rows, small_count, self_ref, cross_ref, core_ref, dq_ref, one_ref, own_ref, near_x_ref,
+    core_x_ref, strip_ref, gain_two_ref, bias_q_ref, bias_kv_ref, grad_ref, here_ref, there_ref,
+):
+    count = self_ref.shape[0]
+    strip_q = strip_ref.shape[1] - HD
+    parts = (self_ref[...], core_ref[0], cross_ref[0], core_ref[1])
+    near = jnp.concatenate(parts, axis=0)
+    grad = tn(one_ref[...], near)
+    gain_one = jnp.zeros((1, D), jnp.float32)
+    for d in range(4):
+        x = (own_ref[...], core_x_ref[0], near_x_ref[...], core_x_ref[1])[d][:, :D].astype(jnp.float32)
+        root = lax.rsqrt(jnp.mean(x * x, axis=1, keepdims=True) + NORM_EPS)
+        hone = nt(dq_ref[count * d : count * (d + 1)], strip_ref[:, :strip_q])
+        hone = hone + nt(parts[d], strip_ref[:, strip_q:])
+        gain_one = gain_one + jnp.sum(hone * x * root, axis=0, keepdims=True)
+        out_ref = (here_ref, there_ref)[d % 2]
+        out_ref[count * (d // 2) : count * (d // 2 + 1)] = hone.astype(jnp.bfloat16)
+    vector = jnp.concatenate([gain_one, gain_two_ref[...], bias_q_ref[...], bias_kv_ref[...]], axis=1)
+    extra = grad_ref.shape[1] - rows
+    for b in range(blk_count):
+        grad_ref[b, :rows] = grad[rows * b : rows * (b + 1)].astype(jnp.bfloat16)
+        lines = []
+        for line in range(extra):
+            size = min(HD, max(small_count - line * HD, 0))
+            begin = small_count * b + line * HD
+            pieces = [vector[:, begin : begin + size]] if size > 0 else []
+            if size < HD:
+                pieces.append(jnp.zeros((1, HD - size), jnp.float32))
+            lines.append(pieces[0] if len(pieces) == 1 else jnp.concatenate(pieces, axis=1))
+        grad_ref[b, rows:] = jnp.concatenate(lines, axis=0).astype(jnp.bfloat16)
+
+
+def kv_grad_rows(rows, small_count):
+    needed = rows + -(-small_count // HD)
+    return needed + -needed % 16
+
+
+def make_kv_grad(blk_count, rows, small_count, own, cross, core, dq, one, x_own, x_cross, x_core, strip, gain_two, bias_q, bias_kv):
+    count = own.shape[0]
+    height = kv_grad_rows(rows, small_count)
+    return pl.pallas_call(
+        functools.partial(kv_grad_body, blk_count, rows, small_count),
+        in_specs=[pl.BlockSpec(memory_space=pltpu.VMEM)] * 12,
+        out_specs=[pl.BlockSpec(memory_space=pltpu.VMEM)] * 3,
+        out_shape=[
+            jax.ShapeDtypeStruct((blk_count, height, HD), jnp.bfloat16),
+            jax.ShapeDtypeStruct((2 * count, D), jnp.bfloat16),
+            jax.ShapeDtypeStruct((2 * count, D), jnp.bfloat16),
+        ],
+        compiler_params=pltpu.CompilerParams(vmem_limit_bytes=VMEM),
+        cost_estimate=SMALL_COST,
+        name="kv_grad",
+    )(own, cross, core, dq, one, x_own, x_cross, x_core, strip, gain_two, bias_q, bias_kv)
+
+
 CORE = [(0, 1), (1, 0), (2, 3), (3, 2)]
 CROSS = [(0, 2), (2, 0), (1, 3), (3, 1)]
 DIAG = [(0, 3), (3, 0), (1, 2), (2, 1)]
@@ -580,10 +797,6 @@
 def gather_near_stacked(values):
     both = jnp.stack([values, swap_cross(values)])
     return jnp.concatenate([both, swap_core(both)])
-
-
-def ring_order(count):
-    return list(range(0, count, 2)) + list(range(count - 1, 0, -2))
 
 
 def ring_groups(count):
@@ -668,9 +881,8 @@
     strip_local = jnp.concatenate([strip_local, small_send.reshape(-1, strip_wide)])
     ring = ring_order(blk_count)
     strip_ring = gather_ring(strip_local)
-    strip = jnp.concatenate([strip_ring[ring.index(b), :weight_rows] for b in range(blk_count)])
-    small_all = jnp.stack([strip_ring[ring.index(b), weight_rows:] for b in range(blk_count)])
-    small_all = small_all.reshape(blk_count, -1)
+    small_ring = strip_ring[:, weight_rows:].reshape(blk_count, -1)[:, small_count : small_count + token_count]
+    small_all = jnp.stack([small_ring[ring.index(b)] for b in range(blk_count)])
     digits = low(jnp.stack([positions // 64, positions % 64], axis=1))
     digits = jnp.pad(digits, ((0, 0), (0, HD - 2)))
     token_send = jnp.concatenate([flat_low, digits], axis=1)
@@ -698,27 +910,21 @@
     picked_a, picked_b = pick_columns(ids, w_gate, w_up, blk_count)
     got_a = swap_blk(picked_a[1], team)
     down_here = low(lax.dynamic_slice_in_dim(w_down, quarter * grp, quarter, 0))
-    down_got = swap_blk(after(down_here, token_cross), bits[0])
-    down_here = place(down_here, down_got, [], bits[0])
+    down_got = swap_blk(after(down_here, strip_ring), bits[0])
     pair_a = team_pair(picked_a[0], got_a)
     token_core = swap_core(jnp.stack([token_send, token_cross]))
-    near_all = jnp.concatenate([token_send, token_core[0], token_cross, token_core[1]])
-    near_all = after(near_all, (pair_a, down_here, dy_cross, dy_over))
-    dy_first = swap_blk(dy_cross[:half], team)
-    dy_second = swap_cross(dy_over[half:])
-    near_tokens = near_all[:, :D]
-    near_positions = 64.0 * wide(near_all[:, D]) + wide(near_all[:, D + 1])
-    vector = wide(small_all[:, :small_count].reshape(-1))
+    token_core = after(token_core, (pair_a, dy_cross, dy_over))
+    freqs = ROPE_BASE ** (-2.0 * jnp.arange(HD // 2, dtype=jnp.float32) / HD)
+    freqs = jnp.concatenate([freqs, freqs])[None]
+    mixed_own, mixed_core, mixed_far, near_one, strip, vector = mix(
+        ids, token_send, token_cross, token_core, strip_ring, freqs, blk_count, weight_rows, small_count
+    )
+    dy_first = swap_blk(after(dy_cross, mixed_own)[:half], team)
+    dy_second = swap_cross(after(dy_over, mixed_own)[half:])
+    vector = vector[0]
     gain_one = vector[:D]
     gain_two = vector[D : 2 * D]
-    bias = vector[2 * D :]
-    strip_bias = jnp.concatenate(
-        [
-            lax.dynamic_slice_in_dim(bias, strip_q * grp, strip_q, 0),
-            lax.dynamic_slice_in_dim(bias, kv_at, HD, 0),
-        ]
-    )
-    seg_all = small_all[:, small_count : small_count + token_count].astype(jnp.int32)
+    seg_all = small_all.astype(jnp.int32)
     seg_all = seg_all.reshape(blk_count, rows_here, block_len)
     seg_key = jnp.broadcast_to(
         seg_all.transpose(1, 0, 2).reshape(rows_here, seq_len)[:, :, None], (rows_here, seq_len, HD)
@@ -727,22 +933,10 @@
     first_blk = jnp.sum((seg_all[:, :, -1] < segment_ids[None, :, 0]).astype(jnp.int32), axis=0)
     attend_ids = jnp.concatenate([blk[None], first_blk])
 
-    near_wide = wide(near_tokens)
-    near_one = low(norm_apply(near_wide, gain_one))
-    mixed = jnp.dot(near_one, strip, preferred_element_type=jnp.float32) + strip_bias
-    angles = angles_of(near_positions)[:, None, :]
-    turned = jnp.arange(strip_heads + 1)[None, :, None] < strip_heads + 1 - core_id
-    angles = jnp.where(turned, angles, 0.0)
-    strip_out = low(
-        rotate_by(
-            mixed.reshape(4 * token_count, strip_heads + 1, HD), jnp.cos(angles), jnp.sin(angles)
-        )
-    ).reshape(4, token_count, strip_q + HD)
-    strips = by_place(exchange_near(strip_out))
-    query = jnp.concatenate([part[:, :strip_q] for part in strips], axis=1)
-    key_value = jnp.concatenate([strips[k][:, strip_q:] for k in (0, 2, 1, 3)], axis=1)
-    key_value = key_value.reshape(rows_here, block_len, 2 * KVD)
-    key_value = after(key_value, (dy_first, dy_second))
+    mixed_cross = swap_cross(mixed_far)
+    mixed_core = swap_core(jnp.stack([mixed_core, mixed_cross[1]]))
+    query, packed_kv = pack(ids, mixed_own, mixed_cross, mixed_core)
+    key_value = packed_kv.reshape(rows_here, block_len, 2 * KVD)
     kv_all = gather_ring(key_value)
     dy_chip = jnp.concatenate([dy_low, dy_cross, dy_over, dy_first, dy_second])
     dy_team = jnp.concatenate([dy_chip, swap_core(dy_chip)])
@@ -770,20 +964,20 @@
             done = done + [bit]
         return values
 
-    pair_a_got = swap_blk(pair_a, bits[0])
+    pair_a_got = swap_blk(after(pair_a, mixed_own), bits[0])
+    down_here = place(down_here, after(down_got, mixed_own), [], bits[0])
     down_here = lows_of(down_here, [bits[0]]).reshape(2 * blk_count // 4, quarter, D)
-    got_b = swap_blk(after(picked_b[1], strip_out), team)
-    pair_a = place(pair_a, after(pair_a_got, key_value), [team], bits[0], 1)
-    pair_b = team_pair(picked_b[0], after(got_b, key_value))
-    kv_all = after(kv_all, (pair_a, pair_b, down_here, dy_team))
-
-    gate_up_a = lows_of(after(pair_a, kv_all), [bits[0], team], 1).reshape(2, D, -1)
-    pair_b = after(pair_b, kv_all)
+    got_b = swap_blk(after(picked_b[1], mixed_own), team)
+    pair_a_got, got_b = after((pair_a_got, got_b), kv_all)
+    kv_all = after(kv_all, (pair_a_got, got_b, down_here))
+    pair_a = place(pair_a, pair_a_got, [team], bits[0], 1)
+    gate_up_a = lows_of(pair_a, [bits[0], team], 1).reshape(2, D, -1)
+    pair_b = team_pair(picked_b[0], got_b)
     pair_b_got = swap_blk(pair_b, bits[0])
     down_a = down_here[:, :size_first].reshape(widths[0], D)
     down_b = down_here[:, size_first:].reshape(widths[1], D)
 
-    out_ring = after(out_ring, key_value)
+    out_ring = after(out_ring, packed_kv)
     out_strip = jnp.concatenate([out_ring[ring.index(b)] for b in range(blk_count)])
     out_cross = swap_cross(out_strip)
     out_core = swap_core(jnp.stack([out_strip, after(out_cross, kv_all)]))
@@ -797,7 +991,7 @@
     h_team = lax.all_gather(h_two, ("grp", "blk"), axis=0, tiled=True, axis_index_groups=teams)
     pair_b_got = after(pair_b_got, (h_two, gate_up_a))
     pair_b = place(pair_b, pair_b_got, [team], bits[0], 1)
-    h_team = after(h_team, (gate_up_a, pair_b))
+    h_team = after(h_team, (gate_up_a, pair_b, dy_team))
     hidden_a, d_gate_a, d_up_a, part_a = middle(order, h_team, dy_team, gate_up_a, down_a)
     gate_up_b = lows_of(pair_b, [bits[0], team], 1, hidden_a).reshape(2, D, -1)
     down_grad_a = down_grad(hidden_a, dy_team)
@@ -860,6 +1054,8 @@
         over = jnp.concatenate([over[:half], low(wide(over[half:]) + wide(second))])
         return swap_cross(cross), swap_blk(over, team)
 
+    near_att_cross = swap_cross(after(att_in, hidden_a))
+    d_htwo_part = after(d_htwo_part, (first_a[1], down_share_a, near_att_cross))
     d_came = swap_core(d_htwo_part[chip_rows:])
     down_grad_b = down_grad(hidden_b, dy_team)
     rows_b = part_sent(
@@ -873,7 +1069,7 @@
     d_cross, d_over = scatter_near(d_chip, *d_far)
     out_part = down(*after((hidden_a, hidden_b), d_far), down_a, down_b, token_count)
     out_came = swap_core(out_part[chip_rows:])
-    mid_a = columns_mid(*after(first_a, out_part))
+    mid_a = columns_mid(*after(first_a, d_far))
     second_a = part_sent(mid_a, 1, bits[0])
     d_cross, d_over = after((d_cross, d_over), out_part)
     d_htwo = wide(d_chip[:token_count]) + wide(d_cross) + wide(d_over)
@@ -881,7 +1077,7 @@
     norm_value_two, norm_back_two = jax.vjp(norm_apply, resid, gain_two)
     d_resid_norm, grad_gain_two = norm_back_two(d_htwo)
     d_resid = wide(dy_low) + d_resid_norm
-    d_att = after(low(d_resid), down_share_a)
+    d_att = low(d_resid)
     rows_b = rows_second(*after(rows_b, d_att))
 
     d_attended = low(right_transposed(d_att, out_full))
@@ -918,33 +1114,35 @@
     query_grad = low(left_product(near_one, near_dq)).reshape(block_shape)
     steps_query = part_sent(query_grad, len(bits) - 1, bits[-1])
     near_a = gather_near_stacked(columns_last(*after(third_a, d_query)))
-    dkv = wide(after(dkv, (query_grad, down_share_b))).reshape(token_count, 2, KVH, HD)
-    d_key = low(rotate_by(dkv[:, 0], cosine[:, None], -sine[:, None]))
-    d_value = low(dkv[:, 1])
-    near_dkv = to_strips([(d_value if k % 2 else d_key)[:, k // 2] for k in range(4)])
-    near_dkv = after(near_dkv, near_a)
-    kv_grad = low(left_product(near_one, near_dkv)).reshape(block_shape)
-    grad_bias = jnp.concatenate(
-        [
-            jnp.sum(wide(part), axis=0)
-            for part in (d_query, d_key.reshape(token_count, KVD), d_value.reshape(token_count, KVD))
-        ]
-    )
-    near_hone = right_transposed(near_dq, strip[:, :strip_q]) + right_transposed(
-        near_dkv, strip[:, strip_q:]
-    )
-    near_rms = lax.rsqrt(jnp.mean(near_wide * near_wide, axis=-1, keepdims=True) + NORM_EPS)
-    gain_one_part = jnp.sum(near_hone * near_wide * near_rms, axis=0)
+    dkv = after(dkv, (query_grad, down_share_b))
+    own_part, core_part, far_part, bias_kv = turn_dkv(
+        ids, dkv, jnp.concatenate([cosine, cosine], axis=1), jnp.concatenate([sine, sine], axis=1)
+    )
+    bias_q = jnp.sum(wide(d_query), axis=0)
+    d_key = own_part
+    cross_part = swap_cross(far_part)
+    core_part = swap_core(jnp.stack([core_part, cross_part[1]]))
+    kv_grad, hone_here, hone_there = make_kv_grad(
+        blk_count,
+        weight_rows,
+        small_count,
+        own_part,
+        cross_part,
+        core_part,
+        near_dq,
+        near_one,
+        token_send,
+        token_cross,
+        token_core,
+        strip,
+        grad_gain_two[None],
+        bias_q[None],
+        bias_kv,
+    )
     vector_rows = -(-small_count // HD)
-    vector_term = jnp.concatenate([gain_one_part, grad_gain_two, grad_bias])
-    vector_term = vector_term.reshape(blk_count, small_count)
-    vector_term = jnp.pad(vector_term, ((0, 0), (0, vector_rows * HD - small_count)))
-    vector_term = low(vector_term).reshape((2,) * len(bits) + (vector_rows, HD))
-    kv_grad = jnp.concatenate([kv_grad, vector_term], axis=-2)
-    kv_pad = -kv_grad.shape[-2] % 16
-    kv_grad = jnp.pad(kv_grad, ((0, 0),) * (len(bits)) + ((0, kv_pad), (0, 0)))
+    kv_grad = kv_grad.reshape((2,) * len(bits) + kv_grad.shape[1:])
     steps_kv = part_sent(kv_grad, len(bits) - 1, bits[-1])
-    second_b = part_sent(columns_mid(*after(first_b, dkv)), 1, bits[0])
+    second_b = part_sent(columns_mid(*after(first_b, d_query)), 1, bits[0])
     share_down = after(jnp.concatenate([down_share_a, down_share_b]), dkv)
     grad_down = lax.all_gather(share_down, "grp", axis=0, tiled=True)
     for i in range(len(bits) - 2, -1, -1):
@@ -952,33 +1150,34 @@
         kv_sum = part_sum(*steps_kv)
         kv_grad = kv_sum
         steps_kv = part_sent(kv_sum, i, bits[i])
-    share_kv_all = wide(steps_kv[0]) + wide(steps_kv[1])
+    share_kv_all = wide(steps_kv[0]) + wide(after(steps_kv[1], near_a))
     share_kv = low(share_kv_all[:weight_rows])
     vector_part = share_kv_all[weight_rows : weight_rows + vector_rows]
     sum_b, third_b = columns_third(*after(second_b, kv_grad))
     share_query = part_sum(*after(steps_query, kv_grad))
-    near_att = jnp.concatenate(gather_near(after(att_in, hidden_a)))
+    near_att = swap_core(jnp.stack([att_in, near_att_cross]))
+    near_att = jnp.concatenate([att_in, near_att[0], near_att_cross, near_att[1]])
     near_datt = to_strips([d_att[:, strip_q * k : strip_q * (k + 1)] for k in range(4)])
     out_grad = low(left_product(near_att, after(near_datt, d_attended))).reshape(block_shape)
     steps_out = part_sent(out_grad, len(bits) - 1, bits[-1])
-    anchors = [d_query, d_key]
+    anchors = [near_dq, near_dq]
     for i in range(len(bits) - 2, -1, -1):
         anchor = anchors[min(len(bits) - 2 - i, 1)]
         steps_out = part_sent(part_sum(*after(steps_out, anchor)), i, bits[i])
-    share_out = part_sum(*after(steps_out, kv_grad))
-
-    near_b = gather_near_stacked(columns_last(*third_b))
+    share_out = part_sum(*after(steps_out, own_part))
+
+    own_b = columns_last(*after(third_b, share_kv_all))
+    cross_b = swap_cross(own_b)
+    near_b = jnp.stack([own_b, cross_b])
+    near_b = jnp.concatenate([near_b, swap_core(near_b)])
     grad_out = jnp.concatenate(gather_grp(share_out), axis=1)
     query_parts = gather_grp(share_query)
     key_parts = gather_grp(share_kv)
     grad_attend = jnp.concatenate(query_parts + [key_parts[k] for k in (0, 2, 1, 3)], axis=1)
 
-    sides = low(near_hone[token_count : 2 * token_count]), low(near_hone[3 * token_count :])
-    other = wide(swap_core(jnp.concatenate(sides)))
-    d_hone = near_hone[:token_count] + other[:token_count]
-    d_hone_cross = swap_cross(
-        low(near_hone[2 * token_count : 3 * token_count] + other[token_count:])
-    )
+    other = wide(swap_core(hone_there))
+    d_hone = wide(hone_here[:token_count]) + other[:token_count]
+    d_hone_cross = swap_cross(low(wide(hone_here[token_count:]) + other[token_count:]))
     square_sum = square_total(
         [
             wide(s)
@@ -996,7 +1195,7 @@
     factor = jnp.minimum(1.0, CLIP_NORM / (grad_norm + 1e-06))
     out_chip = chip_sum(out_part, after(out_came, kv_grad))
     out_far = scatter_far(out_chip)
-    factor = after(factor, out_chip)
+    factor = after(factor, (out_chip, cross_b))
 
     new_first_gate, new_second_gate, new_gate = adam_columns(
         0, ids, factor[None], near_a, near_b, w_gate, first_gate, second_gate, blk_count, RATE_GATE, WEIGHT_DECAY

time: 870 us -> 870 us (level)
  waiting for transfers between devices: 286 us -> 343 us
  local copies, waits for them, and re-layouts: 132 us -> 92.6 us
  other arithmetic: 159 us -> 125 us
  Pallas kernels: 161 us -> 181 us
  matrix products: 23.9 us -> 7.22 us
  starting transfers between devices: 75.3 us -> 91.7 us
    ppermute x34, waiting for transfers between devices: 231 us -> 276 us  [swap_blk(): return lax.ppermute(values, 'blk', [(i, i ^ bit) for i in range(count)])]
    ppermute x20, waiting for transfers between devices: 45.6 us -> 65.1 us  [swap_cross(): return lax.ppermute(values, 'grp', CROSS)]
    pallas_call x0 -> x4, Pallas kernels: none -> 18.2 us  [the longest x1 8.06 us: mix(): pl.pallas_call(functools.partial(mix_body, blk_count, rows, small_count),...]
    ppermute x34, starting transfers between devices: 52.5 us -> 63.1 us  [swap_blk(): return lax.ppermute(values, 'blk', [(i, i ^ bit) for i in range(count)])]
    slice x19 -> x7, local copies, waits for them, and re-layouts: 10.7 us -> 0.73 us  [the longest x1 0.62 us: on_device(): gain_one = vector[:D]]
    unnamed x268 -> x283, local copies, waits for them, and re-layouts: 50.4 us -> 42.9 us
  transfers between devices with their start and end apart: 78 -> 78, of which waited for: 28 -> 29; matrix products, arithmetic and copies ran while one was open for 32% -> 21% of each run, Pallas kernels for 13% -> 18%
where the time goes in v7:
time: 870 us; the launch traced here: 862 us
  waiting for transfers between devices  343 us (39%)
  Pallas kernels  181 us (21%)
  other arithmetic  125 us (14%)
  local copies, waits for them, and re-layouts  92.6 us (11%)
  starting transfers between devices  91.7 us (11%)
  between operations  22.1 us (3%)
    ppermute x34, waiting for transfers between devices, swap_blk(): return lax.ppermute(values, 'blk', [(i, i ^ bit) for i in range(count)])  276 us
    ppermute x20, waiting for transfers between devices, swap_cross(): return lax.ppermute(values, 'grp', CROSS)  65.1 us
    ppermute x34, starting transfers between devices, swap_blk(): return lax.ppermute(values, 'blk', [(i, i ^ bit) for i in range(count)])  63.1 us
    pallas_call x2, Pallas kernels, middle(): pl.pallas_call(functools.partial(middle_body, prev is not None), grid_spe...  60.5 us
    unnamed x283, local copies, waits for them, and re-layouts  42.9 us
    pallas_call x2, Pallas kernels, adam_columns(): pl.pallas_call(functools.partial(adam_body, blk_count, rate, decay), grid...  35.2 us
    convert_element_type x21, other arithmetic, low(): return values.astype(jnp.bfloat16)  26.2 us
    ppermute x20, starting transfers between devices, swap_cross(): return lax.ppermute(values, 'grp', CROSS)  26.2 us
  transfers between devices with their start and end apart: 78, of which 29 were waited for; matrix products, arithmetic and copies ran while one was open for 21% of the time, Pallas kernels for 18%

profile of v7, /device:TPU:0, one launch (start us, length us, event | category | flops | bytes accessed | tf_op | source)
XLA Modules:
  0.0 861.9 jit_solution(15204593373065169415)
XLA Ops:
  15.4 18.9 %collective-permute-done.cross_ref.near_x_ref = bf16[256,1664]{1,0:T(8,128)(2,1)S(1)} collective-permute-done((bf16[256,1664]{1,0:T(8,128)(2,1)S(1)}, bf16[256,1664]{1,0:T(8,128)(2,1)S(1)}, u32[]{:S(2)}, u32[]{:S(2)}) %collective-permute-start) | collective-permute-done | bytes 852000 | tf_op jit(solution)/shard_map/ppermute | solution.py:686
  51.5 11.2 %collective-permute-done.2 = bf16[2,192,512]{2,1,0:T(8,128)(2,1)S(1)} collective-permute-done((bf16[2,192,512]{2,1,0:T(8,128)(2,1)S(1)}, bf16[2,192,512]{2,1,0:T(8,128)(2,1)S(1)}, u32[]{:S(2)}, u32[]{:S(2)}) %collective-permute-start.2) | collective-permute-done | bytes 393248 | tf_op jit(solution)/shard_map/ppermute | solution.py:695
  64.8 21.8 %collective-permute-done.4 = bf16[256,1536]{1,0:T(8,128)(2,1)S(1)} collective-permute-done((bf16[256,1536]{1,0:T(8,128)(2,1)}, bf16[256,1536]{1,0:T(8,128)(2,1)S(1)}, u32[]{:S(2)}, u32[]{:S(2)}) %collective-permute-start.4) | collective-permute-done | bytes 786464 | tf_op jit(solution)/shard_map/ppermute | solution.py:695
  88.4 8.1 mix.1
  113.4 28.6 %collective-permute-done.9 = bf16[280,1536]{1,0:T(8,128)(2,1)} collective-permute-done((bf16[280,1536]{1,0:T(8,128)(2,1)S(1)}, bf16[280,1536]{1,0:T(8,128)(2,1)}, u32[]{:S(2)}, u32[]{:S(2)}) %collective-permute-start.9) | collective-permute-done | bytes 860192 | tf_op jit(solution)/shard_map/ppermute | solution.py:695
  167.2 39.1 %collective-permute-done.10 = bf16[2,280,1536]{2,1,0:T(8,128)(2,1)} collective-permute-done((bf16[2,280,1536]{2,1,0:T(8,128)(2,1)}, bf16[2,280,1536]{2,1,0:T(8,128)(2,1)}, u32[]{:S(2)}, u32[]{:S(2)}) %collective-permute-start.10) | collective-permute-done | bytes 1720352 | tf_op jit(solution)/shard_map/ppermute | solution.py:695
  249.3 12.9 %collective-permute-start.14 = (bf16[2,2,192,608]{3,2,0,1:T(8,128)(2,1)}, bf16[2,2,192,608]{3,2,0,1:T(8,128)(2,1)}, u32[]{:S(2)}, u32[]{:S(2)}) collective-permute-start(bf16[2,2,192,608]{3,2,0,1:T(8,128)(2,1)} %pad_maximum_fusion.14), channel_id=1, source_target_pairs={{0,4},{1,5},{2,6},{3,7},{4,0},{5,1},{6,2},{7,3},{8,12},{9,13},{10,... | collective-permute-start | bytes 2801672 | tf_op jit(solution)/shard_map/ppermute | solution.py:695
  267.6 15.7 %collective-permute-done.13 = bf16[2,2,2,192,512]{4,3,0,2,1:T(8,128)(2,1)} collective-permute-done((bf16[2,2,2,192,512]{4,3,0,2,1:T(8,128)(2,1)}, bf16[2,2,2,192,512]{4,3,0,2,1:T(8,128)(2,1)}, u32[]{:S(2)}, u32[]{:S(2)}) %collective-permute-start.13) | collective-permute-done | bytes 1572896 | tf_op jit(solution)/shard_map/ppermute | solution.py:695
  287.3 17.6 %collective-permute-done.14 = bf16[2,2,192,608]{3,2,0,1:T(8,128)(2,1)} collective-permute-done((bf16[2,2,192,608]{3,2,0,1:T(8,128)(2,1)}, bf16[2,2,192,608]{3,2,0,1:T(8,128)(2,1)}, u32[]{:S(2)}, u32[]{:S(2)}) %collective-permute-start.14) | collective-permute-done | bytes 933920 | tf_op jit(solution)/shard_map/ppermute | solution.py:695
  308.9 23.2 %middle.2 = (bf16[2048,512]{1,0:T(8,128)(2,1)S(1)}, bf16[2048,512]{1,0:T(8,128)(2,1)S(1)}, bf16[2048,512]{1,0:T(8,128)(2,1)}, bf16[2048,1536]{1,0:T(8,128)(2,1)}) custom-call(s32[8]{0:T(128)S(1)} %stack.301.order, bf16[2048,1536]{1,0:T(8,128)(2,1)} %all-gather.10.cloned.1.call-done.h_ref, bf16[2048,1536]{1,0:T(8,128)(2,1)} %constant_dynamic-update-slice_fusion.12.dy_ref, ...), custom_call_target="tpu_custom_call" | custom-call | flops 1000 | bytes 1000 | tf_op jit(solution)/shard_map/middle/pallas_call | solution.py:370
  346.8 10.1 %two_grads.2 = bf16[2,1536,512]{2,1,0:T(8,128)(2,1)} custom-call(bf16[2048,1536]{1,0:T(8,128)(2,1)} %all-gather.10.cloned.1.call-done.h_ref, bf16[2048,512]{1,0:T(8,128)(2,1)S(1)} %copy-done.22, bf16[2048,512]{1,0:T(8,128)(2,1)S(1)} %copy-done.23), custom_call_target="tpu_custom_call" | custom-call | flops 1000 | bytes 1000 | tf_op jit(solution)/shard_map/two_grads/pallas_call | solution.py:403
  362.4 38.3 %collective-permute-done.18 = bf16[2,2,2,192,608]{4,3,0,2,1:T(8,128)(2,1)} collective-permute-done((bf16[2,2,2,192,608]{4,3,0,2,1:T(8,128)(2,1)}, bf16[2,2,2,192,608]{4,3,0,2,1:T(8,128)(2,1)}, u32[]{:S(2)}, u32[]{:S(2)}) %collective-permute-start.18) | collective-permute-done | bytes 1867808 | tf_op jit(solution)/shard_map/ppermute | solution.py:695
  405.7 37.3 %middle.3 = (bf16[2048,608]{1,0:T(8,128)(2,1)S(1)}, bf16[2048,608]{1,0:T(8,128)(2,1)}, bf16[2048,608]{1,0:T(8,128)(2,1)}, bf16[2048,1536]{1,0:T(8,128)(2,1)}) custom-call(s32[8]{0:T(128)S(1)} %stack.301.order, bf16[2048,1536]{1,0:T(8,128)(2,1)} %all-gather.10.cloned.1.call-done.h_ref, bf16[2048,1536]{1,0:T(8,128)(2,1)} %constant_dynamic-update-slice_fusion.12.dy_ref, ...), custom_call_target="tpu_custom_call" | custom-call | flops 1000 | bytes 1000 | tf_op jit(solution)/shard_map/middle/pallas_call | solution.py:370
  468.4 13.7 %two_grads.3 = bf16[2,1536,608]{2,1,0:T(8,128)(2,1)} custom-call(bf16[2048,1536]{1,0:T(8,128)(2,1)} %all-gather.10.cloned.1.call-done.h_ref, bf16[2048,608]{1,0:T(8,128)(2,1)S(1)} %copy-done.19, bf16[2048,608]{1,0:T(8,128)(2,1)S(1)} %copy-done.20), custom_call_target="tpu_custom_call" | custom-call | flops 1000 | bytes 1000 | tf_op jit(solution)/shard_map/two_grads/pallas_call | solution.py:403
  499.0 11.5 %down.1 = bf16[2048,1536]{1,0:T(8,128)(2,1)} custom-call(bf16[2048,512]{1,0:T(8,128)(2,1)S(1)} %copy-done.6, bf16[2048,608]{1,0:T(8,128)(2,1)} %copy-done.1, bf16[512,1536]{1,0:T(8,128)(2,1)S(1)} %bitcast.408, bf16[608,1536]{1,0:T(8,128)(2,1)S(1)} %bitcast.406), custom_call_target="tpu_custom_call" | custom-call | flops 1000 | bytes 1000 | tf_op jit(solution)/shard_map/down/pallas_call | solution.py:443
  520.3 8.0 attend_back.1
  548.6 20.8 %collective-permute-done.39 = bf16[2,192,512]{2,1,0:T(8,128)(2,1)S(1)} collective-permute-done((bf16[2,192,512]{2,1,0:T(8,128)(2,1)S(1)}, bf16[2,192,512]{2,1,0:T(8,128)(2,1)S(1)}, u32[]{:S(2)}, u32[]{:S(2)}) %collective-permute-start.39) | collective-permute-done | bytes 393248 | tf_op jit(solution)/shard_map/ppermute | solution.py:695
  581.7 9.0 %collective-permute-done.40 = bf16[2,2,192,512]{3,2,1,0:T(8,128)(2,1)} collective-permute-done((bf16[2,2,192,512]{3,2,1,0:T(8,128)(2,1)}, bf16[2,2,192,512]{3,2,1,0:T(8,128)(2,1)}, u32[]{:S(2)}, u32[]{:S(2)}) %collective-permute-start.40) | collective-permute-done | bytes 786464 | tf_op jit(solution)/shard_map/ppermute | solution.py:686
  615.5 37.8 %collective-permute-done.50 = bf16[192,384]{1,0:T(8,128)(2,1)} collective-permute-done((bf16[192,384]{1,0:T(8,128)(2,1)}, bf16[192,384]{1,0:T(8,128)(2,1)}, u32[]{:S(2)}, u32[]{:S(2)}) %collective-permute-start.50) | collective-permute-done | bytes 147488 | tf_op jit(solution)/shard_map/ppermute | solution.py:695
  739.9 24.5 %collective-permute-done.59 = bf16[2,2,192,608]{3,2,1,0:T(8,128)(2,1)S(1)} collective-permute-done((bf16[2,2,192,608]{3,2,1,0:T(8,128)(2,1)S(1)}, bf16[2,2,192,608]{3,2,1,0:T(8,128)(2,1)S(1)}, u32[]{:S(2)}, u32[]{:S(2)}) %collective-permute-start.59) | collective-permute-done | bytes 933920 | tf_op jit(solution)/shard_map/ppermute | solution.py:686
  776.1 17.6 %adam_columns.2 = (f32[192,8960]{1,0:T(8,128)}, f32[192,8960]{1,0:T(8,128)}, f32[192,8960]{1,0:T(8,128)}) custom-call(s32[2]{0:T(128)S(1)} %pad_add_fusion.2.ids, f32[1]{0:T(128)} %bitcast.131.factor_ref, bf16[4,2,2,192,512]{4,3,2,1,0:T(8,128)(2,1)S(1)} %pad_maximum_fusion.5.first_ref, bf16[4,2,2,192,608]{4,3,2,1,0:T(8,128)(2,1)} %pad_maximum_fusion.2.second_ref, ...), custom_call_target="tpu_custom_call" | custom-call | flops 1000 | bytes 1000 | tf_op jit(solution)/shard_map/adam_columns/pallas_call | solution.py:155
  793.7 17.6 %adam_columns.3 = (f32[192,8960]{1,0:T(8,128)}, f32[192,8960]{1,0:T(8,128)}, f32[192,8960]{1,0:T(8,128)}) custom-call(s32[2]{0:T(128)S(1)} %pad_add_fusion.2.ids, f32[1]{0:T(128)} %bitcast.131.factor_ref, bf16[4,2,2,192,512]{4,3,2,1,0:T(8,128)(2,1)S(1)} %pad_maximum_fusion.5.first_ref, bf16[4,2,2,192,608]{4,3,2,1,0:T(8,128)(2,1)} %pad_maximum_fusion.2.second_ref, ...), custom_call_target="tpu_custom_call" | custom-call | flops 1000 | bytes 1000 | tf_op jit(solution)/shard_map/adam_columns/pallas_call | solution.py:155
  813.2 16.9 %multiply_subtract_fusion = (f32[1120,1536]{1,0:T(8,128)}, f32[1120,1536]{1,0:T(8,128)}, f32[1120,1536]{1,0:T(8,128)}) fusion(f32[1120,1536]{1,0:T(8,128)} %param.30, bf16[1120,1536]{1,0:T(8,128)(2,1)} %all-gather.12.cloned.1.call-done, f32[]{:T(128)} %min.3, f32[1120,1536]{1,0:T(8,128)} %param.36, f32[1120,1536]{1,0:T(8,128)} %param.42), kind=kLoop, calls=%fused_computation.2 | loop fusion | flops 29245440 | bytes 44728324 | tf_op jit(solution)/shard_map/sub | solution.py:67
  836.1 14.8 %collective-permute-done.61 = bf16[256,1536]{1,0:T(8,128)(2,1)S(1)} collective-permute-done((bf16[256,1536]{1,0:T(8,128)(2,1)S(1)}, bf16[256,1536]{1,0:T(8,128)(2,1)S(1)}, u32[]{:S(2)}, u32[]{:S(2)}) %collective-permute-start.61) | collective-permute-done | bytes 786464 | tf_op jit(solution)/shard_map/ppermute | solution.py:695
  (622 shorter events, 364.8 us)
Async XLA Ops:
  11.4 138.1 %all-gather.16.cloned.1.call-start = ((), (), s32[]{:S(2)}) async-start(), calls=%async_computation.8 | async-start | bytes 1327104 | tf_op jit(solution)/shard_map/all_gather | solution.py:808
  35.8 52.5 %collective-permute-start.1 = (bf16[2,256,1664]{2,1,0:T(8,128)(2,1)}, bf16[2,256,1664]{2,1,0:T(8,128)(2,1)S(1)}, u32[]{:S(2)}, u32[]{:S(2)}) collective-permute-start(bf16[2,256,1664]{2,1,0:T(8,128)(2,1)} %pad_maximum_fusion.10), channel_id=1, source_target_pairs={{0,8},{8,0},{16,24},{24,16},{1,9},{9,1},{17,25},{25,17},{2,10},{10... | collective-permute-start | bytes 5111816 | tf_op jit(solution)/shard_map/ppermute | solution.py:682
  46.3 163.9 %all-gather.8.cloned.1.call-start = ((), (), s32[]{:S(2)}) async-start(), calls=%async_computation.2 | async-start | bytes 2359296 | tf_op jit(solution)/shard_map/all_gather | solution.py:808
  143.5 165.5 %all-gather.10.cloned.1.call-start = ((), (), s32[]{:S(2)}) async-start(), calls=%async_computation.3 | async-start | bytes 7077888 | tf_op jit(solution)/shard_map/all_gather | solution.py:991
  148.0 58.3 %collective-permute-start.10 = (bf16[2,280,1536]{2,1,0:T(8,128)(2,1)}, bf16[2,280,1536]{2,1,0:T(8,128)(2,1)}, u32[]{:S(2)}, u32[]{:S(2)}) collective-permute-start(bf16[2,280,1536]{2,1,0:T(8,128)(2,1)} %pad_maximum_fusion.9), channel_id=1, source_target_pairs={{0,1},{1,0},{2,3},{3,2},{4,5},{5,4},{6,7},{7,6},{8,9},{9,8},{10,11... | collective-permute-start | bytes 5160968 | tf_op jit(solution)/shard_map/ppermute | solution.py:695
  162.3 47.9 %collective-permute-start.11 = (bf16[1536,384]{1,0:T(8,128)(2,1)}, bf16[1536,384]{1,0:T(8,128)(2,1)}, u32[]{:S(2)}, u32[]{:S(2)}) collective-permute-start(bf16[1536,384]{1,0:T(8,128)(2,1)} %bitcast_dynamic-update-slice_fusion), channel_id=1, source_target_pairs={{0,16},{16,0},{8,24},{24,8},{1,17},{17,1},{9,25},{25,9},{2,18},{18... | collective-permute-start | bytes 3538952 | tf_op jit(solution)/shard_map/ppermute | solution.py:686
  163.1 47.1 %collective-permute-start.7 = (bf16[2,2,192,512]{3,2,0,1:T(8,128)(2,1)S(1)}, bf16[2,2,192,512]{3,2,0,1:T(8,128)(2,1)S(1)}, u32[]{:S(2)}, u32[]{:S(2)}) collective-permute-start(bf16[2,2,192,512]{3,2,0,1:T(8,128)(2,1)S(1)} %copy-done.102), channel_id=1, source_target_pairs={{0,4},{1,5},{2,6},{3,7},{4,0},{5,1},{6,2},{7,3},{8,12},{9,13},{10,... | collective-permute-start | bytes 2359304 | tf_op jit(solution)/shard_map/ppermute | solution.py:695
  163.1 47.0 %collective-permute-start.8 = (bf16[2,192,608]{2,1,0:T(8,128)(2,1)S(1)}, bf16[2,192,608]{2,1,0:T(8,128)(2,1)}, u32[]{:S(2)}, u32[]{:S(2)}) collective-permute-start(bf16[2,192,608]{2,1,0:T(8,128)(2,1)S(1)} %slice_bitcast_fusion.4), channel_id=1, source_target_pairs={{0,2},{1,3},{2,0},{3,1},{4,6},{5,7},{6,4},{7,5},{8,10},{9,11},{10,... | collective-permute-start | bytes 1400840 | tf_op jit(solution)/shard_map/ppermute | solution.py:695
  228.9 216.5 %reduce-scatter.3.cloned.1.call-start = ((), (), s32[]{:S(2)}) async-start(), calls=%async_computation.4 | async-start | bytes 1966080 | tf_op jit(solution)/shard_map/reduce_scatter | solution.py:998
  249.3 55.6 %collective-permute-start.14 = (bf16[2,2,192,608]{3,2,0,1:T(8,128)(2,1)}, bf16[2,2,192,608]{3,2,0,1:T(8,128)(2,1)}, u32[]{:S(2)}, u32[]{:S(2)}) collective-permute-start(bf16[2,2,192,608]{3,2,0,1:T(8,128)(2,1)} %pad_maximum_fusion.14), channel_id=1, source_target_pairs={{0,4},{1,5},{2,6},{3,7},{4,0},{5,1},{6,2},{7,3},{8,12},{9,13},{10,... | collective-permute-start | bytes 2801672 | tf_op jit(solution)/shard_map/ppermute | solution.py:695
  341.5 269.9 %reduce-scatter.5.cloned.1.call-start = ((), (), s32[]{:S(2)}) async-start(), calls=%async_computation.5 | async-start | bytes 2359296 | tf_op jit(solution)/shard_map/reduce_scatter | solution.py:1099
  342.0 58.7 %collective-permute-start.18 = (bf16[2,2,2,192,608]{4,3,0,2,1:T(8,128)(2,1)}, bf16[2,2,2,192,608]{4,3,0,2,1:T(8,128)(2,1)}, u32[]{:S(2)}, u32[]{:S(2)}) collective-permute-start(bf16[2,2,2,192,608]{4,3,0,2,1:T(8,128)(2,1)} %pad_maximum_fusion.7), channel_id=1, source_target_pairs={{0,1},{1,0},{2,3},{3,2},{4,5},{5,4},{6,7},{7,6},{8,9},{9,8},{10,11... | collective-permute-start | bytes 5603336 | tf_op jit(solution)/shard_map/ppermute | solution.py:695
  360.5 84.9 %collective-permute-start.19 = (bf16[2,2,2,192,512]{4,3,2,1,0:T(8,128)(2,1)S(1)}, bf16[2,2,2,192,512]{4,3,2,1,0:T(8,128)(2,1)}, u32[]{:S(2)}, u32[]{:S(2)}) collective-permute-start(bf16[2,2,2,192,512]{4,3,2,1,0:T(8,128)(2,1)S(1)} %get-tuple-element.282), channel_id=1, source_target_pairs={{0,1},{1,0},{2,3},{3,2},{4,5},{5,4},{6,7},{7,6},{8,9},{9,8},{10,11... | collective-permute-start | bytes 4718600 | tf_op jit(solution)/shard_map/ppermute | solution.py:695
  360.9 83.7 %collective-permute-start.20 = (bf16[256,1536]{1,0:T(8,128)(2,1)S(1)}, bf16[256,1536]{1,0:T(8,128)(2,1)S(1)}, u32[]{:S(2)}, u32[]{:S(2)}) collective-permute-start(bf16[256,1536]{1,0:T(8,128)(2,1)S(1)} %copy-done.15), channel_id=1, source_target_pairs={{0,16},{16,0},{8,24},{24,8},{1,17},{17,1},{9,25},{25,9},{2,18},{18... | collective-permute-start | bytes 2359304 | tf_op jit(solution)/shard_map/ppermute | solution.py:686
  467.4 63.5 %collective-permute-start.29 = (bf16[2,152,1536]{2,1,0:T(8,128)(2,1)}, bf16[2,152,1536]{2,1,0:T(8,128)(2,1)}, u32[]{:S(2)}, u32[]{:S(2)}) collective-permute-start(bf16[2,152,1536]{2,1,0:T(8,128)(2,1)} %get-tuple-element.295), channel_id=1, source_target_pairs={{0,1},{1,0},{2,3},{3,2},{4,5},{5,4},{6,7},{7,6},{8,9},{9,8},{10,11... | collective-permute-start | bytes 2801672 | tf_op jit(solution)/shard_map/ppermute | solution.py:695
  493.4 80.8 %collective-permute-start.51 = (bf16[2,2,2,192,608]{4,3,2,1,0:T(8,128)(2,1)}, bf16[2,2,2,192,608]{4,3,2,1,0:T(8,128)(2,1)}, u32[]{:S(2)}, u32[]{:S(2)}) collective-permute-start(bf16[2,2,2,192,608]{4,3,2,1,0:T(8,128)(2,1)} %get-tuple-element.269), channel_id=1, source_target_pairs={{0,1},{1,0},{2,3},{3,2},{4,5},{5,4},{6,7},{7,6},{8,9},{9,8},{10,11... | collective-permute-start | bytes 5603336 | tf_op jit(solution)/shard_map/ppermute | solution.py:695
  514.4 197.3 %collective-permute-start.24 = (bf16[1024,1536]{1,0:T(8,128)(2,1)}, bf16[1024,1536]{1,0:T(8,128)(2,1)}, u32[]{:S(2)}, u32[]{:S(2)}) collective-permute-start(bf16[1024,1536]{1,0:T(8,128)(2,1)} %slice.381), channel_id=1, source_target_pairs={{0,8},{8,0},{16,24},{24,16},{1,9},{9,1},{17,25},{25,17},{2,10},{10... | collective-permute-start | bytes 9437192 | tf_op jit(solution)/shard_map/ppermute | solution.py:682
  539.4 273.8 %all-gather.12.cloned.1.call-start = ((), (), s32[]{:S(2)}) async-start(), calls=%async_computation.6 | async-start | bytes 4300800 | tf_op jit(solution)/shard_map/all_gather | solution.py:1147
  598.3 54.9 %collective-permute-start.42 = (bf16[2,2,192,384]{3,2,1,0:T(8,128)(2,1)}, bf16[2,2,192,384]{3,2,1,0:T(8,128)(2,1)}, u32[]{:S(2)}, u32[]{:S(2)}) collective-permute-start(bf16[2,2,192,384]{3,2,1,0:T(8,128)(2,1)} %get-tuple-element.309), channel_id=1, source_target_pairs={{0,1},{1,0},{2,3},{3,2},{4,5},{5,4},{6,7},{7,6},{8,9},{9,8},{10,11... | collective-permute-start | bytes 1769480 | tf_op jit(solution)/shard_map/ppermute | solution.py:695
  600.1 83.6 %collective-permute-start.52 = (bf16[2,2,192,608]{3,2,1,0:T(8,128)(2,1)}, bf16[2,2,192,608]{3,2,1,0:T(8,128)(2,1)}, u32[]{:S(2)}, u32[]{:S(2)}) collective-permute-start(bf16[2,2,192,608]{3,2,1,0:T(8,128)(2,1)} %get-tuple-element.291), channel_id=1, source_target_pairs={{0,4},{1,5},{2,6},{3,7},{4,0},{5,1},{6,2},{7,3},{8,12},{9,13},{10,... | collective-permute-start | bytes 2801672 | tf_op jit(solution)/shard_map/ppermute | solution.py:695
  613.3 45.1 %collective-permute-start.31 = (bf16[2,256,128]{2,1,0:T(8,128)(2,1)S(1)}, bf16[2,256,128]{2,1,0:T(8,128)(2,1)S(1)}, u32[]{:S(2)}, u32[]{:S(2)}) collective-permute-start(bf16[2,256,128]{2,1,0:T(8,128)(2,1)S(1)} %get-tuple-element.181), channel_id=1, source_target_pairs={{0,16},{16,0},{8,24},{24,8},{1,17},{17,1},{9,25},{25,9},{2,18},{18... | collective-permute-start | bytes 393224 | tf_op jit(solution)/shard_map/ppermute | solution.py:686
  726.9 103.2 %collective-permute-start.35 = (bf16[128,1536]{1,0:T(8,128)(2,1)}, bf16[128,1536]{1,0:T(8,128)(2,1)}, u32[]{:S(2)}, u32[]{:S(2)}) collective-permute-start(bf16[128,1536]{1,0:T(8,128)(2,1)} %get-tuple-element.278), channel_id=1, source_target_pairs={{0,2},{1,3},{2,0},{3,1},{4,6},{5,7},{6,4},{7,5},{8,10},{9,11},{10,... | collective-permute-start | bytes 1179656 | tf_op jit(solution)/shard_map/ppermute | solution.py:695
  729.9 100.1 %collective-permute-start.36 = (bf16[128,1536]{1,0:T(8,128)(2,1)}, bf16[128,1536]{1,0:T(8,128)(2,1)}, u32[]{:S(2)}, u32[]{:S(2)}) collective-permute-start(bf16[128,1536]{1,0:T(8,128)(2,1)} %get-tuple-element.277), channel_id=1, source_target_pairs={{0,16},{16,0},{8,24},{24,8},{1,17},{17,1},{9,25},{25,9},{2,18},{18... | collective-permute-start | bytes 1179656 | tf_op jit(solution)/shard_map/ppermute | solution.py:686
  766.9 44.4 %collective-permute-start.64 = (bf16[256,1536]{1,0:T(8,128)(2,1)}, bf16[256,1536]{1,0:T(8,128)(2,1)}, u32[]{:S(2)}, u32[]{:S(2)}) collective-permute-start(bf16[256,1536]{1,0:T(8,128)(2,1)} %fusion.18), channel_id=1, source_target_pairs={{0,16},{16,0},{8,24},{24,8},{1,17},{17,1},{9,25},{25,9},{2,18},{18... | collective-permute-start | bytes 2359304 | tf_op jit(solution)/shard_map/ppermute | solution.py:686
  (186 other events, 2242.6 us)
Sparse Core Ops, SparseCore 0:
  11.5 34.7 all-gather.13
  48.4 33.1 all-gather.15
  143.6 60.8 all-gather.7
  229.0 64.7 all-gather.9
  341.6 44.2 reduce-scatter.2
  539.5 47.5 reduce-scatter.4
  703.2 35.2 all-gather.11

commit v8 on v7

--- a/solution.py
+++ b/solution.py
@@ -886,8 +886,9 @@
     digits = low(jnp.stack([positions // 64, positions % 64], axis=1))
     digits = jnp.pad(digits, ((0, 0), (0, HD - 2)))
     token_send = jnp.concatenate([flat_low, digits], axis=1)
-    token_cross = swap_cross(token_send)
-    dy_over = swap_blk(dy_low, team)
+    picked_a, picked_b = pick_columns(ids, w_gate, w_up, blk_count)
+    token_cross = after(swap_cross(token_send), (picked_a, strip_ring))
+    dy_over = swap_blk(after(dy_low, token_cross), team)
     dy_cross = swap_cross(after(dy_low, token_cross))
 
     def place(values, other, done, bit, lead=0):
@@ -907,20 +908,15 @@
 
     out_local = low(lax.dynamic_slice_in_dim(w_out, strip_q * grp, strip_q, 1))
     out_ring = gather_ring(after(out_local, strip_ring))
-    picked_a, picked_b = pick_columns(ids, w_gate, w_up, blk_count)
     got_a = swap_blk(picked_a[1], team)
     down_here = low(lax.dynamic_slice_in_dim(w_down, quarter * grp, quarter, 0))
     down_got = swap_blk(after(down_here, strip_ring), bits[0])
-    pair_a = team_pair(picked_a[0], got_a)
     token_core = swap_core(jnp.stack([token_send, token_cross]))
-    token_core = after(token_core, (pair_a, dy_cross, dy_over))
     freqs = ROPE_BASE ** (-2.0 * jnp.arange(HD // 2, dtype=jnp.float32) / HD)
     freqs = jnp.concatenate([freqs, freqs])[None]
     mixed_own, mixed_core, mixed_far, near_one, strip, vector = mix(
         ids, token_send, token_cross, token_core, strip_ring, freqs, blk_count, weight_rows, small_count
     )
-    dy_first = swap_blk(after(dy_cross, mixed_own)[:half], team)
-    dy_second = swap_cross(after(dy_over, mixed_own)[half:])
     vector = vector[0]
     gain_one = vector[:D]
     gain_two = vector[D : 2 * D]
@@ -938,8 +934,6 @@
     query, packed_kv = pack(ids, mixed_own, mixed_cross, mixed_core)
     key_value = packed_kv.reshape(rows_here, block_len, 2 * KVD)
     kv_all = gather_ring(key_value)
-    dy_chip = jnp.concatenate([dy_low, dy_cross, dy_over, dy_first, dy_second])
-    dy_team = jnp.concatenate([dy_chip, swap_core(dy_chip)])
 
     teams = [
         [g * blk_count + (i | t) for g in range(4) for t in (0, team)]
@@ -964,19 +958,21 @@
             done = done + [bit]
         return values
 
-    pair_a_got = swap_blk(after(pair_a, mixed_own), bits[0])
-    down_here = place(down_here, after(down_got, mixed_own), [], bits[0])
-    down_here = lows_of(down_here, [bits[0]]).reshape(2 * blk_count // 4, quarter, D)
     got_b = swap_blk(after(picked_b[1], mixed_own), team)
-    pair_a_got, got_b = after((pair_a_got, got_b), kv_all)
-    kv_all = after(kv_all, (pair_a_got, got_b, down_here))
+    down_got, dy_cross, dy_over = after((down_got, dy_cross, dy_over), packed_kv)
+    pair_a = team_pair(picked_a[0], after(got_a, packed_kv))
+    kv_all = after(kv_all, (got_b, down_got, dy_cross, dy_over))
+    pair_a = after(pair_a, kv_all)
+    pair_a_got = swap_blk(pair_a, bits[0])
+    down_here = place(down_here, down_got, [], bits[0])
+    dy_first = swap_blk(dy_cross[:half], team)
+    dy_second = swap_cross(dy_over[half:])
+    dy_chip = jnp.concatenate([dy_low, dy_cross, dy_over, dy_first, dy_second])
+    dy_team = jnp.concatenate([dy_chip, swap_core(dy_chip)])
     pair_a = place(pair_a, pair_a_got, [team], bits[0], 1)
     gate_up_a = lows_of(pair_a, [bits[0], team], 1).reshape(2, D, -1)
     pair_b = team_pair(picked_b[0], got_b)
-    pair_b_got = swap_blk(pair_b, bits[0])
-    down_a = down_here[:, :size_first].reshape(widths[0], D)
-    down_b = down_here[:, size_first:].reshape(widths[1], D)
-
+    pair_b_got = swap_blk(after(pair_b, pair_a_got), bits[0])
     out_ring = after(out_ring, packed_kv)
     out_strip = jnp.concatenate([out_ring[ring.index(b)] for b in range(blk_count)])
     out_cross = swap_cross(out_strip)
@@ -984,10 +980,15 @@
     out_full = jnp.concatenate(by_place([out_strip, out_core[0], out_cross, out_core[1]]), axis=1)
 
     att_in, lse = attend(attend_ids, query, kv_all, seg_key, seg_query, block_len)
+    down_here = lows_of(down_here, [bits[0]], 0, att_in).reshape(2 * blk_count // 4, quarter, D)
+    down_a = down_here[:, :size_first].reshape(widths[0], D)
+    down_b = down_here[:, size_first:].reshape(widths[1], D)
+
 
     flat = wide(flat_low)
     resid = flat + jnp.dot(att_in, out_full, preferred_element_type=jnp.float32)
     h_two = low(norm_apply(resid, gain_two))
+    h_two = after(h_two, (pair_a_got, down_here))
     h_team = lax.all_gather(h_two, ("grp", "blk"), axis=0, tiled=True, axis_index_groups=teams)
     pair_b_got = after(pair_b_got, (h_two, gate_up_a))
     pair_b = place(pair_b, pair_b_got, [team], bits[0], 1)
@@ -1114,6 +1115,7 @@
     query_grad = low(left_product(near_one, near_dq)).reshape(block_shape)
     steps_query = part_sent(query_grad, len(bits) - 1, bits[-1])
     near_a = gather_near_stacked(columns_last(*after(third_a, d_query)))
+    second_b = part_sent(columns_mid(*after(first_b, d_query)), 1, bits[0])
     dkv = after(dkv, (query_grad, down_share_b))
     own_part, core_part, far_part, bias_kv = turn_dkv(
         ids, dkv, jnp.concatenate([cosine, cosine], axis=1), jnp.concatenate([sine, sine], axis=1)
@@ -1142,7 +1144,6 @@
     vector_rows = -(-small_count // HD)
     kv_grad = kv_grad.reshape((2,) * len(bits) + kv_grad.shape[1:])
     steps_kv = part_sent(kv_grad, len(bits) - 1, bits[-1])
-    second_b = part_sent(columns_mid(*after(first_b, d_query)), 1, bits[0])
     share_down = after(jnp.concatenate([down_share_a, down_share_b]), dkv)
     grad_down = lax.all_gather(share_down, "grp", axis=0, tiled=True)
     for i in range(len(bits) - 2, -1, -1):
@@ -1150,10 +1151,10 @@
         kv_sum = part_sum(*steps_kv)
         kv_grad = kv_sum
         steps_kv = part_sent(kv_sum, i, bits[i])
-    share_kv_all = wide(steps_kv[0]) + wide(after(steps_kv[1], near_a))
+    sum_b, third_b = columns_third(*after(second_b, kv_grad))
+    share_kv_all = wide(steps_kv[0]) + wide(after(steps_kv[1], (near_a, third_b[1])))
     share_kv = low(share_kv_all[:weight_rows])
     vector_part = share_kv_all[weight_rows : weight_rows + vector_rows]
-    sum_b, third_b = columns_third(*after(second_b, kv_grad))
     share_query = part_sum(*after(steps_query, kv_grad))
     near_att = swap_core(jnp.stack([att_in, near_att_cross]))
     near_att = jnp.concatenate([att_in, near_att[0], near_att_cross, near_att[1]])
@@ -1164,9 +1165,9 @@
     for i in range(len(bits) - 2, -1, -1):
         anchor = anchors[min(len(bits) - 2 - i, 1)]
         steps_out = part_sent(part_sum(*after(steps_out, anchor)), i, bits[i])
-    share_out = part_sum(*after(steps_out, own_part))
-
-    own_b = columns_last(*after(third_b, share_kv_all))
+    share_out = part_sum(*after(steps_out, kv_grad))
+
+    own_b = columns_last(*third_b)
     cross_b = swap_cross(own_b)
     near_b = jnp.stack([own_b, cross_b])
     near_b = jnp.concatenate([near_b, swap_core(near_b)])
@@ -1221,8 +1222,7 @@
         small_params, factor * share_vector, first_small, second_small, RATE_VECTOR, 0.0
     )
 
-    out_far = after(out_far, new_down)
-    out_near = after(scatter_near(out_chip, *out_far), (new_gate, new_up))
+    out_near = after(scatter_near(out_chip, *after(out_far, factor)), (new_gate, new_up))
     out_tokens = low(resid + wide(out_chip[:token_count]) + wide(out_near[0]) + wide(out_near[1]))
     return (
         out_tokens.reshape(rows_here, block_len, D),

time: 870 us -> 823 us (0.946)
  starting transfers between devices: 91.7 us -> 60.9 us
  waiting for transfers between devices: 343 us -> 318 us
    ppermute x34, starting transfers between devices: 63.1 us -> 39.3 us  [swap_blk(): return lax.ppermute(values, 'blk', [(i, i ^ bit) for i in range(count)])]
    ppermute x34, waiting for transfers between devices: 276 us -> 255 us  [swap_blk(): return lax.ppermute(values, 'blk', [(i, i ^ bit) for i in range(count)])]
    ppermute x20, waiting for transfers between devices: 65.1 us -> 49.1 us  [swap_cross(): return lax.ppermute(values, 'grp', CROSS)]
    all_gather x3, waiting for transfers between devices: 0.45 us -> 12.2 us  [gather_ring(): lax.all_gather(values, ('grp', 'blk'), axis=0, axis_index_groups=ring_gro...]
    unnamed x283 -> x277, local copies, waits for them, and re-layouts: 42.9 us -> 44.9 us
  transfers between devices with their start and end apart: 78 -> 78, of which waited for: 29 -> 32; matrix products, arithmetic and copies ran while one was open for 21% -> 22% of each run, Pallas kernels for 18% -> 19%
where the time goes in v8:
time: 823 us; the launch traced here: 815 us
  waiting for transfers between devices  318 us (39%)
  Pallas kernels  181 us (22%)
  other arithmetic  129 us (16%)
  local copies, waits for them, and re-layouts  96.5 us (12%)
  starting transfers between devices  60.9 us (7%)
  between operations  22 us (3%)
    ppermute x34, waiting for transfers between devices, swap_blk(): return lax.ppermute(values, 'blk', [(i, i ^ bit) for i in range(count)])  255 us
    pallas_call x2, Pallas kernels, middle(): pl.pallas_call(functools.partial(middle_body, prev is not None), grid_spe...  60.7 us
    ppermute x20, waiting for transfers between devices, swap_cross(): return lax.ppermute(values, 'grp', CROSS)  49.1 us
    unnamed x277, local copies, waits for them, and re-layouts  44.9 us
    ppermute x34, starting transfers between devices, swap_blk(): return lax.ppermute(values, 'blk', [(i, i ^ bit) for i in range(count)])  39.3 us
    pallas_call x2, Pallas kernels, adam_columns(): pl.pallas_call(functools.partial(adam_body, blk_count, rate, decay), grid...  35.1 us
    convert_element_type x21, other arithmetic, low(): return values.astype(jnp.bfloat16)  26.8 us
    pallas_call x2, Pallas kernels, two_grads(): pl.pallas_call(two_grads_body, grid=(D // step,), in_specs=[pl.BlockSpec(...  23.4 us
  transfers between devices with their start and end apart: 78, of which 32 were waited for; matrix products, arithmetic and copies ran while one was open for 22% of the time, Pallas kernels for 19%

profile of v8, /device:TPU:0, one launch (start us, length us, event | category | flops | bytes accessed | tf_op | source)
XLA Modules:
  0.0 814.9 jit_solution(16593373194357033073)
XLA Ops:
  23.8 10.6 %collective-permute-done.cross_ref.near_x_ref = bf16[256,1664]{1,0:T(8,128)(2,1)S(1)} collective-permute-done((bf16[256,1664]{1,0:T(8,128)(2,1)S(1)}, bf16[256,1664]{1,0:T(8,128)(2,1)S(1)}, u32[]{:S(2)}, u32[]{:S(2)}) %collective-permute-start) | collective-permute-done | bytes 852000 | tf_op jit(solution)/shard_map/ppermute | solution.py:686
  34.4 11.9 %all-gather.14.cloned.1.call-done = bf16[1664,512]{1,0:T(8,128)(2,1)} async-done(((bf16[208,512]{1,0:T(8,128)(2,1)}), bf16[1664,512]{1,0:T(8,128)(2,1)}) %all-gather.14.cloned.1.call-update) | async-done | bytes 1703952 | tf_op jit(solution)/shard_map/all_gather | solution.py:808
  63.7 9.4 %collective-permute-done.2.cross_ref = bf16[2,256,512]{2,1,0:T(8,128)(2,1)S(1)} collective-permute-done((bf16[2,256,512]{2,1,0:T(8,128)(2,1)S(1)}, bf16[2,256,512]{2,1,0:T(8,128)(2,1)S(1)}, u32[]{:S(2)}, u32[]{:S(2)}) %collective-permute-start.2) | collective-permute-done | bytes 524320 | tf_op jit(solution)/shard_map/ppermute | solution.py:686
  97.5 30.0 %collective-permute-done.7 = bf16[256,1536]{1,0:T(8,128)(2,1)} collective-permute-done((bf16[256,1536]{1,0:T(8,128)(2,1)S(1)}, bf16[256,1536]{1,0:T(8,128)(2,1)}, u32[]{:S(2)}, u32[]{:S(2)}) %collective-permute-start.7) | collective-permute-done | bytes 786464 | tf_op jit(solution)/shard_map/ppermute | solution.py:695
  134.7 11.2 %collective-permute-done.4 = bf16[2,192,608]{2,1,0:T(8,128)(2,1)S(1)} collective-permute-done((bf16[2,192,608]{2,1,0:T(8,128)(2,1)}, bf16[2,192,608]{2,1,0:T(8,128)(2,1)S(1)}, u32[]{:S(2)}, u32[]{:S(2)}) %collective-permute-start.4) | collective-permute-done | bytes 466976 | tf_op jit(solution)/shard_map/ppermute | solution.py:695
  158.2 17.1 %collective-permute-done.12 = bf16[2,280,1536]{2,1,0:T(8,128)(2,1)} collective-permute-done((bf16[2,280,1536]{2,1,0:T(8,128)(2,1)}, bf16[2,280,1536]{2,1,0:T(8,128)(2,1)}, u32[]{:S(2)}, u32[]{:S(2)}) %collective-permute-start.12) | collective-permute-done | bytes 1720352 | tf_op jit(solution)/shard_map/ppermute | solution.py:695
  199.3 9.3 %collective-permute-done.15 = bf16[128,1536]{1,0:T(8,128)(2,1)S(1)} collective-permute-done((bf16[128,1536]{1,0:T(8,128)(2,1)S(1)}, bf16[128,1536]{1,0:T(8,128)(2,1)S(1)}, u32[]{:S(2)}, u32[]{:S(2)}) %collective-permute-start.15) | collective-permute-done | bytes 393248 | tf_op jit(solution)/shard_map/ppermute | solution.py:695
  222.4 27.8 %collective-permute-done.13 = bf16[2,2,2,192,512]{4,3,0,2,1:T(8,128)(2,1)} collective-permute-done((bf16[2,2,2,192,512]{4,3,0,2,1:T(8,128)(2,1)}, bf16[2,2,2,192,512]{4,3,0,2,1:T(8,128)(2,1)}, u32[]{:S(2)}, u32[]{:S(2)}) %collective-permute-start.13) | collective-permute-done | bytes 1572896 | tf_op jit(solution)/shard_map/ppermute | solution.py:695
  266.0 23.3 %middle.2 = (bf16[2048,512]{1,0:T(8,128)(2,1)S(1)}, bf16[2048,512]{1,0:T(8,128)(2,1)S(1)}, bf16[2048,512]{1,0:T(8,128)(2,1)}, bf16[2048,1536]{1,0:T(8,128)(2,1)}) custom-call(s32[8]{0:T(128)S(1)} %stack.292.order, bf16[2048,1536]{1,0:T(8,128)(2,1)} %all-gather.10.cloned.1.call-done.h_ref, bf16[2048,1536]{1,0:T(8,128)(2,1)} %constant_dynamic-update-slice_fusion.12.dy_ref, ...), custom_call_target="tpu_custom_call" | custom-call | flops 1000 | bytes 1000 | tf_op jit(solution)/shard_map/middle/pallas_call | solution.py:370
  303.4 10.1 %two_grads.2 = bf16[2,1536,512]{2,1,0:T(8,128)(2,1)} custom-call(bf16[2048,1536]{1,0:T(8,128)(2,1)} %all-gather.10.cloned.1.call-done.h_ref, bf16[2048,512]{1,0:T(8,128)(2,1)S(1)} %copy-done.22, bf16[2048,512]{1,0:T(8,128)(2,1)S(1)} %copy-done.23), custom_call_target="tpu_custom_call" | custom-call | flops 1000 | bytes 1000 | tf_op jit(solution)/shard_map/two_grads/pallas_call | solution.py:403
  318.3 39.6 %collective-permute-done.18 = bf16[2,2,2,192,608]{4,3,0,2,1:T(8,128)(2,1)} collective-permute-done((bf16[2,2,2,192,608]{4,3,0,2,1:T(8,128)(2,1)}, bf16[2,2,2,192,608]{4,3,0,2,1:T(8,128)(2,1)}, u32[]{:S(2)}, u32[]{:S(2)}) %collective-permute-start.18) | collective-permute-done | bytes 1867808 | tf_op jit(solution)/shard_map/ppermute | solution.py:695
  362.9 37.4 %middle.3 = (bf16[2048,608]{1,0:T(8,128)(2,1)S(1)}, bf16[2048,608]{1,0:T(8,128)(2,1)}, bf16[2048,608]{1,0:T(8,128)(2,1)}, bf16[2048,1536]{1,0:T(8,128)(2,1)}) custom-call(s32[8]{0:T(128)S(1)} %stack.292.order, bf16[2048,1536]{1,0:T(8,128)(2,1)} %all-gather.10.cloned.1.call-done.h_ref, bf16[2048,1536]{1,0:T(8,128)(2,1)} %constant_dynamic-update-slice_fusion.12.dy_ref, ...), custom_call_target="tpu_custom_call" | custom-call | flops 1000 | bytes 1000 | tf_op jit(solution)/shard_map/middle/pallas_call | solution.py:370
  426.5 13.3 %two_grads.3 = bf16[2,1536,608]{2,1,0:T(8,128)(2,1)} custom-call(bf16[2048,1536]{1,0:T(8,128)(2,1)} %all-gather.10.cloned.1.call-done.h_ref, bf16[2048,608]{1,0:T(8,128)(2,1)S(1)} %copy-done.19, bf16[2048,608]{1,0:T(8,128)(2,1)S(1)} %copy-done.20), custom_call_target="tpu_custom_call" | custom-call | flops 1000 | bytes 1000 | tf_op jit(solution)/shard_map/two_grads/pallas_call | solution.py:403
  452.5 11.5 %down.1 = bf16[2048,1536]{1,0:T(8,128)(2,1)} custom-call(bf16[2048,512]{1,0:T(8,128)(2,1)S(1)} %copy-done.6, bf16[2048,608]{1,0:T(8,128)(2,1)} %copy-done.1, bf16[512,1536]{1,0:T(8,128)(2,1)S(1)} %bitcast.413, bf16[608,1536]{1,0:T(8,128)(2,1)S(1)} %bitcast.411), custom_call_target="tpu_custom_call" | custom-call | flops 1000 | bytes 1000 | tf_op jit(solution)/shard_map/down/pallas_call | solution.py:443
  494.7 35.4 %collective-permute-done.38 = bf16[2,2,192,512]{3,2,1,0:T(8,128)(2,1)} collective-permute-done((bf16[2,2,192,512]{3,2,1,0:T(8,128)(2,1)}, bf16[2,2,192,512]{3,2,1,0:T(8,128)(2,1)}, u32[]{:S(2)}, u32[]{:S(2)}) %collective-permute-start.38) | collective-permute-done | bytes 786464 | tf_op jit(solution)/shard_map/ppermute | solution.py:695
  534.2 21.3 %collective-permute-done.39 = bf16[2,192,512]{2,1,0:T(8,128)(2,1)S(1)} collective-permute-done((bf16[2,192,512]{2,1,0:T(8,128)(2,1)S(1)}, bf16[2,192,512]{2,1,0:T(8,128)(2,1)S(1)}, u32[]{:S(2)}, u32[]{:S(2)}) %collective-permute-start.39) | collective-permute-done | bytes 393248 | tf_op jit(solution)/shard_map/ppermute | solution.py:695
  567.9 9.0 %collective-permute-done.40 = bf16[2,2,192,512]{3,2,1,0:T(8,128)(2,1)} collective-permute-done((bf16[2,2,192,512]{3,2,1,0:T(8,128)(2,1)}, bf16[2,2,192,512]{3,2,1,0:T(8,128)(2,1)}, u32[]{:S(2)}, u32[]{:S(2)}) %collective-permute-start.40) | collective-permute-done | bytes 786464 | tf_op jit(solution)/shard_map/ppermute | solution.py:686
  609.2 8.4 %kv_grad.1 = (bf16[8,208,128]{2,1,0:T(8,128)(2,1)S(1)}, bf16[512,1536]{1,0:T(8,128)(2,1)S(1)}, bf16[512,1536]{1,0:T(8,128)(2,1)}) custom-call(bf16[256,128]{1,0:T(8,128)(2,1)S(1)} %get-tuple-element.182.self_ref, bf16[2,256,128]{2,1,0:T(8,128)(2,1)S(1)} %collective-permute-done.31.cross_ref, bf16[2,256,128]{2,1,0:T(8,128)(2,1)S(1)} %collective-permute-done.32.core_ref, ...), custom_call_target="tpu_custom_call" | custom-call | flops 1000 | bytes 1000 | tf_op jit(solution)/shard_map/kv_grad/pallas_call | solution.py:653
  628.0 11.8 %collective-permute-done.34 = bf16[2,208,128]{2,1,0:T(8,128)(2,1)S(1)} collective-permute-done((bf16[2,208,128]{2,1,0:T(8,128)(2,1)S(1)}, bf16[2,208,128]{2,1,0:T(8,128)(2,1)S(1)}, u32[]{:S(2)}, u32[]{:S(2)}) %collective-permute-start.34) | collective-permute-done | bytes 106528 | tf_op jit(solution)/shard_map/ppermute | solution.py:695
  664.5 15.2 %collective-permute-done.37 = bf16[208,128]{1,0:T(8,128)(2,1)S(1)} collective-permute-done((bf16[208,128]{1,0:T(8,128)(2,1)S(1)}, bf16[208,128]{1,0:T(8,128)(2,1)S(1)}, u32[]{:S(2)}, u32[]{:S(2)}) %collective-permute-start.37) | collective-permute-done | bytes 53280 | tf_op jit(solution)/shard_map/ppermute | solution.py:695
  715.4 16.1 %collective-permute-done.59 = bf16[2,2,192,608]{3,2,1,0:T(8,128)(2,1)} collective-permute-done((bf16[2,2,192,608]{3,2,1,0:T(8,128)(2,1)}, bf16[2,2,192,608]{3,2,1,0:T(8,128)(2,1)}, u32[]{:S(2)}, u32[]{:S(2)}) %collective-permute-start.59) | collective-permute-done | bytes 933920 | tf_op jit(solution)/shard_map/ppermute | solution.py:686
  747.7 17.5 %adam_columns.2 = (f32[192,8960]{1,0:T(8,128)}, f32[192,8960]{1,0:T(8,128)}, f32[192,8960]{1,0:T(8,128)}) custom-call(s32[2]{0:T(128)S(1)} %copy-done.42, f32[1]{0:T(128)} %bitcast.131.factor_ref, bf16[4,2,2,192,512]{4,3,2,1,0:T(8,128)(2,1)S(1)} %pad_maximum_fusion.5.first_ref, bf16[4,2,2,192,608]{4,3,2,1,0:T(8,128)(2,1)} %pad_maximum_fusion.2.second_ref, ...), custom_call_target="tpu_custom_call" | custom-call | flops 1000 | bytes 1000 | tf_op jit(solution)/shard_map/adam_columns/pallas_call | solution.py:155
  765.2 17.5 %adam_columns.3 = (f32[192,8960]{1,0:T(8,128)}, f32[192,8960]{1,0:T(8,128)}, f32[192,8960]{1,0:T(8,128)}) custom-call(s32[2]{0:T(128)S(1)} %copy-done.42, f32[1]{0:T(128)} %bitcast.131.factor_ref, bf16[4,2,2,192,512]{4,3,2,1,0:T(8,128)(2,1)S(1)} %pad_maximum_fusion.5.first_ref, bf16[4,2,2,192,608]{4,3,2,1,0:T(8,128)(2,1)} %pad_maximum_fusion.2.second_ref, ...), custom_call_target="tpu_custom_call" | custom-call | flops 1000 | bytes 1000 | tf_op jit(solution)/shard_map/adam_columns/pallas_call | solution.py:155
  789.8 16.7 %multiply_subtract_fusion = (f32[1120,1536]{1,0:T(8,128)}, f32[1120,1536]{1,0:T(8,128)}, f32[1120,1536]{1,0:T(8,128)}) fusion(f32[1120,1536]{1,0:T(8,128)} %param.30, bf16[1120,1536]{1,0:T(8,128)(2,1)} %all-gather.12.cloned.1.call-done, f32[]{:T(128)} %min.3, f32[1120,1536]{1,0:T(8,128)} %param.42, f32[1120,1536]{1,0:T(8,128)} %param.36), kind=kLoop, calls=%fused_computation.2 | loop fusion | flops 29245440 | bytes 44728324 | tf_op jit(solution)/shard_map/sub | solution.py:67
  (616 shorter events, 361.3 us)
Async XLA Ops:
  11.4 71.8 %all-gather.16.cloned.1.call-start = ((), (), s32[]{:S(2)}) async-start(), calls=%async_computation.8 | async-start | bytes 1327104 | tf_op jit(solution)/shard_map/all_gather | solution.py:808
  49.3 96.8 %all-gather.8.cloned.1.call-start = ((), (), s32[]{:S(2)}) async-start(), calls=%async_computation.2 | async-start | bytes 2359296 | tf_op jit(solution)/shard_map/all_gather | solution.py:808
  61.4 89.7 %collective-permute-start.10 = (bf16[2,192,512]{2,1,0:T(8,128)(2,1)}, bf16[2,192,512]{2,1,0:T(8,128)(2,1)}, u32[]{:S(2)}, u32[]{:S(2)}) collective-permute-start(bf16[2,192,512]{2,1,0:T(8,128)(2,1)} %slice_bitcast_fusion.5), channel_id=1, source_target_pairs={{0,2},{1,3},{2,0},{3,1},{4,6},{5,7},{6,4},{7,5},{8,10},{9,11},{10,... | collective-permute-start | bytes 1179656 | tf_op jit(solution)/shard_map/ppermute | solution.py:695
  77.4 50.1 %collective-permute-start.7 = (bf16[256,1536]{1,0:T(8,128)(2,1)S(1)}, bf16[256,1536]{1,0:T(8,128)(2,1)}, u32[]{:S(2)}, u32[]{:S(2)}) collective-permute-start(bf16[256,1536]{1,0:T(8,128)(2,1)S(1)} %bitcast.433), channel_id=1, source_target_pairs={{0,2},{1,3},{2,0},{3,1},{4,6},{5,7},{6,4},{7,5},{8,10},{9,11},{10,... | collective-permute-start | bytes 2359304 | tf_op jit(solution)/shard_map/ppermute | solution.py:695
  79.9 51.3 %collective-permute-start.5 = (bf16[280,1536]{1,0:T(8,128)(2,1)}, bf16[280,1536]{1,0:T(8,128)(2,1)}, u32[]{:S(2)}, u32[]{:S(2)}) collective-permute-start(bf16[280,1536]{1,0:T(8,128)(2,1)} %dynamic-slice_convert_fusion), channel_id=1, source_target_pairs={{0,4},{1,5},{2,6},{3,7},{4,0},{5,1},{6,2},{7,3},{8,12},{9,13},{10,... | collective-permute-start | bytes 2580488 | tf_op jit(solution)/shard_map/ppermute | solution.py:695
  82.8 183.2 %all-gather.10.cloned.1.call-start = ((), (), s32[]{:S(2)}) async-start(), calls=%async_computation.3 | async-start | bytes 7077888 | tf_op jit(solution)/shard_map/all_gather | solution.py:992
  95.9 50.2 %collective-permute-start.8 = (bf16[1536,384]{1,0:T(8,128)(2,1)}, bf16[1536,384]{1,0:T(8,128)(2,1)}, u32[]{:S(2)}, u32[]{:S(2)}) collective-permute-start(bf16[1536,384]{1,0:T(8,128)(2,1)} %bitcast_dynamic-update-slice_fusion), channel_id=1, source_target_pairs={{0,16},{16,0},{8,24},{24,8},{1,17},{17,1},{9,25},{25,9},{2,18},{18... | collective-permute-start | bytes 3538952 | tf_op jit(solution)/shard_map/ppermute | solution.py:686
  190.2 212.4 %reduce-scatter.3.cloned.1.call-start = ((), (), s32[]{:S(2)}) async-start(), calls=%async_computation.4 | async-start | bytes 1966080 | tf_op jit(solution)/shard_map/reduce_scatter | solution.py:999
  298.7 296.7 %reduce-scatter.5.cloned.1.call-start = ((), (), s32[]{:S(2)}) async-start(), calls=%async_computation.5 | async-start | bytes 2359296 | tf_op jit(solution)/shard_map/reduce_scatter | solution.py:1100
  299.2 58.7 %collective-permute-start.18 = (bf16[2,2,2,192,608]{4,3,0,2,1:T(8,128)(2,1)}, bf16[2,2,2,192,608]{4,3,0,2,1:T(8,128)(2,1)}, u32[]{:S(2)}, u32[]{:S(2)}) collective-permute-start(bf16[2,2,2,192,608]{4,3,0,2,1:T(8,128)(2,1)} %pad_maximum_fusion.7), channel_id=1, source_target_pairs={{0,1},{1,0},{2,3},{3,2},{4,5},{5,4},{6,7},{7,6},{8,9},{9,8},{10,11... | collective-permute-start | bytes 5603336 | tf_op jit(solution)/shard_map/ppermute | solution.py:695
  317.0 85.7 %collective-permute-start.19 = (bf16[2,2,2,192,512]{4,3,2,1,0:T(8,128)(2,1)S(1)}, bf16[2,2,2,192,512]{4,3,2,1,0:T(8,128)(2,1)}, u32[]{:S(2)}, u32[]{:S(2)}) collective-permute-start(bf16[2,2,2,192,512]{4,3,2,1,0:T(8,128)(2,1)S(1)} %get-tuple-element.282), channel_id=1, source_target_pairs={{0,1},{1,0},{2,3},{3,2},{4,5},{5,4},{6,7},{7,6},{8,9},{9,8},{10,11... | collective-permute-start | bytes 4718600 | tf_op jit(solution)/shard_map/ppermute | solution.py:695
  318.2 83.6 %collective-permute-start.20 = (bf16[256,1536]{1,0:T(8,128)(2,1)S(1)}, bf16[256,1536]{1,0:T(8,128)(2,1)S(1)}, u32[]{:S(2)}, u32[]{:S(2)}) collective-permute-start(bf16[256,1536]{1,0:T(8,128)(2,1)S(1)} %copy-done.15), channel_id=1, source_target_pairs={{0,16},{16,0},{8,24},{24,8},{1,17},{17,1},{9,25},{25,9},{2,18},{18... | collective-permute-start | bytes 2359304 | tf_op jit(solution)/shard_map/ppermute | solution.py:686
  425.2 61.9 %collective-permute-start.29 = (bf16[2,152,1536]{2,1,0:T(8,128)(2,1)}, bf16[2,152,1536]{2,1,0:T(8,128)(2,1)}, u32[]{:S(2)}, u32[]{:S(2)}) collective-permute-start(bf16[2,152,1536]{2,1,0:T(8,128)(2,1)} %get-tuple-element.295), channel_id=1, source_target_pairs={{0,1},{1,0},{2,3},{3,2},{4,5},{5,4},{6,7},{7,6},{8,9},{9,8},{10,11... | collective-permute-start | bytes 2801672 | tf_op jit(solution)/shard_map/ppermute | solution.py:695
  451.6 107.6 %collective-permute-start.42 = (bf16[2,2,2,192,608]{4,3,2,1,0:T(8,128)(2,1)}, bf16[2,2,2,192,608]{4,3,2,1,0:T(8,128)(2,1)}, u32[]{:S(2)}, u32[]{:S(2)}) collective-permute-start(bf16[2,2,2,192,608]{4,3,2,1,0:T(8,128)(2,1)} %get-tuple-element.269), channel_id=1, source_target_pairs={{0,1},{1,0},{2,3},{3,2},{4,5},{5,4},{6,7},{7,6},{8,9},{9,8},{10,11... | collective-permute-start | bytes 5603336 | tf_op jit(solution)/shard_map/ppermute | solution.py:695
  467.9 172.0 %collective-permute-start.24 = (bf16[1024,1536]{1,0:T(8,128)(2,1)}, bf16[1024,1536]{1,0:T(8,128)(2,1)}, u32[]{:S(2)}, u32[]{:S(2)}) collective-permute-start(bf16[1024,1536]{1,0:T(8,128)(2,1)} %slice.381), channel_id=1, source_target_pairs={{0,8},{8,0},{16,24},{24,16},{1,9},{9,1},{17,25},{25,17},{2,10},{10... | collective-permute-start | bytes 9437192 | tf_op jit(solution)/shard_map/ppermute | solution.py:682
  470.8 59.3 %collective-permute-start.38 = (bf16[2,2,192,512]{3,2,1,0:T(8,128)(2,1)}, bf16[2,2,192,512]{3,2,1,0:T(8,128)(2,1)}, u32[]{:S(2)}, u32[]{:S(2)}) collective-permute-start(bf16[2,2,192,512]{3,2,1,0:T(8,128)(2,1)} %get-tuple-element.301), channel_id=1, source_target_pairs={{0,4},{1,5},{2,6},{3,7},{4,0},{5,1},{6,2},{7,3},{8,12},{9,13},{10,... | collective-permute-start | bytes 2359304 | tf_op jit(solution)/shard_map/ppermute | solution.py:695
  485.3 304.5 %all-gather.12.cloned.1.call-start = ((), (), s32[]{:S(2)}) async-start(), calls=%async_computation.6 | async-start | bytes 4300800 | tf_op jit(solution)/shard_map/all_gather | solution.py:1148
  488.7 69.0 %collective-permute-start.30 = (bf16[152,1536]{1,0:T(8,128)(2,1)S(1)}, bf16[152,1536]{1,0:T(8,128)(2,1)S(1)}, u32[]{:S(2)}, u32[]{:S(2)}) collective-permute-start(bf16[152,1536]{1,0:T(8,128)(2,1)S(1)} %get-tuple-element.317), channel_id=1, source_target_pairs={{0,4},{1,5},{2,6},{3,7},{4,0},{5,1},{6,2},{7,3},{8,12},{9,13},{10,... | collective-permute-start | bytes 1400840 | tf_op jit(solution)/shard_map/ppermute | solution.py:695
  585.8 60.0 %collective-permute-start.43 = (bf16[2,2,192,608]{3,2,1,0:T(8,128)(2,1)}, bf16[2,2,192,608]{3,2,1,0:T(8,128)(2,1)}, u32[]{:S(2)}, u32[]{:S(2)}) collective-permute-start(bf16[2,2,192,608]{3,2,1,0:T(8,128)(2,1)} %get-tuple-element.291), channel_id=1, source_target_pairs={{0,4},{1,5},{2,6},{3,7},{4,0},{5,1},{6,2},{7,3},{8,12},{9,13},{10,... | collective-permute-start | bytes 2801672 | tf_op jit(solution)/shard_map/ppermute | solution.py:695
  593.7 55.1 %collective-permute-start.53 = (bf16[192,384]{1,0:T(8,128)(2,1)}, bf16[192,384]{1,0:T(8,128)(2,1)}, u32[]{:S(2)}, u32[]{:S(2)}) collective-permute-start(bf16[192,384]{1,0:T(8,128)(2,1)} %get-tuple-element.363), channel_id=1, source_target_pairs={{0,4},{1,5},{2,6},{3,7},{4,0},{5,1},{6,2},{7,3},{8,12},{9,13},{10,... | collective-permute-start | bytes 442376 | tf_op jit(solution)/shard_map/ppermute | solution.py:695
  619.4 91.8 %collective-permute-start.63 = (bf16[512,1536]{1,0:T(8,128)(2,1)}, bf16[512,1536]{1,0:T(8,128)(2,1)}, u32[]{:S(2)}, u32[]{:S(2)}) collective-permute-start(bf16[512,1536]{1,0:T(8,128)(2,1)} %get-tuple-element.222), channel_id=1, source_target_pairs={{0,8},{8,0},{16,24},{24,16},{1,9},{9,1},{17,25},{25,17},{2,10},{10... | collective-permute-start | bytes 4718600 | tf_op jit(solution)/shard_map/ppermute | solution.py:682
  658.6 73.0 %collective-permute-start.35 = (bf16[128,1536]{1,0:T(8,128)(2,1)}, bf16[128,1536]{1,0:T(8,128)(2,1)}, u32[]{:S(2)}, u32[]{:S(2)}) collective-permute-start(bf16[128,1536]{1,0:T(8,128)(2,1)} %get-tuple-element.278), channel_id=1, source_target_pairs={{0,2},{1,3},{2,0},{3,1},{4,6},{5,7},{6,4},{7,5},{8,10},{9,11},{10,... | collective-permute-start | bytes 1179656 | tf_op jit(solution)/shard_map/ppermute | solution.py:695
  658.6 72.9 %collective-permute-start.36 = (bf16[128,1536]{1,0:T(8,128)(2,1)}, bf16[128,1536]{1,0:T(8,128)(2,1)}, u32[]{:S(2)}, u32[]{:S(2)}) collective-permute-start(bf16[128,1536]{1,0:T(8,128)(2,1)} %get-tuple-element.277), channel_id=1, source_target_pairs={{0,16},{16,0},{8,24},{24,8},{1,17},{17,1},{9,25},{25,9},{2,18},{18... | collective-permute-start | bytes 1179656 | tf_op jit(solution)/shard_map/ppermute | solution.py:686
  714.3 68.5 %collective-permute-start.64 = (bf16[256,1536]{1,0:T(8,128)(2,1)}, bf16[256,1536]{1,0:T(8,128)(2,1)}, u32[]{:S(2)}, u32[]{:S(2)}) collective-permute-start(bf16[256,1536]{1,0:T(8,128)(2,1)} %fusion.18), channel_id=1, source_target_pairs={{0,16},{16,0},{8,24},{24,8},{1,17},{17,1},{9,25},{25,9},{2,18},{18... | collective-permute-start | bytes 2359304 | tf_op jit(solution)/shard_map/ppermute | solution.py:686
  (183 other events, 1946.3 us)
Sparse Core Ops, SparseCore 0:
  11.5 34.7 all-gather.13
  49.4 31.7 all-gather.15
  83.3 62.7 all-gather.7
  190.4 62.8 all-gather.9
  298.8 42.7 reduce-scatter.2
  485.4 67.3 reduce-scatter.4
  604.5 29.1 all-gather.11

commit v9 on v8

--- a/solution.py
+++ b/solution.py
@@ -908,9 +908,7 @@
 
     out_local = low(lax.dynamic_slice_in_dim(w_out, strip_q * grp, strip_q, 1))
     out_ring = gather_ring(after(out_local, strip_ring))
-    got_a = swap_blk(picked_a[1], team)
     down_here = low(lax.dynamic_slice_in_dim(w_down, quarter * grp, quarter, 0))
-    down_got = swap_blk(after(down_here, strip_ring), bits[0])
     token_core = swap_core(jnp.stack([token_send, token_cross]))
     freqs = ROPE_BASE ** (-2.0 * jnp.arange(HD // 2, dtype=jnp.float32) / HD)
     freqs = jnp.concatenate([freqs, freqs])[None]
@@ -931,6 +929,8 @@
 
     mixed_cross = swap_cross(mixed_far)
     mixed_core = swap_core(jnp.stack([mixed_core, mixed_cross[1]]))
+    got_a = swap_blk(picked_a[1], team)
+    mixed_core = after(mixed_core, got_a)
     query, packed_kv = pack(ids, mixed_own, mixed_cross, mixed_core)
     key_value = packed_kv.reshape(rows_here, block_len, 2 * KVD)
     kv_all = gather_ring(key_value)
@@ -959,12 +959,11 @@
         return values
 
     got_b = swap_blk(after(picked_b[1], mixed_own), team)
-    down_got, dy_cross, dy_over = after((down_got, dy_cross, dy_over), packed_kv)
+    dy_cross, dy_over = after((dy_cross, dy_over), packed_kv)
     pair_a = team_pair(picked_a[0], after(got_a, packed_kv))
-    kv_all = after(kv_all, (got_b, down_got, dy_cross, dy_over))
+    kv_all = after(kv_all, (got_b, dy_cross, dy_over))
     pair_a = after(pair_a, kv_all)
     pair_a_got = swap_blk(pair_a, bits[0])
-    down_here = place(down_here, down_got, [], bits[0])
     dy_first = swap_blk(dy_cross[:half], team)
     dy_second = swap_cross(dy_over[half:])
     dy_chip = jnp.concatenate([dy_low, dy_cross, dy_over, dy_first, dy_second])
@@ -980,22 +979,22 @@
     out_full = jnp.concatenate(by_place([out_strip, out_core[0], out_cross, out_core[1]]), axis=1)
 
     att_in, lse = attend(attend_ids, query, kv_all, seg_key, seg_query, block_len)
-    down_here = lows_of(down_here, [bits[0]], 0, att_in).reshape(2 * blk_count // 4, quarter, D)
-    down_a = down_here[:, :size_first].reshape(widths[0], D)
-    down_b = down_here[:, size_first:].reshape(widths[1], D)
-
-
     flat = wide(flat_low)
     resid = flat + jnp.dot(att_in, out_full, preferred_element_type=jnp.float32)
     h_two = low(norm_apply(resid, gain_two))
-    h_two = after(h_two, (pair_a_got, down_here))
+    h_two = after(h_two, pair_a_got)
+    down_got = after(swap_blk(after(down_here, kv_all), bits[0]), h_two)
+    down_here = place(down_here, down_got, [], bits[0])
+    down_here = lows_of(down_here, [bits[0]]).reshape(2 * blk_count // 4, quarter, D)
+    down_a = down_here[:, :size_first].reshape(widths[0], D)
+    down_b = down_here[:, size_first:].reshape(widths[1], D)
     h_team = lax.all_gather(h_two, ("grp", "blk"), axis=0, tiled=True, axis_index_groups=teams)
     pair_b_got = after(pair_b_got, (h_two, gate_up_a))
     pair_b = place(pair_b, pair_b_got, [team], bits[0], 1)
     h_team = after(h_team, (gate_up_a, pair_b, dy_team))
     hidden_a, d_gate_a, d_up_a, part_a = middle(order, h_team, dy_team, gate_up_a, down_a)
     gate_up_b = lows_of(pair_b, [bits[0], team], 1, hidden_a).reshape(2, D, -1)
-    down_grad_a = down_grad(hidden_a, dy_team)
+    down_grad_a = down_grad(after(hidden_a, gate_up_b), dy_team)
     down_share_a = lax.psum_scatter(
         down_grad_a, "blk", scatter_dimension=0, axis_index_groups=peers, tiled=True
     )
@@ -1062,6 +1061,8 @@
     rows_b = part_sent(
         down_grad_b.reshape((2,) + low_shape + (size_second, D)), len(lows), lows[-1]
     )
+    mid_a = columns_mid(*after(first_a, d_came))
+    second_a = part_sent(mid_a, 1, bits[0])
     d_chip = chip_sum(d_htwo_part, after(d_came, down_grad_b))
     d_far = scatter_far(d_chip)
     column_grad_b = two_grads(h_team, *after((d_gate_b, d_up_b), d_chip))
@@ -1070,8 +1071,6 @@
     d_cross, d_over = scatter_near(d_chip, *d_far)
     out_part = down(*after((hidden_a, hidden_b), d_far), down_a, down_b, token_count)
     out_came = swap_core(out_part[chip_rows:])
-    mid_a = columns_mid(*after(first_a, d_far))
-    second_a = part_sent(mid_a, 1, bits[0])
     d_cross, d_over = after((d_cross, d_over), out_part)
     d_htwo = wide(d_chip[:token_count]) + wide(d_cross) + wide(d_over)
 
@@ -1105,7 +1104,7 @@
         tiled=True,
     )
     down_share_b = part_sum(*after(rows_b, d_query))
-    sum_a, third_a = columns_third(*after(second_a, d_query))
+    sum_a, third_a = columns_third(*after(second_a, d_att))
 
     def to_strips(parts):
         return jnp.concatenate(exchange_near(by_place(parts)))

time: 823 us -> 814 us (0.989)
  starting transfers between devices: 60.9 us -> 70.7 us
  local copies, waits for them, and re-layouts: 96.5 us -> 86.7 us
    ppermute x34, waiting for transfers between devices: 255 us -> 209 us  [swap_blk(): return lax.ppermute(values, 'blk', [(i, i ^ bit) for i in range(count)])]
    ppermute x20, waiting for transfers between devices: 49.1 us -> 91.3 us  [swap_cross(): return lax.ppermute(values, 'grp', CROSS)]
    unnamed x277 -> x271, local copies, waits for them, and re-layouts: 44.9 us -> 39.4 us
  transfers between devices with their start and end apart: 78 -> 78, of which waited for: 32 -> 31; matrix products, arithmetic and copies ran while one was open for 22% -> 20% of each run, Pallas kernels for 19% -> 22%
where the time goes in v9:
time: 814 us; the launch traced here: 806 us
  waiting for transfers between devices  314 us (39%)
  Pallas kernels  182 us (22%)
  other arithmetic  123 us (15%)
  local copies, waits for them, and re-layouts  86.7 us (11%)
  starting transfers between devices  70.7 us (9%)
  between operations  22.1 us (3%)
    ppermute x34, waiting for transfers between devices, swap_blk(): return lax.ppermute(values, 'blk', [(i, i ^ bit) for i in range(count)])  209 us
    ppermute x20, waiting for transfers between devices, swap_cross(): return lax.ppermute(values, 'grp', CROSS)  91.3 us
    pallas_call x2, Pallas kernels, middle(): pl.pallas_call(functools.partial(middle_body, prev is not None), grid_spe...  60.7 us
    ppermute x34, starting transfers between devices, swap_blk(): return lax.ppermute(values, 'blk', [(i, i ^ bit) for i in range(count)])  43.2 us
    unnamed x271, local copies, waits for them, and re-layouts  39.4 us
    pallas_call x2, Pallas kernels, adam_columns(): pl.pallas_call(functools.partial(adam_body, blk_count, rate, decay), grid...  35.1 us
    convert_element_type x21, other arithmetic, low(): return values.astype(jnp.bfloat16)  27 us
    ppermute x20, starting transfers between devices, swap_cross(): return lax.ppermute(values, 'grp', CROSS)  24.5 us
  transfers between devices with their start and end apart: 78, of which 31 were waited for; matrix products, arithmetic and copies ran while one was open for 20% of the time, Pallas kernels for 22%

profile of v9, /device:TPU:0, one launch (start us, length us, event | category | flops | bytes accessed | tf_op | source)
XLA Modules:
  0.0 806.0 jit_solution(147473647280637133)
XLA Ops:
  23.8 10.6 %collective-permute-done.cross_ref.near_x_ref = bf16[256,1664]{1,0:T(8,128)(2,1)S(1)} collective-permute-done((bf16[256,1664]{1,0:T(8,128)(2,1)S(1)}, bf16[256,1664]{1,0:T(8,128)(2,1)S(1)}, u32[]{:S(2)}, u32[]{:S(2)}) %collective-permute-start) | collective-permute-done | bytes 852000 | tf_op jit(solution)/shard_map/ppermute | solution.py:686
  34.4 11.9 %all-gather.14.cloned.1.call-done = bf16[1664,512]{1,0:T(8,128)(2,1)} async-done(((bf16[208,512]{1,0:T(8,128)(2,1)}), bf16[1664,512]{1,0:T(8,128)(2,1)}) %all-gather.14.cloned.1.call-update) | async-done | bytes 1703952 | tf_op jit(solution)/shard_map/all_gather | solution.py:808
  60.7 12.5 %collective-permute-done.2.cross_ref = bf16[2,256,512]{2,1,0:T(8,128)(2,1)S(1)} collective-permute-done((bf16[2,256,512]{2,1,0:T(8,128)(2,1)S(1)}, bf16[2,256,512]{2,1,0:T(8,128)(2,1)S(1)}, u32[]{:S(2)}, u32[]{:S(2)}) %collective-permute-start.2) | collective-permute-done | bytes 524320 | tf_op jit(solution)/shard_map/ppermute | solution.py:686
  74.9 10.8 %collective-permute-done.4 = bf16[2,192,512]{2,1,0:T(8,128)(2,1)S(1)} collective-permute-done((bf16[2,192,512]{2,1,0:T(8,128)(2,1)S(1)}, bf16[2,192,512]{2,1,0:T(8,128)(2,1)S(1)}, u32[]{:S(2)}, u32[]{:S(2)}) %collective-permute-start.4) | collective-permute-done | bytes 393248 | tf_op jit(solution)/shard_map/ppermute | solution.py:695
  100.6 39.2 %collective-permute-done.6 = bf16[256,1536]{1,0:T(8,128)(2,1)} collective-permute-done((bf16[256,1536]{1,0:T(8,128)(2,1)}, bf16[256,1536]{1,0:T(8,128)(2,1)}, u32[]{:S(2)}, u32[]{:S(2)}) %collective-permute-start.6) | collective-permute-done | bytes 786464 | tf_op jit(solution)/shard_map/ppermute | solution.py:686
  161.6 23.6 %collective-permute-done.10 = bf16[2,2,192,512]{3,2,0,1:T(8,128)(2,1)} collective-permute-done((bf16[2,2,192,512]{3,2,0,1:T(8,128)(2,1)S(1)}, bf16[2,2,192,512]{3,2,0,1:T(8,128)(2,1)}, u32[]{:S(2)}, u32[]{:S(2)}) %collective-permute-start.10) | collective-permute-done | bytes 786464 | tf_op jit(solution)/shard_map/ppermute | solution.py:695
  196.7 9.0 %collective-permute-done.13 = bf16[128,1536]{1,0:T(8,128)(2,1)S(1)} collective-permute-done((bf16[128,1536]{1,0:T(8,128)(2,1)S(1)}, bf16[128,1536]{1,0:T(8,128)(2,1)S(1)}, u32[]{:S(2)}, u32[]{:S(2)}) %collective-permute-start.13) | collective-permute-done | bytes 393248 | tf_op jit(solution)/shard_map/ppermute | solution.py:695
  215.9 51.1 %collective-permute-done.16 = bf16[280,1536]{1,0:T(8,128)(2,1)} collective-permute-done((bf16[280,1536]{1,0:T(8,128)(2,1)S(1)}, bf16[280,1536]{1,0:T(8,128)(2,1)}, u32[]{:S(2)}, u32[]{:S(2)}) %collective-permute-start.16) | collective-permute-done | bytes 860192 | tf_op jit(solution)/shard_map/ppermute | solution.py:695
  276.0 14.6 %collective-permute-done.12 = bf16[2,2,192,608]{3,2,0,1:T(8,128)(2,1)S(1)} collective-permute-done((bf16[2,2,192,608]{3,2,0,1:T(8,128)(2,1)S(1)}, bf16[2,2,192,608]{3,2,0,1:T(8,128)(2,1)S(1)}, u32[]{:S(2)}, u32[]{:S(2)}) %collective-permute-start.12) | collective-permute-done | bytes 933920 | tf_op jit(solution)/shard_map/ppermute | solution.py:695
  297.8 13.5 %collective-permute-done.17 = bf16[2,280,1536]{2,1,0:T(8,128)(2,1)} collective-permute-done((bf16[2,280,1536]{2,1,0:T(8,128)(2,1)}, bf16[2,280,1536]{2,1,0:T(8,128)(2,1)}, u32[]{:S(2)}, u32[]{:S(2)}) %collective-permute-start.17) | collective-permute-done | bytes 1720352 | tf_op jit(solution)/shard_map/ppermute | solution.py:695
  315.4 23.3 %middle.2 = (bf16[2048,512]{1,0:T(8,128)(2,1)S(1)}, bf16[2048,512]{1,0:T(8,128)(2,1)S(1)}, bf16[2048,512]{1,0:T(8,128)(2,1)}, bf16[2048,1536]{1,0:T(8,128)(2,1)}) custom-call(s32[8]{0:T(128)S(1)} %stack.292.order, bf16[2048,1536]{1,0:T(8,128)(2,1)} %all-gather.10.cloned.1.call-done.h_ref, bf16[2048,1536]{1,0:T(8,128)(2,1)} %constant_dynamic-update-slice_fusion.12.dy_ref, ...), custom_call_target="tpu_custom_call" | custom-call | flops 1000 | bytes 1000 | tf_op jit(solution)/shard_map/middle/pallas_call | solution.py:370
  338.7 11.6 %collective-permute-done.18 = bf16[2,2,2,192,608]{4,3,0,2,1:T(8,128)(2,1)} collective-permute-done((bf16[2,2,2,192,608]{4,3,0,2,1:T(8,128)(2,1)}, bf16[2,2,2,192,608]{4,3,0,2,1:T(8,128)(2,1)}, u32[]{:S(2)}, u32[]{:S(2)}) %collective-permute-start.18) | collective-permute-done | bytes 1867808 | tf_op jit(solution)/shard_map/ppermute | solution.py:695
  365.7 10.0 %two_grads.2 = bf16[2,1536,512]{2,1,0:T(8,128)(2,1)} custom-call(bf16[2048,1536]{1,0:T(8,128)(2,1)} %all-gather.10.cloned.1.call-done.h_ref, bf16[2048,512]{1,0:T(8,128)(2,1)S(1)} %copy-done.22, bf16[2048,512]{1,0:T(8,128)(2,1)S(1)} %copy-done.23), custom_call_target="tpu_custom_call" | custom-call | flops 1000 | bytes 1000 | tf_op jit(solution)/shard_map/two_grads/pallas_call | solution.py:403
  381.6 37.4 %middle.3 = (bf16[2048,608]{1,0:T(8,128)(2,1)S(1)}, bf16[2048,608]{1,0:T(8,128)(2,1)}, bf16[2048,608]{1,0:T(8,128)(2,1)}, bf16[2048,1536]{1,0:T(8,128)(2,1)}) custom-call(s32[8]{0:T(128)S(1)} %stack.292.order, bf16[2048,1536]{1,0:T(8,128)(2,1)} %all-gather.10.cloned.1.call-done.h_ref, bf16[2048,1536]{1,0:T(8,128)(2,1)} %constant_dynamic-update-slice_fusion.12.dy_ref, ...), custom_call_target="tpu_custom_call" | custom-call | flops 1000 | bytes 1000 | tf_op jit(solution)/shard_map/middle/pallas_call | solution.py:370
  445.9 13.1 %two_grads.3 = bf16[2,1536,608]{2,1,0:T(8,128)(2,1)} custom-call(bf16[2048,1536]{1,0:T(8,128)(2,1)} %all-gather.10.cloned.1.call-done.h_ref, bf16[2048,608]{1,0:T(8,128)(2,1)S(1)} %copy-done.19, bf16[2048,608]{1,0:T(8,128)(2,1)S(1)} %copy-done.20), custom_call_target="tpu_custom_call" | custom-call | flops 1000 | bytes 1000 | tf_op jit(solution)/shard_map/two_grads/pallas_call | solution.py:403
  475.4 11.7 %down.1 = bf16[2048,1536]{1,0:T(8,128)(2,1)} custom-call(bf16[2048,512]{1,0:T(8,128)(2,1)S(1)} %copy-done.6, bf16[2048,608]{1,0:T(8,128)(2,1)} %copy-done.1, bf16[512,1536]{1,0:T(8,128)(2,1)S(1)} %bitcast.413, bf16[608,1536]{1,0:T(8,128)(2,1)S(1)} %bitcast.411), custom_call_target="tpu_custom_call" | custom-call | flops 1000 | bytes 1000 | tf_op jit(solution)/shard_map/down/pallas_call | solution.py:443
  524.3 21.4 %collective-permute-done.39 = bf16[2,192,512]{2,1,0:T(8,128)(2,1)S(1)} collective-permute-done((bf16[2,192,512]{2,1,0:T(8,128)(2,1)S(1)}, bf16[2,192,512]{2,1,0:T(8,128)(2,1)S(1)}, u32[]{:S(2)}, u32[]{:S(2)}) %collective-permute-start.39) | collective-permute-done | bytes 393248 | tf_op jit(solution)/shard_map/ppermute | solution.py:695
  558.0 9.0 %collective-permute-done.40 = bf16[2,2,192,512]{3,2,1,0:T(8,128)(2,1)} collective-permute-done((bf16[2,2,192,512]{3,2,1,0:T(8,128)(2,1)}, bf16[2,2,192,512]{3,2,1,0:T(8,128)(2,1)}, u32[]{:S(2)}, u32[]{:S(2)}) %collective-permute-start.40) | collective-permute-done | bytes 786464 | tf_op jit(solution)/shard_map/ppermute | solution.py:686
  618.6 11.8 %collective-permute-done.34 = bf16[2,208,128]{2,1,0:T(8,128)(2,1)S(1)} collective-permute-done((bf16[2,208,128]{2,1,0:T(8,128)(2,1)S(1)}, bf16[2,208,128]{2,1,0:T(8,128)(2,1)S(1)}, u32[]{:S(2)}, u32[]{:S(2)}) %collective-permute-start.34) | collective-permute-done | bytes 106528 | tf_op jit(solution)/shard_map/ppermute | solution.py:695
  655.4 15.5 %collective-permute-done.37 = bf16[208,128]{1,0:T(8,128)(2,1)S(1)} collective-permute-done((bf16[208,128]{1,0:T(8,128)(2,1)S(1)}, bf16[208,128]{1,0:T(8,128)(2,1)S(1)}, u32[]{:S(2)}, u32[]{:S(2)}) %collective-permute-start.37) | collective-permute-done | bytes 53280 | tf_op jit(solution)/shard_map/ppermute | solution.py:695
  706.6 16.0 %collective-permute-done.59 = bf16[2,2,192,608]{3,2,1,0:T(8,128)(2,1)} collective-permute-done((bf16[2,2,192,608]{3,2,1,0:T(8,128)(2,1)}, bf16[2,2,192,608]{3,2,1,0:T(8,128)(2,1)}, u32[]{:S(2)}, u32[]{:S(2)}) %collective-permute-start.59) | collective-permute-done | bytes 933920 | tf_op jit(solution)/shard_map/ppermute | solution.py:686
  738.8 17.5 %adam_columns.2 = (f32[192,8960]{1,0:T(8,128)}, f32[192,8960]{1,0:T(8,128)}, f32[192,8960]{1,0:T(8,128)}) custom-call(s32[2]{0:T(128)S(1)} %copy-done.40, f32[1]{0:T(128)} %bitcast.131.factor_ref, bf16[4,2,2,192,512]{4,3,2,1,0:T(8,128)(2,1)S(1)} %pad_maximum_fusion.5.first_ref, bf16[4,2,2,192,608]{4,3,2,1,0:T(8,128)(2,1)} %pad_maximum_fusion.2.second_ref, ...), custom_call_target="tpu_custom_call" | custom-call | flops 1000 | bytes 1000 | tf_op jit(solution)/shard_map/adam_columns/pallas_call | solution.py:155
  756.3 17.5 %adam_columns.3 = (f32[192,8960]{1,0:T(8,128)}, f32[192,8960]{1,0:T(8,128)}, f32[192,8960]{1,0:T(8,128)}) custom-call(s32[2]{0:T(128)S(1)} %copy-done.40, f32[1]{0:T(128)} %bitcast.131.factor_ref, bf16[4,2,2,192,512]{4,3,2,1,0:T(8,128)(2,1)S(1)} %pad_maximum_fusion.5.first_ref, bf16[4,2,2,192,608]{4,3,2,1,0:T(8,128)(2,1)} %pad_maximum_fusion.2.second_ref, ...), custom_call_target="tpu_custom_call" | custom-call | flops 1000 | bytes 1000 | tf_op jit(solution)/shard_map/adam_columns/pallas_call | solution.py:155
  780.9 16.7 %multiply_subtract_fusion = (f32[1120,1536]{1,0:T(8,128)}, f32[1120,1536]{1,0:T(8,128)}, f32[1120,1536]{1,0:T(8,128)}) fusion(f32[1120,1536]{1,0:T(8,128)} %param.30, bf16[1120,1536]{1,0:T(8,128)(2,1)} %all-gather.12.cloned.1.call-done, f32[]{:T(128)} %min.3, f32[1120,1536]{1,0:T(8,128)} %param.42, f32[1120,1536]{1,0:T(8,128)} %param.36), kind=kLoop, calls=%fused_computation.2 | loop fusion | flops 29245440 | bytes 44728324 | tf_op jit(solution)/shard_map/sub | solution.py:67
  (610 shorter events, 354.5 us)
Async XLA Ops:
  11.4 76.0 %all-gather.16.cloned.1.call-start = ((), (), s32[]{:S(2)}) async-start(), calls=%async_computation.8 | async-start | bytes 1327104 | tf_op jit(solution)/shard_map/all_gather | solution.py:808
  49.3 92.9 %all-gather.8.cloned.1.call-start = ((), (), s32[]{:S(2)}) async-start(), calls=%async_computation.2 | async-start | bytes 2359296 | tf_op jit(solution)/shard_map/all_gather | solution.py:808
  87.1 228.3 %all-gather.10.cloned.1.call-start = ((), (), s32[]{:S(2)}) async-start(), calls=%async_computation.3 | async-start | bytes 7077888 | tf_op jit(solution)/shard_map/all_gather | solution.py:991
  95.2 47.0 %collective-permute-start.8 = (bf16[1536,384]{1,0:T(8,128)(2,1)S(1)}, bf16[1536,384]{1,0:T(8,128)(2,1)}, u32[]{:S(2)}, u32[]{:S(2)}) collective-permute-start(bf16[1536,384]{1,0:T(8,128)(2,1)S(1)} %bitcast_dynamic-update-slice_fusion), channel_id=1, source_target_pairs={{0,16},{16,0},{8,24},{24,8},{1,17},{17,1},{9,25},{25,9},{2,18},{18... | collective-permute-start | bytes 3538952 | tf_op jit(solution)/shard_map/ppermute | solution.py:686
  98.6 43.6 %collective-permute-start.5 = (bf16[2,192,608]{2,1,0:T(8,128)(2,1)S(1)}, bf16[2,192,608]{2,1,0:T(8,128)(2,1)S(1)}, u32[]{:S(2)}, u32[]{:S(2)}) collective-permute-start(bf16[2,192,608]{2,1,0:T(8,128)(2,1)S(1)} %slice_bitcast_fusion.4), channel_id=1, source_target_pairs={{0,2},{1,3},{2,0},{3,1},{4,6},{5,7},{6,4},{7,5},{8,10},{9,11},{10,... | collective-permute-start | bytes 1400840 | tf_op jit(solution)/shard_map/ppermute | solution.py:695
  185.2 236.3 %reduce-scatter.3.cloned.1.call-start = ((), (), s32[]{:S(2)}) async-start(), calls=%async_computation.4 | async-start | bytes 1966080 | tf_op jit(solution)/shard_map/reduce_scatter | solution.py:998
  207.6 86.4 %collective-permute-start.15 = (bf16[1024,1536]{1,0:T(8,128)(2,1)}, bf16[1024,1536]{1,0:T(8,128)(2,1)}, u32[]{:S(2)}, u32[]{:S(2)}) collective-permute-start(bf16[1024,1536]{1,0:T(8,128)(2,1)} %get-tuple-element.361), channel_id=1, source_target_pairs={{0,8},{8,0},{16,24},{24,16},{1,9},{9,1},{17,25},{25,17},{2,10},{10... | collective-permute-start | bytes 9437192 | tf_op jit(solution)/shard_map/ppermute | solution.py:682
  207.6 59.4 %collective-permute-start.16 = (bf16[280,1536]{1,0:T(8,128)(2,1)S(1)}, bf16[280,1536]{1,0:T(8,128)(2,1)}, u32[]{:S(2)}, u32[]{:S(2)}) collective-permute-start(bf16[280,1536]{1,0:T(8,128)(2,1)S(1)} %dynamic-slice_convert_fusion), channel_id=1, source_target_pairs={{0,4},{1,5},{2,6},{3,7},{4,0},{5,1},{6,2},{7,3},{8,12},{9,13},{10,... | collective-permute-start | bytes 2580488 | tf_op jit(solution)/shard_map/ppermute | solution.py:695
  210.8 61.2 %collective-permute-start.11 = (bf16[2,2,2,192,512]{4,3,0,2,1:T(8,128)(2,1)}, bf16[2,2,2,192,512]{4,3,0,2,1:T(8,128)(2,1)}, u32[]{:S(2)}, u32[]{:S(2)}) collective-permute-start(bf16[2,2,2,192,512]{4,3,0,2,1:T(8,128)(2,1)} %pad_maximum_fusion.11), channel_id=1, source_target_pairs={{0,1},{1,0},{2,3},{3,2},{4,5},{5,4},{6,7},{7,6},{8,9},{9,8},{10,11... | collective-permute-start | bytes 4718600 | tf_op jit(solution)/shard_map/ppermute | solution.py:695
  214.6 76.0 %collective-permute-start.12 = (bf16[2,2,192,608]{3,2,0,1:T(8,128)(2,1)S(1)}, bf16[2,2,192,608]{3,2,0,1:T(8,128)(2,1)S(1)}, u32[]{:S(2)}, u32[]{:S(2)}) collective-permute-start(bf16[2,2,192,608]{3,2,0,1:T(8,128)(2,1)S(1)} %pad_maximum_fusion.14), channel_id=1, source_target_pairs={{0,4},{1,5},{2,6},{3,7},{4,0},{5,1},{6,2},{7,3},{8,12},{9,13},{10,... | collective-permute-start | bytes 2801672 | tf_op jit(solution)/shard_map/ppermute | solution.py:695
  292.5 57.8 %collective-permute-start.18 = (bf16[2,2,2,192,608]{4,3,0,2,1:T(8,128)(2,1)}, bf16[2,2,2,192,608]{4,3,0,2,1:T(8,128)(2,1)}, u32[]{:S(2)}, u32[]{:S(2)}) collective-permute-start(bf16[2,2,2,192,608]{4,3,0,2,1:T(8,128)(2,1)} %pad_maximum_fusion.7), channel_id=1, source_target_pairs={{0,1},{1,0},{2,3},{3,2},{4,5},{5,4},{6,7},{7,6},{8,9},{9,8},{10,11... | collective-permute-start | bytes 5603336 | tf_op jit(solution)/shard_map/ppermute | solution.py:695
  362.0 224.7 %reduce-scatter.5.cloned.1.call-start = ((), (), s32[]{:S(2)}) async-start(), calls=%async_computation.5 | async-start | bytes 2359296 | tf_op jit(solution)/shard_map/reduce_scatter | solution.py:1099
  444.8 63.6 %collective-permute-start.29 = (bf16[2,152,1536]{2,1,0:T(8,128)(2,1)}, bf16[2,152,1536]{2,1,0:T(8,128)(2,1)}, u32[]{:S(2)}, u32[]{:S(2)}) collective-permute-start(bf16[2,152,1536]{2,1,0:T(8,128)(2,1)} %get-tuple-element.297), channel_id=1, source_target_pairs={{0,1},{1,0},{2,3},{3,2},{4,5},{5,4},{6,7},{7,6},{8,9},{9,8},{10,11... | collective-permute-start | bytes 2801672 | tf_op jit(solution)/shard_map/ppermute | solution.py:695
  474.5 75.6 %collective-permute-start.42 = (bf16[2,2,2,192,608]{4,3,2,1,0:T(8,128)(2,1)}, bf16[2,2,2,192,608]{4,3,2,1,0:T(8,128)(2,1)}, u32[]{:S(2)}, u32[]{:S(2)}) collective-permute-start(bf16[2,2,2,192,608]{4,3,2,1,0:T(8,128)(2,1)} %get-tuple-element.271), channel_id=1, source_target_pairs={{0,1},{1,0},{2,3},{3,2},{4,5},{5,4},{6,7},{7,6},{8,9},{9,8},{10,11... | collective-permute-start | bytes 5603336 | tf_op jit(solution)/shard_map/ppermute | solution.py:695
  490.9 140.0 %collective-permute-start.24 = (bf16[1024,1536]{1,0:T(8,128)(2,1)}, bf16[1024,1536]{1,0:T(8,128)(2,1)}, u32[]{:S(2)}, u32[]{:S(2)}) collective-permute-start(bf16[1024,1536]{1,0:T(8,128)(2,1)} %slice.381), channel_id=1, source_target_pairs={{0,8},{8,0},{16,24},{24,16},{1,9},{9,1},{17,25},{25,17},{2,10},{10... | collective-permute-start | bytes 9437192 | tf_op jit(solution)/shard_map/ppermute | solution.py:682
  506.5 274.4 %all-gather.12.cloned.1.call-start = ((), (), s32[]{:S(2)}) async-start(), calls=%async_computation.6 | async-start | bytes 4300800 | tf_op jit(solution)/shard_map/all_gather | solution.py:1147
  575.5 61.2 %collective-permute-start.43 = (bf16[2,2,192,608]{3,2,1,0:T(8,128)(2,1)}, bf16[2,2,192,608]{3,2,1,0:T(8,128)(2,1)}, u32[]{:S(2)}, u32[]{:S(2)}) collective-permute-start(bf16[2,2,192,608]{3,2,1,0:T(8,128)(2,1)} %get-tuple-element.293), channel_id=1, source_target_pairs={{0,4},{1,5},{2,6},{3,7},{4,0},{5,1},{6,2},{7,3},{8,12},{9,13},{10,... | collective-permute-start | bytes 2801672 | tf_op jit(solution)/shard_map/ppermute | solution.py:695
  584.9 55.0 %collective-permute-start.53 = (bf16[192,384]{1,0:T(8,128)(2,1)}, bf16[192,384]{1,0:T(8,128)(2,1)}, u32[]{:S(2)}, u32[]{:S(2)}) collective-permute-start(bf16[192,384]{1,0:T(8,128)(2,1)} %get-tuple-element.365), channel_id=1, source_target_pairs={{0,4},{1,5},{2,6},{3,7},{4,0},{5,1},{6,2},{7,3},{8,12},{9,13},{10,... | collective-permute-start | bytes 442376 | tf_op jit(solution)/shard_map/ppermute | solution.py:695
  609.6 93.0 %collective-permute-start.63 = (bf16[512,1536]{1,0:T(8,128)(2,1)}, bf16[512,1536]{1,0:T(8,128)(2,1)}, u32[]{:S(2)}, u32[]{:S(2)}) collective-permute-start(bf16[512,1536]{1,0:T(8,128)(2,1)} %get-tuple-element.224), channel_id=1, source_target_pairs={{0,8},{8,0},{16,24},{24,16},{1,9},{9,1},{17,25},{25,17},{2,10},{10... | collective-permute-start | bytes 4718600 | tf_op jit(solution)/shard_map/ppermute | solution.py:682
  649.7 72.9 %collective-permute-start.35 = (bf16[128,1536]{1,0:T(8,128)(2,1)}, bf16[128,1536]{1,0:T(8,128)(2,1)}, u32[]{:S(2)}, u32[]{:S(2)}) collective-permute-start(bf16[128,1536]{1,0:T(8,128)(2,1)} %get-tuple-element.280), channel_id=1, source_target_pairs={{0,2},{1,3},{2,0},{3,1},{4,6},{5,7},{6,4},{7,5},{8,10},{9,11},{10,... | collective-permute-start | bytes 1179656 | tf_op jit(solution)/shard_map/ppermute | solution.py:695
  649.8 72.8 %collective-permute-start.36 = (bf16[128,1536]{1,0:T(8,128)(2,1)}, bf16[128,1536]{1,0:T(8,128)(2,1)}, u32[]{:S(2)}, u32[]{:S(2)}) collective-permute-start(bf16[128,1536]{1,0:T(8,128)(2,1)} %get-tuple-element.279), channel_id=1, source_target_pairs={{0,16},{16,0},{8,24},{24,8},{1,17},{17,1},{9,25},{25,9},{2,18},{18... | collective-permute-start | bytes 1179656 | tf_op jit(solution)/shard_map/ppermute | solution.py:686
  705.6 68.4 %collective-permute-start.64 = (bf16[256,1536]{1,0:T(8,128)(2,1)}, bf16[256,1536]{1,0:T(8,128)(2,1)}, u32[]{:S(2)}, u32[]{:S(2)}) collective-permute-start(bf16[256,1536]{1,0:T(8,128)(2,1)} %fusion.18), channel_id=1, source_target_pairs={{0,16},{16,0},{8,24},{24,8},{1,17},{17,1},{9,25},{25,9},{2,18},{18... | collective-permute-start | bytes 2359304 | tf_op jit(solution)/shard_map/ppermute | solution.py:686
  724.9 49.0 %collective-permute-start.60 = (bf16[256,1536]{1,0:T(8,128)(2,1)}, bf16[256,1536]{1,0:T(8,128)(2,1)}, u32[]{:S(2)}, u32[]{:S(2)}) collective-permute-start(bf16[256,1536]{1,0:T(8,128)(2,1)} %pad_maximum_fusion.25), channel_id=1, source_target_pairs={{0,16},{16,0},{8,24},{24,8},{1,17},{17,1},{9,25},{25,9},{2,18},{18... | collective-permute-start | bytes 2359304 | tf_op jit(solution)/shard_map/ppermute | solution.py:686
  728.6 45.3 %collective-permute-start.61 = (bf16[256,1536]{1,0:T(8,128)(2,1)}, bf16[256,1536]{1,0:T(8,128)(2,1)}, u32[]{:S(2)}, u32[]{:S(2)}) collective-permute-start(bf16[256,1536]{1,0:T(8,128)(2,1)} %pad_maximum_fusion.26), channel_id=1, source_target_pairs={{0,2},{1,3},{2,0},{3,1},{4,6},{5,7},{6,4},{7,5},{8,10},{9,11},{10,... | collective-permute-start | bytes 2359304 | tf_op jit(solution)/shard_map/ppermute | solution.py:695
  (180 other events, 1879.2 us)
Sparse Core Ops, SparseCore 0:
  11.5 34.7 all-gather.13
  49.4 30.3 all-gather.15
  87.2 43.6 all-gather.7
  185.3 83.4 all-gather.9
  362.2 43.4 reduce-scatter.2
  506.6 53.2 reduce-scatter.4
  596.1 28.3 all-gather.11

commit v10 on v9

--- a/solution.py
+++ b/solution.py
@@ -887,9 +887,10 @@
     digits = jnp.pad(digits, ((0, 0), (0, HD - 2)))
     token_send = jnp.concatenate([flat_low, digits], axis=1)
     picked_a, picked_b = pick_columns(ids, w_gate, w_up, blk_count)
-    token_cross = after(swap_cross(token_send), (picked_a, strip_ring))
-    dy_over = swap_blk(after(dy_low, token_cross), team)
-    dy_cross = swap_cross(after(dy_low, token_cross))
+    got_a = swap_blk(picked_a[1], team)
+    dy_cross = swap_cross(after(dy_low, picked_a))
+    dy_over = swap_blk(after(dy_low, strip_ring), team)
+    token_cross = after(swap_cross(token_send), (picked_a, strip_ring, got_a, dy_cross))
 
     def place(values, other, done, bit, lead=0):
         mine = blk_bit(bit)
@@ -927,10 +928,11 @@
     first_blk = jnp.sum((seg_all[:, :, -1] < segment_ids[None, :, 0]).astype(jnp.int32), axis=0)
     attend_ids = jnp.concatenate([blk[None], first_blk])
 
+    dy_first = swap_blk(dy_cross[:half], team)
+    dy_second = swap_cross(dy_over[half:])
     mixed_cross = swap_cross(mixed_far)
     mixed_core = swap_core(jnp.stack([mixed_core, mixed_cross[1]]))
-    got_a = swap_blk(picked_a[1], team)
-    mixed_core = after(mixed_core, got_a)
+    mixed_core = after(mixed_core, dy_over)
     query, packed_kv = pack(ids, mixed_own, mixed_cross, mixed_core)
     key_value = packed_kv.reshape(rows_here, block_len, 2 * KVD)
     kv_all = gather_ring(key_value)
@@ -959,13 +961,11 @@
         return values
 
     got_b = swap_blk(after(picked_b[1], mixed_own), team)
-    dy_cross, dy_over = after((dy_cross, dy_over), packed_kv)
-    pair_a = team_pair(picked_a[0], after(got_a, packed_kv))
-    kv_all = after(kv_all, (got_b, dy_cross, dy_over))
-    pair_a = after(pair_a, kv_all)
+    pair_a = team_pair(picked_a[0], after(got_a, mixed_own))
     pair_a_got = swap_blk(pair_a, bits[0])
-    dy_first = swap_blk(dy_cross[:half], team)
-    dy_second = swap_cross(dy_over[half:])
+    pair_a_got, got_b = after((pair_a_got, got_b), kv_all)
+    kv_all = after(kv_all, (pair_a_got, got_b, dy_first, dy_second))
+    down_got = swap_blk(after(down_here, kv_all), bits[0])
     dy_chip = jnp.concatenate([dy_low, dy_cross, dy_over, dy_first, dy_second])
     dy_team = jnp.concatenate([dy_chip, swap_core(dy_chip)])
     pair_a = place(pair_a, pair_a_got, [team], bits[0], 1)
@@ -982,8 +982,6 @@
     flat = wide(flat_low)
     resid = flat + jnp.dot(att_in, out_full, preferred_element_type=jnp.float32)
     h_two = low(norm_apply(resid, gain_two))
-    h_two = after(h_two, pair_a_got)
-    down_got = after(swap_blk(after(down_here, kv_all), bits[0]), h_two)
     down_here = place(down_here, down_got, [], bits[0])
     down_here = lows_of(down_here, [bits[0]]).reshape(2 * blk_count // 4, quarter, D)
     down_a = down_here[:, :size_first].reshape(widths[0], D)
@@ -1113,15 +1111,15 @@
     block_shape = (2,) * len(bits) + (weight_rows, -1)
     query_grad = low(left_product(near_one, near_dq)).reshape(block_shape)
     steps_query = part_sent(query_grad, len(bits) - 1, bits[-1])
-    near_a = gather_near_stacked(columns_last(*after(third_a, d_query)))
     second_b = part_sent(columns_mid(*after(first_b, d_query)), 1, bits[0])
-    dkv = after(dkv, (query_grad, down_share_b))
+    dkv = after(dkv, down_share_b)
     own_part, core_part, far_part, bias_kv = turn_dkv(
         ids, dkv, jnp.concatenate([cosine, cosine], axis=1), jnp.concatenate([sine, sine], axis=1)
     )
     bias_q = jnp.sum(wide(d_query), axis=0)
     d_key = own_part
     cross_part = swap_cross(far_part)
+    near_a = gather_near_stacked(columns_last(*after(third_a, own_part)))
     core_part = swap_core(jnp.stack([core_part, cross_part[1]]))
     kv_grad, hone_here, hone_there = make_kv_grad(
         blk_count,
@@ -1151,7 +1149,7 @@
         kv_grad = kv_sum
         steps_kv = part_sent(kv_sum, i, bits[i])
     sum_b, third_b = columns_third(*after(second_b, kv_grad))
-    share_kv_all = wide(steps_kv[0]) + wide(after(steps_kv[1], (near_a, third_b[1])))
+    share_kv_all = wide(steps_kv[0]) + wide(after(steps_kv[1], third_b[1]))
     share_kv = low(share_kv_all[:weight_rows])
     vector_part = share_kv_all[weight_rows : weight_rows + vector_rows]
     share_query = part_sum(*after(steps_query, kv_grad))
@@ -1195,7 +1193,7 @@
     factor = jnp.minimum(1.0, CLIP_NORM / (grad_norm + 1e-06))
     out_chip = chip_sum(out_part, after(out_came, kv_grad))
     out_far = scatter_far(out_chip)
-    factor = after(factor, (out_chip, cross_b))
+    factor = after(factor, (out_chip, cross_b, near_a))
 
     new_first_gate, new_second_gate, new_gate = adam_columns(
         0, ids, factor[None], near_a, near_b, w_gate, first_gate, second_gate, blk_count, RATE_GATE, WEIGHT_DECAY

time: 814 us -> 805 us (0.989)
  waiting for transfers between devices: 314 us -> 295 us
  starting transfers between devices: 70.7 us -> 87.9 us
    ppermute x20, waiting for transfers between devices: 91.3 us -> 49.9 us  [swap_cross(): return lax.ppermute(values, 'grp', CROSS)]
    ppermute x34, waiting for transfers between devices: 209 us -> 240 us  [swap_blk(): return lax.ppermute(values, 'blk', [(i, i ^ bit) for i in range(count)])]
    ppermute x34, starting transfers between devices: 43.2 us -> 59.4 us  [swap_blk(): return lax.ppermute(values, 'blk', [(i, i ^ bit) for i in range(count)])]
    all_gather x3, waiting for transfers between devices: 11.9 us -> 2.03 us  [gather_ring(): lax.all_gather(values, ('grp', 'blk'), axis=0, axis_index_groups=ring_gro...]
    unnamed x271 -> x275, local copies, waits for them, and re-layouts: 39.4 us -> 34.7 us
  transfers between devices with their start and end apart: 78 -> 78, of which waited for: 31 -> 31; matrix products, arithmetic and copies ran while one was open for 20% -> 19% of each run, Pallas kernels for 22% -> 22%
where the time goes in v10:
time: 805 us; the launch traced here: 797 us
  waiting for transfers between devices  295 us (37%)
  Pallas kernels  182 us (23%)
  other arithmetic  118 us (15%)
  starting transfers between devices  87.9 us (11%)
  local copies, waits for them, and re-layouts  83.5 us (10%)
  between operations  22.2 us (3%)
  matrix products  8.46 us (1%)
    ppermute x34, waiting for transfers between devices, swap_blk(): return lax.ppermute(values, 'blk', [(i, i ^ bit) for i in range(count)])  240 us
    pallas_call x2, Pallas kernels, middle(): pl.pallas_call(functools.partial(middle_body, prev is not None), grid_spe...  60.5 us
    ppermute x34, starting transfers between devices, swap_blk(): return lax.ppermute(values, 'blk', [(i, i ^ bit) for i in range(count)])  59.4 us
    ppermute x20, waiting for transfers between devices, swap_cross(): return lax.ppermute(values, 'grp', CROSS)  49.9 us
    pallas_call x2, Pallas kernels, adam_columns(): pl.pallas_call(functools.partial(adam_body, blk_count, rate, decay), grid...  35.2 us
    unnamed x275, local copies, waits for them, and re-layouts  34.7 us
    ppermute x20, starting transfers between devices, swap_cross(): return lax.ppermute(values, 'grp', CROSS)  25.1 us
    convert_element_type x21, other arithmetic, low(): return values.astype(jnp.bfloat16)  23.9 us
  transfers between devices with their start and end apart: 78, of which 31 were waited for; matrix products, arithmetic and copies ran while one was open for 19% of the time, Pallas kernels for 22%

profile of v10, /device:TPU:0, one launch (start us, length us, event | category | flops | bytes accessed | tf_op | source)
XLA Modules:
  0.0 797.3 jit_solution(17967426413645520723)
XLA Ops:
  25.1 17.3 %collective-permute-done.1 = bf16[2,192,512]{2,1,0:T(8,128)(2,1)S(1)} collective-permute-done((bf16[2,192,512]{2,1,0:T(8,128)(2,1)S(1)}, bf16[2,192,512]{2,1,0:T(8,128)(2,1)S(1)}, u32[]{:S(2)}, u32[]{:S(2)}) %collective-permute-start.1) | collective-permute-done | bytes 393248 | tf_op jit(solution)/shard_map/ppermute | solution.py:695
  42.4 8.8 %collective-permute-done.2 = bf16[256,1536]{1,0:T(8,128)(2,1)S(1)} collective-permute-done((bf16[256,1536]{1,0:T(8,128)(2,1)S(1)}, bf16[256,1536]{1,0:T(8,128)(2,1)S(1)}, u32[]{:S(2)}, u32[]{:S(2)}) %collective-permute-start.2) | collective-permute-done | bytes 786464 | tf_op jit(solution)/shard_map/ppermute | solution.py:686
  68.4 10.6 %collective-permute-done.4.cross_ref = bf16[2,256,512]{2,1,0:T(8,128)(2,1)S(1)} collective-permute-done((bf16[2,256,512]{2,1,0:T(8,128)(2,1)S(1)}, bf16[2,256,512]{2,1,0:T(8,128)(2,1)S(1)}, u32[]{:S(2)}, u32[]{:S(2)}) %collective-permute-start.4) | collective-permute-done | bytes 524320 | tf_op jit(solution)/shard_map/ppermute | solution.py:686
  79.2 15.5 %collective-permute-done.6 = bf16[256,1536]{1,0:T(8,128)(2,1)S(1)} collective-permute-done((bf16[256,1536]{1,0:T(8,128)(2,1)S(1)}, bf16[256,1536]{1,0:T(8,128)(2,1)S(1)}, u32[]{:S(2)}, u32[]{:S(2)}) %collective-permute-start.6) | collective-permute-done | bytes 786464 | tf_op jit(solution)/shard_map/ppermute | solution.py:695
  114.6 34.7 %collective-permute-done.8 = bf16[2,192,608]{2,1,0:T(8,128)(2,1)} collective-permute-done((bf16[2,192,608]{2,1,0:T(8,128)(2,1)}, bf16[2,192,608]{2,1,0:T(8,128)(2,1)}, u32[]{:S(2)}, u32[]{:S(2)}) %collective-permute-start.8) | collective-permute-done | bytes 466976 | tf_op jit(solution)/shard_map/ppermute | solution.py:695
  149.3 10.3 %collective-permute-done.7 = bf16[2,2,192,512]{3,2,0,1:T(8,128)(2,1)} collective-permute-done((bf16[2,2,192,512]{3,2,0,1:T(8,128)(2,1)}, bf16[2,2,192,512]{3,2,0,1:T(8,128)(2,1)}, u32[]{:S(2)}, u32[]{:S(2)}) %collective-permute-start.7) | collective-permute-done | bytes 786464 | tf_op jit(solution)/shard_map/ppermute | solution.py:695
  200.1 48.6 %collective-permute-done.16 = bf16[280,1536]{1,0:T(8,128)(2,1)} collective-permute-done((bf16[280,1536]{1,0:T(8,128)(2,1)}, bf16[280,1536]{1,0:T(8,128)(2,1)}, u32[]{:S(2)}, u32[]{:S(2)}) %collective-permute-start.16) | collective-permute-done | bytes 860192 | tf_op jit(solution)/shard_map/ppermute | solution.py:695
  256.6 19.0 %collective-permute-done.14 = bf16[2,2,192,608]{3,2,0,1:T(8,128)(2,1)S(1)} collective-permute-done((bf16[2,2,192,608]{3,2,0,1:T(8,128)(2,1)S(1)}, bf16[2,2,192,608]{3,2,0,1:T(8,128)(2,1)S(1)}, u32[]{:S(2)}, u32[]{:S(2)}) %collective-permute-start.14) | collective-permute-done | bytes 933920 | tf_op jit(solution)/shard_map/ppermute | solution.py:695
  282.1 10.9 %collective-permute-done.17 = bf16[2,280,1536]{2,1,0:T(8,128)(2,1)} collective-permute-done((bf16[2,280,1536]{2,1,0:T(8,128)(2,1)}, bf16[2,280,1536]{2,1,0:T(8,128)(2,1)}, u32[]{:S(2)}, u32[]{:S(2)}) %collective-permute-start.17) | collective-permute-done | bytes 1720352 | tf_op jit(solution)/shard_map/ppermute | solution.py:695
  297.1 23.2 %middle.2 = (bf16[2048,512]{1,0:T(8,128)(2,1)S(1)}, bf16[2048,512]{1,0:T(8,128)(2,1)S(1)}, bf16[2048,512]{1,0:T(8,128)(2,1)}, bf16[2048,1536]{1,0:T(8,128)(2,1)}) custom-call(s32[8]{0:T(128)S(1)} %stack.295.order, bf16[2048,1536]{1,0:T(8,128)(2,1)} %all-gather.10.cloned.1.call-done.h_ref, bf16[2048,1536]{1,0:T(8,128)(2,1)} %constant_dynamic-update-slice_fusion.12.dy_ref, ...), custom_call_target="tpu_custom_call" | custom-call | flops 1000 | bytes 1000 | tf_op jit(solution)/shard_map/middle/pallas_call | solution.py:370
  320.3 10.1 %collective-permute-done.18 = bf16[2,2,2,192,608]{4,3,0,2,1:T(8,128)(2,1)} collective-permute-done((bf16[2,2,2,192,608]{4,3,0,2,1:T(8,128)(2,1)}, bf16[2,2,2,192,608]{4,3,0,2,1:T(8,128)(2,1)}, u32[]{:S(2)}, u32[]{:S(2)}) %collective-permute-start.18) | collective-permute-done | bytes 1867808 | tf_op jit(solution)/shard_map/ppermute | solution.py:695
  345.9 10.1 %two_grads.2 = bf16[2,1536,512]{2,1,0:T(8,128)(2,1)} custom-call(bf16[2048,1536]{1,0:T(8,128)(2,1)} %all-gather.10.cloned.1.call-done.h_ref, bf16[2048,512]{1,0:T(8,128)(2,1)S(1)} %copy-done.21, bf16[2048,512]{1,0:T(8,128)(2,1)S(1)} %copy-done.22), custom_call_target="tpu_custom_call" | custom-call | flops 1000 | bytes 1000 | tf_op jit(solution)/shard_map/two_grads/pallas_call | solution.py:403
  364.4 37.3 %middle.3 = (bf16[2048,608]{1,0:T(8,128)(2,1)S(1)}, bf16[2048,608]{1,0:T(8,128)(2,1)}, bf16[2048,608]{1,0:T(8,128)(2,1)}, bf16[2048,1536]{1,0:T(8,128)(2,1)}) custom-call(s32[8]{0:T(128)S(1)} %stack.295.order, bf16[2048,1536]{1,0:T(8,128)(2,1)} %all-gather.10.cloned.1.call-done.h_ref, bf16[2048,1536]{1,0:T(8,128)(2,1)} %constant_dynamic-update-slice_fusion.12.dy_ref, ...), custom_call_target="tpu_custom_call" | custom-call | flops 1000 | bytes 1000 | tf_op jit(solution)/shard_map/middle/pallas_call | solution.py:370
  434.6 13.5 %two_grads.3 = bf16[2,1536,608]{2,1,0:T(8,128)(2,1)} custom-call(bf16[2048,1536]{1,0:T(8,128)(2,1)} %all-gather.10.cloned.1.call-done.h_ref, bf16[2048,608]{1,0:T(8,128)(2,1)S(1)} %copy-done.18, bf16[2048,608]{1,0:T(8,128)(2,1)S(1)} %copy-done.19), custom_call_target="tpu_custom_call" | custom-call | flops 1000 | bytes 1000 | tf_op jit(solution)/shard_map/two_grads/pallas_call | solution.py:403
  466.5 11.6 %down.1 = bf16[2048,1536]{1,0:T(8,128)(2,1)} custom-call(bf16[2048,512]{1,0:T(8,128)(2,1)S(1)} %copy-done.6, bf16[2048,608]{1,0:T(8,128)(2,1)} %copy-done.1, bf16[512,1536]{1,0:T(8,128)(2,1)S(1)} %bitcast.413, bf16[608,1536]{1,0:T(8,128)(2,1)S(1)} %bitcast.411), custom_call_target="tpu_custom_call" | custom-call | flops 1000 | bytes 1000 | tf_op jit(solution)/shard_map/down/pallas_call | solution.py:443
  488.0 8.0 %attend_back.1 = (bf16[256,1536]{1,0:T(8,128)(2,1)S(1)}, bf16[8,2,128,512]{3,2,1,0:T(8,128)(2,1)}) custom-call(s32[3]{0:T(128)S(1)} %copy-done.35, bf16[256,1536]{1,0:T(8,128)(2,1)S(1)} %copy-done.13, bf16[8,2,128,512]{3,2,1,0:T(8,128)(2,1)} %all-gather.8.cloned.1.call-done.k_ref.v_ref, bf16[8,2,128,512]{3,2,1,0:T(8,128)(2,1)} %all-gather.8.cloned.1.call-done.k_ref.v_ref, ...), custom_call_target="tpu_custom_call" | custom-call | flops 1000 | bytes 1000 | tf_op jit(solution)/shard_map/attend_back/pallas_call | solution.py:311
  545.1 16.3 %collective-permute-done.47 = bf16[2,2,192,384]{3,2,1,0:T(8,128)(2,1)S(1)} collective-permute-done((bf16[2,2,192,384]{3,2,1,0:T(8,128)(2,1)S(1)}, bf16[2,2,192,384]{3,2,1,0:T(8,128)(2,1)S(1)}, u32[]{:S(2)}, u32[]{:S(2)}) %collective-permute-start.47) | collective-permute-done | bytes 589856 | tf_op jit(solution)/shard_map/ppermute | solution.py:695
  584.8 9.0 %kv_grad.1 = (bf16[8,208,128]{2,1,0:T(8,128)(2,1)S(1)}, bf16[512,1536]{1,0:T(8,128)(2,1)S(1)}, bf16[512,1536]{1,0:T(8,128)(2,1)}) custom-call(bf16[256,128]{1,0:T(8,128)(2,1)S(1)} %get-tuple-element.179.self_ref, bf16[2,256,128]{2,1,0:T(8,128)(2,1)S(1)} %collective-permute-done.29.cross_ref, bf16[2,256,128]{2,1,0:T(8,128)(2,1)S(1)} %collective-permute-done.30.core_ref, ...), custom_call_target="tpu_custom_call" | custom-call | flops 1000 | bytes 1000 | tf_op jit(solution)/shard_map/kv_grad/pallas_call | solution.py:653
  608.3 11.9 %collective-permute-done.34 = bf16[2,208,128]{2,1,0:T(8,128)(2,1)S(1)} collective-permute-done((bf16[2,208,128]{2,1,0:T(8,128)(2,1)S(1)}, bf16[2,208,128]{2,1,0:T(8,128)(2,1)S(1)}, u32[]{:S(2)}, u32[]{:S(2)}) %collective-permute-start.34) | collective-permute-done | bytes 106528 | tf_op jit(solution)/shard_map/ppermute | solution.py:695
  646.7 14.7 %collective-permute-done.37 = bf16[208,128]{1,0:T(8,128)(2,1)S(1)} collective-permute-done((bf16[208,128]{1,0:T(8,128)(2,1)S(1)}, bf16[208,128]{1,0:T(8,128)(2,1)S(1)}, u32[]{:S(2)}, u32[]{:S(2)}) %collective-permute-start.37) | collective-permute-done | bytes 53280 | tf_op jit(solution)/shard_map/ppermute | solution.py:695
  699.0 15.7 %collective-permute-done.56 = bf16[2,2,192,608]{3,2,1,0:T(8,128)(2,1)S(1)} collective-permute-done((bf16[2,2,192,608]{3,2,1,0:T(8,128)(2,1)}, bf16[2,2,192,608]{3,2,1,0:T(8,128)(2,1)S(1)}, u32[]{:S(2)}, u32[]{:S(2)}) %collective-permute-start.56) | collective-permute-done | bytes 933920 | tf_op jit(solution)/shard_map/ppermute | solution.py:686
  731.2 17.6 %adam_columns.2 = (f32[192,8960]{1,0:T(8,128)}, f32[192,8960]{1,0:T(8,128)}, f32[192,8960]{1,0:T(8,128)}) custom-call(s32[2]{0:T(128)S(1)} %pad_add_fusion.2.ids, f32[1]{0:T(128)} %bitcast.131.factor_ref, bf16[4,2,2,192,512]{4,3,2,1,0:T(8,128)(2,1)S(1)} %pad_maximum_fusion.5.first_ref, bf16[4,2,2,192,608]{4,3,2,1,0:T(8,128)(2,1)} %pad_maximum_fusion.2.second_ref, ...), custom_call_target="tpu_custom_call" | custom-call | flops 1000 | bytes 1000 | tf_op jit(solution)/shard_map/adam_columns/pallas_call | solution.py:155
  748.7 17.6 %adam_columns.3 = (f32[192,8960]{1,0:T(8,128)}, f32[192,8960]{1,0:T(8,128)}, f32[192,8960]{1,0:T(8,128)}) custom-call(s32[2]{0:T(128)S(1)} %pad_add_fusion.2.ids, f32[1]{0:T(128)} %bitcast.131.factor_ref, bf16[4,2,2,192,512]{4,3,2,1,0:T(8,128)(2,1)S(1)} %pad_maximum_fusion.5.first_ref, bf16[4,2,2,192,608]{4,3,2,1,0:T(8,128)(2,1)} %pad_maximum_fusion.2.second_ref, ...), custom_call_target="tpu_custom_call" | custom-call | flops 1000 | bytes 1000 | tf_op jit(solution)/shard_map/adam_columns/pallas_call | solution.py:155
  772.2 16.7 %multiply_subtract_fusion = (f32[1120,1536]{1,0:T(8,128)}, f32[1120,1536]{1,0:T(8,128)}, f32[1120,1536]{1,0:T(8,128)}) fusion(f32[1120,1536]{1,0:T(8,128)} %param.30, bf16[1120,1536]{1,0:T(8,128)(2,1)} %all-gather.12.cloned.1.call-done, f32[]{:T(128)} %min.3, f32[1120,1536]{1,0:T(8,128)} %param.42, f32[1120,1536]{1,0:T(8,128)} %param.36), kind=kLoop, calls=%fused_computation.2 | loop fusion | flops 29245440 | bytes 44728324 | tf_op jit(solution)/shard_map/sub | solution.py:67
  (615 shorter events, 365.9 us)
Async XLA Ops:
  11.4 85.1 %all-gather.16.cloned.1.call-start = ((), (), s32[]{:S(2)}) async-start(), calls=%async_computation.8 | async-start | bytes 1327104 | tf_op jit(solution)/shard_map/all_gather | solution.py:808
  55.3 106.4 %all-gather.8.cloned.1.call-start = ((), (), s32[]{:S(2)}) async-start(), calls=%async_computation.2 | async-start | bytes 2359296 | tf_op jit(solution)/shard_map/all_gather | solution.py:808
  96.2 200.9 %all-gather.10.cloned.1.call-start = ((), (), s32[]{:S(2)}) async-start(), calls=%async_computation.3 | async-start | bytes 7077888 | tf_op jit(solution)/shard_map/all_gather | solution.py:989
  104.2 57.4 %collective-permute-start.11 = (bf16[1536,384]{1,0:T(8,128)(2,1)S(1)}, bf16[1536,384]{1,0:T(8,128)(2,1)}, u32[]{:S(2)}, u32[]{:S(2)}) collective-permute-start(bf16[1536,384]{1,0:T(8,128)(2,1)S(1)} %bitcast_dynamic-update-slice_fusion), channel_id=1, source_target_pairs={{0,16},{16,0},{8,24},{24,8},{1,17},{17,1},{9,25},{25,9},{2,18},{18... | collective-permute-start | bytes 3538952 | tf_op jit(solution)/shard_map/ppermute | solution.py:686
  107.4 52.2 %collective-permute-start.7 = (bf16[2,2,192,512]{3,2,0,1:T(8,128)(2,1)}, bf16[2,2,192,512]{3,2,0,1:T(8,128)(2,1)}, u32[]{:S(2)}, u32[]{:S(2)}) collective-permute-start(bf16[2,2,192,512]{3,2,0,1:T(8,128)(2,1)} %pad_maximum_fusion.19), channel_id=1, source_target_pairs={{0,4},{1,5},{2,6},{3,7},{4,0},{5,1},{6,2},{7,3},{8,12},{9,13},{10,... | collective-permute-start | bytes 2359304 | tf_op jit(solution)/shard_map/ppermute | solution.py:695
  180.0 224.1 %reduce-scatter.3.cloned.1.call-start = ((), (), s32[]{:S(2)}) async-start(), calls=%async_computation.4 | async-start | bytes 1966080 | tf_op jit(solution)/shard_map/reduce_scatter | solution.py:996
  189.6 88.7 %collective-permute-start.15 = (bf16[1024,1536]{1,0:T(8,128)(2,1)}, bf16[1024,1536]{1,0:T(8,128)(2,1)}, u32[]{:S(2)}, u32[]{:S(2)}) collective-permute-start(bf16[1024,1536]{1,0:T(8,128)(2,1)} %get-tuple-element.357), channel_id=1, source_target_pairs={{0,8},{8,0},{16,24},{24,16},{1,9},{9,1},{17,25},{25,17},{2,10},{10... | collective-permute-start | bytes 9437192 | tf_op jit(solution)/shard_map/ppermute | solution.py:682
  190.1 58.6 %collective-permute-start.16 = (bf16[280,1536]{1,0:T(8,128)(2,1)}, bf16[280,1536]{1,0:T(8,128)(2,1)}, u32[]{:S(2)}, u32[]{:S(2)}) collective-permute-start(bf16[280,1536]{1,0:T(8,128)(2,1)} %dynamic-slice_convert_fusion), channel_id=1, source_target_pairs={{0,4},{1,5},{2,6},{3,7},{4,0},{5,1},{6,2},{7,3},{8,12},{9,13},{10,... | collective-permute-start | bytes 2580488 | tf_op jit(solution)/shard_map/ppermute | solution.py:695
  198.1 54.7 %collective-permute-start.13 = (bf16[2,2,2,192,512]{4,3,0,2,1:T(8,128)(2,1)}, bf16[2,2,2,192,512]{4,3,0,2,1:T(8,128)(2,1)}, u32[]{:S(2)}, u32[]{:S(2)}) collective-permute-start(bf16[2,2,2,192,512]{4,3,0,2,1:T(8,128)(2,1)} %pad_maximum_fusion.11), channel_id=1, source_target_pairs={{0,1},{1,0},{2,3},{3,2},{4,5},{5,4},{6,7},{7,6},{8,9},{9,8},{10,11... | collective-permute-start | bytes 4718600 | tf_op jit(solution)/shard_map/ppermute | solution.py:695
  200.0 75.7 %collective-permute-start.14 = (bf16[2,2,192,608]{3,2,0,1:T(8,128)(2,1)S(1)}, bf16[2,2,192,608]{3,2,0,1:T(8,128)(2,1)S(1)}, u32[]{:S(2)}, u32[]{:S(2)}) collective-permute-start(bf16[2,2,192,608]{3,2,0,1:T(8,128)(2,1)S(1)} %pad_maximum_fusion.14), channel_id=1, source_target_pairs={{0,4},{1,5},{2,6},{3,7},{4,0},{5,1},{6,2},{7,3},{8,12},{9,13},{10,... | collective-permute-start | bytes 2801672 | tf_op jit(solution)/shard_map/ppermute | solution.py:695
  277.5 52.8 %collective-permute-start.18 = (bf16[2,2,2,192,608]{4,3,0,2,1:T(8,128)(2,1)}, bf16[2,2,2,192,608]{4,3,0,2,1:T(8,128)(2,1)}, u32[]{:S(2)}, u32[]{:S(2)}) collective-permute-start(bf16[2,2,2,192,608]{4,3,0,2,1:T(8,128)(2,1)} %pad_maximum_fusion.7), channel_id=1, source_target_pairs={{0,1},{1,0},{2,3},{3,2},{4,5},{5,4},{6,7},{7,6},{8,9},{9,8},{10,11... | collective-permute-start | bytes 5603336 | tf_op jit(solution)/shard_map/ppermute | solution.py:695
  342.1 232.6 %reduce-scatter.5.cloned.1.call-start = ((), (), s32[]{:S(2)}) async-start(), calls=%async_computation.5 | async-start | bytes 2359296 | tf_op jit(solution)/shard_map/reduce_scatter | solution.py:1097
  433.3 62.8 %collective-permute-start.27 = (bf16[2,152,1536]{2,1,0:T(8,128)(2,1)}, bf16[2,152,1536]{2,1,0:T(8,128)(2,1)}, u32[]{:S(2)}, u32[]{:S(2)}) collective-permute-start(bf16[2,152,1536]{2,1,0:T(8,128)(2,1)} %get-tuple-element.293), channel_id=1, source_target_pairs={{0,1},{1,0},{2,3},{3,2},{4,5},{5,4},{6,7},{7,6},{8,9},{9,8},{10,11... | collective-permute-start | bytes 2801672 | tf_op jit(solution)/shard_map/ppermute | solution.py:695
  458.0 75.7 %collective-permute-start.38 = (bf16[2,2,2,192,608]{4,3,2,1,0:T(8,128)(2,1)}, bf16[2,2,2,192,608]{4,3,2,1,0:T(8,128)(2,1)}, u32[]{:S(2)}, u32[]{:S(2)}) collective-permute-start(bf16[2,2,2,192,608]{4,3,2,1,0:T(8,128)(2,1)} %get-tuple-element.267), channel_id=1, source_target_pairs={{0,1},{1,0},{2,3},{3,2},{4,5},{5,4},{6,7},{7,6},{8,9},{9,8},{10,11... | collective-permute-start | bytes 5603336 | tf_op jit(solution)/shard_map/ppermute | solution.py:695
  482.0 138.4 %collective-permute-start.24 = (bf16[1024,1536]{1,0:T(8,128)(2,1)}, bf16[1024,1536]{1,0:T(8,128)(2,1)}, u32[]{:S(2)}, u32[]{:S(2)}) collective-permute-start(bf16[1024,1536]{1,0:T(8,128)(2,1)} %slice.383), channel_id=1, source_target_pairs={{0,8},{8,0},{16,24},{24,16},{1,9},{9,1},{17,25},{25,17},{2,10},{10... | collective-permute-start | bytes 9437192 | tf_op jit(solution)/shard_map/ppermute | solution.py:682
  496.1 276.2 %all-gather.12.cloned.1.call-start = ((), (), s32[]{:S(2)}) async-start(), calls=%async_computation.6 | async-start | bytes 4300800 | tf_op jit(solution)/shard_map/all_gather | solution.py:1145
  517.1 61.2 %collective-permute-start.57 = (bf16[2,192,512]{2,1,0:T(8,128)(2,1)}, bf16[2,192,512]{2,1,0:T(8,128)(2,1)}, u32[]{:S(2)}, u32[]{:S(2)}) collective-permute-start(bf16[2,192,512]{2,1,0:T(8,128)(2,1)} %get-tuple-element.323), channel_id=1, source_target_pairs={{0,2},{1,3},{2,0},{3,1},{4,6},{5,7},{6,4},{7,5},{8,10},{9,11},{10,... | collective-permute-start | bytes 1179656 | tf_op jit(solution)/shard_map/ppermute | solution.py:695
  565.2 60.8 %collective-permute-start.39 = (bf16[2,2,192,608]{3,2,1,0:T(8,128)(2,1)}, bf16[2,2,192,608]{3,2,1,0:T(8,128)(2,1)}, u32[]{:S(2)}, u32[]{:S(2)}) collective-permute-start(bf16[2,2,192,608]{3,2,1,0:T(8,128)(2,1)} %get-tuple-element.289), channel_id=1, source_target_pairs={{0,4},{1,5},{2,6},{3,7},{4,0},{5,1},{6,2},{7,3},{8,12},{9,13},{10,... | collective-permute-start | bytes 2801672 | tf_op jit(solution)/shard_map/ppermute | solution.py:695
  572.5 58.0 %collective-permute-start.49 = (bf16[192,384]{1,0:T(8,128)(2,1)}, bf16[192,384]{1,0:T(8,128)(2,1)}, u32[]{:S(2)}, u32[]{:S(2)}) collective-permute-start(bf16[192,384]{1,0:T(8,128)(2,1)} %get-tuple-element.361), channel_id=1, source_target_pairs={{0,4},{1,5},{2,6},{3,7},{4,0},{5,1},{6,2},{7,3},{8,12},{9,13},{10,... | collective-permute-start | bytes 442376 | tf_op jit(solution)/shard_map/ppermute | solution.py:695
  583.7 57.5 %collective-permute-start.58 = (bf16[2,2,192,512]{3,2,1,0:T(8,128)(2,1)}, bf16[2,2,192,512]{3,2,1,0:T(8,128)(2,1)S(1)}, u32[]{:S(2)}, u32[]{:S(2)}) collective-permute-start(bf16[2,2,192,512]{3,2,1,0:T(8,128)(2,1)} %get-tuple-element.320), channel_id=1, source_target_pairs={{0,16},{16,0},{8,24},{24,8},{1,17},{17,1},{9,25},{25,9},{2,18},{18... | collective-permute-start | bytes 2359304 | tf_op jit(solution)/shard_map/ppermute | solution.py:686
  620.2 74.7 %collective-permute-start.63 = (bf16[512,1536]{1,0:T(8,128)(2,1)}, bf16[512,1536]{1,0:T(8,128)(2,1)}, u32[]{:S(2)}, u32[]{:S(2)}) collective-permute-start(bf16[512,1536]{1,0:T(8,128)(2,1)} %get-tuple-element.220), channel_id=1, source_target_pairs={{0,8},{8,0},{16,24},{24,16},{1,9},{9,1},{17,25},{25,17},{2,10},{10... | collective-permute-start | bytes 4718600 | tf_op jit(solution)/shard_map/ppermute | solution.py:682
  640.2 77.5 %collective-permute-start.35 = (bf16[128,1536]{1,0:T(8,128)(2,1)}, bf16[128,1536]{1,0:T(8,128)(2,1)}, u32[]{:S(2)}, u32[]{:S(2)}) collective-permute-start(bf16[128,1536]{1,0:T(8,128)(2,1)} %get-tuple-element.276), channel_id=1, source_target_pairs={{0,2},{1,3},{2,0},{3,1},{4,6},{5,7},{6,4},{7,5},{8,10},{9,11},{10,... | collective-permute-start | bytes 1179656 | tf_op jit(solution)/shard_map/ppermute | solution.py:695
  640.3 77.4 %collective-permute-start.36 = (bf16[128,1536]{1,0:T(8,128)(2,1)}, bf16[128,1536]{1,0:T(8,128)(2,1)}, u32[]{:S(2)}, u32[]{:S(2)}) collective-permute-start(bf16[128,1536]{1,0:T(8,128)(2,1)} %get-tuple-element.275), channel_id=1, source_target_pairs={{0,16},{16,0},{8,24},{24,8},{1,17},{17,1},{9,25},{25,9},{2,18},{18... | collective-permute-start | bytes 1179656 | tf_op jit(solution)/shard_map/ppermute | solution.py:686
  697.8 68.6 %collective-permute-start.64 = (bf16[256,1536]{1,0:T(8,128)(2,1)}, bf16[256,1536]{1,0:T(8,128)(2,1)}, u32[]{:S(2)}, u32[]{:S(2)}) collective-permute-start(bf16[256,1536]{1,0:T(8,128)(2,1)} %fusion.18), channel_id=1, source_target_pairs={{0,16},{16,0},{8,24},{24,8},{1,17},{17,1},{9,25},{25,9},{2,18},{18... | collective-permute-start | bytes 2359304 | tf_op jit(solution)/shard_map/ppermute | solution.py:686
  (182 other events, 2023.8 us)
Sparse Core Ops, SparseCore 0:
  11.5 39.8 all-gather.13
  55.4 34.8 all-gather.15
  96.3 65.2 all-gather.7
  180.1 97.6 all-gather.9
  342.3 53.6 reduce-scatter.2
  496.2 60.0 reduce-scatter.4
  580.3 43.5 all-gather.11

commit v11 on v10

--- a/solution.py
+++ b/solution.py
@@ -932,7 +932,9 @@
     dy_second = swap_cross(dy_over[half:])
     mixed_cross = swap_cross(mixed_far)
     mixed_core = swap_core(jnp.stack([mixed_core, mixed_cross[1]]))
-    mixed_core = after(mixed_core, dy_over)
+    pair_a = team_pair(picked_a[0], after(got_a, mixed_own))
+    pair_a_got = swap_blk(pair_a, bits[0])
+    mixed_core = after(mixed_core, (dy_over, pair_a_got))
     query, packed_kv = pack(ids, mixed_own, mixed_cross, mixed_core)
     key_value = packed_kv.reshape(rows_here, block_len, 2 * KVD)
     kv_all = gather_ring(key_value)
@@ -961,17 +963,15 @@
         return values
 
     got_b = swap_blk(after(picked_b[1], mixed_own), team)
-    pair_a = team_pair(picked_a[0], after(got_a, mixed_own))
-    pair_a_got = swap_blk(pair_a, bits[0])
-    pair_a_got, got_b = after((pair_a_got, got_b), kv_all)
-    kv_all = after(kv_all, (pair_a_got, got_b, dy_first, dy_second))
+    pair_a = place(pair_a, after(pair_a_got, packed_kv), [team], bits[0], 1)
+    gate_up_a = lows_of(pair_a, [bits[0], team], 1).reshape(2, D, -1)
+    got_b = after(got_b, kv_all)
+    kv_all = after(kv_all, (gate_up_a, got_b, dy_first, dy_second))
     down_got = swap_blk(after(down_here, kv_all), bits[0])
     dy_chip = jnp.concatenate([dy_low, dy_cross, dy_over, dy_first, dy_second])
     dy_team = jnp.concatenate([dy_chip, swap_core(dy_chip)])
-    pair_a = place(pair_a, pair_a_got, [team], bits[0], 1)
-    gate_up_a = lows_of(pair_a, [bits[0], team], 1).reshape(2, D, -1)
     pair_b = team_pair(picked_b[0], got_b)
-    pair_b_got = swap_blk(after(pair_b, pair_a_got), bits[0])
+    pair_b_got = swap_blk(after(pair_b, down_got), bits[0])
     out_ring = after(out_ring, packed_kv)
     out_strip = jnp.concatenate([out_ring[ring.index(b)] for b in range(blk_count)])
     out_cross = swap_cross(out_strip)
@@ -982,6 +982,7 @@
     flat = wide(flat_low)
     resid = flat + jnp.dot(att_in, out_full, preferred_element_type=jnp.float32)
     h_two = low(norm_apply(resid, gain_two))
+    h_two = after(h_two, down_got)
     down_here = place(down_here, down_got, [], bits[0])
     down_here = lows_of(down_here, [bits[0]]).reshape(2 * blk_count // 4, quarter, D)
     down_a = down_here[:, :size_first].reshape(widths[0], D)
@@ -1164,10 +1165,6 @@
         steps_out = part_sent(part_sum(*after(steps_out, anchor)), i, bits[i])
     share_out = part_sum(*after(steps_out, kv_grad))
 
-    own_b = columns_last(*third_b)
-    cross_b = swap_cross(own_b)
-    near_b = jnp.stack([own_b, cross_b])
-    near_b = jnp.concatenate([near_b, swap_core(near_b)])
     grad_out = jnp.concatenate(gather_grp(share_out), axis=1)
     query_parts = gather_grp(share_query)
     key_parts = gather_grp(share_kv)
@@ -1193,8 +1190,21 @@
     factor = jnp.minimum(1.0, CLIP_NORM / (grad_norm + 1e-06))
     out_chip = chip_sum(out_part, after(out_came, kv_grad))
     out_far = scatter_far(out_chip)
-    factor = after(factor, (out_chip, cross_b, near_a))
-
+    factor = after(factor, (out_chip, near_a))
+
+    new_first_attend, new_second_attend, new_attend = adam_step(
+        w_attend, factor * wide(grad_attend), first_attend, second_attend, RATE_ATTEND, WEIGHT_DECAY
+    )
+    new_first_out, new_second_out, new_out = adam_step(
+        w_out, factor * wide(grad_out), first_out, second_out, RATE_OUT, WEIGHT_DECAY
+    )
+    new_first_down, new_second_down, new_down = adam_step(
+        w_down, factor * wide(grad_down), first_down, second_down, RATE_DOWN, WEIGHT_DECAY
+    )
+    own_b = columns_last(*third_b)
+    cross_b = after(swap_cross(own_b), new_down)
+    near_b = jnp.stack([own_b, cross_b])
+    near_b = jnp.concatenate([near_b, swap_core(near_b)])
     new_first_gate, new_second_gate, new_gate = adam_columns(
         0, ids, factor[None], near_a, near_b, w_gate, first_gate, second_gate, blk_count, RATE_GATE, WEIGHT_DECAY
     )
@@ -1206,15 +1216,6 @@
     d_flat_norm, unused_gain = norm_back_one(d_hone)
     grad_tokens = low(d_resid + d_flat_norm)
 
-    new_first_attend, new_second_attend, new_attend = adam_step(
-        w_attend, factor * wide(grad_attend), first_attend, second_attend, RATE_ATTEND, WEIGHT_DECAY
-    )
-    new_first_out, new_second_out, new_out = adam_step(
-        w_out, factor * wide(grad_out), first_out, second_out, RATE_OUT, WEIGHT_DECAY
-    )
-    new_first_down, new_second_down, new_down = adam_step(
-        w_down, factor * wide(grad_down), first_down, second_down, RATE_DOWN, WEIGHT_DECAY
-    )
     new_first_small, new_second_small, new_small = adam_step(
         small_params, factor * share_vector, first_small, second_small, RATE_VECTOR, 0.0
     )

time: 805 us -> 782 us (0.971)
  waiting for transfers between devices: 295 us -> 278 us
  starting transfers between devices: 87.9 us -> 74.4 us
    ppermute x20, waiting for transfers between devices: 49.9 us -> 35.2 us  [swap_cross(): return lax.ppermute(values, 'grp', CROSS)]
    ppermute x34, starting transfers between devices: 59.4 us -> 48.4 us  [swap_blk(): return lax.ppermute(values, 'blk', [(i, i ^ bit) for i in range(count)])]
    unnamed x275 -> x267, local copies, waits for them, and re-layouts: 34.7 us -> 41.1 us
  transfers between devices with their start and end apart: 78 -> 78, of which waited for: 31 -> 29; matrix products, arithmetic and copies ran while one was open for 19% -> 22% of each run, Pallas kernels for 22% -> 23%
where the time goes in v11:
time: 782 us; the launch traced here: 773 us
  waiting for transfers between devices  278 us (36%)
  Pallas kernels  182 us (23%)
  other arithmetic  118 us (15%)
  local copies, waits for them, and re-layouts  90.2 us (12%)
  starting transfers between devices  74.4 us (10%)
  between operations  22.1 us (3%)
  matrix products  8.63 us (1%)
    ppermute x34, waiting for transfers between devices, swap_blk(): return lax.ppermute(values, 'blk', [(i, i ^ bit) for i in range(count)])  240 us
    pallas_call x2, Pallas kernels, middle(): pl.pallas_call(functools.partial(middle_body, prev is not None), grid_spe...  60.6 us
    ppermute x34, starting transfers between devices, swap_blk(): return lax.ppermute(values, 'blk', [(i, i ^ bit) for i in range(count)])  48.4 us
    unnamed x267, local copies, waits for them, and re-layouts  41.1 us
    pallas_call x2, Pallas kernels, adam_columns(): pl.pallas_call(functools.partial(adam_body, blk_count, rate, decay), grid...  35.5 us
    ppermute x20, waiting for transfers between devices, swap_cross(): return lax.ppermute(values, 'grp', CROSS)  35.2 us
    convert_element_type x21, other arithmetic, low(): return values.astype(jnp.bfloat16)  26.8 us
    sub x4, other arithmetic, adam_step(): weight - rate * (first_hat / (jnp.sqrt(second_hat) + ADAM_EPS) + decay *...  24.3 us
  transfers between devices with their start and end apart: 78, of which 29 were waited for; matrix products, arithmetic and copies ran while one was open for 22% of the time, Pallas kernels for 23%

profile of v11, /device:TPU:0, one launch (start us, length us, event | category | flops | bytes accessed | tf_op | source)
XLA Modules:
  0.0 773.1 jit_solution(778374148541366763)
XLA Ops:
  25.1 17.3 %collective-permute-done.1 = bf16[2,192,512]{2,1,0:T(8,128)(2,1)S(1)} collective-permute-done((bf16[2,192,512]{2,1,0:T(8,128)(2,1)S(1)}, bf16[2,192,512]{2,1,0:T(8,128)(2,1)S(1)}, u32[]{:S(2)}, u32[]{:S(2)}) %collective-permute-start.1) | collective-permute-done | bytes 393248 | tf_op jit(solution)/shard_map/ppermute | solution.py:695
  42.4 8.8 %collective-permute-done.2 = bf16[256,1536]{1,0:T(8,128)(2,1)S(1)} collective-permute-done((bf16[256,1536]{1,0:T(8,128)(2,1)S(1)}, bf16[256,1536]{1,0:T(8,128)(2,1)S(1)}, u32[]{:S(2)}, u32[]{:S(2)}) %collective-permute-start.2) | collective-permute-done | bytes 786464 | tf_op jit(solution)/shard_map/ppermute | solution.py:686
  57.4 7.6 mix.1
  69.7 9.4 %collective-permute-done.4.cross_ref = bf16[2,256,512]{2,1,0:T(8,128)(2,1)S(1)} collective-permute-done((bf16[2,256,512]{2,1,0:T(8,128)(2,1)S(1)}, bf16[2,256,512]{2,1,0:T(8,128)(2,1)S(1)}, u32[]{:S(2)}, u32[]{:S(2)}) %collective-permute-start.4) | collective-permute-done | bytes 524320 | tf_op jit(solution)/shard_map/ppermute | solution.py:686
  79.2 17.0 %collective-permute-done.6 = bf16[256,1536]{1,0:T(8,128)(2,1)S(1)} collective-permute-done((bf16[256,1536]{1,0:T(8,128)(2,1)}, bf16[256,1536]{1,0:T(8,128)(2,1)S(1)}, u32[]{:S(2)}, u32[]{:S(2)}) %collective-permute-start.6) | collective-permute-done | bytes 786464 | tf_op jit(solution)/shard_map/ppermute | solution.py:695
  96.2 17.0 %collective-permute-done.7 = bf16[2,2,192,512]{3,2,0,1:T(8,128)(2,1)S(1)} collective-permute-done((bf16[2,2,192,512]{3,2,0,1:T(8,128)(2,1)S(1)}, bf16[2,2,192,512]{3,2,0,1:T(8,128)(2,1)S(1)}, u32[]{:S(2)}, u32[]{:S(2)}) %collective-permute-start.7) | collective-permute-done | bytes 786464 | tf_op jit(solution)/shard_map/ppermute | solution.py:695
  139.3 34.2 %collective-permute-done.8 = bf16[2,2,2,192,512]{4,3,0,2,1:T(8,128)(2,1)} collective-permute-done((bf16[2,2,2,192,512]{4,3,0,2,1:T(8,128)(2,1)}, bf16[2,2,2,192,512]{4,3,0,2,1:T(8,128)(2,1)}, u32[]{:S(2)}, u32[]{:S(2)}) %collective-permute-start.8) | collective-permute-done | bytes 1572896 | tf_op jit(solution)/shard_map/ppermute | solution.py:695
  196.0 28.2 %collective-permute-done.14 = bf16[280,1536]{1,0:T(8,128)(2,1)} collective-permute-done((bf16[280,1536]{1,0:T(8,128)(2,1)}, bf16[280,1536]{1,0:T(8,128)(2,1)}, u32[]{:S(2)}, u32[]{:S(2)}) %collective-permute-start.14) | collective-permute-done | bytes 860192 | tf_op jit(solution)/shard_map/ppermute | solution.py:695
  239.5 40.5 %collective-permute-done.15 = bf16[2,2,192,608]{3,2,0,1:T(8,128)(2,1)S(1)} collective-permute-done((bf16[2,2,192,608]{3,2,0,1:T(8,128)(2,1)S(1)}, bf16[2,2,192,608]{3,2,0,1:T(8,128)(2,1)S(1)}, u32[]{:S(2)}, u32[]{:S(2)}) %collective-permute-start.15) | collective-permute-done | bytes 933920 | tf_op jit(solution)/shard_map/ppermute | solution.py:695
  291.2 23.2 %middle.2 = (bf16[2048,512]{1,0:T(8,128)(2,1)S(1)}, bf16[2048,512]{1,0:T(8,128)(2,1)S(1)}, bf16[2048,512]{1,0:T(8,128)(2,1)}, bf16[2048,1536]{1,0:T(8,128)(2,1)}) custom-call(s32[8]{0:T(128)S(1)} %stack.301.order, bf16[2048,1536]{1,0:T(8,128)(2,1)} %all-gather.10.cloned.1.call-done.h_ref, bf16[2048,1536]{1,0:T(8,128)(2,1)} %constant_dynamic-update-slice_fusion.12.dy_ref, ...), custom_call_target="tpu_custom_call" | custom-call | flops 1000 | bytes 1000 | tf_op jit(solution)/shard_map/middle/pallas_call | solution.py:370
  314.4 12.2 %collective-permute-done.18 = bf16[2,2,2,192,608]{4,3,0,2,1:T(8,128)(2,1)} collective-permute-done((bf16[2,2,2,192,608]{4,3,0,2,1:T(8,128)(2,1)}, bf16[2,2,2,192,608]{4,3,0,2,1:T(8,128)(2,1)}, u32[]{:S(2)}, u32[]{:S(2)}) %collective-permute-start.18) | collective-permute-done | bytes 1867808 | tf_op jit(solution)/shard_map/ppermute | solution.py:695
  342.2 10.1 %two_grads.2 = bf16[2,1536,512]{2,1,0:T(8,128)(2,1)} custom-call(bf16[2048,1536]{1,0:T(8,128)(2,1)} %all-gather.10.cloned.1.call-done.h_ref, bf16[2048,512]{1,0:T(8,128)(2,1)S(1)} %copy-done.21, bf16[2048,512]{1,0:T(8,128)(2,1)S(1)} %copy-done.22), custom_call_target="tpu_custom_call" | custom-call | flops 1000 | bytes 1000 | tf_op jit(solution)/shard_map/two_grads/pallas_call | solution.py:403
  358.6 37.4 %middle.3 = (bf16[2048,608]{1,0:T(8,128)(2,1)S(1)}, bf16[2048,608]{1,0:T(8,128)(2,1)}, bf16[2048,608]{1,0:T(8,128)(2,1)}, bf16[2048,1536]{1,0:T(8,128)(2,1)}) custom-call(s32[8]{0:T(128)S(1)} %stack.301.order, bf16[2048,1536]{1,0:T(8,128)(2,1)} %all-gather.10.cloned.1.call-done.h_ref, bf16[2048,1536]{1,0:T(8,128)(2,1)} %constant_dynamic-update-slice_fusion.12.dy_ref, ...), custom_call_target="tpu_custom_call" | custom-call | flops 1000 | bytes 1000 | tf_op jit(solution)/shard_map/middle/pallas_call | solution.py:370
  423.4 13.5 %two_grads.3 = bf16[2,1536,608]{2,1,0:T(8,128)(2,1)} custom-call(bf16[2048,1536]{1,0:T(8,128)(2,1)} %all-gather.10.cloned.1.call-done.h_ref, bf16[2048,608]{1,0:T(8,128)(2,1)S(1)} %copy-done.18, bf16[2048,608]{1,0:T(8,128)(2,1)S(1)} %copy-done.19), custom_call_target="tpu_custom_call" | custom-call | flops 1000 | bytes 1000 | tf_op jit(solution)/shard_map/two_grads/pallas_call | solution.py:403
  452.1 11.6 %down.1 = bf16[2048,1536]{1,0:T(8,128)(2,1)} custom-call(bf16[2048,512]{1,0:T(8,128)(2,1)S(1)} %copy-done.6, bf16[2048,608]{1,0:T(8,128)(2,1)} %copy-done.1, bf16[512,1536]{1,0:T(8,128)(2,1)S(1)} %bitcast.413, bf16[608,1536]{1,0:T(8,128)(2,1)S(1)} %bitcast.411), custom_call_target="tpu_custom_call" | custom-call | flops 1000 | bytes 1000 | tf_op jit(solution)/shard_map/down/pallas_call | solution.py:443
  473.6 8.0 %attend_back.1 = (bf16[256,1536]{1,0:T(8,128)(2,1)S(1)}, bf16[8,2,128,512]{3,2,1,0:T(8,128)(2,1)}) custom-call(s32[3]{0:T(128)S(1)} %copy-done.37, bf16[256,1536]{1,0:T(8,128)(2,1)S(1)} %copy-done.13, bf16[8,2,128,512]{3,2,1,0:T(8,128)(2,1)} %all-gather.8.cloned.1.call-done.k_ref.v_ref, bf16[8,2,128,512]{3,2,1,0:T(8,128)(2,1)} %all-gather.8.cloned.1.call-done.k_ref.v_ref, ...), custom_call_target="tpu_custom_call" | custom-call | flops 1000 | bytes 1000 | tf_op jit(solution)/shard_map/attend_back/pallas_call | solution.py:311
  510.5 10.1 %collective-permute-done.28 = bf16[152,1536]{1,0:T(8,128)(2,1)S(1)} collective-permute-done((bf16[152,1536]{1,0:T(8,128)(2,1)S(1)}, bf16[152,1536]{1,0:T(8,128)(2,1)S(1)}, u32[]{:S(2)}, u32[]{:S(2)}) %collective-permute-start.28) | collective-permute-done | bytes 466976 | tf_op jit(solution)/shard_map/ppermute | solution.py:695
  533.4 15.0 %collective-permute-done.47 = bf16[2,2,192,384]{3,2,1,0:T(8,128)(2,1)S(1)} collective-permute-done((bf16[2,2,192,384]{3,2,1,0:T(8,128)(2,1)S(1)}, bf16[2,2,192,384]{3,2,1,0:T(8,128)(2,1)S(1)}, u32[]{:S(2)}, u32[]{:S(2)}) %collective-permute-start.47) | collective-permute-done | bytes 589856 | tf_op jit(solution)/shard_map/ppermute | solution.py:695
  571.8 8.8 %kv_grad.1 = (bf16[8,208,128]{2,1,0:T(8,128)(2,1)S(1)}, bf16[512,1536]{1,0:T(8,128)(2,1)S(1)}, bf16[512,1536]{1,0:T(8,128)(2,1)}) custom-call(bf16[256,128]{1,0:T(8,128)(2,1)S(1)} %get-tuple-element.182.self_ref, bf16[2,256,128]{2,1,0:T(8,128)(2,1)S(1)} %collective-permute-done.29.cross_ref, bf16[2,256,128]{2,1,0:T(8,128)(2,1)S(1)} %collective-permute-done.30.core_ref, ...), custom_call_target="tpu_custom_call" | custom-call | flops 1000 | bytes 1000 | tf_op jit(solution)/shard_map/kv_grad/pallas_call | solution.py:653
  594.0 12.3 %collective-permute-done.34 = bf16[2,208,128]{2,1,0:T(8,128)(2,1)S(1)} collective-permute-done((bf16[2,208,128]{2,1,0:T(8,128)(2,1)S(1)}, bf16[2,208,128]{2,1,0:T(8,128)(2,1)S(1)}, u32[]{:S(2)}, u32[]{:S(2)}) %collective-permute-start.34) | collective-permute-done | bytes 106528 | tf_op jit(solution)/shard_map/ppermute | solution.py:695
  631.9 16.3 %collective-permute-done.37 = bf16[208,128]{1,0:T(8,128)(2,1)S(1)} collective-permute-done((bf16[208,128]{1,0:T(8,128)(2,1)S(1)}, bf16[208,128]{1,0:T(8,128)(2,1)S(1)}, u32[]{:S(2)}, u32[]{:S(2)}) %collective-permute-start.37) | collective-permute-done | bytes 53280 | tf_op jit(solution)/shard_map/ppermute | solution.py:695
  689.2 17.0 %multiply_subtract_fusion = (f32[1120,1536]{1,0:T(8,128)}, f32[1120,1536]{1,0:T(8,128)}, f32[1120,1536]{1,0:T(8,128)}) fusion(f32[1120,1536]{1,0:T(8,128)} %param.30, bf16[1120,1536]{1,0:T(8,128)(2,1)} %all-gather.12.cloned.1.call-done, f32[]{:T(128)} %min.3, f32[1120,1536]{1,0:T(8,128)} %param.36, f32[1120,1536]{1,0:T(8,128)} %param.42), kind=kLoop, calls=%fused_computation.2 | loop fusion | flops 29245440 | bytes 44728324 | tf_op jit(solution)/shard_map/sub | solution.py:67
  721.8 17.6 %adam_columns.2 = (f32[192,8960]{1,0:T(8,128)}, f32[192,8960]{1,0:T(8,128)}, f32[192,8960]{1,0:T(8,128)}) custom-call(s32[2]{0:T(128)S(1)} %pad_add_fusion.2.ids, f32[1]{0:T(128)} %bitcast.127.factor_ref, bf16[4,2,2,192,512]{4,3,2,1,0:T(8,128)(2,1)S(1)} %pad_maximum_fusion.5.first_ref, bf16[4,2,2,192,608]{4,3,2,1,0:T(8,128)(2,1)} %pad_maximum_fusion.2.second_ref, ...), custom_call_target="tpu_custom_call" | custom-call | flops 1000 | bytes 1000 | tf_op jit(solution)/shard_map/adam_columns/pallas_call | solution.py:155
  739.4 17.9 %adam_columns.3 = (f32[192,8960]{1,0:T(8,128)}, f32[192,8960]{1,0:T(8,128)}, f32[192,8960]{1,0:T(8,128)}) custom-call(s32[2]{0:T(128)S(1)} %pad_add_fusion.2.ids, f32[1]{0:T(128)} %bitcast.127.factor_ref, bf16[4,2,2,192,512]{4,3,2,1,0:T(8,128)(2,1)S(1)} %pad_maximum_fusion.5.first_ref, bf16[4,2,2,192,608]{4,3,2,1,0:T(8,128)(2,1)} %pad_maximum_fusion.2.second_ref, ...), custom_call_target="tpu_custom_call" | custom-call | flops 1000 | bytes 1000 | tf_op jit(solution)/shard_map/adam_columns/pallas_call | solution.py:155
  (607 shorter events, 340.0 us)
Async XLA Ops:
  11.4 107.6 %all-gather.16.cloned.1.call-start = ((), (), s32[]{:S(2)}) async-start(), calls=%async_computation.8 | async-start | bytes 1327104 | tf_op jit(solution)/shard_map/all_gather | solution.py:808
  55.3 122.1 %all-gather.8.cloned.1.call-start = ((), (), s32[]{:S(2)}) async-start(), calls=%async_computation.2 | async-start | bytes 2359296 | tf_op jit(solution)/shard_map/all_gather | solution.py:808
  67.0 46.2 %collective-permute-start.7 = (bf16[2,2,192,512]{3,2,0,1:T(8,128)(2,1)S(1)}, bf16[2,2,192,512]{3,2,0,1:T(8,128)(2,1)S(1)}, u32[]{:S(2)}, u32[]{:S(2)}) collective-permute-start(bf16[2,2,192,512]{3,2,0,1:T(8,128)(2,1)S(1)} %pad_maximum_fusion.19), channel_id=1, source_target_pairs={{0,4},{1,5},{2,6},{3,7},{4,0},{5,1},{6,2},{7,3},{8,12},{9,13},{10,... | collective-permute-start | bytes 2359304 | tf_op jit(solution)/shard_map/ppermute | solution.py:695
  114.6 176.5 %all-gather.10.cloned.1.call-start = ((), (), s32[]{:S(2)}) async-start(), calls=%async_computation.3 | async-start | bytes 7077888 | tf_op jit(solution)/shard_map/all_gather | solution.py:990
  117.4 56.1 %collective-permute-start.8 = (bf16[2,2,2,192,512]{4,3,0,2,1:T(8,128)(2,1)}, bf16[2,2,2,192,512]{4,3,0,2,1:T(8,128)(2,1)}, u32[]{:S(2)}, u32[]{:S(2)}) collective-permute-start(bf16[2,2,2,192,512]{4,3,0,2,1:T(8,128)(2,1)} %pad_maximum_fusion.11), channel_id=1, source_target_pairs={{0,1},{1,0},{2,3},{3,2},{4,5},{5,4},{6,7},{7,6},{8,9},{9,8},{10,11... | collective-permute-start | bytes 4718600 | tf_op jit(solution)/shard_map/ppermute | solution.py:695
  131.7 45.7 %collective-permute-start.12 = (bf16[1536,384]{1,0:T(8,128)(2,1)}, bf16[1536,384]{1,0:T(8,128)(2,1)}, u32[]{:S(2)}, u32[]{:S(2)}) collective-permute-start(bf16[1536,384]{1,0:T(8,128)(2,1)} %bitcast_dynamic-update-slice_fusion), channel_id=1, source_target_pairs={{0,16},{16,0},{8,24},{24,8},{1,17},{17,1},{9,25},{25,9},{2,18},{18... | collective-permute-start | bytes 3538952 | tf_op jit(solution)/shard_map/ppermute | solution.py:686
  224.2 174.2 %reduce-scatter.3.cloned.1.call-start = ((), (), s32[]{:S(2)}) async-start(), calls=%async_computation.4 | async-start | bytes 1966080 | tf_op jit(solution)/shard_map/reduce_scatter | solution.py:997
  231.6 51.6 %collective-permute-start.16 = (bf16[1024,1536]{1,0:T(8,128)(2,1)}, bf16[1024,1536]{1,0:T(8,128)(2,1)}, u32[]{:S(2)}, u32[]{:S(2)}) collective-permute-start(bf16[1024,1536]{1,0:T(8,128)(2,1)} %get-tuple-element.361), channel_id=1, source_target_pairs={{0,8},{8,0},{16,24},{24,16},{1,9},{9,1},{17,25},{25,17},{2,10},{10... | collective-permute-start | bytes 9437192 | tf_op jit(solution)/shard_map/ppermute | solution.py:682
  238.1 49.1 %collective-permute-start.17 = (bf16[2,280,1536]{2,1,0:T(8,128)(2,1)}, bf16[2,280,1536]{2,1,0:T(8,128)(2,1)}, u32[]{:S(2)}, u32[]{:S(2)}) collective-permute-start(bf16[2,280,1536]{2,1,0:T(8,128)(2,1)} %pad_maximum_fusion.9), channel_id=1, source_target_pairs={{0,1},{1,0},{2,3},{3,2},{4,5},{5,4},{6,7},{7,6},{8,9},{9,8},{10,11... | collective-permute-start | bytes 5160968 | tf_op jit(solution)/shard_map/ppermute | solution.py:695
  338.4 222.0 %reduce-scatter.5.cloned.1.call-start = ((), (), s32[]{:S(2)}) async-start(), calls=%async_computation.5 | async-start | bytes 2359296 | tf_op jit(solution)/shard_map/reduce_scatter | solution.py:1098
  422.3 59.4 %collective-permute-start.27 = (bf16[2,152,1536]{2,1,0:T(8,128)(2,1)}, bf16[2,152,1536]{2,1,0:T(8,128)(2,1)}, u32[]{:S(2)}, u32[]{:S(2)}) collective-permute-start(bf16[2,152,1536]{2,1,0:T(8,128)(2,1)} %get-tuple-element.297), channel_id=1, source_target_pairs={{0,1},{1,0},{2,3},{3,2},{4,5},{5,4},{6,7},{7,6},{8,9},{9,8},{10,11... | collective-permute-start | bytes 2801672 | tf_op jit(solution)/shard_map/ppermute | solution.py:695
  446.9 74.8 %collective-permute-start.38 = (bf16[2,2,2,192,608]{4,3,2,1,0:T(8,128)(2,1)}, bf16[2,2,2,192,608]{4,3,2,1,0:T(8,128)(2,1)}, u32[]{:S(2)}, u32[]{:S(2)}) collective-permute-start(bf16[2,2,2,192,608]{4,3,2,1,0:T(8,128)(2,1)} %get-tuple-element.271), channel_id=1, source_target_pairs={{0,1},{1,0},{2,3},{3,2},{4,5},{5,4},{6,7},{7,6},{8,9},{9,8},{10,11... | collective-permute-start | bytes 5603336 | tf_op jit(solution)/shard_map/ppermute | solution.py:695
  467.6 138.8 %collective-permute-start.24 = (bf16[1024,1536]{1,0:T(8,128)(2,1)}, bf16[1024,1536]{1,0:T(8,128)(2,1)}, u32[]{:S(2)}, u32[]{:S(2)}) collective-permute-start(bf16[1024,1536]{1,0:T(8,128)(2,1)} %slice.383), channel_id=1, source_target_pairs={{0,8},{8,0},{16,24},{24,16},{1,9},{9,1},{17,25},{25,17},{2,10},{10... | collective-permute-start | bytes 9437192 | tf_op jit(solution)/shard_map/ppermute | solution.py:682
  481.7 207.5 %all-gather.12.cloned.1.call-start = ((), (), s32[]{:S(2)}) async-start(), calls=%async_computation.6 | async-start | bytes 4300800 | tf_op jit(solution)/shard_map/all_gather | solution.py:1146
  503.1 62.7 %collective-permute-start.56 = (bf16[2,192,512]{2,1,0:T(8,128)(2,1)}, bf16[2,192,512]{2,1,0:T(8,128)(2,1)}, u32[]{:S(2)}, u32[]{:S(2)}) collective-permute-start(bf16[2,192,512]{2,1,0:T(8,128)(2,1)} %get-tuple-element.327), channel_id=1, source_target_pairs={{0,2},{1,3},{2,0},{3,1},{4,6},{5,7},{6,4},{7,5},{8,10},{9,11},{10,... | collective-permute-start | bytes 1179656 | tf_op jit(solution)/shard_map/ppermute | solution.py:695
  552.2 59.8 %collective-permute-start.39 = (bf16[2,2,192,608]{3,2,1,0:T(8,128)(2,1)}, bf16[2,2,192,608]{3,2,1,0:T(8,128)(2,1)}, u32[]{:S(2)}, u32[]{:S(2)}) collective-permute-start(bf16[2,2,192,608]{3,2,1,0:T(8,128)(2,1)} %get-tuple-element.293), channel_id=1, source_target_pairs={{0,4},{1,5},{2,6},{3,7},{4,0},{5,1},{6,2},{7,3},{8,12},{9,13},{10,... | collective-permute-start | bytes 2801672 | tf_op jit(solution)/shard_map/ppermute | solution.py:695
  560.1 56.4 %collective-permute-start.49 = (bf16[192,384]{1,0:T(8,128)(2,1)}, bf16[192,384]{1,0:T(8,128)(2,1)}, u32[]{:S(2)}, u32[]{:S(2)}) collective-permute-start(bf16[192,384]{1,0:T(8,128)(2,1)} %get-tuple-element.365), channel_id=1, source_target_pairs={{0,4},{1,5},{2,6},{3,7},{4,0},{5,1},{6,2},{7,3},{8,12},{9,13},{10,... | collective-permute-start | bytes 442376 | tf_op jit(solution)/shard_map/ppermute | solution.py:695
  571.1 56.2 %collective-permute-start.57 = (bf16[2,2,192,512]{3,2,1,0:T(8,128)(2,1)S(1)}, bf16[2,2,192,512]{3,2,1,0:T(8,128)(2,1)S(1)}, u32[]{:S(2)}, u32[]{:S(2)}) collective-permute-start(bf16[2,2,192,512]{3,2,1,0:T(8,128)(2,1)S(1)} %get-tuple-element.324), channel_id=1, source_target_pairs={{0,16},{16,0},{8,24},{24,8},{1,17},{17,1},{9,25},{25,9},{2,18},{18... | collective-permute-start | bytes 2359304 | tf_op jit(solution)/shard_map/ppermute | solution.py:686
  606.3 72.9 %collective-permute-start.63 = (bf16[512,1536]{1,0:T(8,128)(2,1)}, bf16[512,1536]{1,0:T(8,128)(2,1)}, u32[]{:S(2)}, u32[]{:S(2)}) collective-permute-start(bf16[512,1536]{1,0:T(8,128)(2,1)} %get-tuple-element.224), channel_id=1, source_target_pairs={{0,8},{8,0},{16,24},{24,16},{1,9},{9,1},{17,25},{25,17},{2,10},{10... | collective-permute-start | bytes 4718600 | tf_op jit(solution)/shard_map/ppermute | solution.py:682
  627.3 58.3 %collective-permute-start.35 = (bf16[128,1536]{1,0:T(8,128)(2,1)}, bf16[128,1536]{1,0:T(8,128)(2,1)}, u32[]{:S(2)}, u32[]{:S(2)}) collective-permute-start(bf16[128,1536]{1,0:T(8,128)(2,1)} %get-tuple-element.280), channel_id=1, source_target_pairs={{0,2},{1,3},{2,0},{3,1},{4,6},{5,7},{6,4},{7,5},{8,10},{9,11},{10,... | collective-permute-start | bytes 1179656 | tf_op jit(solution)/shard_map/ppermute | solution.py:695
  630.9 53.0 %collective-permute-start.58 = (bf16[2,2,2,192,512]{4,3,2,1,0:T(8,128)(2,1)}, bf16[2,2,2,192,512]{4,3,2,1,0:T(8,128)(2,1)}, u32[]{:S(2)}, u32[]{:S(2)}) collective-permute-start(bf16[2,2,2,192,512]{4,3,2,1,0:T(8,128)(2,1)} %pad_maximum_fusion.13), channel_id=1, source_target_pairs={{0,8},{8,0},{16,24},{24,16},{1,9},{9,1},{17,25},{25,17},{2,10},{10... | collective-permute-start | bytes 4718600 | tf_op jit(solution)/shard_map/ppermute | solution.py:682
  682.9 74.4 %collective-permute-start.64 = (bf16[256,1536]{1,0:T(8,128)(2,1)}, bf16[256,1536]{1,0:T(8,128)(2,1)}, u32[]{:S(2)}, u32[]{:S(2)}) collective-permute-start(bf16[256,1536]{1,0:T(8,128)(2,1)} %fusion.18), channel_id=1, source_target_pairs={{0,16},{16,0},{8,24},{24,8},{1,17},{17,1},{9,25},{25,9},{2,18},{18... | collective-permute-start | bytes 2359304 | tf_op jit(solution)/shard_map/ppermute | solution.py:686
  688.2 69.1 %collective-permute-start.59 = (bf16[256,1536]{1,0:T(8,128)(2,1)}, bf16[256,1536]{1,0:T(8,128)(2,1)}, u32[]{:S(2)}, u32[]{:S(2)}) collective-permute-start(bf16[256,1536]{1,0:T(8,128)(2,1)} %pad_maximum_fusion.25), channel_id=1, source_target_pairs={{0,16},{16,0},{8,24},{24,8},{1,17},{17,1},{9,25},{25,9},{2,18},{18... | collective-permute-start | bytes 2359304 | tf_op jit(solution)/shard_map/ppermute | solution.py:686
  709.4 47.9 %collective-permute-start.60 = (bf16[256,1536]{1,0:T(8,128)(2,1)}, bf16[256,1536]{1,0:T(8,128)(2,1)}, u32[]{:S(2)}, u32[]{:S(2)}) collective-permute-start(bf16[256,1536]{1,0:T(8,128)(2,1)} %pad_maximum_fusion.26), channel_id=1, source_target_pairs={{0,2},{1,3},{2,0},{3,1},{4,6},{5,7},{6,4},{7,5},{8,10},{9,11},{10,... | collective-permute-start | bytes 2359304 | tf_op jit(solution)/shard_map/ppermute | solution.py:695
  (178 other events, 2217.3 us)
Sparse Core Ops, SparseCore 0:
  11.5 39.8 all-gather.13
  55.4 54.4 all-gather.15
  114.8 47.7 all-gather.7
  224.3 66.5 all-gather.9
  338.6 43.6 reduce-scatter.2
  481.8 60.3 reduce-scatter.4
  567.6 43.0 all-gather.11

commit v12 on v11

--- a/solution.py
+++ b/solution.py
@@ -117,17 +117,21 @@
     )(ids, gate, up)
 
 
-def near_at(away):
-    return (away & 1) * 2 + (away >> 1)
-
-
-def adam_body(blk_count, rate, decay, ids, factor_ref, first_ref, second_ref, w_ref, m_ref, v_ref, m_out, v_out, w_out):
+def adam_body(blk_count, rate, decay, ids, factor_ref, first_ref, first_far_ref, second_ref, second_far_ref, w_ref, m_ref, v_ref, m_out, v_out, w_out):
     per = blk_count // 4
     sizes = [size for at, size in halves_of(FF // blk_count // 4)]
-    grads = [
-        [[ref[near_at(ids[0] ^ k), bit] for bit in range(2)] for k in range(4)]
-        for ref in (first_ref, second_ref)
-    ]
+    grads = []
+    for near_ref, far_ref in ((first_ref, first_far_ref), (second_ref, second_far_ref)):
+        by_grp = []
+        for k in range(4):
+            away = ids[0] ^ k
+            bits_of_k = []
+            for bit in range(2):
+                near = near_ref[away >> 1, bit].astype(jnp.float32)
+                far = far_ref[away >> 1, bit].astype(jnp.float32)
+                bits_of_k.append(jnp.where((away & 1) == 1, far, near))
+            by_grp.append(bits_of_k)
+        grads.append(by_grp)
     parts = []
     for high in range(2):
         for bit in range(2):
@@ -136,7 +140,7 @@
                 for k in range(4):
                     for part, size in zip(grads, sizes):
                         parts.append(part[k][bit][:, place * size : (place + 1) * size])
-    grad = jnp.concatenate(parts, axis=1).astype(jnp.float32) * factor_ref[0]
+    grad = jnp.concatenate(parts, axis=1) * factor_ref[0]
     m, v, w = adam_step(w_ref[...], grad, m_ref[...], v_ref[...], rate, decay)
     m_out[...] = m
     v_out[...] = v
@@ -149,8 +153,8 @@
     spec = pl.BlockSpec((step, FF), lambda i, ids: (i, 0))
     shape = jax.ShapeDtypeStruct((rows, FF), jnp.float32)
     grads = [
-        pl.BlockSpec((4, None, 2, step, g.shape[-1]), lambda i, ids: (0, which, 0, i, 0))
-        for g in (first, second)
+        pl.BlockSpec((2, None, 2, step, g.shape[-1]), lambda i, ids: (0, which, 0, i, 0))
+        for g in first + second
     ]
     return pl.pallas_call(
         functools.partial(adam_body, blk_count, rate, decay),
@@ -164,7 +168,7 @@
         compiler_params=pltpu.CompilerParams(vmem_limit_bytes=VMEM),
         cost_estimate=SMALL_COST,
         name="adam_columns",
-    )(ids, factor, first, second, w, m, v)
+    )(ids, factor, *first, *second, w, m, v)
 
 
 def nt(a, b, **kw):
@@ -338,8 +342,9 @@
 
 
 def middle_body(add, order, h_ref, dy_ref, wg_ref, wu_ref, wd_ref, *refs):
-    prev_ref = refs[0] if add else None
-    hid_ref, dg_ref, du_ref, dh_ref = refs[-4:]
+    prev_refs = refs[:2] if add else None
+    hid_ref, dg_ref, du_ref, dh_ref, dh_far_ref = refs[-5:]
+    here = pl.program_id(0) < 4
     h = h_ref[...]
     gate = nn(h, wg_ref[...])
     up = nn(h, wu_ref[...])
@@ -353,8 +358,17 @@
     du_ref[...] = du
     dh = nt(dg, wg_ref[...]) + nt(du, wu_ref[...])
     if add:
-        dh = dh + prev_ref[...].astype(jnp.float32)
-    dh_ref[...] = dh.astype(jnp.bfloat16)
+        prev = jnp.where(here, prev_refs[0][...].astype(jnp.float32), prev_refs[1][...].astype(jnp.float32))
+        dh = dh + prev
+    dh = dh.astype(jnp.bfloat16)
+
+    @pl.when(here)
+    def _():
+        dh_ref[...] = dh
+
+    @pl.when(jnp.logical_not(here))
+    def _():
+        dh_far_ref[...] = dh
 
 
 def middle(order, h, dy, gate_up, wd, prev=None):
@@ -366,7 +380,9 @@
     part = pl.BlockSpec((step, wide_here), lambda i, order: (i, 0))
     part_placed = pl.BlockSpec((step, wide_here), lambda i, order: (order[i], 0))
     once = pl.Buffered(1)
-    extra = [] if prev is None else [prev]
+    extra = [] if prev is None else list(prev)
+    near = pl.BlockSpec((step, D), lambda i, order: (jnp.minimum(i, 3), 0))
+    far = pl.BlockSpec((step, D), lambda i, order: (jnp.maximum(i - 4, 0), 0))
     return pl.pallas_call(
         functools.partial(middle_body, prev is not None),
         grid_spec=pltpu.PrefetchScalarGridSpec(
@@ -379,11 +395,11 @@
                 pl.BlockSpec((None, D, wide_here), lambda i, order: (1, 0, 0), pipeline_mode=once),
                 pl.BlockSpec((wide_here, D), lambda i, order: (0, 0), pipeline_mode=once),
             ]
-            + [row] * len(extra),
-            out_specs=[part, part_placed, part_placed, row],
+            + [near, far][: len(extra)],
+            out_specs=[part, part_placed, part_placed, near, far],
         ),
         out_shape=[jax.ShapeDtypeStruct((count, wide_here), jnp.bfloat16)] * 3
-        + [jax.ShapeDtypeStruct((count, D), jnp.bfloat16)],
+        + [jax.ShapeDtypeStruct((count // 2, D), jnp.bfloat16)] * 2,
         compiler_params=pltpu.CompilerParams(vmem_limit_bytes=VMEM),
         cost_estimate=SMALL_COST,
         name="middle",
@@ -426,9 +442,18 @@
         cost_estimate=SMALL_COST,
         name="down_grad")(hid, dy)
 
-def down_body(hid_a_ref, hid_b_ref, wd_a_ref, wd_b_ref, o_ref):
+def down_body(hid_a_ref, hid_b_ref, wd_a_ref, wd_b_ref, o_ref, o_far_ref):
     out = nn(hid_a_ref[...], wd_a_ref[...]) + nn(hid_b_ref[...], wd_b_ref[...])
-    o_ref[...] = out.astype(jnp.bfloat16)
+    out = out.astype(jnp.bfloat16)
+    here = pl.program_id(0) < 4
+
+    @pl.when(here)
+    def _():
+        o_ref[...] = out
+
+    @pl.when(jnp.logical_not(here))
+    def _():
+        o_far_ref[...] = out
 
 
 def down(hid_a, hid_b, wd_a, wd_b, step):
@@ -444,8 +469,11 @@
         down_body,
         grid=(count // step,),
         in_specs=[rows(hid_a), rows(hid_b), whole(wd_a), whole(wd_b)],
-        out_specs=pl.BlockSpec((step, D), lambda i: (i, 0)),
-        out_shape=jax.ShapeDtypeStruct((count, D), jnp.bfloat16),
+        out_specs=[
+            pl.BlockSpec((step, D), lambda i: (jnp.minimum(i, 3), 0)),
+            pl.BlockSpec((step, D), lambda i: (jnp.maximum(i - 4, 0), 0)),
+        ],
+        out_shape=[jax.ShapeDtypeStruct((count // 2, D), jnp.bfloat16)] * 2,
         compiler_params=pltpu.CompilerParams(vmem_limit_bytes=VMEM),
         cost_estimate=SMALL_COST,
         name="down",
@@ -796,7 +824,7 @@
 
 def gather_near_stacked(values):
     both = jnp.stack([values, swap_cross(values)])
-    return jnp.concatenate([both, swap_core(both)])
+    return [both, swap_core(both)]
 
 
 def ring_groups(count):
@@ -889,7 +917,6 @@
     picked_a, picked_b = pick_columns(ids, w_gate, w_up, blk_count)
     got_a = swap_blk(picked_a[1], team)
     dy_cross = swap_cross(after(dy_low, picked_a))
-    dy_over = swap_blk(after(dy_low, strip_ring), team)
     token_cross = after(swap_cross(token_send), (picked_a, strip_ring, got_a, dy_cross))
 
     def place(values, other, done, bit, lead=0):
@@ -928,13 +955,12 @@
     first_blk = jnp.sum((seg_all[:, :, -1] < segment_ids[None, :, 0]).astype(jnp.int32), axis=0)
     attend_ids = jnp.concatenate([blk[None], first_blk])
 
-    dy_first = swap_blk(dy_cross[:half], team)
-    dy_second = swap_cross(dy_over[half:])
     mixed_cross = swap_cross(mixed_far)
     mixed_core = swap_core(jnp.stack([mixed_core, mixed_cross[1]]))
     pair_a = team_pair(picked_a[0], after(got_a, mixed_own))
     pair_a_got = swap_blk(pair_a, bits[0])
-    mixed_core = after(mixed_core, (dy_over, pair_a_got))
+    mixed_core = after(mixed_core, pair_a_got)
+    down_got = swap_blk(after(down_here, mixed_own), bits[0])
     query, packed_kv = pack(ids, mixed_own, mixed_cross, mixed_core)
     key_value = packed_kv.reshape(rows_here, block_len, 2 * KVD)
     kv_all = gather_ring(key_value)
@@ -963,15 +989,19 @@
         return values
 
     got_b = swap_blk(after(picked_b[1], mixed_own), team)
+    dy_over = swap_blk(after(dy_low, packed_kv), team)
     pair_a = place(pair_a, after(pair_a_got, packed_kv), [team], bits[0], 1)
-    gate_up_a = lows_of(pair_a, [bits[0], team], 1).reshape(2, D, -1)
-    got_b = after(got_b, kv_all)
-    kv_all = after(kv_all, (gate_up_a, got_b, dy_first, dy_second))
-    down_got = swap_blk(after(down_here, kv_all), bits[0])
+    got_b, down_got, dy_over = after((got_b, down_got, dy_over), kv_all)
+    kv_all = after(kv_all, (got_b, down_got, dy_over, pair_a))
+    pair_a_got = swap_blk(pair_a, lows[0])
+    down_here = place(down_here, down_got, [], bits[0])
+    down_here = lows_of(down_here, [bits[0]]).reshape(2 * blk_count // 4, quarter, D)
+    dy_first = swap_blk(dy_cross[:half], team)
+    dy_second = swap_cross(dy_over[half:])
     dy_chip = jnp.concatenate([dy_low, dy_cross, dy_over, dy_first, dy_second])
     dy_team = jnp.concatenate([dy_chip, swap_core(dy_chip)])
     pair_b = team_pair(picked_b[0], got_b)
-    pair_b_got = swap_blk(after(pair_b, down_got), bits[0])
+    pair_b_got = swap_blk(pair_b, bits[0])
     out_ring = after(out_ring, packed_kv)
     out_strip = jnp.concatenate([out_ring[ring.index(b)] for b in range(blk_count)])
     out_cross = swap_cross(out_strip)
@@ -982,16 +1012,21 @@
     flat = wide(flat_low)
     resid = flat + jnp.dot(att_in, out_full, preferred_element_type=jnp.float32)
     h_two = low(norm_apply(resid, gain_two))
-    h_two = after(h_two, down_got)
-    down_here = place(down_here, down_got, [], bits[0])
-    down_here = lows_of(down_here, [bits[0]]).reshape(2 * blk_count // 4, quarter, D)
+    h_two = after(h_two, pair_a_got)
+    pair_a_got = after(pair_a_got, h_two)
+    pair_a = place(pair_a, pair_a_got, [bits[0], team], lows[0], 1)
+    for i in range(1, len(lows)):
+        done = [bits[0], team] + lows[:i]
+        pair_a = place(pair_a, swap_blk(pair_a, lows[i]), done, lows[i], 1)
+    gate_up_a = pair_a.reshape(2, D, -1)
+    pair_b_got = after(pair_b_got, h_two)
     down_a = down_here[:, :size_first].reshape(widths[0], D)
     down_b = down_here[:, size_first:].reshape(widths[1], D)
     h_team = lax.all_gather(h_two, ("grp", "blk"), axis=0, tiled=True, axis_index_groups=teams)
     pair_b_got = after(pair_b_got, (h_two, gate_up_a))
     pair_b = place(pair_b, pair_b_got, [team], bits[0], 1)
     h_team = after(h_team, (gate_up_a, pair_b, dy_team))
-    hidden_a, d_gate_a, d_up_a, part_a = middle(order, h_team, dy_team, gate_up_a, down_a)
+    hidden_a, d_gate_a, d_up_a, *part_a = middle(order, h_team, dy_team, gate_up_a, down_a)
     gate_up_b = lows_of(pair_b, [bits[0], team], 1, hidden_a).reshape(2, D, -1)
     down_grad_a = down_grad(after(hidden_a, gate_up_b), dy_team)
     down_share_a = lax.psum_scatter(
@@ -1036,12 +1071,12 @@
         )
 
     first_a = columns_first(column_grad_a)
-    hidden_b, d_gate_b, d_up_b, d_htwo_part = middle(
+    hidden_b, d_gate_b, d_up_b, d_here, d_there = middle(
         order, after(h_team, (column_grad_a, down_grad_a)), dy_team, gate_up_b, down_b, part_a
     )
 
     def chip_sum(values, came):
-        return low(wide(values[:chip_rows]) + wide(came))
+        return low(wide(values) + wide(came))
 
     def scatter_far(chip):
         far = chip[3 * token_count :]
@@ -1054,22 +1089,22 @@
         return swap_cross(cross), swap_blk(over, team)
 
     near_att_cross = swap_cross(after(att_in, hidden_a))
-    d_htwo_part = after(d_htwo_part, (first_a[1], down_share_a, near_att_cross))
-    d_came = swap_core(d_htwo_part[chip_rows:])
+    d_there = after(d_there, (first_a[1], down_share_a, near_att_cross))
+    d_came = swap_core(d_there)
     down_grad_b = down_grad(hidden_b, dy_team)
     rows_b = part_sent(
         down_grad_b.reshape((2,) + low_shape + (size_second, D)), len(lows), lows[-1]
     )
     mid_a = columns_mid(*after(first_a, d_came))
     second_a = part_sent(mid_a, 1, bits[0])
-    d_chip = chip_sum(d_htwo_part, after(d_came, down_grad_b))
+    d_chip = chip_sum(d_here, after(d_came, down_grad_b))
     d_far = scatter_far(d_chip)
     column_grad_b = two_grads(h_team, *after((d_gate_b, d_up_b), d_chip))
     first_b = columns_first(column_grad_b)
     d_far = after(d_far, column_grad_b)
     d_cross, d_over = scatter_near(d_chip, *d_far)
-    out_part = down(*after((hidden_a, hidden_b), d_far), down_a, down_b, token_count)
-    out_came = swap_core(out_part[chip_rows:])
+    out_part, out_there = down(*after((hidden_a, hidden_b), d_far), down_a, down_b, token_count)
+    out_came = swap_core(out_there)
     d_cross, d_over = after((d_cross, d_over), out_part)
     d_htwo = wide(d_chip[:token_count]) + wide(d_cross) + wide(d_over)
 
@@ -1159,7 +1194,7 @@
     near_datt = to_strips([d_att[:, strip_q * k : strip_q * (k + 1)] for k in range(4)])
     out_grad = low(left_product(near_att, after(near_datt, d_attended))).reshape(block_shape)
     steps_out = part_sent(out_grad, len(bits) - 1, bits[-1])
-    anchors = [near_dq, near_dq]
+    anchors = [own_part, kv_grad]
     for i in range(len(bits) - 2, -1, -1):
         anchor = anchors[min(len(bits) - 2 - i, 1)]
         steps_out = part_sent(part_sum(*after(steps_out, anchor)), i, bits[i])
@@ -1204,7 +1239,7 @@
     own_b = columns_last(*third_b)
     cross_b = after(swap_cross(own_b), new_down)
     near_b = jnp.stack([own_b, cross_b])
-    near_b = jnp.concatenate([near_b, swap_core(near_b)])
+    near_b = [near_b, swap_core(near_b)]
     new_first_gate, new_second_gate, new_gate = adam_columns(
         0, ids, factor[None], near_a, near_b, w_gate, first_gate, second_gate, blk_count, RATE_GATE, WEIGHT_DECAY
     )

time: 782 us -> 788 us (level)
  waiting for transfers between devices: 278 us -> 293 us
  local copies, waits for them, and re-layouts: 90.2 us -> 78.5 us
    unnamed x267 -> x291, local copies, waits for them, and re-layouts: 41.1 us -> 37.9 us
  transfers between devices with their start and end apart: 78 -> 78, of which waited for: 29 -> 32; matrix products, arithmetic and copies ran while one was open for 22% -> 21% of each run, Pallas kernels for 23% -> 23%
where the time goes in v12:
time: 788 us; the launch traced here: 780 us
  waiting for transfers between devices  293 us (37%)
  Pallas kernels  186 us (24%)
  other arithmetic  120 us (15%)
  local copies, waits for them, and re-layouts  78.5 us (10%)
  starting transfers between devices  73.3 us (9%)
  between operations  22.2 us (3%)
    ppermute x34, waiting for transfers between devices, swap_blk(): return lax.ppermute(values, 'blk', [(i, i ^ bit) for i in range(count)])  247 us
    pallas_call x2, Pallas kernels, middle(): pl.pallas_call(functools.partial(middle_body, prev is not None), grid_spe...  63.4 us
    ppermute x34, starting transfers between devices, swap_blk(): return lax.ppermute(values, 'blk', [(i, i ^ bit) for i in range(count)])  51 us
    unnamed x291, local copies, waits for them, and re-layouts  37.9 us
    pallas_call x2, Pallas kernels, adam_columns(): pl.pallas_call(functools.partial(adam_body, blk_count, rate, decay), grid...  36.4 us
    ppermute x20, waiting for transfers between devices, swap_cross(): return lax.ppermute(values, 'grp', CROSS)  35.3 us
    convert_element_type x21, other arithmetic, low(): return values.astype(jnp.bfloat16)  30.8 us
    pallas_call x2, Pallas kernels, two_grads(): pl.pallas_call(two_grads_body, grid=(D // step,), in_specs=[pl.BlockSpec(...  23.7 us
  transfers between devices with their start and end apart: 78, of which 32 were waited for; matrix products, arithmetic and copies ran while one was open for 21% of the time, Pallas kernels for 23%

profile of v12, /device:TPU:0, one launch (start us, length us, event | category | flops | bytes accessed | tf_op | source)
XLA Modules:
  0.0 780.2 jit_solution(4789533908053558515)
XLA Ops:
  25.1 17.3 %collective-permute-done.1 = bf16[2,192,512]{2,1,0:T(8,128)(2,1)S(1)} collective-permute-done((bf16[2,192,512]{2,1,0:T(8,128)(2,1)S(1)}, bf16[2,192,512]{2,1,0:T(8,128)(2,1)S(1)}, u32[]{:S(2)}, u32[]{:S(2)}) %collective-permute-start.1) | collective-permute-done | bytes 393248 | tf_op jit(solution)/shard_map/ppermute | solution.py:723
  42.4 8.8 %collective-permute-done.2 = bf16[256,1536]{1,0:T(8,128)(2,1)S(1)} collective-permute-done((bf16[256,1536]{1,0:T(8,128)(2,1)}, bf16[256,1536]{1,0:T(8,128)(2,1)S(1)}, u32[]{:S(2)}, u32[]{:S(2)}) %collective-permute-start.2) | collective-permute-done | bytes 786464 | tf_op jit(solution)/shard_map/ppermute | solution.py:714
  57.4 7.6 mix.1
  69.7 9.4 %collective-permute-done.4.cross_ref = bf16[2,256,512]{2,1,0:T(8,128)(2,1)S(1)} collective-permute-done((bf16[2,256,512]{2,1,0:T(8,128)(2,1)S(1)}, bf16[2,256,512]{2,1,0:T(8,128)(2,1)S(1)}, u32[]{:S(2)}, u32[]{:S(2)}) %collective-permute-start.4) | collective-permute-done | bytes 524320 | tf_op jit(solution)/shard_map/ppermute | solution.py:714
  79.2 33.3 %collective-permute-done.6 = bf16[2,2,192,512]{3,2,0,1:T(8,128)(2,1)S(1)} collective-permute-done((bf16[2,2,192,512]{3,2,0,1:T(8,128)(2,1)S(1)}, bf16[2,2,192,512]{3,2,0,1:T(8,128)(2,1)S(1)}, u32[]{:S(2)}, u32[]{:S(2)}) %collective-permute-start.6) | collective-permute-done | bytes 786464 | tf_op jit(solution)/shard_map/ppermute | solution.py:723
  132.8 56.0 %collective-permute-done.7 = bf16[2,192,608]{2,1,0:T(8,128)(2,1)S(1)} collective-permute-done((bf16[2,192,608]{2,1,0:T(8,128)(2,1)}, bf16[2,192,608]{2,1,0:T(8,128)(2,1)S(1)}, u32[]{:S(2)}, u32[]{:S(2)}) %collective-permute-start.7) | collective-permute-done | bytes 466976 | tf_op jit(solution)/shard_map/ppermute | solution.py:723
  208.7 23.7 %collective-permute-done.12 = bf16[2,2,2,192,512]{4,3,0,2,1:T(8,128)(2,1)} collective-permute-done((bf16[2,2,2,192,512]{4,3,0,2,1:T(8,128)(2,1)}, bf16[2,2,2,192,512]{4,3,0,2,1:T(8,128)(2,1)}, u32[]{:S(2)}, u32[]{:S(2)}) %collective-permute-start.12) | collective-permute-done | bytes 1572896 | tf_op jit(solution)/shard_map/ppermute | solution.py:723
  241.5 7.6 collective-permute-done.14
  264.1 37.2 %collective-permute-done.13 = bf16[2,2,192,608]{3,2,0,1:T(8,128)(2,1)} collective-permute-done((bf16[2,2,192,608]{3,2,0,1:T(8,128)(2,1)}, bf16[2,2,192,608]{3,2,0,1:T(8,128)(2,1)}, u32[]{:S(2)}, u32[]{:S(2)}) %collective-permute-start.13) | collective-permute-done | bytes 933920 | tf_op jit(solution)/shard_map/ppermute | solution.py:723
  314.0 24.3 %middle.2 = (bf16[2048,512]{1,0:T(8,128)(2,1)S(1)}, bf16[2048,512]{1,0:T(8,128)(2,1)S(1)}, bf16[2048,512]{1,0:T(8,128)(2,1)}, bf16[1024,1536]{1,0:T(8,128)(2,1)}, bf16[1024,1536]{1,0:T(8,128)(2,1)}) custom-call(s32[8]{0:T(128)S(1)} %stack.298.order, bf16[2048,1536]{1,0:T(8,128)(2,1)} %all-gather.10.cloned.1.call-done.h_ref, ...), custom_call_target="tpu_custom_call" | custom-call | flops 1000 | bytes 1000 | tf_op jit(solution)/shard_map/middle/pallas_call | solution.py:386
  338.4 10.7 %collective-permute-done.18 = bf16[2,2,2,192,608]{4,3,0,2,1:T(8,128)(2,1)} collective-permute-done((bf16[2,2,2,192,608]{4,3,0,2,1:T(8,128)(2,1)}, bf16[2,2,2,192,608]{4,3,0,2,1:T(8,128)(2,1)}, u32[]{:S(2)}, u32[]{:S(2)}) %collective-permute-start.18) | collective-permute-done | bytes 1867808 | tf_op jit(solution)/shard_map/ppermute | solution.py:723
  354.1 6.7 down_grad.2
  364.6 10.2 %two_grads.2 = bf16[2,1536,512]{2,1,0:T(8,128)(2,1)} custom-call(bf16[2048,1536]{1,0:T(8,128)(2,1)} %all-gather.10.cloned.1.call-done.h_ref, bf16[2048,512]{1,0:T(8,128)(2,1)S(1)} %copy-done.21, bf16[2048,512]{1,0:T(8,128)(2,1)S(1)} %copy-done.22), custom_call_target="tpu_custom_call" | custom-call | flops 1000 | bytes 1000 | tf_op jit(solution)/shard_map/two_grads/pallas_call | solution.py:419
  381.9 39.1 %middle.3 = (bf16[2048,608]{1,0:T(8,128)(2,1)S(1)}, bf16[2048,608]{1,0:T(8,128)(2,1)}, bf16[2048,608]{1,0:T(8,128)(2,1)}, bf16[1024,1536]{1,0:T(8,128)(2,1)}, bf16[1024,1536]{1,0:T(8,128)(2,1)}) custom-call(s32[8]{0:T(128)S(1)} %stack.298.order, bf16[2048,1536]{1,0:T(8,128)(2,1)} %all-gather.10.cloned.1.call-done.h_ref, ...), custom_call_target="tpu_custom_call" | custom-call | flops 1000 | bytes 1000 | tf_op jit(solution)/shard_map/middle/pallas_call | solution.py:386
  444.3 13.5 %two_grads.3 = bf16[2,1536,608]{2,1,0:T(8,128)(2,1)} custom-call(bf16[2048,1536]{1,0:T(8,128)(2,1)} %all-gather.10.cloned.1.call-done.h_ref, bf16[2048,608]{1,0:T(8,128)(2,1)S(1)} %copy-done.18, bf16[2048,608]{1,0:T(8,128)(2,1)S(1)} %copy-done.19), custom_call_target="tpu_custom_call" | custom-call | flops 1000 | bytes 1000 | tf_op jit(solution)/shard_map/two_grads/pallas_call | solution.py:419
  474.9 12.7 %down.1 = (bf16[1024,1536]{1,0:T(8,128)(2,1)}, bf16[1024,1536]{1,0:T(8,128)(2,1)}) custom-call(bf16[2048,512]{1,0:T(8,128)(2,1)S(1)} %copy-done.6, bf16[2048,608]{1,0:T(8,128)(2,1)} %copy-done.1, bf16[512,1536]{1,0:T(8,128)(2,1)S(1)} %bitcast.413, bf16[608,1536]{1,0:T(8,128)(2,1)S(1)} %bitcast.411), custom_call_target="tpu_custom_call" | custom-call | flops 1000 | bytes 1000 | tf_op jit(solution)/shard_map/down/pallas_call | solution.py:468
  497.9 8.0 %attend_back.1 = (bf16[256,1536]{1,0:T(8,128)(2,1)S(1)}, bf16[8,2,128,512]{3,2,1,0:T(8,128)(2,1)}) custom-call(s32[3]{0:T(128)S(1)} %copy-done.38, bf16[256,1536]{1,0:T(8,128)(2,1)S(1)} %copy-done.13, bf16[8,2,128,512]{3,2,1,0:T(8,128)(2,1)} %all-gather.8.cloned.1.call-done.k_ref.v_ref, bf16[8,2,128,512]{3,2,1,0:T(8,128)(2,1)} %all-gather.8.cloned.1.call-done.k_ref.v_ref, ...), custom_call_target="tpu_custom_call" | custom-call | flops 1000 | bytes 1000 | tf_op jit(solution)/shard_map/attend_back/pallas_call | solution.py:315
  531.4 7.2 collective-permute-done.28
  572.3 9.8 %collective-permute-done.47 = bf16[2,2,192,384]{3,2,1,0:T(8,128)(2,1)} collective-permute-done((bf16[2,2,192,384]{3,2,1,0:T(8,128)(2,1)}, bf16[2,2,192,384]{3,2,1,0:T(8,128)(2,1)}, u32[]{:S(2)}, u32[]{:S(2)}) %collective-permute-start.47) | collective-permute-done | bytes 589856 | tf_op jit(solution)/shard_map/ppermute | solution.py:723
  590.4 8.1 %kv_grad.1 = (bf16[8,208,128]{2,1,0:T(8,128)(2,1)S(1)}, bf16[512,1536]{1,0:T(8,128)(2,1)S(1)}, bf16[512,1536]{1,0:T(8,128)(2,1)}) custom-call(bf16[256,128]{1,0:T(8,128)(2,1)S(1)} %get-tuple-element.196.self_ref, bf16[2,256,128]{2,1,0:T(8,128)(2,1)S(1)} %collective-permute-done.29.cross_ref, bf16[2,256,128]{2,1,0:T(8,128)(2,1)S(1)} %collective-permute-done.30.core_ref, ...), custom_call_target="tpu_custom_call" | custom-call | flops 1000 | bytes 1000 | tf_op jit(solution)/shard_map/kv_grad/pallas_call | solution.py:681
  598.6 10.8 %collective-permute-done.42 = bf16[2,192,384]{2,1,0:T(8,128)(2,1)} collective-permute-done((bf16[2,192,384]{2,1,0:T(8,128)(2,1)}, bf16[2,192,384]{2,1,0:T(8,128)(2,1)}, u32[]{:S(2)}, u32[]{:S(2)}) %collective-permute-start.42) | collective-permute-done | bytes 294944 | tf_op jit(solution)/shard_map/ppermute | solution.py:723
  698.2 17.0 %multiply_subtract_fusion = (f32[1120,1536]{1,0:T(8,128)}, f32[1120,1536]{1,0:T(8,128)}, f32[1120,1536]{1,0:T(8,128)}) fusion(f32[1120,1536]{1,0:T(8,128)} %param.30, bf16[1120,1536]{1,0:T(8,128)(2,1)} %all-gather.12.cloned.1.call-done, f32[]{:T(128)} %min.3, f32[1120,1536]{1,0:T(8,128)} %param.36, f32[1120,1536]{1,0:T(8,128)} %param.42), kind=kLoop, calls=%fused_computation.2 | loop fusion | flops 29245440 | bytes 44728324 | tf_op jit(solution)/shard_map/sub | solution.py:67
  728.0 18.0 %adam_columns.2 = (f32[192,8960]{1,0:T(8,128)}, f32[192,8960]{1,0:T(8,128)}, f32[192,8960]{1,0:T(8,128)}) custom-call(s32[2]{0:T(128)S(1)} %pad_add_fusion.2.ids, f32[1]{0:T(128)} %bitcast.127.factor_ref, bf16[2,2,2,192,512]{4,3,2,1,0:T(8,128)(2,1)S(1)} %pad_maximum_fusion.11.first_ref, ...), custom_call_target="tpu_custom_call" | custom-call | flops 1000 | bytes 1000 | tf_op jit(solution)/shard_map/adam_columns/pallas_call | solution.py:159
  746.0 18.3 %adam_columns.3 = (f32[192,8960]{1,0:T(8,128)}, f32[192,8960]{1,0:T(8,128)}, f32[192,8960]{1,0:T(8,128)}) custom-call(s32[2]{0:T(128)S(1)} %pad_add_fusion.2.ids, f32[1]{0:T(128)} %bitcast.127.factor_ref, bf16[2,2,2,192,512]{4,3,2,1,0:T(8,128)(2,1)S(1)} %pad_maximum_fusion.11.first_ref, ...), custom_call_target="tpu_custom_call" | custom-call | flops 1000 | bytes 1000 | tf_op jit(solution)/shard_map/adam_columns/pallas_call | solution.py:159
  (626 shorter events, 342.4 us)
Async XLA Ops:
  11.4 102.9 %all-gather.16.cloned.1.call-start = ((), (), s32[]{:S(2)}) async-start(), calls=%async_computation.8 | async-start | bytes 1327104 | tf_op jit(solution)/shard_map/all_gather | solution.py:836
  55.3 133.6 %all-gather.8.cloned.1.call-start = ((), (), s32[]{:S(2)}) async-start(), calls=%async_computation.2 | async-start | bytes 2359296 | tf_op jit(solution)/shard_map/all_gather | solution.py:836
  113.9 200.1 %all-gather.10.cloned.1.call-start = ((), (), s32[]{:S(2)}) async-start(), calls=%async_computation.3 | async-start | bytes 7077888 | tf_op jit(solution)/shard_map/all_gather | solution.py:1025
  121.9 67.0 %collective-permute-start.10 = (bf16[1536,384]{1,0:T(8,128)(2,1)S(1)}, bf16[1536,384]{1,0:T(8,128)(2,1)}, u32[]{:S(2)}, u32[]{:S(2)}) collective-permute-start(bf16[1536,384]{1,0:T(8,128)(2,1)S(1)} %bitcast_dynamic-update-slice_fusion), channel_id=1, source_target_pairs={{0,16},{16,0},{8,24},{24,8},{1,17},{17,1},{9,25},{25,9},{2,18},{18... | collective-permute-start | bytes 3538952 | tf_op jit(solution)/shard_map/ppermute | solution.py:714
  125.9 62.9 %collective-permute-start.8 = (bf16[280,1536]{1,0:T(8,128)(2,1)}, bf16[280,1536]{1,0:T(8,128)(2,1)}, u32[]{:S(2)}, u32[]{:S(2)}) collective-permute-start(bf16[280,1536]{1,0:T(8,128)(2,1)} %dynamic-slice_convert_fusion), channel_id=1, source_target_pairs={{0,4},{1,5},{2,6},{3,7},{4,0},{5,1},{6,2},{7,3},{8,12},{9,13},{10,... | collective-permute-start | bytes 2580488 | tf_op jit(solution)/shard_map/ppermute | solution.py:723
  125.9 62.9 %collective-permute-start.9 = (bf16[256,1536]{1,0:T(8,128)(2,1)}, bf16[256,1536]{1,0:T(8,128)(2,1)}, u32[]{:S(2)}, u32[]{:S(2)}) collective-permute-start(bf16[256,1536]{1,0:T(8,128)(2,1)} %bitcast.9), channel_id=1, source_target_pairs={{0,2},{1,3},{2,0},{3,1},{4,6},{5,7},{6,4},{7,5},{8,10},{9,11},{10,... | collective-permute-start | bytes 2359304 | tf_op jit(solution)/shard_map/ppermute | solution.py:723
  129.6 59.2 %collective-permute-start.7 = (bf16[2,192,608]{2,1,0:T(8,128)(2,1)}, bf16[2,192,608]{2,1,0:T(8,128)(2,1)S(1)}, u32[]{:S(2)}, u32[]{:S(2)}) collective-permute-start(bf16[2,192,608]{2,1,0:T(8,128)(2,1)} %slice_bitcast_fusion.4), channel_id=1, source_target_pairs={{0,2},{1,3},{2,0},{3,1},{4,6},{5,7},{6,4},{7,5},{8,10},{9,11},{10,... | collective-permute-start | bytes 1400840 | tf_op jit(solution)/shard_map/ppermute | solution.py:723
  232.4 191.0 %reduce-scatter.3.cloned.1.call-start = ((), (), s32[]{:S(2)}) async-start(), calls=%async_computation.4 | async-start | bytes 1966080 | tf_op jit(solution)/shard_map/reduce_scatter | solution.py:1032
  253.4 56.9 %collective-permute-start.16 = (bf16[1024,1536]{1,0:T(8,128)(2,1)}, bf16[1024,1536]{1,0:T(8,128)(2,1)}, u32[]{:S(2)}, u32[]{:S(2)}) collective-permute-start(bf16[1024,1536]{1,0:T(8,128)(2,1)} %get-tuple-element.375), channel_id=1, source_target_pairs={{0,8},{8,0},{16,24},{24,16},{1,9},{9,1},{17,25},{25,17},{2,10},{10... | collective-permute-start | bytes 9437192 | tf_op jit(solution)/shard_map/ppermute | solution.py:710
  254.8 46.5 %collective-permute-start.13 = (bf16[2,2,192,608]{3,2,0,1:T(8,128)(2,1)}, bf16[2,2,192,608]{3,2,0,1:T(8,128)(2,1)}, u32[]{:S(2)}, u32[]{:S(2)}) collective-permute-start(bf16[2,2,192,608]{3,2,0,1:T(8,128)(2,1)} %pad_maximum_fusion.12), channel_id=1, source_target_pairs={{0,4},{1,5},{2,6},{3,7},{4,0},{5,1},{6,2},{7,3},{8,12},{9,13},{10,... | collective-permute-start | bytes 2801672 | tf_op jit(solution)/shard_map/ppermute | solution.py:723
  258.4 47.8 %collective-permute-start.17 = (bf16[2,280,1536]{2,1,0:T(8,128)(2,1)}, bf16[2,280,1536]{2,1,0:T(8,128)(2,1)}, u32[]{:S(2)}, u32[]{:S(2)}) collective-permute-start(bf16[2,280,1536]{2,1,0:T(8,128)(2,1)} %pad_maximum_fusion.7), channel_id=1, source_target_pairs={{0,1},{1,0},{2,3},{3,2},{4,5},{5,4},{6,7},{7,6},{8,9},{9,8},{10,11... | collective-permute-start | bytes 5160968 | tf_op jit(solution)/shard_map/ppermute | solution.py:723
  360.9 201.7 %reduce-scatter.5.cloned.1.call-start = ((), (), s32[]{:S(2)}) async-start(), calls=%async_computation.5 | async-start | bytes 2359296 | tf_op jit(solution)/shard_map/reduce_scatter | solution.py:1133
  443.0 63.0 %collective-permute-start.27 = (bf16[2,152,1536]{2,1,0:T(8,128)(2,1)}, bf16[2,152,1536]{2,1,0:T(8,128)(2,1)}, u32[]{:S(2)}, u32[]{:S(2)}) collective-permute-start(bf16[2,152,1536]{2,1,0:T(8,128)(2,1)} %get-tuple-element.311), channel_id=1, source_target_pairs={{0,1},{1,0},{2,3},{3,2},{4,5},{5,4},{6,7},{7,6},{8,9},{9,8},{10,11... | collective-permute-start | bytes 2801672 | tf_op jit(solution)/shard_map/ppermute | solution.py:723
  468.5 71.2 %collective-permute-start.38 = (bf16[2,2,2,192,608]{4,3,2,1,0:T(8,128)(2,1)}, bf16[2,2,2,192,608]{4,3,2,1,0:T(8,128)(2,1)}, u32[]{:S(2)}, u32[]{:S(2)}) collective-permute-start(bf16[2,2,2,192,608]{4,3,2,1,0:T(8,128)(2,1)} %get-tuple-element.285), channel_id=1, source_target_pairs={{0,1},{1,0},{2,3},{3,2},{4,5},{5,4},{6,7},{7,6},{8,9},{9,8},{10,11... | collective-permute-start | bytes 5603336 | tf_op jit(solution)/shard_map/ppermute | solution.py:723
  487.6 133.8 %collective-permute-start.24 = (bf16[1024,1536]{1,0:T(8,128)(2,1)}, bf16[1024,1536]{1,0:T(8,128)(2,1)}, u32[]{:S(2)}, u32[]{:S(2)}) collective-permute-start(bf16[1024,1536]{1,0:T(8,128)(2,1)} %get-tuple-element.185), channel_id=1, source_target_pairs={{0,8},{8,0},{16,24},{24,16},{1,9},{9,1},{17,25},{25,17},{2,10},{10... | collective-permute-start | bytes 9437192 | tf_op jit(solution)/shard_map/ppermute | solution.py:710
  506.0 192.3 %all-gather.12.cloned.1.call-start = ((), (), s32[]{:S(2)}) async-start(), calls=%async_computation.6 | async-start | bytes 4300800 | tf_op jit(solution)/shard_map/all_gather | solution.py:1181
  524.4 59.9 %collective-permute-start.56 = (bf16[2,192,512]{2,1,0:T(8,128)(2,1)}, bf16[2,192,512]{2,1,0:T(8,128)(2,1)}, u32[]{:S(2)}, u32[]{:S(2)}) collective-permute-start(bf16[2,192,512]{2,1,0:T(8,128)(2,1)} %get-tuple-element.341), channel_id=1, source_target_pairs={{0,2},{1,3},{2,0},{3,1},{4,6},{5,7},{6,4},{7,5},{8,10},{9,11},{10,... | collective-permute-start | bytes 1179656 | tf_op jit(solution)/shard_map/ppermute | solution.py:723
  556.8 69.9 %collective-permute-start.39 = (bf16[2,2,192,608]{3,2,1,0:T(8,128)(2,1)}, bf16[2,2,192,608]{3,2,1,0:T(8,128)(2,1)}, u32[]{:S(2)}, u32[]{:S(2)}) collective-permute-start(bf16[2,2,192,608]{3,2,1,0:T(8,128)(2,1)} %get-tuple-element.307), channel_id=1, source_target_pairs={{0,4},{1,5},{2,6},{3,7},{4,0},{5,1},{6,2},{7,3},{8,12},{9,13},{10,... | collective-permute-start | bytes 2801672 | tf_op jit(solution)/shard_map/ppermute | solution.py:723
  584.3 47.0 %collective-permute-start.48 = (bf16[2,192,384]{2,1,0:T(8,128)(2,1)}, bf16[2,192,384]{2,1,0:T(8,128)(2,1)}, u32[]{:S(2)}, u32[]{:S(2)}) collective-permute-start(bf16[2,192,384]{2,1,0:T(8,128)(2,1)} %get-tuple-element.361), channel_id=1, source_target_pairs={{0,2},{1,3},{2,0},{3,1},{4,6},{5,7},{6,4},{7,5},{8,10},{9,11},{10,... | collective-permute-start | bytes 884744 | tf_op jit(solution)/shard_map/ppermute | solution.py:723
  589.9 55.1 %collective-permute-start.57 = (bf16[2,2,192,512]{3,2,1,0:T(8,128)(2,1)S(1)}, bf16[2,2,192,512]{3,2,1,0:T(8,128)(2,1)S(1)}, u32[]{:S(2)}, u32[]{:S(2)}) collective-permute-start(bf16[2,2,192,512]{3,2,1,0:T(8,128)(2,1)S(1)} %get-tuple-element.338), channel_id=1, source_target_pairs={{0,16},{16,0},{8,24},{24,8},{1,17},{17,1},{9,25},{25,9},{2,18},{18... | collective-permute-start | bytes 2359304 | tf_op jit(solution)/shard_map/ppermute | solution.py:714
  621.3 68.4 %collective-permute-start.63 = (bf16[512,1536]{1,0:T(8,128)(2,1)}, bf16[512,1536]{1,0:T(8,128)(2,1)}, u32[]{:S(2)}, u32[]{:S(2)}) collective-permute-start(bf16[512,1536]{1,0:T(8,128)(2,1)} %get-tuple-element.238), channel_id=1, source_target_pairs={{0,8},{8,0},{16,24},{24,16},{1,9},{9,1},{17,25},{25,17},{2,10},{10... | collective-permute-start | bytes 4718600 | tf_op jit(solution)/shard_map/ppermute | solution.py:710
  626.7 67.8 %collective-permute-start.35 = (bf16[128,1536]{1,0:T(8,128)(2,1)}, bf16[128,1536]{1,0:T(8,128)(2,1)}, u32[]{:S(2)}, u32[]{:S(2)}) collective-permute-start(bf16[128,1536]{1,0:T(8,128)(2,1)} %get-tuple-element.294), channel_id=1, source_target_pairs={{0,2},{1,3},{2,0},{3,1},{4,6},{5,7},{6,4},{7,5},{8,10},{9,11},{10,... | collective-permute-start | bytes 1179656 | tf_op jit(solution)/shard_map/ppermute | solution.py:723
  693.7 70.7 %collective-permute-start.64 = (bf16[256,1536]{1,0:T(8,128)(2,1)}, bf16[256,1536]{1,0:T(8,128)(2,1)}, u32[]{:S(2)}, u32[]{:S(2)}) collective-permute-start(bf16[256,1536]{1,0:T(8,128)(2,1)} %fusion.18), channel_id=1, source_target_pairs={{0,16},{16,0},{8,24},{24,8},{1,17},{17,1},{9,25},{25,9},{2,18},{18... | collective-permute-start | bytes 2359304 | tf_op jit(solution)/shard_map/ppermute | solution.py:714
  696.9 67.4 %collective-permute-start.59 = (bf16[256,1536]{1,0:T(8,128)(2,1)}, bf16[256,1536]{1,0:T(8,128)(2,1)}, u32[]{:S(2)}, u32[]{:S(2)}) collective-permute-start(bf16[256,1536]{1,0:T(8,128)(2,1)} %pad_maximum_fusion.23), channel_id=1, source_target_pairs={{0,16},{16,0},{8,24},{24,8},{1,17},{17,1},{9,25},{25,9},{2,18},{18... | collective-permute-start | bytes 2359304 | tf_op jit(solution)/shard_map/ppermute | solution.py:714
  (190 other events, 2166.5 us)
Sparse Core Ops, SparseCore 0:
  11.5 39.8 all-gather.13
  55.4 50.5 all-gather.15
  114.1 72.2 all-gather.7
  232.5 71.8 all-gather.9
  361.0 44.8 reduce-scatter.2
  506.1 56.5 reduce-scatter.4
  586.5 43.0 all-gather.11

commit v13 on v12

--- a/solution.py
+++ b/solution.py
@@ -917,6 +917,7 @@
     picked_a, picked_b = pick_columns(ids, w_gate, w_up, blk_count)
     got_a = swap_blk(picked_a[1], team)
     dy_cross = swap_cross(after(dy_low, picked_a))
+    dy_over = swap_blk(after(dy_low, strip_ring), team)
     token_cross = after(swap_cross(token_send), (picked_a, strip_ring, got_a, dy_cross))
 
     def place(values, other, done, bit, lead=0):
@@ -959,7 +960,7 @@
     mixed_core = swap_core(jnp.stack([mixed_core, mixed_cross[1]]))
     pair_a = team_pair(picked_a[0], after(got_a, mixed_own))
     pair_a_got = swap_blk(pair_a, bits[0])
-    mixed_core = after(mixed_core, pair_a_got)
+    mixed_core = after(mixed_core, (pair_a_got, dy_over))
     down_got = swap_blk(after(down_here, mixed_own), bits[0])
     query, packed_kv = pack(ids, mixed_own, mixed_cross, mixed_core)
     key_value = packed_kv.reshape(rows_here, block_len, 2 * KVD)
@@ -989,18 +990,17 @@
         return values
 
     got_b = swap_blk(after(picked_b[1], mixed_own), team)
-    dy_over = swap_blk(after(dy_low, packed_kv), team)
     pair_a = place(pair_a, after(pair_a_got, packed_kv), [team], bits[0], 1)
-    got_b, down_got, dy_over = after((got_b, down_got, dy_over), kv_all)
-    kv_all = after(kv_all, (got_b, down_got, dy_over, pair_a))
-    pair_a_got = swap_blk(pair_a, lows[0])
+    pair_y_got = swap_blk(pair_a, lows[0])
+    got_b, down_got = after((got_b, down_got), kv_all)
+    kv_all = after(kv_all, (got_b, down_got, pair_y_got))
     down_here = place(down_here, down_got, [], bits[0])
     down_here = lows_of(down_here, [bits[0]]).reshape(2 * blk_count // 4, quarter, D)
     dy_first = swap_blk(dy_cross[:half], team)
     dy_second = swap_cross(dy_over[half:])
     dy_chip = jnp.concatenate([dy_low, dy_cross, dy_over, dy_first, dy_second])
     dy_team = jnp.concatenate([dy_chip, swap_core(dy_chip)])
-    pair_b = team_pair(picked_b[0], got_b)
+    pair_b = team_pair(picked_b[0], after(got_b, kv_all))
     pair_b_got = swap_blk(pair_b, bits[0])
     out_ring = after(out_ring, packed_kv)
     out_strip = jnp.concatenate([out_ring[ring.index(b)] for b in range(blk_count)])
@@ -1012,9 +1012,7 @@
     flat = wide(flat_low)
     resid = flat + jnp.dot(att_in, out_full, preferred_element_type=jnp.float32)
     h_two = low(norm_apply(resid, gain_two))
-    h_two = after(h_two, pair_a_got)
-    pair_a_got = after(pair_a_got, h_two)
-    pair_a = place(pair_a, pair_a_got, [bits[0], team], lows[0], 1)
+    pair_a = place(pair_a, after(pair_y_got, h_two), [bits[0], team], lows[0], 1)
     for i in range(1, len(lows)):
         done = [bits[0], team] + lows[:i]
         pair_a = place(pair_a, swap_blk(pair_a, lows[i]), done, lows[i], 1)
@@ -1207,7 +1205,8 @@
 
     other = wide(swap_core(hone_there))
     d_hone = wide(hone_here[:token_count]) + other[:token_count]
-    d_hone_cross = swap_cross(low(wide(hone_here[token_count:]) + other[token_count:]))
+    d_hone_send = low(wide(hone_here[token_count:]) + other[token_count:])
+    d_hone_cross = swap_cross(d_hone_send)
     square_sum = square_total(
         [
             wide(s)
@@ -1215,6 +1214,7 @@
         ]
     )
     packed = jnp.concatenate([vector_part, jnp.full((8, HD), square_sum)])
+    packed = after(packed, (d_hone_send, d_hone))
     packed = packed + swap_cross(packed)
     packed = packed + swap_core(packed)
     share_vector = packed[:vector_rows].reshape(-1)[:small_count]

time: 788 us -> 763 us (0.968)
  waiting for transfers between devices: 293 us -> 274 us
    ppermute x34, waiting for transfers between devices: 247 us -> 227 us  [swap_blk(): return lax.ppermute(values, 'blk', [(i, i ^ bit) for i in range(count)])]
    convert_element_type x21 -> x20, other arithmetic: 30.8 us -> 28.3 us  [low(): return values.astype(jnp.bfloat16)]
    unnamed x291 -> x275, local copies, waits for them, and re-layouts: 37.9 us -> 35.9 us
  transfers between devices with their start and end apart: 78 -> 78, of which waited for: 32 -> 33; matrix products, arithmetic and copies ran while one was open for 21% -> 20% of each run, Pallas kernels for 23% -> 24%
where the time goes in v13:
time: 763 us; the launch traced here: 755 us
  waiting for transfers between devices  274 us (36%)
  Pallas kernels  185 us (24%)
  other arithmetic  113 us (15%)
  starting transfers between devices  77 us (10%)
  local copies, waits for them, and re-layouts  76.8 us (10%)
  between operations  22.2 us (3%)
    ppermute x34, waiting for transfers between devices, swap_blk(): return lax.ppermute(values, 'blk', [(i, i ^ bit) for i in range(count)])  227 us
    pallas_call x2, Pallas kernels, middle(): pl.pallas_call(functools.partial(middle_body, prev is not None), grid_spe...  63.4 us
    ppermute x34, starting transfers between devices, swap_blk(): return lax.ppermute(values, 'blk', [(i, i ^ bit) for i in range(count)])  50.3 us
    ppermute x20, waiting for transfers between devices, swap_cross(): return lax.ppermute(values, 'grp', CROSS)  41.9 us
    pallas_call x2, Pallas kernels, adam_columns(): pl.pallas_call(functools.partial(adam_body, blk_count, rate, decay), grid...  36.1 us
    unnamed x275, local copies, waits for them, and re-layouts  35.9 us
    convert_element_type x20, other arithmetic, low(): return values.astype(jnp.bfloat16)  28.3 us
    ppermute x20, starting transfers between devices, swap_cross(): return lax.ppermute(values, 'grp', CROSS)  24.1 us
  transfers between devices with their start and end apart: 78, of which 33 were waited for; matrix products, arithmetic and copies ran while one was open for 20% of the time, Pallas kernels for 24%

profile of v13, /device:TPU:0, one launch (start us, length us, event | category | flops | bytes accessed | tf_op | source)
XLA Modules:
  0.0 755.4 jit_solution(5978556382409896560)
XLA Ops:
  25.1 17.3 %collective-permute-done.1 = bf16[2,192,512]{2,1,0:T(8,128)(2,1)S(1)} collective-permute-done((bf16[2,192,512]{2,1,0:T(8,128)(2,1)S(1)}, bf16[2,192,512]{2,1,0:T(8,128)(2,1)S(1)}, u32[]{:S(2)}, u32[]{:S(2)}) %collective-permute-start.1) | collective-permute-done | bytes 393248 | tf_op jit(solution)/shard_map/ppermute | solution.py:723
  42.4 8.8 %collective-permute-done.2 = bf16[256,1536]{1,0:T(8,128)(2,1)S(1)} collective-permute-done((bf16[256,1536]{1,0:T(8,128)(2,1)S(1)}, bf16[256,1536]{1,0:T(8,128)(2,1)S(1)}, u32[]{:S(2)}, u32[]{:S(2)}) %collective-permute-start.2) | collective-permute-done | bytes 786464 | tf_op jit(solution)/shard_map/ppermute | solution.py:714
  69.7 9.4 %collective-permute-done.4.cross_ref = bf16[2,256,512]{2,1,0:T(8,128)(2,1)S(1)} collective-permute-done((bf16[2,256,512]{2,1,0:T(8,128)(2,1)S(1)}, bf16[2,256,512]{2,1,0:T(8,128)(2,1)S(1)}, u32[]{:S(2)}, u32[]{:S(2)}) %collective-permute-start.4) | collective-permute-done | bytes 524320 | tf_op jit(solution)/shard_map/ppermute | solution.py:714
  79.2 16.9 %collective-permute-done.7 = bf16[256,1536]{1,0:T(8,128)(2,1)S(1)} collective-permute-done((bf16[256,1536]{1,0:T(8,128)(2,1)}, bf16[256,1536]{1,0:T(8,128)(2,1)S(1)}, u32[]{:S(2)}, u32[]{:S(2)}) %collective-permute-start.7) | collective-permute-done | bytes 786464 | tf_op jit(solution)/shard_map/ppermute | solution.py:723
  96.2 17.0 %collective-permute-done.6 = bf16[2,2,192,512]{3,2,0,1:T(8,128)(2,1)S(1)} collective-permute-done((bf16[2,2,192,512]{3,2,0,1:T(8,128)(2,1)S(1)}, bf16[2,2,192,512]{3,2,0,1:T(8,128)(2,1)S(1)}, u32[]{:S(2)}, u32[]{:S(2)}) %collective-permute-start.6) | collective-permute-done | bytes 786464 | tf_op jit(solution)/shard_map/ppermute | solution.py:723
  133.4 39.6 %collective-permute-done.8 = bf16[2,192,608]{2,1,0:T(8,128)(2,1)S(1)} collective-permute-done((bf16[2,192,608]{2,1,0:T(8,128)(2,1)}, bf16[2,192,608]{2,1,0:T(8,128)(2,1)S(1)}, u32[]{:S(2)}, u32[]{:S(2)}) %collective-permute-start.8) | collective-permute-done | bytes 466976 | tf_op jit(solution)/shard_map/ppermute | solution.py:723
  173.0 9.6 %collective-permute-done.9 = bf16[280,1536]{1,0:T(8,128)(2,1)} collective-permute-done((bf16[280,1536]{1,0:T(8,128)(2,1)}, bf16[280,1536]{1,0:T(8,128)(2,1)}, u32[]{:S(2)}, u32[]{:S(2)}) %collective-permute-start.9) | collective-permute-done | bytes 860192 | tf_op jit(solution)/shard_map/ppermute | solution.py:723
  236.3 34.6 %collective-permute-done.13 = bf16[2,2,192,608]{3,2,0,1:T(8,128)(2,1)S(1)} collective-permute-done((bf16[2,2,192,608]{3,2,0,1:T(8,128)(2,1)S(1)}, bf16[2,2,192,608]{3,2,0,1:T(8,128)(2,1)S(1)}, u32[]{:S(2)}, u32[]{:S(2)}) %collective-permute-start.13) | collective-permute-done | bytes 933920 | tf_op jit(solution)/shard_map/ppermute | solution.py:723
  281.3 24.3 %middle.2 = (bf16[2048,512]{1,0:T(8,128)(2,1)S(1)}, bf16[2048,512]{1,0:T(8,128)(2,1)S(1)}, bf16[2048,512]{1,0:T(8,128)(2,1)}, bf16[1024,1536]{1,0:T(8,128)(2,1)}, bf16[1024,1536]{1,0:T(8,128)(2,1)}) custom-call(s32[8]{0:T(128)S(1)} %stack.298.order, bf16[2048,1536]{1,0:T(8,128)(2,1)} %all-gather.10.cloned.1.call-done.h_ref, ...), custom_call_target="tpu_custom_call" | custom-call | flops 1000 | bytes 1000 | tf_op jit(solution)/shard_map/middle/pallas_call | solution.py:386
  305.7 12.0 %collective-permute-done.18 = bf16[2,2,2,192,608]{4,3,0,2,1:T(8,128)(2,1)} collective-permute-done((bf16[2,2,2,192,608]{4,3,0,2,1:T(8,128)(2,1)}, bf16[2,2,2,192,608]{4,3,0,2,1:T(8,128)(2,1)}, u32[]{:S(2)}, u32[]{:S(2)}) %collective-permute-start.18) | collective-permute-done | bytes 1867808 | tf_op jit(solution)/shard_map/ppermute | solution.py:723
  333.2 10.1 %two_grads.2 = bf16[2,1536,512]{2,1,0:T(8,128)(2,1)} custom-call(bf16[2048,1536]{1,0:T(8,128)(2,1)} %all-gather.10.cloned.1.call-done.h_ref, bf16[2048,512]{1,0:T(8,128)(2,1)S(1)} %copy-done.21, bf16[2048,512]{1,0:T(8,128)(2,1)S(1)} %copy-done.22), custom_call_target="tpu_custom_call" | custom-call | flops 1000 | bytes 1000 | tf_op jit(solution)/shard_map/two_grads/pallas_call | solution.py:419
  348.3 39.1 %middle.3 = (bf16[2048,608]{1,0:T(8,128)(2,1)S(1)}, bf16[2048,608]{1,0:T(8,128)(2,1)}, bf16[2048,608]{1,0:T(8,128)(2,1)}, bf16[1024,1536]{1,0:T(8,128)(2,1)}, bf16[1024,1536]{1,0:T(8,128)(2,1)}) custom-call(s32[8]{0:T(128)S(1)} %stack.298.order, bf16[2048,1536]{1,0:T(8,128)(2,1)} %all-gather.10.cloned.1.call-done.h_ref, ...), custom_call_target="tpu_custom_call" | custom-call | flops 1000 | bytes 1000 | tf_op jit(solution)/shard_map/middle/pallas_call | solution.py:386
  412.1 13.5 %two_grads.3 = bf16[2,1536,608]{2,1,0:T(8,128)(2,1)} custom-call(bf16[2048,1536]{1,0:T(8,128)(2,1)} %all-gather.10.cloned.1.call-done.h_ref, bf16[2048,608]{1,0:T(8,128)(2,1)S(1)} %copy-done.18, bf16[2048,608]{1,0:T(8,128)(2,1)S(1)} %copy-done.19), custom_call_target="tpu_custom_call" | custom-call | flops 1000 | bytes 1000 | tf_op jit(solution)/shard_map/two_grads/pallas_call | solution.py:419
  441.2 12.7 %down.1 = (bf16[1024,1536]{1,0:T(8,128)(2,1)}, bf16[1024,1536]{1,0:T(8,128)(2,1)}) custom-call(bf16[2048,512]{1,0:T(8,128)(2,1)S(1)} %copy-done.6, bf16[2048,608]{1,0:T(8,128)(2,1)} %copy-done.1, bf16[512,1536]{1,0:T(8,128)(2,1)S(1)} %bitcast.413, bf16[608,1536]{1,0:T(8,128)(2,1)S(1)} %bitcast.411), custom_call_target="tpu_custom_call" | custom-call | flops 1000 | bytes 1000 | tf_op jit(solution)/shard_map/down/pallas_call | solution.py:468
  463.7 8.0 %attend_back.1 = (bf16[256,1536]{1,0:T(8,128)(2,1)S(1)}, bf16[8,2,128,512]{3,2,1,0:T(8,128)(2,1)}) custom-call(s32[3]{0:T(128)S(1)} %copy-done.37, bf16[256,1536]{1,0:T(8,128)(2,1)S(1)} %copy-done.13, bf16[8,2,128,512]{3,2,1,0:T(8,128)(2,1)} %all-gather.8.cloned.1.call-done.k_ref.v_ref, bf16[8,2,128,512]{3,2,1,0:T(8,128)(2,1)} %all-gather.8.cloned.1.call-done.k_ref.v_ref, ...), custom_call_target="tpu_custom_call" | custom-call | flops 1000 | bytes 1000 | tf_op jit(solution)/shard_map/attend_back/pallas_call | solution.py:315
  499.0 9.5 %collective-permute-done.28 = bf16[152,1536]{1,0:T(8,128)(2,1)S(1)} collective-permute-done((bf16[152,1536]{1,0:T(8,128)(2,1)S(1)}, bf16[152,1536]{1,0:T(8,128)(2,1)S(1)}, u32[]{:S(2)}, u32[]{:S(2)}) %collective-permute-start.28) | collective-permute-done | bytes 466976 | tf_op jit(solution)/shard_map/ppermute | solution.py:723
  539.4 8.1 %collective-permute-done.47 = bf16[2,2,192,384]{3,2,1,0:T(8,128)(2,1)} collective-permute-done((bf16[2,2,192,384]{3,2,1,0:T(8,128)(2,1)}, bf16[2,2,192,384]{3,2,1,0:T(8,128)(2,1)}, u32[]{:S(2)}, u32[]{:S(2)}) %collective-permute-start.47) | collective-permute-done | bytes 589856 | tf_op jit(solution)/shard_map/ppermute | solution.py:723
  557.3 8.1 %kv_grad.1 = (bf16[8,208,128]{2,1,0:T(8,128)(2,1)S(1)}, bf16[512,1536]{1,0:T(8,128)(2,1)S(1)}, bf16[512,1536]{1,0:T(8,128)(2,1)}) custom-call(bf16[256,128]{1,0:T(8,128)(2,1)S(1)} %get-tuple-element.195.self_ref, bf16[2,256,128]{2,1,0:T(8,128)(2,1)S(1)} %collective-permute-done.29.cross_ref, bf16[2,256,128]{2,1,0:T(8,128)(2,1)S(1)} %collective-permute-done.30.core_ref, ...), custom_call_target="tpu_custom_call" | custom-call | flops 1000 | bytes 1000 | tf_op jit(solution)/shard_map/kv_grad/pallas_call | solution.py:681
  565.5 10.5 %collective-permute-done.42 = bf16[2,192,384]{2,1,0:T(8,128)(2,1)} collective-permute-done((bf16[2,192,384]{2,1,0:T(8,128)(2,1)}, bf16[2,192,384]{2,1,0:T(8,128)(2,1)}, u32[]{:S(2)}, u32[]{:S(2)}) %collective-permute-start.42) | collective-permute-done | bytes 294944 | tf_op jit(solution)/shard_map/ppermute | solution.py:723
  610.0 10.8 %collective-permute-done.69 = bf16[192,384]{1,0:T(8,128)(2,1)S(1)} collective-permute-done((bf16[192,384]{1,0:T(8,128)(2,1)S(1)}, bf16[192,384]{1,0:T(8,128)(2,1)S(1)}, u32[]{:S(2)}, u32[]{:S(2)}) %collective-permute-start.69) | collective-permute-done | bytes 147488 | tf_op jit(solution)/shard_map/ppermute | solution.py:714
  627.0 9.9 %collective-permute-done.40 = bf16[2,192,608]{2,1,0:T(8,128)(2,1)S(1)} collective-permute-done((bf16[2,192,608]{2,1,0:T(8,128)(2,1)S(1)}, bf16[2,192,608]{2,1,0:T(8,128)(2,1)S(1)}, u32[]{:S(2)}, u32[]{:S(2)}) %collective-permute-start.40) | collective-permute-done | bytes 466976 | tf_op jit(solution)/shard_map/ppermute | solution.py:723
  674.7 17.0 %multiply_subtract_fusion = (f32[1120,1536]{1,0:T(8,128)}, f32[1120,1536]{1,0:T(8,128)}, f32[1120,1536]{1,0:T(8,128)}) fusion(f32[1120,1536]{1,0:T(8,128)} %param.30, bf16[1120,1536]{1,0:T(8,128)(2,1)} %all-gather.12.cloned.1.call-done, f32[]{:T(128)} %min.3, f32[1120,1536]{1,0:T(8,128)} %param.36, f32[1120,1536]{1,0:T(8,128)} %param.42), kind=kLoop, calls=%fused_computation.2 | loop fusion | flops 29245440 | bytes 44728324 | tf_op jit(solution)/shard_map/sub | solution.py:67
  703.4 18.0 %adam_columns.2 = (f32[192,8960]{1,0:T(8,128)}, f32[192,8960]{1,0:T(8,128)}, f32[192,8960]{1,0:T(8,128)}) custom-call(s32[2]{0:T(128)S(1)} %pad_add_fusion.1.ids, f32[1]{0:T(128)} %bitcast.127.factor_ref, bf16[2,2,2,192,512]{4,3,2,1,0:T(8,128)(2,1)S(1)} %pad_maximum_fusion.11.first_ref, ...), custom_call_target="tpu_custom_call" | custom-call | flops 1000 | bytes 1000 | tf_op jit(solution)/shard_map/adam_columns/pallas_call | solution.py:159
  721.5 18.0 %adam_columns.3 = (f32[192,8960]{1,0:T(8,128)}, f32[192,8960]{1,0:T(8,128)}, f32[192,8960]{1,0:T(8,128)}) custom-call(s32[2]{0:T(128)S(1)} %pad_add_fusion.1.ids, f32[1]{0:T(128)} %bitcast.127.factor_ref, bf16[2,2,2,192,512]{4,3,2,1,0:T(8,128)(2,1)S(1)} %pad_maximum_fusion.11.first_ref, ...), custom_call_target="tpu_custom_call" | custom-call | flops 1000 | bytes 1000 | tf_op jit(solution)/shard_map/adam_columns/pallas_call | solution.py:159
  (610 shorter events, 350.2 us)
Async XLA Ops:
  11.4 106.8 %all-gather.16.cloned.1.call-start = ((), (), s32[]{:S(2)}) async-start(), calls=%async_computation.8 | async-start | bytes 1327104 | tf_op jit(solution)/shard_map/all_gather | solution.py:836
  55.3 127.3 %all-gather.8.cloned.1.call-start = ((), (), s32[]{:S(2)}) async-start(), calls=%async_computation.2 | async-start | bytes 2359296 | tf_op jit(solution)/shard_map/all_gather | solution.py:836
  67.0 46.2 %collective-permute-start.6 = (bf16[2,2,192,512]{3,2,0,1:T(8,128)(2,1)S(1)}, bf16[2,2,192,512]{3,2,0,1:T(8,128)(2,1)S(1)}, u32[]{:S(2)}, u32[]{:S(2)}) collective-permute-start(bf16[2,2,192,512]{3,2,0,1:T(8,128)(2,1)S(1)} %pad_maximum_fusion.17), channel_id=1, source_target_pairs={{0,4},{1,5},{2,6},{3,7},{4,0},{5,1},{6,2},{7,3},{8,12},{9,13},{10,... | collective-permute-start | bytes 2359304 | tf_op jit(solution)/shard_map/ppermute | solution.py:723
  114.6 166.7 %all-gather.10.cloned.1.call-start = ((), (), s32[]{:S(2)}) async-start(), calls=%async_computation.3 | async-start | bytes 7077888 | tf_op jit(solution)/shard_map/all_gather | solution.py:1023
  116.7 65.9 %collective-permute-start.10 = (bf16[2,2,2,192,512]{4,3,0,2,1:T(8,128)(2,1)}, bf16[2,2,2,192,512]{4,3,0,2,1:T(8,128)(2,1)}, u32[]{:S(2)}, u32[]{:S(2)}) collective-permute-start(bf16[2,2,2,192,512]{4,3,0,2,1:T(8,128)(2,1)} %pad_maximum_fusion.9), channel_id=1, source_target_pairs={{0,1},{1,0},{2,3},{3,2},{4,5},{5,4},{6,7},{7,6},{8,9},{9,8},{10,11... | collective-permute-start | bytes 4718600 | tf_op jit(solution)/shard_map/ppermute | solution.py:723
  125.8 56.8 %collective-permute-start.11 = (bf16[1536,384]{1,0:T(8,128)(2,1)S(1)}, bf16[1536,384]{1,0:T(8,128)(2,1)}, u32[]{:S(2)}, u32[]{:S(2)}) collective-permute-start(bf16[1536,384]{1,0:T(8,128)(2,1)S(1)} %bitcast_dynamic-update-slice_fusion), channel_id=1, source_target_pairs={{0,16},{16,0},{8,24},{24,8},{1,17},{17,1},{9,25},{25,9},{2,18},{18... | collective-permute-start | bytes 3538952 | tf_op jit(solution)/shard_map/ppermute | solution.py:714
  129.7 52.9 %collective-permute-start.9 = (bf16[280,1536]{1,0:T(8,128)(2,1)}, bf16[280,1536]{1,0:T(8,128)(2,1)}, u32[]{:S(2)}, u32[]{:S(2)}) collective-permute-start(bf16[280,1536]{1,0:T(8,128)(2,1)} %dynamic-slice_convert_fusion), channel_id=1, source_target_pairs={{0,4},{1,5},{2,6},{3,7},{4,0},{5,1},{6,2},{7,3},{8,12},{9,13},{10,... | collective-permute-start | bytes 2580488 | tf_op jit(solution)/shard_map/ppermute | solution.py:723
  201.8 187.9 %reduce-scatter.3.cloned.1.call-start = ((), (), s32[]{:S(2)}) async-start(), calls=%async_computation.4 | async-start | bytes 1966080 | tf_op jit(solution)/shard_map/reduce_scatter | solution.py:1030
  219.7 53.7 %collective-permute-start.16 = (bf16[1024,1536]{1,0:T(8,128)(2,1)}, bf16[1024,1536]{1,0:T(8,128)(2,1)}, u32[]{:S(2)}, u32[]{:S(2)}) collective-permute-start(bf16[1024,1536]{1,0:T(8,128)(2,1)} %get-tuple-element.377), channel_id=1, source_target_pairs={{0,8},{8,0},{16,24},{24,16},{1,9},{9,1},{17,25},{25,17},{2,10},{10... | collective-permute-start | bytes 9437192 | tf_op jit(solution)/shard_map/ppermute | solution.py:710
  220.0 50.9 %collective-permute-start.13 = (bf16[2,2,192,608]{3,2,0,1:T(8,128)(2,1)S(1)}, bf16[2,2,192,608]{3,2,0,1:T(8,128)(2,1)S(1)}, u32[]{:S(2)}, u32[]{:S(2)}) collective-permute-start(bf16[2,2,192,608]{3,2,0,1:T(8,128)(2,1)S(1)} %pad_maximum_fusion.12), channel_id=1, source_target_pairs={{0,4},{1,5},{2,6},{3,7},{4,0},{5,1},{6,2},{7,3},{8,12},{9,13},{10,... | collective-permute-start | bytes 2801672 | tf_op jit(solution)/shard_map/ppermute | solution.py:723
  329.5 197.0 %reduce-scatter.5.cloned.1.call-start = ((), (), s32[]{:S(2)}) async-start(), calls=%async_computation.5 | async-start | bytes 2359296 | tf_op jit(solution)/shard_map/reduce_scatter | solution.py:1131
  410.6 61.2 %collective-permute-start.27 = (bf16[2,152,1536]{2,1,0:T(8,128)(2,1)}, bf16[2,152,1536]{2,1,0:T(8,128)(2,1)}, u32[]{:S(2)}, u32[]{:S(2)}) collective-permute-start(bf16[2,152,1536]{2,1,0:T(8,128)(2,1)} %get-tuple-element.313), channel_id=1, source_target_pairs={{0,1},{1,0},{2,3},{3,2},{4,5},{5,4},{6,7},{7,6},{8,9},{9,8},{10,11... | collective-permute-start | bytes 2801672 | tf_op jit(solution)/shard_map/ppermute | solution.py:723
  435.5 74.1 %collective-permute-start.38 = (bf16[2,2,2,192,608]{4,3,2,1,0:T(8,128)(2,1)}, bf16[2,2,2,192,608]{4,3,2,1,0:T(8,128)(2,1)}, u32[]{:S(2)}, u32[]{:S(2)}) collective-permute-start(bf16[2,2,2,192,608]{4,3,2,1,0:T(8,128)(2,1)} %get-tuple-element.287), channel_id=1, source_target_pairs={{0,1},{1,0},{2,3},{3,2},{4,5},{5,4},{6,7},{7,6},{8,9},{9,8},{10,11... | collective-permute-start | bytes 5603336 | tf_op jit(solution)/shard_map/ppermute | solution.py:723
  453.8 134.1 %collective-permute-start.24 = (bf16[1024,1536]{1,0:T(8,128)(2,1)}, bf16[1024,1536]{1,0:T(8,128)(2,1)}, u32[]{:S(2)}, u32[]{:S(2)}) collective-permute-start(bf16[1024,1536]{1,0:T(8,128)(2,1)} %get-tuple-element.184), channel_id=1, source_target_pairs={{0,8},{8,0},{16,24},{24,16},{1,9},{9,1},{17,25},{25,17},{2,10},{10... | collective-permute-start | bytes 9437192 | tf_op jit(solution)/shard_map/ppermute | solution.py:710
  471.8 202.9 %all-gather.12.cloned.1.call-start = ((), (), s32[]{:S(2)}) async-start(), calls=%async_computation.6 | async-start | bytes 4300800 | tf_op jit(solution)/shard_map/all_gather | solution.py:1179
  492.7 57.0 %collective-permute-start.57 = (bf16[2,192,512]{2,1,0:T(8,128)(2,1)}, bf16[2,192,512]{2,1,0:T(8,128)(2,1)}, u32[]{:S(2)}, u32[]{:S(2)}) collective-permute-start(bf16[2,192,512]{2,1,0:T(8,128)(2,1)} %get-tuple-element.343), channel_id=1, source_target_pairs={{0,2},{1,3},{2,0},{3,1},{4,6},{5,7},{6,4},{7,5},{8,10},{9,11},{10,... | collective-permute-start | bytes 1179656 | tf_op jit(solution)/shard_map/ppermute | solution.py:723
  523.7 69.5 %collective-permute-start.39 = (bf16[2,2,192,608]{3,2,1,0:T(8,128)(2,1)}, bf16[2,2,192,608]{3,2,1,0:T(8,128)(2,1)}, u32[]{:S(2)}, u32[]{:S(2)}) collective-permute-start(bf16[2,2,192,608]{3,2,1,0:T(8,128)(2,1)} %get-tuple-element.309), channel_id=1, source_target_pairs={{0,4},{1,5},{2,6},{3,7},{4,0},{5,1},{6,2},{7,3},{8,12},{9,13},{10,... | collective-permute-start | bytes 2801672 | tf_op jit(solution)/shard_map/ppermute | solution.py:723
  549.7 48.2 %collective-permute-start.48 = (bf16[2,192,384]{2,1,0:T(8,128)(2,1)}, bf16[2,192,384]{2,1,0:T(8,128)(2,1)}, u32[]{:S(2)}, u32[]{:S(2)}) collective-permute-start(bf16[2,192,384]{2,1,0:T(8,128)(2,1)} %get-tuple-element.363), channel_id=1, source_target_pairs={{0,2},{1,3},{2,0},{3,1},{4,6},{5,7},{6,4},{7,5},{8,10},{9,11},{10,... | collective-permute-start | bytes 884744 | tf_op jit(solution)/shard_map/ppermute | solution.py:723
  555.3 53.8 %collective-permute-start.58 = (bf16[2,2,192,512]{3,2,1,0:T(8,128)(2,1)S(1)}, bf16[2,2,192,512]{3,2,1,0:T(8,128)(2,1)S(1)}, u32[]{:S(2)}, u32[]{:S(2)}) collective-permute-start(bf16[2,2,192,512]{3,2,1,0:T(8,128)(2,1)S(1)} %get-tuple-element.340), channel_id=1, source_target_pairs={{0,16},{16,0},{8,24},{24,8},{1,17},{17,1},{9,25},{25,9},{2,18},{18... | collective-permute-start | bytes 2359304 | tf_op jit(solution)/shard_map/ppermute | solution.py:714
  587.9 56.5 %collective-permute-start.51 = (bf16[512,1536]{1,0:T(8,128)(2,1)}, bf16[512,1536]{1,0:T(8,128)(2,1)}, u32[]{:S(2)}, u32[]{:S(2)}) collective-permute-start(bf16[512,1536]{1,0:T(8,128)(2,1)} %get-tuple-element.227), channel_id=1, source_target_pairs={{0,8},{8,0},{16,24},{24,16},{1,9},{9,1},{17,25},{25,17},{2,10},{10... | collective-permute-start | bytes 4718600 | tf_op jit(solution)/shard_map/ppermute | solution.py:710
  593.2 77.3 %collective-permute-start.35 = (bf16[128,1536]{1,0:T(8,128)(2,1)}, bf16[128,1536]{1,0:T(8,128)(2,1)}, u32[]{:S(2)}, u32[]{:S(2)}) collective-permute-start(bf16[128,1536]{1,0:T(8,128)(2,1)} %get-tuple-element.296), channel_id=1, source_target_pairs={{0,2},{1,3},{2,0},{3,1},{4,6},{5,7},{6,4},{7,5},{8,10},{9,11},{10,... | collective-permute-start | bytes 1179656 | tf_op jit(solution)/shard_map/ppermute | solution.py:723
  607.1 63.5 %collective-permute-start.36 = (bf16[128,1536]{1,0:T(8,128)(2,1)}, bf16[128,1536]{1,0:T(8,128)(2,1)}, u32[]{:S(2)}, u32[]{:S(2)}) collective-permute-start(bf16[128,1536]{1,0:T(8,128)(2,1)} %get-tuple-element.295), channel_id=1, source_target_pairs={{0,16},{16,0},{8,24},{24,8},{1,17},{17,1},{9,25},{25,9},{2,18},{18... | collective-permute-start | bytes 1179656 | tf_op jit(solution)/shard_map/ppermute | solution.py:714
  667.9 71.6 %collective-permute-start.64 = (bf16[256,1536]{1,0:T(8,128)(2,1)}, bf16[256,1536]{1,0:T(8,128)(2,1)}, u32[]{:S(2)}, u32[]{:S(2)}) collective-permute-start(bf16[256,1536]{1,0:T(8,128)(2,1)} %get-tuple-element.282), channel_id=1, source_target_pairs={{0,16},{16,0},{8,24},{24,8},{1,17},{17,1},{9,25},{25,9},{2,18},{18... | collective-permute-start | bytes 2359304 | tf_op jit(solution)/shard_map/ppermute | solution.py:714
  674.0 65.5 %collective-permute-start.60 = (bf16[256,1536]{1,0:T(8,128)(2,1)}, bf16[256,1536]{1,0:T(8,128)(2,1)}, u32[]{:S(2)}, u32[]{:S(2)}) collective-permute-start(bf16[256,1536]{1,0:T(8,128)(2,1)} %pad_maximum_fusion.23), channel_id=1, source_target_pairs={{0,16},{16,0},{8,24},{24,8},{1,17},{17,1},{9,25},{25,9},{2,18},{18... | collective-permute-start | bytes 2359304 | tf_op jit(solution)/shard_map/ppermute | solution.py:714
  (182 other events, 2066.5 us)
Sparse Core Ops, SparseCore 0:
  11.5 39.8 all-gather.13
  55.4 54.4 all-gather.15
  114.7 61.3 all-gather.7
  201.9 72.5 all-gather.9
  329.6 42.4 reduce-scatter.2
  471.9 54.5 reduce-scatter.4
  551.9 43.2 all-gather.11

commit v14 on v13

--- a/solution.py
+++ b/solution.py
@@ -1177,31 +1177,26 @@
     steps_kv = part_sent(kv_grad, len(bits) - 1, bits[-1])
     share_down = after(jnp.concatenate([down_share_a, down_share_b]), dkv)
     grad_down = lax.all_gather(share_down, "grp", axis=0, tiled=True)
+    marks = [hone_there]
     for i in range(len(bits) - 2, -1, -1):
-        steps_query = part_sent(part_sum(*after(steps_query, d_key)), i, bits[i])
         kv_sum = part_sum(*steps_kv)
-        kv_grad = kv_sum
         steps_kv = part_sent(kv_sum, i, bits[i])
-    sum_b, third_b = columns_third(*after(second_b, kv_grad))
-    share_kv_all = wide(steps_kv[0]) + wide(after(steps_kv[1], third_b[1]))
+        marks.append(kv_sum)
+    for n, i in enumerate(range(len(bits) - 2, -1, -1)):
+        steps_query = part_sent(part_sum(*after(steps_query, marks[n + 1])), i, bits[i])
+    sum_b, third_b = columns_third(*after(second_b, marks[-1]))
+    share_kv_all = wide(steps_kv[0]) + wide(steps_kv[1])
     share_kv = low(share_kv_all[:weight_rows])
     vector_part = share_kv_all[weight_rows : weight_rows + vector_rows]
-    share_query = part_sum(*after(steps_query, kv_grad))
+    share_query = part_sum(*after(steps_query, marks[-1]))
     near_att = swap_core(jnp.stack([att_in, near_att_cross]))
     near_att = jnp.concatenate([att_in, near_att[0], near_att_cross, near_att[1]])
     near_datt = to_strips([d_att[:, strip_q * k : strip_q * (k + 1)] for k in range(4)])
     out_grad = low(left_product(near_att, after(near_datt, d_attended))).reshape(block_shape)
     steps_out = part_sent(out_grad, len(bits) - 1, bits[-1])
-    anchors = [own_part, kv_grad]
-    for i in range(len(bits) - 2, -1, -1):
-        anchor = anchors[min(len(bits) - 2 - i, 1)]
-        steps_out = part_sent(part_sum(*after(steps_out, anchor)), i, bits[i])
-    share_out = part_sum(*after(steps_out, kv_grad))
-
-    grad_out = jnp.concatenate(gather_grp(share_out), axis=1)
-    query_parts = gather_grp(share_query)
-    key_parts = gather_grp(share_kv)
-    grad_attend = jnp.concatenate(query_parts + [key_parts[k] for k in (0, 2, 1, 3)], axis=1)
+    for n, i in enumerate(range(len(bits) - 2, -1, -1)):
+        steps_out = part_sent(part_sum(*after(steps_out, marks[n + 1])), i, bits[i])
+    share_out = part_sum(*after(steps_out, marks[-1]))
 
     other = wide(swap_core(hone_there))
     d_hone = wide(hone_here[:token_count]) + other[:token_count]
@@ -1217,13 +1212,19 @@
     packed = after(packed, (d_hone_send, d_hone))
     packed = packed + swap_cross(packed)
     packed = packed + swap_core(packed)
+    grad_out = jnp.concatenate(gather_grp(after(share_out, packed)), axis=1)
+    query_parts = gather_grp(after(share_query, packed))
+    key_parts = gather_grp(after(share_kv, packed))
+    grad_attend = jnp.concatenate(query_parts + [key_parts[k] for k in (0, 2, 1, 3)], axis=1)
+
     share_vector = packed[:vector_rows].reshape(-1)[:small_count]
     square_sum = packed[vector_rows:] + jnp.sum(share_vector * share_vector)
+    square_sum = after(square_sum, third_b[1])
     for bit in bits:
         square_sum = square_sum + swap_blk(square_sum, bit)
     grad_norm = jnp.sqrt(square_sum[0, 0])
     factor = jnp.minimum(1.0, CLIP_NORM / (grad_norm + 1e-06))
-    out_chip = chip_sum(out_part, after(out_came, kv_grad))
+    out_chip = chip_sum(out_part, after(out_came, marks[1]))
     out_far = scatter_far(out_chip)
     factor = after(factor, (out_chip, near_a))
 

time: 763 us -> 761 us (level)
  waiting for transfers between devices: 274 us -> 243 us
  starting transfers between devices: 77 us -> 101 us
    ppermute x34, waiting for transfers between devices: 227 us -> 201 us  [swap_blk(): return lax.ppermute(values, 'blk', [(i, i ^ bit) for i in range(count)])]
    ppermute x34, starting transfers between devices: 50.3 us -> 72 us  [swap_blk(): return lax.ppermute(values, 'blk', [(i, i ^ bit) for i in range(count)])]
    ppermute x20, waiting for transfers between devices: 41.9 us -> 30 us  [swap_cross(): return lax.ppermute(values, 'grp', CROSS)]
    unnamed x275 -> x281, local copies, waits for them, and re-layouts: 35.9 us -> 34.8 us
  transfers between devices with their start and end apart: 78 -> 78, of which waited for: 33 -> 26; matrix products, arithmetic and copies ran while one was open for 20% -> 20% of each run, Pallas kernels for 24% -> 24%
where the time goes in v14:
time: 761 us; the launch traced here: 754 us
  waiting for transfers between devices  243 us (32%)
  Pallas kernels  185 us (24%)
  other arithmetic  119 us (16%)
  starting transfers between devices  101 us (13%)
  local copies, waits for them, and re-layouts  76.2 us (10%)
  between operations  22.2 us (3%)
    ppermute x34, waiting for transfers between devices, swap_blk(): return lax.ppermute(values, 'blk', [(i, i ^ bit) for i in range(count)])  201 us
    ppermute x34, starting transfers between devices, swap_blk(): return lax.ppermute(values, 'blk', [(i, i ^ bit) for i in range(count)])  72 us
    pallas_call x2, Pallas kernels, middle(): pl.pallas_call(functools.partial(middle_body, prev is not None), grid_spe...  63.5 us
    pallas_call x2, Pallas kernels, adam_columns(): pl.pallas_call(functools.partial(adam_body, blk_count, rate, decay), grid...  36.1 us
    unnamed x281, local copies, waits for them, and re-layouts  34.8 us
    ppermute x20, waiting for transfers between devices, swap_cross(): return lax.ppermute(values, 'grp', CROSS)  30 us
    convert_element_type x20, other arithmetic, low(): return values.astype(jnp.bfloat16)  26.6 us
    ppermute x20, starting transfers between devices, swap_cross(): return lax.ppermute(values, 'grp', CROSS)  25.9 us
  transfers between devices with their start and end apart: 78, of which 26 were waited for; matrix products, arithmetic and copies ran while one was open for 20% of the time, Pallas kernels for 24%

profile of v14, /device:TPU:0, one launch (start us, length us, event | category | flops | bytes accessed | tf_op | source)
XLA Modules:
  0.0 753.6 jit_solution(15977064194227603606)
XLA Ops:
  25.1 17.3 %collective-permute-done.1 = bf16[2,192,512]{2,1,0:T(8,128)(2,1)S(1)} collective-permute-done((bf16[2,192,512]{2,1,0:T(8,128)(2,1)S(1)}, bf16[2,192,512]{2,1,0:T(8,128)(2,1)S(1)}, u32[]{:S(2)}, u32[]{:S(2)}) %collective-permute-start.1) | collective-permute-done | bytes 393248 | tf_op jit(solution)/shard_map/ppermute | solution.py:723
  42.4 8.8 %collective-permute-done.2 = bf16[256,1536]{1,0:T(8,128)(2,1)S(1)} collective-permute-done((bf16[256,1536]{1,0:T(8,128)(2,1)S(1)}, bf16[256,1536]{1,0:T(8,128)(2,1)S(1)}, u32[]{:S(2)}, u32[]{:S(2)}) %collective-permute-start.2) | collective-permute-done | bytes 786464 | tf_op jit(solution)/shard_map/ppermute | solution.py:714
  69.7 9.4 %collective-permute-done.4.cross_ref = bf16[2,256,512]{2,1,0:T(8,128)(2,1)S(1)} collective-permute-done((bf16[2,256,512]{2,1,0:T(8,128)(2,1)S(1)}, bf16[2,256,512]{2,1,0:T(8,128)(2,1)S(1)}, u32[]{:S(2)}, u32[]{:S(2)}) %collective-permute-start.4) | collective-permute-done | bytes 524320 | tf_op jit(solution)/shard_map/ppermute | solution.py:714
  79.2 16.9 %collective-permute-done.7 = bf16[256,1536]{1,0:T(8,128)(2,1)S(1)} collective-permute-done((bf16[256,1536]{1,0:T(8,128)(2,1)}, bf16[256,1536]{1,0:T(8,128)(2,1)S(1)}, u32[]{:S(2)}, u32[]{:S(2)}) %collective-permute-start.7) | collective-permute-done | bytes 786464 | tf_op jit(solution)/shard_map/ppermute | solution.py:723
  96.2 17.0 %collective-permute-done.6 = bf16[2,2,192,512]{3,2,0,1:T(8,128)(2,1)S(1)} collective-permute-done((bf16[2,2,192,512]{3,2,0,1:T(8,128)(2,1)S(1)}, bf16[2,2,192,512]{3,2,0,1:T(8,128)(2,1)S(1)}, u32[]{:S(2)}, u32[]{:S(2)}) %collective-permute-start.6) | collective-permute-done | bytes 786464 | tf_op jit(solution)/shard_map/ppermute | solution.py:723
  133.4 39.6 %collective-permute-done.8 = bf16[2,192,608]{2,1,0:T(8,128)(2,1)S(1)} collective-permute-done((bf16[2,192,608]{2,1,0:T(8,128)(2,1)}, bf16[2,192,608]{2,1,0:T(8,128)(2,1)S(1)}, u32[]{:S(2)}, u32[]{:S(2)}) %collective-permute-start.8) | collective-permute-done | bytes 466976 | tf_op jit(solution)/shard_map/ppermute | solution.py:723
  173.0 9.6 %collective-permute-done.9 = bf16[280,1536]{1,0:T(8,128)(2,1)} collective-permute-done((bf16[280,1536]{1,0:T(8,128)(2,1)}, bf16[280,1536]{1,0:T(8,128)(2,1)}, u32[]{:S(2)}, u32[]{:S(2)}) %collective-permute-start.9) | collective-permute-done | bytes 860192 | tf_op jit(solution)/shard_map/ppermute | solution.py:723
  219.8 8.6 %collective-permute-start.13 = (bf16[2,2,192,608]{3,2,0,1:T(8,128)(2,1)S(1)}, bf16[2,2,192,608]{3,2,0,1:T(8,128)(2,1)S(1)}, u32[]{:S(2)}, u32[]{:S(2)}) collective-permute-start(bf16[2,2,192,608]{3,2,0,1:T(8,128)(2,1)S(1)} %pad_maximum_fusion.12), channel_id=1, source_target_pairs={{0,4},{1,5},{2,6},{3,7},{4,0},{5,1},{6,2},{7,3},{8,12},{9,13},{10,... | collective-permute-start | bytes 2801672 | tf_op jit(solution)/shard_map/ppermute | solution.py:723
  236.8 34.6 %collective-permute-done.13 = bf16[2,2,192,608]{3,2,0,1:T(8,128)(2,1)S(1)} collective-permute-done((bf16[2,2,192,608]{3,2,0,1:T(8,128)(2,1)S(1)}, bf16[2,2,192,608]{3,2,0,1:T(8,128)(2,1)S(1)}, u32[]{:S(2)}, u32[]{:S(2)}) %collective-permute-start.13) | collective-permute-done | bytes 933920 | tf_op jit(solution)/shard_map/ppermute | solution.py:723
  281.3 24.3 %middle.2 = (bf16[2048,512]{1,0:T(8,128)(2,1)S(1)}, bf16[2048,512]{1,0:T(8,128)(2,1)S(1)}, bf16[2048,512]{1,0:T(8,128)(2,1)}, bf16[1024,1536]{1,0:T(8,128)(2,1)}, bf16[1024,1536]{1,0:T(8,128)(2,1)}) custom-call(s32[8]{0:T(128)S(1)} %stack.298.order, bf16[2048,1536]{1,0:T(8,128)(2,1)} %all-gather.10.cloned.1.call-done.h_ref, ...), custom_call_target="tpu_custom_call" | custom-call | flops 1000 | bytes 1000 | tf_op jit(solution)/shard_map/middle/pallas_call | solution.py:386
  305.7 12.7 %collective-permute-done.18 = bf16[2,2,2,192,608]{4,3,0,2,1:T(8,128)(2,1)} collective-permute-done((bf16[2,2,2,192,608]{4,3,0,2,1:T(8,128)(2,1)}, bf16[2,2,2,192,608]{4,3,0,2,1:T(8,128)(2,1)}, u32[]{:S(2)}, u32[]{:S(2)}) %collective-permute-start.18) | collective-permute-done | bytes 1867808 | tf_op jit(solution)/shard_map/ppermute | solution.py:723
  333.8 10.3 %two_grads.2 = bf16[2,1536,512]{2,1,0:T(8,128)(2,1)} custom-call(bf16[2048,1536]{1,0:T(8,128)(2,1)} %all-gather.10.cloned.1.call-done.h_ref, bf16[2048,512]{1,0:T(8,128)(2,1)S(1)} %copy-done.21, bf16[2048,512]{1,0:T(8,128)(2,1)S(1)} %copy-done.22), custom_call_target="tpu_custom_call" | custom-call | flops 1000 | bytes 1000 | tf_op jit(solution)/shard_map/two_grads/pallas_call | solution.py:419
  348.6 39.1 %middle.3 = (bf16[2048,608]{1,0:T(8,128)(2,1)S(1)}, bf16[2048,608]{1,0:T(8,128)(2,1)}, bf16[2048,608]{1,0:T(8,128)(2,1)}, bf16[1024,1536]{1,0:T(8,128)(2,1)}, bf16[1024,1536]{1,0:T(8,128)(2,1)}) custom-call(s32[8]{0:T(128)S(1)} %stack.298.order, bf16[2048,1536]{1,0:T(8,128)(2,1)} %all-gather.10.cloned.1.call-done.h_ref, ...), custom_call_target="tpu_custom_call" | custom-call | flops 1000 | bytes 1000 | tf_op jit(solution)/shard_map/middle/pallas_call | solution.py:386
  412.5 13.5 %two_grads.3 = bf16[2,1536,608]{2,1,0:T(8,128)(2,1)} custom-call(bf16[2048,1536]{1,0:T(8,128)(2,1)} %all-gather.10.cloned.1.call-done.h_ref, bf16[2048,608]{1,0:T(8,128)(2,1)S(1)} %copy-done.18, bf16[2048,608]{1,0:T(8,128)(2,1)S(1)} %copy-done.19), custom_call_target="tpu_custom_call" | custom-call | flops 1000 | bytes 1000 | tf_op jit(solution)/shard_map/two_grads/pallas_call | solution.py:419
  441.9 12.7 %down.1 = (bf16[1024,1536]{1,0:T(8,128)(2,1)}, bf16[1024,1536]{1,0:T(8,128)(2,1)}) custom-call(bf16[2048,512]{1,0:T(8,128)(2,1)S(1)} %copy-done.6, bf16[2048,608]{1,0:T(8,128)(2,1)} %copy-done.1, bf16[512,1536]{1,0:T(8,128)(2,1)S(1)} %bitcast.413, bf16[608,1536]{1,0:T(8,128)(2,1)S(1)} %bitcast.411), custom_call_target="tpu_custom_call" | custom-call | flops 1000 | bytes 1000 | tf_op jit(solution)/shard_map/down/pallas_call | solution.py:468
  465.3 8.0 %attend_back.1 = (bf16[256,1536]{1,0:T(8,128)(2,1)S(1)}, bf16[8,2,128,512]{3,2,1,0:T(8,128)(2,1)}) custom-call(s32[3]{0:T(128)S(1)} %copy-done.37, bf16[256,1536]{1,0:T(8,128)(2,1)S(1)} %copy-done.13, bf16[8,2,128,512]{3,2,1,0:T(8,128)(2,1)} %all-gather.8.cloned.1.call-done.k_ref.v_ref, bf16[8,2,128,512]{3,2,1,0:T(8,128)(2,1)} %all-gather.8.cloned.1.call-done.k_ref.v_ref, ...), custom_call_target="tpu_custom_call" | custom-call | flops 1000 | bytes 1000 | tf_op jit(solution)/shard_map/attend_back/pallas_call | solution.py:315
  523.8 9.6 %reduce-scatter.5.cloned.1.call-done.dkv_ref = bf16[256,512]{1,0:T(8,128)(2,1)} async-done(((bf16[2048,512]{1,0:T(8,128)(2,1)}), bf16[256,512]{1,0:T(8,128)(2,1)}) %reduce-scatter.5.cloned.1.call-update) | async-done | bytes 262160 | tf_op jit(solution)/shard_map/reduce_scatter | solution.py:1131
  565.3 18.1 %collective-permute-start.36 = (bf16[2,208,128]{2,1,0:T(8,128)(2,1)S(1)}, bf16[2,208,128]{2,1,0:T(8,128)(2,1)S(1)}, u32[]{:S(2)}, u32[]{:S(2)}) collective-permute-start(bf16[2,208,128]{2,1,0:T(8,128)(2,1)S(1)} %dynamic-slice_bitcast_fusion.27), channel_id=1, source_target_pairs={{0,2},{1,3},{2,0},{3,1},{4,6},{5,7},{6,4},{7,5},{8,10},{9,11},{10,... | collective-permute-start | bytes 319496 | tf_op jit(solution)/shard_map/ppermute | solution.py:723
  592.1 8.0 %collective-permute-done.37 = bf16[208,128]{1,0:T(8,128)(2,1)S(1)} collective-permute-done((bf16[208,128]{1,0:T(8,128)(2,1)S(1)}, bf16[208,128]{1,0:T(8,128)(2,1)S(1)}, u32[]{:S(2)}, u32[]{:S(2)}) %collective-permute-start.37) | collective-permute-done | bytes 53280 | tf_op jit(solution)/shard_map/ppermute | solution.py:723
  605.2 8.5 %collective-permute-done.40 = bf16[192,384]{1,0:T(8,128)(2,1)S(1)} collective-permute-done((bf16[192,384]{1,0:T(8,128)(2,1)S(1)}, bf16[192,384]{1,0:T(8,128)(2,1)S(1)}, u32[]{:S(2)}, u32[]{:S(2)}) %collective-permute-start.40) | collective-permute-done | bytes 147488 | tf_op jit(solution)/shard_map/ppermute | solution.py:723
  633.5 8.1 %collective-permute-done.53 = bf16[2,192,608]{2,1,0:T(8,128)(2,1)S(1)} collective-permute-done((bf16[2,192,608]{2,1,0:T(8,128)(2,1)S(1)}, bf16[2,192,608]{2,1,0:T(8,128)(2,1)S(1)}, u32[]{:S(2)}, u32[]{:S(2)}) %collective-permute-start.53) | collective-permute-done | bytes 466976 | tf_op jit(solution)/shard_map/ppermute | solution.py:723
  672.2 17.0 %multiply_subtract_fusion = (f32[1120,1536]{1,0:T(8,128)}, f32[1120,1536]{1,0:T(8,128)}, f32[1120,1536]{1,0:T(8,128)}) fusion(f32[1120,1536]{1,0:T(8,128)} %param.30, bf16[1120,1536]{1,0:T(8,128)(2,1)} %all-gather.12.cloned.1.call-done, f32[]{:T(128)} %min.3, f32[1120,1536]{1,0:T(8,128)} %param.36, f32[1120,1536]{1,0:T(8,128)} %param.42), kind=kLoop, calls=%fused_computation.2 | loop fusion | flops 29245440 | bytes 44728324 | tf_op jit(solution)/shard_map/sub | solution.py:67
  701.7 18.0 %adam_columns.2 = (f32[192,8960]{1,0:T(8,128)}, f32[192,8960]{1,0:T(8,128)}, f32[192,8960]{1,0:T(8,128)}) custom-call(s32[2]{0:T(128)S(1)} %pad_add_fusion.1.ids, f32[1]{0:T(128)} %bitcast.127.factor_ref, bf16[2,2,2,192,512]{4,3,2,1,0:T(8,128)(2,1)S(1)} %pad_maximum_fusion.11.first_ref, ...), custom_call_target="tpu_custom_call" | custom-call | flops 1000 | bytes 1000 | tf_op jit(solution)/shard_map/adam_columns/pallas_call | solution.py:159
  719.7 18.0 %adam_columns.3 = (f32[192,8960]{1,0:T(8,128)}, f32[192,8960]{1,0:T(8,128)}, f32[192,8960]{1,0:T(8,128)}) custom-call(s32[2]{0:T(128)S(1)} %pad_add_fusion.1.ids, f32[1]{0:T(128)} %bitcast.127.factor_ref, bf16[2,2,2,192,512]{4,3,2,1,0:T(8,128)(2,1)S(1)} %pad_maximum_fusion.11.first_ref, ...), custom_call_target="tpu_custom_call" | custom-call | flops 1000 | bytes 1000 | tf_op jit(solution)/shard_map/adam_columns/pallas_call | solution.py:159
  (616 shorter events, 343.5 us)
Async XLA Ops:
  11.4 106.8 %all-gather.16.cloned.1.call-start = ((), (), s32[]{:S(2)}) async-start(), calls=%async_computation.8 | async-start | bytes 1327104 | tf_op jit(solution)/shard_map/all_gather | solution.py:836
  55.3 127.3 %all-gather.8.cloned.1.call-start = ((), (), s32[]{:S(2)}) async-start(), calls=%async_computation.2 | async-start | bytes 2359296 | tf_op jit(solution)/shard_map/all_gather | solution.py:836
  67.0 46.2 %collective-permute-start.6 = (bf16[2,2,192,512]{3,2,0,1:T(8,128)(2,1)S(1)}, bf16[2,2,192,512]{3,2,0,1:T(8,128)(2,1)S(1)}, u32[]{:S(2)}, u32[]{:S(2)}) collective-permute-start(bf16[2,2,192,512]{3,2,0,1:T(8,128)(2,1)S(1)} %pad_maximum_fusion.17), channel_id=1, source_target_pairs={{0,4},{1,5},{2,6},{3,7},{4,0},{5,1},{6,2},{7,3},{8,12},{9,13},{10,... | collective-permute-start | bytes 2359304 | tf_op jit(solution)/shard_map/ppermute | solution.py:723
  114.6 166.7 %all-gather.10.cloned.1.call-start = ((), (), s32[]{:S(2)}) async-start(), calls=%async_computation.3 | async-start | bytes 7077888 | tf_op jit(solution)/shard_map/all_gather | solution.py:1023
  116.7 65.9 %collective-permute-start.10 = (bf16[2,2,2,192,512]{4,3,0,2,1:T(8,128)(2,1)}, bf16[2,2,2,192,512]{4,3,0,2,1:T(8,128)(2,1)}, u32[]{:S(2)}, u32[]{:S(2)}) collective-permute-start(bf16[2,2,2,192,512]{4,3,0,2,1:T(8,128)(2,1)} %pad_maximum_fusion.9), channel_id=1, source_target_pairs={{0,1},{1,0},{2,3},{3,2},{4,5},{5,4},{6,7},{7,6},{8,9},{9,8},{10,11... | collective-permute-start | bytes 4718600 | tf_op jit(solution)/shard_map/ppermute | solution.py:723
  125.8 56.8 %collective-permute-start.11 = (bf16[1536,384]{1,0:T(8,128)(2,1)S(1)}, bf16[1536,384]{1,0:T(8,128)(2,1)}, u32[]{:S(2)}, u32[]{:S(2)}) collective-permute-start(bf16[1536,384]{1,0:T(8,128)(2,1)S(1)} %bitcast_dynamic-update-slice_fusion), channel_id=1, source_target_pairs={{0,16},{16,0},{8,24},{24,8},{1,17},{17,1},{9,25},{25,9},{2,18},{18... | collective-permute-start | bytes 3538952 | tf_op jit(solution)/shard_map/ppermute | solution.py:714
  129.7 52.9 %collective-permute-start.9 = (bf16[280,1536]{1,0:T(8,128)(2,1)}, bf16[280,1536]{1,0:T(8,128)(2,1)}, u32[]{:S(2)}, u32[]{:S(2)}) collective-permute-start(bf16[280,1536]{1,0:T(8,128)(2,1)} %dynamic-slice_convert_fusion), channel_id=1, source_target_pairs={{0,4},{1,5},{2,6},{3,7},{4,0},{5,1},{6,2},{7,3},{8,12},{9,13},{10,... | collective-permute-start | bytes 2580488 | tf_op jit(solution)/shard_map/ppermute | solution.py:723
  201.8 188.3 %reduce-scatter.3.cloned.1.call-start = ((), (), s32[]{:S(2)}) async-start(), calls=%async_computation.4 | async-start | bytes 1966080 | tf_op jit(solution)/shard_map/reduce_scatter | solution.py:1030
  219.6 53.8 %collective-permute-start.16 = (bf16[1024,1536]{1,0:T(8,128)(2,1)}, bf16[1024,1536]{1,0:T(8,128)(2,1)}, u32[]{:S(2)}, u32[]{:S(2)}) collective-permute-start(bf16[1024,1536]{1,0:T(8,128)(2,1)} %get-tuple-element.383), channel_id=1, source_target_pairs={{0,8},{8,0},{16,24},{24,16},{1,9},{9,1},{17,25},{25,17},{2,10},{10... | collective-permute-start | bytes 9437192 | tf_op jit(solution)/shard_map/ppermute | solution.py:710
  219.8 51.6 %collective-permute-start.13 = (bf16[2,2,192,608]{3,2,0,1:T(8,128)(2,1)S(1)}, bf16[2,2,192,608]{3,2,0,1:T(8,128)(2,1)S(1)}, u32[]{:S(2)}, u32[]{:S(2)}) collective-permute-start(bf16[2,2,192,608]{3,2,0,1:T(8,128)(2,1)S(1)} %pad_maximum_fusion.12), channel_id=1, source_target_pairs={{0,4},{1,5},{2,6},{3,7},{4,0},{5,1},{6,2},{7,3},{8,12},{9,13},{10,... | collective-permute-start | bytes 2801672 | tf_op jit(solution)/shard_map/ppermute | solution.py:723
  330.1 203.3 %reduce-scatter.5.cloned.1.call-start = ((), (), s32[]{:S(2)}) async-start(), calls=%async_computation.5 | async-start | bytes 2359296 | tf_op jit(solution)/shard_map/reduce_scatter | solution.py:1131
  410.5 62.9 %collective-permute-start.27 = (bf16[2,152,1536]{2,1,0:T(8,128)(2,1)}, bf16[2,152,1536]{2,1,0:T(8,128)(2,1)}, u32[]{:S(2)}, u32[]{:S(2)}) collective-permute-start(bf16[2,152,1536]{2,1,0:T(8,128)(2,1)} %get-tuple-element.319), channel_id=1, source_target_pairs={{0,1},{1,0},{2,3},{3,2},{4,5},{5,4},{6,7},{7,6},{8,9},{9,8},{10,11... | collective-permute-start | bytes 2801672 | tf_op jit(solution)/shard_map/ppermute | solution.py:723
  437.6 46.3 %collective-permute-start.47 = (bf16[2,2,192,512]{3,2,1,0:T(8,128)(2,1)}, bf16[2,2,192,512]{3,2,1,0:T(8,128)(2,1)}, u32[]{:S(2)}, u32[]{:S(2)}) collective-permute-start(bf16[2,2,192,512]{3,2,1,0:T(8,128)(2,1)} %get-tuple-element.323), channel_id=1, source_target_pairs={{0,4},{1,5},{2,6},{3,7},{4,0},{5,1},{6,2},{7,3},{8,12},{9,13},{10,... | collective-permute-start | bytes 2359304 | tf_op jit(solution)/shard_map/ppermute | solution.py:723
  440.7 68.9 %collective-permute-start.48 = (bf16[2,2,2,192,608]{4,3,2,1,0:T(8,128)(2,1)}, bf16[2,2,2,192,608]{4,3,2,1,0:T(8,128)(2,1)}, u32[]{:S(2)}, u32[]{:S(2)}) collective-permute-start(bf16[2,2,2,192,608]{4,3,2,1,0:T(8,128)(2,1)} %get-tuple-element.293), channel_id=1, source_target_pairs={{0,1},{1,0},{2,3},{3,2},{4,5},{5,4},{6,7},{7,6},{8,9},{9,8},{10,11... | collective-permute-start | bytes 5603336 | tf_op jit(solution)/shard_map/ppermute | solution.py:723
  454.5 107.3 %collective-permute-start.24 = (bf16[1024,1536]{1,0:T(8,128)(2,1)}, bf16[1024,1536]{1,0:T(8,128)(2,1)}, u32[]{:S(2)}, u32[]{:S(2)}) collective-permute-start(bf16[1024,1536]{1,0:T(8,128)(2,1)} %get-tuple-element.187), channel_id=1, source_target_pairs={{0,8},{8,0},{16,24},{24,16},{1,9},{9,1},{17,25},{25,17},{2,10},{10... | collective-permute-start | bytes 9437192 | tf_op jit(solution)/shard_map/ppermute | solution.py:710
  473.4 198.8 %all-gather.12.cloned.1.call-start = ((), (), s32[]{:S(2)}) async-start(), calls=%async_computation.6 | async-start | bytes 4300800 | tf_op jit(solution)/shard_map/all_gather | solution.py:1179
  493.4 46.0 %collective-permute-start.57 = (bf16[2,192,512]{2,1,0:T(8,128)(2,1)}, bf16[2,192,512]{2,1,0:T(8,128)(2,1)}, u32[]{:S(2)}, u32[]{:S(2)}) collective-permute-start(bf16[2,192,512]{2,1,0:T(8,128)(2,1)} %get-tuple-element.349), channel_id=1, source_target_pairs={{0,2},{1,3},{2,0},{3,1},{4,6},{5,7},{6,4},{7,5},{8,10},{9,11},{10,... | collective-permute-start | bytes 1179656 | tf_op jit(solution)/shard_map/ppermute | solution.py:723
  513.2 75.6 %collective-permute-start.49 = (bf16[2,2,192,608]{3,2,1,0:T(8,128)(2,1)}, bf16[2,2,192,608]{3,2,1,0:T(8,128)(2,1)}, u32[]{:S(2)}, u32[]{:S(2)}) collective-permute-start(bf16[2,2,192,608]{3,2,1,0:T(8,128)(2,1)} %get-tuple-element.315), channel_id=1, source_target_pairs={{0,4},{1,5},{2,6},{3,7},{4,0},{5,1},{6,2},{7,3},{8,12},{9,13},{10,... | collective-permute-start | bytes 2801672 | tf_op jit(solution)/shard_map/ppermute | solution.py:723
  517.6 47.7 %collective-permute-start.38 = (bf16[2,2,192,384]{3,2,1,0:T(8,128)(2,1)}, bf16[2,2,192,384]{3,2,1,0:T(8,128)(2,1)}, u32[]{:S(2)}, u32[]{:S(2)}) collective-permute-start(bf16[2,2,192,384]{3,2,1,0:T(8,128)(2,1)} %get-tuple-element.335), channel_id=1, source_target_pairs={{0,1},{1,0},{2,3},{3,2},{4,5},{5,4},{6,7},{7,6},{8,9},{9,8},{10,11... | collective-permute-start | bytes 1769480 | tf_op jit(solution)/shard_map/ppermute | solution.py:723
  559.8 81.8 %collective-permute-start.58 = (bf16[2,2,192,512]{3,2,1,0:T(8,128)(2,1)}, bf16[2,2,192,512]{3,2,1,0:T(8,128)(2,1)}, u32[]{:S(2)}, u32[]{:S(2)}) collective-permute-start(bf16[2,2,192,512]{3,2,1,0:T(8,128)(2,1)} %get-tuple-element.346), channel_id=1, source_target_pairs={{0,16},{16,0},{8,24},{24,8},{1,17},{17,1},{9,25},{25,9},{2,18},{18... | collective-permute-start | bytes 2359304 | tf_op jit(solution)/shard_map/ppermute | solution.py:714
  561.9 61.7 %collective-permute-start.50 = (bf16[512,1536]{1,0:T(8,128)(2,1)}, bf16[512,1536]{1,0:T(8,128)(2,1)}, u32[]{:S(2)}, u32[]{:S(2)}) collective-permute-start(bf16[512,1536]{1,0:T(8,128)(2,1)} %get-tuple-element.229), channel_id=1, source_target_pairs={{0,8},{8,0},{16,24},{24,16},{1,9},{9,1},{17,25},{25,17},{2,10},{10... | collective-permute-start | bytes 4718600 | tf_op jit(solution)/shard_map/ppermute | solution.py:710
  665.7 72.0 %collective-permute-start.64 = (bf16[256,1536]{1,0:T(8,128)(2,1)}, bf16[256,1536]{1,0:T(8,128)(2,1)}, u32[]{:S(2)}, u32[]{:S(2)}) collective-permute-start(bf16[256,1536]{1,0:T(8,128)(2,1)} %get-tuple-element.288), channel_id=1, source_target_pairs={{0,16},{16,0},{8,24},{24,8},{1,17},{17,1},{9,25},{25,9},{2,18},{18... | collective-permute-start | bytes 2359304 | tf_op jit(solution)/shard_map/ppermute | solution.py:714
  671.9 65.9 %collective-permute-start.60 = (bf16[256,1536]{1,0:T(8,128)(2,1)}, bf16[256,1536]{1,0:T(8,128)(2,1)}, u32[]{:S(2)}, u32[]{:S(2)}) collective-permute-start(bf16[256,1536]{1,0:T(8,128)(2,1)} %pad_maximum_fusion.23), channel_id=1, source_target_pairs={{0,16},{16,0},{8,24},{24,8},{1,17},{17,1},{9,25},{25,9},{2,18},{18... | collective-permute-start | bytes 2359304 | tf_op jit(solution)/shard_map/ppermute | solution.py:714
  691.9 45.8 %collective-permute-start.61 = (bf16[256,1536]{1,0:T(8,128)(2,1)}, bf16[256,1536]{1,0:T(8,128)(2,1)}, u32[]{:S(2)}, u32[]{:S(2)}) collective-permute-start(bf16[256,1536]{1,0:T(8,128)(2,1)} %pad_maximum_fusion.24), channel_id=1, source_target_pairs={{0,2},{1,3},{2,0},{3,1},{4,6},{5,7},{6,4},{7,5},{8,10},{9,11},{10,... | collective-permute-start | bytes 2359304 | tf_op jit(solution)/shard_map/ppermute | solution.py:723
  (185 other events, 2069.6 us)
Sparse Core Ops, SparseCore 0:
  11.5 39.8 all-gather.13
  55.4 54.4 all-gather.15
  114.7 61.3 all-gather.7
  201.9 73.1 all-gather.9
  330.2 42.1 reduce-scatter.2
  473.5 59.8 reduce-scatter.4
  542.0 57.5 all-gather.11

commit v15 on v14

--- a/solution.py
+++ b/solution.py
@@ -995,13 +995,14 @@
     got_b, down_got = after((got_b, down_got), kv_all)
     kv_all = after(kv_all, (got_b, down_got, pair_y_got))
     down_here = place(down_here, down_got, [], bits[0])
-    down_here = lows_of(down_here, [bits[0]]).reshape(2 * blk_count // 4, quarter, D)
+    down_y_got = swap_blk(down_here, lows[0])
+    down_here = place(down_here, down_y_got, [bits[0]], lows[0])
+    for n in range(1, len(lows)):
+        done = [bits[0]] + lows[:n]
+        down_here = place(down_here, swap_blk(down_here, lows[n]), done, lows[n])
+    down_here = down_here.reshape(2 * blk_count // 4, quarter, D)
     dy_first = swap_blk(dy_cross[:half], team)
     dy_second = swap_cross(dy_over[half:])
-    dy_chip = jnp.concatenate([dy_low, dy_cross, dy_over, dy_first, dy_second])
-    dy_team = jnp.concatenate([dy_chip, swap_core(dy_chip)])
-    pair_b = team_pair(picked_b[0], after(got_b, kv_all))
-    pair_b_got = swap_blk(pair_b, bits[0])
     out_ring = after(out_ring, packed_kv)
     out_strip = jnp.concatenate([out_ring[ring.index(b)] for b in range(blk_count)])
     out_cross = swap_cross(out_strip)
@@ -1009,6 +1010,8 @@
     out_full = jnp.concatenate(by_place([out_strip, out_core[0], out_cross, out_core[1]]), axis=1)
 
     att_in, lse = attend(attend_ids, query, kv_all, seg_key, seg_query, block_len)
+    pair_b = team_pair(picked_b[0], after(got_b, att_in))
+    pair_b_got = swap_blk(pair_b, bits[0])
     flat = wide(flat_low)
     resid = flat + jnp.dot(att_in, out_full, preferred_element_type=jnp.float32)
     h_two = low(norm_apply(resid, gain_two))
@@ -1017,7 +1020,10 @@
         done = [bits[0], team] + lows[:i]
         pair_a = place(pair_a, swap_blk(pair_a, lows[i]), done, lows[i], 1)
     gate_up_a = pair_a.reshape(2, D, -1)
-    pair_b_got = after(pair_b_got, h_two)
+    pair_b_got = after(pair_b_got, (h_two, down_y_got))
+    dy_first, dy_second = after((dy_first, dy_second), pair_b_got)
+    dy_chip = jnp.concatenate([dy_low, dy_cross, dy_over, dy_first, dy_second])
+    dy_team = jnp.concatenate([dy_chip, swap_core(dy_chip)])
     down_a = down_here[:, :size_first].reshape(widths[0], D)
     down_b = down_here[:, size_first:].reshape(widths[1], D)
     h_team = lax.all_gather(h_two, ("grp", "blk"), axis=0, tiled=True, axis_index_groups=teams)
@@ -1144,7 +1150,13 @@
     near_dq = to_strips([d_query[:, strip_q * k : strip_q * (k + 1)] for k in range(4)])
     block_shape = (2,) * len(bits) + (weight_rows, -1)
     query_grad = low(left_product(near_one, near_dq)).reshape(block_shape)
-    steps_query = part_sent(query_grad, len(bits) - 1, bits[-1])
+
+    near_att = swap_core(jnp.stack([att_in, near_att_cross]))
+    near_att = jnp.concatenate([att_in, near_att[0], near_att_cross, near_att[1]])
+    near_datt = to_strips([d_att[:, strip_q * k : strip_q * (k + 1)] for k in range(4)])
+    out_grad = low(left_product(near_att, after(near_datt, d_attended))).reshape(block_shape)
+    query_out = jnp.concatenate([query_grad, out_grad], axis=-1)
+    steps_query = part_sent(query_out, len(bits) - 1, bits[-1])
     second_b = part_sent(columns_mid(*after(first_b, d_query)), 1, bits[0])
     dkv = after(dkv, down_share_b)
     own_part, core_part, far_part, bias_kv = turn_dkv(
@@ -1188,15 +1200,7 @@
     share_kv_all = wide(steps_kv[0]) + wide(steps_kv[1])
     share_kv = low(share_kv_all[:weight_rows])
     vector_part = share_kv_all[weight_rows : weight_rows + vector_rows]
-    share_query = part_sum(*after(steps_query, marks[-1]))
-    near_att = swap_core(jnp.stack([att_in, near_att_cross]))
-    near_att = jnp.concatenate([att_in, near_att[0], near_att_cross, near_att[1]])
-    near_datt = to_strips([d_att[:, strip_q * k : strip_q * (k + 1)] for k in range(4)])
-    out_grad = low(left_product(near_att, after(near_datt, d_attended))).reshape(block_shape)
-    steps_out = part_sent(out_grad, len(bits) - 1, bits[-1])
-    for n, i in enumerate(range(len(bits) - 2, -1, -1)):
-        steps_out = part_sent(part_sum(*after(steps_out, marks[n + 1])), i, bits[i])
-    share_out = part_sum(*after(steps_out, marks[-1]))
+    share_query_out = part_sum(*after(steps_query, marks[-1]))
 
     other = wide(swap_core(hone_there))
     d_hone = wide(hone_here[:token_count]) + other[:token_count]
@@ -1205,18 +1209,19 @@
     square_sum = square_total(
         [
             wide(s)
-            for s in (share_query, share_kv, share_out, sum_a, sum_b, share_down)
+            for s in (share_query_out, share_kv, sum_a, sum_b, share_down)
         ]
     )
     packed = jnp.concatenate([vector_part, jnp.full((8, HD), square_sum)])
     packed = after(packed, (d_hone_send, d_hone))
     packed = packed + swap_cross(packed)
     packed = packed + swap_core(packed)
-    grad_out = jnp.concatenate(gather_grp(after(share_out, packed)), axis=1)
-    query_parts = gather_grp(after(share_query, packed))
-    key_parts = gather_grp(after(share_kv, packed))
-    grad_attend = jnp.concatenate(query_parts + [key_parts[k] for k in (0, 2, 1, 3)], axis=1)
-
+    parts = gather_grp(after(jnp.concatenate([share_query_out, share_kv], axis=1), packed))
+    grad_out = jnp.concatenate([part[:, strip_q : 2 * strip_q] for part in parts], axis=1)
+    grad_attend = jnp.concatenate(
+        [part[:, :strip_q] for part in parts] + [parts[k][:, 2 * strip_q :] for k in (0, 2, 1, 3)],
+        axis=1,
+    )
     share_vector = packed[:vector_rows].reshape(-1)[:small_count]
     square_sum = packed[vector_rows:] + jnp.sum(share_vector * share_vector)
     square_sum = after(square_sum, third_b[1])

time: 761 us -> 751 us (0.987)
  starting transfers between devices: 101 us -> 90.4 us
    ppermute x20 -> x18, starting transfers between devices: 25.9 us -> 20.5 us  [swap_cross(): return lax.ppermute(values, 'grp', CROSS)]
    ppermute x34 -> x31, starting transfers between devices: 72 us -> 67.7 us  [swap_blk(): return lax.ppermute(values, 'blk', [(i, i ^ bit) for i in range(count)])]
    unnamed x281 -> x286, local copies, waits for them, and re-layouts: 34.8 us -> 38 us
    ppermute x20 -> x18, waiting for transfers between devices: 30 us -> 27.8 us  [swap_cross(): return lax.ppermute(values, 'grp', CROSS)]
    ppermute x34 -> x31, waiting for transfers between devices: 201 us -> 204 us  [swap_blk(): return lax.ppermute(values, 'blk', [(i, i ^ bit) for i in range(count)])]
    convert_element_type x20 -> x18, other arithmetic: 26.6 us -> 27.1 us  [low(): return values.astype(jnp.bfloat16)]
  transfers between devices with their start and end apart: 78 -> 71, of which waited for: 26 -> 26; matrix products, arithmetic and copies ran while one was open for 20% -> 20% of each run, Pallas kernels for 24% -> 24%
where the time goes in v15:
time: 751 us; the launch traced here: 743 us
  waiting for transfers between devices  245 us (33%)
  Pallas kernels  185 us (25%)
  other arithmetic  114 us (15%)
  starting transfers between devices  90.4 us (12%)
  local copies, waits for them, and re-layouts  79 us (11%)
  between operations  21.5 us (3%)
    ppermute x31, waiting for transfers between devices, swap_blk(): return lax.ppermute(values, 'blk', [(i, i ^ bit) for i in range(count)])  204 us
    ppermute x31, starting transfers between devices, swap_blk(): return lax.ppermute(values, 'blk', [(i, i ^ bit) for i in range(count)])  67.7 us
    pallas_call x2, Pallas kernels, middle(): pl.pallas_call(functools.partial(middle_body, prev is not None), grid_spe...  63.3 us
    unnamed x286, local copies, waits for them, and re-layouts  38 us
    pallas_call x2, Pallas kernels, adam_columns(): pl.pallas_call(functools.partial(adam_body, blk_count, rate, decay), grid...  36.1 us
    ppermute x18, waiting for transfers between devices, swap_cross(): return lax.ppermute(values, 'grp', CROSS)  27.8 us
    convert_element_type x18, other arithmetic, low(): return values.astype(jnp.bfloat16)  27.1 us
    sub x4, other arithmetic, adam_step(): weight - rate * (first_hat / (jnp.sqrt(second_hat) + ADAM_EPS) + decay *...  24.2 us
  transfers between devices with their start and end apart: 71, of which 26 were waited for; matrix products, arithmetic and copies ran while one was open for 20% of the time, Pallas kernels for 24%

profile of v15, /device:TPU:0, one launch (start us, length us, event | category | flops | bytes accessed | tf_op | source)
XLA Modules:
  0.0 742.5 jit_solution(3241555150143361887)
XLA Ops:
  25.1 17.3 %collective-permute-done.1 = bf16[2,192,512]{2,1,0:T(8,128)(2,1)S(1)} collective-permute-done((bf16[2,192,512]{2,1,0:T(8,128)(2,1)S(1)}, bf16[2,192,512]{2,1,0:T(8,128)(2,1)S(1)}, u32[]{:S(2)}, u32[]{:S(2)}) %collective-permute-start.1) | collective-permute-done | bytes 393248 | tf_op jit(solution)/shard_map/ppermute | solution.py:723
  42.4 8.8 %collective-permute-done.2 = bf16[256,1536]{1,0:T(8,128)(2,1)S(1)} collective-permute-done((bf16[256,1536]{1,0:T(8,128)(2,1)S(1)}, bf16[256,1536]{1,0:T(8,128)(2,1)S(1)}, u32[]{:S(2)}, u32[]{:S(2)}) %collective-permute-start.2) | collective-permute-done | bytes 786464 | tf_op jit(solution)/shard_map/ppermute | solution.py:714
  69.7 9.4 %collective-permute-done.4.cross_ref = bf16[2,256,512]{2,1,0:T(8,128)(2,1)S(1)} collective-permute-done((bf16[2,256,512]{2,1,0:T(8,128)(2,1)S(1)}, bf16[2,256,512]{2,1,0:T(8,128)(2,1)S(1)}, u32[]{:S(2)}, u32[]{:S(2)}) %collective-permute-start.4) | collective-permute-done | bytes 524320 | tf_op jit(solution)/shard_map/ppermute | solution.py:714
  79.2 16.9 %collective-permute-done.7 = bf16[256,1536]{1,0:T(8,128)(2,1)S(1)} collective-permute-done((bf16[256,1536]{1,0:T(8,128)(2,1)}, bf16[256,1536]{1,0:T(8,128)(2,1)S(1)}, u32[]{:S(2)}, u32[]{:S(2)}) %collective-permute-start.7) | collective-permute-done | bytes 786464 | tf_op jit(solution)/shard_map/ppermute | solution.py:723
  96.2 17.1 %collective-permute-done.6 = bf16[2,2,192,512]{3,2,0,1:T(8,128)(2,1)S(1)} collective-permute-done((bf16[2,2,192,512]{3,2,0,1:T(8,128)(2,1)S(1)}, bf16[2,2,192,512]{3,2,0,1:T(8,128)(2,1)S(1)}, u32[]{:S(2)}, u32[]{:S(2)}) %collective-permute-start.6) | collective-permute-done | bytes 786464 | tf_op jit(solution)/shard_map/ppermute | solution.py:723
  132.7 40.2 %collective-permute-done.8 = bf16[2,192,608]{2,1,0:T(8,128)(2,1)S(1)} collective-permute-done((bf16[2,192,608]{2,1,0:T(8,128)(2,1)S(1)}, bf16[2,192,608]{2,1,0:T(8,128)(2,1)S(1)}, u32[]{:S(2)}, u32[]{:S(2)}) %collective-permute-start.8) | collective-permute-done | bytes 466976 | tf_op jit(solution)/shard_map/ppermute | solution.py:723
  172.9 9.7 %collective-permute-done.9 = bf16[280,1536]{1,0:T(8,128)(2,1)} collective-permute-done((bf16[280,1536]{1,0:T(8,128)(2,1)}, bf16[280,1536]{1,0:T(8,128)(2,1)}, u32[]{:S(2)}, u32[]{:S(2)}) %collective-permute-start.9) | collective-permute-done | bytes 860192 | tf_op jit(solution)/shard_map/ppermute | solution.py:723
  218.0 33.6 %collective-permute-done.13 = bf16[2,2,192,608]{3,2,0,1:T(8,128)(2,1)S(1)} collective-permute-done((bf16[2,2,192,608]{3,2,0,1:T(8,128)(2,1)S(1)}, bf16[2,2,192,608]{3,2,0,1:T(8,128)(2,1)S(1)}, u32[]{:S(2)}, u32[]{:S(2)}) %collective-permute-start.13) | collective-permute-done | bytes 933920 | tf_op jit(solution)/shard_map/ppermute | solution.py:723
  269.7 24.3 %middle.2 = (bf16[2048,512]{1,0:T(8,128)(2,1)S(1)}, bf16[2048,512]{1,0:T(8,128)(2,1)S(1)}, bf16[2048,512]{1,0:T(8,128)(2,1)}, bf16[1024,1536]{1,0:T(8,128)(2,1)}, bf16[1024,1536]{1,0:T(8,128)(2,1)}) custom-call(s32[8]{0:T(128)S(1)} %stack.280.order, bf16[2048,1536]{1,0:T(8,128)(2,1)} %all-gather.10.cloned.1.call-done.h_ref, ...), custom_call_target="tpu_custom_call" | custom-call | flops 1000 | bytes 1000 | tf_op jit(solution)/shard_map/middle/pallas_call | solution.py:386
  294.0 11.9 %collective-permute-done.18 = bf16[2,2,2,192,608]{4,3,0,2,1:T(8,128)(2,1)} collective-permute-done((bf16[2,2,2,192,608]{4,3,0,2,1:T(8,128)(2,1)}, bf16[2,2,2,192,608]{4,3,0,2,1:T(8,128)(2,1)}, u32[]{:S(2)}, u32[]{:S(2)}) %collective-permute-start.18) | collective-permute-done | bytes 1867808 | tf_op jit(solution)/shard_map/ppermute | solution.py:723
  321.4 10.1 %two_grads.2 = bf16[2,1536,512]{2,1,0:T(8,128)(2,1)} custom-call(bf16[2048,1536]{1,0:T(8,128)(2,1)} %all-gather.10.cloned.1.call-done.h_ref, bf16[2048,512]{1,0:T(8,128)(2,1)S(1)} %copy-done.21, bf16[2048,512]{1,0:T(8,128)(2,1)S(1)} %copy-done.22), custom_call_target="tpu_custom_call" | custom-call | flops 1000 | bytes 1000 | tf_op jit(solution)/shard_map/two_grads/pallas_call | solution.py:419
  337.1 39.0 %middle.3 = (bf16[2048,608]{1,0:T(8,128)(2,1)S(1)}, bf16[2048,608]{1,0:T(8,128)(2,1)}, bf16[2048,608]{1,0:T(8,128)(2,1)}, bf16[1024,1536]{1,0:T(8,128)(2,1)}, bf16[1024,1536]{1,0:T(8,128)(2,1)}) custom-call(s32[8]{0:T(128)S(1)} %stack.280.order, bf16[2048,1536]{1,0:T(8,128)(2,1)} %all-gather.10.cloned.1.call-done.h_ref, ...), custom_call_target="tpu_custom_call" | custom-call | flops 1000 | bytes 1000 | tf_op jit(solution)/shard_map/middle/pallas_call | solution.py:386
  401.7 13.5 %two_grads.3 = bf16[2,1536,608]{2,1,0:T(8,128)(2,1)} custom-call(bf16[2048,1536]{1,0:T(8,128)(2,1)} %all-gather.10.cloned.1.call-done.h_ref, bf16[2048,608]{1,0:T(8,128)(2,1)S(1)} %copy-done.18, bf16[2048,608]{1,0:T(8,128)(2,1)S(1)} %copy-done.19), custom_call_target="tpu_custom_call" | custom-call | flops 1000 | bytes 1000 | tf_op jit(solution)/shard_map/two_grads/pallas_call | solution.py:419
  432.6 12.7 %down.1 = (bf16[1024,1536]{1,0:T(8,128)(2,1)}, bf16[1024,1536]{1,0:T(8,128)(2,1)}) custom-call(bf16[2048,512]{1,0:T(8,128)(2,1)S(1)} %copy-done.6, bf16[2048,608]{1,0:T(8,128)(2,1)} %copy-done.1, bf16[512,1536]{1,0:T(8,128)(2,1)S(1)} %bitcast.341, bf16[608,1536]{1,0:T(8,128)(2,1)S(1)} %bitcast.339), custom_call_target="tpu_custom_call" | custom-call | flops 1000 | bytes 1000 | tf_op jit(solution)/shard_map/down/pallas_call | solution.py:468
  455.3 8.0 %attend_back.1 = (bf16[256,1536]{1,0:T(8,128)(2,1)S(1)}, bf16[8,2,128,512]{3,2,1,0:T(8,128)(2,1)}) custom-call(s32[3]{0:T(128)S(1)} %copy-done.37, bf16[256,1536]{1,0:T(8,128)(2,1)S(1)} %copy-done.13, bf16[8,2,128,512]{3,2,1,0:T(8,128)(2,1)} %all-gather.8.cloned.1.call-done.k_ref.v_ref, bf16[8,2,128,512]{3,2,1,0:T(8,128)(2,1)} %all-gather.8.cloned.1.call-done.k_ref.v_ref, ...), custom_call_target="tpu_custom_call" | custom-call | flops 1000 | bytes 1000 | tf_op jit(solution)/shard_map/attend_back/pallas_call | solution.py:315
  489.6 8.0 %collective-permute-done.28 = bf16[152,1536]{1,0:T(8,128)(2,1)S(1)} collective-permute-done((bf16[152,1536]{1,0:T(8,128)(2,1)S(1)}, bf16[152,1536]{1,0:T(8,128)(2,1)S(1)}, u32[]{:S(2)}, u32[]{:S(2)}) %collective-permute-start.28) | collective-permute-done | bytes 466976 | tf_op jit(solution)/shard_map/ppermute | solution.py:723
  510.9 13.5 %reduce-scatter.5.cloned.1.call-done.dkv_ref = bf16[256,512]{1,0:T(8,128)(2,1)} async-done(((bf16[2048,512]{1,0:T(8,128)(2,1)}), bf16[256,512]{1,0:T(8,128)(2,1)}) %reduce-scatter.5.cloned.1.call-update) | async-done | bytes 262160 | tf_op jit(solution)/shard_map/reduce_scatter | solution.py:1137
  541.6 16.8 %collective-permute-start.33 = (bf16[2,2,208,128]{3,2,0,1:T(8,128)(2,1)S(1)}, bf16[2,2,208,128]{3,2,0,1:T(8,128)(2,1)S(1)}, u32[]{:S(2)}, u32[]{:S(2)}) collective-permute-start(bf16[2,2,208,128]{3,2,0,1:T(8,128)(2,1)S(1)} %bitcast.380), channel_id=1, source_target_pairs={{0,1},{1,0},{2,3},{3,2},{4,5},{5,4},{6,7},{7,6},{8,9},{9,8},{10,11... | collective-permute-start | bytes 638984 | tf_op jit(solution)/shard_map/ppermute | solution.py:723
  581.2 8.8 %collective-permute-done.37 = bf16[208,128]{1,0:T(8,128)(2,1)S(1)} collective-permute-done((bf16[208,128]{1,0:T(8,128)(2,1)S(1)}, bf16[208,128]{1,0:T(8,128)(2,1)S(1)}, u32[]{:S(2)}, u32[]{:S(2)}) %collective-permute-start.37) | collective-permute-done | bytes 53280 | tf_op jit(solution)/shard_map/ppermute | solution.py:723
  594.6 12.3 %collective-permute-done.43 = bf16[192,768]{1,0:T(8,128)(2,1)S(1)} collective-permute-done((bf16[192,768]{1,0:T(8,128)(2,1)S(1)}, bf16[192,768]{1,0:T(8,128)(2,1)S(1)}, u32[]{:S(2)}, u32[]{:S(2)}) %collective-permute-start.43) | collective-permute-done | bytes 294944 | tf_op jit(solution)/shard_map/ppermute | solution.py:723
  623.3 8.1 %collective-permute-done.50 = bf16[2,192,608]{2,1,0:T(8,128)(2,1)S(1)} collective-permute-done((bf16[2,192,608]{2,1,0:T(8,128)(2,1)S(1)}, bf16[2,192,608]{2,1,0:T(8,128)(2,1)S(1)}, u32[]{:S(2)}, u32[]{:S(2)}) %collective-permute-start.50) | collective-permute-done | bytes 466976 | tf_op jit(solution)/shard_map/ppermute | solution.py:723
  659.3 17.0 %multiply_subtract_fusion = (f32[1120,1536]{1,0:T(8,128)}, f32[1120,1536]{1,0:T(8,128)}, f32[1120,1536]{1,0:T(8,128)}) fusion(f32[1120,1536]{1,0:T(8,128)} %param.30, bf16[1120,1536]{1,0:T(8,128)(2,1)} %all-gather.12.cloned.1.call-done, f32[]{:T(128)} %min.3, f32[1120,1536]{1,0:T(8,128)} %param.36, f32[1120,1536]{1,0:T(8,128)} %param.42), kind=kLoop, calls=%fused_computation.2 | loop fusion | flops 29245440 | bytes 44728324 | tf_op jit(solution)/shard_map/sub | solution.py:67
  690.6 18.0 %adam_columns.2 = (f32[192,8960]{1,0:T(8,128)}, f32[192,8960]{1,0:T(8,128)}, f32[192,8960]{1,0:T(8,128)}) custom-call(s32[2]{0:T(128)S(1)} %pad_add_fusion.1.ids, f32[1]{0:T(128)} %bitcast.121.factor_ref, bf16[2,2,2,192,512]{4,3,2,1,0:T(8,128)(2,1)S(1)} %pad_maximum_fusion.11.first_ref, ...), custom_call_target="tpu_custom_call" | custom-call | flops 1000 | bytes 1000 | tf_op jit(solution)/shard_map/adam_columns/pallas_call | solution.py:159
  708.6 18.0 %adam_columns.3 = (f32[192,8960]{1,0:T(8,128)}, f32[192,8960]{1,0:T(8,128)}, f32[192,8960]{1,0:T(8,128)}) custom-call(s32[2]{0:T(128)S(1)} %pad_add_fusion.1.ids, f32[1]{0:T(128)} %bitcast.121.factor_ref, bf16[2,2,2,192,512]{4,3,2,1,0:T(8,128)(2,1)S(1)} %pad_maximum_fusion.11.first_ref, ...), custom_call_target="tpu_custom_call" | custom-call | flops 1000 | bytes 1000 | tf_op jit(solution)/shard_map/adam_columns/pallas_call | solution.py:159
  (597 shorter events, 327.8 us)
Async XLA Ops:
  11.4 106.8 %all-gather.16.cloned.1.call-start = ((), (), s32[]{:S(2)}) async-start(), calls=%async_computation.8 | async-start | bytes 1327104 | tf_op jit(solution)/shard_map/all_gather | solution.py:836
  55.3 127.3 %all-gather.8.cloned.1.call-start = ((), (), s32[]{:S(2)}) async-start(), calls=%async_computation.2 | async-start | bytes 2359296 | tf_op jit(solution)/shard_map/all_gather | solution.py:836
  67.0 46.2 %collective-permute-start.6 = (bf16[2,2,192,512]{3,2,0,1:T(8,128)(2,1)S(1)}, bf16[2,2,192,512]{3,2,0,1:T(8,128)(2,1)S(1)}, u32[]{:S(2)}, u32[]{:S(2)}) collective-permute-start(bf16[2,2,192,512]{3,2,0,1:T(8,128)(2,1)S(1)} %pad_maximum_fusion.17), channel_id=1, source_target_pairs={{0,4},{1,5},{2,6},{3,7},{4,0},{5,1},{6,2},{7,3},{8,12},{9,13},{10,... | collective-permute-start | bytes 2359304 | tf_op jit(solution)/shard_map/ppermute | solution.py:723
  114.6 155.1 %all-gather.10.cloned.1.call-start = ((), (), s32[]{:S(2)}) async-start(), calls=%async_computation.3 | async-start | bytes 7077888 | tf_op jit(solution)/shard_map/all_gather | solution.py:1029
  116.7 65.9 %collective-permute-start.10 = (bf16[2,2,2,192,512]{4,3,0,2,1:T(8,128)(2,1)}, bf16[2,2,2,192,512]{4,3,0,2,1:T(8,128)(2,1)}, u32[]{:S(2)}, u32[]{:S(2)}) collective-permute-start(bf16[2,2,2,192,512]{4,3,0,2,1:T(8,128)(2,1)} %pad_maximum_fusion.9), channel_id=1, source_target_pairs={{0,1},{1,0},{2,3},{3,2},{4,5},{5,4},{6,7},{7,6},{8,9},{9,8},{10,11... | collective-permute-start | bytes 4718600 | tf_op jit(solution)/shard_map/ppermute | solution.py:723
  125.8 56.7 %collective-permute-start.11 = (bf16[1536,384]{1,0:T(8,128)(2,1)S(1)}, bf16[1536,384]{1,0:T(8,128)(2,1)}, u32[]{:S(2)}, u32[]{:S(2)}) collective-permute-start(bf16[1536,384]{1,0:T(8,128)(2,1)S(1)} %bitcast_dynamic-update-slice_fusion), channel_id=1, source_target_pairs={{0,16},{16,0},{8,24},{24,8},{1,17},{17,1},{9,25},{25,9},{2,18},{18... | collective-permute-start | bytes 3538952 | tf_op jit(solution)/shard_map/ppermute | solution.py:714
  129.7 52.8 %collective-permute-start.9 = (bf16[280,1536]{1,0:T(8,128)(2,1)}, bf16[280,1536]{1,0:T(8,128)(2,1)}, u32[]{:S(2)}, u32[]{:S(2)}) collective-permute-start(bf16[280,1536]{1,0:T(8,128)(2,1)} %dynamic-slice_convert_fusion), channel_id=1, source_target_pairs={{0,4},{1,5},{2,6},{3,7},{4,0},{5,1},{6,2},{7,3},{8,12},{9,13},{10,... | collective-permute-start | bytes 2580488 | tf_op jit(solution)/shard_map/ppermute | solution.py:723
  200.2 178.2 %reduce-scatter.3.cloned.1.call-start = ((), (), s32[]{:S(2)}) async-start(), calls=%async_computation.4 | async-start | bytes 1966080 | tf_op jit(solution)/shard_map/reduce_scatter | solution.py:1036
  203.5 48.1 %collective-permute-start.14 = (bf16[2,280,1536]{2,1,0:T(8,128)(2,1)S(1)}, bf16[2,280,1536]{2,1,0:T(8,128)(2,1)}, u32[]{:S(2)}, u32[]{:S(2)}) collective-permute-start(bf16[2,280,1536]{2,1,0:T(8,128)(2,1)S(1)} %pad_maximum_fusion.7), channel_id=1, source_target_pairs={{0,1},{1,0},{2,3},{3,2},{4,5},{5,4},{6,7},{7,6},{8,9},{9,8},{10,11... | collective-permute-start | bytes 5160968 | tf_op jit(solution)/shard_map/ppermute | solution.py:723
  204.5 47.0 %collective-permute-start.13 = (bf16[2,2,192,608]{3,2,0,1:T(8,128)(2,1)S(1)}, bf16[2,2,192,608]{3,2,0,1:T(8,128)(2,1)S(1)}, u32[]{:S(2)}, u32[]{:S(2)}) collective-permute-start(bf16[2,2,192,608]{3,2,0,1:T(8,128)(2,1)S(1)} %pad_maximum_fusion.12), channel_id=1, source_target_pairs={{0,4},{1,5},{2,6},{3,7},{4,0},{5,1},{6,2},{7,3},{8,12},{9,13},{10,... | collective-permute-start | bytes 2801672 | tf_op jit(solution)/shard_map/ppermute | solution.py:723
  317.7 206.7 %reduce-scatter.5.cloned.1.call-start = ((), (), s32[]{:S(2)}) async-start(), calls=%async_computation.5 | async-start | bytes 2359296 | tf_op jit(solution)/shard_map/reduce_scatter | solution.py:1137
  400.3 63.1 %collective-permute-start.27 = (bf16[2,152,1536]{2,1,0:T(8,128)(2,1)}, bf16[2,152,1536]{2,1,0:T(8,128)(2,1)}, u32[]{:S(2)}, u32[]{:S(2)}) collective-permute-start(bf16[2,152,1536]{2,1,0:T(8,128)(2,1)} %get-tuple-element.307), channel_id=1, source_target_pairs={{0,1},{1,0},{2,3},{3,2},{4,5},{5,4},{6,7},{7,6},{8,9},{9,8},{10,11... | collective-permute-start | bytes 2801672 | tf_op jit(solution)/shard_map/ppermute | solution.py:723
  425.6 47.2 %collective-permute-start.44 = (bf16[2,2,192,512]{3,2,1,0:T(8,128)(2,1)}, bf16[2,2,192,512]{3,2,1,0:T(8,128)(2,1)}, u32[]{:S(2)}, u32[]{:S(2)}) collective-permute-start(bf16[2,2,192,512]{3,2,1,0:T(8,128)(2,1)} %get-tuple-element.311), channel_id=1, source_target_pairs={{0,4},{1,5},{2,6},{3,7},{4,0},{5,1},{6,2},{7,3},{8,12},{9,13},{10,... | collective-permute-start | bytes 2359304 | tf_op jit(solution)/shard_map/ppermute | solution.py:723
  431.5 67.2 %collective-permute-start.45 = (bf16[2,2,2,192,608]{4,3,2,1,0:T(8,128)(2,1)}, bf16[2,2,2,192,608]{4,3,2,1,0:T(8,128)(2,1)}, u32[]{:S(2)}, u32[]{:S(2)}) collective-permute-start(bf16[2,2,2,192,608]{4,3,2,1,0:T(8,128)(2,1)} %get-tuple-element.279), channel_id=1, source_target_pairs={{0,1},{1,0},{2,3},{3,2},{4,5},{5,4},{6,7},{7,6},{8,9},{9,8},{10,11... | collective-permute-start | bytes 5603336 | tf_op jit(solution)/shard_map/ppermute | solution.py:723
  445.3 119.2 %collective-permute-start.24 = (bf16[1024,1536]{1,0:T(8,128)(2,1)}, bf16[1024,1536]{1,0:T(8,128)(2,1)}, u32[]{:S(2)}, u32[]{:S(2)}) collective-permute-start(bf16[1024,1536]{1,0:T(8,128)(2,1)} %get-tuple-element.183), channel_id=1, source_target_pairs={{0,8},{8,0},{16,24},{24,16},{1,9},{9,1},{17,25},{25,17},{2,10},{10... | collective-permute-start | bytes 9437192 | tf_op jit(solution)/shard_map/ppermute | solution.py:710
  463.4 195.9 %all-gather.12.cloned.1.call-start = ((), (), s32[]{:S(2)}) async-start(), calls=%async_computation.6 | async-start | bytes 4300800 | tf_op jit(solution)/shard_map/all_gather | solution.py:1191
  482.6 46.9 %collective-permute-start.54 = (bf16[2,192,512]{2,1,0:T(8,128)(2,1)}, bf16[2,192,512]{2,1,0:T(8,128)(2,1)}, u32[]{:S(2)}, u32[]{:S(2)}) collective-permute-start(bf16[2,192,512]{2,1,0:T(8,128)(2,1)} %get-tuple-element.339), channel_id=1, source_target_pairs={{0,2},{1,3},{2,0},{3,1},{4,6},{5,7},{6,4},{7,5},{8,10},{9,11},{10,... | collective-permute-start | bytes 1179656 | tf_op jit(solution)/shard_map/ppermute | solution.py:723
  502.4 75.6 %collective-permute-start.46 = (bf16[2,2,192,608]{3,2,1,0:T(8,128)(2,1)}, bf16[2,2,192,608]{3,2,1,0:T(8,128)(2,1)}, u32[]{:S(2)}, u32[]{:S(2)}) collective-permute-start(bf16[2,2,192,608]{3,2,1,0:T(8,128)(2,1)} %get-tuple-element.303), channel_id=1, source_target_pairs={{0,4},{1,5},{2,6},{3,7},{4,0},{5,1},{6,2},{7,3},{8,12},{9,13},{10,... | collective-permute-start | bytes 2801672 | tf_op jit(solution)/shard_map/ppermute | solution.py:723
  510.6 62.8 %collective-permute-start.41 = (bf16[2,2,192,768]{3,2,1,0:T(8,128)(2,1)}, bf16[2,2,192,768]{3,2,1,0:T(8,128)(2,1)}, u32[]{:S(2)}, u32[]{:S(2)}) collective-permute-start(bf16[2,2,192,768]{3,2,1,0:T(8,128)(2,1)} %get-tuple-element.301), channel_id=1, source_target_pairs={{0,1},{1,0},{2,3},{3,2},{4,5},{5,4},{6,7},{7,6},{8,9},{9,8},{10,11... | collective-permute-start | bytes 3538952 | tf_op jit(solution)/shard_map/ppermute | solution.py:723
  564.3 47.3 %collective-permute-start.47 = (bf16[512,1536]{1,0:T(8,128)(2,1)}, bf16[512,1536]{1,0:T(8,128)(2,1)}, u32[]{:S(2)}, u32[]{:S(2)}) collective-permute-start(bf16[512,1536]{1,0:T(8,128)(2,1)} %get-tuple-element.219), channel_id=1, source_target_pairs={{0,8},{8,0},{16,24},{24,16},{1,9},{9,1},{17,25},{25,17},{2,10},{10... | collective-permute-start | bytes 4718600 | tf_op jit(solution)/shard_map/ppermute | solution.py:710
  594.5 53.7 %collective-permute-start.56 = (bf16[2,2,2,192,512]{4,3,2,1,0:T(8,128)(2,1)S(1)}, bf16[2,2,2,192,512]{4,3,2,1,0:T(8,128)(2,1)S(1)}, u32[]{:S(2)}, u32[]{:S(2)}) collective-permute-start(bf16[2,2,2,192,512]{4,3,2,1,0:T(8,128)(2,1)S(1)} %pad_maximum_fusion.11.first_ref), channel_id=1, source_target_pairs={{0,8},{8,0},{16,24},{24,16},{1,9},{9,1},{17,25},{25,17},{2,10},{10... | collective-permute-start | bytes 4718600 | tf_op jit(solution)/shard_map/ppermute | solution.py:710
  645.4 81.3 %collective-permute-start.61 = (bf16[256,1536]{1,0:T(8,128)(2,1)}, bf16[256,1536]{1,0:T(8,128)(2,1)}, u32[]{:S(2)}, u32[]{:S(2)}) collective-permute-start(bf16[256,1536]{1,0:T(8,128)(2,1)} %get-tuple-element.274), channel_id=1, source_target_pairs={{0,16},{16,0},{8,24},{24,8},{1,17},{17,1},{9,25},{25,9},{2,18},{18... | collective-permute-start | bytes 2359304 | tf_op jit(solution)/shard_map/ppermute | solution.py:714
  650.9 75.8 %collective-permute-start.57 = (bf16[256,1536]{1,0:T(8,128)(2,1)}, bf16[256,1536]{1,0:T(8,128)(2,1)}, u32[]{:S(2)}, u32[]{:S(2)}) collective-permute-start(bf16[256,1536]{1,0:T(8,128)(2,1)} %pad_maximum_fusion.23), channel_id=1, source_target_pairs={{0,16},{16,0},{8,24},{24,8},{1,17},{17,1},{9,25},{25,9},{2,18},{18... | collective-permute-start | bytes 2359304 | tf_op jit(solution)/shard_map/ppermute | solution.py:714
  652.1 74.5 %collective-permute-start.58 = (bf16[256,1536]{1,0:T(8,128)(2,1)}, bf16[256,1536]{1,0:T(8,128)(2,1)}, u32[]{:S(2)}, u32[]{:S(2)}) collective-permute-start(bf16[256,1536]{1,0:T(8,128)(2,1)} %pad_maximum_fusion.24), channel_id=1, source_target_pairs={{0,2},{1,3},{2,0},{3,1},{4,6},{5,7},{6,4},{7,5},{8,10},{9,11},{10,... | collective-permute-start | bytes 2359304 | tf_op jit(solution)/shard_map/ppermute | solution.py:723
  (179 other events, 2021.2 us)
Sparse Core Ops, SparseCore 0:
  11.5 39.8 all-gather.13
  55.4 54.4 all-gather.15
  114.7 61.3 all-gather.7
  200.4 69.2 all-gather.9
  317.8 44.3 reduce-scatter.2
  463.5 60.8 reduce-scatter.4
  529.7 54.8 all-gather.11

commit v16 on v15

--- a/solution.py
+++ b/solution.py
@@ -149,7 +149,7 @@
 
 def adam_columns(which, ids, factor, first, second, w, m, v, blk_count, rate, decay):
     rows = w.shape[0]
-    step = 32 if rows % 32 == 0 else rows
+    step = 96 if rows % 96 == 0 else rows
     spec = pl.BlockSpec((step, FF), lambda i, ids: (i, 0))
     shape = jax.ShapeDtypeStruct((rows, FF), jnp.float32)
     grads = [
@@ -1165,7 +1165,7 @@
     bias_q = jnp.sum(wide(d_query), axis=0)
     d_key = own_part
     cross_part = swap_cross(far_part)
-    near_a = gather_near_stacked(columns_last(*after(third_a, own_part)))
+    own_a = columns_last(*after(third_a, own_part))
     core_part = swap_core(jnp.stack([core_part, cross_part[1]]))
     kv_grad, hone_here, hone_there = make_kv_grad(
         blk_count,
@@ -1194,6 +1194,7 @@
         kv_sum = part_sum(*steps_kv)
         steps_kv = part_sent(kv_sum, i, bits[i])
         marks.append(kv_sum)
+    near_a = gather_near_stacked(after(own_a, marks[-1]))
     for n, i in enumerate(range(len(bits) - 2, -1, -1)):
         steps_query = part_sent(part_sum(*after(steps_query, marks[n + 1])), i, bits[i])
     sum_b, third_b = columns_third(*after(second_b, marks[-1]))

time: 751 us -> 753 us (level)
  waiting for transfers between devices: 245 us -> 278 us
  starting transfers between devices: 90.4 us -> 69.1 us
    ppermute x31, starting transfers between devices: 67.7 us -> 42.4 us  [swap_blk(): return lax.ppermute(values, 'blk', [(i, i ^ bit) for i in range(count)])]
    ppermute x18, waiting for transfers between devices: 27.8 us -> 47.9 us  [swap_cross(): return lax.ppermute(values, 'grp', CROSS)]
    reduce_scatter x1, waiting for transfers between devices: 13.5 us -> 26.6 us  [on_device(): lax.psum_scatter(dkv.reshape(blk_count * token_count, 2 * KVD), ('grp', '...]
    unnamed x286 -> x292, local copies, waits for them, and re-layouts: 38 us -> 36.6 us
  transfers between devices with their start and end apart: 71 -> 71, of which waited for: 26 -> 29; matrix products, arithmetic and copies ran while one was open for 20% -> 20% of each run, Pallas kernels for 24% -> 23%
where the time goes in v16:
time: 753 us; the launch traced here: 745 us
  waiting for transfers between devices  278 us (37%)
  Pallas kernels  182 us (24%)
  other arithmetic  112 us (15%)
  local copies, waits for them, and re-layouts  76 us (10%)
  starting transfers between devices  69.1 us (9%)
  between operations  21.4 us (3%)
    ppermute x31, waiting for transfers between devices, swap_blk(): return lax.ppermute(values, 'blk', [(i, i ^ bit) for i in range(count)])  201 us
    pallas_call x2, Pallas kernels, middle(): pl.pallas_call(functools.partial(middle_body, prev is not None), grid_spe...  63.3 us
    ppermute x18, waiting for transfers between devices, swap_cross(): return lax.ppermute(values, 'grp', CROSS)  47.9 us
    ppermute x31, starting transfers between devices, swap_blk(): return lax.ppermute(values, 'blk', [(i, i ^ bit) for i in range(count)])  42.4 us
    unnamed x292, local copies, waits for them, and re-layouts  36.6 us
    pallas_call x2, Pallas kernels, adam_columns(): pl.pallas_call(functools.partial(adam_body, blk_count, rate, decay), grid...  32.1 us
    reduce_scatter x1, waiting for transfers between devices, on_device(): lax.psum_scatter(dkv.reshape(blk_count * token_count, 2 * KVD), ('grp', '...  26.6 us
    convert_element_type x18, other arithmetic, low(): return values.astype(jnp.bfloat16)  25.3 us
  transfers between devices with their start and end apart: 71, of which 29 were waited for; matrix products, arithmetic and copies ran while one was open for 20% of the time, Pallas kernels for 23%

profile of v16, /device:TPU:0, one launch (start us, length us, event | category | flops | bytes accessed | tf_op | source)
XLA Modules:
  0.0 745.2 jit_solution(2902804681528061033)
XLA Ops:
  25.1 17.3 %collective-permute-done.1 = bf16[2,192,512]{2,1,0:T(8,128)(2,1)S(1)} collective-permute-done((bf16[2,192,512]{2,1,0:T(8,128)(2,1)S(1)}, bf16[2,192,512]{2,1,0:T(8,128)(2,1)S(1)}, u32[]{:S(2)}, u32[]{:S(2)}) %collective-permute-start.1) | collective-permute-done | bytes 393248 | tf_op jit(solution)/shard_map/ppermute | solution.py:723
  42.4 8.8 %collective-permute-done.2 = bf16[256,1536]{1,0:T(8,128)(2,1)S(1)} collective-permute-done((bf16[256,1536]{1,0:T(8,128)(2,1)S(1)}, bf16[256,1536]{1,0:T(8,128)(2,1)S(1)}, u32[]{:S(2)}, u32[]{:S(2)}) %collective-permute-start.2) | collective-permute-done | bytes 786464 | tf_op jit(solution)/shard_map/ppermute | solution.py:714
  69.7 9.4 %collective-permute-done.4.cross_ref = bf16[2,256,512]{2,1,0:T(8,128)(2,1)S(1)} collective-permute-done((bf16[2,256,512]{2,1,0:T(8,128)(2,1)S(1)}, bf16[2,256,512]{2,1,0:T(8,128)(2,1)S(1)}, u32[]{:S(2)}, u32[]{:S(2)}) %collective-permute-start.4) | collective-permute-done | bytes 524320 | tf_op jit(solution)/shard_map/ppermute | solution.py:714
  79.2 17.0 %collective-permute-done.7 = bf16[256,1536]{1,0:T(8,128)(2,1)S(1)} collective-permute-done((bf16[256,1536]{1,0:T(8,128)(2,1)}, bf16[256,1536]{1,0:T(8,128)(2,1)S(1)}, u32[]{:S(2)}, u32[]{:S(2)}) %collective-permute-start.7) | collective-permute-done | bytes 786464 | tf_op jit(solution)/shard_map/ppermute | solution.py:723
  96.2 17.0 %collective-permute-done.6 = bf16[2,2,192,512]{3,2,0,1:T(8,128)(2,1)S(1)} collective-permute-done((bf16[2,2,192,512]{3,2,0,1:T(8,128)(2,1)S(1)}, bf16[2,2,192,512]{3,2,0,1:T(8,128)(2,1)S(1)}, u32[]{:S(2)}, u32[]{:S(2)}) %collective-permute-start.6) | collective-permute-done | bytes 786464 | tf_op jit(solution)/shard_map/ppermute | solution.py:723
  133.0 40.1 %collective-permute-done.8 = bf16[2,192,608]{2,1,0:T(8,128)(2,1)S(1)} collective-permute-done((bf16[2,192,608]{2,1,0:T(8,128)(2,1)S(1)}, bf16[2,192,608]{2,1,0:T(8,128)(2,1)S(1)}, u32[]{:S(2)}, u32[]{:S(2)}) %collective-permute-start.8) | collective-permute-done | bytes 466976 | tf_op jit(solution)/shard_map/ppermute | solution.py:723
  173.1 9.7 %collective-permute-done.9 = bf16[280,1536]{1,0:T(8,128)(2,1)} collective-permute-done((bf16[280,1536]{1,0:T(8,128)(2,1)}, bf16[280,1536]{1,0:T(8,128)(2,1)}, u32[]{:S(2)}, u32[]{:S(2)}) %collective-permute-start.9) | collective-permute-done | bytes 860192 | tf_op jit(solution)/shard_map/ppermute | solution.py:723
  216.5 35.2 %collective-permute-done.13 = bf16[2,2,192,608]{3,2,0,1:T(8,128)(2,1)S(1)} collective-permute-done((bf16[2,2,192,608]{3,2,0,1:T(8,128)(2,1)S(1)}, bf16[2,2,192,608]{3,2,0,1:T(8,128)(2,1)S(1)}, u32[]{:S(2)}, u32[]{:S(2)}) %collective-permute-start.13) | collective-permute-done | bytes 933920 | tf_op jit(solution)/shard_map/ppermute | solution.py:723
  269.6 24.3 %middle.2 = (bf16[2048,512]{1,0:T(8,128)(2,1)S(1)}, bf16[2048,512]{1,0:T(8,128)(2,1)S(1)}, bf16[2048,512]{1,0:T(8,128)(2,1)}, bf16[1024,1536]{1,0:T(8,128)(2,1)}, bf16[1024,1536]{1,0:T(8,128)(2,1)}) custom-call(s32[8]{0:T(128)S(1)} %stack.280.order, bf16[2048,1536]{1,0:T(8,128)(2,1)} %all-gather.10.cloned.1.call-done.h_ref, ...), custom_call_target="tpu_custom_call" | custom-call | flops 1000 | bytes 1000 | tf_op jit(solution)/shard_map/middle/pallas_call | solution.py:386
  293.9 12.3 %collective-permute-done.18 = bf16[2,2,2,192,608]{4,3,0,2,1:T(8,128)(2,1)} collective-permute-done((bf16[2,2,2,192,608]{4,3,0,2,1:T(8,128)(2,1)}, bf16[2,2,2,192,608]{4,3,0,2,1:T(8,128)(2,1)}, u32[]{:S(2)}, u32[]{:S(2)}) %collective-permute-start.18) | collective-permute-done | bytes 1867808 | tf_op jit(solution)/shard_map/ppermute | solution.py:723
  321.4 10.1 %two_grads.2 = bf16[2,1536,512]{2,1,0:T(8,128)(2,1)} custom-call(bf16[2048,1536]{1,0:T(8,128)(2,1)} %all-gather.10.cloned.1.call-done.h_ref, bf16[2048,512]{1,0:T(8,128)(2,1)S(1)} %copy-done.21, bf16[2048,512]{1,0:T(8,128)(2,1)S(1)} %copy-done.22), custom_call_target="tpu_custom_call" | custom-call | flops 1000 | bytes 1000 | tf_op jit(solution)/shard_map/two_grads/pallas_call | solution.py:419
  336.6 39.0 %middle.3 = (bf16[2048,608]{1,0:T(8,128)(2,1)S(1)}, bf16[2048,608]{1,0:T(8,128)(2,1)}, bf16[2048,608]{1,0:T(8,128)(2,1)}, bf16[1024,1536]{1,0:T(8,128)(2,1)}, bf16[1024,1536]{1,0:T(8,128)(2,1)}) custom-call(s32[8]{0:T(128)S(1)} %stack.280.order, bf16[2048,1536]{1,0:T(8,128)(2,1)} %all-gather.10.cloned.1.call-done.h_ref, ...), custom_call_target="tpu_custom_call" | custom-call | flops 1000 | bytes 1000 | tf_op jit(solution)/shard_map/middle/pallas_call | solution.py:386
  402.4 13.5 %two_grads.3 = bf16[2,1536,608]{2,1,0:T(8,128)(2,1)} custom-call(bf16[2048,1536]{1,0:T(8,128)(2,1)} %all-gather.10.cloned.1.call-done.h_ref, bf16[2048,608]{1,0:T(8,128)(2,1)S(1)} %copy-done.18, bf16[2048,608]{1,0:T(8,128)(2,1)S(1)} %copy-done.19), custom_call_target="tpu_custom_call" | custom-call | flops 1000 | bytes 1000 | tf_op jit(solution)/shard_map/two_grads/pallas_call | solution.py:419
  431.9 12.9 %down.1 = (bf16[1024,1536]{1,0:T(8,128)(2,1)}, bf16[1024,1536]{1,0:T(8,128)(2,1)}) custom-call(bf16[2048,512]{1,0:T(8,128)(2,1)S(1)} %copy-done.6, bf16[2048,608]{1,0:T(8,128)(2,1)} %copy-done.1, bf16[512,1536]{1,0:T(8,128)(2,1)S(1)} %bitcast.340, bf16[608,1536]{1,0:T(8,128)(2,1)S(1)} %bitcast.338), custom_call_target="tpu_custom_call" | custom-call | flops 1000 | bytes 1000 | tf_op jit(solution)/shard_map/down/pallas_call | solution.py:468
  455.9 8.0 %attend_back.1 = (bf16[256,1536]{1,0:T(8,128)(2,1)S(1)}, bf16[8,2,128,512]{3,2,1,0:T(8,128)(2,1)}) custom-call(s32[3]{0:T(128)S(1)} %copy-done.37, bf16[256,1536]{1,0:T(8,128)(2,1)S(1)} %copy-done.13, bf16[8,2,128,512]{3,2,1,0:T(8,128)(2,1)} %all-gather.8.cloned.1.call-done.k_ref.v_ref, bf16[8,2,128,512]{3,2,1,0:T(8,128)(2,1)} %all-gather.8.cloned.1.call-done.k_ref.v_ref, ...), custom_call_target="tpu_custom_call" | custom-call | flops 1000 | bytes 1000 | tf_op jit(solution)/shard_map/attend_back/pallas_call | solution.py:315
  488.9 9.9 %collective-permute-done.28 = bf16[152,1536]{1,0:T(8,128)(2,1)S(1)} collective-permute-done((bf16[152,1536]{1,0:T(8,128)(2,1)S(1)}, bf16[152,1536]{1,0:T(8,128)(2,1)S(1)}, u32[]{:S(2)}, u32[]{:S(2)}) %collective-permute-start.28) | collective-permute-done | bytes 466976 | tf_op jit(solution)/shard_map/ppermute | solution.py:723
  513.5 26.6 %reduce-scatter.5.cloned.1.call-done.dkv_ref = bf16[256,512]{1,0:T(8,128)(2,1)} async-done(((bf16[2048,512]{1,0:T(8,128)(2,1)}), bf16[256,512]{1,0:T(8,128)(2,1)}) %reduce-scatter.5.cloned.1.call-update) | async-done | bytes 262160 | tf_op jit(solution)/shard_map/reduce_scatter | solution.py:1137
  549.5 8.4 %kv_grad.1 = (bf16[8,208,128]{2,1,0:T(8,128)(2,1)S(1)}, bf16[512,1536]{1,0:T(8,128)(2,1)S(1)}, bf16[512,1536]{1,0:T(8,128)(2,1)}) custom-call(bf16[256,128]{1,0:T(8,128)(2,1)S(1)} %get-tuple-element.195.self_ref, bf16[2,256,128]{2,1,0:T(8,128)(2,1)S(1)} %collective-permute-done.29.cross_ref, bf16[2,256,128]{2,1,0:T(8,128)(2,1)S(1)} %collective-permute-done.30.core_ref, ...), custom_call_target="tpu_custom_call" | custom-call | flops 1000 | bytes 1000 | tf_op jit(solution)/shard_map/kv_grad/pallas_call | solution.py:681
  579.3 10.6 %collective-permute-done.42 = bf16[2,192,768]{2,1,0:T(8,128)(2,1)S(1)} collective-permute-done((bf16[2,192,768]{2,1,0:T(8,128)(2,1)S(1)}, bf16[2,192,768]{2,1,0:T(8,128)(2,1)S(1)}, u32[]{:S(2)}, u32[]{:S(2)}) %collective-permute-start.42) | collective-permute-done | bytes 589856 | tf_op jit(solution)/shard_map/ppermute | solution.py:723
  590.9 13.8 %collective-permute-done.43 = bf16[192,768]{1,0:T(8,128)(2,1)S(1)} collective-permute-done((bf16[192,768]{1,0:T(8,128)(2,1)S(1)}, bf16[192,768]{1,0:T(8,128)(2,1)S(1)}, u32[]{:S(2)}, u32[]{:S(2)}) %collective-permute-start.43) | collective-permute-done | bytes 294944 | tf_op jit(solution)/shard_map/ppermute | solution.py:723
  640.5 13.6 %collective-permute-done.55 = bf16[2,2,192,512]{3,2,1,0:T(8,128)(2,1)S(1)} collective-permute-done((bf16[2,2,192,512]{3,2,1,0:T(8,128)(2,1)S(1)}, bf16[2,2,192,512]{3,2,1,0:T(8,128)(2,1)S(1)}, u32[]{:S(2)}, u32[]{:S(2)}) %collective-permute-start.55) | collective-permute-done | bytes 786464 | tf_op jit(solution)/shard_map/ppermute | solution.py:714
  668.8 17.0 %multiply_subtract_fusion = (f32[1120,1536]{1,0:T(8,128)}, f32[1120,1536]{1,0:T(8,128)}, f32[1120,1536]{1,0:T(8,128)}) fusion(f32[1120,1536]{1,0:T(8,128)} %param.30, bf16[1120,1536]{1,0:T(8,128)(2,1)} %all-gather.12.cloned.1.call-done, f32[]{:T(128)} %min.3, f32[1120,1536]{1,0:T(8,128)} %param.36, f32[1120,1536]{1,0:T(8,128)} %param.42), kind=kLoop, calls=%fused_computation.2 | loop fusion | flops 29245440 | bytes 44728324 | tf_op jit(solution)/shard_map/sub | solution.py:67
  697.4 15.9 %adam_columns.2 = (f32[192,8960]{1,0:T(8,128)}, f32[192,8960]{1,0:T(8,128)}, f32[192,8960]{1,0:T(8,128)}) custom-call(s32[2]{0:T(128)S(1)} %pad_add_fusion.1.ids, f32[1]{0:T(128)} %bitcast.121.factor_ref, bf16[2,2,2,192,512]{4,3,2,1,0:T(8,128)(2,1)S(1)} %pad_maximum_fusion.11.first_ref, ...), custom_call_target="tpu_custom_call" | custom-call | flops 1000 | bytes 1000 | tf_op jit(solution)/shard_map/adam_columns/pallas_call | solution.py:159
  713.4 16.2 %adam_columns.3 = (f32[192,8960]{1,0:T(8,128)}, f32[192,8960]{1,0:T(8,128)}, f32[192,8960]{1,0:T(8,128)}) custom-call(s32[2]{0:T(128)S(1)} %pad_add_fusion.1.ids, f32[1]{0:T(128)} %bitcast.121.factor_ref, bf16[2,2,2,192,512]{4,3,2,1,0:T(8,128)(2,1)S(1)} %pad_maximum_fusion.11.first_ref, ...), custom_call_target="tpu_custom_call" | custom-call | flops 1000 | bytes 1000 | tf_op jit(solution)/shard_map/adam_columns/pallas_call | solution.py:159
  (603 shorter events, 317.2 us)
Async XLA Ops:
  11.4 107.1 %all-gather.16.cloned.1.call-start = ((), (), s32[]{:S(2)}) async-start(), calls=%async_computation.8 | async-start | bytes 1327104 | tf_op jit(solution)/shard_map/all_gather | solution.py:836
  55.3 127.5 %all-gather.8.cloned.1.call-start = ((), (), s32[]{:S(2)}) async-start(), calls=%async_computation.2 | async-start | bytes 2359296 | tf_op jit(solution)/shard_map/all_gather | solution.py:836
  67.0 46.2 %collective-permute-start.6 = (bf16[2,2,192,512]{3,2,0,1:T(8,128)(2,1)S(1)}, bf16[2,2,192,512]{3,2,0,1:T(8,128)(2,1)S(1)}, u32[]{:S(2)}, u32[]{:S(2)}) collective-permute-start(bf16[2,2,192,512]{3,2,0,1:T(8,128)(2,1)S(1)} %pad_maximum_fusion.17), channel_id=1, source_target_pairs={{0,4},{1,5},{2,6},{3,7},{4,0},{5,1},{6,2},{7,3},{8,12},{9,13},{10,... | collective-permute-start | bytes 2359304 | tf_op jit(solution)/shard_map/ppermute | solution.py:723
  114.6 154.9 %all-gather.10.cloned.1.call-start = ((), (), s32[]{:S(2)}) async-start(), calls=%async_computation.3 | async-start | bytes 7077888 | tf_op jit(solution)/shard_map/all_gather | solution.py:1029
  117.0 65.8 %collective-permute-start.10 = (bf16[2,2,2,192,512]{4,3,0,2,1:T(8,128)(2,1)}, bf16[2,2,2,192,512]{4,3,0,2,1:T(8,128)(2,1)}, u32[]{:S(2)}, u32[]{:S(2)}) collective-permute-start(bf16[2,2,2,192,512]{4,3,0,2,1:T(8,128)(2,1)} %pad_maximum_fusion.9), channel_id=1, source_target_pairs={{0,1},{1,0},{2,3},{3,2},{4,5},{5,4},{6,7},{7,6},{8,9},{9,8},{10,11... | collective-permute-start | bytes 4718600 | tf_op jit(solution)/shard_map/ppermute | solution.py:723
  126.1 56.6 %collective-permute-start.11 = (bf16[1536,384]{1,0:T(8,128)(2,1)S(1)}, bf16[1536,384]{1,0:T(8,128)(2,1)}, u32[]{:S(2)}, u32[]{:S(2)}) collective-permute-start(bf16[1536,384]{1,0:T(8,128)(2,1)S(1)} %bitcast_dynamic-update-slice_fusion), channel_id=1, source_target_pairs={{0,16},{16,0},{8,24},{24,8},{1,17},{17,1},{9,25},{25,9},{2,18},{18... | collective-permute-start | bytes 3538952 | tf_op jit(solution)/shard_map/ppermute | solution.py:714
  130.0 52.7 %collective-permute-start.9 = (bf16[280,1536]{1,0:T(8,128)(2,1)}, bf16[280,1536]{1,0:T(8,128)(2,1)}, u32[]{:S(2)}, u32[]{:S(2)}) collective-permute-start(bf16[280,1536]{1,0:T(8,128)(2,1)} %dynamic-slice_convert_fusion), channel_id=1, source_target_pairs={{0,4},{1,5},{2,6},{3,7},{4,0},{5,1},{6,2},{7,3},{8,12},{9,13},{10,... | collective-permute-start | bytes 2580488 | tf_op jit(solution)/shard_map/ppermute | solution.py:723
  200.5 177.6 %reduce-scatter.3.cloned.1.call-start = ((), (), s32[]{:S(2)}) async-start(), calls=%async_computation.4 | async-start | bytes 1966080 | tf_op jit(solution)/shard_map/reduce_scatter | solution.py:1036
  202.9 48.8 %collective-permute-start.14 = (bf16[2,280,1536]{2,1,0:T(8,128)(2,1)S(1)}, bf16[2,280,1536]{2,1,0:T(8,128)(2,1)}, u32[]{:S(2)}, u32[]{:S(2)}) collective-permute-start(bf16[2,280,1536]{2,1,0:T(8,128)(2,1)S(1)} %pad_maximum_fusion.7), channel_id=1, source_target_pairs={{0,1},{1,0},{2,3},{3,2},{4,5},{5,4},{6,7},{7,6},{8,9},{9,8},{10,11... | collective-permute-start | bytes 5160968 | tf_op jit(solution)/shard_map/ppermute | solution.py:723
  204.7 47.0 %collective-permute-start.13 = (bf16[2,2,192,608]{3,2,0,1:T(8,128)(2,1)S(1)}, bf16[2,2,192,608]{3,2,0,1:T(8,128)(2,1)S(1)}, u32[]{:S(2)}, u32[]{:S(2)}) collective-permute-start(bf16[2,2,192,608]{3,2,0,1:T(8,128)(2,1)S(1)} %pad_maximum_fusion.12), channel_id=1, source_target_pairs={{0,4},{1,5},{2,6},{3,7},{4,0},{5,1},{6,2},{7,3},{8,12},{9,13},{10,... | collective-permute-start | bytes 2801672 | tf_op jit(solution)/shard_map/ppermute | solution.py:723
  260.8 45.4 %collective-permute-start.18 = (bf16[2,2,2,192,608]{4,3,0,2,1:T(8,128)(2,1)}, bf16[2,2,2,192,608]{4,3,0,2,1:T(8,128)(2,1)}, u32[]{:S(2)}, u32[]{:S(2)}) collective-permute-start(bf16[2,2,2,192,608]{4,3,0,2,1:T(8,128)(2,1)} %pad_maximum_fusion.5), channel_id=1, source_target_pairs={{0,1},{1,0},{2,3},{3,2},{4,5},{5,4},{6,7},{7,6},{8,9},{9,8},{10,11... | collective-permute-start | bytes 5603336 | tf_op jit(solution)/shard_map/ppermute | solution.py:723
  318.0 222.1 %reduce-scatter.5.cloned.1.call-start = ((), (), s32[]{:S(2)}) async-start(), calls=%async_computation.5 | async-start | bytes 2359296 | tf_op jit(solution)/shard_map/reduce_scatter | solution.py:1137
  400.8 63.2 %collective-permute-start.27 = (bf16[2,152,1536]{2,1,0:T(8,128)(2,1)}, bf16[2,152,1536]{2,1,0:T(8,128)(2,1)}, u32[]{:S(2)}, u32[]{:S(2)}) collective-permute-start(bf16[2,152,1536]{2,1,0:T(8,128)(2,1)} %get-tuple-element.309), channel_id=1, source_target_pairs={{0,1},{1,0},{2,3},{3,2},{4,5},{5,4},{6,7},{7,6},{8,9},{9,8},{10,11... | collective-permute-start | bytes 2801672 | tf_op jit(solution)/shard_map/ppermute | solution.py:723
  425.8 47.4 %collective-permute-start.44 = (bf16[2,2,192,512]{3,2,1,0:T(8,128)(2,1)}, bf16[2,2,192,512]{3,2,1,0:T(8,128)(2,1)}, u32[]{:S(2)}, u32[]{:S(2)}) collective-permute-start(bf16[2,2,192,512]{3,2,1,0:T(8,128)(2,1)} %get-tuple-element.313), channel_id=1, source_target_pairs={{0,4},{1,5},{2,6},{3,7},{4,0},{5,1},{6,2},{7,3},{8,12},{9,13},{10,... | collective-permute-start | bytes 2359304 | tf_op jit(solution)/shard_map/ppermute | solution.py:723
  430.9 69.1 %collective-permute-start.45 = (bf16[2,2,2,192,608]{4,3,2,1,0:T(8,128)(2,1)}, bf16[2,2,2,192,608]{4,3,2,1,0:T(8,128)(2,1)}, u32[]{:S(2)}, u32[]{:S(2)}) collective-permute-start(bf16[2,2,2,192,608]{4,3,2,1,0:T(8,128)(2,1)} %get-tuple-element.281), channel_id=1, source_target_pairs={{0,1},{1,0},{2,3},{3,2},{4,5},{5,4},{6,7},{7,6},{8,9},{9,8},{10,11... | collective-permute-start | bytes 5603336 | tf_op jit(solution)/shard_map/ppermute | solution.py:723
  444.9 120.9 %collective-permute-start.24 = (bf16[1024,1536]{1,0:T(8,128)(2,1)}, bf16[1024,1536]{1,0:T(8,128)(2,1)}, u32[]{:S(2)}, u32[]{:S(2)}) collective-permute-start(bf16[1024,1536]{1,0:T(8,128)(2,1)} %get-tuple-element.184), channel_id=1, source_target_pairs={{0,8},{8,0},{16,24},{24,16},{1,9},{9,1},{17,25},{25,17},{2,10},{10... | collective-permute-start | bytes 9437192 | tf_op jit(solution)/shard_map/ppermute | solution.py:710
  464.0 204.8 %all-gather.12.cloned.1.call-start = ((), (), s32[]{:S(2)}) async-start(), calls=%async_computation.6 | async-start | bytes 4300800 | tf_op jit(solution)/shard_map/all_gather | solution.py:1191
  483.6 61.8 %collective-permute-start.54 = (bf16[2,192,512]{2,1,0:T(8,128)(2,1)}, bf16[2,192,512]{2,1,0:T(8,128)(2,1)}, u32[]{:S(2)}, u32[]{:S(2)}) collective-permute-start(bf16[2,192,512]{2,1,0:T(8,128)(2,1)} %get-tuple-element.339), channel_id=1, source_target_pairs={{0,2},{1,3},{2,0},{3,1},{4,6},{5,7},{6,4},{7,5},{8,10},{9,11},{10,... | collective-permute-start | bytes 1179656 | tf_op jit(solution)/shard_map/ppermute | solution.py:723
  503.6 72.5 %collective-permute-start.46 = (bf16[2,2,192,608]{3,2,1,0:T(8,128)(2,1)}, bf16[2,2,192,608]{3,2,1,0:T(8,128)(2,1)}, u32[]{:S(2)}, u32[]{:S(2)}) collective-permute-start(bf16[2,2,192,608]{3,2,1,0:T(8,128)(2,1)} %get-tuple-element.305), channel_id=1, source_target_pairs={{0,4},{1,5},{2,6},{3,7},{4,0},{5,1},{6,2},{7,3},{8,12},{9,13},{10,... | collective-permute-start | bytes 2801672 | tf_op jit(solution)/shard_map/ppermute | solution.py:723
  511.8 60.6 %collective-permute-start.41 = (bf16[2,2,192,768]{3,2,1,0:T(8,128)(2,1)}, bf16[2,2,192,768]{3,2,1,0:T(8,128)(2,1)}, u32[]{:S(2)}, u32[]{:S(2)}) collective-permute-start(bf16[2,2,192,768]{3,2,1,0:T(8,128)(2,1)} %get-tuple-element.303), channel_id=1, source_target_pairs={{0,1},{1,0},{2,3},{3,2},{4,5},{5,4},{6,7},{7,6},{8,9},{9,8},{10,11... | collective-permute-start | bytes 3538952 | tf_op jit(solution)/shard_map/ppermute | solution.py:723
  560.6 48.7 %collective-permute-start.47 = (bf16[512,1536]{1,0:T(8,128)(2,1)}, bf16[512,1536]{1,0:T(8,128)(2,1)}, u32[]{:S(2)}, u32[]{:S(2)}) collective-permute-start(bf16[512,1536]{1,0:T(8,128)(2,1)} %get-tuple-element.220), channel_id=1, source_target_pairs={{0,8},{8,0},{16,24},{24,16},{1,9},{9,1},{17,25},{25,17},{2,10},{10... | collective-permute-start | bytes 4718600 | tf_op jit(solution)/shard_map/ppermute | solution.py:710
  638.7 47.1 %collective-permute-start.59 = (bf16[2,2,192,608]{3,2,1,0:T(8,128)(2,1)}, bf16[2,2,192,608]{3,2,1,0:T(8,128)(2,1)}, u32[]{:S(2)}, u32[]{:S(2)}) collective-permute-start(bf16[2,2,192,608]{3,2,1,0:T(8,128)(2,1)} %get-tuple-element.332), channel_id=1, source_target_pairs={{0,16},{16,0},{8,24},{24,8},{1,17},{17,1},{9,25},{25,9},{2,18},{18... | collective-permute-start | bytes 2801672 | tf_op jit(solution)/shard_map/ppermute | solution.py:714
  659.0 70.5 %collective-permute-start.61 = (bf16[256,1536]{1,0:T(8,128)(2,1)}, bf16[256,1536]{1,0:T(8,128)(2,1)}, u32[]{:S(2)}, u32[]{:S(2)}) collective-permute-start(bf16[256,1536]{1,0:T(8,128)(2,1)} %get-tuple-element.276), channel_id=1, source_target_pairs={{0,16},{16,0},{8,24},{24,8},{1,17},{17,1},{9,25},{25,9},{2,18},{18... | collective-permute-start | bytes 2359304 | tf_op jit(solution)/shard_map/ppermute | solution.py:714
  668.5 61.0 %collective-permute-start.57 = (bf16[256,1536]{1,0:T(8,128)(2,1)}, bf16[256,1536]{1,0:T(8,128)(2,1)}, u32[]{:S(2)}, u32[]{:S(2)}) collective-permute-start(bf16[256,1536]{1,0:T(8,128)(2,1)} %pad_maximum_fusion.23), channel_id=1, source_target_pairs={{0,16},{16,0},{8,24},{24,8},{1,17},{17,1},{9,25},{25,9},{2,18},{18... | collective-permute-start | bytes 2359304 | tf_op jit(solution)/shard_map/ppermute | solution.py:714
  (182 other events, 2089.2 us)
Sparse Core Ops, SparseCore 0:
  11.5 39.8 all-gather.13
  55.4 54.4 all-gather.15
  114.7 61.4 all-gather.7
  200.6 68.9 all-gather.9
  318.1 43.7 reduce-scatter.2
  464.1 75.9 reduce-scatter.4
  545.5 29.0 all-gather.11

commit v17 on v16

--- a/solution.py
+++ b/solution.py
@@ -1194,7 +1194,7 @@
         kv_sum = part_sum(*steps_kv)
         steps_kv = part_sent(kv_sum, i, bits[i])
         marks.append(kv_sum)
-    near_a = gather_near_stacked(after(own_a, marks[-1]))
+    cross_a = swap_cross(after(own_a, marks[-1]))
     for n, i in enumerate(range(len(bits) - 2, -1, -1)):
         steps_query = part_sent(part_sum(*after(steps_query, marks[n + 1])), i, bits[i])
     sum_b, third_b = columns_third(*after(second_b, marks[-1]))
@@ -1217,12 +1217,8 @@
     packed = after(packed, (d_hone_send, d_hone))
     packed = packed + swap_cross(packed)
     packed = packed + swap_core(packed)
-    parts = gather_grp(after(jnp.concatenate([share_query_out, share_kv], axis=1), packed))
-    grad_out = jnp.concatenate([part[:, strip_q : 2 * strip_q] for part in parts], axis=1)
-    grad_attend = jnp.concatenate(
-        [part[:, :strip_q] for part in parts] + [parts[k][:, 2 * strip_q :] for k in (0, 2, 1, 3)],
-        axis=1,
-    )
+    share_rest = after(jnp.concatenate([share_query_out, share_kv], axis=1), packed)
+    cross_rest = swap_cross(share_rest)
     share_vector = packed[:vector_rows].reshape(-1)[:small_count]
     square_sum = packed[vector_rows:] + jnp.sum(share_vector * share_vector)
     square_sum = after(square_sum, third_b[1])
@@ -1232,17 +1228,27 @@
     factor = jnp.minimum(1.0, CLIP_NORM / (grad_norm + 1e-06))
     out_chip = chip_sum(out_part, after(out_came, marks[1]))
     out_far = scatter_far(out_chip)
-    factor = after(factor, (out_chip, near_a))
-
+    factor = after(factor, out_chip)
+
+    new_first_down, new_second_down, new_down = adam_step(
+        w_down, factor * wide(grad_down), first_down, second_down, RATE_DOWN, WEIGHT_DECAY
+    )
+    cross_rest = after(cross_rest, new_down)
+    core_rest = swap_core(jnp.stack([share_rest, cross_rest]))
+    parts = by_place([share_rest, core_rest[0], cross_rest, core_rest[1]])
+    grad_out = jnp.concatenate([part[:, strip_q : 2 * strip_q] for part in parts], axis=1)
+    grad_attend = jnp.concatenate(
+        [part[:, :strip_q] for part in parts] + [parts[k][:, 2 * strip_q :] for k in (0, 2, 1, 3)],
+        axis=1,
+    )
     new_first_attend, new_second_attend, new_attend = adam_step(
         w_attend, factor * wide(grad_attend), first_attend, second_attend, RATE_ATTEND, WEIGHT_DECAY
     )
     new_first_out, new_second_out, new_out = adam_step(
         w_out, factor * wide(grad_out), first_out, second_out, RATE_OUT, WEIGHT_DECAY
     )
-    new_first_down, new_second_down, new_down = adam_step(
-        w_down, factor * wide(grad_down), first_down, second_down, RATE_DOWN, WEIGHT_DECAY
-    )
+    near_a = jnp.stack([own_a, after(cross_a, new_down)])
+    near_a = [near_a, swap_core(near_a)]
     own_b = columns_last(*third_b)
     cross_b = after(swap_cross(own_b), new_down)
     near_b = jnp.stack([own_b, cross_b])

time: 753 us -> 768 us (1.020)
  waiting for transfers between devices: 278 us -> 291 us
    ppermute x18, waiting for transfers between devices: 47.9 us -> 56 us  [swap_cross(): return lax.ppermute(values, 'grp', CROSS)]
    unnamed x292 -> x278, local copies, waits for them, and re-layouts: 36.6 us -> 37 us
  transfers between devices with their start and end apart: 71 -> 71, of which waited for: 29 -> 28; matrix products, arithmetic and copies ran while one was open for 20% -> 19% of each run, Pallas kernels for 23% -> 23%
where the time goes in v17:
time: 768 us; the launch traced here: 760 us
  waiting for transfers between devices  291 us (38%)
  Pallas kernels  182 us (24%)
  other arithmetic  114 us (15%)
  local copies, waits for them, and re-layouts  73.7 us (10%)
  starting transfers between devices  71.8 us (9%)
  between operations  21.3 us (3%)
    ppermute x31, waiting for transfers between devices, swap_blk(): return lax.ppermute(values, 'blk', [(i, i ^ bit) for i in range(count)])  205 us
    pallas_call x2, Pallas kernels, middle(): pl.pallas_call(functools.partial(middle_body, prev is not None), grid_spe...  63.3 us
    ppermute x18, waiting for transfers between devices, swap_cross(): return lax.ppermute(values, 'grp', CROSS)  56 us
    ppermute x31, starting transfers between devices, swap_blk(): return lax.ppermute(values, 'blk', [(i, i ^ bit) for i in range(count)])  46.5 us
    unnamed x278, local copies, waits for them, and re-layouts  37 us
    pallas_call x2, Pallas kernels, adam_columns(): pl.pallas_call(functools.partial(adam_body, blk_count, rate, decay), grid...  32.1 us
    reduce_scatter x1, waiting for transfers between devices, on_device(): lax.psum_scatter(dkv.reshape(blk_count * token_count, 2 * KVD), ('grp', '...  27.7 us
    convert_element_type x18, other arithmetic, low(): return values.astype(jnp.bfloat16)  25.6 us
  transfers between devices with their start and end apart: 71, of which 28 were waited for; matrix products, arithmetic and copies ran while one was open for 19% of the time, Pallas kernels for 23%

profile of v17, /device:TPU:0, one launch (start us, length us, event | category | flops | bytes accessed | tf_op | source)
XLA Modules:
  0.0 760.4 jit_solution(12874859911102260259)
XLA Ops:
  25.1 17.3 %collective-permute-done.1 = bf16[2,192,512]{2,1,0:T(8,128)(2,1)S(1)} collective-permute-done((bf16[2,192,512]{2,1,0:T(8,128)(2,1)S(1)}, bf16[2,192,512]{2,1,0:T(8,128)(2,1)S(1)}, u32[]{:S(2)}, u32[]{:S(2)}) %collective-permute-start.1) | collective-permute-done | bytes 393248 | tf_op jit(solution)/shard_map/ppermute | solution.py:723
  42.4 8.8 %collective-permute-done.2 = bf16[256,1536]{1,0:T(8,128)(2,1)S(1)} collective-permute-done((bf16[256,1536]{1,0:T(8,128)(2,1)S(1)}, bf16[256,1536]{1,0:T(8,128)(2,1)S(1)}, u32[]{:S(2)}, u32[]{:S(2)}) %collective-permute-start.2) | collective-permute-done | bytes 786464 | tf_op jit(solution)/shard_map/ppermute | solution.py:714
  69.7 9.4 %collective-permute-done.4.cross_ref = bf16[2,256,512]{2,1,0:T(8,128)(2,1)S(1)} collective-permute-done((bf16[2,256,512]{2,1,0:T(8,128)(2,1)S(1)}, bf16[2,256,512]{2,1,0:T(8,128)(2,1)S(1)}, u32[]{:S(2)}, u32[]{:S(2)}) %collective-permute-start.4) | collective-permute-done | bytes 524320 | tf_op jit(solution)/shard_map/ppermute | solution.py:714
  79.2 17.0 %collective-permute-done.7 = bf16[256,1536]{1,0:T(8,128)(2,1)S(1)} collective-permute-done((bf16[256,1536]{1,0:T(8,128)(2,1)}, bf16[256,1536]{1,0:T(8,128)(2,1)S(1)}, u32[]{:S(2)}, u32[]{:S(2)}) %collective-permute-start.7) | collective-permute-done | bytes 786464 | tf_op jit(solution)/shard_map/ppermute | solution.py:723
  96.2 17.0 %collective-permute-done.6 = bf16[2,2,192,512]{3,2,0,1:T(8,128)(2,1)S(1)} collective-permute-done((bf16[2,2,192,512]{3,2,0,1:T(8,128)(2,1)S(1)}, bf16[2,2,192,512]{3,2,0,1:T(8,128)(2,1)S(1)}, u32[]{:S(2)}, u32[]{:S(2)}) %collective-permute-start.6) | collective-permute-done | bytes 786464 | tf_op jit(solution)/shard_map/ppermute | solution.py:723
  133.0 40.1 %collective-permute-done.8 = bf16[2,192,608]{2,1,0:T(8,128)(2,1)S(1)} collective-permute-done((bf16[2,192,608]{2,1,0:T(8,128)(2,1)S(1)}, bf16[2,192,608]{2,1,0:T(8,128)(2,1)S(1)}, u32[]{:S(2)}, u32[]{:S(2)}) %collective-permute-start.8) | collective-permute-done | bytes 466976 | tf_op jit(solution)/shard_map/ppermute | solution.py:723
  173.1 9.7 %collective-permute-done.9 = bf16[280,1536]{1,0:T(8,128)(2,1)} collective-permute-done((bf16[280,1536]{1,0:T(8,128)(2,1)}, bf16[280,1536]{1,0:T(8,128)(2,1)}, u32[]{:S(2)}, u32[]{:S(2)}) %collective-permute-start.9) | collective-permute-done | bytes 860192 | tf_op jit(solution)/shard_map/ppermute | solution.py:723
  216.5 35.2 %collective-permute-done.13 = bf16[2,2,192,608]{3,2,0,1:T(8,128)(2,1)S(1)} collective-permute-done((bf16[2,2,192,608]{3,2,0,1:T(8,128)(2,1)S(1)}, bf16[2,2,192,608]{3,2,0,1:T(8,128)(2,1)S(1)}, u32[]{:S(2)}, u32[]{:S(2)}) %collective-permute-start.13) | collective-permute-done | bytes 933920 | tf_op jit(solution)/shard_map/ppermute | solution.py:723
  270.7 24.3 %middle.2 = (bf16[2048,512]{1,0:T(8,128)(2,1)S(1)}, bf16[2048,512]{1,0:T(8,128)(2,1)S(1)}, bf16[2048,512]{1,0:T(8,128)(2,1)}, bf16[1024,1536]{1,0:T(8,128)(2,1)}, bf16[1024,1536]{1,0:T(8,128)(2,1)}) custom-call(s32[8]{0:T(128)S(1)} %stack.280.order, bf16[2048,1536]{1,0:T(8,128)(2,1)} %all-gather.10.cloned.1.call-done.h_ref, ...), custom_call_target="tpu_custom_call" | custom-call | flops 1000 | bytes 1000 | tf_op jit(solution)/shard_map/middle/pallas_call | solution.py:386
  295.0 11.1 %collective-permute-done.18 = bf16[2,2,2,192,608]{4,3,0,2,1:T(8,128)(2,1)} collective-permute-done((bf16[2,2,2,192,608]{4,3,0,2,1:T(8,128)(2,1)}, bf16[2,2,2,192,608]{4,3,0,2,1:T(8,128)(2,1)}, u32[]{:S(2)}, u32[]{:S(2)}) %collective-permute-start.18) | collective-permute-done | bytes 1867808 | tf_op jit(solution)/shard_map/ppermute | solution.py:723
  321.3 10.2 %two_grads.2 = bf16[2,1536,512]{2,1,0:T(8,128)(2,1)} custom-call(bf16[2048,1536]{1,0:T(8,128)(2,1)} %all-gather.10.cloned.1.call-done.h_ref, bf16[2048,512]{1,0:T(8,128)(2,1)S(1)} %copy-done.21, bf16[2048,512]{1,0:T(8,128)(2,1)S(1)} %copy-done.22), custom_call_target="tpu_custom_call" | custom-call | flops 1000 | bytes 1000 | tf_op jit(solution)/shard_map/two_grads/pallas_call | solution.py:419
  336.2 39.0 %middle.3 = (bf16[2048,608]{1,0:T(8,128)(2,1)S(1)}, bf16[2048,608]{1,0:T(8,128)(2,1)}, bf16[2048,608]{1,0:T(8,128)(2,1)}, bf16[1024,1536]{1,0:T(8,128)(2,1)}, bf16[1024,1536]{1,0:T(8,128)(2,1)}) custom-call(s32[8]{0:T(128)S(1)} %stack.280.order, bf16[2048,1536]{1,0:T(8,128)(2,1)} %all-gather.10.cloned.1.call-done.h_ref, ...), custom_call_target="tpu_custom_call" | custom-call | flops 1000 | bytes 1000 | tf_op jit(solution)/shard_map/middle/pallas_call | solution.py:386
  401.8 13.5 %two_grads.3 = bf16[2,1536,608]{2,1,0:T(8,128)(2,1)} custom-call(bf16[2048,1536]{1,0:T(8,128)(2,1)} %all-gather.10.cloned.1.call-done.h_ref, bf16[2048,608]{1,0:T(8,128)(2,1)S(1)} %copy-done.18, bf16[2048,608]{1,0:T(8,128)(2,1)S(1)} %copy-done.19), custom_call_target="tpu_custom_call" | custom-call | flops 1000 | bytes 1000 | tf_op jit(solution)/shard_map/two_grads/pallas_call | solution.py:419
  432.4 12.9 %down.1 = (bf16[1024,1536]{1,0:T(8,128)(2,1)}, bf16[1024,1536]{1,0:T(8,128)(2,1)}) custom-call(bf16[2048,512]{1,0:T(8,128)(2,1)S(1)} %copy-done.6, bf16[2048,608]{1,0:T(8,128)(2,1)} %copy-done.1, bf16[512,1536]{1,0:T(8,128)(2,1)S(1)} %bitcast.341, bf16[608,1536]{1,0:T(8,128)(2,1)S(1)} %bitcast.339), custom_call_target="tpu_custom_call" | custom-call | flops 1000 | bytes 1000 | tf_op jit(solution)/shard_map/down/pallas_call | solution.py:468
  455.5 8.0 %attend_back.1 = (bf16[256,1536]{1,0:T(8,128)(2,1)S(1)}, bf16[8,2,128,512]{3,2,1,0:T(8,128)(2,1)}) custom-call(s32[3]{0:T(128)S(1)} %copy-done.37, bf16[256,1536]{1,0:T(8,128)(2,1)S(1)} %copy-done.13, bf16[8,2,128,512]{3,2,1,0:T(8,128)(2,1)} %all-gather.8.cloned.1.call-done.k_ref.v_ref, bf16[8,2,128,512]{3,2,1,0:T(8,128)(2,1)} %all-gather.8.cloned.1.call-done.k_ref.v_ref, ...), custom_call_target="tpu_custom_call" | custom-call | flops 1000 | bytes 1000 | tf_op jit(solution)/shard_map/attend_back/pallas_call | solution.py:315
  489.6 7.7 %collective-permute-done.28 = bf16[152,1536]{1,0:T(8,128)(2,1)S(1)} collective-permute-done((bf16[152,1536]{1,0:T(8,128)(2,1)S(1)}, bf16[152,1536]{1,0:T(8,128)(2,1)S(1)}, u32[]{:S(2)}, u32[]{:S(2)}) %collective-permute-start.28) | collective-permute-done | bytes 466976 | tf_op jit(solution)/shard_map/ppermute | solution.py:723
  512.7 27.7 %reduce-scatter.5.cloned.1.call-done.dkv_ref = bf16[256,512]{1,0:T(8,128)(2,1)} async-done(((bf16[2048,512]{1,0:T(8,128)(2,1)}), bf16[256,512]{1,0:T(8,128)(2,1)}) %reduce-scatter.5.cloned.1.call-update) | async-done | bytes 262160 | tf_op jit(solution)/shard_map/reduce_scatter | solution.py:1137
  550.0 8.4 %kv_grad.1 = (bf16[8,208,128]{2,1,0:T(8,128)(2,1)S(1)}, bf16[512,1536]{1,0:T(8,128)(2,1)S(1)}, bf16[512,1536]{1,0:T(8,128)(2,1)}) custom-call(bf16[256,128]{1,0:T(8,128)(2,1)S(1)} %get-tuple-element.197.self_ref, bf16[2,256,128]{2,1,0:T(8,128)(2,1)S(1)} %collective-permute-done.29.cross_ref, bf16[2,256,128]{2,1,0:T(8,128)(2,1)S(1)} %collective-permute-done.30.core_ref, ...), custom_call_target="tpu_custom_call" | custom-call | flops 1000 | bytes 1000 | tf_op jit(solution)/shard_map/kv_grad/pallas_call | solution.py:681
  580.8 10.1 %collective-permute-done.42 = bf16[2,192,768]{2,1,0:T(8,128)(2,1)S(1)} collective-permute-done((bf16[2,192,768]{2,1,0:T(8,128)(2,1)S(1)}, bf16[2,192,768]{2,1,0:T(8,128)(2,1)S(1)}, u32[]{:S(2)}, u32[]{:S(2)}) %collective-permute-start.42) | collective-permute-done | bytes 589856 | tf_op jit(solution)/shard_map/ppermute | solution.py:723
  591.9 14.0 %collective-permute-done.43 = bf16[192,768]{1,0:T(8,128)(2,1)S(1)} collective-permute-done((bf16[192,768]{1,0:T(8,128)(2,1)S(1)}, bf16[192,768]{1,0:T(8,128)(2,1)S(1)}, u32[]{:S(2)}, u32[]{:S(2)}) %collective-permute-start.43) | collective-permute-done | bytes 294944 | tf_op jit(solution)/shard_map/ppermute | solution.py:723
  650.5 16.9 %multiply_subtract_fusion = (f32[1120,1536]{1,0:T(8,128)}, f32[1120,1536]{1,0:T(8,128)}, f32[1120,1536]{1,0:T(8,128)}) fusion(f32[1120,1536]{1,0:T(8,128)} %param.30, bf16[1120,1536]{1,0:T(8,128)(2,1)} %all-gather.12.cloned.1.call-done, f32[]{:T(128)} %min.3, f32[1120,1536]{1,0:T(8,128)} %param.36, f32[1120,1536]{1,0:T(8,128)} %param.42), kind=kLoop, calls=%fused_computation.2 | loop fusion | flops 29245440 | bytes 44728324 | tf_op jit(solution)/shard_map/sub | solution.py:67
  667.4 26.3 %collective-permute-done.62 = bf16[192,896]{1,0:T(8,128)(2,1)} collective-permute-done((bf16[192,896]{1,0:T(8,128)(2,1)S(1)}, bf16[192,896]{1,0:T(8,128)(2,1)}, u32[]{:S(2)}, u32[]{:S(2)}) %collective-permute-start.62) | collective-permute-done | bytes 344096 | tf_op jit(solution)/shard_map/ppermute | solution.py:714
  712.8 15.9 %adam_columns.2 = (f32[192,8960]{1,0:T(8,128)}, f32[192,8960]{1,0:T(8,128)}, f32[192,8960]{1,0:T(8,128)}) custom-call(s32[2]{0:T(128)S(1)} %pad_add_fusion.1.ids, f32[1]{0:T(128)} %bitcast.114.factor_ref, bf16[2,2,2,192,512]{4,3,2,1,0:T(8,128)(2,1)S(1)} %pad_maximum_fusion.11.first_ref, ...), custom_call_target="tpu_custom_call" | custom-call | flops 1000 | bytes 1000 | tf_op jit(solution)/shard_map/adam_columns/pallas_call | solution.py:159
  728.7 16.2 %adam_columns.3 = (f32[192,8960]{1,0:T(8,128)}, f32[192,8960]{1,0:T(8,128)}, f32[192,8960]{1,0:T(8,128)}) custom-call(s32[2]{0:T(128)S(1)} %pad_add_fusion.1.ids, f32[1]{0:T(128)} %bitcast.114.factor_ref, bf16[2,2,2,192,512]{4,3,2,1,0:T(8,128)(2,1)S(1)} %pad_maximum_fusion.11.first_ref, ...), custom_call_target="tpu_custom_call" | custom-call | flops 1000 | bytes 1000 | tf_op jit(solution)/shard_map/adam_columns/pallas_call | solution.py:159
  (589 shorter events, 322.4 us)
Async XLA Ops:
  11.4 107.1 %all-gather.16.cloned.1.call-start = ((), (), s32[]{:S(2)}) async-start(), calls=%async_computation.8 | async-start | bytes 1327104 | tf_op jit(solution)/shard_map/all_gather | solution.py:836
  55.3 127.5 %all-gather.8.cloned.1.call-start = ((), (), s32[]{:S(2)}) async-start(), calls=%async_computation.2 | async-start | bytes 2359296 | tf_op jit(solution)/shard_map/all_gather | solution.py:836
  114.6 156.1 %all-gather.10.cloned.1.call-start = ((), (), s32[]{:S(2)}) async-start(), calls=%async_computation.3 | async-start | bytes 7077888 | tf_op jit(solution)/shard_map/all_gather | solution.py:1029
  117.0 65.8 %collective-permute-start.10 = (bf16[2,2,2,192,512]{4,3,0,2,1:T(8,128)(2,1)}, bf16[2,2,2,192,512]{4,3,0,2,1:T(8,128)(2,1)}, u32[]{:S(2)}, u32[]{:S(2)}) collective-permute-start(bf16[2,2,2,192,512]{4,3,0,2,1:T(8,128)(2,1)} %pad_maximum_fusion.9), channel_id=1, source_target_pairs={{0,1},{1,0},{2,3},{3,2},{4,5},{5,4},{6,7},{7,6},{8,9},{9,8},{10,11... | collective-permute-start | bytes 4718600 | tf_op jit(solution)/shard_map/ppermute | solution.py:723
  126.1 56.6 %collective-permute-start.11 = (bf16[1536,384]{1,0:T(8,128)(2,1)S(1)}, bf16[1536,384]{1,0:T(8,128)(2,1)}, u32[]{:S(2)}, u32[]{:S(2)}) collective-permute-start(bf16[1536,384]{1,0:T(8,128)(2,1)S(1)} %bitcast_dynamic-update-slice_fusion), channel_id=1, source_target_pairs={{0,16},{16,0},{8,24},{24,8},{1,17},{17,1},{9,25},{25,9},{2,18},{18... | collective-permute-start | bytes 3538952 | tf_op jit(solution)/shard_map/ppermute | solution.py:714
  130.0 52.7 %collective-permute-start.9 = (bf16[280,1536]{1,0:T(8,128)(2,1)}, bf16[280,1536]{1,0:T(8,128)(2,1)}, u32[]{:S(2)}, u32[]{:S(2)}) collective-permute-start(bf16[280,1536]{1,0:T(8,128)(2,1)} %dynamic-slice_convert_fusion), channel_id=1, source_target_pairs={{0,4},{1,5},{2,6},{3,7},{4,0},{5,1},{6,2},{7,3},{8,12},{9,13},{10,... | collective-permute-start | bytes 2580488 | tf_op jit(solution)/shard_map/ppermute | solution.py:723
  200.5 177.9 %reduce-scatter.3.cloned.1.call-start = ((), (), s32[]{:S(2)}) async-start(), calls=%async_computation.4 | async-start | bytes 1966080 | tf_op jit(solution)/shard_map/reduce_scatter | solution.py:1036
  202.9 48.8 %collective-permute-start.14 = (bf16[2,280,1536]{2,1,0:T(8,128)(2,1)S(1)}, bf16[2,280,1536]{2,1,0:T(8,128)(2,1)}, u32[]{:S(2)}, u32[]{:S(2)}) collective-permute-start(bf16[2,280,1536]{2,1,0:T(8,128)(2,1)S(1)} %pad_maximum_fusion.7), channel_id=1, source_target_pairs={{0,1},{1,0},{2,3},{3,2},{4,5},{5,4},{6,7},{7,6},{8,9},{9,8},{10,11... | collective-permute-start | bytes 5160968 | tf_op jit(solution)/shard_map/ppermute | solution.py:723
  317.9 222.4 %reduce-scatter.5.cloned.1.call-start = ((), (), s32[]{:S(2)}) async-start(), calls=%async_computation.5 | async-start | bytes 2359296 | tf_op jit(solution)/shard_map/reduce_scatter | solution.py:1137
  400.0 63.6 %collective-permute-start.27 = (bf16[2,152,1536]{2,1,0:T(8,128)(2,1)}, bf16[2,152,1536]{2,1,0:T(8,128)(2,1)}, u32[]{:S(2)}, u32[]{:S(2)}) collective-permute-start(bf16[2,152,1536]{2,1,0:T(8,128)(2,1)} %get-tuple-element.313), channel_id=1, source_target_pairs={{0,1},{1,0},{2,3},{3,2},{4,5},{5,4},{6,7},{7,6},{8,9},{9,8},{10,11... | collective-permute-start | bytes 2801672 | tf_op jit(solution)/shard_map/ppermute | solution.py:723
  425.6 47.1 %collective-permute-start.44 = (bf16[2,2,192,512]{3,2,1,0:T(8,128)(2,1)}, bf16[2,2,192,512]{3,2,1,0:T(8,128)(2,1)}, u32[]{:S(2)}, u32[]{:S(2)}) collective-permute-start(bf16[2,2,192,512]{3,2,1,0:T(8,128)(2,1)} %get-tuple-element.317), channel_id=1, source_target_pairs={{0,4},{1,5},{2,6},{3,7},{4,0},{5,1},{6,2},{7,3},{8,12},{9,13},{10,... | collective-permute-start | bytes 2359304 | tf_op jit(solution)/shard_map/ppermute | solution.py:723
  431.3 67.1 %collective-permute-start.45 = (bf16[2,2,2,192,608]{4,3,2,1,0:T(8,128)(2,1)}, bf16[2,2,2,192,608]{4,3,2,1,0:T(8,128)(2,1)}, u32[]{:S(2)}, u32[]{:S(2)}) collective-permute-start(bf16[2,2,2,192,608]{4,3,2,1,0:T(8,128)(2,1)} %get-tuple-element.285), channel_id=1, source_target_pairs={{0,1},{1,0},{2,3},{3,2},{4,5},{5,4},{6,7},{7,6},{8,9},{9,8},{10,11... | collective-permute-start | bytes 5603336 | tf_op jit(solution)/shard_map/ppermute | solution.py:723
  445.4 120.9 %collective-permute-start.24 = (bf16[1024,1536]{1,0:T(8,128)(2,1)}, bf16[1024,1536]{1,0:T(8,128)(2,1)}, u32[]{:S(2)}, u32[]{:S(2)}) collective-permute-start(bf16[1024,1536]{1,0:T(8,128)(2,1)} %get-tuple-element.186), channel_id=1, source_target_pairs={{0,8},{8,0},{16,24},{24,16},{1,9},{9,1},{17,25},{25,17},{2,10},{10... | collective-permute-start | bytes 9437192 | tf_op jit(solution)/shard_map/ppermute | solution.py:710
  463.6 186.9 %all-gather.12.cloned.1.call-start = ((), (), s32[]{:S(2)}) async-start(), calls=%async_computation.6 | async-start | bytes 4300800 | tf_op jit(solution)/shard_map/all_gather | solution.py:1191
  483.8 62.2 %collective-permute-start.56 = (bf16[2,192,512]{2,1,0:T(8,128)(2,1)}, bf16[2,192,512]{2,1,0:T(8,128)(2,1)}, u32[]{:S(2)}, u32[]{:S(2)}) collective-permute-start(bf16[2,192,512]{2,1,0:T(8,128)(2,1)} %get-tuple-element.345), channel_id=1, source_target_pairs={{0,2},{1,3},{2,0},{3,1},{4,6},{5,7},{6,4},{7,5},{8,10},{9,11},{10,... | collective-permute-start | bytes 1179656 | tf_op jit(solution)/shard_map/ppermute | solution.py:723
  502.1 75.5 %collective-permute-start.46 = (bf16[2,2,192,608]{3,2,1,0:T(8,128)(2,1)}, bf16[2,2,192,608]{3,2,1,0:T(8,128)(2,1)}, u32[]{:S(2)}, u32[]{:S(2)}) collective-permute-start(bf16[2,2,192,608]{3,2,1,0:T(8,128)(2,1)} %get-tuple-element.309), channel_id=1, source_target_pairs={{0,4},{1,5},{2,6},{3,7},{4,0},{5,1},{6,2},{7,3},{8,12},{9,13},{10,... | collective-permute-start | bytes 2801672 | tf_op jit(solution)/shard_map/ppermute | solution.py:723
  510.3 62.9 %collective-permute-start.41 = (bf16[2,2,192,768]{3,2,1,0:T(8,128)(2,1)}, bf16[2,2,192,768]{3,2,1,0:T(8,128)(2,1)}, u32[]{:S(2)}, u32[]{:S(2)}) collective-permute-start(bf16[2,2,192,768]{3,2,1,0:T(8,128)(2,1)} %get-tuple-element.307), channel_id=1, source_target_pairs={{0,1},{1,0},{2,3},{3,2},{4,5},{5,4},{6,7},{7,6},{8,9},{9,8},{10,11... | collective-permute-start | bytes 3538952 | tf_op jit(solution)/shard_map/ppermute | solution.py:723
  561.4 49.2 %collective-permute-start.47 = (bf16[512,1536]{1,0:T(8,128)(2,1)}, bf16[512,1536]{1,0:T(8,128)(2,1)}, u32[]{:S(2)}, u32[]{:S(2)}) collective-permute-start(bf16[512,1536]{1,0:T(8,128)(2,1)} %get-tuple-element.222), channel_id=1, source_target_pairs={{0,8},{8,0},{16,24},{24,16},{1,9},{9,1},{17,25},{25,17},{2,10},{10... | collective-permute-start | bytes 4718600 | tf_op jit(solution)/shard_map/ppermute | solution.py:710
  620.8 75.6 %collective-permute-start.57 = (bf16[2,2,192,512]{3,2,1,0:T(8,128)(2,1)}, bf16[2,2,192,512]{3,2,1,0:T(8,128)(2,1)}, u32[]{:S(2)}, u32[]{:S(2)}) collective-permute-start(bf16[2,2,192,512]{3,2,1,0:T(8,128)(2,1)} %get-tuple-element.230), channel_id=1, source_target_pairs={{0,16},{16,0},{8,24},{24,8},{1,17},{17,1},{9,25},{25,9},{2,18},{18... | collective-permute-start | bytes 2359304 | tf_op jit(solution)/shard_map/ppermute | solution.py:714
  638.4 61.3 %collective-permute-start.59 = (bf16[2,2,192,608]{3,2,1,0:T(8,128)(2,1)}, bf16[2,2,192,608]{3,2,1,0:T(8,128)(2,1)}, u32[]{:S(2)}, u32[]{:S(2)}) collective-permute-start(bf16[2,2,192,608]{3,2,1,0:T(8,128)(2,1)} %get-tuple-element.336), channel_id=1, source_target_pairs={{0,16},{16,0},{8,24},{24,8},{1,17},{17,1},{9,25},{25,9},{2,18},{18... | collective-permute-start | bytes 2801672 | tf_op jit(solution)/shard_map/ppermute | solution.py:714
  642.5 102.4 %collective-permute-start.61 = (bf16[256,1536]{1,0:T(8,128)(2,1)}, bf16[256,1536]{1,0:T(8,128)(2,1)}, u32[]{:S(2)}, u32[]{:S(2)}) collective-permute-start(bf16[256,1536]{1,0:T(8,128)(2,1)} %get-tuple-element.280), channel_id=1, source_target_pairs={{0,16},{16,0},{8,24},{24,8},{1,17},{17,1},{9,25},{25,9},{2,18},{18... | collective-permute-start | bytes 2359304 | tf_op jit(solution)/shard_map/ppermute | solution.py:714
  645.3 48.4 %collective-permute-start.62 = (bf16[192,896]{1,0:T(8,128)(2,1)S(1)}, bf16[192,896]{1,0:T(8,128)(2,1)}, u32[]{:S(2)}, u32[]{:S(2)}) collective-permute-start(bf16[192,896]{1,0:T(8,128)(2,1)S(1)} %pad_maximum_fusion.32), channel_id=1, source_target_pairs={{0,16},{16,0},{8,24},{24,8},{1,17},{17,1},{9,25},{25,9},{2,18},{18... | collective-permute-start | bytes 1032200 | tf_op jit(solution)/shard_map/ppermute | solution.py:714
  648.9 96.0 %collective-permute-start.54 = (bf16[256,1536]{1,0:T(8,128)(2,1)}, bf16[256,1536]{1,0:T(8,128)(2,1)}, u32[]{:S(2)}, u32[]{:S(2)}) collective-permute-start(bf16[256,1536]{1,0:T(8,128)(2,1)} %pad_maximum_fusion.22), channel_id=1, source_target_pairs={{0,16},{16,0},{8,24},{24,8},{1,17},{17,1},{9,25},{25,9},{2,18},{18... | collective-permute-start | bytes 2359304 | tf_op jit(solution)/shard_map/ppermute | solution.py:714
  696.5 48.5 %collective-permute-start.55 = (bf16[256,1536]{1,0:T(8,128)(2,1)}, bf16[256,1536]{1,0:T(8,128)(2,1)}, u32[]{:S(2)}, u32[]{:S(2)}) collective-permute-start(bf16[256,1536]{1,0:T(8,128)(2,1)} %pad_maximum_fusion.23), channel_id=1, source_target_pairs={{0,2},{1,3},{2,0},{3,1},{4,6},{5,7},{6,4},{7,5},{8,10},{9,11},{10,... | collective-permute-start | bytes 2359304 | tf_op jit(solution)/shard_map/ppermute | solution.py:723
  (175 other events, 2229.6 us)
Sparse Core Ops, SparseCore 0:
  11.5 39.8 all-gather.13
  55.4 54.4 all-gather.15
  114.7 61.4 all-gather.7
  200.6 70.0 all-gather.9
  318.0 44.3 reduce-scatter.2
  463.7 76.5 reduce-scatter.4
  546.1 29.0 all-gather.11
